TPU v7x, 32 devices: a whole 2x2x4 slice. The times are simulated.
32 devices in a mesh: utt: 2 (over y), tm: 16 (over z, x, core).
Axes of the slice: x: 2, y: 2, z: 4, core: 2. Of those that a mesh axis runs over, the one named last changes fastest.
Arguments:
- stem: bfloat16 [4096, 1280], P(('utt', 'tm')), parts along dimension 0, may hold values from -8 to 8
- norm_gain: float32 [1280], replicated, may hold values from 0.25 to 1.75
- qkv_weight: bfloat16 [1280, 3840], P('tm'), may hold values from -0.2934839 to 0.2934839
- segment_ids: int32 [4096], P(('utt', 'tm')), parts along dimension 0, may hold values from 1 to 5, as said below
- dec_queries: bfloat16 [64, 1280], P(('utt', 'tm')), parts along dimension 0, may hold values from -9 to 9
- stretch_mask: int32 [64, 16], P(('utt', 'tm')), parts along dimension 0, may hold values 0 or 1
Outputs:
- memory: bfloat16 [4096, 1280], P(('utt', 'tm')), parts along dimension 0
- cross_out: bfloat16 [64, 1280], P(('utt', 'tm')), parts along dimension 0
There are 2 independent parts, one for each index of `utt`. A program takes and returns all parts, laid end to end along the dimension named above; an argument that names none is the same for every part. Nothing has to cross between parts.
Inputs may be any that keep to these rules, and one draw needn't show every extreme that they name: `segment_ids`: ids start at 1 and rise by one from run to run; each id covers one contiguous run of at most 512 positions, and the last run is exactly 512 positions long.
All inputs are finite; a program needn't handle non-finite values. No bound on the sum of `stretch_mask` on one device may be relied on, other than what follows from the above.
Results may differ from a plain program's by a relative error of at most 0.0062.
Values may be sent and summed in bfloat16 or wider, within the bound.
No kernel may reach another device: no remote copies, remote signals or barrier semaphores. Data moves between devices by JAX's collectives and lax.ppermute only.
A program may use at most 64 MiB of HBM per device.

v0:
```python
import math

import jax
import jax.numpy as jnp
from jax import lax
from jax.sharding import PartitionSpec as P

HD = 64


def from_behind(block, axis, distance):
    devices = range(lax.axis_size(axis))
    route = [(i - distance, i) for i in devices if i - distance in devices]
    return lax.ppermute(block, axis, route)


def on_device(stem, norm_gain, qkv_weight, segment_ids, dec_queries, stretch_mask):
    rows, width = stem.shape
    heads = width // HD
    scale = HD ** (-0.5)
    values_in = stem.astype(jnp.float32)
    mean = jnp.mean(values_in, axis=-1, keepdims=True)
    var = jnp.mean((values_in - mean) ** 2, axis=-1, keepdims=True)
    normed = ((values_in - mean) * lax.rsqrt(var + 1e-05) * norm_gain).astype(jnp.bfloat16)
    projected = jnp.dot(
        normed,
        lax.all_gather(qkv_weight, "tm", axis=0, tiled=True),
        preferred_element_type=jnp.float32,
    ).astype(jnp.bfloat16)
    query_part = projected[:, :width]
    keyvals = projected[:, width:]
    kv_pieces = []
    seg_pieces = []
    for offset in range(-4, 5):
        if offset == 0:
            kv_pieces.append(keyvals)
            seg_pieces.append(segment_ids)
        else:
            kv_pieces.append(from_behind(keyvals, "tm", -offset))
            seg_pieces.append(from_behind(segment_ids, "tm", -offset))
    extended = jnp.concatenate(kv_pieces, axis=0)
    seg_wide = jnp.concatenate(seg_pieces, axis=0)
    same = segment_ids[:, None] == seg_wide[None, :]
    group = math.gcd(heads, 4)
    span = group * HD
    groups = heads // group

    def attend(index):
        start = index * span
        query_group = lax.dynamic_slice_in_dim(query_part, start, span, 1).reshape(rows, group, HD)
        key_group = lax.dynamic_slice_in_dim(extended, start, span, 1).reshape(-1, group, HD)
        value_group = lax.dynamic_slice_in_dim(extended, width + start, span, 1).reshape(
            -1, group, HD
        )
        scores = (
            jnp.einsum("qhd,khd->hqk", query_group, key_group, preferred_element_type=jnp.float32)
            * scale
        )
        scores = jnp.where(same[None], scores, jnp.float32(-1e30))
        top = jnp.max(scores, axis=-1, keepdims=True)
        raised = jnp.exp(scores - top)
        probs = (raised / jnp.sum(raised, axis=-1, keepdims=True)).astype(jnp.bfloat16)
        context = jnp.einsum("hqk,khd->qhd", probs, value_group, preferred_element_type=jnp.float32)
        return context.reshape(rows, span)

    contexts = lax.map(attend, jnp.arange(groups, dtype=jnp.int32))
    context = jnp.transpose(contexts, (1, 0, 2)).reshape(rows, width)
    memory = (values_in + context).astype(jnp.bfloat16)
    tokens_dev = dec_queries.shape[0]
    all_queries = lax.all_gather(dec_queries, "tm", axis=0, tiled=True)
    all_masks = lax.all_gather(stretch_mask, "tm", axis=0, tiled=True)
    total_tokens = all_queries.shape[0]
    device = lax.axis_index("tm")
    column = lax.dynamic_slice_in_dim(all_masks, device, 1, 1)[:, 0]
    owner = jnp.arange(total_tokens, dtype=jnp.int32) // tokens_dev
    allowed = (column == 1) | (owner == device)
    query_heads = all_queries.reshape(total_tokens, heads, HD)
    memory_heads = memory.reshape(rows, heads, HD)
    cross = (
        jnp.einsum("thd,phd->htp", query_heads, memory_heads, preferred_element_type=jnp.float32)
        * scale
    )
    local_top = jnp.max(cross, axis=-1)
    weights = jnp.where(
        allowed[None, :, None], jnp.exp(cross - local_top[:, :, None]), jnp.float32(0.0)
    )
    denom = jnp.transpose(jnp.sum(weights, axis=-1))
    numer = jnp.einsum(
        "htp,phd->thd",
        weights.astype(jnp.bfloat16),
        memory_heads,
        preferred_element_type=jnp.float32,
    )
    top_masked = jnp.transpose(jnp.where(allowed[None, :], local_top, jnp.float32(-1e30)))
    num_all, top_all, den_all = (
        lax.all_to_all(numer[None], "tm", split_axis=1, concat_axis=0, tiled=True),
        lax.all_to_all(top_masked[None], "tm", split_axis=1, concat_axis=0, tiled=True),
        lax.all_to_all(denom[None], "tm", split_axis=1, concat_axis=0, tiled=True),
    )
    best = jnp.max(top_all, axis=0)
    factor = jnp.exp(top_all - best[None])
    num_total = jnp.sum(factor[..., None] * num_all, axis=0)
    den_total = jnp.sum(factor * den_all, axis=0)
    cross_out = (num_total / den_total[..., None]).reshape(tokens_dev, width).astype(jnp.bfloat16)
    return (memory, cross_out)


def solution(mesh):
    placed = (
        P(("utt", "tm"), None),
        P(),
        P("tm", None),
        P(("utt", "tm")),
        P(("utt", "tm"), None),
        P(("utt", "tm"), None),
    )
    return jax.shard_map(
        on_device,
        mesh=mesh,
        in_specs=placed,
        out_specs=(P(("utt", "tm"), None), P(("utt", "tm"), None)),
        check_vma=False,
    )
```

profile of v0, /device:TPU:0, one launch (start us, length us, event | category | flops | bytes accessed | tf_op | source)
XLA Modules:
  0.0 267.6 jit_solution(11485604024538364622)
XLA Ops:
  7.2 0.7 all-gather.4.cloned.1.call-update
  7.9 4.9 %collective-permute-start.8 = (s32[128]{0:T(128)}, s32[128]{0:T(128)S(1)}, u32[]{:S(2)}, u32[]{:S(2)}) collective-permute-start(s32[128]{0:T(128)} %param.11), channel_id=1, source_target_pairs={{0,4},{1,5},{2,6},{3,7},{4,8},{5,9},{6,10},{7,11},{8,12},{9,13},{1... | collective-permute-start | bytes 1544 | tf_op jit(solution)/shard_map/ppermute | solution.py:14
  12.8 2.6 collective-permute-start.9
  15.4 3.5 %collective-permute-start.10 = (s32[128]{0:T(128)}, s32[128]{0:T(128)S(1)}, u32[]{:S(2)}, u32[]{:S(2)}) collective-permute-start(s32[128]{0:T(128)} %param.11), channel_id=1, source_target_pairs={{0,2},{1,3},{2,4},{3,5},{4,6},{5,7},{6,8},{7,9},{8,10},{9,11},{10,... | collective-permute-start | bytes 1544 | tf_op jit(solution)/shard_map/ppermute | solution.py:14
  18.9 2.6 collective-permute-start.11
  21.5 1.3 collective-permute-start.12
  22.8 1.2 copy.47
  24.0 20.7 %all-gather = s32[16,2,16]{2,1,0:T(2,128)S(1)} all-gather(s32[1,2,16]{2,1,0:T(2,128)} %bitcast.74), channel_id=1, replica_groups=mesh['utt'=2,'tm'=16] {'tm'}, dimensions={0}, use_global_device_ids=true | all-gather | bytes 2176 | tf_op jit(solution)/shard_map/all_gather | solution.py:71
  45.2 18.4 %all-gather.1 = bf16[16,2,1280]{2,1,0:T(2,128)(2,1)S(1)} all-gather(bf16[1,2,1280]{2,1,0:T(2,128)(2,1)} %bitcast.73), channel_id=1, replica_groups=mesh['utt'=2,'tm'=16] {'tm'}, dimensions={0}, use_global_device_ids=true | all-gather | bytes 87040 | tf_op jit(solution)/shard_map/all_gather | solution.py:70
  63.8 1.3 collective-permute-start.13
  65.1 1.3 collective-permute-start.14
  66.4 1.3 collective-permute-start.15
  67.8 29.5 %all-gather.4.cloned.1.call-done = bf16[1280,3840]{1,0:T(8,128)(2,1)} async-done(((bf16[80,3840]{1,0:T(8,128)(2,1)}), bf16[1280,3840]{1,0:T(8,128)(2,1)}) %all-gather.4.cloned.1.call-update) | async-done | bytes 9830416 | tf_op jit(solution)/shard_map/all_gather | solution.py:27
  97.3 5.4 %convolution_convert_fusion = bf16[128,3840]{1,0:T(8,128)(2,1)S(1)} fusion(bf16[1280,3840]{1,0:T(8,128)(2,1)} %all-gather.4.cloned.1.call-done, bf16[128,1280]{0,1:T(8,128)(2,1)S(1)} %copy.47, f32[1280]{0:T(1024)} %param.9, f32[128]{0:T(128)S(1)} %add_rsqrt_fusion, f32[128]{0:T(128)S(1)} %broadcast_multiply_fusion), kind=kOutput, calls=%fused_computation.16 | convolution fusion | flops 1259601920 | bytes 11147264 | tf_op jit(solution)/shard_map/dot_general | solution.py:25
  102.7 2.5 collective-permute-start
  105.3 2.2 collective-permute-start.1
  107.7 4.1 %collective-permute-start.2 = (bf16[128,2560]{1,0:T(8,128)(2,1)S(1)}, bf16[128,2560]{1,0:T(8,128)(2,1)S(1)}, u32[]{:S(2)}, u32[]{:S(2)}) collective-permute-start(bf16[128,2560]{1,0:T(8,128)(2,1)S(1)} %slice.8), channel_id=1, source_target_pairs={{0,2},{1,3},{2,4},{3,5},{4,6},{5,7},{6,8},{7,9},{8,10},{9,11},{10,... | collective-permute-start | bytes 1966088 | tf_op jit(solution)/shard_map/ppermute | solution.py:14
  111.8 1.4 collective-permute-start.3
  113.2 1.3 collective-permute-start.4
  114.5 5.8 %collective-permute-done = bf16[128,2560]{1,0:T(8,128)(2,1)S(1)} collective-permute-done((bf16[128,2560]{1,0:T(8,128)(2,1)S(1)}, bf16[128,2560]{1,0:T(8,128)(2,1)S(1)}, u32[]{:S(2)}, u32[]{:S(2)}) %collective-permute-start) | collective-permute-done | bytes 655392 | tf_op jit(solution)/shard_map/ppermute | solution.py:14
  120.3 1.3 collective-permute-start.5
  121.6 0.9 constant_dynamic-update-slice_fusion.9
  122.5 1.3 collective-permute-start.6
  123.8 0.9 constant_dynamic-update-slice_fusion.8
  124.7 37.1 %collective-permute-done.2 = bf16[128,2560]{1,0:T(8,128)(2,1)S(1)} collective-permute-done((bf16[128,2560]{1,0:T(8,128)(2,1)S(1)}, bf16[128,2560]{1,0:T(8,128)(2,1)S(1)}, u32[]{:S(2)}, u32[]{:S(2)}) %collective-permute-start.2) | collective-permute-done | bytes 655392 | tf_op jit(solution)/shard_map/ppermute | solution.py:14
  161.7 1.3 collective-permute-start.7
  163.0 0.9 constant_dynamic-update-slice_fusion.7
  163.9 0.9 constant_dynamic-update-slice_fusion.6
  164.8 0.9 constant_dynamic-update-slice_fusion.5
  165.8 0.9 constant_dynamic-update-slice_fusion.4
  166.7 0.9 constant_dynamic-update-slice_fusion.3
  167.6 0.9 constant_dynamic-update-slice_fusion.2
  168.5 6.2 %collective-permute-done.7 = bf16[128,2560]{1,0:T(8,128)(2,1)S(1)} collective-permute-done((bf16[128,2560]{1,0:T(8,128)(2,1)S(1)}, bf16[128,2560]{1,0:T(8,128)(2,1)S(1)}, u32[]{:S(2)}, u32[]{:S(2)}) %collective-permute-start.7) | collective-permute-done | bytes 655392 | tf_op jit(solution)/shard_map/ppermute | solution.py:14
  174.6 0.9 constant_dynamic-update-slice_fusion.1
  175.5 8.9 %copy.48 = bf16[1152,2560]{0,1:T(8,128)(2,1)} copy(bf16[1152,2560]{1,0:T(8,128)(2,1)} %constant_dynamic-update-slice_fusion.1) | data formatting | bytes 11796480
  184.5 38.2 %while.13 = (s32[]{:T(128)}, f32[5,128,256]{1,2,0:T(8,128)S(1)}, s32[5]{0:T(128)S(1)}, bf16[1152,2560]{0,1:T(8,128)(2,1)}, bf16[128,1280]{1,0:T(8,128)(2,1)S(1)}...) while((s32[]{:T(128)}, f32[5,128,256]{1,2,0:T(8,128)S(1)}, ...), condition=%wide.region_5.6_spmd.clone, body=%wide.region_2.5_spmd.clone.sunk | while | flops 154682496 | bytes 9282818 | solution.py:66
  185.7 1.3 constant_dynamic-slice_fusion.5
  187.4 2.4 fusion.45
  189.7 2.3 fusion.46
  193.3 1.3 constant_dynamic-slice_fusion.5
  195.0 2.4 fusion.45
  197.4 2.3 fusion.46
  201.0 1.3 constant_dynamic-slice_fusion.5
  202.6 2.4 fusion.45
  205.0 2.3 fusion.46
  208.6 1.3 constant_dynamic-slice_fusion.5
  210.3 2.4 fusion.45
  212.7 2.3 fusion.46
  216.3 1.3 constant_dynamic-slice_fusion.5
  217.9 2.4 fusion.45
  220.3 2.3 fusion.46
  223.3 0.7 copy.56
  224.0 5.7 %all-to-all-start.2 = ((f32[1,32,20]{2,0,1:T(1,128)}), f32[1,32,20]{2,0,1:T(1,128)S(1)}, u32[]{:S(2)}, u32[]{:S(2)}) async-start(f32[1,32,20]{2,0,1:T(1,128)} %copy.56), calls=%async_computation.2 | async-start | bytes 32768 | tf_op jit(solution)/shard_map/all_to_all | solution.py:98
  229.7 0.7 copy.52
  230.4 5.8 %all-to-all-done.2 = f32[1,32,20]{2,0,1:T(1,128)S(1)} async-done(((f32[1,32,20]{2,0,1:T(1,128)}), f32[1,32,20]{2,0,1:T(1,128)S(1)}, u32[]{:S(2)}, u32[]{:S(2)}) %all-to-all-start.2) | async-done | bytes 2592 | tf_op jit(solution)/shard_map/all_to_all | solution.py:98
  236.2 3.5 %all-to-all-start = ((f32[1,32,20]{2,0,1:T(1,128)}), f32[1,32,20]{2,0,1:T(1,128)S(1)}, u32[]{:S(2)}, u32[]{:S(2)}) async-start(f32[1,32,20]{2,0,1:T(1,128)} %copy.52), calls=%async_computation | async-start | bytes 32768 | tf_op jit(solution)/shard_map/all_to_all | solution.py:97
  240.9 1.5 reduce
  242.4 0.9 reshape.135
  243.2 2.9 %all-to-all-done = f32[1,32,20]{2,0,1:T(1,128)S(1)} async-done(((f32[1,32,20]{2,0,1:T(1,128)}), f32[1,32,20]{2,0,1:T(1,128)S(1)}, u32[]{:S(2)}, u32[]{:S(2)}) %all-to-all-start) | async-done | bytes 2592 | tf_op jit(solution)/shard_map/all_to_all | solution.py:97
  246.2 3.5 %all-to-all-start.1 = ((f32[16,1,2560]{2,1,0:T(1,128)}), f32[16,1,2560]{2,1,0:T(1,128)S(1)}, u32[]{:S(2)}, u32[]{:S(2)}) async-start(f32[16,1,2560]{2,1,0:T(1,128)} %reshape.135), calls=%async_computation.1 | async-start | bytes 327680 | tf_op jit(solution)/shard_map/all_to_all | solution.py:96
  249.7 0.9 copy.59
  251.0 7.1 %all-to-all-done.1 = f32[16,1,2560]{2,1,0:T(1,128)S(1)} async-done(((f32[16,1,2560]{2,1,0:T(1,128)}), f32[16,1,2560]{2,1,0:T(1,128)S(1)}, u32[]{:S(2)}, u32[]{:S(2)}) %all-to-all-start.1) | async-done | bytes 163872 | tf_op jit(solution)/shard_map/all_to_all | solution.py:96
  258.1 1.0 reduce.1
  260.1 0.7 convert_element_type.33
  (82 shorter events, 8.5 us)
Async XLA Ops:
  7.2 90.1 %all-gather.4.cloned.1.call-start = ((), (), s32[]{:S(2)}) async-start(), calls=%async_computation.3 | async-start | bytes 10444800 | tf_op jit(solution)/shard_map/all_gather | solution.py:27
  7.9 55.9 %collective-permute-start.8 = (s32[128]{0:T(128)}, s32[128]{0:T(128)S(1)}, u32[]{:S(2)}, u32[]{:S(2)}) collective-permute-start(s32[128]{0:T(128)} %param.11), channel_id=1, source_target_pairs={{0,4},{1,5},{2,6},{3,7},{4,8},{5,9},{6,10},{7,11},{8,12},{9,13},{1... | collective-permute-start | bytes 1544 | tf_op jit(solution)/shard_map/ppermute | solution.py:14
  12.8 52.3 %collective-permute-start.9 = (s32[128]{0:T(128)}, s32[128]{0:T(128)S(1)}, u32[]{:S(2)}, u32[]{:S(2)}) collective-permute-start(s32[128]{0:T(128)} %param.11), channel_id=1, source_target_pairs={{0,3},{1,4},{2,5},{3,6},{4,7},{5,8},{6,9},{7,10},{8,11},{9,12},{10... | collective-permute-start | bytes 1544 | tf_op jit(solution)/shard_map/ppermute | solution.py:14
  15.4 51.0 %collective-permute-start.10 = (s32[128]{0:T(128)}, s32[128]{0:T(128)S(1)}, u32[]{:S(2)}, u32[]{:S(2)}) collective-permute-start(s32[128]{0:T(128)} %param.11), channel_id=1, source_target_pairs={{0,2},{1,3},{2,4},{3,5},{4,6},{5,7},{6,8},{7,9},{8,10},{9,11},{10,... | collective-permute-start | bytes 1544 | tf_op jit(solution)/shard_map/ppermute | solution.py:14
  18.9 83.9 %collective-permute-start.11 = (s32[128]{0:T(128)}, s32[128]{0:T(128)S(1)}, u32[]{:S(2)}, u32[]{:S(2)}) collective-permute-start(s32[128]{0:T(128)} %param.11), channel_id=1, source_target_pairs={{0,1},{1,2},{2,3},{3,4},{4,5},{5,6},{6,7},{7,8},{8,9},{9,10},{10,1... | collective-permute-start | bytes 1544 | tf_op jit(solution)/shard_map/ppermute | solution.py:14
  21.5 83.8 %collective-permute-start.12 = (s32[128]{0:T(128)}, s32[128]{0:T(128)S(1)}, u32[]{:S(2)}, u32[]{:S(2)}) collective-permute-start(s32[128]{0:T(128)} %param.11), channel_id=1, source_target_pairs={{1,0},{2,1},{3,2},{4,3},{5,4},{6,5},{7,6},{8,7},{9,8},{10,9},{11,1... | collective-permute-start | bytes 1544 | tf_op jit(solution)/shard_map/ppermute | solution.py:14
  63.8 43.8 %collective-permute-start.13 = (s32[128]{0:T(128)}, s32[128]{0:T(128)S(1)}, u32[]{:S(2)}, u32[]{:S(2)}) collective-permute-start(s32[128]{0:T(128)} %param.11), channel_id=1, source_target_pairs={{2,0},{3,1},{4,2},{5,3},{6,4},{7,5},{8,6},{9,7},{10,8},{11,9},{12,... | collective-permute-start | bytes 1544 | tf_op jit(solution)/shard_map/ppermute | solution.py:14
  65.1 42.5 %collective-permute-start.14 = (s32[128]{0:T(128)}, s32[128]{0:T(128)S(1)}, u32[]{:S(2)}, u32[]{:S(2)}) collective-permute-start(s32[128]{0:T(128)} %param.11), channel_id=1, source_target_pairs={{3,0},{4,1},{5,2},{6,3},{7,4},{8,5},{9,6},{10,7},{11,8},{12,9},{13... | collective-permute-start | bytes 1544 | tf_op jit(solution)/shard_map/ppermute | solution.py:14
  66.4 41.2 %collective-permute-start.15 = (s32[128]{0:T(128)}, s32[128]{0:T(128)S(1)}, u32[]{:S(2)}, u32[]{:S(2)}) collective-permute-start(s32[128]{0:T(128)} %param.11), channel_id=1, source_target_pairs={{4,0},{5,1},{6,2},{7,3},{8,4},{9,5},{10,6},{11,7},{12,8},{13,9},{1... | collective-permute-start | bytes 1544 | tf_op jit(solution)/shard_map/ppermute | solution.py:14
  67.8 37.5 %copy-start.1 = (s32[128]{0:T(128)S(1)}, s32[128]{0:T(128)}, u32[]{:S(2)}) copy-start(s32[128]{0:T(128)} %param.11) | copy-start | bytes 1540
  102.7 65.8 %copy-start = (bf16[128,3840]{1,0:T(8,128)(2,1)}, bf16[128,3840]{1,0:T(8,128)(2,1)S(1)}, u32[]{:S(2)}) copy-start(bf16[128,3840]{1,0:T(8,128)(2,1)S(1)} %convolution_convert_fusion) | copy-start | bytes 2949124
  102.7 17.6 %collective-permute-start = (bf16[128,2560]{1,0:T(8,128)(2,1)S(1)}, bf16[128,2560]{1,0:T(8,128)(2,1)S(1)}, u32[]{:S(2)}, u32[]{:S(2)}) collective-permute-start(bf16[128,2560]{1,0:T(8,128)(2,1)S(1)} %slice.8), channel_id=1, source_target_pairs={{0,4},{1,5},{2,6},{3,7},{4,8},{5,9},{6,10},{7,11},{8,12},{9,13},{1... | collective-permute-start | bytes 1966088 | tf_op jit(solution)/shard_map/ppermute | solution.py:14
  105.3 17.1 %collective-permute-start.1 = (bf16[128,2560]{1,0:T(8,128)(2,1)S(1)}, bf16[128,2560]{1,0:T(8,128)(2,1)S(1)}, u32[]{:S(2)}, u32[]{:S(2)}) collective-permute-start(bf16[128,2560]{1,0:T(8,128)(2,1)S(1)} %slice.8), channel_id=1, source_target_pairs={{0,3},{1,4},{2,5},{3,6},{4,7},{5,8},{6,9},{7,10},{8,11},{9,12},{10... | collective-permute-start | bytes 1966088 | tf_op jit(solution)/shard_map/ppermute | solution.py:14
  107.7 54.1 %collective-permute-start.2 = (bf16[128,2560]{1,0:T(8,128)(2,1)S(1)}, bf16[128,2560]{1,0:T(8,128)(2,1)S(1)}, u32[]{:S(2)}, u32[]{:S(2)}) collective-permute-start(bf16[128,2560]{1,0:T(8,128)(2,1)S(1)} %slice.8), channel_id=1, source_target_pairs={{0,2},{1,3},{2,4},{3,5},{4,6},{5,7},{6,8},{7,9},{8,10},{9,11},{10,... | collective-permute-start | bytes 1966088 | tf_op jit(solution)/shard_map/ppermute | solution.py:14
  111.8 52.1 %collective-permute-start.3 = (bf16[128,2560]{1,0:T(8,128)(2,1)S(1)}, bf16[128,2560]{1,0:T(8,128)(2,1)S(1)}, u32[]{:S(2)}, u32[]{:S(2)}) collective-permute-start(bf16[128,2560]{1,0:T(8,128)(2,1)S(1)} %slice.8), channel_id=1, source_target_pairs={{0,1},{1,2},{2,3},{3,4},{4,5},{5,6},{6,7},{7,8},{8,9},{9,10},{10,1... | collective-permute-start | bytes 1966088 | tf_op jit(solution)/shard_map/ppermute | solution.py:14
  113.2 52.6 %collective-permute-start.4 = (bf16[128,2560]{1,0:T(8,128)(2,1)S(1)}, bf16[128,2560]{1,0:T(8,128)(2,1)S(1)}, u32[]{:S(2)}, u32[]{:S(2)}) collective-permute-start(bf16[128,2560]{1,0:T(8,128)(2,1)S(1)} %slice.8), channel_id=1, source_target_pairs={{1,0},{2,1},{3,2},{4,3},{5,4},{6,5},{7,6},{8,7},{9,8},{10,9},{11,1... | collective-permute-start | bytes 1966088 | tf_op jit(solution)/shard_map/ppermute | solution.py:14
  120.3 46.4 %collective-permute-start.5 = (bf16[128,2560]{1,0:T(8,128)(2,1)S(1)}, bf16[128,2560]{1,0:T(8,128)(2,1)S(1)}, u32[]{:S(2)}, u32[]{:S(2)}) collective-permute-start(bf16[128,2560]{1,0:T(8,128)(2,1)S(1)} %slice.8), channel_id=1, source_target_pairs={{2,0},{3,1},{4,2},{5,3},{6,4},{7,5},{8,6},{9,7},{10,8},{11,9},{12,... | collective-permute-start | bytes 1966088 | tf_op jit(solution)/shard_map/ppermute | solution.py:14
  122.5 45.1 %collective-permute-start.6 = (bf16[128,2560]{1,0:T(8,128)(2,1)S(1)}, bf16[128,2560]{1,0:T(8,128)(2,1)S(1)}, u32[]{:S(2)}, u32[]{:S(2)}) collective-permute-start(bf16[128,2560]{1,0:T(8,128)(2,1)S(1)} %slice.8), channel_id=1, source_target_pairs={{3,0},{4,1},{5,2},{6,3},{7,4},{8,5},{9,6},{10,7},{11,8},{12,9},{13... | collective-permute-start | bytes 1966088 | tf_op jit(solution)/shard_map/ppermute | solution.py:14
  161.7 12.9 %collective-permute-start.7 = (bf16[128,2560]{1,0:T(8,128)(2,1)S(1)}, bf16[128,2560]{1,0:T(8,128)(2,1)S(1)}, u32[]{:S(2)}, u32[]{:S(2)}) collective-permute-start(bf16[128,2560]{1,0:T(8,128)(2,1)S(1)} %slice.8), channel_id=1, source_target_pairs={{4,0},{5,1},{6,2},{7,3},{8,4},{9,5},{10,6},{11,7},{12,8},{13,9},{1... | collective-permute-start | bytes 1966088 | tf_op jit(solution)/shard_map/ppermute | solution.py:14
  175.5 8.9 %slice-start = ((bf16[128,3840]{1,0:T(8,128)(2,1)}), bf16[128,1280]{1,0:T(8,128)(2,1)S(1)}, s32[]{:S(2)}) async-start(bf16[128,3840]{1,0:T(8,128)(2,1)} %copy-done), calls=%async_computation.4 | async-start | bytes 655360 | tf_op jit(solution)/shard_map/slice | solution.py:30
  224.0 12.2 %all-to-all-start.2 = ((f32[1,32,20]{2,0,1:T(1,128)}), f32[1,32,20]{2,0,1:T(1,128)S(1)}, u32[]{:S(2)}, u32[]{:S(2)}) async-start(f32[1,32,20]{2,0,1:T(1,128)} %copy.56), calls=%async_computation.2 | async-start | bytes 32768 | tf_op jit(solution)/shard_map/all_to_all | solution.py:98
  236.2 9.9 %all-to-all-start = ((f32[1,32,20]{2,0,1:T(1,128)}), f32[1,32,20]{2,0,1:T(1,128)S(1)}, u32[]{:S(2)}, u32[]{:S(2)}) async-start(f32[1,32,20]{2,0,1:T(1,128)} %copy.52), calls=%async_computation | async-start | bytes 32768 | tf_op jit(solution)/shard_map/all_to_all | solution.py:97
  246.2 11.9 %all-to-all-start.1 = ((f32[16,1,2560]{2,1,0:T(1,128)}), f32[16,1,2560]{2,1,0:T(1,128)S(1)}, u32[]{:S(2)}, u32[]{:S(2)}) async-start(f32[16,1,2560]{2,1,0:T(1,128)} %reshape.135), calls=%async_computation.1 | async-start | bytes 327680 | tf_op jit(solution)/shard_map/all_to_all | solution.py:96
Sparse Core Ops, SparseCore 0:
  10.3 86.9 all-gather.3
where the time goes:
time: 269 us; the launch traced here: 268 us
  waiting for transfers between devices  95.1 us (35%)
  starting transfers between devices  46.9 us (17%)
  blocking collectives  39.1 us (15%)
  local copies, waits for them, and re-layouts  34.3 us (13%)
  matrix products  29.4 us (11%)
  between operations  14.5 us (5%)
  other arithmetic  4.68 us (2%)
  loops' own time  3.65 us (1%)
    ppermute x16, waiting for transfers between devices, from_behind(): return lax.ppermute(block, axis, route)  49.1 us
    ppermute x16, starting transfers between devices, from_behind(): return lax.ppermute(block, axis, route)  34.2 us
    all_gather x1, waiting for transfers between devices, on_device(): lax.all_gather(qkv_weight, 'tm', axis=0, tiled=True)  29.5 us
    all_gather x1, blocking collectives, on_device(): all_masks = lax.all_gather(stretch_mask, 'tm', axis=0, tiled=True)  20.7 us
    unnamed x27, local copies, waits for them, and re-layouts  20.1 us
    all_gather x1, blocking collectives, on_device(): all_queries = lax.all_gather(dec_queries, 'tm', axis=0, tiled=True)  18.4 us
    sub x5, matrix products, attend(): raised = jnp.exp(scores - top)  11.9 us
    dot_general x5, matrix products, attend(): jnp.einsum('hqk,khd->qhd', probs, value_group, preferred_element_type=jnp...  11.5 us
  transfers between devices with their start and end apart: 20, of which 7 were waited for; matrix products, arithmetic and copies ran while one was open for 7% of the time, Pallas kernels for 0%

commit v1 on v0

v1 whole, which is shorter than its diff:
```python
import functools

import jax
import jax.numpy as jnp
from jax import lax
from jax.experimental import pallas as pl
from jax.experimental.pallas import tpu as pltpu
from jax.sharding import PartitionSpec as P

HD = 64
WIDE = 256
GROUP = 320
BF = jnp.bfloat16
F32 = jnp.float32
LOW = -1e30
VMEM = pl.BlockSpec(memory_space=pltpu.VMEM)
SMEM = pl.BlockSpec(memory_space=pltpu.SMEM)


def send(block, route):
    return lax.ppermute(block, "tm", route)


def swap(block, n, mask):
    return send(block, [(d, d ^ mask) for d in range(n)])


def group_of(array, g):
    return array[:, WIDE * g : WIDE * g + WIDE], array[:, 1024 + HD * g : 1024 + HD * g + HD]


def weight_group(weight, g):
    width = weight.shape[1] // 3
    parts = [group_of(weight[:, i * width : (i + 1) * width], g) for i in range(3)]
    (q0, q1), (k0, k1), (v0, v1) = parts
    return jnp.concatenate([q0, k0, v0, k1, v1, q1], axis=1)


def token_group(queries, mask, g):
    wide, tail = group_of(queries, g)
    tokens, blocks = mask.shape
    gap = jnp.zeros((tokens, HD), BF)
    return jnp.concatenate([wide, tail, gap, mask.astype(BF)], axis=1)


def encoder_kernel(n_blocks, n_parts, depth, places, gain, *refs):
    blocks = refs[:n_blocks]
    parts = refs[n_blocks : n_blocks + n_parts]
    memory, normed, weight, ids, residual, queries, keyvals = refs[n_blocks + n_parts :]
    group = places[n_blocks + n_parts + 1]
    halo_on = places[n_blocks + n_parts]

    ids[...] = jnp.zeros_like(ids)
    for i, part in enumerate(parts):
        row = pl.multiple_of(places[n_blocks + i] * depth, 16)
        weight[pl.ds(row, depth), :] = part[:depth, :]

    for i, block in enumerate(blocks):
        place = pl.multiple_of(places[i], 128)
        values = block[:128, :].astype(F32)
        mean = jnp.mean(values, axis=-1, keepdims=True)
        centred = values - mean
        var = jnp.mean(centred * centred, axis=-1, keepdims=True)
        normed[pl.ds(place, 128), :] = (centred * lax.rsqrt(var + 1e-05) * gain[...]).astype(BF)
        marks = block[128:136, :256].astype(F32)
        found = marks[:, :128] * 128.0 + marks[:, 128:]
        if i >= 8:
            found = found * halo_on.astype(F32)
        ids[:, pl.ds(place, 128)] = found

        if i < 8:

            @pl.when(place // 512 == 1)
            def _():
                row = pl.multiple_of(place - 512, 128)
                residual[pl.ds(row, 128), :WIDE] = block[
                    :128, pl.ds(pl.multiple_of(group * WIDE, 128), WIDE)
                ]
                slab = block[:128, pl.ds(pl.multiple_of(1024 + group // 2 * 128, 128), 128)]
                odd = jnp.broadcast_to(lax.rem(group, 2), (128, HD)) == 1
                residual[pl.ds(row, 128), WIDE:] = jnp.where(odd, slab[:, HD:], slab[:, :HD])

    def project(step, carry):
        row = pl.multiple_of(step * 256, 256)
        rows = normed[pl.ds(row, 256), :]
        keyvals[pl.ds(row, 256), :] = jnp.dot(
            rows, weight[:, 256:896], preferred_element_type=F32
        ).astype(BF)
        return carry

    lax.fori_loop(0, 6, project, 0)

    def project_queries(step, carry):
        row = pl.multiple_of(step * 256, 256)
        rows = normed[pl.ds(row + 512, 256), :]
        queries[pl.ds(row, 256), :WIDE] = (
            jnp.dot(rows, weight[:, :WIDE], preferred_element_type=F32).astype(BF)
        )
        tail = jnp.dot(rows, weight[:, 896:960], preferred_element_type=F32).astype(BF)
        queries[pl.ds(row, 256), WIDE:] = jnp.concatenate([tail, jnp.zeros_like(tail)], axis=1)
        return carry

    lax.fori_loop(0, 2, project_queries, 0)

    def attend(step, carry):
        row = pl.multiple_of(step * 128, 128)
        mine = jnp.broadcast_to(ids[0:1, pl.ds(row + 512, 128)], (128, 128)).T[:, 0:1]
        wide = ids[0:1, pl.ds(row, 1152)]
        bias = jnp.where(mine == wide, 0.0, LOW)
        lane = lax.broadcasted_iota(jnp.int32, (128, 128), 1)
        contexts = []
        for slab in range(3):
            query = queries[pl.ds(row, 128), 128 * slab : 128 * slab + 128] * BF(0.125)
            if slab < 2:
                none = jnp.zeros_like(query)
                heads = [jnp.where(lane < HD, query, none), jnp.where(lane < HD, none, query)]
                keys = keyvals[pl.ds(row, 1152), 128 * slab : 128 * slab + 128]
                vals = keyvals[pl.ds(row, 1152), WIDE + 128 * slab : WIDE + 128 * slab + 128]
            else:
                heads = [query]
                keys = vals = keyvals[pl.ds(row, 1152), 512:640]
            outs = []
            for head in heads:
                scores = lax.dot_general(
                    head, keys, (((1,), (1,)), ((), ())), preferred_element_type=F32
                )
                scores = scores + bias
                raised = jnp.exp(scores - jnp.max(scores, axis=-1, keepdims=True))
                total = jnp.sum(raised, axis=-1, keepdims=True)
                out = jnp.dot(raised.astype(BF), vals, preferred_element_type=F32)
                outs.append(out / total)
            if slab < 2:
                context = jnp.where(lane < HD, outs[0], outs[1])
                stem = residual[pl.ds(row, 128), 128 * slab : 128 * slab + 128].astype(F32)
                memory[pl.ds(row, 128), 128 * slab : 128 * slab + 128] = (stem + context).astype(BF)
            else:
                stem = residual[pl.ds(row, 128), WIDE:].astype(F32)
                memory[pl.ds(row, 128), WIDE:] = (stem + outs[0][:, HD:]).astype(BF)
        return carry

    lax.fori_loop(0, 4, attend, 0)


def encoder(places, gain, blocks, parts, depth):
    body = functools.partial(encoder_kernel, len(blocks), len(parts), depth)
    return pl.pallas_call(
        body,
        out_shape=jax.ShapeDtypeStruct((512, GROUP), BF),
        in_specs=[SMEM] + [VMEM] * (1 + len(blocks) + len(parts)),
        out_specs=VMEM,
        scratch_shapes=[
            pltpu.VMEM((1536, 1280), BF),
            pltpu.VMEM((1280, 960), BF),
            pltpu.VMEM((8, 1536), F32),
            pltpu.VMEM((512, GROUP), BF),
            pltpu.VMEM((512, 384), BF),
            pltpu.VMEM((1536, 640), BF),
        ],
        compiler_params=pltpu.CompilerParams(vmem_limit_bytes=48 * 1024 * 1024),
    )(places, gain, *blocks, *parts)


def spread(columns, rows, slab):
    lane = lax.broadcasted_iota(jnp.int32, (rows, 128), 1)
    return jnp.where(lane < HD, columns[2 * slab], columns[min(2 * slab + 1, 4)])


def cross_kernel(place, memory, tokens, out):
    count = tokens.shape[0]
    blocks = tokens.shape[1] - 384
    first = place[0]
    me = place[1]
    spot = lax.broadcasted_iota(jnp.int32, (count, blocks), 1)
    asked = tokens[:, 384:].astype(F32)
    order = lax.broadcasted_iota(jnp.int32, (count, 1), 0)
    half = count // 2
    relative = 2 * (lax.rem(order, half) // 2) + order // half
    owner = relative ^ me
    allowed = []
    for b in range(4):
        ask = jnp.sum(jnp.where(spot == first + b, asked, 0.0), axis=-1, keepdims=True)
        allowed.append((ask > 0.5) | (owner == first + b))
    lane = lax.broadcasted_iota(jnp.int32, (count, 128), 1)
    bias = jnp.concatenate(
        [jnp.broadcast_to(jnp.where(a, 0.0, LOW), (count, 128)) for a in allowed], axis=1
    )
    stats = jnp.zeros((count, 128), F32)
    for slab in range(3):
        query = tokens[:, 128 * slab : 128 * slab + 128] * BF(0.125)
        if slab < 2:
            none = jnp.zeros_like(query)
            heads = [jnp.where(lane < HD, query, none), jnp.where(lane < HD, none, query)]
            held = memory[:, 128 * slab : 128 * slab + 128]
        else:
            heads = [query[:, :HD]]
            held = memory[:, WIDE:]
        outs = []
        for i, head in enumerate(heads):
            cross = lax.dot_general(
                head, held, (((1,), (1,)), ((), ())), preferred_element_type=F32
            )
            cross = jnp.where(bias < 0.0, LOW, cross)
            top = jnp.max(cross, axis=-1, keepdims=True)
            raised = jnp.where(bias < 0.0, 0.0, jnp.exp(cross - top))
            den = jnp.sum(raised, axis=-1, keepdims=True)
            outs.append(jnp.dot(raised.astype(BF), held, preferred_element_type=F32))
            stats = jnp.where(lane == 2 * slab + i, top, stats)
            stats = jnp.where(lane == 8 + 2 * slab + i, den, stats)
        if slab < 2:
            out[:, 128 * slab : 128 * slab + 128] = jnp.where(lane < HD, outs[0], outs[1])
        else:
            out[:, WIDE:384] = jnp.concatenate([outs[0], jnp.zeros_like(outs[0])], axis=1)
    out[:, 384:] = stats


def cross_partial(place, memory, tokens):
    return pl.pallas_call(
        cross_kernel,
        out_shape=jax.ShapeDtypeStruct((tokens.shape[0], 512), F32),
        in_specs=[SMEM, VMEM, VMEM],
        out_specs=VMEM,
    )(place, memory, tokens)


def merge_kernel(last, mine, theirs, out):
    rows = theirs.shape[0]
    ours = mine[:rows, 384:]
    other = theirs[:, 384:]
    lane = lax.broadcasted_iota(jnp.int32, (rows, 128), 1)
    stats = jnp.zeros((rows, 128), F32)
    left, right, dens = [], [], []
    for head in range(5):
        a, b = ours[:, head : head + 1], other[:, head : head + 1]
        best = jnp.maximum(a, b)
        a, b = jnp.exp(a - best), jnp.exp(b - best)
        den = a * ours[:, 8 + head : 9 + head] + b * other[:, 8 + head : 9 + head]
        left.append(a)
        right.append(b)
        dens.append(den)
        stats = jnp.where(lane == head, best, stats)
        stats = jnp.where(lane == 8 + head, den, stats)
    for slab in range(3):
        span = slice(128 * slab, 128 * slab + 128)
        total = spread(left, rows, slab) * mine[:rows, span] + spread(right, rows, slab) * theirs[:, span]
        if last:
            out[:, span] = (total / spread(dens, rows, slab)).astype(BF)
        else:
            out[:, span] = total
    if not last:
        out[:, 384:] = stats


def merge(mine, theirs, last):
    rows = theirs.shape[0]
    shape = jax.ShapeDtypeStruct((rows, 384), BF) if last else jax.ShapeDtypeStruct((rows, 512), F32)
    return pl.pallas_call(
        functools.partial(merge_kernel, last),
        out_shape=shape,
        in_specs=[VMEM, VMEM],
        out_specs=VMEM,
    )(mine, theirs)


def gather_groups(pieces, group):
    wide, tail = [], []
    for g in range(4):
        turn = group ^ g
        piece = jnp.where(
            turn < 2,
            jnp.where(turn == 0, pieces[0], pieces[1]),
            jnp.where(turn == 2, pieces[2], pieces[3]),
        )
        wide.append(piece[:, :WIDE])
        tail.append(piece[:, WIDE:GROUP])
    return jnp.concatenate(wide + tail, axis=1)


def on_device(stem, norm_gain, qkv_weight, segment_ids, dec_queries, stretch_mask):
    n = lax.axis_size("tm")
    layers = n // 4
    me = lax.axis_index("tm")
    z, x, c = me // 4, (me // 2) % 2, me % 2
    p, k = z % 2, z // 2
    quarter = 2 * k + c
    group = 2 * p + x
    depth = qkv_weight.shape[0]

    digits = jnp.concatenate([segment_ids // 128, segment_ids % 128]).astype(BF)
    extra = jnp.zeros((8, stem.shape[1]), BF).at[0, :256].set(digits)
    own = jnp.concatenate([stem, extra], axis=0)

    steps = [1 if i % 2 else -1 for i in range(layers)]
    near = [
        (4 * i + j, 4 * (i + s) + j)
        for i, s in enumerate(steps)
        for j in range(4)
        if 0 <= i + s < layers
    ]
    far = [
        (4 * i + j, 4 * (i + 2 * s) + j)
        for i, s in enumerate(steps)
        for j in range(4)
        if 0 <= i + 2 * s < layers
    ]
    pair = swap(own, n, 4)
    halo_near = send(own, near)
    halo_far = send(own, far)
    own_x = swap(own, n, 2)
    pair_x = swap(pair, n, 2)
    if layers == 4:
        halo = jnp.where((z == 1) | (z == 2), halo_near, halo_far)
        halo_x = swap(halo, n, 2)
        halo_on = (c != k).astype(jnp.int32)
        halo_c, halo_xc = swap(halo, n, 1), swap(halo_x, n, 1)
    else:
        left = jnp.where(p == 0, halo_near, halo_far)
        right = jnp.where(p == 0, halo_far, halo_near)
        left_x, right_x = swap(left, n, 2), swap(right, n, 2)
        halo = jnp.where(c == 0, left, right)
        halo_x = jnp.where(c == 0, left_x, right_x)
        halo_c = swap(jnp.where(c == 0, right, left), n, 1)
        halo_xc = swap(jnp.where(c == 0, right_x, left_x), n, 1)
        halo_on = jnp.int32(1)
    blocks = [own, swap(own, n, 1), own_x, swap(own_x, n, 1)]
    blocks += [pair, swap(pair, n, 1), pair_x, swap(pair_x, n, 1)]
    blocks += [halo, halo_c, halo_x, halo_xc]
    starts = [512 * (p - c + 1), 512 * (2 - p - c), 1024 * c]
    inner = [128 * (2 * x + c), 128 * (2 * x + 1 - c), 128 * (2 - 2 * x + c), 128 * (3 - 2 * x - c)]
    places = [s + i for s in starts for i in inner]

    if depth % 16 == 0 and layers == 4:
        payload = jnp.stack(
            [
                jnp.concatenate(
                    [
                        weight_group(qkv_weight, g),
                        jnp.pad(
                            token_group(dec_queries, stretch_mask, g),
                            ((0, 6), (0, 960 - 384 - stretch_mask.shape[1])),
                        ),
                    ],
                    axis=0,
                )
                for g in range(4)
            ]
        )
        chosen = [
            [
                lax.dynamic_index_in_dim(payload, 2 * (p ^ a) + (x ^ b), 0, keepdims=False)
                for b in range(2)
            ]
            for a in range(2)
        ]
        parts = {}
        for far_z in (3, 2, 1, 0):
            for far_x in (1, 0):
                mask = 4 * far_z + 2 * far_x
                part = chosen[far_z % 2][far_x]
                if mask:
                    part = swap(part, n, mask)
                parts[mask] = part
                parts[mask + 1] = swap(part, n, 1)
        order = [m for core in range(2) for m in range(core, n, 2)]
        tokens = jnp.concatenate(
            [parts[m][depth : depth + 2, : 384 + stretch_mask.shape[1]] for m in order], axis=0
        )
        part_places = [me ^ m for m in order]
        weights = [parts[m] for m in order]
    else:
        whole = lax.all_gather(qkv_weight, "tm", axis=0, tiled=True)
        grouped = jnp.stack([weight_group(whole, g) for g in range(4)])
        weights = [lax.dynamic_index_in_dim(grouped, group, 0, keepdims=False)]
        part_places = [jnp.int32(0)]
        depth = whole.shape[0]
        packed = jnp.stack([token_group(dec_queries, stretch_mask, g) for g in range(4)])
        every = lax.all_gather(packed, "tm", axis=1, tiled=True)
        every = lax.dynamic_index_in_dim(every, group, 0, keepdims=False)
        order = jnp.array([m for core in range(2) for m in range(core, n, 2)], jnp.int32)
        rows = 2 * (order ^ me)
        tokens = jnp.take(every, jnp.stack([rows, rows + 1], axis=1).reshape(-1), axis=0)

    table = jnp.stack([jnp.asarray(v, jnp.int32) for v in places + part_places + [halo_on, group]])
    held = encoder(table, norm_gain.reshape(1, -1), blocks, weights, depth)

    pieces = []
    for turn in range(2):
        rows = lax.dynamic_slice_in_dim(held, 256 * (x ^ turn), 256, 0)
        route = [
            (
                8 * (d // 8) + 4 * (d // 4 % 2) + (d & 2) + (d & 1),
                8 * (d // 8) + 4 * (d & 1) + ((d & 2) ^ (2 * turn)) + (d // 4 % 2),
            )
            for d in range(n)
        ]
        got = send(rows, route)
        keep = lax.dynamic_slice_in_dim(got, 128 * c, 128, 0)
        give = swap(lax.dynamic_slice_in_dim(got, 128 * (1 - c), 128, 0), n, 1)
        pieces.append((keep, give))
    memory = gather_groups(
        [pieces[0][0], pieces[1][0], pieces[0][1], pieces[1][1]], 2 * c + x
    )

    place = jnp.stack([4 * quarter, me]).astype(jnp.int32)
    partial = cross_partial(place, held, tokens)
    bits = [1]
    step = n // 2
    while step >= 8:
        bits.append(step)
        step //= 2
    for i, bit in enumerate(bits):
        half = partial.shape[0] // 2
        theirs = swap(partial[half:], n, bit)
        partial = merge(partial, theirs, i == len(bits) - 1)
    final = [partial[0:2]]
    for i in (1, 2, 3):
        final.append(swap(partial[2 * i : 2 * i + 2], n, 2 * i))
    cross_out = gather_groups(final, group)
    return (memory, cross_out)


def solution(mesh):
    placed = (
        P(("utt", "tm"), None),
        P(),
        P("tm", None),
        P(("utt", "tm")),
        P(("utt", "tm"), None),
        P(("utt", "tm"), None),
    )
    return jax.shard_map(
        on_device,
        mesh=mesh,
        in_specs=placed,
        out_specs=(P(("utt", "tm"), None), P(("utt", "tm"), None)),
        check_vma=False,
    )
```

time: 269 us -> 167 us (0.62)
  blocking collectives: 39.1 us -> 0 us
  waiting for transfers between devices: 95.1 us -> 61.2 us
  matrix products: 29.4 us -> 0 us
  Pallas kernels: 0 us -> 26 us
  between operations: 14.5 us -> 1.3 us
  starting transfers between devices: 46.9 us -> 35.8 us
  local copies, waits for them, and re-layouts: 34.3 us -> 38.8 us
  loops' own time: 3.65 us -> 0 us
    all_gather x2 -> x0, blocking collectives: 39.1 us -> none  [the longest x1 20.7 us: on_device(): all_masks = lax.all_gather(stretch_mask, 'tm', axis=0, tiled=True)]
    all_gather x1 -> x0, waiting for transfers between devices: 29.5 us -> none  [on_device(): lax.all_gather(qkv_weight, 'tm', axis=0, tiled=True)]
    pallas_call x0 -> x4, Pallas kernels: none -> 26 us  [the longest x1 19.8 us: encoder(): pl.pallas_call(body, out_shape=jax.ShapeDtypeStruct((512, GROUP), BF), in...]
    dot_general x8 -> x0, matrix products: 17.5 us -> none  [the longest x5 11.5 us: attend(): jnp.einsum('hqk,khd->qhd', probs, value_group, preferred_element_type=jnp...]
    slice x3 -> x39, local copies, waits for them, and re-layouts: 0.05 us -> 16.6 us  [the longest x16 12.1 us: on_device(): parts[m][depth:depth + 2, :384 + stretch_mask.shape[1]]]
    all_to_all x3 -> x0, waiting for transfers between devices: 15.9 us -> none  [the longest x1 7.14 us: on_device(): lax.all_to_all(numer[None], 'tm', split_axis=1, concat_axis=0, tiled=True)]
    all_to_all x3 -> x0, starting transfers between devices: 12.7 us -> none  [the longest x1 5.71 us: on_device(): lax.all_to_all(denom[None], 'tm', split_axis=1, concat_axis=0, tiled=True)]
    ppermute x16 -> x36, waiting for transfers between devices: 49.1 us -> 61.2 us  [send(): return lax.ppermute(block, 'tm', route)]
  transfers between devices with their start and end apart: 20 -> 36, of which waited for: 7 -> 13; matrix products, arithmetic and copies ran while one was open for 7% -> 12% of each run, Pallas kernels for 0% -> 1%
where the time goes in v1:
time: 167 us; the launch traced here: 166 us
  waiting for transfers between devices  61.2 us (37%)
  local copies, waits for them, and re-layouts  38.8 us (23%)
  starting transfers between devices  35.8 us (21%)
  Pallas kernels  26 us (16%)
  other arithmetic  2.65 us (2%)
    ppermute x36, waiting for transfers between devices, send(): return lax.ppermute(block, 'tm', route)  61.2 us
    ppermute x36, starting transfers between devices, send(): return lax.ppermute(block, 'tm', route)  35.8 us
    pallas_call x1, Pallas kernels, encoder(): pl.pallas_call(body, out_shape=jax.ShapeDtypeStruct((512, GROUP), BF), in...  19.8 us
    unnamed x72, local copies, waits for them, and re-layouts  16.8 us
    slice x16, local copies, waits for them, and re-layouts, on_device(): parts[m][depth:depth + 2, :384 + stretch_mask.shape[1]]  12.1 us
  transfers between devices with their start and end apart: 36, of which 13 were waited for; matrix products, arithmetic and copies ran while one was open for 12% of the time, Pallas kernels for 1%

profile of v1, /device:TPU:0, one launch (start us, length us, event | category | flops | bytes accessed | tf_op | source)
XLA Modules:
  0.0 165.7 jit_solution(2535158335678125717)
XLA Ops:
  1.4 1.0 fusion.21
  2.5 1.0 fusion.20
  5.0 3.0 %collective-permute-start.12 = (bf16[88,960]{1,0:T(8,128)(2,1)S(1)}, bf16[88,960]{1,0:T(8,128)(2,1)S(1)}, u32[]{:S(2)}, u32[]{:S(2)}) collective-permute-start(bf16[88,960]{1,0:T(8,128)(2,1)S(1)} %get-tuple-element.16), channel_id=1, source_target_pairs={{0,2},{1,3},{2,0},{3,1},{4,6},{5,7},{6,4},{7,5},{8,10},{9,11},{10,... | collective-permute-start | bytes 506888 | tf_op jit(solution)/shard_map/ppermute | solution.py:21
  8.0 1.6 collective-permute-start.13
  10.3 1.3 collective-permute-start.8
  11.6 0.9 collective-permute-done.12.refs_13_
  12.5 4.5 %collective-permute-start.15 = (bf16[88,960]{1,0:T(8,128)(2,1)S(1)}, bf16[88,960]{1,0:T(8,128)(2,1)S(1)}, u32[]{:S(2)}, u32[]{:S(2)}) collective-permute-start(bf16[88,960]{1,0:T(8,128)(2,1)S(1)} %get-tuple-element.17.refs_12_), channel_id=1, source_target_pairs={{0,8},{1,9},{2,10},{3,11},{4,12},{5,13},{6,14},{7,15},{8,0},{9,1},... | collective-permute-start | bytes 506888 | tf_op jit(solution)/shard_map/ppermute | solution.py:21
  17.1 1.0 collective-permute-start.16
  18.1 3.4 %collective-permute-start.17 = (bf16[88,960]{1,0:T(8,128)(2,1)S(1)}, bf16[88,960]{1,0:T(8,128)(2,1)S(1)}, u32[]{:S(2)}, u32[]{:S(2)}) collective-permute-start(bf16[88,960]{1,0:T(8,128)(2,1)S(1)} %get-tuple-element.15), channel_id=1, source_target_pairs={{0,12},{1,13},{2,14},{3,15},{4,8},{5,9},{6,10},{7,11},{8,4},{9,5},... | collective-permute-start | bytes 506888 | tf_op jit(solution)/shard_map/ppermute | solution.py:21
  21.4 25.5 %collective-permute-done.15.refs_16_ = bf16[88,960]{1,0:T(8,128)(2,1)S(1)} collective-permute-done((bf16[88,960]{1,0:T(8,128)(2,1)S(1)}, bf16[88,960]{1,0:T(8,128)(2,1)S(1)}, u32[]{:S(2)}, u32[]{:S(2)}) %collective-permute-start.15) | collective-permute-done | bytes 168992 | tf_op jit(solution)/shard_map/ppermute | solution.py:21
  47.0 3.4 %collective-permute-start.18 = (bf16[88,960]{1,0:T(8,128)(2,1)S(1)}, bf16[88,960]{1,0:T(8,128)(2,1)S(1)}, u32[]{:S(2)}, u32[]{:S(2)}) collective-permute-start(bf16[88,960]{1,0:T(8,128)(2,1)S(1)} %get-tuple-element.14), channel_id=1, source_target_pairs={{0,14},{1,15},{2,12},{3,13},{4,10},{5,11},{6,8},{7,9},{8,6},{9,7},... | collective-permute-start | bytes 506888 | tf_op jit(solution)/shard_map/ppermute | solution.py:21
  50.4 5.2 %collective-permute-done.16.refs_17_ = bf16[88,960]{1,0:T(8,128)(2,1)S(1)} collective-permute-done((bf16[88,960]{1,0:T(8,128)(2,1)S(1)}, bf16[88,960]{1,0:T(8,128)(2,1)S(1)}, u32[]{:S(2)}, u32[]{:S(2)}) %collective-permute-start.16) | collective-permute-done | bytes 168992 | tf_op jit(solution)/shard_map/ppermute | solution.py:21
  56.1 5.7 %collective-permute-start.3 = (bf16[136,1280]{1,0:T(8,128)(2,1)S(1)}, bf16[136,1280]{1,0:T(8,128)(2,1)S(1)}, u32[]{:S(2)}, u32[]{:S(2)}) collective-permute-start(bf16[136,1280]{1,0:T(8,128)(2,1)S(1)} %pad_maximum_fusion.1.refs_0_), channel_id=1, source_target_pairs={{0,4},{1,5},{2,6},{3,7},{4,0},{5,1},{6,2},{7,3},{8,12},{9,13},{10,... | collective-permute-start | bytes 1044488 | tf_op jit(solution)/shard_map/ppermute | solution.py:21
  62.9 1.0 broadcast_select_fusion.refs_8_
  64.8 3.1 %collective-permute-done.3.refs_4_ = bf16[136,1280]{1,0:T(8,128)(2,1)S(1)} collective-permute-done((bf16[136,1280]{1,0:T(8,128)(2,1)S(1)}, bf16[136,1280]{1,0:T(8,128)(2,1)S(1)}, u32[]{:S(2)}, u32[]{:S(2)}) %collective-permute-start.3) | collective-permute-done | bytes 348192 | tf_op jit(solution)/shard_map/ppermute | solution.py:21
  67.9 1.4 collective-permute-start.5
  70.1 1.4 collective-permute-done.25.refs_26_
  71.6 1.3 collective-permute-done.26.refs_27_
  73.7 1.5 collective-permute-done.1.refs_2_
  75.3 7.5 %collective-permute-done.5.refs_6_ = bf16[136,1280]{1,0:T(8,128)(2,1)S(1)} collective-permute-done((bf16[136,1280]{1,0:T(8,128)(2,1)S(1)}, bf16[136,1280]{1,0:T(8,128)(2,1)S(1)}, u32[]{:S(2)}, u32[]{:S(2)}) %collective-permute-start.5) | collective-permute-done | bytes 348192 | tf_op jit(solution)/shard_map/ppermute | solution.py:21
  82.7 7.0 %collective-permute-done.10.refs_10_ = bf16[136,1280]{1,0:T(8,128)(2,1)} collective-permute-done((bf16[136,1280]{1,0:T(8,128)(2,1)S(1)}, bf16[136,1280]{1,0:T(8,128)(2,1)}, u32[]{:S(2)}, u32[]{:S(2)}) %collective-permute-start.10) | collective-permute-done | bytes 348192 | tf_op jit(solution)/shard_map/ppermute | solution.py:21
  91.3 0.7 slice.342
  92.0 0.7 slice.343
  92.7 0.7 slice.344
  93.4 0.7 slice.345
  94.1 0.7 slice.346
  94.8 0.7 slice.347
  95.5 0.7 slice.348
  96.2 0.7 slice.349
  96.9 0.7 slice.350
  97.6 0.7 slice.351
  98.3 1.3 slice.352
  99.5 1.3 slice.353
  100.8 1.3 slice.354
  102.1 1.3 slice.355
  103.4 3.2 %concatenate.80.tokens = bf16[32,400]{1,0:T(8,128)(2,1)} concatenate(bf16[2,400]{1,0:T(2,128)(2,1)S(1)} %slice.340, bf16[2,400]{1,0:T(2,128)(2,1)S(1)} %slice.341, bf16[2,400]{1,0:T(2,128)(2,1)S(1)} %slice.342, bf16[2,400]{1,0:T(2,128)(2,1)S(1)} %slice.343, bf16[2,400]{1,0:T(2,128)(2,1)S(1)} %slice.344, bf16[2,400]{1,0:T(2,128)(2,1)S(1)} %slice.345, bf16[2,400]{1,0:T(2,128)(2,1)S(1)} %slice.346, ...), dimensions={0} | concatenate | bytes 51200 | tf_op jit(solution)/shard_map/concatenate | solution.py:364
  106.6 0.9 copy-done.1
  107.5 0.9 copy-done.3
  108.4 0.9 copy-done.5
  109.4 0.9 copy-done.7
  110.3 0.9 copy-done.9
  111.2 0.9 copy-done.11
  112.1 0.9 copy-done.13
  113.0 0.9 copy-done.15
  114.0 0.9 copy-done.17
  114.9 0.9 copy-done.19
  115.8 0.9 copy-done.21
  116.7 0.9 copy-done.23
  117.7 0.9 copy-done.25
  118.6 0.9 copy-done.27
  119.5 19.8 %shard_map.77.memory = bf16[512,320]{1,0:T(8,128)(2,1)} custom-call(s32[30]{0:T(128)S(1)} %stack.149.places, f32[1,1280]{1,0:T(1,128)S(1)} %reshape.57.gain, bf16[136,1280]{1,0:T(8,128)(2,1)S(1)} %pad_maximum_fusion.1.refs_0_, bf16[136,1280]{1,0:T(8,128)(2,1)S(1)} %collective-permute-done.refs_1_, bf16[136,1280]{1,0:T(8,128)(2,1)S(1)} %collective-permute-done.1.refs_2_, ...), custom_call_target="tpu_custom_call" | custom-call | tf_op jit(solution)/shard_map/pallas_call | solution.py:146
  139.3 3.1 %shard_map.78.mine = f32[32,512]{1,0:T(8,128)} custom-call(s32[2]{0:T(128)} %pad_add_fusion.place, bf16[512,320]{1,0:T(8,128)(2,1)} %shard_map.77.memory, bf16[32,400]{1,0:T(8,128)(2,1)} %concatenate.80.tokens), custom_call_target="tpu_custom_call" | custom-call | tf_op jit(solution)/shard_map/pallas_call | solution.py:217
  142.4 0.8 slice.356
  143.5 0.9 collective-permute-done.31.theirs
  145.0 1.6 shard_map.79.mine
  146.6 0.7 slice.357
  149.0 3.0 %collective-permute-done.32.theirs = f32[8,512]{1,0:T(8,128)S(1)} collective-permute-done((f32[8,512]{1,0:T(8,128)S(1)}, f32[8,512]{1,0:T(8,128)S(1)}, u32[]{:S(2)}, u32[]{:S(2)}) %collective-permute-start.32) | collective-permute-done | bytes 16416 | tf_op jit(solution)/shard_map/ppermute | solution.py:21
  152.6 1.5 shard_map.80
  154.1 0.8 fusion.22
  155.5 3.1 %collective-permute-start.34 = (bf16[2,384]{1,0:T(2,128)(2,1)S(1)}, bf16[2,384]{1,0:T(2,128)(2,1)S(1)}, u32[]{:S(2)}, u32[]{:S(2)}) collective-permute-start(bf16[2,384]{1,0:T(2,128)(2,1)S(1)} %get-tuple-element.53), channel_id=1, source_target_pairs={{0,4},{1,5},{2,6},{3,7},{4,0},{5,1},{6,2},{7,3},{8,12},{9,13},{10,... | collective-permute-start | bytes 4616 | tf_op jit(solution)/shard_map/ppermute | solution.py:21
  159.3 0.9 collective-permute-done.34
  160.2 2.9 %collective-permute-done.35 = bf16[2,384]{1,0:T(2,128)(2,1)S(1)} collective-permute-done((bf16[2,384]{1,0:T(2,128)(2,1)S(1)}, bf16[2,384]{1,0:T(2,128)(2,1)S(1)}, u32[]{:S(2)}, u32[]{:S(2)}) %collective-permute-start.35) | collective-permute-done | bytes 1568 | tf_op jit(solution)/shard_map/ppermute | solution.py:21
  163.1 0.7 broadcast_select_fusion.3
  164.8 0.8 concatenate.79
  (150 shorter events, 13.9 us)
Async XLA Ops:
  4.9 4.7 %copy-start.29 = (bf16[128,1280]{1,0:T(8,128)(2,1)S(1)}, bf16[128,1280]{1,0:T(8,128)(2,1)}, u32[]{:S(2)}) copy-start(bf16[128,1280]{1,0:T(8,128)(2,1)} %param.8) | copy-start | bytes 983044
  5.0 7.6 %collective-permute-start.12 = (bf16[88,960]{1,0:T(8,128)(2,1)S(1)}, bf16[88,960]{1,0:T(8,128)(2,1)S(1)}, u32[]{:S(2)}, u32[]{:S(2)}) collective-permute-start(bf16[88,960]{1,0:T(8,128)(2,1)S(1)} %get-tuple-element.16), channel_id=1, source_target_pairs={{0,2},{1,3},{2,0},{3,1},{4,6},{5,7},{6,4},{7,5},{8,10},{9,11},{10,... | collective-permute-start | bytes 506888 | tf_op jit(solution)/shard_map/ppermute | solution.py:21
  8.0 1.6 copy-start.35
  8.0 9.1 %collective-permute-start.13 = (bf16[88,960]{1,0:T(8,128)(2,1)S(1)}, bf16[88,960]{1,0:T(8,128)(2,1)S(1)}, u32[]{:S(2)}, u32[]{:S(2)}) collective-permute-start(bf16[88,960]{1,0:T(8,128)(2,1)S(1)} %get-tuple-element.15), channel_id=1, source_target_pairs={{0,4},{1,5},{2,6},{3,7},{4,0},{5,1},{6,2},{7,3},{8,12},{9,13},{10,... | collective-permute-start | bytes 506888 | tf_op jit(solution)/shard_map/ppermute | solution.py:21
  9.6 8.5 %collective-permute-start.14 = (bf16[88,960]{1,0:T(8,128)(2,1)S(1)}, bf16[88,960]{1,0:T(8,128)(2,1)S(1)}, u32[]{:S(2)}, u32[]{:S(2)}) collective-permute-start(bf16[88,960]{1,0:T(8,128)(2,1)S(1)} %get-tuple-element.14), channel_id=1, source_target_pairs={{0,6},{1,7},{2,4},{3,5},{4,2},{5,3},{6,0},{7,1},{8,14},{9,15},{10,... | collective-permute-start | bytes 506888 | tf_op jit(solution)/shard_map/ppermute | solution.py:21
  9.6 52.8 %collective-permute-start.7 = (bf16[136,1280]{1,0:T(8,128)(2,1)S(1)}, bf16[136,1280]{1,0:T(8,128)(2,1)S(1)}, u32[]{:S(2)}, u32[]{:S(2)}) collective-permute-start(bf16[136,1280]{1,0:T(8,128)(2,1)S(1)} %pad_maximum_fusion.1.refs_0_), channel_id=1, source_target_pairs={{4,8},{5,9},{6,10},{7,11},{8,4},{9,5},{10,6},{11,7},{20,24},{21,25... | collective-permute-start | bytes 1044488 | tf_op jit(solution)/shard_map/ppermute | solution.py:21
  10.3 52.1 %collective-permute-start.8 = (bf16[136,1280]{1,0:T(8,128)(2,1)S(1)}, bf16[136,1280]{1,0:T(8,128)(2,1)}, u32[]{:S(2)}, u32[]{:S(2)}) collective-permute-start(bf16[136,1280]{1,0:T(8,128)(2,1)S(1)} %pad_maximum_fusion.1.refs_0_), channel_id=1, source_target_pairs={{4,12},{5,13},{6,14},{7,15},{8,0},{9,1},{10,2},{11,3},{20,28},{21,... | collective-permute-start | bytes 1044488 | tf_op jit(solution)/shard_map/ppermute | solution.py:21
  12.5 34.4 %collective-permute-start.15 = (bf16[88,960]{1,0:T(8,128)(2,1)S(1)}, bf16[88,960]{1,0:T(8,128)(2,1)S(1)}, u32[]{:S(2)}, u32[]{:S(2)}) collective-permute-start(bf16[88,960]{1,0:T(8,128)(2,1)S(1)} %get-tuple-element.17.refs_12_), channel_id=1, source_target_pairs={{0,8},{1,9},{2,10},{3,11},{4,12},{5,13},{6,14},{7,15},{8,0},{9,1},... | collective-permute-start | bytes 506888 | tf_op jit(solution)/shard_map/ppermute | solution.py:21
  17.1 46.9 %copy-start = (bf16[88,960]{1,0:T(8,128)(2,1)}, bf16[88,960]{1,0:T(8,128)(2,1)S(1)}, u32[]{:S(2)}) copy-start(bf16[88,960]{1,0:T(8,128)(2,1)S(1)} %collective-permute-done.13.refs_14_) | copy-start | bytes 506884
  17.1 38.6 %collective-permute-start.16 = (bf16[88,960]{1,0:T(8,128)(2,1)S(1)}, bf16[88,960]{1,0:T(8,128)(2,1)S(1)}, u32[]{:S(2)}, u32[]{:S(2)}) collective-permute-start(bf16[88,960]{1,0:T(8,128)(2,1)S(1)} %get-tuple-element.16), channel_id=1, source_target_pairs={{0,10},{1,11},{2,8},{3,9},{4,14},{5,15},{6,12},{7,13},{8,2},{9,3},... | collective-permute-start | bytes 506888 | tf_op jit(solution)/shard_map/ppermute | solution.py:21
  18.1 45.9 %copy-start.2 = (bf16[88,960]{1,0:T(8,128)(2,1)}, bf16[88,960]{1,0:T(8,128)(2,1)S(1)}, u32[]{:S(2)}) copy-start(bf16[88,960]{1,0:T(8,128)(2,1)S(1)} %collective-permute-done.14.refs_15_) | copy-start | bytes 506884
  18.1 37.6 %collective-permute-start.17 = (bf16[88,960]{1,0:T(8,128)(2,1)S(1)}, bf16[88,960]{1,0:T(8,128)(2,1)S(1)}, u32[]{:S(2)}, u32[]{:S(2)}) collective-permute-start(bf16[88,960]{1,0:T(8,128)(2,1)S(1)} %get-tuple-element.15), channel_id=1, source_target_pairs={{0,12},{1,13},{2,14},{3,15},{4,8},{5,9},{6,10},{7,11},{8,4},{9,5},... | collective-permute-start | bytes 506888 | tf_op jit(solution)/shard_map/ppermute | solution.py:21
  47.0 17.0 %copy-start.4 = (bf16[88,960]{1,0:T(8,128)(2,1)}, bf16[88,960]{1,0:T(8,128)(2,1)S(1)}, u32[]{:S(2)}) copy-start(bf16[88,960]{1,0:T(8,128)(2,1)S(1)} %collective-permute-done.15.refs_16_) | copy-start | bytes 506884
  47.0 9.2 %collective-permute-start.18 = (bf16[88,960]{1,0:T(8,128)(2,1)S(1)}, bf16[88,960]{1,0:T(8,128)(2,1)S(1)}, u32[]{:S(2)}, u32[]{:S(2)}) collective-permute-start(bf16[88,960]{1,0:T(8,128)(2,1)S(1)} %get-tuple-element.14), channel_id=1, source_target_pairs={{0,14},{1,15},{2,12},{3,13},{4,10},{5,11},{6,8},{7,9},{8,6},{9,7},... | collective-permute-start | bytes 506888 | tf_op jit(solution)/shard_map/ppermute | solution.py:21
  55.6 8.4 %copy-start.6 = (bf16[88,960]{1,0:T(8,128)(2,1)}, bf16[88,960]{1,0:T(8,128)(2,1)S(1)}, u32[]{:S(2)}) copy-start(bf16[88,960]{1,0:T(8,128)(2,1)S(1)} %collective-permute-done.16.refs_17_) | copy-start | bytes 506884
  55.6 6.3 %collective-permute-start.19 = (bf16[88,960]{1,0:T(8,128)(2,1)S(1)}, bf16[88,960]{1,0:T(8,128)(2,1)S(1)}, u32[]{:S(2)}, u32[]{:S(2)}) collective-permute-start(bf16[88,960]{1,0:T(8,128)(2,1)S(1)} %get-tuple-element.17.refs_12_), channel_id=1, source_target_pairs={{0,1},{1,0},{2,3},{3,2},{4,5},{5,4},{6,7},{7,6},{8,9},{9,8},{10,11... | collective-permute-start | bytes 506888 | tf_op jit(solution)/shard_map/ppermute | solution.py:21
  55.6 14.4 %copy-start.8 = (bf16[88,960]{1,0:T(8,128)(2,1)}, bf16[88,960]{1,0:T(8,128)(2,1)S(1)}, u32[]{:S(2)}) copy-start(bf16[88,960]{1,0:T(8,128)(2,1)S(1)} %collective-permute-done.17.refs_18_) | copy-start | bytes 506884
  55.6 6.2 %collective-permute-start.20 = (bf16[88,960]{1,0:T(8,128)(2,1)S(1)}, bf16[88,960]{1,0:T(8,128)(2,1)S(1)}, u32[]{:S(2)}, u32[]{:S(2)}) collective-permute-start(bf16[88,960]{1,0:T(8,128)(2,1)S(1)} %collective-permute-done.12.refs_13_), channel_id=1, source_target_pairs={{0,1},{1,0},{2,3},{3,2},{4,5},{5,4},{6,7},{7,6},{8,9},{9,8},{10,11... | collective-permute-start | bytes 506888 | tf_op jit(solution)/shard_map/ppermute | solution.py:21
  56.1 17.6 %copy-start.10 = (bf16[88,960]{1,0:T(8,128)(2,1)}, bf16[88,960]{1,0:T(8,128)(2,1)S(1)}, u32[]{:S(2)}) copy-start(bf16[88,960]{1,0:T(8,128)(2,1)S(1)} %collective-permute-done.18.refs_19_) | copy-start | bytes 506884
  56.1 11.8 %collective-permute-start.3 = (bf16[136,1280]{1,0:T(8,128)(2,1)S(1)}, bf16[136,1280]{1,0:T(8,128)(2,1)S(1)}, u32[]{:S(2)}, u32[]{:S(2)}) collective-permute-start(bf16[136,1280]{1,0:T(8,128)(2,1)S(1)} %pad_maximum_fusion.1.refs_0_), channel_id=1, source_target_pairs={{0,4},{1,5},{2,6},{3,7},{4,0},{5,1},{6,2},{7,3},{8,12},{9,13},{10,... | collective-permute-start | bytes 1044488 | tf_op jit(solution)/shard_map/ppermute | solution.py:21
  61.9 2.1 %collective-permute-start.21 = (bf16[88,960]{1,0:T(8,128)(2,1)S(1)}, bf16[88,960]{1,0:T(8,128)(2,1)S(1)}, u32[]{:S(2)}, u32[]{:S(2)}) collective-permute-start(bf16[88,960]{1,0:T(8,128)(2,1)S(1)} %collective-permute-done.13.refs_14_), channel_id=1, source_target_pairs={{0,1},{1,0},{2,3},{3,2},{4,5},{5,4},{6,7},{7,6},{8,9},{9,8},{10,11... | collective-permute-start | bytes 506888 | tf_op jit(solution)/shard_map/ppermute | solution.py:21
  61.9 2.3 %copy-start.14 = (bf16[88,960]{1,0:T(8,128)(2,1)}, bf16[88,960]{1,0:T(8,128)(2,1)S(1)}, u32[]{:S(2)}) copy-start(bf16[88,960]{1,0:T(8,128)(2,1)S(1)} %collective-permute-done.20.refs_21_) | copy-start | bytes 506884
  61.9 2.3 %collective-permute-start.22 = (bf16[88,960]{1,0:T(8,128)(2,1)S(1)}, bf16[88,960]{1,0:T(8,128)(2,1)S(1)}, u32[]{:S(2)}, u32[]{:S(2)}) collective-permute-start(bf16[88,960]{1,0:T(8,128)(2,1)S(1)} %collective-permute-done.14.refs_15_), channel_id=1, source_target_pairs={{0,1},{1,0},{2,3},{3,2},{4,5},{5,4},{6,7},{7,6},{8,9},{9,8},{10,11... | collective-permute-start | bytes 506888 | tf_op jit(solution)/shard_map/ppermute | solution.py:21
  62.4 6.9 %collective-permute-start.23 = (bf16[88,960]{1,0:T(8,128)(2,1)S(1)}, bf16[88,960]{1,0:T(8,128)(2,1)S(1)}, u32[]{:S(2)}, u32[]{:S(2)}) collective-permute-start(bf16[88,960]{1,0:T(8,128)(2,1)S(1)} %collective-permute-done.15.refs_16_), channel_id=1, source_target_pairs={{0,1},{1,0},{2,3},{3,2},{4,5},{5,4},{6,7},{7,6},{8,9},{9,8},{10,11... | collective-permute-start | bytes 506888 | tf_op jit(solution)/shard_map/ppermute | solution.py:21
  62.5 7.4 %collective-permute-start.24 = (bf16[88,960]{1,0:T(8,128)(2,1)S(1)}, bf16[88,960]{1,0:T(8,128)(2,1)S(1)}, u32[]{:S(2)}, u32[]{:S(2)}) collective-permute-start(bf16[88,960]{1,0:T(8,128)(2,1)S(1)} %collective-permute-done.16.refs_17_), channel_id=1, source_target_pairs={{0,1},{1,0},{2,3},{3,2},{4,5},{5,4},{6,7},{7,6},{8,9},{9,8},{10,11... | collective-permute-start | bytes 506888 | tf_op jit(solution)/shard_map/ppermute | solution.py:21
  64.0 9.6 %collective-permute-start = (bf16[136,1280]{1,0:T(8,128)(2,1)S(1)}, bf16[136,1280]{1,0:T(8,128)(2,1)S(1)}, u32[]{:S(2)}, u32[]{:S(2)}) collective-permute-start(bf16[136,1280]{1,0:T(8,128)(2,1)S(1)} %pad_maximum_fusion.1.refs_0_), channel_id=1, source_target_pairs={{0,1},{1,0},{2,3},{3,2},{4,5},{5,4},{6,7},{7,6},{8,9},{9,8},{10,11... | collective-permute-start | bytes 1044488 | tf_op jit(solution)/shard_map/ppermute | solution.py:21
  64.2 25.5 %copy-start.18 = (bf16[88,960]{1,0:T(8,128)(2,1)}, bf16[88,960]{1,0:T(8,128)(2,1)S(1)}, u32[]{:S(2)}) copy-start(bf16[88,960]{1,0:T(8,128)(2,1)S(1)} %collective-permute-done.22.refs_23_) | copy-start | bytes 506884
  64.2 11.0 %collective-permute-start.1 = (bf16[136,1280]{1,0:T(8,128)(2,1)S(1)}, bf16[136,1280]{1,0:T(8,128)(2,1)S(1)}, u32[]{:S(2)}, u32[]{:S(2)}) collective-permute-start(bf16[136,1280]{1,0:T(8,128)(2,1)S(1)} %pad_maximum_fusion.1.refs_0_), channel_id=1, source_target_pairs={{0,2},{1,3},{2,0},{3,1},{4,6},{5,7},{6,4},{7,5},{8,10},{9,11},{10,... | collective-permute-start | bytes 1044488 | tf_op jit(solution)/shard_map/ppermute | solution.py:21
  67.9 14.8 %collective-permute-start.5 = (bf16[136,1280]{1,0:T(8,128)(2,1)S(1)}, bf16[136,1280]{1,0:T(8,128)(2,1)S(1)}, u32[]{:S(2)}, u32[]{:S(2)}) collective-permute-start(bf16[136,1280]{1,0:T(8,128)(2,1)S(1)} %collective-permute-done.3.refs_4_), channel_id=1, source_target_pairs={{0,2},{1,3},{2,0},{3,1},{4,6},{5,7},{6,4},{7,5},{8,10},{9,11},{10,... | collective-permute-start | bytes 1044488 | tf_op jit(solution)/shard_map/ppermute | solution.py:21
  69.3 20.4 %copy-start.20 = (bf16[88,960]{1,0:T(8,128)(2,1)}, bf16[88,960]{1,0:T(8,128)(2,1)S(1)}, u32[]{:S(2)}) copy-start(bf16[88,960]{1,0:T(8,128)(2,1)S(1)} %collective-permute-done.23.refs_24_) | copy-start | bytes 506884
  69.3 20.4 %collective-permute-start.10 = (bf16[136,1280]{1,0:T(8,128)(2,1)S(1)}, bf16[136,1280]{1,0:T(8,128)(2,1)}, u32[]{:S(2)}, u32[]{:S(2)}) collective-permute-start(bf16[136,1280]{1,0:T(8,128)(2,1)S(1)} %broadcast_select_fusion.refs_8_), channel_id=1, source_target_pairs={{0,2},{1,3},{2,0},{3,1},{4,6},{5,7},{6,4},{7,5},{8,10},{9,11},{10,... | collective-permute-start | bytes 1044488 | tf_op jit(solution)/shard_map/ppermute | solution.py:21
  70.0 19.7 %copy-start.22 = (bf16[88,960]{1,0:T(8,128)(2,1)}, bf16[88,960]{1,0:T(8,128)(2,1)S(1)}, u32[]{:S(2)}) copy-start(bf16[88,960]{1,0:T(8,128)(2,1)S(1)} %collective-permute-done.24.refs_25_) | copy-start | bytes 506884
  70.0 1.5 collective-permute-start.25
  71.5 1.6 copy-start.24
  71.5 1.4 collective-permute-start.26
  72.9 33.7 %collective-permute-start.9 = (bf16[136,1280]{1,0:T(8,128)(2,1)S(1)}, bf16[136,1280]{1,0:T(8,128)(2,1)}, u32[]{:S(2)}, u32[]{:S(2)}) collective-permute-start(bf16[136,1280]{1,0:T(8,128)(2,1)S(1)} %broadcast_select_fusion.refs_8_), channel_id=1, source_target_pairs={{0,1},{1,0},{2,3},{3,2},{4,5},{5,4},{6,7},{7,6},{8,9},{9,8},{10,11... | collective-permute-start | bytes 1044488 | tf_op jit(solution)/shard_map/ppermute | solution.py:21
  73.6 33.0 %collective-permute-start.4 = (bf16[136,1280]{1,0:T(8,128)(2,1)S(1)}, bf16[136,1280]{1,0:T(8,128)(2,1)S(1)}, u32[]{:S(2)}, u32[]{:S(2)}) collective-permute-start(bf16[136,1280]{1,0:T(8,128)(2,1)S(1)} %collective-permute-done.3.refs_4_), channel_id=1, source_target_pairs={{0,1},{1,0},{2,3},{3,2},{4,5},{5,4},{6,7},{7,6},{8,9},{9,8},{10,11... | collective-permute-start | bytes 1044488 | tf_op jit(solution)/shard_map/ppermute | solution.py:21
  75.2 31.3 %collective-permute-start.2 = (bf16[136,1280]{1,0:T(8,128)(2,1)S(1)}, bf16[136,1280]{1,0:T(8,128)(2,1)S(1)}, u32[]{:S(2)}, u32[]{:S(2)}) collective-permute-start(bf16[136,1280]{1,0:T(8,128)(2,1)S(1)} %collective-permute-done.1.refs_2_), channel_id=1, source_target_pairs={{0,1},{1,0},{2,3},{3,2},{4,5},{5,4},{6,7},{7,6},{8,9},{9,8},{10,11... | collective-permute-start | bytes 1044488 | tf_op jit(solution)/shard_map/ppermute | solution.py:21
  82.7 23.9 %collective-permute-start.6 = (bf16[136,1280]{1,0:T(8,128)(2,1)S(1)}, bf16[136,1280]{1,0:T(8,128)(2,1)S(1)}, u32[]{:S(2)}, u32[]{:S(2)}) collective-permute-start(bf16[136,1280]{1,0:T(8,128)(2,1)S(1)} %collective-permute-done.5.refs_6_), channel_id=1, source_target_pairs={{0,1},{1,0},{2,3},{3,2},{4,5},{5,4},{6,7},{7,6},{8,9},{9,8},{10,11... | collective-permute-start | bytes 1044488 | tf_op jit(solution)/shard_map/ppermute | solution.py:21
  89.7 16.8 %collective-permute-start.11 = (bf16[136,1280]{1,0:T(8,128)(2,1)}, bf16[136,1280]{1,0:T(8,128)(2,1)}, u32[]{:S(2)}, u32[]{:S(2)}) collective-permute-start(bf16[136,1280]{1,0:T(8,128)(2,1)} %collective-permute-done.10.refs_10_), channel_id=1, source_target_pairs={{0,1},{1,0},{2,3},{3,2},{4,5},{5,4},{6,7},{7,6},{8,9},{9,8},{10,11... | collective-permute-start | bytes 1044488 | tf_op jit(solution)/shard_map/ppermute | solution.py:21
  106.6 0.9 copy-start.1
  107.5 0.9 copy-start.3
  108.4 0.9 copy-start.5
  109.4 0.9 copy-start.7
  110.3 0.9 copy-start.9
  111.2 0.9 copy-start.11
  112.1 0.9 copy-start.13
  113.0 0.9 copy-start.15
  114.0 0.9 copy-start.17
  114.9 0.9 copy-start.19
  115.8 0.9 copy-start.21
  116.7 0.9 copy-start.23
  117.7 0.9 copy-start.25
  118.6 0.9 copy-start.27
  139.3 8.4 %copy-start.28 = (bf16[512,320]{1,0:T(8,128)(2,1)S(1)}, bf16[512,320]{1,0:T(8,128)(2,1)}, u32[]{:S(2)}) copy-start(bf16[512,320]{1,0:T(8,128)(2,1)} %shard_map.77.memory) | copy-start | bytes 983044
  143.1 1.3 collective-permute-start.31
  147.4 4.6 %collective-permute-start.32 = (f32[8,512]{1,0:T(8,128)S(1)}, f32[8,512]{1,0:T(8,128)S(1)}, u32[]{:S(2)}, u32[]{:S(2)}) collective-permute-start(f32[8,512]{1,0:T(8,128)S(1)} %slice.357), channel_id=1, source_target_pairs={{0,8},{1,9},{2,10},{3,11},{4,12},{5,13},{6,14},{7,15},{8,0},{9,1},... | collective-permute-start | bytes 49160 | tf_op jit(solution)/shard_map/ppermute | solution.py:21
  147.7 10.9 %collective-permute-start.27 = (bf16[256,320]{1,0:T(8,128)(2,1)S(1)}, bf16[256,320]{1,0:T(8,128)(2,1)S(1)}, u32[]{:S(2)}, u32[]{:S(2)}) collective-permute-start(bf16[256,320]{1,0:T(8,128)(2,1)S(1)} %get-tuple-element.47), channel_id=1, source_target_pairs={{0,0},{1,4},{2,2},{3,6},{4,1},{5,5},{6,3},{7,7},{8,8},{9,12},{10,1... | collective-permute-start | bytes 491528 | tf_op jit(solution)/shard_map/ppermute | solution.py:21
  148.4 10.3 %collective-permute-start.28 = (bf16[256,320]{1,0:T(8,128)(2,1)S(1)}, bf16[256,320]{1,0:T(8,128)(2,1)S(1)}, u32[]{:S(2)}, u32[]{:S(2)}) collective-permute-start(bf16[256,320]{1,0:T(8,128)(2,1)S(1)} %get-tuple-element.46), channel_id=1, source_target_pairs={{0,2},{1,6},{2,0},{3,4},{4,3},{5,7},{6,1},{7,5},{8,10},{9,14},{10,... | collective-permute-start | bytes 491528 | tf_op jit(solution)/shard_map/ppermute | solution.py:21
  154.9 4.4 %collective-permute-start.33 = (bf16[2,384]{1,0:T(2,128)(2,1)S(1)}, bf16[2,384]{1,0:T(2,128)(2,1)S(1)}, u32[]{:S(2)}, u32[]{:S(2)}) collective-permute-start(bf16[2,384]{1,0:T(2,128)(2,1)S(1)} %get-tuple-element.54), channel_id=1, source_target_pairs={{0,2},{1,3},{2,0},{3,1},{4,6},{5,7},{6,4},{7,5},{8,10},{9,11},{10,... | collective-permute-start | bytes 4616 | tf_op jit(solution)/shard_map/ppermute | solution.py:21
  155.5 4.7 %collective-permute-start.34 = (bf16[2,384]{1,0:T(2,128)(2,1)S(1)}, bf16[2,384]{1,0:T(2,128)(2,1)S(1)}, u32[]{:S(2)}, u32[]{:S(2)}) collective-permute-start(bf16[2,384]{1,0:T(2,128)(2,1)S(1)} %get-tuple-element.53), channel_id=1, source_target_pairs={{0,4},{1,5},{2,6},{3,7},{4,0},{5,1},{6,2},{7,3},{8,12},{9,13},{10,... | collective-permute-start | bytes 4616 | tf_op jit(solution)/shard_map/ppermute | solution.py:21
  158.6 4.5 %collective-permute-start.35 = (bf16[2,384]{1,0:T(2,128)(2,1)S(1)}, bf16[2,384]{1,0:T(2,128)(2,1)S(1)}, u32[]{:S(2)}, u32[]{:S(2)}) collective-permute-start(bf16[2,384]{1,0:T(2,128)(2,1)S(1)} %get-tuple-element.52), channel_id=1, source_target_pairs={{0,6},{1,7},{2,4},{3,5},{4,2},{5,3},{6,0},{7,1},{8,14},{9,15},{10,... | collective-permute-start | bytes 4616 | tf_op jit(solution)/shard_map/ppermute | solution.py:21
  158.6 5.9 %collective-permute-start.29 = (bf16[128,320]{1,0:T(8,128)(2,1)S(1)}, bf16[128,320]{1,0:T(8,128)(2,1)S(1)}, u32[]{:S(2)}, u32[]{:S(2)}) collective-permute-start(bf16[128,320]{1,0:T(8,128)(2,1)S(1)} %constant_dynamic-slice_fusion.1), channel_id=1, source_target_pairs={{0,1},{1,0},{2,3},{3,2},{4,5},{5,4},{6,7},{7,6},{8,9},{9,8},{10,11... | collective-permute-start | bytes 245768 | tf_op jit(solution)/shard_map/ppermute | solution.py:21
  158.8 5.8 %collective-permute-start.30 = (bf16[128,320]{1,0:T(8,128)(2,1)S(1)}, bf16[128,320]{1,0:T(8,128)(2,1)S(1)}, u32[]{:S(2)}, u32[]{:S(2)}) collective-permute-start(bf16[128,320]{1,0:T(8,128)(2,1)S(1)} %constant_dynamic-slice_fusion), channel_id=1, source_target_pairs={{0,1},{1,0},{2,3},{3,2},{4,5},{5,4},{6,7},{7,6},{8,9},{9,8},{10,11... | collective-permute-start | bytes 245768 | tf_op jit(solution)/shard_map/ppermute | solution.py:21
  (8 other events, 5.5 us)

commit v2 on v1

--- a/solution.py
+++ b/solution.py
@@ -25,6 +25,10 @@
     return send(block, [(d, d ^ mask) for d in range(n)])
 
 
+def scalars(values):
+    return jnp.stack([jnp.asarray(v, jnp.int32) for v in values])
+
+
 def group_of(array, g):
     return array[:, WIDE * g : WIDE * g + WIDE], array[:, 1024 + HD * g : 1024 + HD * g + HD]
 
@@ -38,23 +42,16 @@
 
 def token_group(queries, mask, g):
     wide, tail = group_of(queries, g)
-    tokens, blocks = mask.shape
-    gap = jnp.zeros((tokens, HD), BF)
-    return jnp.concatenate([wide, tail, gap, mask.astype(BF)], axis=1)
-
-
-def encoder_kernel(n_blocks, n_parts, depth, places, gain, *refs):
-    blocks = refs[:n_blocks]
-    parts = refs[n_blocks : n_blocks + n_parts]
-    memory, normed, weight, ids, residual, queries, keyvals = refs[n_blocks + n_parts :]
-    group = places[n_blocks + n_parts + 1]
-    halo_on = places[n_blocks + n_parts]
-
+    heads = [wide[:, HD * i : HD * i + HD] for i in range(4)] + [tail]
+    asked = jnp.pad(mask.astype(BF), ((0, 0), (0, HD - mask.shape[1])))
+    return jnp.concatenate(heads + [asked], axis=0)
+
+
+def norm_kernel(places, gain, *refs):
+    blocks, (normed, ids, residual) = refs[:4], refs[4:]
+    group = places[4]
+    real = places[5].astype(F32)
     ids[...] = jnp.zeros_like(ids)
-    for i, part in enumerate(parts):
-        row = pl.multiple_of(places[n_blocks + i] * depth, 16)
-        weight[pl.ds(row, depth), :] = part[:depth, :]
-
     for i, block in enumerate(blocks):
         place = pl.multiple_of(places[i], 128)
         values = block[:128, :].astype(F32)
@@ -63,44 +60,69 @@
         var = jnp.mean(centred * centred, axis=-1, keepdims=True)
         normed[pl.ds(place, 128), :] = (centred * lax.rsqrt(var + 1e-05) * gain[...]).astype(BF)
         marks = block[128:136, :256].astype(F32)
-        found = marks[:, :128] * 128.0 + marks[:, 128:]
-        if i >= 8:
-            found = found * halo_on.astype(F32)
-        ids[:, pl.ds(place, 128)] = found
-
-        if i < 8:
-
-            @pl.when(place // 512 == 1)
+        ids[:, pl.ds(place, 128)] = (marks[:, :128] * 128.0 + marks[:, 128:]) * real
+        residual[pl.ds(place, 128), :WIDE] = block[
+            :128, pl.ds(pl.multiple_of(group * WIDE, 128), WIDE)
+        ]
+        slab = block[:128, pl.ds(pl.multiple_of(1024 + group // 2 * 128, 128), 128)]
+        odd = jnp.broadcast_to(lax.rem(group, 2), (128, HD)) == 1
+        residual[pl.ds(place, 128), WIDE:] = jnp.where(odd, slab[:, HD:], slab[:, :HD])
+
+
+def norm_layer(places, gain, blocks):
+    return pl.pallas_call(
+        norm_kernel,
+        out_shape=(
+            jax.ShapeDtypeStruct((512, 1280), BF),
+            jax.ShapeDtypeStruct((8, 512), F32),
+            jax.ShapeDtypeStruct((512, GROUP), BF),
+        ),
+        in_specs=[SMEM] + [VMEM] * 5,
+        out_specs=(VMEM, VMEM, VMEM),
+        compiler_params=pltpu.CompilerParams(vmem_limit_bytes=16 * 1024 * 1024),
+    )(places, gain, *blocks)
+
+
+def encoder_kernel(n_parts, depth, places, *refs):
+    layers = [refs[3 * i : 3 * i + 3] for i in range(3)]
+    parts = refs[9 : 9 + n_parts]
+    memory, weight, ids, residual, queries, keyvals = refs[9 + n_parts :]
+
+    for i, part in enumerate(parts):
+        row = pl.multiple_of(places[3 + i] * depth, 16)
+        weight[pl.ds(row, depth), :] = part[...]
+
+    for i, (normed, marks, kept) in enumerate(layers):
+        place = pl.multiple_of(places[i], 512)
+        ids[:, pl.ds(place, 512)] = marks[...]
+
+        def project(step, carry):
+            row = pl.multiple_of(step * 256, 256)
+            to = pl.multiple_of(place + row, 256)
+            keyvals[pl.ds(to, 256), :] = jnp.dot(
+                normed[pl.ds(row, 256), :], weight[:, 256:896], preferred_element_type=F32
+            ).astype(BF)
+            return carry
+
+        lax.fori_loop(0, 2, project, 0)
+        if i < 2:
+
+            @pl.when(place == 512)
             def _():
-                row = pl.multiple_of(place - 512, 128)
-                residual[pl.ds(row, 128), :WIDE] = block[
-                    :128, pl.ds(pl.multiple_of(group * WIDE, 128), WIDE)
-                ]
-                slab = block[:128, pl.ds(pl.multiple_of(1024 + group // 2 * 128, 128), 128)]
-                odd = jnp.broadcast_to(lax.rem(group, 2), (128, HD)) == 1
-                residual[pl.ds(row, 128), WIDE:] = jnp.where(odd, slab[:, HD:], slab[:, :HD])
-
-    def project(step, carry):
-        row = pl.multiple_of(step * 256, 256)
-        rows = normed[pl.ds(row, 256), :]
-        keyvals[pl.ds(row, 256), :] = jnp.dot(
-            rows, weight[:, 256:896], preferred_element_type=F32
-        ).astype(BF)
-        return carry
-
-    lax.fori_loop(0, 6, project, 0)
-
-    def project_queries(step, carry):
-        row = pl.multiple_of(step * 256, 256)
-        rows = normed[pl.ds(row + 512, 256), :]
-        queries[pl.ds(row, 256), :WIDE] = (
-            jnp.dot(rows, weight[:, :WIDE], preferred_element_type=F32).astype(BF)
-        )
-        tail = jnp.dot(rows, weight[:, 896:960], preferred_element_type=F32).astype(BF)
-        queries[pl.ds(row, 256), WIDE:] = jnp.concatenate([tail, jnp.zeros_like(tail)], axis=1)
-        return carry
-
-    lax.fori_loop(0, 2, project_queries, 0)
+                residual[...] = kept[...]
+
+                def project_queries(step, carry):
+                    row = pl.multiple_of(step * 256, 256)
+                    rows = normed[pl.ds(row, 256), :]
+                    queries[pl.ds(row, 256), :WIDE] = jnp.dot(
+                        rows, weight[:, :WIDE], preferred_element_type=F32
+                    ).astype(BF)
+                    tail = jnp.dot(rows, weight[:, 896:], preferred_element_type=F32).astype(BF)
+                    lane = lax.broadcasted_iota(jnp.int32, tail.shape, 1)
+                    queries[pl.ds(row, 256), WIDE:] = jnp.where(lane < HD, tail, jnp.zeros_like(tail))
+                    return carry
+
+                lax.fori_loop(0, 2, project_queries, 0)
 
     def attend(step, carry):
         row = pl.multiple_of(step * 128, 128)
@@ -108,7 +130,6 @@
         wide = ids[0:1, pl.ds(row, 1152)]
         bias = jnp.where(mine == wide, 0.0, LOW)
         lane = lax.broadcasted_iota(jnp.int32, (128, 128), 1)
-        contexts = []
         for slab in range(3):
             query = queries[pl.ds(row, 128), 128 * slab : 128 * slab + 128] * BF(0.125)
             if slab < 2:
@@ -141,23 +162,21 @@
     lax.fori_loop(0, 4, attend, 0)
 
 
-def encoder(places, gain, blocks, parts, depth):
-    body = functools.partial(encoder_kernel, len(blocks), len(parts), depth)
+def encoder(places, layers, parts, depth):
     return pl.pallas_call(
-        body,
+        functools.partial(encoder_kernel, len(parts), depth),
         out_shape=jax.ShapeDtypeStruct((512, GROUP), BF),
-        in_specs=[SMEM] + [VMEM] * (1 + len(blocks) + len(parts)),
+        in_specs=[SMEM] + [VMEM] * (9 + len(parts)),
         out_specs=VMEM,
         scratch_shapes=[
-            pltpu.VMEM((1536, 1280), BF),
-            pltpu.VMEM((1280, 960), BF),
+            pltpu.VMEM((1280, 1024), BF),
             pltpu.VMEM((8, 1536), F32),
             pltpu.VMEM((512, GROUP), BF),
             pltpu.VMEM((512, 384), BF),
             pltpu.VMEM((1536, 640), BF),
         ],
-        compiler_params=pltpu.CompilerParams(vmem_limit_bytes=48 * 1024 * 1024),
-    )(places, gain, *blocks, *parts)
+        compiler_params=pltpu.CompilerParams(vmem_limit_bytes=20 * 1024 * 1024),
+    )(places, *[a for layer in layers for a in layer], *parts)
 
 
 def spread(columns, rows, slab):
@@ -165,20 +184,30 @@
     return jnp.where(lane < HD, columns[2 * slab], columns[min(2 * slab + 1, 4)])
 
 
-def cross_kernel(place, memory, tokens, out):
-    count = tokens.shape[0]
-    blocks = tokens.shape[1] - 384
-    first = place[0]
-    me = place[1]
+def cross_kernel(chips, place, memory, *refs):
+    parts, (out, tokens) = refs[:-2], refs[-2:]
+    first, me, core, straight = place[0], place[1], place[2], place[3]
+    count = out.shape[0]
+    half = count // 2
+    if chips:
+        for i in range(len(parts) // 2):
+            here, there = parts[2 * i][:24, 960:], parts[2 * i + 1][:24, 960:]
+            rows = jnp.where(jnp.broadcast_to(straight, (24, HD)) == 1, here.astype(F32), there.astype(F32))
+            for h in range(6):
+                low, high = rows[4 * h : 4 * h + 2], rows[4 * h + 2 : 4 * h + 4]
+                flip = jnp.broadcast_to(core, (2, HD)) == 1
+                tokens[h, 2 * i : 2 * i + 2, :] = jnp.where(flip, high, low)
+                tokens[h, half + 2 * i : half + 2 * i + 2, :] = jnp.where(flip, low, high)
+    else:
+        tokens[...] = parts[0][...].astype(F32)
+    blocks = HD
     spot = lax.broadcasted_iota(jnp.int32, (count, blocks), 1)
-    asked = tokens[:, 384:].astype(F32)
     order = lax.broadcasted_iota(jnp.int32, (count, 1), 0)
-    half = count // 2
     relative = 2 * (lax.rem(order, half) // 2) + order // half
     owner = relative ^ me
     allowed = []
     for b in range(4):
-        ask = jnp.sum(jnp.where(spot == first + b, asked, 0.0), axis=-1, keepdims=True)
+        ask = jnp.sum(jnp.where(spot == first + b, tokens[5], 0.0), axis=-1, keepdims=True)
         allowed.append((ask > 0.5) | (owner == first + b))
     lane = lax.broadcasted_iota(jnp.int32, (count, 128), 1)
     bias = jnp.concatenate(
@@ -186,13 +215,15 @@
     )
     stats = jnp.zeros((count, 128), F32)
     for slab in range(3):
-        query = tokens[:, 128 * slab : 128 * slab + 128] * BF(0.125)
+        heads = [(tokens[h] * 0.125).astype(BF) for h in range(2 * slab, min(2 * slab + 2, 5))]
+        none = jnp.zeros_like(heads[0])
         if slab < 2:
-            none = jnp.zeros_like(query)
-            heads = [jnp.where(lane < HD, query, none), jnp.where(lane < HD, none, query)]
+            heads = [
+                jnp.concatenate([heads[0], none], axis=1),
+                jnp.concatenate([none, heads[1]], axis=1),
+            ]
             held = memory[:, 128 * slab : 128 * slab + 128]
         else:
-            heads = [query[:, :HD]]
             held = memory[:, WIDE:]
         outs = []
         for i, head in enumerate(heads):
@@ -213,13 +244,14 @@
     out[:, 384:] = stats
 
 
-def cross_partial(place, memory, tokens):
+def cross_partial(place, memory, parts, count, chips):
     return pl.pallas_call(
-        cross_kernel,
-        out_shape=jax.ShapeDtypeStruct((tokens.shape[0], 512), F32),
-        in_specs=[SMEM, VMEM, VMEM],
+        functools.partial(cross_kernel, chips),
+        out_shape=jax.ShapeDtypeStruct((count, 512), F32),
+        in_specs=[SMEM] + [VMEM] * (1 + len(parts)),
         out_specs=VMEM,
-    )(place, memory, tokens)
+        scratch_shapes=[pltpu.VMEM((6, count, HD), F32)],
+    )(place, memory, *parts)
 
 
 def merge_kernel(last, mine, theirs, out):
@@ -321,66 +353,84 @@
         halo_c = swap(jnp.where(c == 0, right, left), n, 1)
         halo_xc = swap(jnp.where(c == 0, right_x, left_x), n, 1)
         halo_on = jnp.int32(1)
-    blocks = [own, swap(own, n, 1), own_x, swap(own_x, n, 1)]
-    blocks += [pair, swap(pair, n, 1), pair_x, swap(pair_x, n, 1)]
-    blocks += [halo, halo_c, halo_x, halo_xc]
-    starts = [512 * (p - c + 1), 512 * (2 - p - c), 1024 * c]
+    own_layer = [own, swap(own, n, 1), own_x, swap(own_x, n, 1)]
+    pair_layer = [pair, swap(pair, n, 1), pair_x, swap(pair_x, n, 1)]
+    halo_layer = [halo, halo_c, halo_x, halo_xc]
     inner = [128 * (2 * x + c), 128 * (2 * x + 1 - c), 128 * (2 - 2 * x + c), 128 * (3 - 2 * x - c)]
-    places = [s + i for s in starts for i in inner]
-
-    if depth % 16 == 0 and layers == 4:
+    gain = norm_gain.reshape(1, -1)
+    layered = []
+    for blocks, real in ((own_layer, 1), (pair_layer, 1), (halo_layer, halo_on)):
+        layered.append(norm_layer(scalars(inner + [group, real]), gain, blocks))
+    places = [512 * (p - c + 1), 512 * (2 - p - c), 1024 * c]
+
+    utts = lax.axis_size("utt")
+    straight = (c == lax.axis_index("utt") % 2).astype(jnp.int32)
+    if depth % 16 == 0 and layers == 4 and utts % 2 == 0:
+        carriers = [(u, d) for u in range(utts) for d in range(n) if d % 2 == u % 2]
+
+        def carry(block, turn_u, turn_d):
+            route = [(u * n + d, (u ^ turn_u) * n + (d ^ turn_d)) for u, d in carriers]
+            return lax.ppermute(block, ("utt", "tm"), route)
+
+        small = jnp.stack([token_group(dec_queries, stretch_mask, g) for g in range(4)])
+        other = swap(small, n, 1)
+        both = jnp.stack(
+            [jnp.where(c == 0, small, other), jnp.where(c == 0, other, small)], axis=1
+        )
+        both = both.reshape(4, 2, 6, 2, HD).transpose(0, 2, 1, 3, 4).reshape(4, 24, HD)
+        both = jnp.pad(both, ((0, 0), (0, depth - 24), (0, 0)))
         payload = jnp.stack(
             [
-                jnp.concatenate(
-                    [
-                        weight_group(qkv_weight, g),
-                        jnp.pad(
-                            token_group(dec_queries, stretch_mask, g),
-                            ((0, 6), (0, 960 - 384 - stretch_mask.shape[1])),
-                        ),
-                    ],
-                    axis=0,
-                )
-                for g in range(4)
+                jnp.concatenate([weight_group(qkv_weight, g), both[g]], axis=1)
+                for g in (0, 2, 1, 3)
             ]
-        )
-        chosen = [
-            [
-                lax.dynamic_index_in_dim(payload, 2 * (p ^ a) + (x ^ b), 0, keepdims=False)
-                for b in range(2)
-            ]
+        ).reshape(2, 2, depth, 1024)
+        mine = lax.dynamic_index_in_dim(payload, x, 0, keepdims=False)
+        across = carry(lax.dynamic_index_in_dim(payload, 1 - x, 0, keepdims=False), 0, 2)
+        ready = [
+            jnp.concatenate(
+                [
+                    lax.dynamic_slice_in_dim(mine, p ^ a, 1, 0),
+                    lax.dynamic_slice_in_dim(across, p ^ a, 1, 0),
+                ]
+            ).reshape(2 * depth, 1024)
             for a in range(2)
         ]
-        parts = {}
-        for far_z in (3, 2, 1, 0):
-            for far_x in (1, 0):
-                mask = 4 * far_z + 2 * far_x
-                part = chosen[far_z % 2][far_x]
-                if mask:
-                    part = swap(part, n, mask)
-                parts[mask] = part
-                parts[mask + 1] = swap(part, n, 1)
-        order = [m for core in range(2) for m in range(core, n, 2)]
-        tokens = jnp.concatenate(
-            [parts[m][depth : depth + 2, : 384 + stretch_mask.shape[1]] for m in order], axis=0
-        )
-        part_places = [me ^ m for m in order]
-        weights = [parts[m] for m in order]
+        here = {0: ready[0]}
+        for turn in (3, 2, 1):
+            here[turn] = carry(ready[turn % 2], 0, 4 * turn)
+        weights, part_places, token_parts = [], [], []
+        own_part = lax.dynamic_index_in_dim(mine, p, 0, keepdims=False)
+        for turn in range(4):
+            traded = carry(here[turn], 1, 0)
+            got = jnp.where(straight == 1, here[turn], traded)
+            if turn == 0:
+                got = got.at[:depth].set(own_part)
+            beside = swap(got, n, 1)
+            for s in range(2):
+                chip = me ^ (4 * turn + 2 * s)
+                for part, source in ((got, chip), (beside, chip ^ 1)):
+                    part = part[s * depth : s * depth + depth]
+                    weights.append(part)
+                    part_places.append(source)
+                    token_parts.append(part)
+        token_parts[1] = token_parts[0]
     else:
         whole = lax.all_gather(qkv_weight, "tm", axis=0, tiled=True)
         grouped = jnp.stack([weight_group(whole, g) for g in range(4)])
         weights = [lax.dynamic_index_in_dim(grouped, group, 0, keepdims=False)]
+        weights = [jnp.pad(weights[0], ((0, 0), (0, HD)))]
         part_places = [jnp.int32(0)]
         depth = whole.shape[0]
         packed = jnp.stack([token_group(dec_queries, stretch_mask, g) for g in range(4)])
-        every = lax.all_gather(packed, "tm", axis=1, tiled=True)
-        every = lax.dynamic_index_in_dim(every, group, 0, keepdims=False)
+        every = lax.all_gather(packed, "tm", axis=0)
+        every = lax.dynamic_index_in_dim(every, group, 1, keepdims=False)
         order = jnp.array([m for core in range(2) for m in range(core, n, 2)], jnp.int32)
-        rows = 2 * (order ^ me)
-        tokens = jnp.take(every, jnp.stack([rows, rows + 1], axis=1).reshape(-1), axis=0)
-
-    table = jnp.stack([jnp.asarray(v, jnp.int32) for v in places + part_places + [halo_on, group]])
-    held = encoder(table, norm_gain.reshape(1, -1), blocks, weights, depth)
+        every = jnp.take(every, order ^ me, axis=0).reshape(n, 6, 2, HD)
+        token_parts = [every.transpose(1, 0, 2, 3).reshape(6, 2 * n, HD)]
+
+    table = scalars(places + part_places)
+    held = encoder(table, layered, weights, depth)
 
     pieces = []
     for turn in range(2):
@@ -400,8 +450,8 @@
         [pieces[0][0], pieces[1][0], pieces[0][1], pieces[1][1]], 2 * c + x
     )
 
-    place = jnp.stack([4 * quarter, me]).astype(jnp.int32)
-    partial = cross_partial(place, held, tokens)
+    place = scalars([4 * quarter, me, c, straight])
+    partial = cross_partial(place, held, token_parts, 2 * n, len(token_parts) > 1)
     bits = [1]
     step = n // 2
     while step >= 8:

time: 167 us -> 119 us (0.71)
  waiting for transfers between devices: 61.2 us -> 33.7 us
  local copies, waits for them, and re-layouts: 38.8 us -> 12.1 us
  starting transfers between devices: 35.8 us -> 41.4 us
    ppermute x36 -> x26, waiting for transfers between devices: 61.2 us -> 26.7 us  [send(): return lax.ppermute(block, 'tm', route)]
    ppermute x0 -> x8, starting transfers between devices: none -> 23.9 us  [carry(): return lax.ppermute(block, ('utt', 'tm'), route)]
    ppermute x36 -> x26, starting transfers between devices: 35.8 us -> 17.5 us  [send(): return lax.ppermute(block, 'tm', route)]
    unnamed x72 -> x42, local copies, waits for them, and re-layouts: 16.8 us -> 2.05 us
    slice x16 -> x9, local copies, waits for them, and re-layouts: 12.1 us -> 0.91 us  [the longest x1 0.73 us: token_group(): heads = [wide[:, HD * i:HD * i + HD] for i in range(4)] + [tail]]
    ppermute x0 -> x8, waiting for transfers between devices: none -> 7.01 us  [carry(): return lax.ppermute(block, ('utt', 'tm'), route)]
    concatenate x6 -> x8, local copies, waits for them, and re-layouts: 3.6 us -> 0.64 us  [the longest x4 0.41 us: on_device(): jnp.concatenate([weight_group(qkv_weight, g), both[g]], axis=1)]
    pallas_call x2 -> x5, Pallas kernels: 22.9 us -> 23.6 us  [the longest x1 14.9 us: encoder(): pl.pallas_call(functools.partial(encoder_kernel, len(parts), depth), out_...]
  transfers between devices with their start and end apart: 36 -> 34, of which waited for: 13 -> 10; matrix products, arithmetic and copies ran while one was open for 12% -> 6% of each run, Pallas kernels for 1% -> 5%
where the time goes in v2:
time: 119 us; the launch traced here: 118 us
  starting transfers between devices  41.4 us (35%)
  waiting for transfers between devices  33.7 us (28%)
  Pallas kernels  26.7 us (22%)
  local copies, waits for them, and re-layouts  12.1 us (10%)
  other arithmetic  2.68 us (2%)
  between operations  1.74 us (1%)
    ppermute x26, waiting for transfers between devices, send(): return lax.ppermute(block, 'tm', route)  26.7 us
    ppermute x8, starting transfers between devices, carry(): return lax.ppermute(block, ('utt', 'tm'), route)  23.9 us
    ppermute x26, starting transfers between devices, send(): return lax.ppermute(block, 'tm', route)  17.5 us
    pallas_call x1, Pallas kernels, encoder(): pl.pallas_call(functools.partial(encoder_kernel, len(parts), depth), out_...  14.9 us
    ppermute x8, waiting for transfers between devices, carry(): return lax.ppermute(block, ('utt', 'tm'), route)  7.01 us
    pallas_call x3, Pallas kernels, norm_layer(): pl.pallas_call(norm_kernel, out_shape=(jax.ShapeDtypeStruct((512, 1280),...  4.73 us
    pallas_call x1, Pallas kernels, cross_partial(): pl.pallas_call(functools.partial(cross_kernel, chips), out_shape=jax.Shap...  3.93 us
    pallas_call x2, Pallas kernels, merge(): pl.pallas_call(functools.partial(merge_kernel, last), out_shape=shape, in...  3.11 us
  transfers between devices with their start and end apart: 34, of which 10 were waited for; matrix products, arithmetic and copies ran while one was open for 6% of the time, Pallas kernels for 5%

profile of v2, /device:TPU:0, one launch (start us, length us, event | category | flops | bytes accessed | tf_op | source)
XLA Modules:
  0.0 118.3 jit_solution(7383740605016857227)
XLA Ops:
  0.6 0.9 fusion.22
  1.6 0.7 slice.371
  2.3 0.7 convert_element_type.23
  3.2 0.5 collective-permute-start.12
  3.7 1.0 fusion.13
  4.8 1.1 fusion.12
  6.1 0.1 concatenate.68
  6.2 0.1 concatenate.67
  6.4 0.1 concatenate.66
  6.5 0.1 concatenate.65
  6.7 4.4 %collective-permute-start.13 = (bf16[2,80,1024]{2,1,0:T(8,128)(2,1)S(1)}, bf16[2,80,1024]{2,1,0:T(8,128)(2,1)S(1)}, u32[]{:S(2)}, u32[]{:S(2)}) collective-permute-start(bf16[2,80,1024]{2,1,0:T(8,128)(2,1)S(1)} %dynamic-slice_bitcast_fusion), channel_id=1, source_target_pairs={{0,2},{2,0},{4,6},{6,4},{8,10},{10,8},{12,14},{14,12},{17,19},{19,... | collective-permute-start | bytes 983048 | tf_op jit(solution)/shard_map/ppermute | solution.py:373
  11.3 0.7 collective-permute-start.7
  12.0 1.3 %collective-permute-start.8 = (bf16[136,1280]{1,0:T(8,128)(2,1)S(1)}, bf16[136,1280]{1,0:T(8,128)(2,1)S(1)}, u32[]{:S(2)}, u32[]{:S(2)}) collective-permute-start(bf16[136,1280]{1,0:T(8,128)(2,1)S(1)} %pad_maximum_fusion.1.refs_0_), channel_id=1, source_target_pairs={{4,12},{5,13},{6,14},{7,15},{8,0},{9,1},{10,2},{11,3},{20,28},{21,... | collective-permute-start | bytes 1044488 | tf_op jit(solution)/shard_map/ppermute | solution.py:21
  13.7 0.7 pad_add_fusion.place
  14.4 4.8 %collective-permute-done.13 = bf16[2,80,1024]{2,1,0:T(8,128)(2,1)S(1)} collective-permute-done((bf16[2,80,1024]{2,1,0:T(8,128)(2,1)S(1)}, bf16[2,80,1024]{2,1,0:T(8,128)(2,1)S(1)}, u32[]{:S(2)}, u32[]{:S(2)}) %collective-permute-start.13) | collective-permute-done | bytes 327712 | tf_op jit(solution)/shard_map/ppermute | solution.py:373
  19.3 1.3 %collective-permute-start.14 = (bf16[160,1024]{1,0:T(8,128)(2,1)S(1)}, bf16[160,1024]{1,0:T(8,128)(2,1)S(1)}, u32[]{:S(2)}, u32[]{:S(2)}) collective-permute-start(bf16[160,1024]{1,0:T(8,128)(2,1)S(1)} %bitcast.69), channel_id=1, source_target_pairs={{0,16},{2,18},{4,20},{6,22},{8,24},{10,26},{12,28},{14,30},{17,1},... | collective-permute-start | bytes 983048 | tf_op jit(solution)/shard_map/ppermute | solution.py:373
  20.7 8.6 %collective-permute-start.19 = (bf16[160,1024]{1,0:T(8,128)(2,1)S(1)}, bf16[160,1024]{1,0:T(8,128)(2,1)S(1)}, u32[]{:S(2)}, u32[]{:S(2)}) collective-permute-start(bf16[160,1024]{1,0:T(8,128)(2,1)S(1)} %bitcast.70), channel_id=1, source_target_pairs={{0,8},{2,10},{4,12},{6,14},{8,0},{10,2},{12,4},{14,6},{17,25},{19,... | collective-permute-start | bytes 983048 | tf_op jit(solution)/shard_map/ppermute | solution.py:373
  29.2 6.8 %collective-permute-done.8 = bf16[136,1280]{1,0:T(8,128)(2,1)S(1)} collective-permute-done((bf16[136,1280]{1,0:T(8,128)(2,1)S(1)}, bf16[136,1280]{1,0:T(8,128)(2,1)S(1)}, u32[]{:S(2)}, u32[]{:S(2)}) %collective-permute-start.8) | collective-permute-done | bytes 348192 | tf_op jit(solution)/shard_map/ppermute | solution.py:21
  36.0 1.9 %collective-permute-start.16 = (bf16[160,1024]{1,0:T(8,128)(2,1)S(1)}, bf16[160,1024]{1,0:T(8,128)(2,1)S(1)}, u32[]{:S(2)}, u32[]{:S(2)}) collective-permute-start(bf16[160,1024]{1,0:T(8,128)(2,1)S(1)} %bitcast.75), channel_id=1, source_target_pairs={{0,4},{2,6},{4,0},{6,2},{8,12},{10,14},{12,8},{14,10},{17,21},{19,... | collective-permute-start | bytes 983048 | tf_op jit(solution)/shard_map/ppermute | solution.py:373
  38.0 2.1 %collective-permute-start.3 = (bf16[136,1280]{1,0:T(8,128)(2,1)S(1)}, bf16[136,1280]{1,0:T(8,128)(2,1)S(1)}, u32[]{:S(2)}, u32[]{:S(2)}) collective-permute-start(bf16[136,1280]{1,0:T(8,128)(2,1)S(1)} %pad_maximum_fusion.1.refs_0_), channel_id=1, source_target_pairs={{0,4},{1,5},{2,6},{3,7},{4,0},{5,1},{6,2},{7,3},{8,12},{9,13},{10,... | collective-permute-start | bytes 1044488 | tf_op jit(solution)/shard_map/ppermute | solution.py:21
  40.1 3.8 %collective-permute-start.22 = (bf16[160,1024]{1,0:T(8,128)(2,1)S(1)}, bf16[160,1024]{1,0:T(8,128)(2,1)S(1)}, u32[]{:S(2)}, u32[]{:S(2)}) collective-permute-start(bf16[160,1024]{1,0:T(8,128)(2,1)S(1)} %bitcast.76), channel_id=1, source_target_pairs={{0,12},{2,14},{4,8},{6,10},{8,4},{10,6},{12,0},{14,2},{17,29},{19,... | collective-permute-start | bytes 983048 | tf_op jit(solution)/shard_map/ppermute | solution.py:373
  44.0 2.2 %collective-permute-done.16 = bf16[160,1024]{1,0:T(8,128)(2,1)S(1)} collective-permute-done((bf16[160,1024]{1,0:T(8,128)(2,1)S(1)}, bf16[160,1024]{1,0:T(8,128)(2,1)S(1)}, u32[]{:S(2)}, u32[]{:S(2)}) %collective-permute-start.16) | collective-permute-done | bytes 327712 | tf_op jit(solution)/shard_map/ppermute | solution.py:373
  46.2 1.3 %collective-permute-start.17 = (bf16[160,1024]{1,0:T(8,128)(2,1)S(1)}, bf16[160,1024]{1,0:T(8,128)(2,1)S(1)}, u32[]{:S(2)}, u32[]{:S(2)}) collective-permute-start(bf16[160,1024]{1,0:T(8,128)(2,1)S(1)} %collective-permute-done.16), channel_id=1, source_target_pairs={{0,16},{2,18},{4,20},{6,22},{8,24},{10,26},{12,28},{14,30},{17,1},... | collective-permute-start | bytes 983048 | tf_op jit(solution)/shard_map/ppermute | solution.py:373
  47.6 1.3 %collective-permute-start.20 = (bf16[160,1024]{1,0:T(8,128)(2,1)S(1)}, bf16[160,1024]{1,0:T(8,128)(2,1)S(1)}, u32[]{:S(2)}, u32[]{:S(2)}) collective-permute-start(bf16[160,1024]{1,0:T(8,128)(2,1)S(1)} %collective-permute-done.19), channel_id=1, source_target_pairs={{0,16},{2,18},{4,20},{6,22},{8,24},{10,26},{12,28},{14,30},{17,1},... | collective-permute-start | bytes 983048 | tf_op jit(solution)/shard_map/ppermute | solution.py:373
  49.0 1.6 %shard_map.77 = (bf16[512,1280]{1,0:T(8,128)(2,1)S(1)}, f32[8,512]{1,0:T(8,128)S(1)}, bf16[512,320]{1,0:T(8,128)(2,1)S(1)}) custom-call(s32[6]{0:T(128)S(1)} %stack.175.places, f32[1,1280]{1,0:T(1,128)S(1)} %reshape.102.gain, bf16[136,1280]{1,0:T(8,128)(2,1)S(1)} %pad_maximum_fusion.1.refs_0_, bf16[136,1280]{1,0:T(8,128)(2,1)S(1)} %collective-permute-done.refs_1_, ...), custom_call_target="tpu_custom_call" | custom-call | tf_op jit(solution)/shard_map/pallas_call | solution.py:73
  50.6 2.8 %collective-permute-done.3.refs_0_ = bf16[136,1280]{1,0:T(8,128)(2,1)S(1)} collective-permute-done((bf16[136,1280]{1,0:T(8,128)(2,1)S(1)}, bf16[136,1280]{1,0:T(8,128)(2,1)S(1)}, u32[]{:S(2)}, u32[]{:S(2)}) %collective-permute-start.3) | collective-permute-done | bytes 348192 | tf_op jit(solution)/shard_map/ppermute | solution.py:21
  53.4 1.5 %collective-permute-start.10 = (bf16[136,1280]{1,0:T(8,128)(2,1)S(1)}, bf16[136,1280]{1,0:T(8,128)(2,1)S(1)}, u32[]{:S(2)}, u32[]{:S(2)}) collective-permute-start(bf16[136,1280]{1,0:T(8,128)(2,1)S(1)} %broadcast_select_fusion.refs_0_), channel_id=1, source_target_pairs={{0,2},{1,3},{2,0},{3,1},{4,6},{5,7},{6,4},{7,5},{8,10},{9,11},{10,... | collective-permute-start | bytes 1044488 | tf_op jit(solution)/shard_map/ppermute | solution.py:21
  54.9 0.5 collective-permute-start.5
  55.4 1.3 %collective-permute-start.23 = (bf16[160,1024]{1,0:T(8,128)(2,1)S(1)}, bf16[160,1024]{1,0:T(8,128)(2,1)S(1)}, u32[]{:S(2)}, u32[]{:S(2)}) collective-permute-start(bf16[160,1024]{1,0:T(8,128)(2,1)S(1)} %collective-permute-done.22), channel_id=1, source_target_pairs={{0,16},{2,18},{4,20},{6,22},{8,24},{10,26},{12,28},{14,30},{17,1},... | collective-permute-start | bytes 983048 | tf_op jit(solution)/shard_map/ppermute | solution.py:373
  56.9 11.8 %collective-permute-done.5.refs_2_ = bf16[136,1280]{1,0:T(8,128)(2,1)S(1)} collective-permute-done((bf16[136,1280]{1,0:T(8,128)(2,1)S(1)}, bf16[136,1280]{1,0:T(8,128)(2,1)S(1)}, u32[]{:S(2)}, u32[]{:S(2)}) %collective-permute-start.5) | collective-permute-done | bytes 348192 | tf_op jit(solution)/shard_map/ppermute | solution.py:21
  68.7 0.5 collective-permute-start.6
  69.5 0.5 collective-permute-start.18
  70.0 0.3 collective-permute-done.15
  70.3 0.1 collective-permute-start.21
  70.5 0.3 collective-permute-done.6.refs_3_
  70.8 0.1 collective-permute-start.24
  71.0 1.6 %shard_map.78 = (bf16[512,1280]{1,0:T(8,128)(2,1)S(1)}, f32[8,512]{1,0:T(8,128)S(1)}, bf16[512,320]{1,0:T(8,128)(2,1)S(1)}) custom-call(s32[6]{0:T(128)S(1)} %stack.175.places, f32[1,1280]{1,0:T(1,128)S(1)} %reshape.102.gain, bf16[136,1280]{1,0:T(8,128)(2,1)S(1)} %collective-permute-done.3.refs_0_, bf16[136,1280]{1,0:T(8,128)(2,1)S(1)} %collective-permute-done.4.refs_1_, ...), custom_call_target="tpu_custom_call" | custom-call | tf_op jit(solution)/shard_map/pallas_call | solution.py:73
  72.6 1.6 %shard_map.79 = (bf16[512,1280]{1,0:T(8,128)(2,1)S(1)}, f32[8,512]{1,0:T(8,128)S(1)}, bf16[512,320]{1,0:T(8,128)(2,1)S(1)}) custom-call(s32[6]{0:T(128)S(1)} %stack.178.places, f32[1,1280]{1,0:T(1,128)S(1)} %reshape.102.gain, bf16[136,1280]{1,0:T(8,128)(2,1)S(1)} %broadcast_select_fusion.refs_0_, bf16[136,1280]{1,0:T(8,128)(2,1)S(1)} %collective-permute-done.9.refs_1_, ...), custom_call_target="tpu_custom_call" | custom-call | tf_op jit(solution)/shard_map/pallas_call | solution.py:73
  74.4 14.9 %shard_map.80.memory = bf16[512,320]{1,0:T(8,128)(2,1)S(1)} custom-call(s32[19]{0:T(128)S(1)} %stack.169.places, bf16[512,1280]{1,0:T(8,128)(2,1)S(1)} %get-tuple-element.35.refs_0_, f32[8,512]{1,0:T(8,128)S(1)} %get-tuple-element.36.refs_1_, bf16[512,320]{1,0:T(8,128)(2,1)S(1)} %get-tuple-element.37.refs_2_, ...), custom_call_target="tpu_custom_call" | custom-call | tf_op jit(solution)/shard_map/pallas_call | solution.py:166
  89.4 0.8 copy-done
  90.2 3.9 %shard_map.81.mine = f32[32,512]{1,0:T(8,128)} custom-call(s32[4]{0:T(128)} %pad_add_fusion.place, bf16[512,320]{1,0:T(8,128)(2,1)} %copy-done, bf16[80,1024]{1,0:T(8,128)(2,1)} %copy-done.1, bf16[80,1024]{1,0:T(8,128)(2,1)} %copy-done.1, bf16[80,1024]{1,0:T(8,128)(2,1)} %copy-done.15, bf16[80,1024]{1,0:T(8,128)(2,1)} %copy-done.8, ...), custom_call_target="tpu_custom_call" | custom-call | tf_op jit(solution)/shard_map/pallas_call | solution.py:248
  94.1 0.8 slice.456
  94.9 0.4 collective-permute-start.29
  95.2 0.9 collective-permute-done.29.theirs
  96.1 0.6 copy-done.17
  96.7 1.6 %shard_map.82.mine = f32[16,512]{1,0:T(8,128)} custom-call(f32[32,512]{1,0:T(8,128)} %shard_map.81.mine, f32[16,512]{1,0:T(8,128)} %copy-done.17), custom_call_target="tpu_custom_call" | custom-call | tf_op jit(solution)/shard_map/pallas_call | solution.py:288
  98.3 0.7 slice.457
  99.0 0.4 collective-permute-start.30
  99.5 1.1 constant_dynamic-slice_fusion.2
  100.6 0.7 collective-permute-start.25
  101.2 1.6 %collective-permute-start.26 = (bf16[256,320]{1,0:T(8,128)(2,1)S(1)}, bf16[256,320]{1,0:T(8,128)(2,1)S(1)}, u32[]{:S(2)}, u32[]{:S(2)}) collective-permute-start(bf16[256,320]{1,0:T(8,128)(2,1)S(1)} %get-tuple-element.76), channel_id=1, source_target_pairs={{0,2},{1,6},{2,0},{3,4},{4,3},{5,7},{6,1},{7,5},{8,10},{9,14},{10,... | collective-permute-start | bytes 491528 | tf_op jit(solution)/shard_map/ppermute | solution.py:21
  102.8 0.9 collective-permute-done.30.theirs
  103.7 0.6 copy-done.18
  104.3 1.5 %shard_map.83 = bf16[8,384]{1,0:T(8,128)(2,1)} custom-call(f32[16,512]{1,0:T(8,128)} %shard_map.82.mine, f32[8,512]{1,0:T(8,128)} %copy-done.18), custom_call_target="tpu_custom_call" | custom-call | tf_op jit(solution)/shard_map/pallas_call | solution.py:288
  105.8 0.8 fusion.21
  106.6 1.6 %collective-permute-start.31 = (bf16[2,384]{1,0:T(2,128)(2,1)S(1)}, bf16[2,384]{1,0:T(2,128)(2,1)S(1)}, u32[]{:S(2)}, u32[]{:S(2)}) collective-permute-start(bf16[2,384]{1,0:T(2,128)(2,1)S(1)} %get-tuple-element.106), channel_id=1, source_target_pairs={{0,2},{1,3},{2,0},{3,1},{4,6},{5,7},{6,4},{7,5},{8,10},{9,11},{10,... | collective-permute-start | bytes 4616 | tf_op jit(solution)/shard_map/ppermute | solution.py:21
  108.2 3.1 %collective-permute-start.32 = (bf16[2,384]{1,0:T(2,128)(2,1)S(1)}, bf16[2,384]{1,0:T(2,128)(2,1)S(1)}, u32[]{:S(2)}, u32[]{:S(2)}) collective-permute-start(bf16[2,384]{1,0:T(2,128)(2,1)S(1)} %get-tuple-element.105), channel_id=1, source_target_pairs={{0,4},{1,5},{2,6},{3,7},{4,0},{5,1},{6,2},{7,3},{8,12},{9,13},{10,... | collective-permute-start | bytes 4616 | tf_op jit(solution)/shard_map/ppermute | solution.py:21
  111.2 0.9 collective-permute-start.33
  112.3 0.5 collective-permute-start.28
  112.8 2.9 %collective-permute-done.33 = bf16[2,384]{1,0:T(2,128)(2,1)S(1)} collective-permute-done((bf16[2,384]{1,0:T(2,128)(2,1)S(1)}, bf16[2,384]{1,0:T(2,128)(2,1)S(1)}, u32[]{:S(2)}, u32[]{:S(2)}) %collective-permute-start.33) | collective-permute-done | bytes 1568 | tf_op jit(solution)/shard_map/ppermute | solution.py:21
  115.7 0.7 broadcast_select_fusion.9
  116.5 0.7 concatenate.72
  117.2 0.1 select_select_fusion
  117.4 0.8 concatenate.71
  (128 shorter events, 2.1 us)
Async XLA Ops:
  0.6 5.3 %copy-start.20 = (s32[128]{0:T(128)S(1)}, s32[128]{0:T(128)}, u32[]{:S(2)}) copy-start(s32[128]{0:T(128)} %param.13) | copy-start | bytes 1540
  3.2 2.8 %collective-permute-start.12 = (bf16[4,12,64]{2,1,0:T(8,128)(2,1)S(1)}, bf16[4,12,64]{2,1,0:T(8,128)(2,1)S(1)}, u32[]{:S(2)}, u32[]{:S(2)}) collective-permute-start(bf16[4,12,64]{2,1,0:T(8,128)(2,1)S(1)} %pad_maximum_fusion.4), channel_id=1, source_target_pairs={{0,1},{1,0},{2,3},{3,2},{4,5},{5,4},{6,7},{7,6},{8,9},{9,8},{10,11... | collective-permute-start | bytes 18440 | tf_op jit(solution)/shard_map/ppermute | solution.py:21
  6.3 4.8 %copy-start.16 = (bf16[128,1280]{1,0:T(8,128)(2,1)S(1)}, bf16[128,1280]{1,0:T(8,128)(2,1)}, u32[]{:S(2)}) copy-start(bf16[128,1280]{1,0:T(8,128)(2,1)} %param.10) | copy-start | bytes 983044
  6.6 6.9 %copy-start.19 = (f32[1280]{0:T(1024)S(1)}, f32[1280]{0:T(1024)}, u32[]{:S(2)}) copy-start(f32[1280]{0:T(1024)} %param.11) | copy-start | bytes 15364
  6.7 12.5 %collective-permute-start.13 = (bf16[2,80,1024]{2,1,0:T(8,128)(2,1)S(1)}, bf16[2,80,1024]{2,1,0:T(8,128)(2,1)S(1)}, u32[]{:S(2)}, u32[]{:S(2)}) collective-permute-start(bf16[2,80,1024]{2,1,0:T(8,128)(2,1)S(1)} %dynamic-slice_bitcast_fusion), channel_id=1, source_target_pairs={{0,2},{2,0},{4,6},{6,4},{8,10},{10,8},{12,14},{14,12},{17,19},{19,... | collective-permute-start | bytes 983048 | tf_op jit(solution)/shard_map/ppermute | solution.py:373
  11.2 26.8 %collective-permute-start = (bf16[136,1280]{1,0:T(8,128)(2,1)S(1)}, bf16[136,1280]{1,0:T(8,128)(2,1)S(1)}, u32[]{:S(2)}, u32[]{:S(2)}) collective-permute-start(bf16[136,1280]{1,0:T(8,128)(2,1)S(1)} %pad_maximum_fusion.1.refs_0_), channel_id=1, source_target_pairs={{0,1},{1,0},{2,3},{3,2},{4,5},{5,4},{6,7},{7,6},{8,9},{9,8},{10,11... | collective-permute-start | bytes 1044488 | tf_op jit(solution)/shard_map/ppermute | solution.py:21
  11.3 28.9 %collective-permute-start.1 = (bf16[136,1280]{1,0:T(8,128)(2,1)S(1)}, bf16[136,1280]{1,0:T(8,128)(2,1)S(1)}, u32[]{:S(2)}, u32[]{:S(2)}) collective-permute-start(bf16[136,1280]{1,0:T(8,128)(2,1)S(1)} %pad_maximum_fusion.1.refs_0_), channel_id=1, source_target_pairs={{0,2},{1,3},{2,0},{3,1},{4,6},{5,7},{6,4},{7,5},{8,10},{9,11},{10,... | collective-permute-start | bytes 1044488 | tf_op jit(solution)/shard_map/ppermute | solution.py:21
  11.3 9.3 %collective-permute-start.7 = (bf16[136,1280]{1,0:T(8,128)(2,1)S(1)}, bf16[136,1280]{1,0:T(8,128)(2,1)S(1)}, u32[]{:S(2)}, u32[]{:S(2)}) collective-permute-start(bf16[136,1280]{1,0:T(8,128)(2,1)S(1)} %pad_maximum_fusion.1.refs_0_), channel_id=1, source_target_pairs={{4,8},{5,9},{6,10},{7,11},{8,4},{9,5},{10,6},{11,7},{20,24},{21,25... | collective-permute-start | bytes 1044488 | tf_op jit(solution)/shard_map/ppermute | solution.py:21
  12.0 24.0 %collective-permute-start.8 = (bf16[136,1280]{1,0:T(8,128)(2,1)S(1)}, bf16[136,1280]{1,0:T(8,128)(2,1)S(1)}, u32[]{:S(2)}, u32[]{:S(2)}) collective-permute-start(bf16[136,1280]{1,0:T(8,128)(2,1)S(1)} %pad_maximum_fusion.1.refs_0_), channel_id=1, source_target_pairs={{4,12},{5,13},{6,14},{7,15},{8,0},{9,1},{10,2},{11,3},{20,28},{21,... | collective-permute-start | bytes 1044488 | tf_op jit(solution)/shard_map/ppermute | solution.py:21
  19.3 24.6 %collective-permute-start.14 = (bf16[160,1024]{1,0:T(8,128)(2,1)S(1)}, bf16[160,1024]{1,0:T(8,128)(2,1)S(1)}, u32[]{:S(2)}, u32[]{:S(2)}) collective-permute-start(bf16[160,1024]{1,0:T(8,128)(2,1)S(1)} %bitcast.69), channel_id=1, source_target_pairs={{0,16},{2,18},{4,20},{6,22},{8,24},{10,26},{12,28},{14,30},{17,1},... | collective-permute-start | bytes 983048 | tf_op jit(solution)/shard_map/ppermute | solution.py:373
  20.7 26.9 %collective-permute-start.19 = (bf16[160,1024]{1,0:T(8,128)(2,1)S(1)}, bf16[160,1024]{1,0:T(8,128)(2,1)S(1)}, u32[]{:S(2)}, u32[]{:S(2)}) collective-permute-start(bf16[160,1024]{1,0:T(8,128)(2,1)S(1)} %bitcast.70), channel_id=1, source_target_pairs={{0,8},{2,10},{4,12},{6,14},{8,0},{10,2},{12,4},{14,6},{17,25},{19,... | collective-permute-start | bytes 983048 | tf_op jit(solution)/shard_map/ppermute | solution.py:373
  36.0 10.1 %collective-permute-start.16 = (bf16[160,1024]{1,0:T(8,128)(2,1)S(1)}, bf16[160,1024]{1,0:T(8,128)(2,1)S(1)}, u32[]{:S(2)}, u32[]{:S(2)}) collective-permute-start(bf16[160,1024]{1,0:T(8,128)(2,1)S(1)} %bitcast.75), channel_id=1, source_target_pairs={{0,4},{2,6},{4,0},{6,2},{8,12},{10,14},{12,8},{14,10},{17,21},{19,... | collective-permute-start | bytes 983048 | tf_op jit(solution)/shard_map/ppermute | solution.py:373
  38.0 15.4 %collective-permute-start.3 = (bf16[136,1280]{1,0:T(8,128)(2,1)S(1)}, bf16[136,1280]{1,0:T(8,128)(2,1)S(1)}, u32[]{:S(2)}, u32[]{:S(2)}) collective-permute-start(bf16[136,1280]{1,0:T(8,128)(2,1)S(1)} %pad_maximum_fusion.1.refs_0_), channel_id=1, source_target_pairs={{0,4},{1,5},{2,6},{3,7},{4,0},{5,1},{6,2},{7,3},{8,12},{9,13},{10,... | collective-permute-start | bytes 1044488 | tf_op jit(solution)/shard_map/ppermute | solution.py:21
  40.1 14.8 %collective-permute-start.22 = (bf16[160,1024]{1,0:T(8,128)(2,1)S(1)}, bf16[160,1024]{1,0:T(8,128)(2,1)S(1)}, u32[]{:S(2)}, u32[]{:S(2)}) collective-permute-start(bf16[160,1024]{1,0:T(8,128)(2,1)S(1)} %bitcast.76), channel_id=1, source_target_pairs={{0,12},{2,14},{4,8},{6,10},{8,4},{10,6},{12,0},{14,2},{17,29},{19,... | collective-permute-start | bytes 983048 | tf_op jit(solution)/shard_map/ppermute | solution.py:373
  43.9 5.1 %collective-permute-start.2 = (bf16[136,1280]{1,0:T(8,128)(2,1)S(1)}, bf16[136,1280]{1,0:T(8,128)(2,1)S(1)}, u32[]{:S(2)}, u32[]{:S(2)}) collective-permute-start(bf16[136,1280]{1,0:T(8,128)(2,1)S(1)} %collective-permute-done.1.refs_2_), channel_id=1, source_target_pairs={{0,1},{1,0},{2,3},{3,2},{4,5},{5,4},{6,7},{7,6},{8,9},{9,8},{10,11... | collective-permute-start | bytes 1044488 | tf_op jit(solution)/shard_map/ppermute | solution.py:21
  46.2 9.3 %collective-permute-start.17 = (bf16[160,1024]{1,0:T(8,128)(2,1)S(1)}, bf16[160,1024]{1,0:T(8,128)(2,1)S(1)}, u32[]{:S(2)}, u32[]{:S(2)}) collective-permute-start(bf16[160,1024]{1,0:T(8,128)(2,1)S(1)} %collective-permute-done.16), channel_id=1, source_target_pairs={{0,16},{2,18},{4,20},{6,22},{8,24},{10,26},{12,28},{14,30},{17,1},... | collective-permute-start | bytes 983048 | tf_op jit(solution)/shard_map/ppermute | solution.py:373
  47.6 9.2 %collective-permute-start.20 = (bf16[160,1024]{1,0:T(8,128)(2,1)S(1)}, bf16[160,1024]{1,0:T(8,128)(2,1)S(1)}, u32[]{:S(2)}, u32[]{:S(2)}) collective-permute-start(bf16[160,1024]{1,0:T(8,128)(2,1)S(1)} %collective-permute-done.19), channel_id=1, source_target_pairs={{0,16},{2,18},{4,20},{6,22},{8,24},{10,26},{12,28},{14,30},{17,1},... | collective-permute-start | bytes 983048 | tf_op jit(solution)/shard_map/ppermute | solution.py:373
  48.9 25.4 %copy-start.1 = (bf16[80,1024]{1,0:T(8,128)(2,1)}, bf16[80,1024]{1,0:T(8,128)(2,1)S(1)}, u32[]{:S(2)}) copy-start(bf16[80,1024]{1,0:T(8,128)(2,1)S(1)} %get-tuple-element.45.refs_9_.refs_0_.refs_1_) | copy-start | bytes 491524
  48.9 25.4 %copy-start.15 = (bf16[80,1024]{1,0:T(8,128)(2,1)}, bf16[80,1024]{1,0:T(8,128)(2,1)S(1)}, u32[]{:S(2)}) copy-start(bf16[80,1024]{1,0:T(8,128)(2,1)S(1)} %slice.434.refs_11_.refs_2_) | copy-start | bytes 491524
  49.0 23.6 %collective-permute-start.9 = (bf16[136,1280]{1,0:T(8,128)(2,1)S(1)}, bf16[136,1280]{1,0:T(8,128)(2,1)S(1)}, u32[]{:S(2)}, u32[]{:S(2)}) collective-permute-start(bf16[136,1280]{1,0:T(8,128)(2,1)S(1)} %broadcast_select_fusion.refs_0_), channel_id=1, source_target_pairs={{0,1},{1,0},{2,3},{3,2},{4,5},{5,4},{6,7},{7,6},{8,9},{9,8},{10,11... | collective-permute-start | bytes 1044488 | tf_op jit(solution)/shard_map/ppermute | solution.py:21
  53.4 15.3 %collective-permute-start.10 = (bf16[136,1280]{1,0:T(8,128)(2,1)S(1)}, bf16[136,1280]{1,0:T(8,128)(2,1)S(1)}, u32[]{:S(2)}, u32[]{:S(2)}) collective-permute-start(bf16[136,1280]{1,0:T(8,128)(2,1)S(1)} %broadcast_select_fusion.refs_0_), channel_id=1, source_target_pairs={{0,2},{1,3},{2,0},{3,1},{4,6},{5,7},{6,4},{7,5},{8,10},{9,11},{10,... | collective-permute-start | bytes 1044488 | tf_op jit(solution)/shard_map/ppermute | solution.py:21
  54.9 13.8 %collective-permute-start.5 = (bf16[136,1280]{1,0:T(8,128)(2,1)S(1)}, bf16[136,1280]{1,0:T(8,128)(2,1)S(1)}, u32[]{:S(2)}, u32[]{:S(2)}) collective-permute-start(bf16[136,1280]{1,0:T(8,128)(2,1)S(1)} %collective-permute-done.3.refs_0_), channel_id=1, source_target_pairs={{0,2},{1,3},{2,0},{3,1},{4,6},{5,7},{6,4},{7,5},{8,10},{9,11},{10,... | collective-permute-start | bytes 1044488 | tf_op jit(solution)/shard_map/ppermute | solution.py:21
  55.4 13.8 %collective-permute-start.23 = (bf16[160,1024]{1,0:T(8,128)(2,1)S(1)}, bf16[160,1024]{1,0:T(8,128)(2,1)S(1)}, u32[]{:S(2)}, u32[]{:S(2)}) collective-permute-start(bf16[160,1024]{1,0:T(8,128)(2,1)S(1)} %collective-permute-done.22), channel_id=1, source_target_pairs={{0,16},{2,18},{4,20},{6,22},{8,24},{10,26},{12,28},{14,30},{17,1},... | collective-permute-start | bytes 983048 | tf_op jit(solution)/shard_map/ppermute | solution.py:373
  56.8 12.6 %collective-permute-start.4 = (bf16[136,1280]{1,0:T(8,128)(2,1)S(1)}, bf16[136,1280]{1,0:T(8,128)(2,1)S(1)}, u32[]{:S(2)}, u32[]{:S(2)}) collective-permute-start(bf16[136,1280]{1,0:T(8,128)(2,1)S(1)} %collective-permute-done.3.refs_0_), channel_id=1, source_target_pairs={{0,1},{1,0},{2,3},{3,2},{4,5},{5,4},{6,7},{7,6},{8,9},{9,8},{10,11... | collective-permute-start | bytes 1044488 | tf_op jit(solution)/shard_map/ppermute | solution.py:21
  68.7 1.6 %collective-permute-start.15 = (bf16[160,1024]{1,0:T(8,128)(2,1)S(1)}, bf16[160,1024]{1,0:T(8,128)(2,1)S(1)}, u32[]{:S(2)}, u32[]{:S(2)}) collective-permute-start(bf16[160,1024]{1,0:T(8,128)(2,1)S(1)} %get-tuple-element.44), channel_id=1, source_target_pairs={{0,1},{1,0},{2,3},{3,2},{4,5},{5,4},{6,7},{7,6},{8,9},{9,8},{10,11... | collective-permute-start | bytes 983048 | tf_op jit(solution)/shard_map/ppermute | solution.py:21
  68.7 2.1 %collective-permute-start.6 = (bf16[136,1280]{1,0:T(8,128)(2,1)S(1)}, bf16[136,1280]{1,0:T(8,128)(2,1)S(1)}, u32[]{:S(2)}, u32[]{:S(2)}) collective-permute-start(bf16[136,1280]{1,0:T(8,128)(2,1)S(1)} %collective-permute-done.5.refs_2_), channel_id=1, source_target_pairs={{0,1},{1,0},{2,3},{3,2},{4,5},{5,4},{6,7},{7,6},{8,9},{9,8},{10,11... | collective-permute-start | bytes 1044488 | tf_op jit(solution)/shard_map/ppermute | solution.py:21
  69.2 3.3 %collective-permute-start.11 = (bf16[136,1280]{1,0:T(8,128)(2,1)S(1)}, bf16[136,1280]{1,0:T(8,128)(2,1)S(1)}, u32[]{:S(2)}, u32[]{:S(2)}) collective-permute-start(bf16[136,1280]{1,0:T(8,128)(2,1)S(1)} %collective-permute-done.10.refs_2_), channel_id=1, source_target_pairs={{0,1},{1,0},{2,3},{3,2},{4,5},{5,4},{6,7},{7,6},{8,9},{9,8},{10,11... | collective-permute-start | bytes 1044488 | tf_op jit(solution)/shard_map/ppermute | solution.py:21
  69.4 5.0 %copy-start.2 = (bf16[80,1024]{1,0:T(8,128)(2,1)}, bf16[80,1024]{1,0:T(8,128)(2,1)S(1)}, u32[]{:S(2)}) copy-start(bf16[80,1024]{1,0:T(8,128)(2,1)S(1)} %get-tuple-element.88.refs_15_.refs_6_) | copy-start | bytes 491524
  69.4 5.0 %copy-start.3 = (bf16[80,1024]{1,0:T(8,128)(2,1)}, bf16[80,1024]{1,0:T(8,128)(2,1)S(1)}, u32[]{:S(2)}) copy-start(bf16[80,1024]{1,0:T(8,128)(2,1)S(1)} %get-tuple-element.89.refs_13_.refs_4_) | copy-start | bytes 491524
  69.4 5.0 %copy-start.4 = (bf16[80,1024]{1,0:T(8,128)(2,1)}, bf16[80,1024]{1,0:T(8,128)(2,1)S(1)}, u32[]{:S(2)}) copy-start(bf16[80,1024]{1,0:T(8,128)(2,1)S(1)} %get-tuple-element.84.refs_19_.refs_10_) | copy-start | bytes 491524
  69.4 5.0 %copy-start.5 = (bf16[80,1024]{1,0:T(8,128)(2,1)}, bf16[80,1024]{1,0:T(8,128)(2,1)S(1)}, u32[]{:S(2)}) copy-start(bf16[80,1024]{1,0:T(8,128)(2,1)S(1)} %get-tuple-element.85.refs_17_.refs_8_) | copy-start | bytes 491524
  69.5 4.7 %collective-permute-start.18 = (bf16[160,1024]{1,0:T(8,128)(2,1)S(1)}, bf16[160,1024]{1,0:T(8,128)(2,1)S(1)}, u32[]{:S(2)}, u32[]{:S(2)}) collective-permute-start(bf16[160,1024]{1,0:T(8,128)(2,1)S(1)} %broadcast_select_fusion.3), channel_id=1, source_target_pairs={{0,1},{1,0},{2,3},{3,2},{4,5},{5,4},{6,7},{7,6},{8,9},{9,8},{10,11... | collective-permute-start | bytes 983048 | tf_op jit(solution)/shard_map/ppermute | solution.py:21
  70.0 4.4 %copy-start.6 = (bf16[80,1024]{1,0:T(8,128)(2,1)}, bf16[80,1024]{1,0:T(8,128)(2,1)S(1)}, u32[]{:S(2)}) copy-start(bf16[80,1024]{1,0:T(8,128)(2,1)S(1)} %get-tuple-element.80.refs_23_.refs_14_) | copy-start | bytes 491524
  70.0 4.4 %copy-start.7 = (bf16[80,1024]{1,0:T(8,128)(2,1)}, bf16[80,1024]{1,0:T(8,128)(2,1)S(1)}, u32[]{:S(2)}) copy-start(bf16[80,1024]{1,0:T(8,128)(2,1)S(1)} %get-tuple-element.81.refs_21_.refs_12_) | copy-start | bytes 491524
  70.3 3.9 %collective-permute-start.21 = (bf16[160,1024]{1,0:T(8,128)(2,1)S(1)}, bf16[160,1024]{1,0:T(8,128)(2,1)S(1)}, u32[]{:S(2)}, u32[]{:S(2)}) collective-permute-start(bf16[160,1024]{1,0:T(8,128)(2,1)S(1)} %broadcast_select_fusion.2), channel_id=1, source_target_pairs={{0,1},{1,0},{2,3},{3,2},{4,5},{5,4},{6,7},{7,6},{8,9},{9,8},{10,11... | collective-permute-start | bytes 983048 | tf_op jit(solution)/shard_map/ppermute | solution.py:21
  70.5 3.9 %copy-start.8 = (bf16[80,1024]{1,0:T(8,128)(2,1)}, bf16[80,1024]{1,0:T(8,128)(2,1)S(1)}, u32[]{:S(2)}) copy-start(bf16[80,1024]{1,0:T(8,128)(2,1)S(1)} %get-tuple-element.92.refs_12_.refs_3_) | copy-start | bytes 491524
  70.8 3.5 %collective-permute-start.24 = (bf16[160,1024]{1,0:T(8,128)(2,1)S(1)}, bf16[160,1024]{1,0:T(8,128)(2,1)S(1)}, u32[]{:S(2)}, u32[]{:S(2)}) collective-permute-start(bf16[160,1024]{1,0:T(8,128)(2,1)S(1)} %broadcast_select_fusion.1), channel_id=1, source_target_pairs={{0,1},{1,0},{2,3},{3,2},{4,5},{5,4},{6,7},{7,6},{8,9},{9,8},{10,11... | collective-permute-start | bytes 983048 | tf_op jit(solution)/shard_map/ppermute | solution.py:21
  74.2 15.2 %copy-start.9 = (bf16[80,1024]{1,0:T(8,128)(2,1)}, bf16[80,1024]{1,0:T(8,128)(2,1)S(1)}, u32[]{:S(2)}) copy-start(bf16[80,1024]{1,0:T(8,128)(2,1)S(1)} %get-tuple-element.86.refs_16_.refs_7_) | copy-start | bytes 491524
  74.2 15.2 %copy-start.10 = (bf16[80,1024]{1,0:T(8,128)(2,1)}, bf16[80,1024]{1,0:T(8,128)(2,1)S(1)}, u32[]{:S(2)}) copy-start(bf16[80,1024]{1,0:T(8,128)(2,1)S(1)} %get-tuple-element.87.refs_14_.refs_5_) | copy-start | bytes 491524
  74.3 15.1 %copy-start.11 = (bf16[80,1024]{1,0:T(8,128)(2,1)}, bf16[80,1024]{1,0:T(8,128)(2,1)S(1)}, u32[]{:S(2)}) copy-start(bf16[80,1024]{1,0:T(8,128)(2,1)S(1)} %get-tuple-element.82.refs_20_.refs_11_) | copy-start | bytes 491524
  74.3 15.1 %copy-start.12 = (bf16[80,1024]{1,0:T(8,128)(2,1)}, bf16[80,1024]{1,0:T(8,128)(2,1)S(1)}, u32[]{:S(2)}) copy-start(bf16[80,1024]{1,0:T(8,128)(2,1)S(1)} %get-tuple-element.83.refs_18_.refs_9_) | copy-start | bytes 491524
  74.3 15.1 %copy-start.13 = (bf16[80,1024]{1,0:T(8,128)(2,1)}, bf16[80,1024]{1,0:T(8,128)(2,1)S(1)}, u32[]{:S(2)}) copy-start(bf16[80,1024]{1,0:T(8,128)(2,1)S(1)} %get-tuple-element.78.refs_24_.refs_15_) | copy-start | bytes 491524
  74.3 15.1 %copy-start.14 = (bf16[80,1024]{1,0:T(8,128)(2,1)}, bf16[80,1024]{1,0:T(8,128)(2,1)S(1)}, u32[]{:S(2)}) copy-start(bf16[80,1024]{1,0:T(8,128)(2,1)S(1)} %get-tuple-element.79.refs_22_.refs_13_) | copy-start | bytes 491524
  89.4 0.8 copy-start
  94.9 1.2 %collective-permute-start.29 = (f32[16,512]{1,0:T(8,128)S(1)}, f32[16,512]{1,0:T(8,128)S(1)}, u32[]{:S(2)}, u32[]{:S(2)}) collective-permute-start(f32[16,512]{1,0:T(8,128)S(1)} %slice.456), channel_id=1, source_target_pairs={{0,1},{1,0},{2,3},{3,2},{4,5},{5,4},{6,7},{7,6},{8,9},{9,8},{10,11... | collective-permute-start | bytes 98312 | tf_op jit(solution)/shard_map/ppermute | solution.py:21
  96.1 0.6 copy-start.17
  99.0 4.6 %collective-permute-start.30 = (f32[8,512]{1,0:T(8,128)S(1)}, f32[8,512]{1,0:T(8,128)S(1)}, u32[]{:S(2)}, u32[]{:S(2)}) collective-permute-start(f32[8,512]{1,0:T(8,128)S(1)} %slice.457), channel_id=1, source_target_pairs={{0,8},{1,9},{2,10},{3,11},{4,12},{5,13},{6,14},{7,15},{8,0},{9,1},... | collective-permute-start | bytes 49160 | tf_op jit(solution)/shard_map/ppermute | solution.py:21
  100.6 11.6 %collective-permute-start.25 = (bf16[256,320]{1,0:T(8,128)(2,1)S(1)}, bf16[256,320]{1,0:T(8,128)(2,1)S(1)}, u32[]{:S(2)}, u32[]{:S(2)}) collective-permute-start(bf16[256,320]{1,0:T(8,128)(2,1)S(1)} %get-tuple-element.77), channel_id=1, source_target_pairs={{0,0},{1,4},{2,2},{3,6},{4,1},{5,5},{6,3},{7,7},{8,8},{9,12},{10,1... | collective-permute-start | bytes 491528 | tf_op jit(solution)/shard_map/ppermute | solution.py:21
  101.2 11.0 %collective-permute-start.26 = (bf16[256,320]{1,0:T(8,128)(2,1)S(1)}, bf16[256,320]{1,0:T(8,128)(2,1)S(1)}, u32[]{:S(2)}, u32[]{:S(2)}) collective-permute-start(bf16[256,320]{1,0:T(8,128)(2,1)S(1)} %get-tuple-element.76), channel_id=1, source_target_pairs={{0,2},{1,6},{2,0},{3,4},{4,3},{5,7},{6,1},{7,5},{8,10},{9,14},{10,... | collective-permute-start | bytes 491528 | tf_op jit(solution)/shard_map/ppermute | solution.py:21
  103.7 0.6 copy-start.18
  106.6 6.2 %collective-permute-start.31 = (bf16[2,384]{1,0:T(2,128)(2,1)S(1)}, bf16[2,384]{1,0:T(2,128)(2,1)S(1)}, u32[]{:S(2)}, u32[]{:S(2)}) collective-permute-start(bf16[2,384]{1,0:T(2,128)(2,1)S(1)} %get-tuple-element.106), channel_id=1, source_target_pairs={{0,2},{1,3},{2,0},{3,1},{4,6},{5,7},{6,4},{7,5},{8,10},{9,11},{10,... | collective-permute-start | bytes 4616 | tf_op jit(solution)/shard_map/ppermute | solution.py:21
  108.2 4.7 %collective-permute-start.32 = (bf16[2,384]{1,0:T(2,128)(2,1)S(1)}, bf16[2,384]{1,0:T(2,128)(2,1)S(1)}, u32[]{:S(2)}, u32[]{:S(2)}) collective-permute-start(bf16[2,384]{1,0:T(2,128)(2,1)S(1)} %get-tuple-element.105), channel_id=1, source_target_pairs={{0,4},{1,5},{2,6},{3,7},{4,0},{5,1},{6,2},{7,3},{8,12},{9,13},{10,... | collective-permute-start | bytes 4616 | tf_op jit(solution)/shard_map/ppermute | solution.py:21
  111.2 4.5 %collective-permute-start.33 = (bf16[2,384]{1,0:T(2,128)(2,1)S(1)}, bf16[2,384]{1,0:T(2,128)(2,1)S(1)}, u32[]{:S(2)}, u32[]{:S(2)}) collective-permute-start(bf16[2,384]{1,0:T(2,128)(2,1)S(1)} %get-tuple-element.104), channel_id=1, source_target_pairs={{0,6},{1,7},{2,4},{3,5},{4,2},{5,3},{6,0},{7,1},{8,14},{9,15},{10,... | collective-permute-start | bytes 4616 | tf_op jit(solution)/shard_map/ppermute | solution.py:21
  112.2 5.0 %collective-permute-start.27 = (bf16[128,320]{1,0:T(8,128)(2,1)S(1)}, bf16[128,320]{1,0:T(8,128)(2,1)S(1)}, u32[]{:S(2)}, u32[]{:S(2)}) collective-permute-start(bf16[128,320]{1,0:T(8,128)(2,1)S(1)} %constant_dynamic-slice_fusion.1), channel_id=1, source_target_pairs={{0,1},{1,0},{2,3},{3,2},{4,5},{5,4},{6,7},{7,6},{8,9},{9,8},{10,11... | collective-permute-start | bytes 245768 | tf_op jit(solution)/shard_map/ppermute | solution.py:21
  112.3 4.9 %collective-permute-start.28 = (bf16[128,320]{1,0:T(8,128)(2,1)S(1)}, bf16[128,320]{1,0:T(8,128)(2,1)S(1)}, u32[]{:S(2)}, u32[]{:S(2)}) collective-permute-start(bf16[128,320]{1,0:T(8,128)(2,1)S(1)} %constant_dynamic-slice_fusion), channel_id=1, source_target_pairs={{0,1},{1,0},{2,3},{3,2},{4,5},{5,4},{6,7},{7,6},{8,9},{9,8},{10,11... | collective-permute-start | bytes 245768 | tf_op jit(solution)/shard_map/ppermute | solution.py:21

commit v3 on v2

v3 whole, which is shorter than its diff:
```python
import functools

import jax
import jax.numpy as jnp
from jax import lax
from jax.experimental import pallas as pl
from jax.experimental.pallas import tpu as pltpu
from jax.sharding import PartitionSpec as P

HD = 64
WIDE = 256
GROUP = 320
BF = jnp.bfloat16
F32 = jnp.float32
LOW = -1e30
VMEM = pl.BlockSpec(memory_space=pltpu.VMEM)
SMEM = pl.BlockSpec(memory_space=pltpu.SMEM)


def send(block, route):
    return lax.ppermute(block, "tm", route)


def swap(block, n, mask):
    return send(block, [(d, d ^ mask) for d in range(n)])


def scalars(values):
    return jnp.stack([jnp.asarray(v, jnp.int32) for v in values])


def group_of(array, g):
    return array[:, WIDE * g : WIDE * g + WIDE], array[:, 1024 + HD * g : 1024 + HD * g + HD]


def weight_group(weight, g):
    width = weight.shape[1] // 3
    parts = [group_of(weight[:, i * width : (i + 1) * width], g) for i in range(3)]
    (q0, q1), (k0, k1), (v0, v1) = parts
    return jnp.concatenate([q0, k0, v0, k1, v1, q1], axis=1)


def token_group(queries, mask, g):
    wide, tail = group_of(queries, g)
    heads = [wide[:, HD * i : HD * i + HD] for i in range(4)] + [tail]
    asked = jnp.pad(mask.astype(BF), ((0, 0), (0, HD - mask.shape[1])))
    return jnp.concatenate(heads + [asked], axis=0)


def pack_kernel(spot, weight, *refs):
    queries, masks, segments = refs[0:2], refs[2:4], refs[4:6]
    outs, lanes = refs[6:8], refs[8]
    x, c = spot[0], spot[1]
    rows, width = weight.shape[0], weight.shape[1] // 3
    blocks = masks[0].shape[1]

    def by_core(index, count):
        flip = jnp.broadcast_to(c, (count, HD)) == 1
        return jnp.where(flip, index[1], index[0]), jnp.where(flip, index[0], index[1])

    for turn in range(2):
        column = x if turn == 0 else 1 - x
        for p in range(2):
            out = outs[turn].at[p]
            wide = pl.multiple_of(WIDE * (2 * p + column), 128)
            tails = []
            for i in range(3):
                out[:, WIDE * i : WIDE * i + WIDE] = weight[
                    :, pl.ds(pl.multiple_of(width * i + wide, 128), WIDE)
                ]
                slab = weight[:, width * i + 1024 + 128 * p : width * i + 1152 + 128 * p]
                odd = jnp.broadcast_to(column, (rows, HD)) == 1
                tails.append(jnp.where(odd, slab[:, HD:], slab[:, :HD]))
            lanes[...] = jnp.zeros_like(lanes)
            tokens = [q[:, pl.ds(wide, WIDE)].astype(F32) for q in queries]
            slabs = [q[:, 1024 + 128 * p : 1152 + 128 * p].astype(F32) for q in queries]
            odd = jnp.broadcast_to(column, (2, HD)) == 1
            for h in range(6):
                if h < 4:
                    found = [t[:, HD * h : HD * h + HD] for t in tokens]
                elif h == 4:
                    found = [jnp.where(odd, t[:, HD:], t[:, :HD]) for t in slabs]
                else:
                    gap = jnp.zeros((2, HD - blocks), F32)
                    found = [m[...].astype(F32) for m in masks]
                    if blocks < HD:
                        found = [jnp.concatenate([m, gap], axis=1) for m in found]
                low, high = by_core(found, 2)
                lanes[4 * h : 4 * h + 2, :] = low
                lanes[4 * h + 2 : 4 * h + 4, :] = high
            ids = [seg[...] for seg in segments]
            digits = [[lax.shift_right_logical(v, 7), v & 127] for v in ids]
            for d in range(2):
                for part in range(2):
                    found = [v[d][:, HD * part : HD * part + HD].astype(F32) for v in digits]
                    low, high = by_core(found, 1)
                    at = 24 + 2 * d + part
                    lanes[at : at + 1, :] = low
                    lanes[at + 4 : at + 5, :] = high
            out[:, 3 * WIDE : 896] = jnp.concatenate(tails[1:], axis=1)
            out[:, 896:] = jnp.concatenate([tails[0], lanes[...].astype(BF)], axis=1)


def pack(spot, weight, *small):
    rows = weight.shape[0]
    shape = jax.ShapeDtypeStruct((2, rows, 1024), BF)
    return pl.pallas_call(
        pack_kernel,
        out_shape=(shape, shape),
        in_specs=[SMEM] + [VMEM] * (1 + len(small)),
        out_specs=(VMEM, VMEM),
        scratch_shapes=[pltpu.VMEM((rows, HD), F32)],
    )(spot, weight, *small)


def norm_kernel(ways, places, gain, *refs):
    blocks, (normed, residual) = refs[: 4 * ways], refs[4 * ways :]
    group = places[4]
    for i in range(4):
        place = pl.multiple_of(places[i], 128)
        values = blocks[i][...]
        if ways == 2:
            first = jnp.broadcast_to(places[5], values.shape) == 1
            values = jnp.where(first, values, blocks[4 + i][...])
        values = values.astype(F32)
        mean = jnp.mean(values, axis=-1, keepdims=True)
        centred = values - mean
        var = jnp.mean(centred * centred, axis=-1, keepdims=True)
        normed[pl.ds(place, 128), :] = (centred * lax.rsqrt(var + 1e-05) * gain[...]).astype(BF)
        block = blocks[i]
        residual[pl.ds(place, 128), :WIDE] = block[
            :, pl.ds(pl.multiple_of(group * WIDE, 128), WIDE)
        ]
        slab = block[:, pl.ds(pl.multiple_of(1024 + group // 2 * 128, 128), 128)]
        odd = jnp.broadcast_to(lax.rem(group, 2), (128, HD)) == 1
        residual[pl.ds(place, 128), WIDE:] = jnp.where(odd, slab[:, HD:], slab[:, :HD])


def norm_layer(places, gain, blocks):
    return pl.pallas_call(
        functools.partial(norm_kernel, len(blocks) // 4),
        out_shape=(
            jax.ShapeDtypeStruct((512, 1280), BF),
            jax.ShapeDtypeStruct((512, GROUP), BF),
        ),
        in_specs=[SMEM] + [VMEM] * (1 + len(blocks)),
        out_specs=(VMEM, VMEM),
        compiler_params=pltpu.CompilerParams(vmem_limit_bytes=16 * 1024 * 1024),
    )(places, gain, *blocks)


def encoder_kernel(n_parts, depth, chips, places, *refs):
    layers = [refs[2 * i : 2 * i + 2] for i in range(3)]
    parts = refs[6 : 6 + n_parts]
    refs = refs[6 + n_parts :]
    if not chips:
        given, refs = refs[0], refs[1:]
    memory, near, away, weight, ids, residual, queries, keys, values = refs
    x, straight, first = places[3], places[4], places[5]

    for i, part in enumerate(parts):
        row = pl.multiple_of(places[6 + i] * depth, 16)
        weight[pl.ds(row, depth), :] = part[...]
    if chips:
        ids[...] = jnp.zeros_like(ids)
        for i in range(n_parts // 2):
            here, there = parts[2 * i][:32, 960:], parts[2 * i + 1][:32, 960:]
            lanes = jnp.where(jnp.broadcast_to(straight, (32, HD)) == 1, here.astype(F32), there.astype(F32))
            found = lanes[24:]
            for core in range(2):
                high = found[4 * core : 4 * core + 2]
                marks = high * 128.0 + found[4 * core + 2 : 4 * core + 4]
                block = places[6 + 2 * i] // 2 * 2 + core - first

                @pl.when((block >= 0) & (block < 12))
                def _():
                    ids[0:1, pl.ds(pl.multiple_of(block * 128, 128), 128)] = jnp.concatenate(
                        [marks[0:1], marks[1:2]], axis=1
                    )

    else:
        ids[...] = given[...]

    for slab in range(3):
        values[:, 256 * slab + 128 : 256 * slab + 256] = jnp.ones((1536, 128), BF)
    for i, (normed, kept) in enumerate(layers):
        place = pl.multiple_of(places[i], 512)
        found = jnp.dot(normed[...], weight[:, 256:896], preferred_element_type=F32).astype(BF)
        keys[pl.ds(place, 512), :256] = found[:, :256]
        keys[pl.ds(place, 512), 256:] = found[:, 512:]
        for slab in range(3):
            values[pl.ds(place, 512), 256 * slab : 256 * slab + 128] = found[
                :, 256 + 128 * slab : 384 + 128 * slab
            ]
        if i < 2:

            @pl.when(place == 512)
            def _():
                residual[...] = kept[...]
                queries[:, :WIDE] = jnp.dot(
                    normed[...], weight[:, :WIDE], preferred_element_type=F32
                ).astype(BF)
                tail = jnp.dot(normed[...], weight[:, 896:], preferred_element_type=F32).astype(BF)
                lane = lax.broadcasted_iota(jnp.int32, tail.shape, 1)
                queries[:, WIDE:] = jnp.where(lane < HD, tail, jnp.zeros_like(tail))

    side = lax.broadcasted_iota(jnp.int32, (8, 128), 0) == lax.broadcasted_iota(
        jnp.int32, (8, 128), 1
    ) // HD
    sides = jnp.where(side, 1.0, 0.0).astype(BF)
    only = jnp.where(side & (lax.broadcasted_iota(jnp.int32, (8, 128), 0) == 0), 1.0, 0.0).astype(BF)
    most = []
    for held in (queries, keys):
        top = jnp.zeros((8, 1), F32)
        for slab in range(3):
            part = held[:, 128 * slab : 128 * slab + 128]
            norms = lax.dot_general(
                sides if slab < 2 else only,
                part * part,
                (((1,), (1,)), ((), ())),
                preferred_element_type=F32,
            )
            top = jnp.maximum(top, jnp.max(norms, axis=-1, keepdims=True))
        most.append(jnp.max(top))
    small = most[0] * most[1] < 220000.0

    def attend(step, shifted):
        row = step * 128 if isinstance(step, int) else pl.multiple_of(step * 128, 128)
        mine = jnp.broadcast_to(ids[0:1, pl.ds(row + 512, 128)], (128, 128)).T[:, 0:1]
        bias = jnp.where(mine == ids[0:1, pl.ds(row, 1152)], 0.0, LOW)
        lane = lax.broadcasted_iota(jnp.int32, (128, 128), 1)
        for slab in range(3):
            span = slice(128 * slab, 128 * slab + 128)
            query = queries[pl.ds(row, 128), span] * BF(0.125)
            mask = bias
            if slab < 2:
                none = jnp.zeros_like(query)
                query = jnp.concatenate(
                    [jnp.where(lane < HD, query, none), jnp.where(lane < HD, none, query)], axis=0
                )
                mask = jnp.concatenate([bias, bias], axis=0)
            scores = lax.dot_general(
                query,
                keys[pl.ds(row, 1152), span],
                (((1,), (1,)), ((), ())),
                preferred_element_type=F32,
            )
            scores = scores + mask
            if shifted:
                scores = scores - jnp.max(scores, axis=-1, keepdims=True)
            raised = jnp.exp(scores).astype(BF)
            out = jnp.dot(
                raised,
                values[pl.ds(row, 1152), 256 * slab : 256 * slab + 256],
                preferred_element_type=F32,
            )
            out = out[:, :128] / out[:, 128:]
            if slab < 2:
                context = jnp.where(lane < HD, out[:128], out[128:])
                stem = residual[pl.ds(row, 128), span].astype(F32)
                memory[pl.ds(row, 128), span] = (stem + context).astype(BF)
            else:
                stem = residual[pl.ds(row, 128), WIDE:].astype(F32)
                memory[pl.ds(row, 128), WIDE:] = (stem + out[:, HD:]).astype(BF)

    @pl.when(small)
    def _():
        for step in range(4):
            attend(step, False)

    @pl.when(jnp.logical_not(small))
    def _():
        lax.fori_loop(0, 4, lambda step, carry: (attend(step, True), carry)[1], 0)

    near[...] = memory[pl.ds(pl.multiple_of(256 * x, 256), 256), :]
    away[...] = memory[pl.ds(pl.multiple_of(256 * (1 - x), 256), 256), :]


def encoder(places, layers, parts, depth, extra):
    operands = [a for layer in layers for a in layer] + parts + extra
    return pl.pallas_call(
        functools.partial(encoder_kernel, len(parts), depth, not extra),
        out_shape=(
            jax.ShapeDtypeStruct((512, GROUP), BF),
            jax.ShapeDtypeStruct((256, GROUP), BF),
            jax.ShapeDtypeStruct((256, GROUP), BF),
        ),
        in_specs=[SMEM] + [VMEM] * len(operands),
        out_specs=(VMEM, VMEM, VMEM),
        scratch_shapes=[
            pltpu.VMEM((1280, 1024), BF),
            pltpu.VMEM((8, 1536), F32),
            pltpu.VMEM((512, GROUP), BF),
            pltpu.VMEM((512, 384), BF),
            pltpu.VMEM((1536, 384), BF),
            pltpu.VMEM((1536, 768), BF),
        ],
        compiler_params=pltpu.CompilerParams(vmem_limit_bytes=24 * 1024 * 1024),
    )(places, *operands)


def spread(columns, rows, slab):
    lane = lax.broadcasted_iota(jnp.int32, (rows, 128), 1)
    return jnp.where(lane < HD, columns[2 * slab], columns[min(2 * slab + 1, 4)])


def cross_kernel(chips, place, memory, *refs):
    tokens, out = refs[-2:]
    count = out.shape[0]
    parts, outs_by_owner = refs[: -2 - count // 8], refs[-2 - count // 8 : -2]
    first, me, core, straight = place[0], place[1], place[2], place[3]
    half = count // 2
    if chips:
        for i in range(len(parts) // 2):
            here, there = parts[2 * i][:24, 960:], parts[2 * i + 1][:24, 960:]
            rows = jnp.where(jnp.broadcast_to(straight, (24, HD)) == 1, here.astype(F32), there.astype(F32))
            for h in range(6):
                low, high = rows[4 * h : 4 * h + 2], rows[4 * h + 2 : 4 * h + 4]
                flip = jnp.broadcast_to(core, (2, HD)) == 1
                tokens[h, 2 * i : 2 * i + 2, :] = jnp.where(flip, high, low)
                tokens[h, half + 2 * i : half + 2 * i + 2, :] = jnp.where(flip, low, high)
    else:
        tokens[...] = parts[0][...].astype(F32)
    blocks = HD
    spot = lax.broadcasted_iota(jnp.int32, (count, blocks), 1)
    order = lax.broadcasted_iota(jnp.int32, (count, 1), 0)
    relative = 2 * (lax.rem(order, half) // 2) + order // half
    owner = relative ^ me
    allowed = []
    for b in range(4):
        ask = jnp.sum(jnp.where(spot == first + b, tokens[5], 0.0), axis=-1, keepdims=True)
        allowed.append((ask > 0.5) | (owner == first + b))
    lane = lax.broadcasted_iota(jnp.int32, (count, 128), 1)
    bias = jnp.concatenate(
        [jnp.broadcast_to(jnp.where(a, 0.0, LOW), (count, 128)) for a in allowed], axis=1
    )
    stats = jnp.zeros((count, 128), F32)
    for slab in range(3):
        heads = [(tokens[h] * 0.125).astype(BF) for h in range(2 * slab, min(2 * slab + 2, 5))]
        none = jnp.zeros_like(heads[0])
        if slab < 2:
            heads = [
                jnp.concatenate([heads[0], none], axis=1),
                jnp.concatenate([none, heads[1]], axis=1),
            ]
            held = memory[:, 128 * slab : 128 * slab + 128]
        else:
            held = memory[:, WIDE:]
        outs = []
        for i, head in enumerate(heads):
            cross = lax.dot_general(
                head, held, (((1,), (1,)), ((), ())), preferred_element_type=F32
            )
            cross = jnp.where(bias < 0.0, LOW, cross)
            top = jnp.max(cross, axis=-1, keepdims=True)
            raised = jnp.where(bias < 0.0, 0.0, jnp.exp(cross - top))
            den = jnp.sum(raised, axis=-1, keepdims=True)
            outs.append(jnp.dot(raised.astype(BF), held, preferred_element_type=F32))
            stats = jnp.where(lane == 2 * slab + i, top, stats)
            stats = jnp.where(lane == 8 + 2 * slab + i, den, stats)
        if slab < 2:
            out[:, 128 * slab : 128 * slab + 128] = jnp.where(lane < HD, outs[0], outs[1])
        else:
            out[:, WIDE:384] = jnp.concatenate([outs[0], jnp.zeros_like(outs[0])], axis=1)
    out[:, 384:] = stats
    for i, owned in enumerate(outs_by_owner):
        owned[...] = out[8 * i : 8 * i + 8, :]


def cross_partial(place, memory, parts, count, chips):
    return pl.pallas_call(
        functools.partial(cross_kernel, chips),
        out_shape=(jax.ShapeDtypeStruct((8, 512), F32),) * (count // 8),
        in_specs=[SMEM] + [VMEM] * (1 + len(parts)),
        out_specs=(VMEM,) * (count // 8),
        scratch_shapes=[pltpu.VMEM((6, count, HD), F32), pltpu.VMEM((count, 512), F32)],
    )(place, memory, *parts)


def merge_kernel(*refs):
    parts, outs, out = refs[:-5], refs[-5:-1], refs[-1]
    stats = [part[:, 384:] for part in parts]
    factors, dens = [[] for _ in parts], []
    for head in range(5):
        tops = [s[:, head : head + 1] for s in stats]
        best = functools.reduce(jnp.maximum, tops)
        den = jnp.zeros_like(best)
        for i, s in enumerate(stats):
            factor = jnp.exp(tops[i] - best)
            den = den + factor * s[:, 8 + head : 9 + head]
            factors[i].append(factor)
        dens.append(den)
    for slab in range(3):
        span = slice(128 * slab, 128 * slab + 128)
        total = jnp.zeros((8, 128), F32)
        for i, part in enumerate(parts):
            total = total + spread(factors[i], 8, slab) * part[:, span]
        out[:, span] = total / spread(dens, 8, slab)
    for i in range(4):
        outs[i][...] = out[2 * i : 2 * i + 2, :].astype(BF)


def merge(parts):
    return pl.pallas_call(
        merge_kernel,
        out_shape=(jax.ShapeDtypeStruct((2, 384), BF),) * 4,
        in_specs=[VMEM] * len(parts),
        out_specs=(VMEM,) * 4,
        scratch_shapes=[pltpu.VMEM((8, 384), F32)],
    )(*parts)


def gather_groups(pieces, group):
    wide, tail = [], []
    for g in range(4):
        turn = group ^ g
        piece = jnp.where(
            turn < 2,
            jnp.where(turn == 0, pieces[0], pieces[1]),
            jnp.where(turn == 2, pieces[2], pieces[3]),
        )
        wide.append(piece[:, :WIDE])
        tail.append(piece[:, WIDE:GROUP])
    return jnp.concatenate(wide + tail, axis=1)


def on_device(stem, norm_gain, qkv_weight, segment_ids, dec_queries, stretch_mask):
    n = lax.axis_size("tm")
    layers = n // 4
    me = lax.axis_index("tm")
    z, x, c = me // 4, (me // 2) % 2, me % 2
    p, k = z % 2, z // 2
    quarter = 2 * k + c
    group = 2 * p + x
    depth = qkv_weight.shape[0]

    layers_route = [1 if i % 2 else -1 for i in range(layers)]
    near_route = [
        (4 * i + j, 4 * (i + s) + j)
        for i, s in enumerate(layers_route)
        for j in range(4)
        if 0 <= i + s < layers
    ]
    near = send(stem, near_route)
    pair = swap(stem, n, 4)
    stem_x = swap(stem, n, 2)
    utts = lax.axis_size("utt")
    straight = (c == lax.axis_index("utt") % 2).astype(jnp.int32)
    gain = norm_gain.reshape(1, -1)
    inner = [128 * (2 * x + c), 128 * (2 * x + 1 - c), 128 * (2 - 2 * x + c), 128 * (3 - 2 * x - c)]
    spots = inner + [group]
    extra = []
    if depth % 16 == 0 and layers == 4 and utts % 2 == 0:
        carriers = [(u, d) for u in range(utts) for d in range(n) if d % 2 == u % 2]

        def carry(block, turn_u, turn_d):
            route = [(u * n + d, (u ^ turn_u) * n + (d ^ turn_d)) for u, d in carriers]
            return lax.ppermute(block, ("utt", "tm"), route)

        small = [dec_queries, stretch_mask, segment_ids.reshape(1, -1)]
        both = [part for piece in small for part in (piece, swap(piece, n, 1))]
        mine, theirs = pack(scalars([x, c]), qkv_weight, *both)
        across = carry(theirs, 0, 2)
        mine_late, across_late, pair, near = lax.optimization_barrier((mine, across, pair, near))
        ready = [
            jnp.concatenate(
                [
                    lax.dynamic_slice_in_dim(mine_late, p ^ a, 1, 0),
                    lax.dynamic_slice_in_dim(across_late, p ^ a, 1, 0),
                ]
            ).reshape(2 * depth, 1024)
            for a in range(2)
        ]
        here = {0: lax.dynamic_index_in_dim(across, p, 0, keepdims=False)}
        for turn in (3, 2, 1):
            here[turn] = carry(ready[turn % 2], 0, 4 * turn)
        own_part = lax.dynamic_index_in_dim(mine, p, 0, keepdims=False)
        weights = [own_part, swap(own_part, n, 1)]
        part_places = [me, me ^ 1]
        for turn in range(4):
            traded = carry(here[turn], 1, 0)
            got = jnp.where(straight == 1, here[turn], traded)
            beside = swap(got, n, 1)
            pieces = got.shape[0] // depth
            for s in range(pieces):
                chip = me ^ (4 * turn + 2 * (s + 2 - pieces))
                for part, source in ((got, chip), (beside, chip ^ 1)):
                    weights.append(part[s * depth : s * depth + depth])
                    part_places.append(source)
        token_parts = [own_part, own_part] + weights[2:]

        beside_route = [
            (d, d ^ 1) for d in range(n) if d % 2 == d // 8
        ]
        inside = [d for d in range(n) if d // 4 in (1, 2)]
        relayed = send(near, [(d, d ^ 4) for d in inside])
        near_x = send(near, [(d, d ^ 2) for d in inside])
        relayed_x = send(relayed, [(d ^ 4, d ^ 6) for d in inside])
        halo_layer = []
        for a, b in ((near, near_x), (relayed, relayed_x)):
            halo_layer += [a, send(a, beside_route), b, send(b, beside_route)]
        halo_spots = spots + [(p != k).astype(jnp.int32)]
    else:
        far = swap(near, n, 4)
        left = jnp.where(p == 0, near, far)
        right = jnp.where(p == 0, far, near)
        left_x, right_x = swap(left, n, 2), swap(right, n, 2)
        halo_layer = [
            jnp.where(c == 0, left, right),
            swap(jnp.where(c == 0, right, left), n, 1),
            jnp.where(c == 0, left_x, right_x),
            swap(jnp.where(c == 0, right_x, left_x), n, 1),
        ]
        halo_spots = spots
        whole = lax.all_gather(qkv_weight, "tm", axis=0, tiled=True)
        grouped = jnp.stack([weight_group(whole, g) for g in range(4)])
        weights = [lax.dynamic_index_in_dim(grouped, group, 0, keepdims=False)]
        weights = [jnp.pad(weights[0], ((0, 0), (0, HD)))]
        part_places = [jnp.int32(0)]
        depth = whole.shape[0]
        packed = jnp.stack([token_group(dec_queries, stretch_mask, g) for g in range(4)])
        every = lax.all_gather(packed, "tm", axis=0)
        every = lax.dynamic_index_in_dim(every, group, 1, keepdims=False)
        order = jnp.array([m for core in range(2) for m in range(core, n, 2)], jnp.int32)
        every = jnp.take(every, order ^ me, axis=0).reshape(n, 6, 2, HD)
        token_parts = [every.transpose(1, 0, 2, 3).reshape(6, 2 * n, HD)]
        marks = lax.all_gather(segment_ids, "tm", axis=0, tiled=True).astype(F32)
        marks = jnp.pad(marks, (512, 512))
        marks = lax.dynamic_slice_in_dim(marks, 512 * quarter, 1536, 0)
        extra = [jnp.broadcast_to(marks[None], (8, 1536))]
    pair_x = swap(pair, n, 2)
    own_layer = [stem, swap(stem, n, 1), stem_x, swap(stem_x, n, 1)]
    pair_layer = [pair, swap(pair, n, 1), pair_x, swap(pair_x, n, 1)]
    layered = []
    for blocks, at in ((own_layer, spots), (pair_layer, spots), (halo_layer, halo_spots)):
        layered.append(norm_layer(scalars(at), gain, blocks))
    places = [512 * (p - c + 1), 512 * (2 - p - c), 1024 * c, x, straight, 4 * quarter - 4]

    table = scalars(places + part_places)
    held, stay, leave = encoder(table, layered, weights, depth, extra)

    pieces = []
    for turn, rows in enumerate((stay, leave)):
        route = [
            (
                8 * (d // 8) + 4 * (d // 4 % 2) + (d & 2) + (d & 1),
                8 * (d // 8) + 4 * (d & 1) + ((d & 2) ^ (2 * turn)) + (d // 4 % 2),
            )
            for d in range(n)
        ]
        got = send(rows, route)
        keep = lax.dynamic_slice_in_dim(got, 128 * c, 128, 0)
        give = swap(lax.dynamic_slice_in_dim(got, 128 * (1 - c), 128, 0), n, 1)
        pieces.append((keep, give))
    memory = gather_groups([pieces[0][0], pieces[1][0], pieces[0][1], pieces[1][1]], 2 * c + x)

    place = scalars([4 * quarter, me, c, straight])
    partial = cross_partial(place, held, token_parts, 2 * n, len(token_parts) > 1)
    owned = [partial[0]]
    outer = n // 8
    for i in range(1, 2 * outer):
        core, turn = i // outer, i % outer
        owned.append(swap(partial[i], n, 8 * turn + core))
    final = merge(owned)
    final = [final[0]] + [swap(final[i], n, 2 * i) for i in (1, 2, 3)]
    cross_out = gather_groups(final, group)
    return (memory, cross_out)


def solution(mesh):
    placed = (
        P(("utt", "tm"), None),
        P(),
        P("tm", None),
        P(("utt", "tm")),
        P(("utt", "tm"), None),
        P(("utt", "tm"), None),
    )
    return jax.shard_map(
        on_device,
        mesh=mesh,
        in_specs=placed,
        out_specs=(P(("utt", "tm"), None), P(("utt", "tm"), None)),
        check_vma=False,
    )
```

time: 119 us -> 118 us (level)
  starting transfers between devices: 41.4 us -> 55.6 us
  waiting for transfers between devices: 33.7 us -> 24.6 us
  local copies, waits for them, and re-layouts: 12.1 us -> 5.79 us
    ppermute x26 -> x33, waiting for transfers between devices: 26.7 us -> 14.1 us  [send(): return lax.ppermute(block, 'tm', route)]
    ppermute x26 -> x33, starting transfers between devices: 17.5 us -> 29.5 us  [send(): return lax.ppermute(block, 'tm', route)]
    slice x15 -> x6, local copies, waits for them, and re-layouts: 6.26 us -> 0.14 us  [on_device(): weights.append(part[s * depth:s * depth + depth])]
    ppermute x8, waiting for transfers between devices: 7.01 us -> 10.5 us  [carry(): return lax.ppermute(block, ('utt', 'tm'), route)]
    ppermute x8, starting transfers between devices: 23.9 us -> 26 us  [carry(): return lax.ppermute(block, ('utt', 'tm'), route)]
    concatenate x5 -> x2, other arithmetic: 0.12 us -> 1.51 us  [on_device(): jnp.concatenate([lax.dynamic_slice_in_dim(mine_late, p ^ a, 1, 0), lax.dy...]
    unnamed x42 -> x50, local copies, waits for them, and re-layouts: 2.05 us -> 2.6 us
  transfers between devices with their start and end apart: 34 -> 41, of which waited for: 10 -> 11; matrix products, arithmetic and copies ran while one was open for 6% -> 5% of each run, Pallas kernels for 5% -> 11%
where the time goes in v3:
time: 118 us
  starting transfers between devices  55.6 us (47%)
  Pallas kernels  26.5 us (22%)
  waiting for transfers between devices  24.6 us (21%)
  local copies, waits for them, and re-layouts  5.79 us (5%)
  other arithmetic  3.7 us (3%)
  between operations  1.64 us (1%)
    ppermute x33, starting transfers between devices, send(): return lax.ppermute(block, 'tm', route)  29.5 us
    ppermute x8, starting transfers between devices, carry(): return lax.ppermute(block, ('utt', 'tm'), route)  26 us
    ppermute x33, waiting for transfers between devices, send(): return lax.ppermute(block, 'tm', route)  14.1 us
    pallas_call x1, Pallas kernels, encoder(): pl.pallas_call(functools.partial(encoder_kernel, len(parts), depth, not e...  13.9 us
    ppermute x8, waiting for transfers between devices, carry(): return lax.ppermute(block, ('utt', 'tm'), route)  10.5 us
    pallas_call x3, Pallas kernels, norm_layer(): pl.pallas_call(functools.partial(norm_kernel, len(blocks) // 4), out_shap...  4.71 us
    pallas_call x1, Pallas kernels, cross_partial(): pl.pallas_call(functools.partial(cross_kernel, chips), out_shape=(jax.Sha...  3.93 us
    unnamed x50, local copies, waits for them, and re-layouts  2.6 us
  transfers between devices with their start and end apart: 41, of which 11 were waited for; matrix products, arithmetic and copies ran while one was open for 5% of the time, Pallas kernels for 11%

profile of v3, /device:TPU:0, one launch (start us, length us, event | category | flops | bytes accessed | tf_op | source)
XLA Modules:
  0.0 117.8 jit_solution(2259439868673899698)
XLA Ops:
  0.6 3.1 %collective-permute-start.7 = (bf16[128,1280]{1,0:T(8,128)(2,1)}, bf16[128,1280]{1,0:T(8,128)(2,1)S(1)}, u32[]{:S(2)}, u32[]{:S(2)}) collective-permute-start(bf16[128,1280]{1,0:T(8,128)(2,1)} %refs_0_.2), channel_id=1, source_target_pairs={{0,4},{1,5},{2,6},{3,7},{4,0},{5,1},{6,2},{7,3},{8,12},{9,13},{10,... | collective-permute-start | bytes 983048 | tf_op jit(solution)/shard_map/ppermute | solution.py:21
  3.7 0.7 collective-permute-start.8
  4.5 0.5 collective-permute-start.4
  5.1 0.6 pad_add_fusion.spot
  5.7 0.3 collective-permute-done.4.refs_3_
  6.0 0.2 collective-permute-done.5.refs_5_
  6.2 0.3 copy-done.23
  6.6 0.2 copy-done.24
  6.8 0.6 copy-done.22
  7.4 2.4 %shard_map.78 = (bf16[2,80,1024]{2,1,0:T(8,128)(2,1)}, bf16[2,80,1024]{2,1,0:T(8,128)(2,1)}) custom-call(s32[2]{0:T(128)} %pad_add_fusion.spot, bf16[80,3840]{1,0:T(8,128)(2,1)} %weight.1, bf16[2,1280]{1,0:T(2,128)(2,1)} %refs_0_.3, bf16[2,1280]{1,0:T(2,128)(2,1)} %copy-done.22, s32[2,16]{1,0:T(2,128)} %refs_2_.1, s32[2,16]{1,0:T(2,128)} %copy-done.23, ...), custom_call_target="tpu_custom_call" | custom-call | tf_op jit(solution)/shard_map/pallas_call | solution.py:107
  9.8 3.4 %collective-permute-start.6 = (bf16[2,80,1024]{2,1,0:T(8,128)(2,1)}, bf16[2,80,1024]{2,1,0:T(8,128)(2,1)S(1)}, u32[]{:S(2)}, u32[]{:S(2)}) collective-permute-start(bf16[2,80,1024]{2,1,0:T(8,128)(2,1)} %get-tuple-element.28), channel_id=1, source_target_pairs={{0,2},{2,0},{4,6},{6,4},{8,10},{10,8},{12,14},{14,12},{17,19},{19,... | collective-permute-start | bytes 983048 | tf_op jit(solution)/shard_map/ppermute | solution.py:458
  13.2 0.6 collective-permute-start.1
  13.8 6.8 %collective-permute-done.6 = bf16[2,80,1024]{2,1,0:T(8,128)(2,1)S(1)} collective-permute-done((bf16[2,80,1024]{2,1,0:T(8,128)(2,1)}, bf16[2,80,1024]{2,1,0:T(8,128)(2,1)S(1)}, u32[]{:S(2)}, u32[]{:S(2)}) %collective-permute-start.6) | collective-permute-done | bytes 327712 | tf_op jit(solution)/shard_map/ppermute | solution.py:458
  20.6 1.1 constant_dynamic-slice_fusion.2
  21.7 0.8 pad_maximum_fusion
  22.4 6.3 %collective-permute-start.22 = (bf16[160,1024]{1,0:T(8,128)(2,1)}, bf16[160,1024]{1,0:T(8,128)(2,1)S(1)}, u32[]{:S(2)}, u32[]{:S(2)}) collective-permute-start(bf16[160,1024]{1,0:T(8,128)(2,1)} %bitcast.32), channel_id=1, source_target_pairs={{0,4},{2,6},{4,0},{6,2},{8,12},{10,14},{12,8},{14,10},{17,21},{19,... | collective-permute-start | bytes 983048 | tf_op jit(solution)/shard_map/ppermute | solution.py:458
  28.7 0.7 pad_maximum_fusion.1
  29.5 1.9 %collective-permute-start.25 = (bf16[160,1024]{1,0:T(8,128)(2,1)}, bf16[160,1024]{1,0:T(8,128)(2,1)S(1)}, u32[]{:S(2)}, u32[]{:S(2)}) collective-permute-start(bf16[160,1024]{1,0:T(8,128)(2,1)} %bitcast.33), channel_id=1, source_target_pairs={{0,8},{2,10},{4,12},{6,14},{8,0},{10,2},{12,4},{14,6},{17,25},{19,... | collective-permute-start | bytes 983048 | tf_op jit(solution)/shard_map/ppermute | solution.py:458
  31.4 1.3 %collective-permute-start.20 = (bf16[80,1024]{1,0:T(8,128)(2,1)S(1)}, bf16[80,1024]{1,0:T(8,128)(2,1)S(1)}, u32[]{:S(2)}, u32[]{:S(2)}) collective-permute-start(bf16[80,1024]{1,0:T(8,128)(2,1)S(1)} %dynamic-slice_bitcast_fusion), channel_id=1, source_target_pairs={{0,16},{2,18},{4,20},{6,22},{8,24},{10,26},{12,28},{14,30},{17,1},... | collective-permute-start | bytes 491528 | tf_op jit(solution)/shard_map/ppermute | solution.py:458
  33.1 0.1 stack.145.places
  33.2 0.5 collective-permute-start.2
  33.7 1.9 %collective-permute-done.20 = bf16[80,1024]{1,0:T(8,128)(2,1)S(1)} collective-permute-done((bf16[80,1024]{1,0:T(8,128)(2,1)S(1)}, bf16[80,1024]{1,0:T(8,128)(2,1)S(1)}, u32[]{:S(2)}, u32[]{:S(2)}) %collective-permute-start.20) | collective-permute-done | bytes 163872 | tf_op jit(solution)/shard_map/ppermute | solution.py:458
  35.5 4.3 %collective-permute-start.28 = (bf16[160,1024]{1,0:T(8,128)(2,1)}, bf16[160,1024]{1,0:T(8,128)(2,1)S(1)}, u32[]{:S(2)}, u32[]{:S(2)}) collective-permute-start(bf16[160,1024]{1,0:T(8,128)(2,1)} %bitcast.32), channel_id=1, source_target_pairs={{0,12},{2,14},{4,8},{6,10},{8,4},{10,6},{12,0},{14,2},{17,29},{19,... | collective-permute-start | bytes 983048 | tf_op jit(solution)/shard_map/ppermute | solution.py:458
  39.8 1.3 %collective-permute-start.23 = (bf16[160,1024]{1,0:T(8,128)(2,1)S(1)}, bf16[160,1024]{1,0:T(8,128)(2,1)S(1)}, u32[]{:S(2)}, u32[]{:S(2)}) collective-permute-start(bf16[160,1024]{1,0:T(8,128)(2,1)S(1)} %collective-permute-done.22), channel_id=1, source_target_pairs={{0,16},{2,18},{4,20},{6,22},{8,24},{10,26},{12,28},{14,30},{17,1},... | collective-permute-start | bytes 983048 | tf_op jit(solution)/shard_map/ppermute | solution.py:458
  41.2 1.3 %collective-permute-done.25 = bf16[160,1024]{1,0:T(8,128)(2,1)S(1)} collective-permute-done((bf16[160,1024]{1,0:T(8,128)(2,1)}, bf16[160,1024]{1,0:T(8,128)(2,1)S(1)}, u32[]{:S(2)}, u32[]{:S(2)}) %collective-permute-start.25) | collective-permute-done | bytes 327712 | tf_op jit(solution)/shard_map/ppermute | solution.py:458
  42.5 1.3 %collective-permute-start.26 = (bf16[160,1024]{1,0:T(8,128)(2,1)S(1)}, bf16[160,1024]{1,0:T(8,128)(2,1)S(1)}, u32[]{:S(2)}, u32[]{:S(2)}) collective-permute-start(bf16[160,1024]{1,0:T(8,128)(2,1)S(1)} %collective-permute-done.25), channel_id=1, source_target_pairs={{0,16},{2,18},{4,20},{6,22},{8,24},{10,26},{12,28},{14,30},{17,1},... | collective-permute-start | bytes 983048 | tf_op jit(solution)/shard_map/ppermute | solution.py:458
  43.9 1.6 %collective-permute-start.10 = (bf16[128,1280]{1,0:T(8,128)(2,1)S(1)}, bf16[128,1280]{1,0:T(8,128)(2,1)S(1)}, u32[]{:S(2)}, u32[]{:S(2)}) collective-permute-start(bf16[128,1280]{1,0:T(8,128)(2,1)S(1)} %collective-permute-done.7.refs_0_), channel_id=1, source_target_pairs={{0,2},{1,3},{2,0},{3,1},{4,6},{5,7},{6,4},{7,5},{8,10},{9,11},{10,... | collective-permute-start | bytes 983048 | tf_op jit(solution)/shard_map/ppermute | solution.py:21
  45.5 1.6 %shard_map.77 = (bf16[512,1280]{1,0:T(8,128)(2,1)S(1)}, bf16[512,320]{1,0:T(8,128)(2,1)S(1)}) custom-call(s32[5]{0:T(128)S(1)} %stack.151.places, f32[1,1280]{1,0:T(1,128)S(1)} %reshape.16.gain, bf16[128,1280]{1,0:T(8,128)(2,1)S(1)} %copy-done.16, bf16[128,1280]{1,0:T(8,128)(2,1)S(1)} %collective-permute-done.refs_1_, ...), custom_call_target="tpu_custom_call" | custom-call | tf_op jit(solution)/shard_map/pallas_call | solution.py:140
  47.1 1.3 %collective-permute-start.15 = (bf16[128,1280]{1,0:T(8,128)(2,1)S(1)}, bf16[128,1280]{1,0:T(8,128)(2,1)S(1)}, u32[]{:S(2)}, u32[]{:S(2)}) collective-permute-start(bf16[128,1280]{1,0:T(8,128)(2,1)S(1)} %collective-permute-done.8.refs_0_), channel_id=1, source_target_pairs={{4,0},{5,1},{6,2},{7,3},{8,12},{9,13},{10,14},{11,15},{20,16},{21,... | collective-permute-start | bytes 983048 | tf_op jit(solution)/shard_map/ppermute | solution.py:21
  48.4 6.3 %collective-permute-start.29 = (bf16[160,1024]{1,0:T(8,128)(2,1)S(1)}, bf16[160,1024]{1,0:T(8,128)(2,1)S(1)}, u32[]{:S(2)}, u32[]{:S(2)}) collective-permute-start(bf16[160,1024]{1,0:T(8,128)(2,1)S(1)} %collective-permute-done.28), channel_id=1, source_target_pairs={{0,16},{2,18},{4,20},{6,22},{8,24},{10,26},{12,28},{14,30},{17,1},... | collective-permute-start | bytes 983048 | tf_op jit(solution)/shard_map/ppermute | solution.py:458
  54.8 1.3 %collective-permute-start.12 = (bf16[128,1280]{1,0:T(8,128)(2,1)S(1)}, bf16[128,1280]{1,0:T(8,128)(2,1)S(1)}, u32[]{:S(2)}, u32[]{:S(2)}) collective-permute-start(bf16[128,1280]{1,0:T(8,128)(2,1)S(1)} %collective-permute-done.8.refs_0_), channel_id=1, source_target_pairs={{0,1},{2,3},{4,5},{6,7},{9,8},{11,10},{13,12},{15,14},{16,17},{18,... | collective-permute-start | bytes 983048 | tf_op jit(solution)/shard_map/ppermute | solution.py:21
  56.1 0.7 collective-permute-start.13
  56.8 1.9 %collective-permute-done.15.refs_4_ = bf16[128,1280]{1,0:T(8,128)(2,1)S(1)} collective-permute-done((bf16[128,1280]{1,0:T(8,128)(2,1)S(1)}, bf16[128,1280]{1,0:T(8,128)(2,1)S(1)}, u32[]{:S(2)}, u32[]{:S(2)}) %collective-permute-start.15) | collective-permute-done | bytes 327712 | tf_op jit(solution)/shard_map/ppermute | solution.py:21
  58.8 0.5 collective-permute-done.29
  59.3 2.4 %collective-permute-start.17 = (bf16[128,1280]{1,0:T(8,128)(2,1)S(1)}, bf16[128,1280]{1,0:T(8,128)(2,1)S(1)}, u32[]{:S(2)}, u32[]{:S(2)}) collective-permute-start(bf16[128,1280]{1,0:T(8,128)(2,1)S(1)} %collective-permute-done.15.refs_4_), channel_id=1, source_target_pairs={{0,2},{1,3},{2,0},{3,1},{12,14},{13,15},{14,12},{15,13},{16,18},{1... | collective-permute-start | bytes 983048 | tf_op jit(solution)/shard_map/ppermute | solution.py:21
  62.0 2.4 %collective-permute-start.16 = (bf16[128,1280]{1,0:T(8,128)(2,1)S(1)}, bf16[128,1280]{1,0:T(8,128)(2,1)S(1)}, u32[]{:S(2)}, u32[]{:S(2)}) collective-permute-start(bf16[128,1280]{1,0:T(8,128)(2,1)S(1)} %collective-permute-done.15.refs_4_), channel_id=1, source_target_pairs={{0,1},{2,3},{4,5},{6,7},{9,8},{11,10},{13,12},{15,14},{16,17},{18,... | collective-permute-start | bytes 983048 | tf_op jit(solution)/shard_map/ppermute | solution.py:21
  64.4 1.3 %collective-permute-start.14 = (bf16[128,1280]{1,0:T(8,128)(2,1)S(1)}, bf16[128,1280]{1,0:T(8,128)(2,1)S(1)}, u32[]{:S(2)}, u32[]{:S(2)}) collective-permute-start(bf16[128,1280]{1,0:T(8,128)(2,1)S(1)} %collective-permute-done.13.refs_2_), channel_id=1, source_target_pairs={{0,1},{2,3},{4,5},{6,7},{9,8},{11,10},{13,12},{15,14},{16,17},{18,... | collective-permute-start | bytes 983048 | tf_op jit(solution)/shard_map/ppermute | solution.py:21
  65.8 5.0 %collective-permute-done.17.refs_6_ = bf16[128,1280]{1,0:T(8,128)(2,1)S(1)} collective-permute-done((bf16[128,1280]{1,0:T(8,128)(2,1)S(1)}, bf16[128,1280]{1,0:T(8,128)(2,1)S(1)}, u32[]{:S(2)}, u32[]{:S(2)}) %collective-permute-start.17) | collective-permute-done | bytes 327712 | tf_op jit(solution)/shard_map/ppermute | solution.py:21
  70.8 1.3 %collective-permute-start.18 = (bf16[128,1280]{1,0:T(8,128)(2,1)S(1)}, bf16[128,1280]{1,0:T(8,128)(2,1)S(1)}, u32[]{:S(2)}, u32[]{:S(2)}) collective-permute-start(bf16[128,1280]{1,0:T(8,128)(2,1)S(1)} %collective-permute-done.17.refs_6_), channel_id=1, source_target_pairs={{0,1},{2,3},{4,5},{6,7},{9,8},{11,10},{13,12},{15,14},{16,17},{18,... | collective-permute-start | bytes 983048 | tf_op jit(solution)/shard_map/ppermute | solution.py:21
  72.1 1.6 %shard_map.79 = (bf16[512,1280]{1,0:T(8,128)(2,1)S(1)}, bf16[512,320]{1,0:T(8,128)(2,1)S(1)}) custom-call(s32[5]{0:T(128)S(1)} %stack.151.places, f32[1,1280]{1,0:T(1,128)S(1)} %reshape.16.gain, bf16[128,1280]{1,0:T(8,128)(2,1)S(1)} %collective-permute-done.7.refs_0_, bf16[128,1280]{1,0:T(8,128)(2,1)S(1)} %collective-permute-done.9.refs_1_, ...), custom_call_target="tpu_custom_call" | custom-call | tf_op jit(solution)/shard_map/pallas_call | solution.py:140
  73.8 0.6 collective-permute-start.19
  74.5 1.6 %shard_map.80 = (bf16[512,1280]{1,0:T(8,128)(2,1)S(1)}, bf16[512,320]{1,0:T(8,128)(2,1)S(1)}) custom-call(s32[6]{0:T(128)S(1)} %stack.156.places, f32[1,1280]{1,0:T(1,128)S(1)} %reshape.16.gain, bf16[128,1280]{1,0:T(8,128)(2,1)S(1)} %collective-permute-done.8.refs_0_, bf16[128,1280]{1,0:T(8,128)(2,1)S(1)} %collective-permute-done.12.refs_1_, ...), custom_call_target="tpu_custom_call" | custom-call | tf_op jit(solution)/shard_map/pallas_call | solution.py:140
  76.3 13.9 %shard_map.81 = (bf16[512,320]{1,0:T(8,128)(2,1)S(1)}, bf16[256,320]{1,0:T(8,128)(2,1)S(1)}, bf16[256,320]{1,0:T(8,128)(2,1)S(1)}) custom-call(s32[22]{0:T(128)S(1)} %stack.145.places, bf16[512,1280]{1,0:T(8,128)(2,1)S(1)} %get-tuple-element.25.refs_0_, bf16[512,320]{1,0:T(8,128)(2,1)S(1)} %get-tuple-element.26.refs_1_, ...), custom_call_target="tpu_custom_call" | custom-call | tf_op jit(solution)/shard_map/pallas_call | solution.py:281
  90.3 0.8 copy-done.15
  91.0 0.7 collective-permute-start.31
  91.7 0.6 collective-permute-start.32
  92.3 0.6 pad_add_fusion.1.place
  92.9 3.9 %shard_map.82 = (f32[8,512]{1,0:T(8,128)}, f32[8,512]{1,0:T(8,128)}, f32[8,512]{1,0:T(8,128)}, f32[8,512]{1,0:T(8,128)}) custom-call(s32[4]{0:T(128)} %pad_add_fusion.1.place, bf16[512,320]{1,0:T(8,128)(2,1)} %copy-done.15, bf16[80,1024]{1,0:T(8,128)(2,1)} %copy-done, bf16[80,1024]{1,0:T(8,128)(2,1)} %copy-done, bf16[80,1024]{1,0:T(8,128)(2,1)} %copy-done.13, ...), custom_call_target="tpu_custom_call" | custom-call | tf_op jit(solution)/shard_map/pallas_call | solution.py:371
  96.8 1.5 %collective-permute-start.35 = (f32[8,512]{1,0:T(8,128)}, f32[8,512]{1,0:T(8,128)S(1)}, u32[]{:S(2)}, u32[]{:S(2)}) collective-permute-start(f32[8,512]{1,0:T(8,128)} %get-tuple-element.41), channel_id=1, source_target_pairs={{0,8},{1,9},{2,10},{3,11},{4,12},{5,13},{6,14},{7,15},{8,0},{9,1},... | collective-permute-start | bytes 49160 | tf_op jit(solution)/shard_map/ppermute | solution.py:21
  98.3 2.4 %collective-permute-start.36 = (f32[8,512]{1,0:T(8,128)}, f32[8,512]{1,0:T(8,128)S(1)}, u32[]{:S(2)}, u32[]{:S(2)}) collective-permute-start(f32[8,512]{1,0:T(8,128)} %get-tuple-element.42), channel_id=1, source_target_pairs={{0,1},{1,0},{2,3},{3,2},{4,5},{5,4},{6,7},{7,6},{8,9},{9,8},{10,11... | collective-permute-start | bytes 49160 | tf_op jit(solution)/shard_map/ppermute | solution.py:21
  100.7 1.5 %collective-permute-start.37 = (f32[8,512]{1,0:T(8,128)}, f32[8,512]{1,0:T(8,128)S(1)}, u32[]{:S(2)}, u32[]{:S(2)}) collective-permute-start(f32[8,512]{1,0:T(8,128)} %get-tuple-element.43), channel_id=1, source_target_pairs={{0,9},{1,8},{2,11},{3,10},{4,13},{5,12},{6,15},{7,14},{8,1},{9,0},... | collective-permute-start | bytes 49160 | tf_op jit(solution)/shard_map/ppermute | solution.py:21
  102.3 2.8 %collective-permute-done.37.refs_3_ = f32[8,512]{1,0:T(8,128)S(1)} collective-permute-done((f32[8,512]{1,0:T(8,128)}, f32[8,512]{1,0:T(8,128)S(1)}, u32[]{:S(2)}, u32[]{:S(2)}) %collective-permute-start.37) | collective-permute-done | bytes 16416 | tf_op jit(solution)/shard_map/ppermute | solution.py:21
  105.0 0.6 copy-done.20
  105.6 1.5 %shard_map.83 = (bf16[2,384]{1,0:T(2,128)(2,1)}, bf16[2,384]{1,0:T(2,128)(2,1)}, bf16[2,384]{1,0:T(2,128)(2,1)}, bf16[2,384]{1,0:T(2,128)(2,1)}) custom-call(f32[8,512]{1,0:T(8,128)} %get-tuple-element.40.refs_0_, f32[8,512]{1,0:T(8,128)} %copy-done.18, f32[8,512]{1,0:T(8,128)} %copy-done.19, f32[8,512]{1,0:T(8,128)} %copy-done.20), custom_call_target="tpu_custom_call" | custom-call | tf_op jit(solution)/shard_map/pallas_call | solution.py:404
  107.2 1.5 %collective-permute-start.38 = (bf16[2,384]{1,0:T(2,128)(2,1)}, bf16[2,384]{1,0:T(2,128)(2,1)S(1)}, u32[]{:S(2)}, u32[]{:S(2)}) collective-permute-start(bf16[2,384]{1,0:T(2,128)(2,1)} %get-tuple-element.45), channel_id=1, source_target_pairs={{0,2},{1,3},{2,0},{3,1},{4,6},{5,7},{6,4},{7,5},{8,10},{9,11},{10,... | collective-permute-start | bytes 4616 | tf_op jit(solution)/shard_map/ppermute | solution.py:21
  108.6 1.9 %collective-permute-start.39 = (bf16[2,384]{1,0:T(2,128)(2,1)}, bf16[2,384]{1,0:T(2,128)(2,1)S(1)}, u32[]{:S(2)}, u32[]{:S(2)}) collective-permute-start(bf16[2,384]{1,0:T(2,128)(2,1)} %get-tuple-element.46), channel_id=1, source_target_pairs={{0,4},{1,5},{2,6},{3,7},{4,0},{5,1},{6,2},{7,3},{8,12},{9,13},{10,... | collective-permute-start | bytes 4616 | tf_op jit(solution)/shard_map/ppermute | solution.py:21
  110.5 0.1 collective-permute-start.40
  110.8 0.5 collective-permute-start.34
  111.3 1.1 collective-permute-done.39
  112.4 2.8 %collective-permute-done.40 = bf16[2,384]{1,0:T(2,128)(2,1)S(1)} collective-permute-done((bf16[2,384]{1,0:T(2,128)(2,1)}, bf16[2,384]{1,0:T(2,128)(2,1)S(1)}, u32[]{:S(2)}, u32[]{:S(2)}) %collective-permute-start.40) | collective-permute-done | bytes 1568 | tf_op jit(solution)/shard_map/ppermute | solution.py:21
  115.2 0.7 broadcast_select_fusion.6
  116.0 0.7 concatenate.15
  116.7 0.1 select_select_fusion
  116.9 0.8 concatenate.14
  (118 shorter events, 1.4 us)
Async XLA Ops:
  0.6 13.2 %collective-permute-start.7 = (bf16[128,1280]{1,0:T(8,128)(2,1)}, bf16[128,1280]{1,0:T(8,128)(2,1)S(1)}, u32[]{:S(2)}, u32[]{:S(2)}) collective-permute-start(bf16[128,1280]{1,0:T(8,128)(2,1)} %refs_0_.2), channel_id=1, source_target_pairs={{0,4},{1,5},{2,6},{3,7},{4,0},{5,1},{6,2},{7,3},{8,12},{9,13},{10,... | collective-permute-start | bytes 983048 | tf_op jit(solution)/shard_map/ppermute | solution.py:21
  3.7 10.1 %collective-permute-start.8 = (bf16[128,1280]{1,0:T(8,128)(2,1)}, bf16[128,1280]{1,0:T(8,128)(2,1)S(1)}, u32[]{:S(2)}, u32[]{:S(2)}) collective-permute-start(bf16[128,1280]{1,0:T(8,128)(2,1)} %refs_0_.2), channel_id=1, source_target_pairs={{4,8},{5,9},{6,10},{7,11},{8,4},{9,5},{10,6},{11,7},{20,24},{21,25... | collective-permute-start | bytes 983048 | tf_op jit(solution)/shard_map/ppermute | solution.py:21
  4.4 1.8 %collective-permute-start.3 = (bf16[2,1280]{1,0:T(2,128)(2,1)}, bf16[2,1280]{1,0:T(2,128)(2,1)S(1)}, u32[]{:S(2)}, u32[]{:S(2)}) collective-permute-start(bf16[2,1280]{1,0:T(2,128)(2,1)} %refs_0_.3), channel_id=1, source_target_pairs={{0,1},{1,0},{2,3},{3,2},{4,5},{5,4},{6,7},{7,6},{8,9},{9,8},{10,11... | collective-permute-start | bytes 15368 | tf_op jit(solution)/shard_map/ppermute | solution.py:21
  4.5 1.5 %collective-permute-start.4 = (s32[2,16]{1,0:T(2,128)}, s32[2,16]{1,0:T(2,128)S(1)}, u32[]{:S(2)}, u32[]{:S(2)}) collective-permute-start(s32[2,16]{1,0:T(2,128)} %refs_2_.1), channel_id=1, source_target_pairs={{0,1},{1,0},{2,3},{3,2},{4,5},{5,4},{6,7},{7,6},{8,9},{9,8},{10,11... | collective-permute-start | bytes 392 | tf_op jit(solution)/shard_map/ppermute | solution.py:21
  5.0 1.3 %collective-permute-start.5 = (s32[1,128]{1,0:T(1,128)}, s32[1,128]{1,0:T(1,128)S(1)}, u32[]{:S(2)}, u32[]{:S(2)}) collective-permute-start(s32[1,128]{1,0:T(1,128)} %bitcast.39), channel_id=1, source_target_pairs={{0,1},{1,0},{2,3},{3,2},{4,5},{5,4},{6,7},{7,6},{8,9},{9,8},{10,11... | collective-permute-start | bytes 1544 | tf_op jit(solution)/shard_map/ppermute | solution.py:21
  6.8 0.6 copy-start.22
  9.8 10.8 %collective-permute-start.6 = (bf16[2,80,1024]{2,1,0:T(8,128)(2,1)}, bf16[2,80,1024]{2,1,0:T(8,128)(2,1)S(1)}, u32[]{:S(2)}, u32[]{:S(2)}) collective-permute-start(bf16[2,80,1024]{2,1,0:T(8,128)(2,1)} %get-tuple-element.28), channel_id=1, source_target_pairs={{0,2},{2,0},{4,6},{6,4},{8,10},{10,8},{12,14},{14,12},{17,19},{19,... | collective-permute-start | bytes 983048 | tf_op jit(solution)/shard_map/ppermute | solution.py:458
  13.2 20.0 %collective-permute-start.1 = (bf16[128,1280]{1,0:T(8,128)(2,1)}, bf16[128,1280]{1,0:T(8,128)(2,1)S(1)}, u32[]{:S(2)}, u32[]{:S(2)}) collective-permute-start(bf16[128,1280]{1,0:T(8,128)(2,1)} %refs_0_.2), channel_id=1, source_target_pairs={{0,2},{1,3},{2,0},{3,1},{4,6},{5,7},{6,4},{7,5},{8,10},{9,11},{10,... | collective-permute-start | bytes 983048 | tf_op jit(solution)/shard_map/ppermute | solution.py:21
  20.6 12.2 %copy-start.16 = (bf16[128,1280]{1,0:T(8,128)(2,1)S(1)}, bf16[128,1280]{1,0:T(8,128)(2,1)}, u32[]{:S(2)}) copy-start(bf16[128,1280]{1,0:T(8,128)(2,1)} %refs_0_.2) | copy-start | bytes 983044
  20.6 12.3 %copy-start.21 = (f32[1280]{0:T(1024)S(1)}, f32[1280]{0:T(1024)}, u32[]{:S(2)}) copy-start(f32[1280]{0:T(1024)} %param.7) | copy-start | bytes 15364
  20.6 20.6 %copy-start.17 = (bf16[2,80,1024]{2,1,0:T(8,128)(2,1)S(1)}, bf16[2,80,1024]{2,1,0:T(8,128)(2,1)}, u32[]{:S(2)}) copy-start(bf16[2,80,1024]{2,1,0:T(8,128)(2,1)} %get-tuple-element.35) | copy-start | bytes 983044
  22.4 17.4 %collective-permute-start.22 = (bf16[160,1024]{1,0:T(8,128)(2,1)}, bf16[160,1024]{1,0:T(8,128)(2,1)S(1)}, u32[]{:S(2)}, u32[]{:S(2)}) collective-permute-start(bf16[160,1024]{1,0:T(8,128)(2,1)} %bitcast.32), channel_id=1, source_target_pairs={{0,4},{2,6},{4,0},{6,2},{8,12},{10,14},{12,8},{14,10},{17,21},{19,... | collective-permute-start | bytes 983048 | tf_op jit(solution)/shard_map/ppermute | solution.py:458
  29.5 13.0 %collective-permute-start.25 = (bf16[160,1024]{1,0:T(8,128)(2,1)}, bf16[160,1024]{1,0:T(8,128)(2,1)S(1)}, u32[]{:S(2)}, u32[]{:S(2)}) collective-permute-start(bf16[160,1024]{1,0:T(8,128)(2,1)} %bitcast.33), channel_id=1, source_target_pairs={{0,8},{2,10},{4,12},{6,14},{8,0},{10,2},{12,4},{14,6},{17,25},{19,... | collective-permute-start | bytes 983048 | tf_op jit(solution)/shard_map/ppermute | solution.py:458
  31.4 4.1 %collective-permute-start.20 = (bf16[80,1024]{1,0:T(8,128)(2,1)S(1)}, bf16[80,1024]{1,0:T(8,128)(2,1)S(1)}, u32[]{:S(2)}, u32[]{:S(2)}) collective-permute-start(bf16[80,1024]{1,0:T(8,128)(2,1)S(1)} %dynamic-slice_bitcast_fusion), channel_id=1, source_target_pairs={{0,16},{2,18},{4,20},{6,22},{8,24},{10,26},{12,28},{14,30},{17,1},... | collective-permute-start | bytes 491528 | tf_op jit(solution)/shard_map/ppermute | solution.py:458
  32.7 11.1 %collective-permute-start = (bf16[128,1280]{1,0:T(8,128)(2,1)S(1)}, bf16[128,1280]{1,0:T(8,128)(2,1)S(1)}, u32[]{:S(2)}, u32[]{:S(2)}) collective-permute-start(bf16[128,1280]{1,0:T(8,128)(2,1)S(1)} %copy-done.16), channel_id=1, source_target_pairs={{0,1},{1,0},{2,3},{3,2},{4,5},{5,4},{6,7},{7,6},{8,9},{9,8},{10,11... | collective-permute-start | bytes 983048 | tf_op jit(solution)/shard_map/ppermute | solution.py:21
  33.2 10.7 %collective-permute-start.2 = (bf16[128,1280]{1,0:T(8,128)(2,1)S(1)}, bf16[128,1280]{1,0:T(8,128)(2,1)S(1)}, u32[]{:S(2)}, u32[]{:S(2)}) collective-permute-start(bf16[128,1280]{1,0:T(8,128)(2,1)S(1)} %collective-permute-done.1.refs_2_), channel_id=1, source_target_pairs={{0,1},{1,0},{2,3},{3,2},{4,5},{5,4},{6,7},{7,6},{8,9},{9,8},{10,11... | collective-permute-start | bytes 983048 | tf_op jit(solution)/shard_map/ppermute | solution.py:21
  35.5 11.5 %collective-permute-start.28 = (bf16[160,1024]{1,0:T(8,128)(2,1)}, bf16[160,1024]{1,0:T(8,128)(2,1)S(1)}, u32[]{:S(2)}, u32[]{:S(2)}) collective-permute-start(bf16[160,1024]{1,0:T(8,128)(2,1)} %bitcast.32), channel_id=1, source_target_pairs={{0,12},{2,14},{4,8},{6,10},{8,4},{10,6},{12,0},{14,2},{17,29},{19,... | collective-permute-start | bytes 983048 | tf_op jit(solution)/shard_map/ppermute | solution.py:458
  39.8 8.6 %collective-permute-start.23 = (bf16[160,1024]{1,0:T(8,128)(2,1)S(1)}, bf16[160,1024]{1,0:T(8,128)(2,1)S(1)}, u32[]{:S(2)}, u32[]{:S(2)}) collective-permute-start(bf16[160,1024]{1,0:T(8,128)(2,1)S(1)} %collective-permute-done.22), channel_id=1, source_target_pairs={{0,16},{2,18},{4,20},{6,22},{8,24},{10,26},{12,28},{14,30},{17,1},... | collective-permute-start | bytes 983048 | tf_op jit(solution)/shard_map/ppermute | solution.py:458
  41.2 35.1 %copy-start = (bf16[80,1024]{1,0:T(8,128)(2,1)}, bf16[80,1024]{1,0:T(8,128)(2,1)S(1)}, u32[]{:S(2)}) copy-start(bf16[80,1024]{1,0:T(8,128)(2,1)S(1)} %dynamic-slice_bitcast_fusion.1.refs_6_.refs_0_.refs_1_) | copy-start | bytes 491524
  42.5 12.3 %collective-permute-start.26 = (bf16[160,1024]{1,0:T(8,128)(2,1)S(1)}, bf16[160,1024]{1,0:T(8,128)(2,1)S(1)}, u32[]{:S(2)}, u32[]{:S(2)}) collective-permute-start(bf16[160,1024]{1,0:T(8,128)(2,1)S(1)} %collective-permute-done.25), channel_id=1, source_target_pairs={{0,16},{2,18},{4,20},{6,22},{8,24},{10,26},{12,28},{14,30},{17,1},... | collective-permute-start | bytes 983048 | tf_op jit(solution)/shard_map/ppermute | solution.py:458
  43.8 32.4 %copy-start.13 = (bf16[80,1024]{1,0:T(8,128)(2,1)}, bf16[80,1024]{1,0:T(8,128)(2,1)S(1)}, u32[]{:S(2)}) copy-start(bf16[80,1024]{1,0:T(8,128)(2,1)S(1)} %broadcast_select_fusion.3.refs_8_.refs_2_) | copy-start | bytes 491524
  43.9 17.9 %collective-permute-start.9 = (bf16[128,1280]{1,0:T(8,128)(2,1)S(1)}, bf16[128,1280]{1,0:T(8,128)(2,1)S(1)}, u32[]{:S(2)}, u32[]{:S(2)}) collective-permute-start(bf16[128,1280]{1,0:T(8,128)(2,1)S(1)} %collective-permute-done.7.refs_0_), channel_id=1, source_target_pairs={{0,1},{1,0},{2,3},{3,2},{4,5},{5,4},{6,7},{7,6},{8,9},{9,8},{10,11... | collective-permute-start | bytes 983048 | tf_op jit(solution)/shard_map/ppermute | solution.py:21
  43.9 12.2 %collective-permute-start.10 = (bf16[128,1280]{1,0:T(8,128)(2,1)S(1)}, bf16[128,1280]{1,0:T(8,128)(2,1)S(1)}, u32[]{:S(2)}, u32[]{:S(2)}) collective-permute-start(bf16[128,1280]{1,0:T(8,128)(2,1)S(1)} %collective-permute-done.7.refs_0_), channel_id=1, source_target_pairs={{0,2},{1,3},{2,0},{3,1},{4,6},{5,7},{6,4},{7,5},{8,10},{9,11},{10,... | collective-permute-start | bytes 983048 | tf_op jit(solution)/shard_map/ppermute | solution.py:21
  47.1 11.7 %collective-permute-start.15 = (bf16[128,1280]{1,0:T(8,128)(2,1)S(1)}, bf16[128,1280]{1,0:T(8,128)(2,1)S(1)}, u32[]{:S(2)}, u32[]{:S(2)}) collective-permute-start(bf16[128,1280]{1,0:T(8,128)(2,1)S(1)} %collective-permute-done.8.refs_0_), channel_id=1, source_target_pairs={{4,0},{5,1},{6,2},{7,3},{8,12},{9,13},{10,14},{11,15},{20,16},{21,... | collective-permute-start | bytes 983048 | tf_op jit(solution)/shard_map/ppermute | solution.py:21
  48.4 10.9 %collective-permute-start.29 = (bf16[160,1024]{1,0:T(8,128)(2,1)S(1)}, bf16[160,1024]{1,0:T(8,128)(2,1)S(1)}, u32[]{:S(2)}, u32[]{:S(2)}) collective-permute-start(bf16[160,1024]{1,0:T(8,128)(2,1)S(1)} %collective-permute-done.28), channel_id=1, source_target_pairs={{0,16},{2,18},{4,20},{6,22},{8,24},{10,26},{12,28},{14,30},{17,1},... | collective-permute-start | bytes 983048 | tf_op jit(solution)/shard_map/ppermute | solution.py:458
  54.8 7.2 %collective-permute-start.12 = (bf16[128,1280]{1,0:T(8,128)(2,1)S(1)}, bf16[128,1280]{1,0:T(8,128)(2,1)S(1)}, u32[]{:S(2)}, u32[]{:S(2)}) collective-permute-start(bf16[128,1280]{1,0:T(8,128)(2,1)S(1)} %collective-permute-done.8.refs_0_), channel_id=1, source_target_pairs={{0,1},{2,3},{4,5},{6,7},{9,8},{11,10},{13,12},{15,14},{16,17},{18,... | collective-permute-start | bytes 983048 | tf_op jit(solution)/shard_map/ppermute | solution.py:21
  56.1 8.2 %collective-permute-start.13 = (bf16[128,1280]{1,0:T(8,128)(2,1)S(1)}, bf16[128,1280]{1,0:T(8,128)(2,1)S(1)}, u32[]{:S(2)}, u32[]{:S(2)}) collective-permute-start(bf16[128,1280]{1,0:T(8,128)(2,1)S(1)} %collective-permute-done.8.refs_0_), channel_id=1, source_target_pairs={{4,6},{5,7},{6,4},{7,5},{8,10},{9,11},{10,8},{11,9},{20,22},{21,23... | collective-permute-start | bytes 983048 | tf_op jit(solution)/shard_map/ppermute | solution.py:21
  58.7 7.0 %collective-permute-start.11 = (bf16[128,1280]{1,0:T(8,128)(2,1)S(1)}, bf16[128,1280]{1,0:T(8,128)(2,1)S(1)}, u32[]{:S(2)}, u32[]{:S(2)}) collective-permute-start(bf16[128,1280]{1,0:T(8,128)(2,1)S(1)} %collective-permute-done.10.refs_2_), channel_id=1, source_target_pairs={{0,1},{1,0},{2,3},{3,2},{4,5},{5,4},{6,7},{7,6},{8,9},{9,8},{10,11... | collective-permute-start | bytes 983048 | tf_op jit(solution)/shard_map/ppermute | solution.py:21
  59.3 11.5 %collective-permute-start.17 = (bf16[128,1280]{1,0:T(8,128)(2,1)S(1)}, bf16[128,1280]{1,0:T(8,128)(2,1)S(1)}, u32[]{:S(2)}, u32[]{:S(2)}) collective-permute-start(bf16[128,1280]{1,0:T(8,128)(2,1)S(1)} %collective-permute-done.15.refs_4_), channel_id=1, source_target_pairs={{0,2},{1,3},{2,0},{3,1},{12,14},{13,15},{14,12},{15,13},{16,18},{1... | collective-permute-start | bytes 983048 | tf_op jit(solution)/shard_map/ppermute | solution.py:21
  61.8 14.5 %copy-start.1 = (bf16[80,1024]{1,0:T(8,128)(2,1)}, bf16[80,1024]{1,0:T(8,128)(2,1)S(1)}, u32[]{:S(2)}) copy-start(bf16[80,1024]{1,0:T(8,128)(2,1)S(1)} %get-tuple-element.66.refs_12_.refs_6_) | copy-start | bytes 491524
  61.8 14.5 %copy-start.2 = (bf16[80,1024]{1,0:T(8,128)(2,1)}, bf16[80,1024]{1,0:T(8,128)(2,1)S(1)}, u32[]{:S(2)}) copy-start(bf16[80,1024]{1,0:T(8,128)(2,1)S(1)} %get-tuple-element.67.refs_10_.refs_4_) | copy-start | bytes 491524
  61.8 11.9 %collective-permute-start.24 = (bf16[160,1024]{1,0:T(8,128)(2,1)S(1)}, bf16[160,1024]{1,0:T(8,128)(2,1)S(1)}, u32[]{:S(2)}, u32[]{:S(2)}) collective-permute-start(bf16[160,1024]{1,0:T(8,128)(2,1)S(1)} %broadcast_select_fusion.2), channel_id=1, source_target_pairs={{0,1},{1,0},{2,3},{3,2},{4,5},{5,4},{6,7},{7,6},{8,9},{9,8},{10,11... | collective-permute-start | bytes 983048 | tf_op jit(solution)/shard_map/ppermute | solution.py:21
  61.9 14.4 %copy-start.3 = (bf16[80,1024]{1,0:T(8,128)(2,1)}, bf16[80,1024]{1,0:T(8,128)(2,1)S(1)}, u32[]{:S(2)}) copy-start(bf16[80,1024]{1,0:T(8,128)(2,1)S(1)} %get-tuple-element.58.refs_16_.refs_10_) | copy-start | bytes 491524
  61.9 14.4 %copy-start.4 = (bf16[80,1024]{1,0:T(8,128)(2,1)}, bf16[80,1024]{1,0:T(8,128)(2,1)S(1)}, u32[]{:S(2)}) copy-start(bf16[80,1024]{1,0:T(8,128)(2,1)S(1)} %get-tuple-element.59.refs_14_.refs_8_) | copy-start | bytes 491524
  62.0 12.4 %collective-permute-start.16 = (bf16[128,1280]{1,0:T(8,128)(2,1)S(1)}, bf16[128,1280]{1,0:T(8,128)(2,1)S(1)}, u32[]{:S(2)}, u32[]{:S(2)}) collective-permute-start(bf16[128,1280]{1,0:T(8,128)(2,1)S(1)} %collective-permute-done.15.refs_4_), channel_id=1, source_target_pairs={{0,1},{2,3},{4,5},{6,7},{9,8},{11,10},{13,12},{15,14},{16,17},{18,... | collective-permute-start | bytes 983048 | tf_op jit(solution)/shard_map/ppermute | solution.py:21
  64.4 9.4 %collective-permute-start.14 = (bf16[128,1280]{1,0:T(8,128)(2,1)S(1)}, bf16[128,1280]{1,0:T(8,128)(2,1)S(1)}, u32[]{:S(2)}, u32[]{:S(2)}) collective-permute-start(bf16[128,1280]{1,0:T(8,128)(2,1)S(1)} %collective-permute-done.13.refs_2_), channel_id=1, source_target_pairs={{0,1},{2,3},{4,5},{6,7},{9,8},{11,10},{13,12},{15,14},{16,17},{18,... | collective-permute-start | bytes 983048 | tf_op jit(solution)/shard_map/ppermute | solution.py:21
  65.7 10.4 %collective-permute-start.27 = (bf16[160,1024]{1,0:T(8,128)(2,1)S(1)}, bf16[160,1024]{1,0:T(8,128)(2,1)S(1)}, u32[]{:S(2)}, u32[]{:S(2)}) collective-permute-start(bf16[160,1024]{1,0:T(8,128)(2,1)S(1)} %broadcast_select_fusion.1), channel_id=1, source_target_pairs={{0,1},{1,0},{2,3},{3,2},{4,5},{5,4},{6,7},{7,6},{8,9},{9,8},{10,11... | collective-permute-start | bytes 983048 | tf_op jit(solution)/shard_map/ppermute | solution.py:21
  70.8 3.7 %collective-permute-start.18 = (bf16[128,1280]{1,0:T(8,128)(2,1)S(1)}, bf16[128,1280]{1,0:T(8,128)(2,1)S(1)}, u32[]{:S(2)}, u32[]{:S(2)}) collective-permute-start(bf16[128,1280]{1,0:T(8,128)(2,1)S(1)} %collective-permute-done.17.refs_6_), channel_id=1, source_target_pairs={{0,1},{2,3},{4,5},{6,7},{9,8},{11,10},{13,12},{15,14},{16,17},{18,... | collective-permute-start | bytes 983048 | tf_op jit(solution)/shard_map/ppermute | solution.py:21
  72.1 4.2 %copy-start.5 = (bf16[80,1024]{1,0:T(8,128)(2,1)}, bf16[80,1024]{1,0:T(8,128)(2,1)S(1)}, u32[]{:S(2)}) copy-start(bf16[80,1024]{1,0:T(8,128)(2,1)S(1)} %get-tuple-element.54.refs_20_.refs_14_) | copy-start | bytes 491524
  72.1 4.2 %copy-start.6 = (bf16[80,1024]{1,0:T(8,128)(2,1)}, bf16[80,1024]{1,0:T(8,128)(2,1)S(1)}, u32[]{:S(2)}) copy-start(bf16[80,1024]{1,0:T(8,128)(2,1)S(1)} %get-tuple-element.55.refs_18_.refs_12_) | copy-start | bytes 491524
  73.7 2.4 %collective-permute-start.30 = (bf16[160,1024]{1,0:T(8,128)(2,1)S(1)}, bf16[160,1024]{1,0:T(8,128)(2,1)S(1)}, u32[]{:S(2)}, u32[]{:S(2)}) collective-permute-start(bf16[160,1024]{1,0:T(8,128)(2,1)S(1)} %broadcast_select_fusion), channel_id=1, source_target_pairs={{0,1},{1,0},{2,3},{3,2},{4,5},{5,4},{6,7},{7,6},{8,9},{9,8},{10,11... | collective-permute-start | bytes 983048 | tf_op jit(solution)/shard_map/ppermute | solution.py:21
  73.8 2.5 %copy-start.7 = (bf16[80,1024]{1,0:T(8,128)(2,1)}, bf16[80,1024]{1,0:T(8,128)(2,1)S(1)}, u32[]{:S(2)}) copy-start(bf16[80,1024]{1,0:T(8,128)(2,1)S(1)} %get-tuple-element.64.refs_13_.refs_7_) | copy-start | bytes 491524
  73.8 2.5 %copy-start.8 = (bf16[80,1024]{1,0:T(8,128)(2,1)}, bf16[80,1024]{1,0:T(8,128)(2,1)S(1)}, u32[]{:S(2)}) copy-start(bf16[80,1024]{1,0:T(8,128)(2,1)S(1)} %get-tuple-element.65.refs_11_.refs_5_) | copy-start | bytes 491524
  73.8 2.4 %collective-permute-start.19 = (bf16[80,1024]{1,0:T(8,128)(2,1)S(1)}, bf16[80,1024]{1,0:T(8,128)(2,1)S(1)}, u32[]{:S(2)}, u32[]{:S(2)}) collective-permute-start(bf16[80,1024]{1,0:T(8,128)(2,1)S(1)} %dynamic-slice_bitcast_fusion.1.refs_6_.refs_0_.refs_1_), channel_id=1, source_target_pairs={{0,1},{1,0},{2,3},{3,2},{4,5},{5,4},{6,7},{7,6},{8,9},{9,8},{10,11... | collective-permute-start | bytes 491528 | tf_op jit(solution)/shard_map/ppermute | solution.py:21
  74.4 1.8 %collective-permute-start.21 = (bf16[80,1024]{1,0:T(8,128)(2,1)S(1)}, bf16[80,1024]{1,0:T(8,128)(2,1)S(1)}, u32[]{:S(2)}, u32[]{:S(2)}) collective-permute-start(bf16[80,1024]{1,0:T(8,128)(2,1)S(1)} %broadcast_select_fusion.3.refs_8_.refs_2_), channel_id=1, source_target_pairs={{0,1},{1,0},{2,3},{3,2},{4,5},{5,4},{6,7},{7,6},{8,9},{9,8},{10,11... | collective-permute-start | bytes 491528 | tf_op jit(solution)/shard_map/ppermute | solution.py:21
  76.1 14.1 %copy-start.9 = (bf16[80,1024]{1,0:T(8,128)(2,1)}, bf16[80,1024]{1,0:T(8,128)(2,1)S(1)}, u32[]{:S(2)}) copy-start(bf16[80,1024]{1,0:T(8,128)(2,1)S(1)} %get-tuple-element.56.refs_17_.refs_11_) | copy-start | bytes 491524
  76.1 14.1 %copy-start.10 = (bf16[80,1024]{1,0:T(8,128)(2,1)}, bf16[80,1024]{1,0:T(8,128)(2,1)S(1)}, u32[]{:S(2)}) copy-start(bf16[80,1024]{1,0:T(8,128)(2,1)S(1)} %get-tuple-element.57.refs_15_.refs_9_) | copy-start | bytes 491524
  76.2 14.1 %copy-start.11 = (bf16[80,1024]{1,0:T(8,128)(2,1)}, bf16[80,1024]{1,0:T(8,128)(2,1)S(1)}, u32[]{:S(2)}) copy-start(bf16[80,1024]{1,0:T(8,128)(2,1)S(1)} %get-tuple-element.52.refs_21_.refs_15_) | copy-start | bytes 491524
  76.2 14.1 %copy-start.12 = (bf16[80,1024]{1,0:T(8,128)(2,1)}, bf16[80,1024]{1,0:T(8,128)(2,1)S(1)}, u32[]{:S(2)}) copy-start(bf16[80,1024]{1,0:T(8,128)(2,1)S(1)} %get-tuple-element.53.refs_19_.refs_13_) | copy-start | bytes 491524
  76.2 14.0 %copy-start.14 = (bf16[80,1024]{1,0:T(8,128)(2,1)}, bf16[80,1024]{1,0:T(8,128)(2,1)S(1)}, u32[]{:S(2)}) copy-start(bf16[80,1024]{1,0:T(8,128)(2,1)S(1)} %collective-permute-done.21.refs_9_.refs_3_) | copy-start | bytes 491524
  90.3 0.8 copy-start.15
  91.0 19.6 %collective-permute-start.31 = (bf16[256,320]{1,0:T(8,128)(2,1)S(1)}, bf16[256,320]{1,0:T(8,128)(2,1)S(1)}, u32[]{:S(2)}, u32[]{:S(2)}) collective-permute-start(bf16[256,320]{1,0:T(8,128)(2,1)S(1)} %get-tuple-element.37), channel_id=1, source_target_pairs={{0,0},{1,4},{2,2},{3,6},{4,1},{5,5},{6,3},{7,7},{8,8},{9,12},{10,1... | collective-permute-start | bytes 491528 | tf_op jit(solution)/shard_map/ppermute | solution.py:21
  91.7 19.0 %collective-permute-start.32 = (bf16[256,320]{1,0:T(8,128)(2,1)S(1)}, bf16[256,320]{1,0:T(8,128)(2,1)S(1)}, u32[]{:S(2)}, u32[]{:S(2)}) collective-permute-start(bf16[256,320]{1,0:T(8,128)(2,1)S(1)} %get-tuple-element.38), channel_id=1, source_target_pairs={{0,2},{1,6},{2,0},{3,4},{4,3},{5,7},{6,1},{7,5},{8,10},{9,14},{10,... | collective-permute-start | bytes 491528 | tf_op jit(solution)/shard_map/ppermute | solution.py:21
  96.8 5.4 %collective-permute-start.35 = (f32[8,512]{1,0:T(8,128)}, f32[8,512]{1,0:T(8,128)S(1)}, u32[]{:S(2)}, u32[]{:S(2)}) collective-permute-start(f32[8,512]{1,0:T(8,128)} %get-tuple-element.41), channel_id=1, source_target_pairs={{0,8},{1,9},{2,10},{3,11},{4,12},{5,13},{6,14},{7,15},{8,0},{9,1},... | collective-permute-start | bytes 49160 | tf_op jit(solution)/shard_map/ppermute | solution.py:21
  98.3 3.9 %collective-permute-start.36 = (f32[8,512]{1,0:T(8,128)}, f32[8,512]{1,0:T(8,128)S(1)}, u32[]{:S(2)}, u32[]{:S(2)}) collective-permute-start(f32[8,512]{1,0:T(8,128)} %get-tuple-element.42), channel_id=1, source_target_pairs={{0,1},{1,0},{2,3},{3,2},{4,5},{5,4},{6,7},{7,6},{8,9},{9,8},{10,11... | collective-permute-start | bytes 49160 | tf_op jit(solution)/shard_map/ppermute | solution.py:21
  100.7 4.3 %collective-permute-start.37 = (f32[8,512]{1,0:T(8,128)}, f32[8,512]{1,0:T(8,128)S(1)}, u32[]{:S(2)}, u32[]{:S(2)}) collective-permute-start(f32[8,512]{1,0:T(8,128)} %get-tuple-element.43), channel_id=1, source_target_pairs={{0,9},{1,8},{2,11},{3,10},{4,13},{5,12},{6,15},{7,14},{8,1},{9,0},... | collective-permute-start | bytes 49160 | tf_op jit(solution)/shard_map/ppermute | solution.py:21
  102.2 2.8 %copy-start.18 = (f32[8,512]{1,0:T(8,128)}, f32[8,512]{1,0:T(8,128)S(1)}, u32[]{:S(2)}) copy-start(f32[8,512]{1,0:T(8,128)S(1)} %collective-permute-done.35.refs_1_) | copy-start | bytes 49156
  102.2 2.8 %copy-start.19 = (f32[8,512]{1,0:T(8,128)}, f32[8,512]{1,0:T(8,128)S(1)}, u32[]{:S(2)}) copy-start(f32[8,512]{1,0:T(8,128)S(1)} %collective-permute-done.36.refs_2_) | copy-start | bytes 49156
  105.0 0.6 copy-start.20
  107.2 4.2 %collective-permute-start.38 = (bf16[2,384]{1,0:T(2,128)(2,1)}, bf16[2,384]{1,0:T(2,128)(2,1)S(1)}, u32[]{:S(2)}, u32[]{:S(2)}) collective-permute-start(bf16[2,384]{1,0:T(2,128)(2,1)} %get-tuple-element.45), channel_id=1, source_target_pairs={{0,2},{1,3},{2,0},{3,1},{4,6},{5,7},{6,4},{7,5},{8,10},{9,11},{10,... | collective-permute-start | bytes 4616 | tf_op jit(solution)/shard_map/ppermute | solution.py:21
  108.6 3.8 %collective-permute-start.39 = (bf16[2,384]{1,0:T(2,128)(2,1)}, bf16[2,384]{1,0:T(2,128)(2,1)S(1)}, u32[]{:S(2)}, u32[]{:S(2)}) collective-permute-start(bf16[2,384]{1,0:T(2,128)(2,1)} %get-tuple-element.46), channel_id=1, source_target_pairs={{0,4},{1,5},{2,6},{3,7},{4,0},{5,1},{6,2},{7,3},{8,12},{9,13},{10,... | collective-permute-start | bytes 4616 | tf_op jit(solution)/shard_map/ppermute | solution.py:21
  110.5 4.7 %collective-permute-start.40 = (bf16[2,384]{1,0:T(2,128)(2,1)}, bf16[2,384]{1,0:T(2,128)(2,1)S(1)}, u32[]{:S(2)}, u32[]{:S(2)}) collective-permute-start(bf16[2,384]{1,0:T(2,128)(2,1)} %get-tuple-element.47), channel_id=1, source_target_pairs={{0,6},{1,7},{2,4},{3,5},{4,2},{5,3},{6,0},{7,1},{8,14},{9,15},{10,... | collective-permute-start | bytes 4616 | tf_op jit(solution)/shard_map/ppermute | solution.py:21
  110.7 6.0 %collective-permute-start.33 = (bf16[128,320]{1,0:T(8,128)(2,1)S(1)}, bf16[128,320]{1,0:T(8,128)(2,1)S(1)}, u32[]{:S(2)}, u32[]{:S(2)}) collective-permute-start(bf16[128,320]{1,0:T(8,128)(2,1)S(1)} %constant_dynamic-slice_fusion.1), channel_id=1, source_target_pairs={{0,1},{1,0},{2,3},{3,2},{4,5},{5,4},{6,7},{7,6},{8,9},{9,8},{10,11... | collective-permute-start | bytes 245768 | tf_op jit(solution)/shard_map/ppermute | solution.py:21
  110.8 5.9 %collective-permute-start.34 = (bf16[128,320]{1,0:T(8,128)(2,1)S(1)}, bf16[128,320]{1,0:T(8,128)(2,1)S(1)}, u32[]{:S(2)}, u32[]{:S(2)}) collective-permute-start(bf16[128,320]{1,0:T(8,128)(2,1)S(1)} %constant_dynamic-slice_fusion), channel_id=1, source_target_pairs={{0,1},{1,0},{2,3},{3,2},{4,5},{5,4},{6,7},{7,6},{8,9},{9,8},{10,11... | collective-permute-start | bytes 245768 | tf_op jit(solution)/shard_map/ppermute | solution.py:21
  (2 other events, 1.1 us)

commit v4 on v3

--- a/solution.py
+++ b/solution.py
@@ -50,7 +50,7 @@
 def pack_kernel(spot, weight, *refs):
     queries, masks, segments = refs[0:2], refs[2:4], refs[4:6]
     outs, lanes = refs[6:8], refs[8]
-    x, c = spot[0], spot[1]
+    x, c = spot[6], spot[7]
     rows, width = weight.shape[0], weight.shape[1] // 3
     blocks = masks[0].shape[1]
 
@@ -113,14 +113,14 @@
     )(spot, weight, *small)
 
 
-def norm_kernel(ways, places, gain, *refs):
+def norm_kernel(ways, table, gain, *refs):
     blocks, (normed, residual) = refs[: 4 * ways], refs[4 * ways :]
-    group = places[4]
+    group = table[4]
     for i in range(4):
-        place = pl.multiple_of(places[i], 128)
+        place = pl.multiple_of(table[i], 128)
         values = blocks[i][...]
         if ways == 2:
-            first = jnp.broadcast_to(places[5], values.shape) == 1
+            first = jnp.broadcast_to(table[5], values.shape) == 1
             values = jnp.where(first, values, blocks[4 + i][...])
         values = values.astype(F32)
         mean = jnp.mean(values, axis=-1, keepdims=True)
@@ -136,7 +136,7 @@
         residual[pl.ds(place, 128), WIDE:] = jnp.where(odd, slab[:, HD:], slab[:, :HD])
 
 
-def norm_layer(places, gain, blocks):
+def norm_layer(table, gain, blocks):
     return pl.pallas_call(
         functools.partial(norm_kernel, len(blocks) // 4),
         out_shape=(
@@ -146,7 +146,7 @@
         in_specs=[SMEM] + [VMEM] * (1 + len(blocks)),
         out_specs=(VMEM, VMEM),
         compiler_params=pltpu.CompilerParams(vmem_limit_bytes=16 * 1024 * 1024),
-    )(places, gain, *blocks)
+    )(table, gain, *blocks)
 
 
 def encoder_kernel(n_parts, depth, chips, places, *refs):
@@ -156,10 +156,10 @@
     if not chips:
         given, refs = refs[0], refs[1:]
     memory, near, away, weight, ids, residual, queries, keys, values = refs
-    x, straight, first = places[3], places[4], places[5]
+    x, straight, first = places[11], places[12], places[13]
 
     for i, part in enumerate(parts):
-        row = pl.multiple_of(places[6 + i] * depth, 16)
+        row = pl.multiple_of(places[14 + i] * depth, 16)
         weight[pl.ds(row, depth), :] = part[...]
     if chips:
         ids[...] = jnp.zeros_like(ids)
@@ -170,7 +170,7 @@
             for core in range(2):
                 high = found[4 * core : 4 * core + 2]
                 marks = high * 128.0 + found[4 * core + 2 : 4 * core + 4]
-                block = places[6 + 2 * i] // 2 * 2 + core - first
+                block = places[14 + 2 * i] // 2 * 2 + core - first
 
                 @pl.when((block >= 0) & (block < 12))
                 def _():
@@ -184,7 +184,7 @@
     for slab in range(3):
         values[:, 256 * slab + 128 : 256 * slab + 256] = jnp.ones((1536, 128), BF)
     for i, (normed, kept) in enumerate(layers):
-        place = pl.multiple_of(places[i], 512)
+        place = pl.multiple_of(places[8 + i], 512)
         found = jnp.dot(normed[...], weight[:, 256:896], preferred_element_type=F32).astype(BF)
         keys[pl.ds(place, 512), :256] = found[:, :256]
         keys[pl.ds(place, 512), 256:] = found[:, 512:]
@@ -299,103 +299,88 @@
     )(places, *operands)
 
 
-def spread(columns, rows, slab):
-    lane = lax.broadcasted_iota(jnp.int32, (rows, 128), 1)
-    return jnp.where(lane < HD, columns[2 * slab], columns[min(2 * slab + 1, 4)])
-
-
-def cross_kernel(chips, place, memory, *refs):
-    tokens, out = refs[-2:]
-    count = out.shape[0]
-    parts, outs_by_owner = refs[: -2 - count // 8], refs[-2 - count // 8 : -2]
-    first, me, core, straight = place[0], place[1], place[2], place[3]
+def cross_kernel(chips, base, table, memory, *refs):
+    tokens, asked, out = refs[-3:]
+    count = asked.shape[0]
+    parts, outs = refs[: -3 - count // 8], refs[-3 - count // 8 : -3]
+    first, me, core, straight = [table[base + i] for i in range(4)]
     half = count // 2
+    tokens[...] = jnp.zeros_like(tokens)
     if chips:
+        flip = jnp.broadcast_to(core, (2, HD)) == 1
         for i in range(len(parts) // 2):
             here, there = parts[2 * i][:24, 960:], parts[2 * i + 1][:24, 960:]
-            rows = jnp.where(jnp.broadcast_to(straight, (24, HD)) == 1, here.astype(F32), there.astype(F32))
+            rows = jnp.where(
+                jnp.broadcast_to(straight, (24, HD)) == 1, here.astype(F32), there.astype(F32)
+            )
             for h in range(6):
                 low, high = rows[4 * h : 4 * h + 2], rows[4 * h + 2 : 4 * h + 4]
-                flip = jnp.broadcast_to(core, (2, HD)) == 1
-                tokens[h, 2 * i : 2 * i + 2, :] = jnp.where(flip, high, low)
-                tokens[h, half + 2 * i : half + 2 * i + 2, :] = jnp.where(flip, low, high)
+                for turn in range(2):
+                    at = half * turn + 2 * i
+                    found = jnp.where(flip, low, high) if turn else jnp.where(flip, high, low)
+                    if h < 5:
+                        tokens[count * h + at : count * h + at + 2, HD * h : HD * h + HD] = found * 0.125
+                    else:
+                        asked[at : at + 2, :] = found
     else:
-        tokens[...] = parts[0][...].astype(F32)
-    blocks = HD
-    spot = lax.broadcasted_iota(jnp.int32, (count, blocks), 1)
+        for h in range(5):
+            tokens[count * h : count * h + count, HD * h : HD * h + HD] = parts[0][h].astype(F32) * 0.125
+        asked[...] = parts[0][5].astype(F32)
+    spot = lax.broadcasted_iota(jnp.int32, (count, HD), 1)
     order = lax.broadcasted_iota(jnp.int32, (count, 1), 0)
-    relative = 2 * (lax.rem(order, half) // 2) + order // half
-    owner = relative ^ me
-    allowed = []
+    owner = (2 * (lax.rem(order, half) // 2) + order // half) ^ me
+    bias = []
     for b in range(4):
-        ask = jnp.sum(jnp.where(spot == first + b, tokens[5], 0.0), axis=-1, keepdims=True)
-        allowed.append((ask > 0.5) | (owner == first + b))
-    lane = lax.broadcasted_iota(jnp.int32, (count, 128), 1)
-    bias = jnp.concatenate(
-        [jnp.broadcast_to(jnp.where(a, 0.0, LOW), (count, 128)) for a in allowed], axis=1
+        ask = jnp.sum(jnp.where(spot == first + b, asked[...], 0.0), axis=-1, keepdims=True)
+        allowed = (ask > 0.5) | (owner == first + b)
+        bias.append(jnp.broadcast_to(jnp.where(allowed, 0.0, LOW), (count, 128)))
+    bias = jnp.concatenate(bias, axis=1)
+    bias = jnp.concatenate([bias] * 5, axis=0)
+    cross = lax.dot_general(
+        tokens[:, :GROUP].astype(BF),
+        memory[...],
+        (((1,), (1,)), ((), ())),
+        preferred_element_type=F32,
     )
-    stats = jnp.zeros((count, 128), F32)
-    for slab in range(3):
-        heads = [(tokens[h] * 0.125).astype(BF) for h in range(2 * slab, min(2 * slab + 2, 5))]
-        none = jnp.zeros_like(heads[0])
-        if slab < 2:
-            heads = [
-                jnp.concatenate([heads[0], none], axis=1),
-                jnp.concatenate([none, heads[1]], axis=1),
-            ]
-            held = memory[:, 128 * slab : 128 * slab + 128]
-        else:
-            held = memory[:, WIDE:]
-        outs = []
-        for i, head in enumerate(heads):
-            cross = lax.dot_general(
-                head, held, (((1,), (1,)), ((), ())), preferred_element_type=F32
-            )
-            cross = jnp.where(bias < 0.0, LOW, cross)
-            top = jnp.max(cross, axis=-1, keepdims=True)
-            raised = jnp.where(bias < 0.0, 0.0, jnp.exp(cross - top))
-            den = jnp.sum(raised, axis=-1, keepdims=True)
-            outs.append(jnp.dot(raised.astype(BF), held, preferred_element_type=F32))
-            stats = jnp.where(lane == 2 * slab + i, top, stats)
-            stats = jnp.where(lane == 8 + 2 * slab + i, den, stats)
-        if slab < 2:
-            out[:, 128 * slab : 128 * slab + 128] = jnp.where(lane < HD, outs[0], outs[1])
-        else:
-            out[:, WIDE:384] = jnp.concatenate([outs[0], jnp.zeros_like(outs[0])], axis=1)
-    out[:, 384:] = stats
-    for i, owned in enumerate(outs_by_owner):
-        owned[...] = out[8 * i : 8 * i + 8, :]
-
-
-def cross_partial(place, memory, parts, count, chips):
+    cross = jnp.where(bias < 0.0, LOW, cross)
+    top = jnp.max(cross, axis=-1, keepdims=True)
+    raised = jnp.where(bias < 0.0, 0.0, jnp.exp(cross - top))
+    den = jnp.sum(raised, axis=-1, keepdims=True)
+    out[...] = jnp.dot(raised.astype(BF), memory[...], preferred_element_type=F32)
+    lane = lax.broadcasted_iota(jnp.int32, (count, HD), 1)
+    for h in range(5):
+        rows = slice(count * h, count * h + count)
+        stats = jnp.where(lane == 0, top[rows], den[rows])
+        both = jnp.concatenate([out[rows, HD * h : HD * h + HD], stats], axis=1)
+        for i, owned in enumerate(outs):
+            owned[8 * h : 8 * h + 8, :] = both[8 * i : 8 * i + 8]
+
+
+def cross_partial(base, table, memory, parts, count, chips):
     return pl.pallas_call(
-        functools.partial(cross_kernel, chips),
-        out_shape=(jax.ShapeDtypeStruct((8, 512), F32),) * (count // 8),
+        functools.partial(cross_kernel, chips, base),
+        out_shape=(jax.ShapeDtypeStruct((40, 128), F32),) * (count // 8),
         in_specs=[SMEM] + [VMEM] * (1 + len(parts)),
         out_specs=(VMEM,) * (count // 8),
-        scratch_shapes=[pltpu.VMEM((6, count, HD), F32), pltpu.VMEM((count, 512), F32)],
-    )(place, memory, *parts)
+        scratch_shapes=[
+            pltpu.VMEM((5 * count, 384), F32),
+            pltpu.VMEM((count, HD), F32),
+            pltpu.VMEM((5 * count, GROUP), F32),
+        ],
+    )(table, memory, *parts)
 
 
 def merge_kernel(*refs):
     parts, outs, out = refs[:-5], refs[-5:-1], refs[-1]
-    stats = [part[:, 384:] for part in parts]
-    factors, dens = [[] for _ in parts], []
-    for head in range(5):
-        tops = [s[:, head : head + 1] for s in stats]
-        best = functools.reduce(jnp.maximum, tops)
-        den = jnp.zeros_like(best)
-        for i, s in enumerate(stats):
-            factor = jnp.exp(tops[i] - best)
-            den = den + factor * s[:, 8 + head : 9 + head]
-            factors[i].append(factor)
-        dens.append(den)
+    tops = [part[:, HD : HD + 1] for part in parts]
+    best = functools.reduce(jnp.maximum, tops)
+    total = jnp.zeros((40, 128), F32)
+    for top, part in zip(tops, parts):
+        total = total + jnp.exp(top - best) * part[...]
+    final = total[:, :HD] / total[:, HD + 1 : HD + 2]
+    heads = [final[8 * h : 8 * h + 8] for h in range(5)] + [jnp.zeros((8, HD), F32)]
     for slab in range(3):
-        span = slice(128 * slab, 128 * slab + 128)
-        total = jnp.zeros((8, 128), F32)
-        for i, part in enumerate(parts):
-            total = total + spread(factors[i], 8, slab) * part[:, span]
-        out[:, span] = total / spread(dens, 8, slab)
+        out[:, 128 * slab : 128 * slab + 128] = jnp.concatenate(heads[2 * slab : 2 * slab + 2], axis=1)
     for i in range(4):
         outs[i][...] = out[2 * i : 2 * i + 2, :].astype(BF)
 
@@ -441,27 +426,38 @@
         for j in range(4)
         if 0 <= i + s < layers
     ]
+    pair = swap(stem, n, 4)
     near = send(stem, near_route)
-    pair = swap(stem, n, 4)
     stem_x = swap(stem, n, 2)
     utts = lax.axis_size("utt")
     straight = (c == lax.axis_index("utt") % 2).astype(jnp.int32)
     gain = norm_gain.reshape(1, -1)
-    inner = [128 * (2 * x + c), 128 * (2 * x + 1 - c), 128 * (2 - 2 * x + c), 128 * (3 - 2 * x - c)]
-    spots = inner + [group]
+    direct = depth % 16 == 0 and layers == 4 and utts % 2 == 0
+    table = [128 * (2 * x + c), 128 * (2 * x + 1 - c), 128 * (2 - 2 * x + c), 128 * (3 - 2 * x - c)]
+    table += [group, p != k, x, c]
+    table += [512 * (p - c + 1), 512 * (2 - p - c), 1024 * c, x, straight, 4 * quarter - 4]
+    sources = [me ^ m for m in range(n)] if direct else [jnp.int32(0)]
+    table = scalars(table + sources + [4 * quarter, me, c, straight])
+    base = 14 + len(sources)
     extra = []
-    if depth % 16 == 0 and layers == 4 and utts % 2 == 0:
+    if direct:
         carriers = [(u, d) for u in range(utts) for d in range(n) if d % 2 == u % 2]
 
         def carry(block, turn_u, turn_d):
             route = [(u * n + d, (u ^ turn_u) * n + (d ^ turn_d)) for u, d in carriers]
             return lax.ppermute(block, ("utt", "tm"), route)
 
+        far = send(stem, [(d, d ^ 8) for d in range(n) if d // 4 in (1, 2)])
         small = [dec_queries, stretch_mask, segment_ids.reshape(1, -1)]
         both = [part for piece in small for part in (piece, swap(piece, n, 1))]
-        mine, theirs = pack(scalars([x, c]), qkv_weight, *both)
+        mine, theirs = pack(table, qkv_weight, *both)
         across = carry(theirs, 0, 2)
-        mine_late, across_late, pair, near = lax.optimization_barrier((mine, across, pair, near))
+        mine_late, across_late, pair, near, far, stem_x = lax.optimization_barrier(
+            (mine, across, pair, near, far, stem_x)
+        )
+        halo = jnp.where((z == 1) | (z == 2), near, far)
+        pair_x = swap(pair, n, 2)
+        halo_x = swap(halo, n, 2)
         ready = [
             jnp.concatenate(
                 [
@@ -472,34 +468,23 @@
             for a in range(2)
         ]
         here = {0: lax.dynamic_index_in_dim(across, p, 0, keepdims=False)}
-        for turn in (3, 2, 1):
+        for turn in (1, 2, 3):
             here[turn] = carry(ready[turn % 2], 0, 4 * turn)
+        here[3], here[2], pair_x, halo_x = lax.optimization_barrier(
+            (here[3], here[2], pair_x, halo_x)
+        )
         own_part = lax.dynamic_index_in_dim(mine, p, 0, keepdims=False)
         weights = [own_part, swap(own_part, n, 1)]
-        part_places = [me, me ^ 1]
         for turn in range(4):
             traded = carry(here[turn], 1, 0)
             got = jnp.where(straight == 1, here[turn], traded)
             beside = swap(got, n, 1)
-            pieces = got.shape[0] // depth
-            for s in range(pieces):
-                chip = me ^ (4 * turn + 2 * (s + 2 - pieces))
-                for part, source in ((got, chip), (beside, chip ^ 1)):
+            for s in range(got.shape[0] // depth):
+                for part in (got, beside):
                     weights.append(part[s * depth : s * depth + depth])
-                    part_places.append(source)
         token_parts = [own_part, own_part] + weights[2:]
-
-        beside_route = [
-            (d, d ^ 1) for d in range(n) if d % 2 == d // 8
-        ]
-        inside = [d for d in range(n) if d // 4 in (1, 2)]
-        relayed = send(near, [(d, d ^ 4) for d in inside])
-        near_x = send(near, [(d, d ^ 2) for d in inside])
-        relayed_x = send(relayed, [(d ^ 4, d ^ 6) for d in inside])
-        halo_layer = []
-        for a, b in ((near, near_x), (relayed, relayed_x)):
-            halo_layer += [a, send(a, beside_route), b, send(b, beside_route)]
-        halo_spots = spots + [(p != k).astype(jnp.int32)]
+        aside = [(d, d ^ 1) for d in range(n) if d % 2 == d // 8]
+        halo_layer = [halo, send(halo, aside), halo_x, send(halo_x, aside)]
     else:
         far = swap(near, n, 4)
         left = jnp.where(p == 0, near, far)
@@ -511,12 +496,10 @@
             jnp.where(c == 0, left_x, right_x),
             swap(jnp.where(c == 0, right_x, left_x), n, 1),
         ]
-        halo_spots = spots
         whole = lax.all_gather(qkv_weight, "tm", axis=0, tiled=True)
         grouped = jnp.stack([weight_group(whole, g) for g in range(4)])
         weights = [lax.dynamic_index_in_dim(grouped, group, 0, keepdims=False)]
         weights = [jnp.pad(weights[0], ((0, 0), (0, HD)))]
-        part_places = [jnp.int32(0)]
         depth = whole.shape[0]
         packed = jnp.stack([token_group(dec_queries, stretch_mask, g) for g in range(4)])
         every = lax.all_gather(packed, "tm", axis=0)
@@ -528,15 +511,10 @@
         marks = jnp.pad(marks, (512, 512))
         marks = lax.dynamic_slice_in_dim(marks, 512 * quarter, 1536, 0)
         extra = [jnp.broadcast_to(marks[None], (8, 1536))]
-    pair_x = swap(pair, n, 2)
+        pair_x = swap(pair, n, 2)
     own_layer = [stem, swap(stem, n, 1), stem_x, swap(stem_x, n, 1)]
     pair_layer = [pair, swap(pair, n, 1), pair_x, swap(pair_x, n, 1)]
-    layered = []
-    for blocks, at in ((own_layer, spots), (pair_layer, spots), (halo_layer, halo_spots)):
-        layered.append(norm_layer(scalars(at), gain, blocks))
-    places = [512 * (p - c + 1), 512 * (2 - p - c), 1024 * c, x, straight, 4 * quarter - 4]
-
-    table = scalars(places + part_places)
+    layered = [norm_layer(table, gain, blocks) for blocks in (own_layer, pair_layer, halo_layer)]
     held, stay, leave = encoder(table, layered, weights, depth, extra)
 
     pieces = []
@@ -554,8 +532,7 @@
         pieces.append((keep, give))
     memory = gather_groups([pieces[0][0], pieces[1][0], pieces[0][1], pieces[1][1]], 2 * c + x)
 
-    place = scalars([4 * quarter, me, c, straight])
-    partial = cross_partial(place, held, token_parts, 2 * n, len(token_parts) > 1)
+    partial = cross_partial(base, table, held, token_parts, 2 * n, direct)
     owned = [partial[0]]
     outer = n // 8
     for i in range(1, 2 * outer):

time: 118 us -> 119 us (level)
  waiting for transfers between devices: 24.6 us -> 35.6 us
  starting transfers between devices: 55.6 us -> 48.2 us
  other arithmetic: 3.7 us -> 1.07 us
    ppermute x33 -> x30, waiting for transfers between devices: 14.1 us -> 22.8 us  [send(): return lax.ppermute(block, 'tm', route)]
    ppermute x8, starting transfers between devices: 26 us -> 21.5 us  [carry(): return lax.ppermute(block, ('utt', 'tm'), route)]
    ppermute x33 -> x30, starting transfers between devices: 29.5 us -> 26.7 us  [send(): return lax.ppermute(block, 'tm', route)]
    ppermute x8, waiting for transfers between devices: 10.5 us -> 12.8 us  [carry(): return lax.ppermute(block, ('utt', 'tm'), route)]
    concatenate x2, other arithmetic: 1.51 us -> 0.07 us  [on_device(): jnp.concatenate([lax.dynamic_slice_in_dim(mine_late, p ^ a, 1, 0), lax.dy...]
    another operation x2 -> x0, other arithmetic: 1.23 us -> none  [scalars(): return jnp.stack([jnp.asarray(v, jnp.int32) for v in values])]
  transfers between devices with their start and end apart: 41 -> 38, of which waited for: 11 -> 11; matrix products, arithmetic and copies ran while one was open for 5% -> 4% of each run, Pallas kernels for 11% -> 10%
where the time goes in v4:
time: 119 us; the launch traced here: 118 us
  starting transfers between devices  48.2 us (41%)
  waiting for transfers between devices  35.6 us (30%)
  Pallas kernels  25.8 us (22%)
  local copies, waits for them, and re-layouts  6.24 us (5%)
  between operations  1.54 us (1%)
    ppermute x30, starting transfers between devices, send(): return lax.ppermute(block, 'tm', route)  26.7 us
    ppermute x30, waiting for transfers between devices, send(): return lax.ppermute(block, 'tm', route)  22.8 us
    ppermute x8, starting transfers between devices, carry(): return lax.ppermute(block, ('utt', 'tm'), route)  21.5 us
    pallas_call x1, Pallas kernels, encoder(): pl.pallas_call(functools.partial(encoder_kernel, len(parts), depth, not e...  13.9 us
    ppermute x8, waiting for transfers between devices, carry(): return lax.ppermute(block, ('utt', 'tm'), route)  12.8 us
    pallas_call x3, Pallas kernels, norm_layer(): pl.pallas_call(functools.partial(norm_kernel, len(blocks) // 4), out_shap...  4.71 us
    pallas_call x1, Pallas kernels, cross_partial(): pl.pallas_call(functools.partial(cross_kernel, chips, base), out_shape=(j...  3.2 us
    pallas_call x1, Pallas kernels, pack(): pl.pallas_call(pack_kernel, out_shape=(shape, shape), in_specs=[SMEM] + [...  2.39 us
  transfers between devices with their start and end apart: 38, of which 11 were waited for; matrix products, arithmetic and copies ran while one was open for 4% of the time, Pallas kernels for 10%

profile of v4, /device:TPU:0, one launch (start us, length us, event | category | flops | bytes accessed | tf_op | source)
XLA Modules:
  0.0 118.5 jit_solution(1392248564496255636)
XLA Ops:
  0.6 3.1 %collective-permute-start.5 = (bf16[128,1280]{1,0:T(8,128)(2,1)}, bf16[128,1280]{1,0:T(8,128)(2,1)S(1)}, u32[]{:S(2)}, u32[]{:S(2)}) collective-permute-start(bf16[128,1280]{1,0:T(8,128)(2,1)} %refs_0_.3), channel_id=1, source_target_pairs={{0,4},{1,5},{2,6},{3,7},{4,0},{5,1},{6,2},{7,3},{8,12},{9,13},{10,... | collective-permute-start | bytes 983048 | tf_op jit(solution)/shard_map/ppermute | solution.py:21
  3.7 0.7 collective-permute-start.6
  4.4 0.1 collective-permute-start.1
  4.5 0.5 collective-permute-start.2
  5.0 0.1 collective-permute-start.3
  5.1 0.7 stack.131.spot.table.places
  5.7 0.3 collective-permute-done.2.refs_3_
  6.0 1.3 %collective-permute-start.7 = (bf16[128,1280]{1,0:T(8,128)(2,1)}, bf16[128,1280]{1,0:T(8,128)(2,1)S(1)}, u32[]{:S(2)}, u32[]{:S(2)}) collective-permute-start(bf16[128,1280]{1,0:T(8,128)(2,1)} %refs_0_.3), channel_id=1, source_target_pairs={{4,12},{5,13},{6,14},{7,15},{8,0},{9,1},{10,2},{11,3},{20,28},{21,... | collective-permute-start | bytes 983048 | tf_op jit(solution)/shard_map/ppermute | solution.py:21
  7.3 1.6 %collective-permute-start.8 = (bf16[128,1280]{1,0:T(8,128)(2,1)}, bf16[128,1280]{1,0:T(8,128)(2,1)S(1)}, u32[]{:S(2)}, u32[]{:S(2)}) collective-permute-start(bf16[128,1280]{1,0:T(8,128)(2,1)} %refs_0_.3), channel_id=1, source_target_pairs={{0,2},{1,3},{2,0},{3,1},{4,6},{5,7},{6,4},{7,5},{8,10},{9,11},{10,... | collective-permute-start | bytes 983048 | tf_op jit(solution)/shard_map/ppermute | solution.py:21
  8.9 0.6 copy-done.22
  9.5 2.4 %shard_map.77 = (bf16[2,80,1024]{2,1,0:T(8,128)(2,1)}, bf16[2,80,1024]{2,1,0:T(8,128)(2,1)}) custom-call(s32[34]{0:T(128)} %stack.131.spot.table.places, bf16[80,3840]{1,0:T(8,128)(2,1)} %weight.1, bf16[2,1280]{1,0:T(2,128)(2,1)} %refs_0_.2, bf16[2,1280]{1,0:T(2,128)(2,1)} %copy-done.22, s32[2,16]{1,0:T(2,128)} %refs_2_.1, s32[2,16]{1,0:T(2,128)} %copy-done.23, ...), custom_call_target="tpu_custom_call" | custom-call | tf_op jit(solution)/shard_map/pallas_call | solution.py:107
  11.9 2.4 %collective-permute-start.4 = (bf16[2,80,1024]{2,1,0:T(8,128)(2,1)}, bf16[2,80,1024]{2,1,0:T(8,128)(2,1)S(1)}, u32[]{:S(2)}, u32[]{:S(2)}) collective-permute-start(bf16[2,80,1024]{2,1,0:T(8,128)(2,1)} %get-tuple-element.32), channel_id=1, source_target_pairs={{0,2},{2,0},{4,6},{6,4},{8,10},{10,8},{12,14},{14,12},{17,19},{19,... | collective-permute-start | bytes 983048 | tf_op jit(solution)/shard_map/ppermute | solution.py:448
  14.3 0.7 reshape.16.gain
  15.1 7.8 %collective-permute-done.7 = bf16[128,1280]{1,0:T(8,128)(2,1)S(1)} collective-permute-done((bf16[128,1280]{1,0:T(8,128)(2,1)}, bf16[128,1280]{1,0:T(8,128)(2,1)S(1)}, u32[]{:S(2)}, u32[]{:S(2)}) %collective-permute-start.7) | collective-permute-done | bytes 327712 | tf_op jit(solution)/shard_map/ppermute | solution.py:21
  22.9 1.0 constant_dynamic-slice_fusion.2
  24.0 4.7 %collective-permute-start.11 = (bf16[160,1024]{1,0:T(8,128)(2,1)S(1)}, bf16[160,1024]{1,0:T(8,128)(2,1)S(1)}, u32[]{:S(2)}, u32[]{:S(2)}) collective-permute-start(bf16[160,1024]{1,0:T(8,128)(2,1)S(1)} %bitcast.39), channel_id=1, source_target_pairs={{0,12},{2,14},{4,8},{6,10},{8,4},{10,6},{12,0},{14,2},{17,29},{19,... | collective-permute-start | bytes 983048 | tf_op jit(solution)/shard_map/ppermute | solution.py:448
  28.6 1.9 %collective-permute-start.21 = (bf16[160,1024]{1,0:T(8,128)(2,1)S(1)}, bf16[160,1024]{1,0:T(8,128)(2,1)S(1)}, u32[]{:S(2)}, u32[]{:S(2)}) collective-permute-start(bf16[160,1024]{1,0:T(8,128)(2,1)S(1)} %bitcast.40), channel_id=1, source_target_pairs={{0,4},{2,6},{4,0},{6,2},{8,12},{10,14},{12,8},{14,10},{17,21},{19,... | collective-permute-start | bytes 983048 | tf_op jit(solution)/shard_map/ppermute | solution.py:448
  30.6 3.8 %collective-permute-start.12 = (bf16[160,1024]{1,0:T(8,128)(2,1)S(1)}, bf16[160,1024]{1,0:T(8,128)(2,1)S(1)}, u32[]{:S(2)}, u32[]{:S(2)}) collective-permute-start(bf16[160,1024]{1,0:T(8,128)(2,1)S(1)} %bitcast.41), channel_id=1, source_target_pairs={{0,8},{2,10},{4,12},{6,14},{8,0},{10,2},{12,4},{14,6},{17,25},{19,... | collective-permute-start | bytes 983048 | tf_op jit(solution)/shard_map/ppermute | solution.py:448
  34.5 1.3 %collective-permute-start.19 = (bf16[80,1024]{1,0:T(8,128)(2,1)S(1)}, bf16[80,1024]{1,0:T(8,128)(2,1)S(1)}, u32[]{:S(2)}, u32[]{:S(2)}) collective-permute-start(bf16[80,1024]{1,0:T(8,128)(2,1)S(1)} %dynamic-slice_bitcast_fusion), channel_id=1, source_target_pairs={{0,16},{2,18},{4,20},{6,22},{8,24},{10,26},{12,28},{14,30},{17,1},... | collective-permute-start | bytes 491528 | tf_op jit(solution)/shard_map/ppermute | solution.py:448
  35.8 2.8 %collective-permute-done.19 = bf16[80,1024]{1,0:T(8,128)(2,1)S(1)} collective-permute-done((bf16[80,1024]{1,0:T(8,128)(2,1)S(1)}, bf16[80,1024]{1,0:T(8,128)(2,1)S(1)}, u32[]{:S(2)}, u32[]{:S(2)}) %collective-permute-start.19) | collective-permute-done | bytes 163872 | tf_op jit(solution)/shard_map/ppermute | solution.py:448
  38.6 0.3 collective-permute-start.9
  38.9 1.5 %collective-permute-start.13 = (bf16[128,1280]{1,0:T(8,128)(2,1)S(1)}, bf16[128,1280]{1,0:T(8,128)(2,1)S(1)}, u32[]{:S(2)}, u32[]{:S(2)}) collective-permute-start(bf16[128,1280]{1,0:T(8,128)(2,1)S(1)} %collective-permute-done.5.refs_0_), channel_id=1, source_target_pairs={{0,2},{1,3},{2,0},{3,1},{4,6},{5,7},{6,4},{7,5},{8,10},{9,11},{10,... | collective-permute-start | bytes 983048 | tf_op jit(solution)/shard_map/ppermute | solution.py:21
  40.4 5.0 %collective-permute-done.12 = bf16[160,1024]{1,0:T(8,128)(2,1)S(1)} collective-permute-done((bf16[160,1024]{1,0:T(8,128)(2,1)S(1)}, bf16[160,1024]{1,0:T(8,128)(2,1)S(1)}, u32[]{:S(2)}, u32[]{:S(2)}) %collective-permute-start.12) | collective-permute-done | bytes 327712 | tf_op jit(solution)/shard_map/ppermute | solution.py:448
  45.4 1.5 %collective-permute-start.14 = (bf16[128,1280]{1,0:T(8,128)(2,1)S(1)}, bf16[128,1280]{1,0:T(8,128)(2,1)S(1)}, u32[]{:S(2)}, u32[]{:S(2)}) collective-permute-start(bf16[128,1280]{1,0:T(8,128)(2,1)S(1)} %broadcast_select_fusion.3.refs_0_), channel_id=1, source_target_pairs={{0,2},{1,3},{2,0},{3,1},{4,6},{5,7},{6,4},{7,5},{8,10},{9,11},{10,... | collective-permute-start | bytes 983048 | tf_op jit(solution)/shard_map/ppermute | solution.py:21
  46.9 1.3 %collective-permute-start.22 = (bf16[160,1024]{1,0:T(8,128)(2,1)S(1)}, bf16[160,1024]{1,0:T(8,128)(2,1)S(1)}, u32[]{:S(2)}, u32[]{:S(2)}) collective-permute-start(bf16[160,1024]{1,0:T(8,128)(2,1)S(1)} %collective-permute-done.21), channel_id=1, source_target_pairs={{0,16},{2,18},{4,20},{6,22},{8,24},{10,26},{12,28},{14,30},{17,1},... | collective-permute-start | bytes 983048 | tf_op jit(solution)/shard_map/ppermute | solution.py:448
  48.3 1.2 collective-permute-done.13.refs_2_
  49.4 6.3 %collective-permute-done.14.refs_2_ = bf16[128,1280]{1,0:T(8,128)(2,1)S(1)} collective-permute-done((bf16[128,1280]{1,0:T(8,128)(2,1)S(1)}, bf16[128,1280]{1,0:T(8,128)(2,1)S(1)}, u32[]{:S(2)}, u32[]{:S(2)}) %collective-permute-start.14) | collective-permute-done | bytes 327712 | tf_op jit(solution)/shard_map/ppermute | solution.py:21
  55.7 1.3 %collective-permute-start.16 = (bf16[128,1280]{1,0:T(8,128)(2,1)S(1)}, bf16[128,1280]{1,0:T(8,128)(2,1)S(1)}, u32[]{:S(2)}, u32[]{:S(2)}) collective-permute-start(bf16[128,1280]{1,0:T(8,128)(2,1)S(1)} %broadcast_select_fusion.3.refs_0_), channel_id=1, source_target_pairs={{0,1},{2,3},{4,5},{6,7},{9,8},{11,10},{13,12},{15,14},{16,17},{18,... | collective-permute-start | bytes 983048 | tf_op jit(solution)/shard_map/ppermute | solution.py:21
  57.0 0.1 collective-permute-start.15
  57.1 4.7 %collective-permute-start.24 = (bf16[160,1024]{1,0:T(8,128)(2,1)S(1)}, bf16[160,1024]{1,0:T(8,128)(2,1)S(1)}, u32[]{:S(2)}, u32[]{:S(2)}) collective-permute-start(bf16[160,1024]{1,0:T(8,128)(2,1)S(1)} %collective-permute-done.12), channel_id=1, source_target_pairs={{0,16},{2,18},{4,20},{6,22},{8,24},{10,26},{12,28},{14,30},{17,1},... | collective-permute-start | bytes 983048 | tf_op jit(solution)/shard_map/ppermute | solution.py:448
  61.9 1.6 %shard_map.78 = (bf16[512,1280]{1,0:T(8,128)(2,1)S(1)}, bf16[512,320]{1,0:T(8,128)(2,1)S(1)}) custom-call(s32[34]{0:T(128)S(1)} %copy-done.17, f32[1,1280]{1,0:T(1,128)S(1)} %reshape.16.gain, bf16[128,1280]{1,0:T(8,128)(2,1)S(1)} %copy-done.16, bf16[128,1280]{1,0:T(8,128)(2,1)S(1)} %collective-permute-done.refs_1_, ...), custom_call_target="tpu_custom_call" | custom-call | tf_op jit(solution)/shard_map/pallas_call | solution.py:140
  63.5 1.3 %collective-permute-start.26 = (bf16[160,1024]{1,0:T(8,128)(2,1)S(1)}, bf16[160,1024]{1,0:T(8,128)(2,1)S(1)}, u32[]{:S(2)}, u32[]{:S(2)}) collective-permute-start(bf16[160,1024]{1,0:T(8,128)(2,1)S(1)} %collective-permute-done.11), channel_id=1, source_target_pairs={{0,16},{2,18},{4,20},{6,22},{8,24},{10,26},{12,28},{14,30},{17,1},... | collective-permute-start | bytes 983048 | tf_op jit(solution)/shard_map/ppermute | solution.py:448
  64.9 5.0 %collective-permute-done.26 = bf16[160,1024]{1,0:T(8,128)(2,1)S(1)} collective-permute-done((bf16[160,1024]{1,0:T(8,128)(2,1)S(1)}, bf16[160,1024]{1,0:T(8,128)(2,1)S(1)}, u32[]{:S(2)}, u32[]{:S(2)}) %collective-permute-start.26) | collective-permute-done | bytes 327712 | tf_op jit(solution)/shard_map/ppermute | solution.py:448
  70.0 1.4 %collective-permute-start.17 = (bf16[128,1280]{1,0:T(8,128)(2,1)S(1)}, bf16[128,1280]{1,0:T(8,128)(2,1)S(1)}, u32[]{:S(2)}, u32[]{:S(2)}) collective-permute-start(bf16[128,1280]{1,0:T(8,128)(2,1)S(1)} %collective-permute-done.14.refs_2_), channel_id=1, source_target_pairs={{0,1},{2,3},{4,5},{6,7},{9,8},{11,10},{13,12},{15,14},{16,17},{18,... | collective-permute-start | bytes 983048 | tf_op jit(solution)/shard_map/ppermute | solution.py:21
  71.4 0.1 collective-permute-start.23
  71.6 0.6 collective-permute-start.25
  72.2 0.1 collective-permute-start.18
  72.3 1.6 %shard_map.79 = (bf16[512,1280]{1,0:T(8,128)(2,1)S(1)}, bf16[512,320]{1,0:T(8,128)(2,1)S(1)}) custom-call(s32[34]{0:T(128)S(1)} %copy-done.17, f32[1,1280]{1,0:T(1,128)S(1)} %reshape.16.gain, bf16[128,1280]{1,0:T(8,128)(2,1)S(1)} %collective-permute-done.5.refs_0_, bf16[128,1280]{1,0:T(8,128)(2,1)S(1)} %collective-permute-done.10.refs_1_, ...), custom_call_target="tpu_custom_call" | custom-call | tf_op jit(solution)/shard_map/pallas_call | solution.py:140
  73.8 0.6 collective-permute-start.20
  74.4 0.1 collective-permute-start.27
  74.5 1.6 %shard_map.80 = (bf16[512,1280]{1,0:T(8,128)(2,1)S(1)}, bf16[512,320]{1,0:T(8,128)(2,1)S(1)}) custom-call(s32[34]{0:T(128)S(1)} %copy-done.17, f32[1,1280]{1,0:T(1,128)S(1)} %reshape.16.gain, bf16[128,1280]{1,0:T(8,128)(2,1)S(1)} %broadcast_select_fusion.3.refs_0_, bf16[128,1280]{1,0:T(8,128)(2,1)S(1)} %collective-permute-done.16.refs_1_, ...), custom_call_target="tpu_custom_call" | custom-call | tf_op jit(solution)/shard_map/pallas_call | solution.py:140
  76.4 13.9 %shard_map.81 = (bf16[512,320]{1,0:T(8,128)(2,1)S(1)}, bf16[256,320]{1,0:T(8,128)(2,1)S(1)}, bf16[256,320]{1,0:T(8,128)(2,1)S(1)}) custom-call(s32[34]{0:T(128)S(1)} %copy-done.17, bf16[512,1280]{1,0:T(8,128)(2,1)S(1)} %get-tuple-element.34.refs_0_, bf16[512,320]{1,0:T(8,128)(2,1)S(1)} %get-tuple-element.35.refs_1_, ...), custom_call_target="tpu_custom_call" | custom-call | tf_op jit(solution)/shard_map/pallas_call | solution.py:281
  90.4 0.7 copy-done.15
  91.1 0.7 collective-permute-start.28
  91.8 1.5 %collective-permute-start.29 = (bf16[256,320]{1,0:T(8,128)(2,1)S(1)}, bf16[256,320]{1,0:T(8,128)(2,1)S(1)}, u32[]{:S(2)}, u32[]{:S(2)}) collective-permute-start(bf16[256,320]{1,0:T(8,128)(2,1)S(1)} %get-tuple-element.50), channel_id=1, source_target_pairs={{0,2},{1,6},{2,0},{3,4},{4,3},{5,7},{6,1},{7,5},{8,10},{9,14},{10,... | collective-permute-start | bytes 491528 | tf_op jit(solution)/shard_map/ppermute | solution.py:21
  93.3 3.2 %shard_map.82 = (f32[40,128]{1,0:T(8,128)}, f32[40,128]{1,0:T(8,128)}, f32[40,128]{1,0:T(8,128)}, f32[40,128]{1,0:T(8,128)}) custom-call(s32[34]{0:T(128)} %stack.131.spot.table.places, bf16[512,320]{1,0:T(8,128)(2,1)} %copy-done.15, bf16[80,1024]{1,0:T(8,128)(2,1)} %copy-done, bf16[80,1024]{1,0:T(8,128)(2,1)} %copy-done, bf16[80,1024]{1,0:T(8,128)(2,1)} %copy-done.13, ...), custom_call_target="tpu_custom_call" | custom-call | tf_op jit(solution)/shard_map/pallas_call | solution.py:360
  96.5 3.2 %collective-permute-start.32 = (f32[40,128]{1,0:T(8,128)}, f32[40,128]{1,0:T(8,128)S(1)}, u32[]{:S(2)}, u32[]{:S(2)}) collective-permute-start(f32[40,128]{1,0:T(8,128)} %get-tuple-element.53), channel_id=1, source_target_pairs={{0,8},{1,9},{2,10},{3,11},{4,12},{5,13},{6,14},{7,15},{8,0},{9,1},... | collective-permute-start | bytes 61448 | tf_op jit(solution)/shard_map/ppermute | solution.py:21
  99.7 2.5 %collective-permute-start.33 = (f32[40,128]{1,0:T(8,128)}, f32[40,128]{1,0:T(8,128)S(1)}, u32[]{:S(2)}, u32[]{:S(2)}) collective-permute-start(f32[40,128]{1,0:T(8,128)} %get-tuple-element.54), channel_id=1, source_target_pairs={{0,1},{1,0},{2,3},{3,2},{4,5},{5,4},{6,7},{7,6},{8,9},{9,8},{10,11... | collective-permute-start | bytes 61448 | tf_op jit(solution)/shard_map/ppermute | solution.py:21
  102.3 0.0 collective-permute-start.34
  102.3 1.0 collective-permute-done.33.refs_2_
  103.3 3.3 %collective-permute-done.34.refs_3_ = f32[40,128]{1,0:T(8,128)S(1)} collective-permute-done((f32[40,128]{1,0:T(8,128)}, f32[40,128]{1,0:T(8,128)S(1)}, u32[]{:S(2)}, u32[]{:S(2)}) %collective-permute-start.34) | collective-permute-done | bytes 20512 | tf_op jit(solution)/shard_map/ppermute | solution.py:21
  106.6 0.6 copy-done.21
  107.2 1.6 %shard_map.83 = (bf16[2,384]{1,0:T(2,128)(2,1)}, bf16[2,384]{1,0:T(2,128)(2,1)}, bf16[2,384]{1,0:T(2,128)(2,1)}, bf16[2,384]{1,0:T(2,128)(2,1)}) custom-call(f32[40,128]{1,0:T(8,128)} %get-tuple-element.52.refs_0_, f32[40,128]{1,0:T(8,128)} %copy-done.19, f32[40,128]{1,0:T(8,128)} %copy-done.20, f32[40,128]{1,0:T(8,128)} %copy-done.21), custom_call_target="tpu_custom_call" | custom-call | tf_op jit(solution)/shard_map/pallas_call | solution.py:389
  108.8 0.6 collective-permute-start.35
  109.4 1.8 %collective-permute-start.36 = (bf16[2,384]{1,0:T(2,128)(2,1)}, bf16[2,384]{1,0:T(2,128)(2,1)S(1)}, u32[]{:S(2)}, u32[]{:S(2)}) collective-permute-start(bf16[2,384]{1,0:T(2,128)(2,1)} %get-tuple-element.58), channel_id=1, source_target_pairs={{0,4},{1,5},{2,6},{3,7},{4,0},{5,1},{6,2},{7,3},{8,12},{9,13},{10,... | collective-permute-start | bytes 4616 | tf_op jit(solution)/shard_map/ppermute | solution.py:21
  111.2 1.1 collective-permute-start.37
  112.3 0.1 collective-permute-start.30
  112.4 0.5 collective-permute-start.31
  113.0 0.2 collective-permute-done.36
  113.2 2.7 %collective-permute-done.37 = bf16[2,384]{1,0:T(2,128)(2,1)S(1)} collective-permute-done((bf16[2,384]{1,0:T(2,128)(2,1)}, bf16[2,384]{1,0:T(2,128)(2,1)S(1)}, u32[]{:S(2)}, u32[]{:S(2)}) %collective-permute-start.37) | collective-permute-done | bytes 1568 | tf_op jit(solution)/shard_map/ppermute | solution.py:21
  115.9 0.7 broadcast_select_fusion.7
  116.7 0.7 concatenate.15
  117.4 0.1 select_select_fusion
  117.6 0.8 concatenate.14
  (109 shorter events, 0.7 us)
Async XLA Ops:
  0.6 14.4 %collective-permute-start.5 = (bf16[128,1280]{1,0:T(8,128)(2,1)}, bf16[128,1280]{1,0:T(8,128)(2,1)S(1)}, u32[]{:S(2)}, u32[]{:S(2)}) collective-permute-start(bf16[128,1280]{1,0:T(8,128)(2,1)} %refs_0_.3), channel_id=1, source_target_pairs={{0,4},{1,5},{2,6},{3,7},{4,0},{5,1},{6,2},{7,3},{8,12},{9,13},{10,... | collective-permute-start | bytes 983048 | tf_op jit(solution)/shard_map/ppermute | solution.py:21
  3.7 11.3 %collective-permute-start.6 = (bf16[128,1280]{1,0:T(8,128)(2,1)}, bf16[128,1280]{1,0:T(8,128)(2,1)S(1)}, u32[]{:S(2)}, u32[]{:S(2)}) collective-permute-start(bf16[128,1280]{1,0:T(8,128)(2,1)} %refs_0_.3), channel_id=1, source_target_pairs={{4,8},{5,9},{6,10},{7,11},{8,4},{9,5},{10,6},{11,7},{20,24},{21,25... | collective-permute-start | bytes 983048 | tf_op jit(solution)/shard_map/ppermute | solution.py:21
  4.4 4.5 %collective-permute-start.1 = (bf16[2,1280]{1,0:T(2,128)(2,1)}, bf16[2,1280]{1,0:T(2,128)(2,1)S(1)}, u32[]{:S(2)}, u32[]{:S(2)}) collective-permute-start(bf16[2,1280]{1,0:T(2,128)(2,1)} %refs_0_.2), channel_id=1, source_target_pairs={{0,1},{1,0},{2,3},{3,2},{4,5},{5,4},{6,7},{7,6},{8,9},{9,8},{10,11... | collective-permute-start | bytes 15368 | tf_op jit(solution)/shard_map/ppermute | solution.py:21
  4.5 1.5 %collective-permute-start.2 = (s32[2,16]{1,0:T(2,128)}, s32[2,16]{1,0:T(2,128)S(1)}, u32[]{:S(2)}, u32[]{:S(2)}) collective-permute-start(s32[2,16]{1,0:T(2,128)} %refs_2_.1), channel_id=1, source_target_pairs={{0,1},{1,0},{2,3},{3,2},{4,5},{5,4},{6,7},{7,6},{8,9},{9,8},{10,11... | collective-permute-start | bytes 392 | tf_op jit(solution)/shard_map/ppermute | solution.py:21
  5.0 2.3 %collective-permute-start.3 = (s32[1,128]{1,0:T(1,128)}, s32[1,128]{1,0:T(1,128)S(1)}, u32[]{:S(2)}, u32[]{:S(2)}) collective-permute-start(s32[1,128]{1,0:T(1,128)} %bitcast.42), channel_id=1, source_target_pairs={{0,1},{1,0},{2,3},{3,2},{4,5},{5,4},{6,7},{7,6},{8,9},{9,8},{10,11... | collective-permute-start | bytes 1544 | tf_op jit(solution)/shard_map/ppermute | solution.py:21
  6.0 2.9 %copy-start.23 = (s32[2,16]{1,0:T(2,128)}, s32[2,16]{1,0:T(2,128)S(1)}, u32[]{:S(2)}) copy-start(s32[2,16]{1,0:T(2,128)S(1)} %collective-permute-done.2.refs_3_) | copy-start | bytes 388
  6.0 16.9 %collective-permute-start.7 = (bf16[128,1280]{1,0:T(8,128)(2,1)}, bf16[128,1280]{1,0:T(8,128)(2,1)S(1)}, u32[]{:S(2)}, u32[]{:S(2)}) collective-permute-start(bf16[128,1280]{1,0:T(8,128)(2,1)} %refs_0_.3), channel_id=1, source_target_pairs={{4,12},{5,13},{6,14},{7,15},{8,0},{9,1},{10,2},{11,3},{20,28},{21,... | collective-permute-start | bytes 983048 | tf_op jit(solution)/shard_map/ppermute | solution.py:21
  7.3 1.6 %copy-start.24 = (s32[1,128]{1,0:T(1,128)}, s32[1,128]{1,0:T(1,128)S(1)}, u32[]{:S(2)}) copy-start(s32[1,128]{1,0:T(1,128)S(1)} %collective-permute-done.3.refs_5_) | copy-start | bytes 1540
  7.3 15.6 %collective-permute-start.8 = (bf16[128,1280]{1,0:T(8,128)(2,1)}, bf16[128,1280]{1,0:T(8,128)(2,1)S(1)}, u32[]{:S(2)}, u32[]{:S(2)}) collective-permute-start(bf16[128,1280]{1,0:T(8,128)(2,1)} %refs_0_.3), channel_id=1, source_target_pairs={{0,2},{1,3},{2,0},{3,1},{4,6},{5,7},{6,4},{7,5},{8,10},{9,11},{10,... | collective-permute-start | bytes 983048 | tf_op jit(solution)/shard_map/ppermute | solution.py:21
  8.9 0.6 copy-start.22
  11.9 11.0 %collective-permute-start.4 = (bf16[2,80,1024]{2,1,0:T(8,128)(2,1)}, bf16[2,80,1024]{2,1,0:T(8,128)(2,1)S(1)}, u32[]{:S(2)}, u32[]{:S(2)}) collective-permute-start(bf16[2,80,1024]{2,1,0:T(8,128)(2,1)} %get-tuple-element.32), channel_id=1, source_target_pairs={{0,2},{2,0},{4,6},{6,4},{8,10},{10,8},{12,14},{14,12},{17,19},{19,... | collective-permute-start | bytes 983048 | tf_op jit(solution)/shard_map/ppermute | solution.py:448
  15.0 42.0 %collective-permute-start = (bf16[128,1280]{1,0:T(8,128)(2,1)}, bf16[128,1280]{1,0:T(8,128)(2,1)S(1)}, u32[]{:S(2)}, u32[]{:S(2)}) collective-permute-start(bf16[128,1280]{1,0:T(8,128)(2,1)} %refs_0_.3), channel_id=1, source_target_pairs={{0,1},{1,0},{2,3},{3,2},{4,5},{5,4},{6,7},{7,6},{8,9},{9,8},{10,11... | collective-permute-start | bytes 983048 | tf_op jit(solution)/shard_map/ppermute | solution.py:21
  23.9 24.3 %copy-start.18 = (bf16[2,80,1024]{2,1,0:T(8,128)(2,1)S(1)}, bf16[2,80,1024]{2,1,0:T(8,128)(2,1)}, u32[]{:S(2)}) copy-start(bf16[2,80,1024]{2,1,0:T(8,128)(2,1)} %get-tuple-element.37) | copy-start | bytes 983044
  24.0 14.9 %collective-permute-start.11 = (bf16[160,1024]{1,0:T(8,128)(2,1)S(1)}, bf16[160,1024]{1,0:T(8,128)(2,1)S(1)}, u32[]{:S(2)}, u32[]{:S(2)}) collective-permute-start(bf16[160,1024]{1,0:T(8,128)(2,1)S(1)} %bitcast.39), channel_id=1, source_target_pairs={{0,12},{2,14},{4,8},{6,10},{8,4},{10,6},{12,0},{14,2},{17,29},{19,... | collective-permute-start | bytes 983048 | tf_op jit(solution)/shard_map/ppermute | solution.py:448
  28.6 18.2 %collective-permute-start.21 = (bf16[160,1024]{1,0:T(8,128)(2,1)S(1)}, bf16[160,1024]{1,0:T(8,128)(2,1)S(1)}, u32[]{:S(2)}, u32[]{:S(2)}) collective-permute-start(bf16[160,1024]{1,0:T(8,128)(2,1)S(1)} %bitcast.40), channel_id=1, source_target_pairs={{0,4},{2,6},{4,0},{6,2},{8,12},{10,14},{12,8},{14,10},{17,21},{19,... | collective-permute-start | bytes 983048 | tf_op jit(solution)/shard_map/ppermute | solution.py:448
  30.6 31.3 %copy-start.16 = (bf16[128,1280]{1,0:T(8,128)(2,1)S(1)}, bf16[128,1280]{1,0:T(8,128)(2,1)}, u32[]{:S(2)}) copy-start(bf16[128,1280]{1,0:T(8,128)(2,1)} %refs_0_.3) | copy-start | bytes 983044
  30.6 31.3 %copy-start.17 = (s32[34]{0:T(128)S(1)}, s32[34]{0:T(128)}, u32[]{:S(2)}) copy-start(s32[34]{0:T(128)} %stack.131.spot.table.places) | copy-start | bytes 412
  30.6 14.8 %collective-permute-start.12 = (bf16[160,1024]{1,0:T(8,128)(2,1)S(1)}, bf16[160,1024]{1,0:T(8,128)(2,1)S(1)}, u32[]{:S(2)}, u32[]{:S(2)}) collective-permute-start(bf16[160,1024]{1,0:T(8,128)(2,1)S(1)} %bitcast.41), channel_id=1, source_target_pairs={{0,8},{2,10},{4,12},{6,14},{8,0},{10,2},{12,4},{14,6},{17,25},{19,... | collective-permute-start | bytes 983048 | tf_op jit(solution)/shard_map/ppermute | solution.py:448
  34.5 4.1 %collective-permute-start.19 = (bf16[80,1024]{1,0:T(8,128)(2,1)S(1)}, bf16[80,1024]{1,0:T(8,128)(2,1)S(1)}, u32[]{:S(2)}, u32[]{:S(2)}) collective-permute-start(bf16[80,1024]{1,0:T(8,128)(2,1)S(1)} %dynamic-slice_bitcast_fusion), channel_id=1, source_target_pairs={{0,16},{2,18},{4,20},{6,22},{8,24},{10,26},{12,28},{14,30},{17,1},... | collective-permute-start | bytes 491528 | tf_op jit(solution)/shard_map/ppermute | solution.py:448
  38.6 18.6 %collective-permute-start.9 = (bf16[128,1280]{1,0:T(8,128)(2,1)S(1)}, bf16[128,1280]{1,0:T(8,128)(2,1)S(1)}, u32[]{:S(2)}, u32[]{:S(2)}) collective-permute-start(bf16[128,1280]{1,0:T(8,128)(2,1)S(1)} %collective-permute-done.8.refs_2_), channel_id=1, source_target_pairs={{0,1},{1,0},{2,3},{3,2},{4,5},{5,4},{6,7},{7,6},{8,9},{9,8},{10,11... | collective-permute-start | bytes 983048 | tf_op jit(solution)/shard_map/ppermute | solution.py:21
  38.9 10.6 %collective-permute-start.13 = (bf16[128,1280]{1,0:T(8,128)(2,1)S(1)}, bf16[128,1280]{1,0:T(8,128)(2,1)S(1)}, u32[]{:S(2)}, u32[]{:S(2)}) collective-permute-start(bf16[128,1280]{1,0:T(8,128)(2,1)S(1)} %collective-permute-done.5.refs_0_), channel_id=1, source_target_pairs={{0,2},{1,3},{2,0},{3,1},{4,6},{5,7},{6,4},{7,5},{8,10},{9,11},{10,... | collective-permute-start | bytes 983048 | tf_op jit(solution)/shard_map/ppermute | solution.py:21
  45.4 10.3 %collective-permute-start.14 = (bf16[128,1280]{1,0:T(8,128)(2,1)S(1)}, bf16[128,1280]{1,0:T(8,128)(2,1)S(1)}, u32[]{:S(2)}, u32[]{:S(2)}) collective-permute-start(bf16[128,1280]{1,0:T(8,128)(2,1)S(1)} %broadcast_select_fusion.3.refs_0_), channel_id=1, source_target_pairs={{0,2},{1,3},{2,0},{3,1},{4,6},{5,7},{6,4},{7,5},{8,10},{9,11},{10,... | collective-permute-start | bytes 983048 | tf_op jit(solution)/shard_map/ppermute | solution.py:21
  46.9 16.6 %collective-permute-start.22 = (bf16[160,1024]{1,0:T(8,128)(2,1)S(1)}, bf16[160,1024]{1,0:T(8,128)(2,1)S(1)}, u32[]{:S(2)}, u32[]{:S(2)}) collective-permute-start(bf16[160,1024]{1,0:T(8,128)(2,1)S(1)} %collective-permute-done.21), channel_id=1, source_target_pairs={{0,16},{2,18},{4,20},{6,22},{8,24},{10,26},{12,28},{14,30},{17,1},... | collective-permute-start | bytes 983048 | tf_op jit(solution)/shard_map/ppermute | solution.py:448
  48.2 28.1 %copy-start = (bf16[80,1024]{1,0:T(8,128)(2,1)}, bf16[80,1024]{1,0:T(8,128)(2,1)S(1)}, u32[]{:S(2)}) copy-start(bf16[80,1024]{1,0:T(8,128)(2,1)S(1)} %dynamic-slice_bitcast_fusion.1.refs_6_.refs_0_.refs_1_) | copy-start | bytes 491524
  48.3 28.0 %copy-start.13 = (bf16[80,1024]{1,0:T(8,128)(2,1)}, bf16[80,1024]{1,0:T(8,128)(2,1)S(1)}, u32[]{:S(2)}) copy-start(bf16[80,1024]{1,0:T(8,128)(2,1)S(1)} %broadcast_select_fusion.4.refs_8_.refs_2_) | copy-start | bytes 491524
  49.4 22.1 %collective-permute-start.10 = (bf16[128,1280]{1,0:T(8,128)(2,1)S(1)}, bf16[128,1280]{1,0:T(8,128)(2,1)S(1)}, u32[]{:S(2)}, u32[]{:S(2)}) collective-permute-start(bf16[128,1280]{1,0:T(8,128)(2,1)S(1)} %collective-permute-done.5.refs_0_), channel_id=1, source_target_pairs={{0,1},{1,0},{2,3},{3,2},{4,5},{5,4},{6,7},{7,6},{8,9},{9,8},{10,11... | collective-permute-start | bytes 983048 | tf_op jit(solution)/shard_map/ppermute | solution.py:21
  55.7 18.1 %collective-permute-start.16 = (bf16[128,1280]{1,0:T(8,128)(2,1)S(1)}, bf16[128,1280]{1,0:T(8,128)(2,1)S(1)}, u32[]{:S(2)}, u32[]{:S(2)}) collective-permute-start(bf16[128,1280]{1,0:T(8,128)(2,1)S(1)} %broadcast_select_fusion.3.refs_0_), channel_id=1, source_target_pairs={{0,1},{2,3},{4,5},{6,7},{9,8},{11,10},{13,12},{15,14},{16,17},{18,... | collective-permute-start | bytes 983048 | tf_op jit(solution)/shard_map/ppermute | solution.py:21
  57.0 15.1 %collective-permute-start.15 = (bf16[128,1280]{1,0:T(8,128)(2,1)S(1)}, bf16[128,1280]{1,0:T(8,128)(2,1)S(1)}, u32[]{:S(2)}, u32[]{:S(2)}) collective-permute-start(bf16[128,1280]{1,0:T(8,128)(2,1)S(1)} %collective-permute-done.13.refs_2_), channel_id=1, source_target_pairs={{0,1},{1,0},{2,3},{3,2},{4,5},{5,4},{6,7},{7,6},{8,9},{9,8},{10,11... | collective-permute-start | bytes 983048 | tf_op jit(solution)/shard_map/ppermute | solution.py:21
  57.1 14.2 %collective-permute-start.24 = (bf16[160,1024]{1,0:T(8,128)(2,1)S(1)}, bf16[160,1024]{1,0:T(8,128)(2,1)S(1)}, u32[]{:S(2)}, u32[]{:S(2)}) collective-permute-start(bf16[160,1024]{1,0:T(8,128)(2,1)S(1)} %collective-permute-done.12), channel_id=1, source_target_pairs={{0,16},{2,18},{4,20},{6,22},{8,24},{10,26},{12,28},{14,30},{17,1},... | collective-permute-start | bytes 983048 | tf_op jit(solution)/shard_map/ppermute | solution.py:448
  63.5 6.5 %collective-permute-start.26 = (bf16[160,1024]{1,0:T(8,128)(2,1)S(1)}, bf16[160,1024]{1,0:T(8,128)(2,1)S(1)}, u32[]{:S(2)}, u32[]{:S(2)}) collective-permute-start(bf16[160,1024]{1,0:T(8,128)(2,1)S(1)} %collective-permute-done.11), channel_id=1, source_target_pairs={{0,16},{2,18},{4,20},{6,22},{8,24},{10,26},{12,28},{14,30},{17,1},... | collective-permute-start | bytes 983048 | tf_op jit(solution)/shard_map/ppermute | solution.py:448
  64.9 11.4 %copy-start.1 = (bf16[80,1024]{1,0:T(8,128)(2,1)}, bf16[80,1024]{1,0:T(8,128)(2,1)S(1)}, u32[]{:S(2)}) copy-start(bf16[80,1024]{1,0:T(8,128)(2,1)S(1)} %get-tuple-element.74.refs_12_.refs_6_) | copy-start | bytes 491524
  64.9 11.4 %copy-start.2 = (bf16[80,1024]{1,0:T(8,128)(2,1)}, bf16[80,1024]{1,0:T(8,128)(2,1)S(1)}, u32[]{:S(2)}) copy-start(bf16[80,1024]{1,0:T(8,128)(2,1)S(1)} %get-tuple-element.75.refs_10_.refs_4_) | copy-start | bytes 491524
  70.0 4.5 %collective-permute-start.17 = (bf16[128,1280]{1,0:T(8,128)(2,1)S(1)}, bf16[128,1280]{1,0:T(8,128)(2,1)S(1)}, u32[]{:S(2)}, u32[]{:S(2)}) collective-permute-start(bf16[128,1280]{1,0:T(8,128)(2,1)S(1)} %collective-permute-done.14.refs_2_), channel_id=1, source_target_pairs={{0,1},{2,3},{4,5},{6,7},{9,8},{11,10},{13,12},{15,14},{16,17},{18,... | collective-permute-start | bytes 983048 | tf_op jit(solution)/shard_map/ppermute | solution.py:21
  71.4 4.7 %collective-permute-start.23 = (bf16[160,1024]{1,0:T(8,128)(2,1)S(1)}, bf16[160,1024]{1,0:T(8,128)(2,1)S(1)}, u32[]{:S(2)}, u32[]{:S(2)}) collective-permute-start(bf16[160,1024]{1,0:T(8,128)(2,1)S(1)} %broadcast_select_fusion.2), channel_id=1, source_target_pairs={{0,1},{1,0},{2,3},{3,2},{4,5},{5,4},{6,7},{7,6},{8,9},{9,8},{10,11... | collective-permute-start | bytes 983048 | tf_op jit(solution)/shard_map/ppermute | solution.py:21
  71.5 4.8 %copy-start.3 = (bf16[80,1024]{1,0:T(8,128)(2,1)}, bf16[80,1024]{1,0:T(8,128)(2,1)S(1)}, u32[]{:S(2)}) copy-start(bf16[80,1024]{1,0:T(8,128)(2,1)S(1)} %get-tuple-element.70.refs_16_.refs_10_) | copy-start | bytes 491524
  71.5 4.8 %copy-start.4 = (bf16[80,1024]{1,0:T(8,128)(2,1)}, bf16[80,1024]{1,0:T(8,128)(2,1)S(1)}, u32[]{:S(2)}) copy-start(bf16[80,1024]{1,0:T(8,128)(2,1)S(1)} %get-tuple-element.71.refs_14_.refs_8_) | copy-start | bytes 491524
  71.6 4.6 %collective-permute-start.25 = (bf16[160,1024]{1,0:T(8,128)(2,1)S(1)}, bf16[160,1024]{1,0:T(8,128)(2,1)S(1)}, u32[]{:S(2)}, u32[]{:S(2)}) collective-permute-start(bf16[160,1024]{1,0:T(8,128)(2,1)S(1)} %broadcast_select_fusion.1), channel_id=1, source_target_pairs={{0,1},{1,0},{2,3},{3,2},{4,5},{5,4},{6,7},{7,6},{8,9},{9,8},{10,11... | collective-permute-start | bytes 983048 | tf_op jit(solution)/shard_map/ppermute | solution.py:21
  72.1 4.2 %copy-start.5 = (bf16[80,1024]{1,0:T(8,128)(2,1)}, bf16[80,1024]{1,0:T(8,128)(2,1)S(1)}, u32[]{:S(2)}) copy-start(bf16[80,1024]{1,0:T(8,128)(2,1)S(1)} %get-tuple-element.66.refs_20_.refs_14_) | copy-start | bytes 491524
  72.2 4.2 %copy-start.6 = (bf16[80,1024]{1,0:T(8,128)(2,1)}, bf16[80,1024]{1,0:T(8,128)(2,1)S(1)}, u32[]{:S(2)}) copy-start(bf16[80,1024]{1,0:T(8,128)(2,1)S(1)} %get-tuple-element.67.refs_18_.refs_12_) | copy-start | bytes 491524
  72.2 4.1 %collective-permute-start.18 = (bf16[80,1024]{1,0:T(8,128)(2,1)S(1)}, bf16[80,1024]{1,0:T(8,128)(2,1)S(1)}, u32[]{:S(2)}, u32[]{:S(2)}) collective-permute-start(bf16[80,1024]{1,0:T(8,128)(2,1)S(1)} %dynamic-slice_bitcast_fusion.1.refs_6_.refs_0_.refs_1_), channel_id=1, source_target_pairs={{0,1},{1,0},{2,3},{3,2},{4,5},{5,4},{6,7},{7,6},{8,9},{9,8},{10,11... | collective-permute-start | bytes 491528 | tf_op jit(solution)/shard_map/ppermute | solution.py:21
  73.8 2.4 %collective-permute-start.20 = (bf16[80,1024]{1,0:T(8,128)(2,1)S(1)}, bf16[80,1024]{1,0:T(8,128)(2,1)S(1)}, u32[]{:S(2)}, u32[]{:S(2)}) collective-permute-start(bf16[80,1024]{1,0:T(8,128)(2,1)S(1)} %broadcast_select_fusion.4.refs_8_.refs_2_), channel_id=1, source_target_pairs={{0,1},{1,0},{2,3},{3,2},{4,5},{5,4},{6,7},{7,6},{8,9},{9,8},{10,11... | collective-permute-start | bytes 491528 | tf_op jit(solution)/shard_map/ppermute | solution.py:21
  74.4 1.8 %collective-permute-start.27 = (bf16[160,1024]{1,0:T(8,128)(2,1)S(1)}, bf16[160,1024]{1,0:T(8,128)(2,1)S(1)}, u32[]{:S(2)}, u32[]{:S(2)}) collective-permute-start(bf16[160,1024]{1,0:T(8,128)(2,1)S(1)} %broadcast_select_fusion), channel_id=1, source_target_pairs={{0,1},{1,0},{2,3},{3,2},{4,5},{5,4},{6,7},{7,6},{8,9},{9,8},{10,11... | collective-permute-start | bytes 983048 | tf_op jit(solution)/shard_map/ppermute | solution.py:21
  76.1 14.2 %copy-start.7 = (bf16[80,1024]{1,0:T(8,128)(2,1)}, bf16[80,1024]{1,0:T(8,128)(2,1)S(1)}, u32[]{:S(2)}) copy-start(bf16[80,1024]{1,0:T(8,128)(2,1)S(1)} %get-tuple-element.72.refs_13_.refs_7_) | copy-start | bytes 491524
  76.1 14.2 %copy-start.8 = (bf16[80,1024]{1,0:T(8,128)(2,1)}, bf16[80,1024]{1,0:T(8,128)(2,1)S(1)}, u32[]{:S(2)}) copy-start(bf16[80,1024]{1,0:T(8,128)(2,1)S(1)} %get-tuple-element.73.refs_11_.refs_5_) | copy-start | bytes 491524
  76.2 14.1 %copy-start.9 = (bf16[80,1024]{1,0:T(8,128)(2,1)}, bf16[80,1024]{1,0:T(8,128)(2,1)S(1)}, u32[]{:S(2)}) copy-start(bf16[80,1024]{1,0:T(8,128)(2,1)S(1)} %get-tuple-element.68.refs_17_.refs_11_) | copy-start | bytes 491524
  76.2 14.1 %copy-start.10 = (bf16[80,1024]{1,0:T(8,128)(2,1)}, bf16[80,1024]{1,0:T(8,128)(2,1)S(1)}, u32[]{:S(2)}) copy-start(bf16[80,1024]{1,0:T(8,128)(2,1)S(1)} %get-tuple-element.69.refs_15_.refs_9_) | copy-start | bytes 491524
  76.2 14.1 %copy-start.11 = (bf16[80,1024]{1,0:T(8,128)(2,1)}, bf16[80,1024]{1,0:T(8,128)(2,1)S(1)}, u32[]{:S(2)}) copy-start(bf16[80,1024]{1,0:T(8,128)(2,1)S(1)} %get-tuple-element.64.refs_21_.refs_15_) | copy-start | bytes 491524
  76.2 14.1 %copy-start.12 = (bf16[80,1024]{1,0:T(8,128)(2,1)}, bf16[80,1024]{1,0:T(8,128)(2,1)S(1)}, u32[]{:S(2)}) copy-start(bf16[80,1024]{1,0:T(8,128)(2,1)S(1)} %get-tuple-element.65.refs_19_.refs_13_) | copy-start | bytes 491524
  76.3 14.1 %copy-start.14 = (bf16[80,1024]{1,0:T(8,128)(2,1)}, bf16[80,1024]{1,0:T(8,128)(2,1)S(1)}, u32[]{:S(2)}) copy-start(bf16[80,1024]{1,0:T(8,128)(2,1)S(1)} %collective-permute-done.20.refs_9_.refs_3_) | copy-start | bytes 491524
  90.4 0.8 copy-start.15
  91.1 21.2 %collective-permute-start.28 = (bf16[256,320]{1,0:T(8,128)(2,1)S(1)}, bf16[256,320]{1,0:T(8,128)(2,1)S(1)}, u32[]{:S(2)}, u32[]{:S(2)}) collective-permute-start(bf16[256,320]{1,0:T(8,128)(2,1)S(1)} %get-tuple-element.49), channel_id=1, source_target_pairs={{0,0},{1,4},{2,2},{3,6},{4,1},{5,5},{6,3},{7,7},{8,8},{9,12},{10,1... | collective-permute-start | bytes 491528 | tf_op jit(solution)/shard_map/ppermute | solution.py:21
  91.8 20.6 %collective-permute-start.29 = (bf16[256,320]{1,0:T(8,128)(2,1)S(1)}, bf16[256,320]{1,0:T(8,128)(2,1)S(1)}, u32[]{:S(2)}, u32[]{:S(2)}) collective-permute-start(bf16[256,320]{1,0:T(8,128)(2,1)S(1)} %get-tuple-element.50), channel_id=1, source_target_pairs={{0,2},{1,6},{2,0},{3,4},{4,3},{5,7},{6,1},{7,5},{8,10},{9,14},{10,... | collective-permute-start | bytes 491528 | tf_op jit(solution)/shard_map/ppermute | solution.py:21
  96.5 5.8 %collective-permute-start.32 = (f32[40,128]{1,0:T(8,128)}, f32[40,128]{1,0:T(8,128)S(1)}, u32[]{:S(2)}, u32[]{:S(2)}) collective-permute-start(f32[40,128]{1,0:T(8,128)} %get-tuple-element.53), channel_id=1, source_target_pairs={{0,8},{1,9},{2,10},{3,11},{4,12},{5,13},{6,14},{7,15},{8,0},{9,1},... | collective-permute-start | bytes 61448 | tf_op jit(solution)/shard_map/ppermute | solution.py:21
  99.7 3.6 %collective-permute-start.33 = (f32[40,128]{1,0:T(8,128)}, f32[40,128]{1,0:T(8,128)S(1)}, u32[]{:S(2)}, u32[]{:S(2)}) collective-permute-start(f32[40,128]{1,0:T(8,128)} %get-tuple-element.54), channel_id=1, source_target_pairs={{0,1},{1,0},{2,3},{3,2},{4,5},{5,4},{6,7},{7,6},{8,9},{9,8},{10,11... | collective-permute-start | bytes 61448 | tf_op jit(solution)/shard_map/ppermute | solution.py:21
  102.3 4.4 %collective-permute-start.34 = (f32[40,128]{1,0:T(8,128)}, f32[40,128]{1,0:T(8,128)S(1)}, u32[]{:S(2)}, u32[]{:S(2)}) collective-permute-start(f32[40,128]{1,0:T(8,128)} %get-tuple-element.55), channel_id=1, source_target_pairs={{0,9},{1,8},{2,11},{3,10},{4,13},{5,12},{6,15},{7,14},{8,1},{9,0},... | collective-permute-start | bytes 61448 | tf_op jit(solution)/shard_map/ppermute | solution.py:21
  102.3 4.3 %copy-start.19 = (f32[40,128]{1,0:T(8,128)}, f32[40,128]{1,0:T(8,128)S(1)}, u32[]{:S(2)}) copy-start(f32[40,128]{1,0:T(8,128)S(1)} %collective-permute-done.32.refs_1_) | copy-start | bytes 61444
  103.3 3.3 %copy-start.20 = (f32[40,128]{1,0:T(8,128)}, f32[40,128]{1,0:T(8,128)S(1)}, u32[]{:S(2)}) copy-start(f32[40,128]{1,0:T(8,128)S(1)} %collective-permute-done.33.refs_2_) | copy-start | bytes 61444
  106.6 0.6 copy-start.21
  108.8 4.2 %collective-permute-start.35 = (bf16[2,384]{1,0:T(2,128)(2,1)}, bf16[2,384]{1,0:T(2,128)(2,1)S(1)}, u32[]{:S(2)}, u32[]{:S(2)}) collective-permute-start(bf16[2,384]{1,0:T(2,128)(2,1)} %get-tuple-element.57), channel_id=1, source_target_pairs={{0,2},{1,3},{2,0},{3,1},{4,6},{5,7},{6,4},{7,5},{8,10},{9,11},{10,... | collective-permute-start | bytes 4616 | tf_op jit(solution)/shard_map/ppermute | solution.py:21
  109.4 3.8 %collective-permute-start.36 = (bf16[2,384]{1,0:T(2,128)(2,1)}, bf16[2,384]{1,0:T(2,128)(2,1)S(1)}, u32[]{:S(2)}, u32[]{:S(2)}) collective-permute-start(bf16[2,384]{1,0:T(2,128)(2,1)} %get-tuple-element.58), channel_id=1, source_target_pairs={{0,4},{1,5},{2,6},{3,7},{4,0},{5,1},{6,2},{7,3},{8,12},{9,13},{10,... | collective-permute-start | bytes 4616 | tf_op jit(solution)/shard_map/ppermute | solution.py:21
  111.2 4.7 %collective-permute-start.37 = (bf16[2,384]{1,0:T(2,128)(2,1)}, bf16[2,384]{1,0:T(2,128)(2,1)S(1)}, u32[]{:S(2)}, u32[]{:S(2)}) collective-permute-start(bf16[2,384]{1,0:T(2,128)(2,1)} %get-tuple-element.59), channel_id=1, source_target_pairs={{0,6},{1,7},{2,4},{3,5},{4,2},{5,3},{6,0},{7,1},{8,14},{9,15},{10,... | collective-permute-start | bytes 4616 | tf_op jit(solution)/shard_map/ppermute | solution.py:21
  112.3 5.1 %collective-permute-start.30 = (bf16[128,320]{1,0:T(8,128)(2,1)S(1)}, bf16[128,320]{1,0:T(8,128)(2,1)S(1)}, u32[]{:S(2)}, u32[]{:S(2)}) collective-permute-start(bf16[128,320]{1,0:T(8,128)(2,1)S(1)} %constant_dynamic-slice_fusion.1), channel_id=1, source_target_pairs={{0,1},{1,0},{2,3},{3,2},{4,5},{5,4},{6,7},{7,6},{8,9},{9,8},{10,11... | collective-permute-start | bytes 245768 | tf_op jit(solution)/shard_map/ppermute | solution.py:21
  112.4 4.9 %collective-permute-start.31 = (bf16[128,320]{1,0:T(8,128)(2,1)S(1)}, bf16[128,320]{1,0:T(8,128)(2,1)S(1)}, u32[]{:S(2)}, u32[]{:S(2)}) collective-permute-start(bf16[128,320]{1,0:T(8,128)(2,1)S(1)} %constant_dynamic-slice_fusion), channel_id=1, source_target_pairs={{0,1},{1,0},{2,3},{3,2},{4,5},{5,4},{6,7},{7,6},{8,9},{9,8},{10,11... | collective-permute-start | bytes 245768 | tf_op jit(solution)/shard_map/ppermute | solution.py:21

commit v5 on v4

--- a/solution.py
+++ b/solution.py
@@ -110,6 +110,7 @@
         in_specs=[SMEM] + [VMEM] * (1 + len(small)),
         out_specs=(VMEM, VMEM),
         scratch_shapes=[pltpu.VMEM((rows, HD), F32)],
+        compiler_params=pltpu.CompilerParams(vmem_limit_bytes=8 * 1024 * 1024),
     )(spot, weight, *small)
 
 
@@ -367,6 +368,7 @@
             pltpu.VMEM((count, HD), F32),
             pltpu.VMEM((5 * count, GROUP), F32),
         ],
+        compiler_params=pltpu.CompilerParams(vmem_limit_bytes=12 * 1024 * 1024),
     )(table, memory, *parts)
 
 
@@ -392,6 +394,7 @@
         in_specs=[VMEM] * len(parts),
         out_specs=(VMEM,) * 4,
         scratch_shapes=[pltpu.VMEM((8, 384), F32)],
+        compiler_params=pltpu.CompilerParams(vmem_limit_bytes=4 * 1024 * 1024),
     )(*parts)
 
 
@@ -452,8 +455,9 @@
         both = [part for piece in small for part in (piece, swap(piece, n, 1))]
         mine, theirs = pack(table, qkv_weight, *both)
         across = carry(theirs, 0, 2)
-        mine_late, across_late, pair, near, far, stem_x = lax.optimization_barrier(
-            (mine, across, pair, near, far, stem_x)
+        stem_c = swap(stem, n, 1)
+        mine_late, across_late, pair, near, stem_x, stem_c = lax.optimization_barrier(
+            (mine, across, pair, near, stem_x, stem_c)
         )
         halo = jnp.where((z == 1) | (z == 2), near, far)
         pair_x = swap(pair, n, 2)
@@ -470,8 +474,8 @@
         here = {0: lax.dynamic_index_in_dim(across, p, 0, keepdims=False)}
         for turn in (1, 2, 3):
             here[turn] = carry(ready[turn % 2], 0, 4 * turn)
-        here[3], here[2], pair_x, halo_x = lax.optimization_barrier(
-            (here[3], here[2], pair_x, halo_x)
+        here[3], here[2], here[0], pair, pair_x, halo, halo_x, stem_x, mine = lax.optimization_barrier(
+            (here[3], here[2], here[0], pair, pair_x, halo, halo_x, stem_x, mine)
         )
         own_part = lax.dynamic_index_in_dim(mine, p, 0, keepdims=False)
         weights = [own_part, swap(own_part, n, 1)]
@@ -486,6 +490,7 @@
         aside = [(d, d ^ 1) for d in range(n) if d % 2 == d // 8]
         halo_layer = [halo, send(halo, aside), halo_x, send(halo_x, aside)]
     else:
+        stem_c = swap(stem, n, 1)
         far = swap(near, n, 4)
         left = jnp.where(p == 0, near, far)
         right = jnp.where(p == 0, far, near)
@@ -512,7 +517,7 @@
         marks = lax.dynamic_slice_in_dim(marks, 512 * quarter, 1536, 0)
         extra = [jnp.broadcast_to(marks[None], (8, 1536))]
         pair_x = swap(pair, n, 2)
-    own_layer = [stem, swap(stem, n, 1), stem_x, swap(stem_x, n, 1)]
+    own_layer = [stem, stem_c, stem_x, swap(stem_x, n, 1)]
     pair_layer = [pair, swap(pair, n, 1), pair_x, swap(pair_x, n, 1)]
     layered = [norm_layer(table, gain, blocks) for blocks in (own_layer, pair_layer, halo_layer)]
     held, stay, leave = encoder(table, layered, weights, depth, extra)

time: 119 us -> 105 us (0.88)
  waiting for transfers between devices: 35.6 us -> 22.6 us
  Pallas kernels: 25.8 us -> 21 us
  starting transfers between devices: 48.2 us -> 52.3 us
    ppermute x30, waiting for transfers between devices: 22.8 us -> 7.58 us  [send(): return lax.ppermute(block, 'tm', route)]
    ppermute x8, starting transfers between devices: 21.5 us -> 25.7 us  [carry(): return lax.ppermute(block, ('utt', 'tm'), route)]
    ppermute x8, waiting for transfers between devices: 12.8 us -> 15 us  [carry(): return lax.ppermute(block, ('utt', 'tm'), route)]
    pallas_call x1, Pallas kernels: 3.2 us -> 1.19 us  [cross_partial(): pl.pallas_call(functools.partial(cross_kernel, chips, base), out_shape=(j...]
    pallas_call x1, Pallas kernels: 1.62 us -> 0.23 us  [merge(): pl.pallas_call(merge_kernel, out_shape=(jax.ShapeDtypeStruct((2, 384), BF...]
    pallas_call x1, Pallas kernels: 2.39 us -> 1.02 us  [pack(): pl.pallas_call(pack_kernel, out_shape=(shape, shape), in_specs=[SMEM] + [...]
    unnamed x50 -> x12, local copies, waits for them, and re-layouts: 2.03 us -> 3.11 us
  transfers between devices with their start and end apart: 38 -> 38, of which waited for: 11 -> 10; matrix products, arithmetic and copies ran while one was open for 4% -> 3% of each run, Pallas kernels for 10% -> 7%
where the time goes in v5:
time: 105 us; the launch traced here: 104 us
  starting transfers between devices  52.3 us (50%)
  waiting for transfers between devices  22.6 us (22%)
  Pallas kernels  21 us (20%)
  local copies, waits for them, and re-layouts  5.07 us (5%)
  other arithmetic  2.12 us (2%)
  between operations  1.23 us (1%)
    ppermute x30, starting transfers between devices, send(): return lax.ppermute(block, 'tm', route)  26.6 us
    ppermute x8, starting transfers between devices, carry(): return lax.ppermute(block, ('utt', 'tm'), route)  25.7 us
    ppermute x8, waiting for transfers between devices, carry(): return lax.ppermute(block, ('utt', 'tm'), route)  15 us
    pallas_call x1, Pallas kernels, encoder(): pl.pallas_call(functools.partial(encoder_kernel, len(parts), depth, not e...  13.9 us
    ppermute x30, waiting for transfers between devices, send(): return lax.ppermute(block, 'tm', route)  7.58 us
    pallas_call x3, Pallas kernels, norm_layer(): pl.pallas_call(functools.partial(norm_kernel, len(blocks) // 4), out_shap...  4.7 us
    unnamed x12, local copies, waits for them, and re-layouts  3.11 us
  transfers between devices with their start and end apart: 38, of which 10 were waited for; matrix products, arithmetic and copies ran while one was open for 3% of the time, Pallas kernels for 7%

profile of v5, /device:TPU:0, one launch (start us, length us, event | category | flops | bytes accessed | tf_op | source)
XLA Modules:
  0.0 104.3 jit_solution(17822318239364435448)
XLA Ops:
  0.6 3.1 %collective-permute-start.4 = (bf16[128,1280]{1,0:T(8,128)(2,1)}, bf16[128,1280]{1,0:T(8,128)(2,1)S(1)}, u32[]{:S(2)}, u32[]{:S(2)}) collective-permute-start(bf16[128,1280]{1,0:T(8,128)(2,1)} %refs_0_.3), channel_id=1, source_target_pairs={{0,4},{1,5},{2,6},{3,7},{4,0},{5,1},{6,2},{7,3},{8,12},{9,13},{10,... | collective-permute-start | bytes 983048 | tf_op jit(solution)/shard_map/ppermute | solution.py:21
  3.7 0.7 collective-permute-start.5
  4.4 0.1 collective-permute-start
  4.5 0.5 collective-permute-start.1
  5.0 0.1 collective-permute-start.2
  5.1 0.1 stack.131.spot.table.places
  5.2 0.8 collective-permute-done.1.refs_3_
  6.0 1.5 %collective-permute-start.6 = (bf16[128,1280]{1,0:T(8,128)(2,1)}, bf16[128,1280]{1,0:T(8,128)(2,1)S(1)}, u32[]{:S(2)}, u32[]{:S(2)}) collective-permute-start(bf16[128,1280]{1,0:T(8,128)(2,1)} %refs_0_.3), channel_id=1, source_target_pairs={{0,2},{1,3},{2,0},{3,1},{4,6},{5,7},{6,4},{7,5},{8,10},{9,11},{10,... | collective-permute-start | bytes 983048 | tf_op jit(solution)/shard_map/ppermute | solution.py:21
  7.5 0.0 collective-permute-start.7
  7.5 1.1 %copy-done = bf16[80,3840]{1,0:T(8,128)(2,1)S(1)} copy-done((bf16[80,3840]{1,0:T(8,128)(2,1)S(1)}, bf16[80,3840]{1,0:T(8,128)(2,1)}, u32[]{:S(2)}) %copy-start) | copy-done | bytes 614424
  8.6 0.7 copy-done.2
  9.3 0.7 copy-done.3
  10.0 0.7 copy-done.4
  10.6 1.0 shard_map.77
  11.7 2.4 %collective-permute-start.3 = (bf16[2,80,1024]{2,1,0:T(8,128)(2,1)S(1)}, bf16[2,80,1024]{2,1,0:T(8,128)(2,1)S(1)}, u32[]{:S(2)}, u32[]{:S(2)}) collective-permute-start(bf16[2,80,1024]{2,1,0:T(8,128)(2,1)S(1)} %get-tuple-element.37), channel_id=1, source_target_pairs={{0,2},{2,0},{4,6},{6,4},{8,10},{10,8},{12,14},{14,12},{17,19},{19,... | collective-permute-start | bytes 983048 | tf_op jit(solution)/shard_map/ppermute | solution.py:451
  14.2 1.3 %collective-permute-start.11 = (bf16[128,1280]{1,0:T(8,128)(2,1)}, bf16[128,1280]{1,0:T(8,128)(2,1)S(1)}, u32[]{:S(2)}, u32[]{:S(2)}) collective-permute-start(bf16[128,1280]{1,0:T(8,128)(2,1)} %refs_0_.3), channel_id=1, source_target_pairs={{4,12},{5,13},{6,14},{7,15},{8,0},{9,1},{10,2},{11,3},{20,28},{21,... | collective-permute-start | bytes 983048 | tf_op jit(solution)/shard_map/ppermute | solution.py:21
  15.5 0.7 collective-permute-done.6.refs_2_
  16.2 4.5 %collective-permute-done.3 = bf16[2,80,1024]{2,1,0:T(8,128)(2,1)S(1)} collective-permute-done((bf16[2,80,1024]{2,1,0:T(8,128)(2,1)S(1)}, bf16[2,80,1024]{2,1,0:T(8,128)(2,1)S(1)}, u32[]{:S(2)}, u32[]{:S(2)}) %collective-permute-start.3) | collective-permute-done | bytes 327712 | tf_op jit(solution)/shard_map/ppermute | solution.py:451
  20.7 0.8 pad_maximum_fusion
  21.5 4.4 %collective-permute-start.8 = (bf16[160,1024]{1,0:T(8,128)(2,1)}, bf16[160,1024]{1,0:T(8,128)(2,1)S(1)}, u32[]{:S(2)}, u32[]{:S(2)}) collective-permute-start(bf16[160,1024]{1,0:T(8,128)(2,1)} %bitcast.31), channel_id=1, source_target_pairs={{0,12},{2,14},{4,8},{6,10},{8,4},{10,6},{12,0},{14,2},{17,29},{19,... | collective-permute-start | bytes 983048 | tf_op jit(solution)/shard_map/ppermute | solution.py:451
  25.9 5.3 %collective-permute-start.9 = (bf16[160,1024]{1,0:T(8,128)(2,1)S(1)}, bf16[160,1024]{1,0:T(8,128)(2,1)S(1)}, u32[]{:S(2)}, u32[]{:S(2)}) collective-permute-start(bf16[160,1024]{1,0:T(8,128)(2,1)S(1)} %bitcast.39), channel_id=1, source_target_pairs={{0,8},{2,10},{4,12},{6,14},{8,0},{10,2},{12,4},{14,6},{17,25},{19,... | collective-permute-start | bytes 983048 | tf_op jit(solution)/shard_map/ppermute | solution.py:451
  31.2 0.6 collective-permute-start.10
  31.8 1.6 %collective-permute-start.12 = (bf16[128,1280]{1,0:T(8,128)(2,1)S(1)}, bf16[128,1280]{1,0:T(8,128)(2,1)S(1)}, u32[]{:S(2)}, u32[]{:S(2)}) collective-permute-start(bf16[128,1280]{1,0:T(8,128)(2,1)S(1)} %broadcast_select_fusion.3.refs_0_), channel_id=1, source_target_pairs={{0,2},{1,3},{2,0},{3,1},{4,6},{5,7},{6,4},{7,5},{8,10},{9,11},{10,... | collective-permute-start | bytes 983048 | tf_op jit(solution)/shard_map/ppermute | solution.py:21
  33.4 1.9 %collective-permute-start.21 = (bf16[160,1024]{1,0:T(8,128)(2,1)}, bf16[160,1024]{1,0:T(8,128)(2,1)}, u32[]{:S(2)}, u32[]{:S(2)}) collective-permute-start(bf16[160,1024]{1,0:T(8,128)(2,1)} %bitcast.31), channel_id=1, source_target_pairs={{0,4},{2,6},{4,0},{6,2},{8,12},{10,14},{12,8},{14,10},{17,21},{19,... | collective-permute-start | bytes 983048 | tf_op jit(solution)/shard_map/ppermute | solution.py:451
  35.4 7.7 %collective-permute-done.9 = bf16[160,1024]{1,0:T(8,128)(2,1)S(1)} collective-permute-done((bf16[160,1024]{1,0:T(8,128)(2,1)S(1)}, bf16[160,1024]{1,0:T(8,128)(2,1)S(1)}, u32[]{:S(2)}, u32[]{:S(2)}) %collective-permute-start.9) | collective-permute-done | bytes 327712 | tf_op jit(solution)/shard_map/ppermute | solution.py:451
  43.1 2.0 %collective-permute-start.19 = (bf16[80,1024]{1,0:T(8,128)(2,1)S(1)}, bf16[80,1024]{1,0:T(8,128)(2,1)}, u32[]{:S(2)}, u32[]{:S(2)}) collective-permute-start(bf16[80,1024]{1,0:T(8,128)(2,1)S(1)} %dynamic-slice_bitcast_fusion.1), channel_id=1, source_target_pairs={{0,16},{2,18},{4,20},{6,22},{8,24},{10,26},{12,28},{14,30},{17,1},... | collective-permute-start | bytes 491528 | tf_op jit(solution)/shard_map/ppermute | solution.py:451
  45.1 0.5 collective-permute-start.14
  45.6 0.1 collective-permute-start.15
  45.6 0.5 collective-permute-done.21
  46.2 1.3 %collective-permute-start.22 = (bf16[160,1024]{1,0:T(8,128)(2,1)}, bf16[160,1024]{1,0:T(8,128)(2,1)S(1)}, u32[]{:S(2)}, u32[]{:S(2)}) collective-permute-start(bf16[160,1024]{1,0:T(8,128)(2,1)} %collective-permute-done.21), channel_id=1, source_target_pairs={{0,16},{2,18},{4,20},{6,22},{8,24},{10,26},{12,28},{14,30},{17,1},... | collective-permute-start | bytes 983048 | tf_op jit(solution)/shard_map/ppermute | solution.py:451
  47.5 4.2 %collective-permute-start.24 = (bf16[160,1024]{1,0:T(8,128)(2,1)S(1)}, bf16[160,1024]{1,0:T(8,128)(2,1)S(1)}, u32[]{:S(2)}, u32[]{:S(2)}) collective-permute-start(bf16[160,1024]{1,0:T(8,128)(2,1)S(1)} %collective-permute-done.9), channel_id=1, source_target_pairs={{0,16},{2,18},{4,20},{6,22},{8,24},{10,26},{12,28},{14,30},{17,1},... | collective-permute-start | bytes 983048 | tf_op jit(solution)/shard_map/ppermute | solution.py:451
  51.7 0.6 collective-permute-done.22
  52.4 4.3 %collective-permute-start.26 = (bf16[160,1024]{1,0:T(8,128)(2,1)S(1)}, bf16[160,1024]{1,0:T(8,128)(2,1)S(1)}, u32[]{:S(2)}, u32[]{:S(2)}) collective-permute-start(bf16[160,1024]{1,0:T(8,128)(2,1)S(1)} %collective-permute-done.8), channel_id=1, source_target_pairs={{0,16},{2,18},{4,20},{6,22},{8,24},{10,26},{12,28},{14,30},{17,1},... | collective-permute-start | bytes 983048 | tf_op jit(solution)/shard_map/ppermute | solution.py:451
  56.7 1.0 broadcast_select_fusion.2
  57.7 1.8 %collective-permute-start.16 = (bf16[128,1280]{1,0:T(8,128)(2,1)S(1)}, bf16[128,1280]{1,0:T(8,128)(2,1)S(1)}, u32[]{:S(2)}, u32[]{:S(2)}) collective-permute-start(bf16[128,1280]{1,0:T(8,128)(2,1)S(1)} %broadcast_select_fusion.3.refs_0_), channel_id=1, source_target_pairs={{0,1},{2,3},{4,5},{6,7},{9,8},{11,10},{13,12},{15,14},{16,17},{18,... | collective-permute-start | bytes 983048 | tf_op jit(solution)/shard_map/ppermute | solution.py:21
  59.6 1.6 %collective-permute-done.26 = bf16[160,1024]{1,0:T(8,128)(2,1)S(1)} collective-permute-done((bf16[160,1024]{1,0:T(8,128)(2,1)S(1)}, bf16[160,1024]{1,0:T(8,128)(2,1)S(1)}, u32[]{:S(2)}, u32[]{:S(2)}) %collective-permute-start.26) | collective-permute-done | bytes 327712 | tf_op jit(solution)/shard_map/ppermute | solution.py:451
  61.2 2.6 %collective-permute-start.17 = (bf16[128,1280]{1,0:T(8,128)(2,1)S(1)}, bf16[128,1280]{1,0:T(8,128)(2,1)S(1)}, u32[]{:S(2)}, u32[]{:S(2)}) collective-permute-start(bf16[128,1280]{1,0:T(8,128)(2,1)S(1)} %collective-permute-done.12.refs_2_), channel_id=1, source_target_pairs={{0,1},{2,3},{4,5},{6,7},{9,8},{11,10},{13,12},{15,14},{16,17},{18,... | collective-permute-start | bytes 983048 | tf_op jit(solution)/shard_map/ppermute | solution.py:21
  63.9 0.1 collective-permute-start.23
  64.0 0.6 collective-permute-start.25
  64.6 1.6 %shard_map.78 = (bf16[512,1280]{1,0:T(8,128)(2,1)S(1)}, bf16[512,320]{1,0:T(8,128)(2,1)S(1)}) custom-call(s32[34]{0:T(128)S(1)} %stack.131.spot.table.places, f32[1,1280]{1,0:T(1,128)S(1)} %reshape.16.gain, bf16[128,1280]{1,0:T(8,128)(2,1)S(1)} %copy-done.1, bf16[128,1280]{1,0:T(8,128)(2,1)S(1)} %collective-permute-done.7.refs_1_, ...), custom_call_target="tpu_custom_call" | custom-call | tf_op jit(solution)/shard_map/pallas_call | solution.py:141
  66.2 0.1 collective-permute-start.18
  66.3 1.6 %shard_map.79 = (bf16[512,1280]{1,0:T(8,128)(2,1)S(1)}, bf16[512,320]{1,0:T(8,128)(2,1)S(1)}) custom-call(s32[34]{0:T(128)S(1)} %stack.131.spot.table.places, f32[1,1280]{1,0:T(1,128)S(1)} %reshape.16.gain, bf16[128,1280]{1,0:T(8,128)(2,1)S(1)} %collective-permute-done.4.refs_0_, bf16[128,1280]{1,0:T(8,128)(2,1)S(1)} %collective-permute-done.14.refs_1_, ...), custom_call_target="tpu_custom_call" | custom-call | tf_op jit(solution)/shard_map/pallas_call | solution.py:141
  67.9 0.6 collective-permute-start.20
  68.4 0.1 collective-permute-start.27
  68.5 1.6 %shard_map.80 = (bf16[512,1280]{1,0:T(8,128)(2,1)S(1)}, bf16[512,320]{1,0:T(8,128)(2,1)S(1)}) custom-call(s32[34]{0:T(128)S(1)} %stack.131.spot.table.places, f32[1,1280]{1,0:T(1,128)S(1)} %reshape.16.gain, bf16[128,1280]{1,0:T(8,128)(2,1)S(1)} %broadcast_select_fusion.3.refs_0_, bf16[128,1280]{1,0:T(8,128)(2,1)S(1)} %collective-permute-done.16.refs_1_, ...), custom_call_target="tpu_custom_call" | custom-call | tf_op jit(solution)/shard_map/pallas_call | solution.py:141
  70.2 13.9 %shard_map.81 = (bf16[512,320]{1,0:T(8,128)(2,1)S(1)}, bf16[256,320]{1,0:T(8,128)(2,1)S(1)}, bf16[256,320]{1,0:T(8,128)(2,1)S(1)}) custom-call(s32[34]{0:T(128)S(1)} %stack.131.spot.table.places, bf16[512,1280]{1,0:T(8,128)(2,1)S(1)} %get-tuple-element.45.refs_0_, bf16[512,320]{1,0:T(8,128)(2,1)S(1)} %get-tuple-element.46.refs_1_, ...), custom_call_target="tpu_custom_call" | custom-call | tf_op jit(solution)/shard_map/pallas_call | solution.py:282
  84.1 0.7 collective-permute-start.28
  84.8 0.6 collective-permute-start.29
  85.4 1.2 %shard_map.82 = (f32[40,128]{1,0:T(8,128)S(1)}, f32[40,128]{1,0:T(8,128)S(1)}, f32[40,128]{1,0:T(8,128)S(1)}, f32[40,128]{1,0:T(8,128)S(1)}) custom-call(s32[34]{0:T(128)S(1)} %stack.131.spot.table.places, bf16[512,320]{1,0:T(8,128)(2,1)S(1)} %get-tuple-element.61.memory, bf16[80,1024]{1,0:T(8,128)(2,1)S(1)} %dynamic-slice_bitcast_fusion.refs_6_.refs_0_.refs_1_, ...), custom_call_target="tpu_custom_call" | custom-call | tf_op jit(solution)/shard_map/pallas_call | solution.py:361
  86.6 0.3 collective-permute-start.32
  86.8 3.8 %collective-permute-start.33 = (f32[40,128]{1,0:T(8,128)S(1)}, f32[40,128]{1,0:T(8,128)S(1)}, u32[]{:S(2)}, u32[]{:S(2)}) collective-permute-start(f32[40,128]{1,0:T(8,128)S(1)} %get-tuple-element.64), channel_id=1, source_target_pairs={{0,1},{1,0},{2,3},{3,2},{4,5},{5,4},{6,7},{7,6},{8,9},{9,8},{10,11... | collective-permute-start | bytes 61448 | tf_op jit(solution)/shard_map/ppermute | solution.py:21
  90.6 1.4 %collective-permute-start.34 = (f32[40,128]{1,0:T(8,128)S(1)}, f32[40,128]{1,0:T(8,128)S(1)}, u32[]{:S(2)}, u32[]{:S(2)}) collective-permute-start(f32[40,128]{1,0:T(8,128)S(1)} %get-tuple-element.65), channel_id=1, source_target_pairs={{0,9},{1,8},{2,11},{3,10},{4,13},{5,12},{6,15},{7,14},{8,1},{9,0},... | collective-permute-start | bytes 61448 | tf_op jit(solution)/shard_map/ppermute | solution.py:21
  92.0 3.0 %collective-permute-done.34.refs_3_ = f32[40,128]{1,0:T(8,128)S(1)} collective-permute-done((f32[40,128]{1,0:T(8,128)S(1)}, f32[40,128]{1,0:T(8,128)S(1)}, u32[]{:S(2)}, u32[]{:S(2)}) %collective-permute-start.34) | collective-permute-done | bytes 20512 | tf_op jit(solution)/shard_map/ppermute | solution.py:21
  95.0 0.2 shard_map.83
  95.2 1.1 %collective-permute-start.35 = (bf16[2,384]{1,0:T(2,128)(2,1)S(1)}, bf16[2,384]{1,0:T(2,128)(2,1)S(1)}, u32[]{:S(2)}, u32[]{:S(2)}) collective-permute-start(bf16[2,384]{1,0:T(2,128)(2,1)S(1)} %get-tuple-element.67), channel_id=1, source_target_pairs={{0,2},{1,3},{2,0},{3,1},{4,6},{5,7},{6,4},{7,5},{8,10},{9,11},{10,... | collective-permute-start | bytes 4616 | tf_op jit(solution)/shard_map/ppermute | solution.py:21
  96.3 1.7 %collective-permute-start.36 = (bf16[2,384]{1,0:T(2,128)(2,1)S(1)}, bf16[2,384]{1,0:T(2,128)(2,1)S(1)}, u32[]{:S(2)}, u32[]{:S(2)}) collective-permute-start(bf16[2,384]{1,0:T(2,128)(2,1)S(1)} %get-tuple-element.68), channel_id=1, source_target_pairs={{0,4},{1,5},{2,6},{3,7},{4,0},{5,1},{6,2},{7,3},{8,12},{9,13},{10,... | collective-permute-start | bytes 4616 | tf_op jit(solution)/shard_map/ppermute | solution.py:21
  98.0 0.8 collective-permute-start.37
  98.8 0.1 collective-permute-start.30
  98.9 0.5 collective-permute-start.31
  99.5 0.4 collective-permute-done.36
  99.9 2.6 %collective-permute-done.37 = bf16[2,384]{1,0:T(2,128)(2,1)S(1)} collective-permute-done((bf16[2,384]{1,0:T(2,128)(2,1)S(1)}, bf16[2,384]{1,0:T(2,128)(2,1)S(1)}, u32[]{:S(2)}, u32[]{:S(2)}) %collective-permute-start.37) | collective-permute-done | bytes 1568 | tf_op jit(solution)/shard_map/ppermute | solution.py:21
  102.5 0.7 concatenate.15
  103.2 0.1 select_select_fusion
  103.5 0.8 concatenate.14
  (71 shorter events, 0.6 us)
Async XLA Ops:
  0.6 13.5 %collective-permute-start.4 = (bf16[128,1280]{1,0:T(8,128)(2,1)}, bf16[128,1280]{1,0:T(8,128)(2,1)S(1)}, u32[]{:S(2)}, u32[]{:S(2)}) collective-permute-start(bf16[128,1280]{1,0:T(8,128)(2,1)} %refs_0_.3), channel_id=1, source_target_pairs={{0,4},{1,5},{2,6},{3,7},{4,0},{5,1},{6,2},{7,3},{8,12},{9,13},{10,... | collective-permute-start | bytes 983048 | tf_op jit(solution)/shard_map/ppermute | solution.py:21
  3.7 11.7 %collective-permute-start.5 = (bf16[128,1280]{1,0:T(8,128)(2,1)}, bf16[128,1280]{1,0:T(8,128)(2,1)S(1)}, u32[]{:S(2)}, u32[]{:S(2)}) collective-permute-start(bf16[128,1280]{1,0:T(8,128)(2,1)} %refs_0_.3), channel_id=1, source_target_pairs={{4,8},{5,9},{6,10},{7,11},{8,4},{9,5},{10,6},{11,7},{20,24},{21,25... | collective-permute-start | bytes 983048 | tf_op jit(solution)/shard_map/ppermute | solution.py:21
  4.4 3.1 %collective-permute-start = (bf16[2,1280]{1,0:T(2,128)(2,1)}, bf16[2,1280]{1,0:T(2,128)(2,1)S(1)}, u32[]{:S(2)}, u32[]{:S(2)}) collective-permute-start(bf16[2,1280]{1,0:T(2,128)(2,1)} %refs_0_.2), channel_id=1, source_target_pairs={{0,1},{1,0},{2,3},{3,2},{4,5},{5,4},{6,7},{7,6},{8,9},{9,8},{10,11... | collective-permute-start | bytes 15368 | tf_op jit(solution)/shard_map/ppermute | solution.py:21
  4.5 1.5 %collective-permute-start.1 = (s32[2,16]{1,0:T(2,128)}, s32[2,16]{1,0:T(2,128)S(1)}, u32[]{:S(2)}, u32[]{:S(2)}) collective-permute-start(s32[2,16]{1,0:T(2,128)} %refs_2_.1), channel_id=1, source_target_pairs={{0,1},{1,0},{2,3},{3,2},{4,5},{5,4},{6,7},{7,6},{8,9},{9,8},{10,11... | collective-permute-start | bytes 392 | tf_op jit(solution)/shard_map/ppermute | solution.py:21
  5.0 2.5 %collective-permute-start.2 = (s32[1,128]{1,0:T(1,128)}, s32[1,128]{1,0:T(1,128)S(1)}, u32[]{:S(2)}, u32[]{:S(2)}) collective-permute-start(s32[1,128]{1,0:T(1,128)} %bitcast.37), channel_id=1, source_target_pairs={{0,1},{1,0},{2,3},{3,2},{4,5},{5,4},{6,7},{7,6},{8,9},{9,8},{10,11... | collective-permute-start | bytes 1544 | tf_op jit(solution)/shard_map/ppermute | solution.py:21
  6.0 10.1 %collective-permute-start.6 = (bf16[128,1280]{1,0:T(8,128)(2,1)}, bf16[128,1280]{1,0:T(8,128)(2,1)S(1)}, u32[]{:S(2)}, u32[]{:S(2)}) collective-permute-start(bf16[128,1280]{1,0:T(8,128)(2,1)} %refs_0_.3), channel_id=1, source_target_pairs={{0,2},{1,3},{2,0},{3,1},{4,6},{5,7},{6,4},{7,5},{8,10},{9,11},{10,... | collective-permute-start | bytes 983048 | tf_op jit(solution)/shard_map/ppermute | solution.py:21
  7.5 8.7 %collective-permute-start.7 = (bf16[128,1280]{1,0:T(8,128)(2,1)}, bf16[128,1280]{1,0:T(8,128)(2,1)S(1)}, u32[]{:S(2)}, u32[]{:S(2)}) collective-permute-start(bf16[128,1280]{1,0:T(8,128)(2,1)} %refs_0_.3), channel_id=1, source_target_pairs={{0,1},{1,0},{2,3},{3,2},{4,5},{5,4},{6,7},{7,6},{8,9},{9,8},{10,11... | collective-permute-start | bytes 983048 | tf_op jit(solution)/shard_map/ppermute | solution.py:21
  7.5 1.1 %copy-start = (bf16[80,3840]{1,0:T(8,128)(2,1)S(1)}, bf16[80,3840]{1,0:T(8,128)(2,1)}, u32[]{:S(2)}) copy-start(bf16[80,3840]{1,0:T(8,128)(2,1)} %weight.1) | copy-start | bytes 1843204
  8.6 0.7 copy-start.2
  9.3 0.7 copy-start.3
  10.0 0.7 copy-start.4
  11.7 9.0 %collective-permute-start.3 = (bf16[2,80,1024]{2,1,0:T(8,128)(2,1)S(1)}, bf16[2,80,1024]{2,1,0:T(8,128)(2,1)S(1)}, u32[]{:S(2)}, u32[]{:S(2)}) collective-permute-start(bf16[2,80,1024]{2,1,0:T(8,128)(2,1)S(1)} %get-tuple-element.37), channel_id=1, source_target_pairs={{0,2},{2,0},{4,6},{6,4},{8,10},{10,8},{12,14},{14,12},{17,19},{19,... | collective-permute-start | bytes 983048 | tf_op jit(solution)/shard_map/ppermute | solution.py:451
  14.2 17.6 %collective-permute-start.11 = (bf16[128,1280]{1,0:T(8,128)(2,1)}, bf16[128,1280]{1,0:T(8,128)(2,1)S(1)}, u32[]{:S(2)}, u32[]{:S(2)}) collective-permute-start(bf16[128,1280]{1,0:T(8,128)(2,1)} %refs_0_.3), channel_id=1, source_target_pairs={{4,12},{5,13},{6,14},{7,15},{8,0},{9,1},{10,2},{11,3},{20,28},{21,... | collective-permute-start | bytes 983048 | tf_op jit(solution)/shard_map/ppermute | solution.py:21
  20.7 24.3 %copy-start.5 = (f32[1280]{0:T(1024)S(1)}, f32[1280]{0:T(1024)}, u32[]{:S(2)}) copy-start(f32[1280]{0:T(1024)} %param.7) | copy-start | bytes 15364
  21.5 13.9 %collective-permute-start.8 = (bf16[160,1024]{1,0:T(8,128)(2,1)}, bf16[160,1024]{1,0:T(8,128)(2,1)S(1)}, u32[]{:S(2)}, u32[]{:S(2)}) collective-permute-start(bf16[160,1024]{1,0:T(8,128)(2,1)} %bitcast.31), channel_id=1, source_target_pairs={{0,12},{2,14},{4,8},{6,10},{8,4},{10,6},{12,0},{14,2},{17,29},{19,... | collective-permute-start | bytes 983048 | tf_op jit(solution)/shard_map/ppermute | solution.py:451
  25.9 17.2 %collective-permute-start.9 = (bf16[160,1024]{1,0:T(8,128)(2,1)S(1)}, bf16[160,1024]{1,0:T(8,128)(2,1)S(1)}, u32[]{:S(2)}, u32[]{:S(2)}) collective-permute-start(bf16[160,1024]{1,0:T(8,128)(2,1)S(1)} %bitcast.39), channel_id=1, source_target_pairs={{0,8},{2,10},{4,12},{6,14},{8,0},{10,2},{12,4},{14,6},{17,25},{19,... | collective-permute-start | bytes 983048 | tf_op jit(solution)/shard_map/ppermute | solution.py:451
  31.2 11.9 %collective-permute-start.10 = (bf16[128,1280]{1,0:T(8,128)(2,1)S(1)}, bf16[128,1280]{1,0:T(8,128)(2,1)S(1)}, u32[]{:S(2)}, u32[]{:S(2)}) collective-permute-start(bf16[128,1280]{1,0:T(8,128)(2,1)S(1)} %collective-permute-done.4.refs_0_), channel_id=1, source_target_pairs={{0,2},{1,3},{2,0},{3,1},{4,6},{5,7},{6,4},{7,5},{8,10},{9,11},{10,... | collective-permute-start | bytes 983048 | tf_op jit(solution)/shard_map/ppermute | solution.py:21
  31.8 11.3 %collective-permute-start.12 = (bf16[128,1280]{1,0:T(8,128)(2,1)S(1)}, bf16[128,1280]{1,0:T(8,128)(2,1)S(1)}, u32[]{:S(2)}, u32[]{:S(2)}) collective-permute-start(bf16[128,1280]{1,0:T(8,128)(2,1)S(1)} %broadcast_select_fusion.3.refs_0_), channel_id=1, source_target_pairs={{0,2},{1,3},{2,0},{3,1},{4,6},{5,7},{6,4},{7,5},{8,10},{9,11},{10,... | collective-permute-start | bytes 983048 | tf_op jit(solution)/shard_map/ppermute | solution.py:21
  33.4 12.8 %collective-permute-start.21 = (bf16[160,1024]{1,0:T(8,128)(2,1)}, bf16[160,1024]{1,0:T(8,128)(2,1)}, u32[]{:S(2)}, u32[]{:S(2)}) collective-permute-start(bf16[160,1024]{1,0:T(8,128)(2,1)} %bitcast.31), channel_id=1, source_target_pairs={{0,4},{2,6},{4,0},{6,2},{8,12},{10,14},{12,8},{14,10},{17,21},{19,... | collective-permute-start | bytes 983048 | tf_op jit(solution)/shard_map/ppermute | solution.py:451
  43.1 4.4 %collective-permute-start.19 = (bf16[80,1024]{1,0:T(8,128)(2,1)S(1)}, bf16[80,1024]{1,0:T(8,128)(2,1)}, u32[]{:S(2)}, u32[]{:S(2)}) collective-permute-start(bf16[80,1024]{1,0:T(8,128)(2,1)S(1)} %dynamic-slice_bitcast_fusion.1), channel_id=1, source_target_pairs={{0,16},{2,18},{4,20},{6,22},{8,24},{10,26},{12,28},{14,30},{17,1},... | collective-permute-start | bytes 491528 | tf_op jit(solution)/shard_map/ppermute | solution.py:451
  45.0 18.9 %collective-permute-start.13 = (bf16[128,1280]{1,0:T(8,128)(2,1)S(1)}, bf16[128,1280]{1,0:T(8,128)(2,1)S(1)}, u32[]{:S(2)}, u32[]{:S(2)}) collective-permute-start(bf16[128,1280]{1,0:T(8,128)(2,1)S(1)} %collective-permute-done.6.refs_2_), channel_id=1, source_target_pairs={{0,1},{1,0},{2,3},{3,2},{4,5},{5,4},{6,7},{7,6},{8,9},{9,8},{10,11... | collective-permute-start | bytes 983048 | tf_op jit(solution)/shard_map/ppermute | solution.py:21
  45.1 19.0 %collective-permute-start.14 = (bf16[128,1280]{1,0:T(8,128)(2,1)S(1)}, bf16[128,1280]{1,0:T(8,128)(2,1)S(1)}, u32[]{:S(2)}, u32[]{:S(2)}) collective-permute-start(bf16[128,1280]{1,0:T(8,128)(2,1)S(1)} %collective-permute-done.4.refs_0_), channel_id=1, source_target_pairs={{0,1},{1,0},{2,3},{3,2},{4,5},{5,4},{6,7},{7,6},{8,9},{9,8},{10,11... | collective-permute-start | bytes 983048 | tf_op jit(solution)/shard_map/ppermute | solution.py:21
  45.6 20.6 %collective-permute-start.15 = (bf16[128,1280]{1,0:T(8,128)(2,1)S(1)}, bf16[128,1280]{1,0:T(8,128)(2,1)S(1)}, u32[]{:S(2)}, u32[]{:S(2)}) collective-permute-start(bf16[128,1280]{1,0:T(8,128)(2,1)S(1)} %collective-permute-done.10.refs_2_), channel_id=1, source_target_pairs={{0,1},{1,0},{2,3},{3,2},{4,5},{5,4},{6,7},{7,6},{8,9},{9,8},{10,11... | collective-permute-start | bytes 983048 | tf_op jit(solution)/shard_map/ppermute | solution.py:21
  46.2 6.2 %collective-permute-start.22 = (bf16[160,1024]{1,0:T(8,128)(2,1)}, bf16[160,1024]{1,0:T(8,128)(2,1)S(1)}, u32[]{:S(2)}, u32[]{:S(2)}) collective-permute-start(bf16[160,1024]{1,0:T(8,128)(2,1)} %collective-permute-done.21), channel_id=1, source_target_pairs={{0,16},{2,18},{4,20},{6,22},{8,24},{10,26},{12,28},{14,30},{17,1},... | collective-permute-start | bytes 983048 | tf_op jit(solution)/shard_map/ppermute | solution.py:451
  47.5 10.2 %collective-permute-start.24 = (bf16[160,1024]{1,0:T(8,128)(2,1)S(1)}, bf16[160,1024]{1,0:T(8,128)(2,1)S(1)}, u32[]{:S(2)}, u32[]{:S(2)}) collective-permute-start(bf16[160,1024]{1,0:T(8,128)(2,1)S(1)} %collective-permute-done.9), channel_id=1, source_target_pairs={{0,16},{2,18},{4,20},{6,22},{8,24},{10,26},{12,28},{14,30},{17,1},... | collective-permute-start | bytes 983048 | tf_op jit(solution)/shard_map/ppermute | solution.py:451
  52.4 8.9 %collective-permute-start.26 = (bf16[160,1024]{1,0:T(8,128)(2,1)S(1)}, bf16[160,1024]{1,0:T(8,128)(2,1)S(1)}, u32[]{:S(2)}, u32[]{:S(2)}) collective-permute-start(bf16[160,1024]{1,0:T(8,128)(2,1)S(1)} %collective-permute-done.8), channel_id=1, source_target_pairs={{0,16},{2,18},{4,20},{6,22},{8,24},{10,26},{12,28},{14,30},{17,1},... | collective-permute-start | bytes 983048 | tf_op jit(solution)/shard_map/ppermute | solution.py:451
  57.7 10.2 %collective-permute-start.16 = (bf16[128,1280]{1,0:T(8,128)(2,1)S(1)}, bf16[128,1280]{1,0:T(8,128)(2,1)S(1)}, u32[]{:S(2)}, u32[]{:S(2)}) collective-permute-start(bf16[128,1280]{1,0:T(8,128)(2,1)S(1)} %broadcast_select_fusion.3.refs_0_), channel_id=1, source_target_pairs={{0,1},{2,3},{4,5},{6,7},{9,8},{11,10},{13,12},{15,14},{16,17},{18,... | collective-permute-start | bytes 983048 | tf_op jit(solution)/shard_map/ppermute | solution.py:21
  59.6 5.0 %copy-start.1 = (bf16[128,1280]{1,0:T(8,128)(2,1)S(1)}, bf16[128,1280]{1,0:T(8,128)(2,1)}, u32[]{:S(2)}) copy-start(bf16[128,1280]{1,0:T(8,128)(2,1)} %refs_0_.3) | copy-start | bytes 983044
  61.2 7.2 %collective-permute-start.17 = (bf16[128,1280]{1,0:T(8,128)(2,1)S(1)}, bf16[128,1280]{1,0:T(8,128)(2,1)S(1)}, u32[]{:S(2)}, u32[]{:S(2)}) collective-permute-start(bf16[128,1280]{1,0:T(8,128)(2,1)S(1)} %collective-permute-done.12.refs_2_), channel_id=1, source_target_pairs={{0,1},{2,3},{4,5},{6,7},{9,8},{11,10},{13,12},{15,14},{16,17},{18,... | collective-permute-start | bytes 983048 | tf_op jit(solution)/shard_map/ppermute | solution.py:21
  63.9 6.2 %collective-permute-start.23 = (bf16[160,1024]{1,0:T(8,128)(2,1)S(1)}, bf16[160,1024]{1,0:T(8,128)(2,1)S(1)}, u32[]{:S(2)}, u32[]{:S(2)}) collective-permute-start(bf16[160,1024]{1,0:T(8,128)(2,1)S(1)} %broadcast_select_fusion.2), channel_id=1, source_target_pairs={{0,1},{1,0},{2,3},{3,2},{4,5},{5,4},{6,7},{7,6},{8,9},{9,8},{10,11... | collective-permute-start | bytes 983048 | tf_op jit(solution)/shard_map/ppermute | solution.py:21
  64.0 6.1 %collective-permute-start.25 = (bf16[160,1024]{1,0:T(8,128)(2,1)S(1)}, bf16[160,1024]{1,0:T(8,128)(2,1)S(1)}, u32[]{:S(2)}, u32[]{:S(2)}) collective-permute-start(bf16[160,1024]{1,0:T(8,128)(2,1)S(1)} %broadcast_select_fusion.1), channel_id=1, source_target_pairs={{0,1},{1,0},{2,3},{3,2},{4,5},{5,4},{6,7},{7,6},{8,9},{9,8},{10,11... | collective-permute-start | bytes 983048 | tf_op jit(solution)/shard_map/ppermute | solution.py:21
  66.2 4.0 %collective-permute-start.18 = (bf16[80,1024]{1,0:T(8,128)(2,1)S(1)}, bf16[80,1024]{1,0:T(8,128)(2,1)S(1)}, u32[]{:S(2)}, u32[]{:S(2)}) collective-permute-start(bf16[80,1024]{1,0:T(8,128)(2,1)S(1)} %dynamic-slice_bitcast_fusion.refs_6_.refs_0_.refs_1_), channel_id=1, source_target_pairs={{0,1},{1,0},{2,3},{3,2},{4,5},{5,4},{6,7},{7,6},{8,9},{9,8},{10,11... | collective-permute-start | bytes 491528 | tf_op jit(solution)/shard_map/ppermute | solution.py:21
  67.9 2.4 %collective-permute-start.20 = (bf16[80,1024]{1,0:T(8,128)(2,1)S(1)}, bf16[80,1024]{1,0:T(8,128)(2,1)S(1)}, u32[]{:S(2)}, u32[]{:S(2)}) collective-permute-start(bf16[80,1024]{1,0:T(8,128)(2,1)S(1)} %broadcast_select_fusion.4.refs_8_.refs_2_), channel_id=1, source_target_pairs={{0,1},{1,0},{2,3},{3,2},{4,5},{5,4},{6,7},{7,6},{8,9},{9,8},{10,11... | collective-permute-start | bytes 491528 | tf_op jit(solution)/shard_map/ppermute | solution.py:21
  68.4 1.7 %collective-permute-start.27 = (bf16[160,1024]{1,0:T(8,128)(2,1)S(1)}, bf16[160,1024]{1,0:T(8,128)(2,1)S(1)}, u32[]{:S(2)}, u32[]{:S(2)}) collective-permute-start(bf16[160,1024]{1,0:T(8,128)(2,1)S(1)} %broadcast_select_fusion), channel_id=1, source_target_pairs={{0,1},{1,0},{2,3},{3,2},{4,5},{5,4},{6,7},{7,6},{8,9},{9,8},{10,11... | collective-permute-start | bytes 983048 | tf_op jit(solution)/shard_map/ppermute | solution.py:21
  84.1 14.7 %collective-permute-start.28 = (bf16[256,320]{1,0:T(8,128)(2,1)S(1)}, bf16[256,320]{1,0:T(8,128)(2,1)S(1)}, u32[]{:S(2)}, u32[]{:S(2)}) collective-permute-start(bf16[256,320]{1,0:T(8,128)(2,1)S(1)} %get-tuple-element.59), channel_id=1, source_target_pairs={{0,0},{1,4},{2,2},{3,6},{4,1},{5,5},{6,3},{7,7},{8,8},{9,12},{10,1... | collective-permute-start | bytes 491528 | tf_op jit(solution)/shard_map/ppermute | solution.py:21
  84.8 14.1 %collective-permute-start.29 = (bf16[256,320]{1,0:T(8,128)(2,1)S(1)}, bf16[256,320]{1,0:T(8,128)(2,1)S(1)}, u32[]{:S(2)}, u32[]{:S(2)}) collective-permute-start(bf16[256,320]{1,0:T(8,128)(2,1)S(1)} %get-tuple-element.60), channel_id=1, source_target_pairs={{0,2},{1,6},{2,0},{3,4},{4,3},{5,7},{6,1},{7,5},{8,10},{9,14},{10,... | collective-permute-start | bytes 491528 | tf_op jit(solution)/shard_map/ppermute | solution.py:21
  86.6 5.4 %collective-permute-start.32 = (f32[40,128]{1,0:T(8,128)S(1)}, f32[40,128]{1,0:T(8,128)S(1)}, u32[]{:S(2)}, u32[]{:S(2)}) collective-permute-start(f32[40,128]{1,0:T(8,128)S(1)} %get-tuple-element.63), channel_id=1, source_target_pairs={{0,8},{1,9},{2,10},{3,11},{4,12},{5,13},{6,14},{7,15},{8,0},{9,1},... | collective-permute-start | bytes 61448 | tf_op jit(solution)/shard_map/ppermute | solution.py:21
  86.8 5.2 %collective-permute-start.33 = (f32[40,128]{1,0:T(8,128)S(1)}, f32[40,128]{1,0:T(8,128)S(1)}, u32[]{:S(2)}, u32[]{:S(2)}) collective-permute-start(f32[40,128]{1,0:T(8,128)S(1)} %get-tuple-element.64), channel_id=1, source_target_pairs={{0,1},{1,0},{2,3},{3,2},{4,5},{5,4},{6,7},{7,6},{8,9},{9,8},{10,11... | collective-permute-start | bytes 61448 | tf_op jit(solution)/shard_map/ppermute | solution.py:21
  90.6 4.4 %collective-permute-start.34 = (f32[40,128]{1,0:T(8,128)S(1)}, f32[40,128]{1,0:T(8,128)S(1)}, u32[]{:S(2)}, u32[]{:S(2)}) collective-permute-start(f32[40,128]{1,0:T(8,128)S(1)} %get-tuple-element.65), channel_id=1, source_target_pairs={{0,9},{1,8},{2,11},{3,10},{4,13},{5,12},{6,15},{7,14},{8,1},{9,0},... | collective-permute-start | bytes 61448 | tf_op jit(solution)/shard_map/ppermute | solution.py:21
  95.2 4.2 %collective-permute-start.35 = (bf16[2,384]{1,0:T(2,128)(2,1)S(1)}, bf16[2,384]{1,0:T(2,128)(2,1)S(1)}, u32[]{:S(2)}, u32[]{:S(2)}) collective-permute-start(bf16[2,384]{1,0:T(2,128)(2,1)S(1)} %get-tuple-element.67), channel_id=1, source_target_pairs={{0,2},{1,3},{2,0},{3,1},{4,6},{5,7},{6,4},{7,5},{8,10},{9,11},{10,... | collective-permute-start | bytes 4616 | tf_op jit(solution)/shard_map/ppermute | solution.py:21
  96.3 3.6 %collective-permute-start.36 = (bf16[2,384]{1,0:T(2,128)(2,1)S(1)}, bf16[2,384]{1,0:T(2,128)(2,1)S(1)}, u32[]{:S(2)}, u32[]{:S(2)}) collective-permute-start(bf16[2,384]{1,0:T(2,128)(2,1)S(1)} %get-tuple-element.68), channel_id=1, source_target_pairs={{0,4},{1,5},{2,6},{3,7},{4,0},{5,1},{6,2},{7,3},{8,12},{9,13},{10,... | collective-permute-start | bytes 4616 | tf_op jit(solution)/shard_map/ppermute | solution.py:21
  98.0 4.5 %collective-permute-start.37 = (bf16[2,384]{1,0:T(2,128)(2,1)S(1)}, bf16[2,384]{1,0:T(2,128)(2,1)S(1)}, u32[]{:S(2)}, u32[]{:S(2)}) collective-permute-start(bf16[2,384]{1,0:T(2,128)(2,1)S(1)} %get-tuple-element.69), channel_id=1, source_target_pairs={{0,6},{1,7},{2,4},{3,5},{4,2},{5,3},{6,0},{7,1},{8,14},{9,15},{10,... | collective-permute-start | bytes 4616 | tf_op jit(solution)/shard_map/ppermute | solution.py:21
  98.8 4.4 %collective-permute-start.30 = (bf16[128,320]{1,0:T(8,128)(2,1)S(1)}, bf16[128,320]{1,0:T(8,128)(2,1)S(1)}, u32[]{:S(2)}, u32[]{:S(2)}) collective-permute-start(bf16[128,320]{1,0:T(8,128)(2,1)S(1)} %constant_dynamic-slice_fusion.1), channel_id=1, source_target_pairs={{0,1},{1,0},{2,3},{3,2},{4,5},{5,4},{6,7},{7,6},{8,9},{9,8},{10,11... | collective-permute-start | bytes 245768 | tf_op jit(solution)/shard_map/ppermute | solution.py:21
  98.9 4.3 %collective-permute-start.31 = (bf16[128,320]{1,0:T(8,128)(2,1)S(1)}, bf16[128,320]{1,0:T(8,128)(2,1)S(1)}, u32[]{:S(2)}, u32[]{:S(2)}) collective-permute-start(bf16[128,320]{1,0:T(8,128)(2,1)S(1)} %constant_dynamic-slice_fusion), channel_id=1, source_target_pairs={{0,1},{1,0},{2,3},{3,2},{4,5},{5,4},{6,7},{7,6},{8,9},{9,8},{10,11... | collective-permute-start | bytes 245768 | tf_op jit(solution)/shard_map/ppermute | solution.py:21

commit v6 on v5

--- a/solution.py
+++ b/solution.py
@@ -23,6 +23,10 @@
 
 def swap(block, n, mask):
     return send(block, [(d, d ^ mask) for d in range(n)])
+
+
+def after(value, *awaited):
+    return lax.optimization_barrier((value, *awaited))[0]
 
 
 def scalars(values):
@@ -110,7 +114,6 @@
         in_specs=[SMEM] + [VMEM] * (1 + len(small)),
         out_specs=(VMEM, VMEM),
         scratch_shapes=[pltpu.VMEM((rows, HD), F32)],
-        compiler_params=pltpu.CompilerParams(vmem_limit_bytes=8 * 1024 * 1024),
     )(spot, weight, *small)
 
 
@@ -150,37 +153,85 @@
     )(table, gain, *blocks)
 
 
-def encoder_kernel(n_parts, depth, chips, places, *refs):
+def prepare_kernel(table, own, *refs):
+    parts, (ids, tokens, asked) = refs[:-3], refs[-3:]
+    straight, first, core = table[12], table[13], table[7]
+    count = asked.shape[0]
+    ids[...] = jnp.zeros_like(ids)
+    tokens[...] = jnp.zeros_like(tokens)
+    flip = jnp.broadcast_to(core, (2, HD)) == 1
+    near = jnp.broadcast_to(straight, (32, HD)) == 1
+    for i in range(count // 2):
+        if i == 0:
+            lanes = own[:32, 960:].astype(F32)
+        else:
+            part, rows = i // 2, slice(0, 32)
+            if i > 1 and i % 2:
+                rows = slice(own.shape[0], own.shape[0] + 32)
+            here, there = parts[2 * part][rows, 960:], parts[2 * part + 1][rows, 960:]
+            lanes = jnp.where(near, here.astype(F32), there.astype(F32))
+        for h in range(6):
+            found = jnp.where(flip, lanes[4 * h + 2 : 4 * h + 4], lanes[4 * h : 4 * h + 2])
+            if h < 5:
+                at = count * h + 2 * i
+                tokens[at : at + 2, HD * h : HD * h + HD] = found * 0.125
+            else:
+                asked[2 * i : 2 * i + 2, :] = found
+        for c in range(2):
+            marks = lanes[24 + 4 * c : 26 + 4 * c] * 128.0 + lanes[26 + 4 * c : 28 + 4 * c]
+            block = table[14 + 2 * i] // 2 * 2 + c - first
+
+            @pl.when((block >= 0) & (block < 12))
+            def _():
+                ids[0:1, pl.ds(pl.multiple_of(block * 128, 128), 128)] = jnp.concatenate(
+                    [marks[0:1], marks[1:2]], axis=1
+                )
+
+
+def prepare(table, own, parts, count):
+    return pl.pallas_call(
+        prepare_kernel,
+        out_shape=(
+            jax.ShapeDtypeStruct((8, 1536), F32),
+            jax.ShapeDtypeStruct((5 * count, GROUP), F32),
+            jax.ShapeDtypeStruct((count, HD), F32),
+        ),
+        in_specs=[SMEM] + [VMEM] * (1 + len(parts)),
+        out_specs=(VMEM,) * 3,
+        compiler_params=pltpu.CompilerParams(vmem_limit_bytes=8 * 1024 * 1024),
+    )(table, own, *parts)
+
+
+def encoder_kernel(n_parts, depth, places, *refs):
     layers = [refs[2 * i : 2 * i + 2] for i in range(3)]
-    parts = refs[6 : 6 + n_parts]
-    refs = refs[6 + n_parts :]
-    if not chips:
-        given, refs = refs[0], refs[1:]
-    memory, near, away, weight, ids, residual, queries, keys, values = refs
-    x, straight, first = places[11], places[12], places[13]
-
-    for i, part in enumerate(parts):
-        row = pl.multiple_of(places[14 + i] * depth, 16)
-        weight[pl.ds(row, depth), :] = part[...]
-    if chips:
-        ids[...] = jnp.zeros_like(ids)
-        for i in range(n_parts // 2):
-            here, there = parts[2 * i][:32, 960:], parts[2 * i + 1][:32, 960:]
-            lanes = jnp.where(jnp.broadcast_to(straight, (32, HD)) == 1, here.astype(F32), there.astype(F32))
-            found = lanes[24:]
-            for core in range(2):
-                high = found[4 * core : 4 * core + 2]
-                marks = high * 128.0 + found[4 * core + 2 : 4 * core + 4]
-                block = places[14 + 2 * i] // 2 * 2 + core - first
-
-                @pl.when((block >= 0) & (block < 12))
-                def _():
-                    ids[0:1, pl.ds(pl.multiple_of(block * 128, 128), 128)] = jnp.concatenate(
-                        [marks[0:1], marks[1:2]], axis=1
-                    )
-
-    else:
-        ids[...] = given[...]
+    ids = refs[6]
+    parts = refs[7 : 7 + n_parts]
+    memory, near, away, weight, residual, queries, keys, values = refs[7 + n_parts :]
+    x, straight = places[11], places[12]
+
+    def place_part(source, rows):
+        weight[pl.ds(pl.multiple_of(source * depth, 16), depth), :] = rows
+
+    for i in range(min(2, n_parts)):
+        place_part(places[14 + i], parts[i][...])
+    for turn in range((n_parts - 2) // 4):
+        came, traded, came_other, traded_other = parts[2 + 4 * turn : 6 + 4 * turn]
+        pieces = came.shape[0] // depth
+
+        def place_turn(mine, other):
+            for s in range(pieces):
+                rows = slice(s * depth, s * depth + depth)
+                at = 14 + 4 * turn + 2 * (s + 2 - pieces)
+                place_part(places[at], mine[rows, :])
+                place_part(places[at + 1], other[rows, :])
+
+        @pl.when(straight == 1)
+        def _():
+            place_turn(came, traded_other)
+
+        @pl.when(straight == 0)
+        def _():
+            place_turn(traded, came_other)
 
     for slab in range(3):
         values[:, 256 * slab + 128 : 256 * slab + 256] = jnp.ones((1536, 128), BF)
@@ -277,10 +328,10 @@
     away[...] = memory[pl.ds(pl.multiple_of(256 * (1 - x), 256), 256), :]
 
 
-def encoder(places, layers, parts, depth, extra):
-    operands = [a for layer in layers for a in layer] + parts + extra
+def encoder(places, layers, ids, parts, depth):
+    operands = [a for layer in layers for a in layer] + [ids] + parts
     return pl.pallas_call(
-        functools.partial(encoder_kernel, len(parts), depth, not extra),
+        functools.partial(encoder_kernel, len(parts), depth),
         out_shape=(
             jax.ShapeDtypeStruct((512, GROUP), BF),
             jax.ShapeDtypeStruct((256, GROUP), BF),
@@ -290,7 +341,6 @@
         out_specs=(VMEM, VMEM, VMEM),
         scratch_shapes=[
             pltpu.VMEM((1280, 1024), BF),
-            pltpu.VMEM((8, 1536), F32),
             pltpu.VMEM((512, GROUP), BF),
             pltpu.VMEM((512, 384), BF),
             pltpu.VMEM((1536, 384), BF),
@@ -300,54 +350,40 @@
     )(places, *operands)
 
 
-def cross_kernel(chips, base, table, memory, *refs):
-    tokens, asked, out = refs[-3:]
+def cross_kernel(base, table, tokens, asked, memory, beside, *refs):
+    outs, out = refs[:-1], refs[-1]
     count = asked.shape[0]
-    parts, outs = refs[: -3 - count // 8], refs[-3 - count // 8 : -3]
-    first, me, core, straight = [table[base + i] for i in range(4)]
-    half = count // 2
-    tokens[...] = jnp.zeros_like(tokens)
-    if chips:
-        flip = jnp.broadcast_to(core, (2, HD)) == 1
-        for i in range(len(parts) // 2):
-            here, there = parts[2 * i][:24, 960:], parts[2 * i + 1][:24, 960:]
-            rows = jnp.where(
-                jnp.broadcast_to(straight, (24, HD)) == 1, here.astype(F32), there.astype(F32)
-            )
-            for h in range(6):
-                low, high = rows[4 * h : 4 * h + 2], rows[4 * h + 2 : 4 * h + 4]
-                for turn in range(2):
-                    at = half * turn + 2 * i
-                    found = jnp.where(flip, low, high) if turn else jnp.where(flip, high, low)
-                    if h < 5:
-                        tokens[count * h + at : count * h + at + 2, HD * h : HD * h + HD] = found * 0.125
-                    else:
-                        asked[at : at + 2, :] = found
-    else:
-        for h in range(5):
-            tokens[count * h : count * h + count, HD * h : HD * h + HD] = parts[0][h].astype(F32) * 0.125
-        asked[...] = parts[0][5].astype(F32)
+    me = table[base + 2]
     spot = lax.broadcasted_iota(jnp.int32, (count, HD), 1)
     order = lax.broadcasted_iota(jnp.int32, (count, 1), 0)
-    owner = (2 * (lax.rem(order, half) // 2) + order // half) ^ me
+    owner = (order // 2 * 2) ^ me
     bias = []
-    for b in range(4):
-        ask = jnp.sum(jnp.where(spot == first + b, asked[...], 0.0), axis=-1, keepdims=True)
-        allowed = (ask > 0.5) | (owner == first + b)
-        bias.append(jnp.broadcast_to(jnp.where(allowed, 0.0, LOW), (count, 128)))
+    for half in range(2):
+        for b in range(4):
+            block = table[base + half] + b
+            ask = jnp.sum(jnp.where(spot == block, asked[...], 0.0), axis=-1, keepdims=True)
+            allowed = (ask > 0.5) | (owner == block)
+            bias.append(jnp.broadcast_to(jnp.where(allowed, 0.0, LOW), (count, 128)))
     bias = jnp.concatenate(bias, axis=1)
     bias = jnp.concatenate([bias] * 5, axis=0)
-    cross = lax.dot_general(
-        tokens[:, :GROUP].astype(BF),
-        memory[...],
-        (((1,), (1,)), ((), ())),
-        preferred_element_type=F32,
+    query = tokens[...].astype(BF)
+    cross = jnp.concatenate(
+        [
+            lax.dot_general(
+                query, held[...], (((1,), (1,)), ((), ())), preferred_element_type=F32
+            )
+            for held in (memory, beside)
+        ],
+        axis=1,
     )
     cross = jnp.where(bias < 0.0, LOW, cross)
     top = jnp.max(cross, axis=-1, keepdims=True)
     raised = jnp.where(bias < 0.0, 0.0, jnp.exp(cross - top))
     den = jnp.sum(raised, axis=-1, keepdims=True)
-    out[...] = jnp.dot(raised.astype(BF), memory[...], preferred_element_type=F32)
+    raised = raised.astype(BF)
+    out[...] = jnp.dot(raised[:, :512], memory[...], preferred_element_type=F32) + jnp.dot(
+        raised[:, 512:], beside[...], preferred_element_type=F32
+    )
     lane = lax.broadcasted_iota(jnp.int32, (count, HD), 1)
     for h in range(5):
         rows = slice(count * h, count * h + count)
@@ -357,19 +393,16 @@
             owned[8 * h : 8 * h + 8, :] = both[8 * i : 8 * i + 8]
 
 
-def cross_partial(base, table, memory, parts, count, chips):
+def cross_partial(base, table, tokens, asked, memory, beside):
+    count = asked.shape[0]
     return pl.pallas_call(
-        functools.partial(cross_kernel, chips, base),
+        functools.partial(cross_kernel, base),
         out_shape=(jax.ShapeDtypeStruct((40, 128), F32),) * (count // 8),
-        in_specs=[SMEM] + [VMEM] * (1 + len(parts)),
+        in_specs=[SMEM] + [VMEM] * 4,
         out_specs=(VMEM,) * (count // 8),
-        scratch_shapes=[
-            pltpu.VMEM((5 * count, 384), F32),
-            pltpu.VMEM((count, HD), F32),
-            pltpu.VMEM((5 * count, GROUP), F32),
-        ],
+        scratch_shapes=[pltpu.VMEM((5 * count, GROUP), F32)],
         compiler_params=pltpu.CompilerParams(vmem_limit_bytes=12 * 1024 * 1024),
-    )(table, memory, *parts)
+    )(table, tokens, asked, memory, beside)
 
 
 def merge_kernel(*refs):
@@ -440,9 +473,8 @@
     table += [group, p != k, x, c]
     table += [512 * (p - c + 1), 512 * (2 - p - c), 1024 * c, x, straight, 4 * quarter - 4]
     sources = [me ^ m for m in range(n)] if direct else [jnp.int32(0)]
-    table = scalars(table + sources + [4 * quarter, me, c, straight])
+    table = scalars(table + sources + [4 * quarter, 4 * (quarter ^ 1), me])
     base = 14 + len(sources)
-    extra = []
     if direct:
         carriers = [(u, d) for u in range(utts) for d in range(n) if d % 2 == u % 2]
 
@@ -450,57 +482,63 @@
             route = [(u * n + d, (u ^ turn_u) * n + (d ^ turn_d)) for u, d in carriers]
             return lax.ppermute(block, ("utt", "tm"), route)
 
-        far = send(stem, [(d, d ^ 8) for d in range(n) if d // 4 in (1, 2)])
+        inside = [d for d in range(n) if d // 4 in (1, 2)]
+        far = send(after(stem, pair, near), [(d, d ^ 8) for d in inside])
         small = [dec_queries, stretch_mask, segment_ids.reshape(1, -1)]
         both = [part for piece in small for part in (piece, swap(piece, n, 1))]
         mine, theirs = pack(table, qkv_weight, *both)
-        across = carry(theirs, 0, 2)
+        across = carry(after(theirs, stem_x), 0, 2)
         stem_c = swap(stem, n, 1)
-        mine_late, across_late, pair, near, stem_x, stem_c = lax.optimization_barrier(
-            (mine, across, pair, near, stem_x, stem_c)
-        )
-        halo = jnp.where((z == 1) | (z == 2), near, far)
-        pair_x = swap(pair, n, 2)
-        halo_x = swap(halo, n, 2)
+        own_layer = norm_layer(table, gain, [stem, stem_c, stem_x, swap(stem_x, n, 1)])
         ready = [
             jnp.concatenate(
                 [
-                    lax.dynamic_slice_in_dim(mine_late, p ^ a, 1, 0),
-                    lax.dynamic_slice_in_dim(across_late, p ^ a, 1, 0),
+                    lax.dynamic_slice_in_dim(mine, p ^ a, 1, 0),
+                    lax.dynamic_slice_in_dim(across, p ^ a, 1, 0),
                 ]
             ).reshape(2 * depth, 1024)
             for a in range(2)
         ]
+        own_part = lax.dynamic_index_in_dim(mine, p, 0, keepdims=False)
+        pair_x = swap(after(pair, across), n, 2)
         here = {0: lax.dynamic_index_in_dim(across, p, 0, keepdims=False)}
-        for turn in (1, 2, 3):
-            here[turn] = carry(ready[turn % 2], 0, 4 * turn)
-        here[3], here[2], here[0], pair, pair_x, halo, halo_x, stem_x, mine = lax.optimization_barrier(
-            (here[3], here[2], here[0], pair, pair_x, halo, halo_x, stem_x, mine)
-        )
-        own_part = lax.dynamic_index_in_dim(mine, p, 0, keepdims=False)
+        here[3] = carry(after(ready[1], far), 0, 12)
+        here[2] = carry(after(ready[0], here[3], own_layer[0]), 0, 8)
+        halo = jnp.where((z == 1) | (z == 2), near, far)
+        halo_x = swap(after(halo, pair_x), n, 2)
+        pair_layer = norm_layer(table, gain, [pair, swap(pair, n, 1), pair_x, swap(pair_x, n, 1)])
+        here[1] = carry(after(ready[1], here[2], pair_layer[0]), 0, 4)
+        aside = [(d, d ^ 1) for d in range(n) if d % 2 == d // 8]
+        halo_layer = norm_layer(table, gain, [halo, send(halo, aside), halo_x, send(halo_x, aside)])
+        traded, came_other, traded_other = {}, {}, {}
+        hold = []
+        for turn in (0, 3, 2, 1):
+            traded[turn] = carry(after(here[turn], *hold), 1, 0)
+            hold = [traded[turn]]
+            came_other[turn] = carry(here[turn], 0, 1)
+            route = [(u * n + (d ^ 1), u * n + d) for u, d in carriers]
+            traded_other[turn] = lax.ppermute(traded[turn], ("utt", "tm"), route)
         weights = [own_part, swap(own_part, n, 1)]
         for turn in range(4):
-            traded = carry(here[turn], 1, 0)
-            got = jnp.where(straight == 1, here[turn], traded)
-            beside = swap(got, n, 1)
-            for s in range(got.shape[0] // depth):
-                for part in (got, beside):
-                    weights.append(part[s * depth : s * depth + depth])
-        token_parts = [own_part, own_part] + weights[2:]
-        aside = [(d, d ^ 1) for d in range(n) if d % 2 == d // 8]
-        halo_layer = [halo, send(halo, aside), halo_x, send(halo_x, aside)]
+            weights += [here[turn], traded[turn], came_other[turn], traded_other[turn]]
+        came = [part for turn in range(4) for part in (here[turn], came_other[turn])]
+        ids, tokens, asked = prepare(table, own_part, came, n)
+        layered = [own_layer, pair_layer, halo_layer]
     else:
-        stem_c = swap(stem, n, 1)
         far = swap(near, n, 4)
         left = jnp.where(p == 0, near, far)
         right = jnp.where(p == 0, far, near)
         left_x, right_x = swap(left, n, 2), swap(right, n, 2)
-        halo_layer = [
+        halo = [
             jnp.where(c == 0, left, right),
             swap(jnp.where(c == 0, right, left), n, 1),
             jnp.where(c == 0, left_x, right_x),
             swap(jnp.where(c == 0, right_x, left_x), n, 1),
         ]
+        pair_x = swap(pair, n, 2)
+        own = [stem, swap(stem, n, 1), stem_x, swap(stem_x, n, 1)]
+        other = [pair, swap(pair, n, 1), pair_x, swap(pair_x, n, 1)]
+        layered = [norm_layer(table, gain, blocks) for blocks in (own, other, halo)]
         whole = lax.all_gather(qkv_weight, "tm", axis=0, tiled=True)
         grouped = jnp.stack([weight_group(whole, g) for g in range(4)])
         weights = [lax.dynamic_index_in_dim(grouped, group, 0, keepdims=False)]
@@ -509,18 +547,21 @@
         packed = jnp.stack([token_group(dec_queries, stretch_mask, g) for g in range(4)])
         every = lax.all_gather(packed, "tm", axis=0)
         every = lax.dynamic_index_in_dim(every, group, 1, keepdims=False)
-        order = jnp.array([m for core in range(2) for m in range(core, n, 2)], jnp.int32)
-        every = jnp.take(every, order ^ me, axis=0).reshape(n, 6, 2, HD)
-        token_parts = [every.transpose(1, 0, 2, 3).reshape(6, 2 * n, HD)]
+        every = jnp.take(every, jnp.arange(0, n, 2, dtype=jnp.int32) ^ me, axis=0)
+        every = every.reshape(n // 2, 6, 2, HD).transpose(1, 0, 2, 3).reshape(6, n, HD).astype(F32)
+        asked = every[5]
+        tokens = jnp.concatenate(
+            [jnp.pad(every[h] * 0.125, ((0, 0), (HD * h, GROUP - HD - HD * h))) for h in range(5)]
+        )
         marks = lax.all_gather(segment_ids, "tm", axis=0, tiled=True).astype(F32)
         marks = jnp.pad(marks, (512, 512))
         marks = lax.dynamic_slice_in_dim(marks, 512 * quarter, 1536, 0)
-        extra = [jnp.broadcast_to(marks[None], (8, 1536))]
-        pair_x = swap(pair, n, 2)
-    own_layer = [stem, stem_c, stem_x, swap(stem_x, n, 1)]
-    pair_layer = [pair, swap(pair, n, 1), pair_x, swap(pair_x, n, 1)]
-    layered = [norm_layer(table, gain, blocks) for blocks in (own_layer, pair_layer, halo_layer)]
-    held, stay, leave = encoder(table, layered, weights, depth, extra)
+        ids = jnp.broadcast_to(marks[None], (8, 1536))
+    held, stay, leave = encoder(table, layered, ids, weights, depth)
+
+    partial = cross_partial(base, table, tokens, asked, held, swap(held, n, 1))
+    owned = [partial[0]] + [swap(partial[i], n, 8 * i) for i in range(1, n // 8)]
+    stay, leave = after(stay, partial[0]), after(leave, partial[0])
 
     pieces = []
     for turn, rows in enumerate((stay, leave)):
@@ -537,12 +578,6 @@
         pieces.append((keep, give))
     memory = gather_groups([pieces[0][0], pieces[1][0], pieces[0][1], pieces[1][1]], 2 * c + x)
 
-    partial = cross_partial(base, table, held, token_parts, 2 * n, direct)
-    owned = [partial[0]]
-    outer = n // 8
-    for i in range(1, 2 * outer):
-        core, turn = i // outer, i % outer
-        owned.append(swap(partial[i], n, 8 * turn + core))
     final = merge(owned)
     final = [final[0]] + [swap(final[i], n, 2 * i) for i in (1, 2, 3)]
     cross_out = gather_groups(final, group)

time: 105 us -> 119 us (1.13)
  waiting for transfers between devices: 22.6 us -> 29.6 us
  starting transfers between devices: 52.3 us -> 56 us
  Pallas kernels: 21 us -> 24.7 us
    ppermute x30 -> x25, waiting for transfers between devices: 7.58 us -> 15.4 us  [send(): return lax.ppermute(block, 'tm', route)]
    ppermute x0 -> x4, starting transfers between devices: none -> 5.16 us  [on_device(): traded_other[turn] = lax.ppermute(traded[turn], ('utt', 'tm'), route)]
    ppermute x8 -> x12, starting transfers between devices: 25.7 us -> 23.6 us  [carry(): return lax.ppermute(block, ('utt', 'tm'), route)]
    pallas_call x2 -> x3, Pallas kernels: 15.1 us -> 16.7 us  [the longest x1 14 us: encoder(): pl.pallas_call(functools.partial(encoder_kernel, len(parts), depth), out_...]
    pallas_call x1, Pallas kernels: 1.02 us -> 2.38 us  [pack(): pl.pallas_call(pack_kernel, out_shape=(shape, shape), in_specs=[SMEM] + [...]
    ppermute x8 -> x12, waiting for transfers between devices: 15 us -> 14.2 us  [carry(): return lax.ppermute(block, ('utt', 'tm'), route)]
    ppermute x30 -> x25, starting transfers between devices: 26.6 us -> 27.2 us  [send(): return lax.ppermute(block, 'tm', route)]
    unnamed x12 -> x28, local copies, waits for them, and re-layouts: 3.11 us -> 2.79 us
  transfers between devices with their start and end apart: 38 -> 41, of which waited for: 10 -> 10; matrix products, arithmetic and copies ran while one was open for 3% -> 3% of each run, Pallas kernels for 7% -> 8%
where the time goes in v6:
time: 119 us
  starting transfers between devices  56 us (47%)
  waiting for transfers between devices  29.6 us (25%)
  Pallas kernels  24.7 us (21%)
  local copies, waits for them, and re-layouts  6.1 us (5%)
  between operations  1.32 us (1%)
    ppermute x25, starting transfers between devices, send(): return lax.ppermute(block, 'tm', route)  27.2 us
    ppermute x12, starting transfers between devices, carry(): return lax.ppermute(block, ('utt', 'tm'), route)  23.6 us
    ppermute x25, waiting for transfers between devices, send(): return lax.ppermute(block, 'tm', route)  15.4 us
    ppermute x12, waiting for transfers between devices, carry(): return lax.ppermute(block, ('utt', 'tm'), route)  14.2 us
    pallas_call x1, Pallas kernels, encoder(): pl.pallas_call(functools.partial(encoder_kernel, len(parts), depth), out_...  14 us
    pallas_call x3, Pallas kernels, norm_layer(): pl.pallas_call(functools.partial(norm_kernel, len(blocks) // 4), out_shap...  5.34 us
    ppermute x4, starting transfers between devices, on_device(): traded_other[turn] = lax.ppermute(traded[turn], ('utt', 'tm'), route)  5.16 us
    unnamed x28, local copies, waits for them, and re-layouts  2.79 us
  transfers between devices with their start and end apart: 41, of which 10 were waited for; matrix products, arithmetic and copies ran while one was open for 3% of the time, Pallas kernels for 8%

profile of v6, /device:TPU:0, one launch (start us, length us, event | category | flops | bytes accessed | tf_op | source)
XLA Modules:
  0.0 118.7 jit_solution(8106206062024925613)
XLA Ops:
  0.6 3.0 %collective-permute-start.1 = (bf16[128,1280]{1,0:T(8,128)(2,1)}, bf16[128,1280]{1,0:T(8,128)(2,1)S(1)}, u32[]{:S(2)}, u32[]{:S(2)}) collective-permute-start(bf16[128,1280]{1,0:T(8,128)(2,1)} %refs_0_.2), channel_id=1, source_target_pairs={{0,2},{1,3},{2,0},{3,1},{4,6},{5,7},{6,4},{7,5},{8,10},{9,11},{10,... | collective-permute-start | bytes 983048 | tf_op jit(solution)/shard_map/ppermute | solution.py:21
  3.6 1.6 %collective-permute-start.3 = (bf16[128,1280]{1,0:T(8,128)(2,1)}, bf16[128,1280]{1,0:T(8,128)(2,1)S(1)}, u32[]{:S(2)}, u32[]{:S(2)}) collective-permute-start(bf16[128,1280]{1,0:T(8,128)(2,1)} %refs_0_.2), channel_id=1, source_target_pairs={{0,4},{1,5},{2,6},{3,7},{4,0},{5,1},{6,2},{7,3},{8,12},{9,13},{10,... | collective-permute-start | bytes 983048 | tf_op jit(solution)/shard_map/ppermute | solution.py:21
  5.2 0.7 collective-permute-start.11
  6.0 0.5 collective-permute-start.6
  6.5 1.0 collective-permute-done.6.refs_3_
  7.5 0.3 collective-permute-start.7
  7.8 0.6 stack.137.table.spot.places
  8.5 0.3 collective-permute-done.7.refs_5_
  8.8 0.5 copy-done.13
  9.3 0.6 copy-done.11
  9.8 2.4 %shard_map.78 = (bf16[2,80,1024]{2,1,0:T(8,128)(2,1)}, bf16[2,80,1024]{2,1,0:T(8,128)(2,1)}) custom-call(s32[33]{0:T(128)} %stack.137.table.spot.places, bf16[80,3840]{1,0:T(8,128)(2,1)} %weight.1, bf16[2,1280]{1,0:T(2,128)(2,1)} %refs_0_.3, bf16[2,1280]{1,0:T(2,128)(2,1)} %copy-done.11, s32[2,16]{1,0:T(2,128)} %refs_2_.1, s32[2,16]{1,0:T(2,128)} %copy-done.12, ...), custom_call_target="tpu_custom_call" | custom-call | tf_op jit(solution)/shard_map/pallas_call | solution.py:111
  12.2 3.0 %collective-permute-start.8 = (bf16[2,80,1024]{2,1,0:T(8,128)(2,1)}, bf16[2,80,1024]{2,1,0:T(8,128)(2,1)S(1)}, u32[]{:S(2)}, u32[]{:S(2)}) collective-permute-start(bf16[2,80,1024]{2,1,0:T(8,128)(2,1)} %get-tuple-element.37), channel_id=1, source_target_pairs={{0,2},{2,0},{4,6},{6,4},{8,10},{10,8},{12,14},{14,12},{17,19},{19,... | collective-permute-start | bytes 983048 | tf_op jit(solution)/shard_map/ppermute | solution.py:483
  15.2 0.1 collective-permute-start
  15.3 1.3 %collective-permute-start.12 = (bf16[128,1280]{1,0:T(8,128)(2,1)}, bf16[128,1280]{1,0:T(8,128)(2,1)S(1)}, u32[]{:S(2)}, u32[]{:S(2)}) collective-permute-start(bf16[128,1280]{1,0:T(8,128)(2,1)} %refs_0_.2), channel_id=1, source_target_pairs={{4,12},{5,13},{6,14},{7,15},{8,0},{9,1},{10,2},{11,3},{20,28},{21,... | collective-permute-start | bytes 983048 | tf_op jit(solution)/shard_map/ppermute | solution.py:21
  16.6 1.0 constant_dynamic-slice_fusion.3
  17.7 0.5 collective-permute-start.2
  18.2 3.2 %collective-permute-done.8 = bf16[2,80,1024]{2,1,0:T(8,128)(2,1)S(1)} collective-permute-done((bf16[2,80,1024]{2,1,0:T(8,128)(2,1)}, bf16[2,80,1024]{2,1,0:T(8,128)(2,1)S(1)}, u32[]{:S(2)}, u32[]{:S(2)}) %collective-permute-start.8) | collective-permute-done | bytes 327712 | tf_op jit(solution)/shard_map/ppermute | solution.py:483
  21.5 7.0 %collective-permute-done.12 = bf16[128,1280]{1,0:T(8,128)(2,1)S(1)} collective-permute-done((bf16[128,1280]{1,0:T(8,128)(2,1)}, bf16[128,1280]{1,0:T(8,128)(2,1)S(1)}, u32[]{:S(2)}, u32[]{:S(2)}) %collective-permute-start.12) | collective-permute-done | bytes 327712 | tf_op jit(solution)/shard_map/ppermute | solution.py:21
  28.5 5.5 %collective-permute-start.17 = (bf16[160,1024]{1,0:T(8,128)(2,1)S(1)}, bf16[160,1024]{1,0:T(8,128)(2,1)S(1)}, u32[]{:S(2)}, u32[]{:S(2)}) collective-permute-start(bf16[160,1024]{1,0:T(8,128)(2,1)S(1)} %bitcast.43), channel_id=1, source_target_pairs={{0,12},{2,14},{4,8},{6,10},{8,4},{10,6},{12,0},{14,2},{17,29},{19,... | collective-permute-start | bytes 983048 | tf_op jit(solution)/shard_map/ppermute | solution.py:483
  33.9 0.9 collective-permute-start.9
  34.8 1.3 %collective-permute-start.24 = (bf16[80,1024]{1,0:T(8,128)(2,1)S(1)}, bf16[80,1024]{1,0:T(8,128)(2,1)S(1)}, u32[]{:S(2)}, u32[]{:S(2)}) collective-permute-start(bf16[80,1024]{1,0:T(8,128)(2,1)S(1)} %bitcast.39), channel_id=1, source_target_pairs={{0,16},{2,18},{4,20},{6,22},{8,24},{10,26},{12,28},{14,30},{17,1},... | collective-permute-start | bytes 491528 | tf_op jit(solution)/shard_map/ppermute | solution.py:483
  36.2 0.7 copy-done.1
  36.9 1.0 copy-done.2
  37.9 1.6 %shard_map.77 = (bf16[512,1280]{1,0:T(8,128)(2,1)S(1)}, bf16[512,320]{1,0:T(8,128)(2,1)S(1)}) custom-call(s32[33]{0:T(128)S(1)} %copy-done.3, f32[1,1280]{1,0:T(1,128)S(1)} %reshape.16.gain, bf16[128,1280]{1,0:T(8,128)(2,1)S(1)} %copy-done, bf16[128,1280]{1,0:T(8,128)(2,1)S(1)} %copy-done.2, bf16[128,1280]{1,0:T(8,128)(2,1)S(1)} %collective-permute-done.1.refs_2_, ...), custom_call_target="tpu_custom_call" | custom-call | tf_op jit(solution)/shard_map/pallas_call | solution.py:144
  39.5 0.8 pad_maximum_fusion.1
  40.2 2.4 %collective-permute-start.18 = (bf16[160,1024]{1,0:T(8,128)(2,1)}, bf16[160,1024]{1,0:T(8,128)(2,1)S(1)}, u32[]{:S(2)}, u32[]{:S(2)}) collective-permute-start(bf16[160,1024]{1,0:T(8,128)(2,1)} %bitcast.35), channel_id=1, source_target_pairs={{0,8},{2,10},{4,12},{6,14},{8,0},{10,2},{12,4},{14,6},{17,25},{19,... | collective-permute-start | bytes 983048 | tf_op jit(solution)/shard_map/ppermute | solution.py:483
  42.7 1.3 %collective-permute-start.26 = (bf16[160,1024]{1,0:T(8,128)(2,1)S(1)}, bf16[160,1024]{1,0:T(8,128)(2,1)S(1)}, u32[]{:S(2)}, u32[]{:S(2)}) collective-permute-start(bf16[160,1024]{1,0:T(8,128)(2,1)S(1)} %collective-permute-done.17.refs_6_.refs_21_), channel_id=1, source_target_pairs={{0,16},{2,18},{4,20},{6,22},{8,24},{10,26},{12,28},{14,30},{17,1},... | collective-permute-start | bytes 983048 | tf_op jit(solution)/shard_map/ppermute | solution.py:483
  44.1 0.5 collective-permute-start.10
  44.6 9.2 %collective-permute-done.18.refs_4_.refs_17_ = bf16[160,1024]{1,0:T(8,128)(2,1)S(1)} collective-permute-done((bf16[160,1024]{1,0:T(8,128)(2,1)}, bf16[160,1024]{1,0:T(8,128)(2,1)S(1)}, u32[]{:S(2)}, u32[]{:S(2)}) %collective-permute-start.18) | collective-permute-done | bytes 327712 | tf_op jit(solution)/shard_map/ppermute | solution.py:483
  53.8 1.3 %collective-permute-start.27 = (bf16[160,1024]{1,0:T(8,128)(2,1)S(1)}, bf16[160,1024]{1,0:T(8,128)(2,1)S(1)}, u32[]{:S(2)}, u32[]{:S(2)}) collective-permute-start(bf16[160,1024]{1,0:T(8,128)(2,1)S(1)} %collective-permute-done.18.refs_4_.refs_17_), channel_id=1, source_target_pairs={{0,16},{2,18},{4,20},{6,22},{8,24},{10,26},{12,28},{14,30},{17,1},... | collective-permute-start | bytes 983048 | tf_op jit(solution)/shard_map/ppermute | solution.py:483
  55.1 2.2 %shard_map.79 = (bf16[512,1280]{1,0:T(8,128)(2,1)S(1)}, bf16[512,320]{1,0:T(8,128)(2,1)S(1)}) custom-call(s32[33]{0:T(128)S(1)} %copy-done.3, f32[1,1280]{1,0:T(1,128)S(1)} %reshape.16.gain, bf16[128,1280]{1,0:T(8,128)(2,1)S(1)} %collective-permute-done.3.refs_0_, bf16[128,1280]{1,0:T(8,128)(2,1)} %collective-permute-done.4.refs_1_, ...), custom_call_target="tpu_custom_call" | custom-call | tf_op jit(solution)/shard_map/pallas_call | solution.py:144
  57.3 2.3 %collective-permute-start.19 = (bf16[160,1024]{1,0:T(8,128)(2,1)S(1)}, bf16[160,1024]{1,0:T(8,128)(2,1)S(1)}, u32[]{:S(2)}, u32[]{:S(2)}) collective-permute-start(bf16[160,1024]{1,0:T(8,128)(2,1)S(1)} %bitcast.44), channel_id=1, source_target_pairs={{0,4},{2,6},{4,0},{6,2},{8,12},{10,14},{12,8},{14,10},{17,21},{19,... | collective-permute-start | bytes 983048 | tf_op jit(solution)/shard_map/ppermute | solution.py:483
  59.7 0.9 collective-permute-start.14
  60.7 1.3 %collective-permute-start.13 = (bf16[128,1280]{1,0:T(8,128)(2,1)S(1)}, bf16[128,1280]{1,0:T(8,128)(2,1)S(1)}, u32[]{:S(2)}, u32[]{:S(2)}) collective-permute-start(bf16[128,1280]{1,0:T(8,128)(2,1)S(1)} %broadcast_select_fusion.refs_0_), channel_id=1, source_target_pairs={{0,1},{2,3},{4,5},{6,7},{9,8},{11,10},{13,12},{15,14},{16,17},{18,... | collective-permute-start | bytes 983048 | tf_op jit(solution)/shard_map/ppermute | solution.py:21
  62.0 1.3 %collective-permute-start.16 = (bf16[80,1024]{1,0:T(8,128)(2,1)S(1)}, bf16[80,1024]{1,0:T(8,128)(2,1)S(1)}, u32[]{:S(2)}, u32[]{:S(2)}) collective-permute-start(bf16[80,1024]{1,0:T(8,128)(2,1)S(1)} %bitcast.40), channel_id=1, source_target_pairs={{0,1},{2,3},{4,5},{6,7},{8,9},{10,11},{12,13},{14,15},{17,16},{19,... | collective-permute-start | bytes 491528 | tf_op jit(solution)/shard_map/ppermute | solution.py:483
  63.3 1.3 %collective-permute-start.22 = (bf16[160,1024]{1,0:T(8,128)(2,1)S(1)}, bf16[160,1024]{1,0:T(8,128)(2,1)S(1)}, u32[]{:S(2)}, u32[]{:S(2)}) collective-permute-start(bf16[160,1024]{1,0:T(8,128)(2,1)S(1)} %collective-permute-done.17.refs_6_.refs_21_), channel_id=1, source_target_pairs={{0,1},{2,3},{4,5},{6,7},{8,9},{10,11},{12,13},{14,15},{17,16},{19,... | collective-permute-start | bytes 983048 | tf_op jit(solution)/shard_map/ppermute | solution.py:483
  64.6 1.7 %collective-permute-done.19.refs_2_.refs_13_ = bf16[160,1024]{1,0:T(8,128)(2,1)S(1)} collective-permute-done((bf16[160,1024]{1,0:T(8,128)(2,1)S(1)}, bf16[160,1024]{1,0:T(8,128)(2,1)S(1)}, u32[]{:S(2)}, u32[]{:S(2)}) %collective-permute-start.19) | collective-permute-done | bytes 327712 | tf_op jit(solution)/shard_map/ppermute | solution.py:483
  66.3 1.3 %collective-permute-start.21 = (bf16[160,1024]{1,0:T(8,128)(2,1)S(1)}, bf16[160,1024]{1,0:T(8,128)(2,1)S(1)}, u32[]{:S(2)}, u32[]{:S(2)}) collective-permute-start(bf16[160,1024]{1,0:T(8,128)(2,1)S(1)} %collective-permute-done.18.refs_4_.refs_17_), channel_id=1, source_target_pairs={{0,1},{2,3},{4,5},{6,7},{8,9},{10,11},{12,13},{14,15},{17,16},{19,... | collective-permute-start | bytes 983048 | tf_op jit(solution)/shard_map/ppermute | solution.py:483
  67.6 1.3 %collective-permute-start.28 = (bf16[160,1024]{1,0:T(8,128)(2,1)S(1)}, bf16[160,1024]{1,0:T(8,128)(2,1)S(1)}, u32[]{:S(2)}, u32[]{:S(2)}) collective-permute-start(bf16[160,1024]{1,0:T(8,128)(2,1)S(1)} %collective-permute-done.19.refs_2_.refs_13_), channel_id=1, source_target_pairs={{0,16},{2,18},{4,20},{6,22},{8,24},{10,26},{12,28},{14,30},{17,1},... | collective-permute-start | bytes 983048 | tf_op jit(solution)/shard_map/ppermute | solution.py:483
  69.0 1.3 %collective-permute-start.15 = (bf16[128,1280]{1,0:T(8,128)(2,1)S(1)}, bf16[128,1280]{1,0:T(8,128)(2,1)S(1)}, u32[]{:S(2)}, u32[]{:S(2)}) collective-permute-start(bf16[128,1280]{1,0:T(8,128)(2,1)S(1)} %collective-permute-done.14.refs_2_), channel_id=1, source_target_pairs={{0,1},{2,3},{4,5},{6,7},{9,8},{11,10},{13,12},{15,14},{16,17},{18,... | collective-permute-start | bytes 983048 | tf_op jit(solution)/shard_map/ppermute | solution.py:21
  70.3 1.3 %collective-permute-start.20 = (bf16[160,1024]{1,0:T(8,128)(2,1)S(1)}, bf16[160,1024]{1,0:T(8,128)(2,1)S(1)}, u32[]{:S(2)}, u32[]{:S(2)}) collective-permute-start(bf16[160,1024]{1,0:T(8,128)(2,1)S(1)} %collective-permute-done.19.refs_2_.refs_13_), channel_id=1, source_target_pairs={{0,1},{2,3},{4,5},{6,7},{8,9},{10,11},{12,13},{14,15},{17,16},{19,... | collective-permute-start | bytes 983048 | tf_op jit(solution)/shard_map/ppermute | solution.py:483
  71.6 1.3 %collective-permute-start.31 = (bf16[160,1024]{1,0:T(8,128)(2,1)S(1)}, bf16[160,1024]{1,0:T(8,128)(2,1)S(1)}, u32[]{:S(2)}, u32[]{:S(2)}) collective-permute-start(bf16[160,1024]{1,0:T(8,128)(2,1)S(1)} %collective-permute-done.26.refs_22_), channel_id=1, source_target_pairs={{1,0},{3,2},{5,4},{7,6},{9,8},{11,10},{13,12},{15,14},{16,17},{18,... | collective-permute-start | bytes 983048 | tf_op jit(solution)/shard_map/ppermute | solution.py:520
  72.9 1.3 %collective-permute-start.30 = (bf16[160,1024]{1,0:T(8,128)(2,1)S(1)}, bf16[160,1024]{1,0:T(8,128)(2,1)S(1)}, u32[]{:S(2)}, u32[]{:S(2)}) collective-permute-start(bf16[160,1024]{1,0:T(8,128)(2,1)S(1)} %collective-permute-done.27.refs_18_), channel_id=1, source_target_pairs={{1,0},{3,2},{5,4},{7,6},{9,8},{11,10},{13,12},{15,14},{16,17},{18,... | collective-permute-start | bytes 983048 | tf_op jit(solution)/shard_map/ppermute | solution.py:520
  74.2 1.3 %collective-permute-start.29 = (bf16[160,1024]{1,0:T(8,128)(2,1)S(1)}, bf16[160,1024]{1,0:T(8,128)(2,1)S(1)}, u32[]{:S(2)}, u32[]{:S(2)}) collective-permute-start(bf16[160,1024]{1,0:T(8,128)(2,1)S(1)} %collective-permute-done.28.refs_14_), channel_id=1, source_target_pairs={{1,0},{3,2},{5,4},{7,6},{9,8},{11,10},{13,12},{15,14},{16,17},{18,... | collective-permute-start | bytes 983048 | tf_op jit(solution)/shard_map/ppermute | solution.py:520
  75.5 1.2 %collective-permute-start.23 = (bf16[80,1024]{1,0:T(8,128)(2,1)S(1)}, bf16[80,1024]{1,0:T(8,128)(2,1)S(1)}, u32[]{:S(2)}, u32[]{:S(2)}) collective-permute-start(bf16[80,1024]{1,0:T(8,128)(2,1)S(1)} %bitcast.36), channel_id=1, source_target_pairs={{0,1},{1,0},{2,3},{3,2},{4,5},{5,4},{6,7},{7,6},{8,9},{9,8},{10,11... | collective-permute-start | bytes 491528 | tf_op jit(solution)/shard_map/ppermute | solution.py:21
  76.8 1.3 %collective-permute-start.25 = (bf16[80,1024]{1,0:T(8,128)(2,1)S(1)}, bf16[80,1024]{1,0:T(8,128)(2,1)S(1)}, u32[]{:S(2)}, u32[]{:S(2)}) collective-permute-start(bf16[80,1024]{1,0:T(8,128)(2,1)S(1)} %collective-permute-done.24.refs_10_), channel_id=1, source_target_pairs={{1,0},{3,2},{5,4},{7,6},{9,8},{11,10},{13,12},{15,14},{16,17},{18,... | collective-permute-start | bytes 491528 | tf_op jit(solution)/shard_map/ppermute | solution.py:520
  78.1 1.6 %shard_map.80 = (bf16[512,1280]{1,0:T(8,128)(2,1)S(1)}, bf16[512,320]{1,0:T(8,128)(2,1)S(1)}) custom-call(s32[33]{0:T(128)S(1)} %copy-done.3, f32[1,1280]{1,0:T(1,128)S(1)} %reshape.16.gain, bf16[128,1280]{1,0:T(8,128)(2,1)S(1)} %broadcast_select_fusion.refs_0_, bf16[128,1280]{1,0:T(8,128)(2,1)S(1)} %collective-permute-done.13.refs_1_, ...), custom_call_target="tpu_custom_call" | custom-call | tf_op jit(solution)/shard_map/pallas_call | solution.py:144
  79.7 1.5 %shard_map.81 = (f32[8,1536]{1,0:T(8,128)S(1)}, f32[80,320]{1,0:T(8,128)S(1)}, f32[16,64]{1,0:T(8,128)S(1)}) custom-call(s32[33]{0:T(128)S(1)} %copy-done.3, bf16[80,1024]{1,0:T(8,128)(2,1)S(1)} %bitcast.37, bf16[80,1024]{1,0:T(8,128)(2,1)S(1)} %bitcast.41, bf16[80,1024]{1,0:T(8,128)(2,1)S(1)} %collective-permute-done.16.refs_1_.refs_11_, ...), custom_call_target="tpu_custom_call" | custom-call | tf_op jit(solution)/shard_map/pallas_call | solution.py:192
  81.2 14.0 %shard_map.82 = (bf16[512,320]{1,0:T(8,128)(2,1)S(1)}, bf16[256,320]{1,0:T(8,128)(2,1)S(1)}, bf16[256,320]{1,0:T(8,128)(2,1)}) custom-call(s32[33]{0:T(128)S(1)} %copy-done.3, bf16[512,1280]{1,0:T(8,128)(2,1)S(1)} %get-tuple-element.34.refs_0_, bf16[512,320]{1,0:T(8,128)(2,1)S(1)} %get-tuple-element.35.refs_1_, ...), custom_call_target="tpu_custom_call" | custom-call | tf_op jit(solution)/shard_map/pallas_call | solution.py:333
  95.1 1.3 %collective-permute-start.32 = (bf16[512,320]{1,0:T(8,128)(2,1)S(1)}, bf16[512,320]{1,0:T(8,128)(2,1)S(1)}, u32[]{:S(2)}, u32[]{:S(2)}) collective-permute-start(bf16[512,320]{1,0:T(8,128)(2,1)S(1)} %get-tuple-element.56.memory), channel_id=1, source_target_pairs={{0,1},{1,0},{2,3},{3,2},{4,5},{5,4},{6,7},{7,6},{8,9},{9,8},{10,11... | collective-permute-start | bytes 983048 | tf_op jit(solution)/shard_map/ppermute | solution.py:21
  96.4 1.3 %collective-permute-done.32.beside = bf16[512,320]{1,0:T(8,128)(2,1)S(1)} collective-permute-done((bf16[512,320]{1,0:T(8,128)(2,1)S(1)}, bf16[512,320]{1,0:T(8,128)(2,1)S(1)}, u32[]{:S(2)}, u32[]{:S(2)}) %collective-permute-start.32) | collective-permute-done | bytes 327712 | tf_op jit(solution)/shard_map/ppermute | solution.py:21
  97.8 1.3 %shard_map.83 = (f32[40,128]{1,0:T(8,128)S(1)}, f32[40,128]{1,0:T(8,128)S(1)}) custom-call(s32[33]{0:T(128)S(1)} %copy-done.3, f32[80,320]{1,0:T(8,128)S(1)} %get-tuple-element.54.tokens, f32[16,64]{1,0:T(8,128)S(1)} %get-tuple-element.55.asked, bf16[512,320]{1,0:T(8,128)(2,1)S(1)} %get-tuple-element.56.memory, ...), custom_call_target="tpu_custom_call" | custom-call | tf_op jit(solution)/shard_map/pallas_call | solution.py:398
  99.1 0.7 collective-permute-start.33
  99.8 3.3 %collective-permute-start.37 = (f32[40,128]{1,0:T(8,128)S(1)}, f32[40,128]{1,0:T(8,128)S(1)}, u32[]{:S(2)}, u32[]{:S(2)}) collective-permute-start(f32[40,128]{1,0:T(8,128)S(1)} %get-tuple-element.61), channel_id=1, source_target_pairs={{0,8},{1,9},{2,10},{3,11},{4,12},{5,13},{6,14},{7,15},{8,0},{9,1},... | collective-permute-start | bytes 61448 | tf_op jit(solution)/shard_map/ppermute | solution.py:21
  103.1 1.9 %collective-permute-done.37.refs_1_ = f32[40,128]{1,0:T(8,128)S(1)} collective-permute-done((f32[40,128]{1,0:T(8,128)S(1)}, f32[40,128]{1,0:T(8,128)S(1)}, u32[]{:S(2)}, u32[]{:S(2)}) %collective-permute-start.37) | collective-permute-done | bytes 20512 | tf_op jit(solution)/shard_map/ppermute | solution.py:21
  105.1 0.2 shard_map.84
  105.3 2.0 %collective-permute-start.38 = (bf16[2,384]{1,0:T(2,128)(2,1)S(1)}, bf16[2,384]{1,0:T(2,128)(2,1)S(1)}, u32[]{:S(2)}, u32[]{:S(2)}) collective-permute-start(bf16[2,384]{1,0:T(2,128)(2,1)S(1)} %get-tuple-element.63), channel_id=1, source_target_pairs={{0,2},{1,3},{2,0},{3,1},{4,6},{5,7},{6,4},{7,5},{8,10},{9,11},{10,... | collective-permute-start | bytes 4616 | tf_op jit(solution)/shard_map/ppermute | solution.py:21
  107.3 5.1 %collective-permute-start.39 = (bf16[2,384]{1,0:T(2,128)(2,1)S(1)}, bf16[2,384]{1,0:T(2,128)(2,1)S(1)}, u32[]{:S(2)}, u32[]{:S(2)}) collective-permute-start(bf16[2,384]{1,0:T(2,128)(2,1)S(1)} %get-tuple-element.64), channel_id=1, source_target_pairs={{0,4},{1,5},{2,6},{3,7},{4,0},{5,1},{6,2},{7,3},{8,12},{9,13},{10,... | collective-permute-start | bytes 4616 | tf_op jit(solution)/shard_map/ppermute | solution.py:21
  112.5 0.5 collective-permute-start.35
  113.0 0.9 collective-permute-done.39
  113.9 2.9 %collective-permute-done.40 = bf16[2,384]{1,0:T(2,128)(2,1)S(1)} collective-permute-done((bf16[2,384]{1,0:T(2,128)(2,1)S(1)}, bf16[2,384]{1,0:T(2,128)(2,1)S(1)}, u32[]{:S(2)}, u32[]{:S(2)}) %collective-permute-start.40) | collective-permute-done | bytes 1568 | tf_op jit(solution)/shard_map/ppermute | solution.py:21
  116.9 0.7 concatenate.15
  117.6 0.1 select_select_fusion
  117.9 0.8 concatenate.14
  (83 shorter events, 0.6 us)
Async XLA Ops:
  0.6 11.6 %collective-permute-start.1 = (bf16[128,1280]{1,0:T(8,128)(2,1)}, bf16[128,1280]{1,0:T(8,128)(2,1)S(1)}, u32[]{:S(2)}, u32[]{:S(2)}) collective-permute-start(bf16[128,1280]{1,0:T(8,128)(2,1)} %refs_0_.2), channel_id=1, source_target_pairs={{0,2},{1,3},{2,0},{3,1},{4,6},{5,7},{6,4},{7,5},{8,10},{9,11},{10,... | collective-permute-start | bytes 983048 | tf_op jit(solution)/shard_map/ppermute | solution.py:21
  3.6 11.7 %collective-permute-start.3 = (bf16[128,1280]{1,0:T(8,128)(2,1)}, bf16[128,1280]{1,0:T(8,128)(2,1)S(1)}, u32[]{:S(2)}, u32[]{:S(2)}) collective-permute-start(bf16[128,1280]{1,0:T(8,128)(2,1)} %refs_0_.2), channel_id=1, source_target_pairs={{0,4},{1,5},{2,6},{3,7},{4,0},{5,1},{6,2},{7,3},{8,12},{9,13},{10,... | collective-permute-start | bytes 983048 | tf_op jit(solution)/shard_map/ppermute | solution.py:21
  5.2 10.1 %collective-permute-start.11 = (bf16[128,1280]{1,0:T(8,128)(2,1)}, bf16[128,1280]{1,0:T(8,128)(2,1)S(1)}, u32[]{:S(2)}, u32[]{:S(2)}) collective-permute-start(bf16[128,1280]{1,0:T(8,128)(2,1)} %refs_0_.2), channel_id=1, source_target_pairs={{4,8},{5,9},{6,10},{7,11},{8,4},{9,5},{10,6},{11,7},{20,24},{21,25... | collective-permute-start | bytes 983048 | tf_op jit(solution)/shard_map/ppermute | solution.py:21
  5.9 2.9 %collective-permute-start.5 = (bf16[2,1280]{1,0:T(2,128)(2,1)}, bf16[2,1280]{1,0:T(2,128)(2,1)S(1)}, u32[]{:S(2)}, u32[]{:S(2)}) collective-permute-start(bf16[2,1280]{1,0:T(2,128)(2,1)} %refs_0_.3), channel_id=1, source_target_pairs={{0,1},{1,0},{2,3},{3,2},{4,5},{5,4},{6,7},{7,6},{8,9},{9,8},{10,11... | collective-permute-start | bytes 15368 | tf_op jit(solution)/shard_map/ppermute | solution.py:21
  6.0 1.5 %collective-permute-start.6 = (s32[2,16]{1,0:T(2,128)}, s32[2,16]{1,0:T(2,128)S(1)}, u32[]{:S(2)}, u32[]{:S(2)}) collective-permute-start(s32[2,16]{1,0:T(2,128)} %refs_2_.1), channel_id=1, source_target_pairs={{0,1},{1,0},{2,3},{3,2},{4,5},{5,4},{6,7},{7,6},{8,9},{9,8},{10,11... | collective-permute-start | bytes 392 | tf_op jit(solution)/shard_map/ppermute | solution.py:21
  7.5 1.3 %copy-start.12 = (s32[2,16]{1,0:T(2,128)}, s32[2,16]{1,0:T(2,128)S(1)}, u32[]{:S(2)}) copy-start(s32[2,16]{1,0:T(2,128)S(1)} %collective-permute-done.6.refs_3_) | copy-start | bytes 388
  7.5 1.3 %collective-permute-start.7 = (s32[1,128]{1,0:T(1,128)}, s32[1,128]{1,0:T(1,128)S(1)}, u32[]{:S(2)}, u32[]{:S(2)}) collective-permute-start(s32[1,128]{1,0:T(1,128)} %bitcast.45), channel_id=1, source_target_pairs={{0,1},{1,0},{2,3},{3,2},{4,5},{5,4},{6,7},{7,6},{8,9},{9,8},{10,11... | collective-permute-start | bytes 1544 | tf_op jit(solution)/shard_map/ppermute | solution.py:21
  8.4 27.7 %copy-start.10 = (f32[1280]{0:T(1024)S(1)}, f32[1280]{0:T(1024)}, u32[]{:S(2)}) copy-start(f32[1280]{0:T(1024)} %param.7) | copy-start | bytes 15364
  8.4 28.5 %copy-start = (bf16[128,1280]{1,0:T(8,128)(2,1)S(1)}, bf16[128,1280]{1,0:T(8,128)(2,1)}, u32[]{:S(2)}) copy-start(bf16[128,1280]{1,0:T(8,128)(2,1)} %refs_0_.2) | copy-start | bytes 983044
  8.4 28.5 %copy-start.3 = (s32[33]{0:T(128)S(1)}, s32[33]{0:T(128)}, u32[]{:S(2)}) copy-start(s32[33]{0:T(128)} %stack.137.table.spot.places) | copy-start | bytes 400
  8.8 0.5 copy-start.13
  9.3 0.6 copy-start.11
  12.2 9.2 %collective-permute-start.8 = (bf16[2,80,1024]{2,1,0:T(8,128)(2,1)}, bf16[2,80,1024]{2,1,0:T(8,128)(2,1)S(1)}, u32[]{:S(2)}, u32[]{:S(2)}) collective-permute-start(bf16[2,80,1024]{2,1,0:T(8,128)(2,1)} %get-tuple-element.37), channel_id=1, source_target_pairs={{0,2},{2,0},{4,6},{6,4},{8,10},{10,8},{12,14},{14,12},{17,19},{19,... | collective-permute-start | bytes 983048 | tf_op jit(solution)/shard_map/ppermute | solution.py:483
  15.2 21.0 %collective-permute-start = (bf16[128,1280]{1,0:T(8,128)(2,1)}, bf16[128,1280]{1,0:T(8,128)(2,1)S(1)}, u32[]{:S(2)}, u32[]{:S(2)}) collective-permute-start(bf16[128,1280]{1,0:T(8,128)(2,1)} %refs_0_.2), channel_id=1, source_target_pairs={{0,1},{1,0},{2,3},{3,2},{4,5},{5,4},{6,7},{7,6},{8,9},{9,8},{10,11... | collective-permute-start | bytes 983048 | tf_op jit(solution)/shard_map/ppermute | solution.py:21
  15.3 1.3 %copy-start.4 = (bf16[128,1280]{1,0:T(8,128)(2,1)}, bf16[128,1280]{1,0:T(8,128)(2,1)S(1)}, u32[]{:S(2)}) copy-start(bf16[128,1280]{1,0:T(8,128)(2,1)S(1)} %collective-permute-done.11) | copy-start | bytes 983044
  15.3 13.1 %collective-permute-start.12 = (bf16[128,1280]{1,0:T(8,128)(2,1)}, bf16[128,1280]{1,0:T(8,128)(2,1)S(1)}, u32[]{:S(2)}, u32[]{:S(2)}) collective-permute-start(bf16[128,1280]{1,0:T(8,128)(2,1)} %refs_0_.2), channel_id=1, source_target_pairs={{4,12},{5,13},{6,14},{7,15},{8,0},{9,1},{10,2},{11,3},{20,28},{21,... | collective-permute-start | bytes 983048 | tf_op jit(solution)/shard_map/ppermute | solution.py:21
  17.7 19.2 %collective-permute-start.2 = (bf16[128,1280]{1,0:T(8,128)(2,1)S(1)}, bf16[128,1280]{1,0:T(8,128)(2,1)S(1)}, u32[]{:S(2)}, u32[]{:S(2)}) collective-permute-start(bf16[128,1280]{1,0:T(8,128)(2,1)S(1)} %collective-permute-done.1.refs_2_), channel_id=1, source_target_pairs={{0,1},{1,0},{2,3},{3,2},{4,5},{5,4},{6,7},{7,6},{8,9},{9,8},{10,11... | collective-permute-start | bytes 983048 | tf_op jit(solution)/shard_map/ppermute | solution.py:21
  21.5 22.6 %copy-start.8 = (bf16[2,80,1024]{2,1,0:T(8,128)(2,1)}, bf16[2,80,1024]{2,1,0:T(8,128)(2,1)S(1)}, u32[]{:S(2)}) copy-start(bf16[2,80,1024]{2,1,0:T(8,128)(2,1)S(1)} %pad_maximum_fusion) | copy-start | bytes 983044
  28.4 7.7 %copy-start.6 = (bf16[128,1280]{1,0:T(8,128)(2,1)}, bf16[128,1280]{1,0:T(8,128)(2,1)S(1)}, u32[]{:S(2)}) copy-start(bf16[128,1280]{1,0:T(8,128)(2,1)S(1)} %collective-permute-done.12) | copy-start | bytes 983044
  28.5 11.8 %collective-permute-start.17 = (bf16[160,1024]{1,0:T(8,128)(2,1)S(1)}, bf16[160,1024]{1,0:T(8,128)(2,1)S(1)}, u32[]{:S(2)}, u32[]{:S(2)}) collective-permute-start(bf16[160,1024]{1,0:T(8,128)(2,1)S(1)} %bitcast.43), channel_id=1, source_target_pairs={{0,12},{2,14},{4,8},{6,10},{8,4},{10,6},{12,0},{14,2},{17,29},{19,... | collective-permute-start | bytes 983048 | tf_op jit(solution)/shard_map/ppermute | solution.py:483
  33.9 10.1 %collective-permute-start.9 = (bf16[128,1280]{1,0:T(8,128)(2,1)S(1)}, bf16[128,1280]{1,0:T(8,128)(2,1)}, u32[]{:S(2)}, u32[]{:S(2)}) collective-permute-start(bf16[128,1280]{1,0:T(8,128)(2,1)S(1)} %collective-permute-done.3.refs_0_), channel_id=1, source_target_pairs={{0,2},{1,3},{2,0},{3,1},{4,6},{5,7},{6,4},{7,5},{8,10},{9,11},{10,... | collective-permute-start | bytes 983048 | tf_op jit(solution)/shard_map/ppermute | solution.py:21
  34.8 7.8 %collective-permute-start.24 = (bf16[80,1024]{1,0:T(8,128)(2,1)S(1)}, bf16[80,1024]{1,0:T(8,128)(2,1)S(1)}, u32[]{:S(2)}, u32[]{:S(2)}) collective-permute-start(bf16[80,1024]{1,0:T(8,128)(2,1)S(1)} %bitcast.39), channel_id=1, source_target_pairs={{0,16},{2,18},{4,20},{6,22},{8,24},{10,26},{12,28},{14,30},{17,1},... | collective-permute-start | bytes 491528 | tf_op jit(solution)/shard_map/ppermute | solution.py:483
  36.2 0.7 copy-start.1
  36.9 1.0 copy-start.2
  40.2 13.6 %collective-permute-start.18 = (bf16[160,1024]{1,0:T(8,128)(2,1)}, bf16[160,1024]{1,0:T(8,128)(2,1)S(1)}, u32[]{:S(2)}, u32[]{:S(2)}) collective-permute-start(bf16[160,1024]{1,0:T(8,128)(2,1)} %bitcast.35), channel_id=1, source_target_pairs={{0,8},{2,10},{4,12},{6,14},{8,0},{10,2},{12,4},{14,6},{17,25},{19,... | collective-permute-start | bytes 983048 | tf_op jit(solution)/shard_map/ppermute | solution.py:483
  42.7 11.1 %collective-permute-start.26 = (bf16[160,1024]{1,0:T(8,128)(2,1)S(1)}, bf16[160,1024]{1,0:T(8,128)(2,1)S(1)}, u32[]{:S(2)}, u32[]{:S(2)}) collective-permute-start(bf16[160,1024]{1,0:T(8,128)(2,1)S(1)} %collective-permute-done.17.refs_6_.refs_21_), channel_id=1, source_target_pairs={{0,16},{2,18},{4,20},{6,22},{8,24},{10,26},{12,28},{14,30},{17,1},... | collective-permute-start | bytes 983048 | tf_op jit(solution)/shard_map/ppermute | solution.py:483
  44.0 11.1 %collective-permute-start.4 = (bf16[128,1280]{1,0:T(8,128)(2,1)S(1)}, bf16[128,1280]{1,0:T(8,128)(2,1)}, u32[]{:S(2)}, u32[]{:S(2)}) collective-permute-start(bf16[128,1280]{1,0:T(8,128)(2,1)S(1)} %collective-permute-done.3.refs_0_), channel_id=1, source_target_pairs={{0,1},{1,0},{2,3},{3,2},{4,5},{5,4},{6,7},{7,6},{8,9},{9,8},{10,11... | collective-permute-start | bytes 983048 | tf_op jit(solution)/shard_map/ppermute | solution.py:21
  44.1 11.0 %collective-permute-start.10 = (bf16[128,1280]{1,0:T(8,128)(2,1)}, bf16[128,1280]{1,0:T(8,128)(2,1)}, u32[]{:S(2)}, u32[]{:S(2)}) collective-permute-start(bf16[128,1280]{1,0:T(8,128)(2,1)} %collective-permute-done.9.refs_2_), channel_id=1, source_target_pairs={{0,1},{1,0},{2,3},{3,2},{4,5},{5,4},{6,7},{7,6},{8,9},{9,8},{10,11... | collective-permute-start | bytes 983048 | tf_op jit(solution)/shard_map/ppermute | solution.py:21
  44.6 12.8 %copy-start.9 = (bf16[2,80,1024]{2,1,0:T(8,128)(2,1)S(1)}, bf16[2,80,1024]{2,1,0:T(8,128)(2,1)}, u32[]{:S(2)}) copy-start(bf16[2,80,1024]{2,1,0:T(8,128)(2,1)} %copy-done.8) | copy-start | bytes 983044
  44.6 15.1 %copy-start.5 = (bf16[128,1280]{1,0:T(8,128)(2,1)S(1)}, bf16[128,1280]{1,0:T(8,128)(2,1)}, u32[]{:S(2)}) copy-start(bf16[128,1280]{1,0:T(8,128)(2,1)} %copy-done.4) | copy-start | bytes 983044
  44.6 15.1 %copy-start.7 = (bf16[128,1280]{1,0:T(8,128)(2,1)S(1)}, bf16[128,1280]{1,0:T(8,128)(2,1)}, u32[]{:S(2)}) copy-start(bf16[128,1280]{1,0:T(8,128)(2,1)} %copy-done.6) | copy-start | bytes 983044
  53.8 9.5 %collective-permute-start.27 = (bf16[160,1024]{1,0:T(8,128)(2,1)S(1)}, bf16[160,1024]{1,0:T(8,128)(2,1)S(1)}, u32[]{:S(2)}, u32[]{:S(2)}) collective-permute-start(bf16[160,1024]{1,0:T(8,128)(2,1)S(1)} %collective-permute-done.18.refs_4_.refs_17_), channel_id=1, source_target_pairs={{0,16},{2,18},{4,20},{6,22},{8,24},{10,26},{12,28},{14,30},{17,1},... | collective-permute-start | bytes 983048 | tf_op jit(solution)/shard_map/ppermute | solution.py:483
  57.3 9.0 %collective-permute-start.19 = (bf16[160,1024]{1,0:T(8,128)(2,1)S(1)}, bf16[160,1024]{1,0:T(8,128)(2,1)S(1)}, u32[]{:S(2)}, u32[]{:S(2)}) collective-permute-start(bf16[160,1024]{1,0:T(8,128)(2,1)S(1)} %bitcast.44), channel_id=1, source_target_pairs={{0,4},{2,6},{4,0},{6,2},{8,12},{10,14},{12,8},{14,10},{17,21},{19,... | collective-permute-start | bytes 983048 | tf_op jit(solution)/shard_map/ppermute | solution.py:483
  59.7 9.2 %collective-permute-start.14 = (bf16[128,1280]{1,0:T(8,128)(2,1)S(1)}, bf16[128,1280]{1,0:T(8,128)(2,1)S(1)}, u32[]{:S(2)}, u32[]{:S(2)}) collective-permute-start(bf16[128,1280]{1,0:T(8,128)(2,1)S(1)} %broadcast_select_fusion.refs_0_), channel_id=1, source_target_pairs={{0,2},{1,3},{2,0},{3,1},{4,6},{5,7},{6,4},{7,5},{8,10},{9,11},{10,... | collective-permute-start | bytes 983048 | tf_op jit(solution)/shard_map/ppermute | solution.py:21
  60.7 9.6 %collective-permute-start.13 = (bf16[128,1280]{1,0:T(8,128)(2,1)S(1)}, bf16[128,1280]{1,0:T(8,128)(2,1)S(1)}, u32[]{:S(2)}, u32[]{:S(2)}) collective-permute-start(bf16[128,1280]{1,0:T(8,128)(2,1)S(1)} %broadcast_select_fusion.refs_0_), channel_id=1, source_target_pairs={{0,1},{2,3},{4,5},{6,7},{9,8},{11,10},{13,12},{15,14},{16,17},{18,... | collective-permute-start | bytes 983048 | tf_op jit(solution)/shard_map/ppermute | solution.py:21
  62.0 5.7 %collective-permute-start.16 = (bf16[80,1024]{1,0:T(8,128)(2,1)S(1)}, bf16[80,1024]{1,0:T(8,128)(2,1)S(1)}, u32[]{:S(2)}, u32[]{:S(2)}) collective-permute-start(bf16[80,1024]{1,0:T(8,128)(2,1)S(1)} %bitcast.40), channel_id=1, source_target_pairs={{0,1},{2,3},{4,5},{6,7},{8,9},{10,11},{12,13},{14,15},{17,16},{19,... | collective-permute-start | bytes 491528 | tf_op jit(solution)/shard_map/ppermute | solution.py:483
  63.3 8.3 %collective-permute-start.22 = (bf16[160,1024]{1,0:T(8,128)(2,1)S(1)}, bf16[160,1024]{1,0:T(8,128)(2,1)S(1)}, u32[]{:S(2)}, u32[]{:S(2)}) collective-permute-start(bf16[160,1024]{1,0:T(8,128)(2,1)S(1)} %collective-permute-done.17.refs_6_.refs_21_), channel_id=1, source_target_pairs={{0,1},{2,3},{4,5},{6,7},{8,9},{10,11},{12,13},{14,15},{17,16},{19,... | collective-permute-start | bytes 983048 | tf_op jit(solution)/shard_map/ppermute | solution.py:483
  66.3 6.6 %collective-permute-start.21 = (bf16[160,1024]{1,0:T(8,128)(2,1)S(1)}, bf16[160,1024]{1,0:T(8,128)(2,1)S(1)}, u32[]{:S(2)}, u32[]{:S(2)}) collective-permute-start(bf16[160,1024]{1,0:T(8,128)(2,1)S(1)} %collective-permute-done.18.refs_4_.refs_17_), channel_id=1, source_target_pairs={{0,1},{2,3},{4,5},{6,7},{8,9},{10,11},{12,13},{14,15},{17,16},{19,... | collective-permute-start | bytes 983048 | tf_op jit(solution)/shard_map/ppermute | solution.py:483
  67.6 6.6 %collective-permute-start.28 = (bf16[160,1024]{1,0:T(8,128)(2,1)S(1)}, bf16[160,1024]{1,0:T(8,128)(2,1)S(1)}, u32[]{:S(2)}, u32[]{:S(2)}) collective-permute-start(bf16[160,1024]{1,0:T(8,128)(2,1)S(1)} %collective-permute-done.19.refs_2_.refs_13_), channel_id=1, source_target_pairs={{0,16},{2,18},{4,20},{6,22},{8,24},{10,26},{12,28},{14,30},{17,1},... | collective-permute-start | bytes 983048 | tf_op jit(solution)/shard_map/ppermute | solution.py:483
  69.0 6.6 %collective-permute-start.15 = (bf16[128,1280]{1,0:T(8,128)(2,1)S(1)}, bf16[128,1280]{1,0:T(8,128)(2,1)S(1)}, u32[]{:S(2)}, u32[]{:S(2)}) collective-permute-start(bf16[128,1280]{1,0:T(8,128)(2,1)S(1)} %collective-permute-done.14.refs_2_), channel_id=1, source_target_pairs={{0,1},{2,3},{4,5},{6,7},{9,8},{11,10},{13,12},{15,14},{16,17},{18,... | collective-permute-start | bytes 983048 | tf_op jit(solution)/shard_map/ppermute | solution.py:21
  70.3 6.5 %collective-permute-start.20 = (bf16[160,1024]{1,0:T(8,128)(2,1)S(1)}, bf16[160,1024]{1,0:T(8,128)(2,1)S(1)}, u32[]{:S(2)}, u32[]{:S(2)}) collective-permute-start(bf16[160,1024]{1,0:T(8,128)(2,1)S(1)} %collective-permute-done.19.refs_2_.refs_13_), channel_id=1, source_target_pairs={{0,1},{2,3},{4,5},{6,7},{8,9},{10,11},{12,13},{14,15},{17,16},{19,... | collective-permute-start | bytes 983048 | tf_op jit(solution)/shard_map/ppermute | solution.py:483
  71.6 9.5 %collective-permute-start.31 = (bf16[160,1024]{1,0:T(8,128)(2,1)S(1)}, bf16[160,1024]{1,0:T(8,128)(2,1)S(1)}, u32[]{:S(2)}, u32[]{:S(2)}) collective-permute-start(bf16[160,1024]{1,0:T(8,128)(2,1)S(1)} %collective-permute-done.26.refs_22_), channel_id=1, source_target_pairs={{1,0},{3,2},{5,4},{7,6},{9,8},{11,10},{13,12},{15,14},{16,17},{18,... | collective-permute-start | bytes 983048 | tf_op jit(solution)/shard_map/ppermute | solution.py:520
  72.9 8.2 %collective-permute-start.30 = (bf16[160,1024]{1,0:T(8,128)(2,1)S(1)}, bf16[160,1024]{1,0:T(8,128)(2,1)S(1)}, u32[]{:S(2)}, u32[]{:S(2)}) collective-permute-start(bf16[160,1024]{1,0:T(8,128)(2,1)S(1)} %collective-permute-done.27.refs_18_), channel_id=1, source_target_pairs={{1,0},{3,2},{5,4},{7,6},{9,8},{11,10},{13,12},{15,14},{16,17},{18,... | collective-permute-start | bytes 983048 | tf_op jit(solution)/shard_map/ppermute | solution.py:520
  74.2 6.9 %collective-permute-start.29 = (bf16[160,1024]{1,0:T(8,128)(2,1)S(1)}, bf16[160,1024]{1,0:T(8,128)(2,1)S(1)}, u32[]{:S(2)}, u32[]{:S(2)}) collective-permute-start(bf16[160,1024]{1,0:T(8,128)(2,1)S(1)} %collective-permute-done.28.refs_14_), channel_id=1, source_target_pairs={{1,0},{3,2},{5,4},{7,6},{9,8},{11,10},{13,12},{15,14},{16,17},{18,... | collective-permute-start | bytes 983048 | tf_op jit(solution)/shard_map/ppermute | solution.py:520
  75.5 5.6 %collective-permute-start.23 = (bf16[80,1024]{1,0:T(8,128)(2,1)S(1)}, bf16[80,1024]{1,0:T(8,128)(2,1)S(1)}, u32[]{:S(2)}, u32[]{:S(2)}) collective-permute-start(bf16[80,1024]{1,0:T(8,128)(2,1)S(1)} %bitcast.36), channel_id=1, source_target_pairs={{0,1},{1,0},{2,3},{3,2},{4,5},{5,4},{6,7},{7,6},{8,9},{9,8},{10,11... | collective-permute-start | bytes 491528 | tf_op jit(solution)/shard_map/ppermute | solution.py:21
  76.8 4.3 %collective-permute-start.25 = (bf16[80,1024]{1,0:T(8,128)(2,1)S(1)}, bf16[80,1024]{1,0:T(8,128)(2,1)S(1)}, u32[]{:S(2)}, u32[]{:S(2)}) collective-permute-start(bf16[80,1024]{1,0:T(8,128)(2,1)S(1)} %collective-permute-done.24.refs_10_), channel_id=1, source_target_pairs={{1,0},{3,2},{5,4},{7,6},{9,8},{11,10},{13,12},{15,14},{16,17},{18,... | collective-permute-start | bytes 491528 | tf_op jit(solution)/shard_map/ppermute | solution.py:520
  95.1 2.6 %collective-permute-start.32 = (bf16[512,320]{1,0:T(8,128)(2,1)S(1)}, bf16[512,320]{1,0:T(8,128)(2,1)S(1)}, u32[]{:S(2)}, u32[]{:S(2)}) collective-permute-start(bf16[512,320]{1,0:T(8,128)(2,1)S(1)} %get-tuple-element.56.memory), channel_id=1, source_target_pairs={{0,1},{1,0},{2,3},{3,2},{4,5},{5,4},{6,7},{7,6},{8,9},{9,8},{10,11... | collective-permute-start | bytes 983048 | tf_op jit(solution)/shard_map/ppermute | solution.py:21
  99.1 13.3 %collective-permute-start.34 = (bf16[256,320]{1,0:T(8,128)(2,1)}, bf16[256,320]{1,0:T(8,128)(2,1)S(1)}, u32[]{:S(2)}, u32[]{:S(2)}) collective-permute-start(bf16[256,320]{1,0:T(8,128)(2,1)} %get-tuple-element.60), channel_id=1, source_target_pairs={{0,2},{1,6},{2,0},{3,4},{4,3},{5,7},{6,1},{7,5},{8,10},{9,14},{10,... | collective-permute-start | bytes 491528 | tf_op jit(solution)/shard_map/ppermute | solution.py:21
  99.1 13.3 %collective-permute-start.33 = (bf16[256,320]{1,0:T(8,128)(2,1)S(1)}, bf16[256,320]{1,0:T(8,128)(2,1)S(1)}, u32[]{:S(2)}, u32[]{:S(2)}) collective-permute-start(bf16[256,320]{1,0:T(8,128)(2,1)S(1)} %get-tuple-element.58), channel_id=1, source_target_pairs={{0,0},{1,4},{2,2},{3,6},{4,1},{5,5},{6,3},{7,7},{8,8},{9,12},{10,1... | collective-permute-start | bytes 491528 | tf_op jit(solution)/shard_map/ppermute | solution.py:21
  99.8 5.2 %collective-permute-start.37 = (f32[40,128]{1,0:T(8,128)S(1)}, f32[40,128]{1,0:T(8,128)S(1)}, u32[]{:S(2)}, u32[]{:S(2)}) collective-permute-start(f32[40,128]{1,0:T(8,128)S(1)} %get-tuple-element.61), channel_id=1, source_target_pairs={{0,8},{1,9},{2,10},{3,11},{4,12},{5,13},{6,14},{7,15},{8,0},{9,1},... | collective-permute-start | bytes 61448 | tf_op jit(solution)/shard_map/ppermute | solution.py:21
  105.3 7.7 %collective-permute-start.38 = (bf16[2,384]{1,0:T(2,128)(2,1)S(1)}, bf16[2,384]{1,0:T(2,128)(2,1)S(1)}, u32[]{:S(2)}, u32[]{:S(2)}) collective-permute-start(bf16[2,384]{1,0:T(2,128)(2,1)S(1)} %get-tuple-element.63), channel_id=1, source_target_pairs={{0,2},{1,3},{2,0},{3,1},{4,6},{5,7},{6,4},{7,5},{8,10},{9,11},{10,... | collective-permute-start | bytes 4616 | tf_op jit(solution)/shard_map/ppermute | solution.py:21
  107.3 6.6 %collective-permute-start.39 = (bf16[2,384]{1,0:T(2,128)(2,1)S(1)}, bf16[2,384]{1,0:T(2,128)(2,1)S(1)}, u32[]{:S(2)}, u32[]{:S(2)}) collective-permute-start(bf16[2,384]{1,0:T(2,128)(2,1)S(1)} %get-tuple-element.64), channel_id=1, source_target_pairs={{0,4},{1,5},{2,6},{3,7},{4,0},{5,1},{6,2},{7,3},{8,12},{9,13},{10,... | collective-permute-start | bytes 4616 | tf_op jit(solution)/shard_map/ppermute | solution.py:21
  112.4 4.5 %collective-permute-start.40 = (bf16[2,384]{1,0:T(2,128)(2,1)S(1)}, bf16[2,384]{1,0:T(2,128)(2,1)S(1)}, u32[]{:S(2)}, u32[]{:S(2)}) collective-permute-start(bf16[2,384]{1,0:T(2,128)(2,1)S(1)} %get-tuple-element.65), channel_id=1, source_target_pairs={{0,6},{1,7},{2,4},{3,5},{4,2},{5,3},{6,0},{7,1},{8,14},{9,15},{10,... | collective-permute-start | bytes 4616 | tf_op jit(solution)/shard_map/ppermute | solution.py:21
  112.4 5.3 %collective-permute-start.36 = (bf16[128,320]{1,0:T(8,128)(2,1)S(1)}, bf16[128,320]{1,0:T(8,128)(2,1)S(1)}, u32[]{:S(2)}, u32[]{:S(2)}) collective-permute-start(bf16[128,320]{1,0:T(8,128)(2,1)S(1)} %constant_dynamic-slice_fusion), channel_id=1, source_target_pairs={{0,1},{1,0},{2,3},{3,2},{4,5},{5,4},{6,7},{7,6},{8,9},{9,8},{10,11... | collective-permute-start | bytes 245768 | tf_op jit(solution)/shard_map/ppermute | solution.py:21
  112.5 5.1 %collective-permute-start.35 = (bf16[128,320]{1,0:T(8,128)(2,1)S(1)}, bf16[128,320]{1,0:T(8,128)(2,1)S(1)}, u32[]{:S(2)}, u32[]{:S(2)}) collective-permute-start(bf16[128,320]{1,0:T(8,128)(2,1)S(1)} %constant_dynamic-slice_fusion.1), channel_id=1, source_target_pairs={{0,1},{1,0},{2,3},{3,2},{4,5},{5,4},{6,7},{7,6},{8,9},{9,8},{10,11... | collective-permute-start | bytes 245768 | tf_op jit(solution)/shard_map/ppermute | solution.py:21

commit v7 on v6

--- a/solution.py
+++ b/solution.py
@@ -51,70 +51,82 @@
     return jnp.concatenate(heads + [asked], axis=0)
 
 
-def pack_kernel(spot, weight, *refs):
-    queries, masks, segments = refs[0:2], refs[2:4], refs[4:6]
-    outs, lanes = refs[6:8], refs[8]
-    x, c = spot[6], spot[7]
+def pack_kernel(table, weight, queries, mask, segments, mine, theirs):
     rows, width = weight.shape[0], weight.shape[1] // 3
-    blocks = masks[0].shape[1]
-
-    def by_core(index, count):
-        flip = jnp.broadcast_to(c, (count, HD)) == 1
-        return jnp.where(flip, index[1], index[0]), jnp.where(flip, index[0], index[1])
-
-    for turn in range(2):
-        column = x if turn == 0 else 1 - x
+    blocks = mask.shape[1]
+    ids = segments[...]
+    digits = [lax.shift_right_logical(ids, 7).astype(F32), (ids & 127).astype(F32)]
+    asked = mask[...].astype(F32)
+    if blocks < HD:
+        asked = jnp.concatenate([asked, jnp.zeros((2, HD - blocks), F32)], axis=1)
+    rest = [asked] + [d[:, HD * i : HD * i + HD] for d in digits for i in range(2)]
+    rest.append(jnp.zeros((rows - 16, HD), F32))
+    for turn, outs in enumerate((mine, theirs)):
+        column = table[6] if turn == 0 else 1 - table[6]
         for p in range(2):
-            out = outs[turn].at[p]
+            out = outs.at[p]
             wide = pl.multiple_of(WIDE * (2 * p + column), 128)
             tails = []
-            for i in range(3):
-                out[:, WIDE * i : WIDE * i + WIDE] = weight[
-                    :, pl.ds(pl.multiple_of(width * i + wide, 128), WIDE)
-                ]
-                slab = weight[:, width * i + 1024 + 128 * p : width * i + 1152 + 128 * p]
-                odd = jnp.broadcast_to(column, (rows, HD)) == 1
+            for i in range(4):
+                source = weight if i < 3 else queries
+                at = width * i if i < 3 else 0
+                slab = source[:, at + 1024 + 128 * p : at + 1152 + 128 * p].astype(F32)
+                odd = jnp.broadcast_to(column, (slab.shape[0], HD)) == 1
                 tails.append(jnp.where(odd, slab[:, HD:], slab[:, :HD]))
-            lanes[...] = jnp.zeros_like(lanes)
-            tokens = [q[:, pl.ds(wide, WIDE)].astype(F32) for q in queries]
-            slabs = [q[:, 1024 + 128 * p : 1152 + 128 * p].astype(F32) for q in queries]
-            odd = jnp.broadcast_to(column, (2, HD)) == 1
-            for h in range(6):
-                if h < 4:
-                    found = [t[:, HD * h : HD * h + HD] for t in tokens]
-                elif h == 4:
-                    found = [jnp.where(odd, t[:, HD:], t[:, :HD]) for t in slabs]
-                else:
-                    gap = jnp.zeros((2, HD - blocks), F32)
-                    found = [m[...].astype(F32) for m in masks]
-                    if blocks < HD:
-                        found = [jnp.concatenate([m, gap], axis=1) for m in found]
-                low, high = by_core(found, 2)
-                lanes[4 * h : 4 * h + 2, :] = low
-                lanes[4 * h + 2 : 4 * h + 4, :] = high
-            ids = [seg[...] for seg in segments]
-            digits = [[lax.shift_right_logical(v, 7), v & 127] for v in ids]
-            for d in range(2):
-                for part in range(2):
-                    found = [v[d][:, HD * part : HD * part + HD].astype(F32) for v in digits]
-                    low, high = by_core(found, 1)
-                    at = 24 + 2 * d + part
-                    lanes[at : at + 1, :] = low
-                    lanes[at + 4 : at + 5, :] = high
-            out[:, 3 * WIDE : 896] = jnp.concatenate(tails[1:], axis=1)
-            out[:, 896:] = jnp.concatenate([tails[0], lanes[...].astype(BF)], axis=1)
-
-
-def pack(spot, weight, *small):
-    rows = weight.shape[0]
-    shape = jax.ShapeDtypeStruct((2, rows, 1024), BF)
+                if i < 3:
+                    out[:, WIDE * i : WIDE * i + WIDE] = weight[
+                        :, pl.ds(pl.multiple_of(at + wide, 128), WIDE)
+                    ]
+            out[:, 3 * WIDE : 896] = jnp.concatenate(tails[1:3], axis=1).astype(BF)
+            asking = queries[:, pl.ds(wide, WIDE)].astype(F32)
+            heads = [asking[:, HD * h : HD * h + HD] for h in range(4)] + [tails[3]]
+            lanes = jnp.concatenate(heads + rest, axis=0)
+            out[:, 896:] = jnp.concatenate([tails[0], lanes], axis=1).astype(BF)
+
+
+def pack(table, weight, queries, mask, segments):
+    shape = jax.ShapeDtypeStruct((2, weight.shape[0], 1024), BF)
     return pl.pallas_call(
         pack_kernel,
         out_shape=(shape, shape),
-        in_specs=[SMEM] + [VMEM] * (1 + len(small)),
-        out_specs=(VMEM, VMEM),
-        scratch_shapes=[pltpu.VMEM((rows, HD), F32)],
-    )(spot, weight, *small)
+        in_specs=[SMEM] + [VMEM] * 4,
+        out_specs=(VMEM,) * 2,
+        compiler_params=pltpu.CompilerParams(vmem_limit_bytes=8 * 1024 * 1024),
+    )(table, weight, queries, mask, segments)
+
+
+def load_kernel(table, *refs):
+    held, outs = refs[:4], refs[4:]
+    x, c, p = table[6], table[7], table[5]
+    own = jnp.broadcast_to(table[12], outs[0].shape) == 1
+    flip_c = jnp.broadcast_to(c, (16, 128)) == 1
+    flip_x = jnp.broadcast_to(x, (16, 128)) == 1
+    for a in range(2):
+        mine, mine_c, across, across_c = [h[pl.ds(p ^ a, 1)][0] for h in held]
+        out = outs[a]
+        out[...] = jnp.where(own, mine, across)
+        lanes = [part[:16, 896:] for part in (mine, mine_c, across, across_c)]
+        rows = []
+        for first, second in (lanes[:2], lanes[2:]):
+            rows.append((jnp.where(flip_c, second, first), jnp.where(flip_c, first, second)))
+        low = [jnp.where(flip_x, there, here) for here, there in zip(*rows)]
+        high = [jnp.where(flip_x, here, there) for here, there in zip(*rows)]
+        lane = lax.broadcasted_iota(jnp.int32, (16, 128), 1)
+        for j, found in enumerate(low + high):
+            out[16 * j : 16 * j + 16, 896:] = jnp.where(
+                lane < HD, out[16 * j : 16 * j + 16, 896:], found
+            )
+
+
+def load(table, *held):
+    rows = held[0].shape[1]
+    return pl.pallas_call(
+        load_kernel,
+        out_shape=(jax.ShapeDtypeStruct((rows, 1024), BF),) * 2,
+        in_specs=[SMEM] + [VMEM] * 4,
+        out_specs=(VMEM,) * 2,
+        compiler_params=pltpu.CompilerParams(vmem_limit_bytes=8 * 1024 * 1024),
+    )(table, *held)
 
 
 def norm_kernel(ways, table, gain, *refs):
@@ -153,33 +165,30 @@
     )(table, gain, *blocks)
 
 
-def prepare_kernel(table, own, *refs):
+def prepare_kernel(table, *refs):
     parts, (ids, tokens, asked) = refs[:-3], refs[-3:]
-    straight, first, core = table[12], table[13], table[7]
+    first, x, core, z = table[13], table[6], table[7], table[14]
     count = asked.shape[0]
     ids[...] = jnp.zeros_like(ids)
     tokens[...] = jnp.zeros_like(tokens)
-    flip = jnp.broadcast_to(core, (2, HD)) == 1
-    near = jnp.broadcast_to(straight, (32, HD)) == 1
-    for i in range(count // 2):
-        if i == 0:
-            lanes = own[:32, 960:].astype(F32)
-        else:
-            part, rows = i // 2, slice(0, 32)
-            if i > 1 and i % 2:
-                rows = slice(own.shape[0], own.shape[0] + 32)
-            here, there = parts[2 * part][rows, 960:], parts[2 * part + 1][rows, 960:]
-            lanes = jnp.where(near, here.astype(F32), there.astype(F32))
+    flip_c = jnp.broadcast_to(core, (2, HD)) == 1
+    flip_x = jnp.broadcast_to(x, (2, HD)) == 1
+    for turn, part in enumerate(parts):
+        lanes = part[:64, 896:].astype(F32)[:, HD:]
         for h in range(6):
-            found = jnp.where(flip, lanes[4 * h + 2 : 4 * h + 4], lanes[4 * h : 4 * h + 2])
-            if h < 5:
-                at = count * h + 2 * i
-                tokens[at : at + 2, HD * h : HD * h + HD] = found * 0.125
-            else:
-                asked[2 * i : 2 * i + 2, :] = found
-        for c in range(2):
-            marks = lanes[24 + 4 * c : 26 + 4 * c] * 128.0 + lanes[26 + 4 * c : 28 + 4 * c]
-            block = table[14 + 2 * i] // 2 * 2 + c - first
+            rows = [lanes[16 * j + 2 * h : 16 * j + 2 * h + 2] for j in range(4)]
+            low = jnp.where(flip_c, rows[1], rows[0])
+            high = jnp.where(flip_c, rows[3], rows[2])
+            for dx in range(2):
+                found = jnp.where(flip_x, low, high) if dx else jnp.where(flip_x, high, low)
+                at = 4 * turn + 2 * dx
+                if h < 5:
+                    tokens[count * h + at : count * h + at + 2, HD * h : HD * h + HD] = found * 0.125
+                else:
+                    asked[at : at + 2, :] = found
+        for j in range(4):
+            marks = lanes[16 * j + 12 : 16 * j + 14] * 128.0 + lanes[16 * j + 14 : 16 * j + 16]
+            block = 4 * (z ^ turn) + j - first
 
             @pl.when((block >= 0) & (block < 12))
             def _():
@@ -188,7 +197,7 @@
                 )
 
 
-def prepare(table, own, parts, count):
+def prepare(table, parts, count):
     return pl.pallas_call(
         prepare_kernel,
         out_shape=(
@@ -196,10 +205,10 @@
             jax.ShapeDtypeStruct((5 * count, GROUP), F32),
             jax.ShapeDtypeStruct((count, HD), F32),
         ),
-        in_specs=[SMEM] + [VMEM] * (1 + len(parts)),
+        in_specs=[SMEM] + [VMEM] * len(parts),
         out_specs=(VMEM,) * 3,
         compiler_params=pltpu.CompilerParams(vmem_limit_bytes=8 * 1024 * 1024),
-    )(table, own, *parts)
+    )(table, *parts)
 
 
 def encoder_kernel(n_parts, depth, places, *refs):
@@ -207,31 +216,10 @@
     ids = refs[6]
     parts = refs[7 : 7 + n_parts]
     memory, near, away, weight, residual, queries, keys, values = refs[7 + n_parts :]
-    x, straight = places[11], places[12]
-
-    def place_part(source, rows):
-        weight[pl.ds(pl.multiple_of(source * depth, 16), depth), :] = rows
-
-    for i in range(min(2, n_parts)):
-        place_part(places[14 + i], parts[i][...])
-    for turn in range((n_parts - 2) // 4):
-        came, traded, came_other, traded_other = parts[2 + 4 * turn : 6 + 4 * turn]
-        pieces = came.shape[0] // depth
-
-        def place_turn(mine, other):
-            for s in range(pieces):
-                rows = slice(s * depth, s * depth + depth)
-                at = 14 + 4 * turn + 2 * (s + 2 - pieces)
-                place_part(places[at], mine[rows, :])
-                place_part(places[at + 1], other[rows, :])
-
-        @pl.when(straight == 1)
-        def _():
-            place_turn(came, traded_other)
-
-        @pl.when(straight == 0)
-        def _():
-            place_turn(traded, came_other)
+    x = places[6]
+    for i, part in enumerate(parts):
+        row = pl.multiple_of(places[15 + i] * depth, 16)
+        weight[pl.ds(row, depth), :] = part[...] if len(part.shape) == 2 else part[pl.ds(places[5], 1)][0]
 
     for slab in range(3):
         values[:, 256 * slab + 128 : 256 * slab + 256] = jnp.ones((1536, 128), BF)
@@ -455,76 +443,64 @@
     group = 2 * p + x
     depth = qkv_weight.shape[0]
 
-    layers_route = [1 if i % 2 else -1 for i in range(layers)]
+    utts = lax.axis_size("utt")
+    moved = lax.axis_index("utt") % 2
+    direct = depth % 16 == 0 and layers == 4 and utts % 2 == 0
+    gain = norm_gain.reshape(1, -1)
+    table = [128 * (2 * x + c), 128 * (2 * x + 1 - c), 128 * (2 - 2 * x + c), 128 * (3 - 2 * x - c)]
+    table += [group, p, x, c]
+    table += [512 * (p - c + 1), 512 * (2 - p - c), 1024 * c, 0, x == moved, 4 * quarter - 4, z]
+    sources = [me, me ^ 1, me ^ 2, me ^ 3] if direct else [jnp.int32(0)]
+    for turn in (1, 2, 3) if direct else ():
+        column = 4 * (z ^ turn) + c
+        for side in (moved, 1 - moved):
+            sources += [column + 2 * side, (column ^ 1) + 2 * side]
+    table = scalars(table + sources + [4 * quarter, 4 * (quarter ^ 1), me])
+    base = 15 + len(sources)
+
+    steps = [1 if i % 2 else -1 for i in range(layers)]
     near_route = [
         (4 * i + j, 4 * (i + s) + j)
-        for i, s in enumerate(layers_route)
+        for i, s in enumerate(steps)
         for j in range(4)
         if 0 <= i + s < layers
     ]
+    near = send(stem, near_route)
     pair = swap(stem, n, 4)
-    near = send(stem, near_route)
-    stem_x = swap(stem, n, 2)
-    utts = lax.axis_size("utt")
-    straight = (c == lax.axis_index("utt") % 2).astype(jnp.int32)
-    gain = norm_gain.reshape(1, -1)
-    direct = depth % 16 == 0 and layers == 4 and utts % 2 == 0
-    table = [128 * (2 * x + c), 128 * (2 * x + 1 - c), 128 * (2 - 2 * x + c), 128 * (3 - 2 * x - c)]
-    table += [group, p != k, x, c]
-    table += [512 * (p - c + 1), 512 * (2 - p - c), 1024 * c, x, straight, 4 * quarter - 4]
-    sources = [me ^ m for m in range(n)] if direct else [jnp.int32(0)]
-    table = scalars(table + sources + [4 * quarter, 4 * (quarter ^ 1), me])
-    base = 14 + len(sources)
     if direct:
-        carriers = [(u, d) for u in range(utts) for d in range(n) if d % 2 == u % 2]
-
-        def carry(block, turn_u, turn_d):
-            route = [(u * n + d, (u ^ turn_u) * n + (d ^ turn_d)) for u, d in carriers]
-            return lax.ppermute(block, ("utt", "tm"), route)
-
-        inside = [d for d in range(n) if d // 4 in (1, 2)]
-        far = send(after(stem, pair, near), [(d, d ^ 8) for d in inside])
-        small = [dec_queries, stretch_mask, segment_ids.reshape(1, -1)]
-        both = [part for piece in small for part in (piece, swap(piece, n, 1))]
-        mine, theirs = pack(table, qkv_weight, *both)
-        across = carry(after(theirs, stem_x), 0, 2)
-        stem_c = swap(stem, n, 1)
-        own_layer = norm_layer(table, gain, [stem, stem_c, stem_x, swap(stem_x, n, 1)])
-        ready = [
-            jnp.concatenate(
-                [
-                    lax.dynamic_slice_in_dim(mine, p ^ a, 1, 0),
-                    lax.dynamic_slice_in_dim(across, p ^ a, 1, 0),
-                ]
-            ).reshape(2 * depth, 1024)
-            for a in range(2)
-        ]
-        own_part = lax.dynamic_index_in_dim(mine, p, 0, keepdims=False)
-        pair_x = swap(after(pair, across), n, 2)
-        here = {0: lax.dynamic_index_in_dim(across, p, 0, keepdims=False)}
-        here[3] = carry(after(ready[1], far), 0, 12)
-        here[2] = carry(after(ready[0], here[3], own_layer[0]), 0, 8)
-        halo = jnp.where((z == 1) | (z == 2), near, far)
+        def trade(block):
+            return lax.ppermute(block, "utt", [(u, u ^ 1) for u in range(utts)])
+
+        mine, theirs = pack(
+            table, qkv_weight, dec_queries, stretch_mask, segment_ids.reshape(1, -1)
+        )
+        across = swap(theirs, n, 2)
+        mine_c, across_c = swap(mine, n, 1), swap(across, n, 1)
+        stem_x = swap(after(stem, across), n, 2)
+        relayed = swap(after(near, pair), n, 4)
+        ready = load(table, mine, mine_c, across, across_c)
+        here = {turn: swap(ready[turn % 2], n, 4 * turn) for turn in (3, 2, 1)}
+        own_layer = norm_layer(
+            table, gain, [stem, swap(stem, n, 1), stem_x, swap(stem_x, n, 1)]
+        )
+        pair_x = swap(after(pair, stem_x), n, 2)
+        halo = jnp.where((z == 1) | (z == 2), near, relayed)
         halo_x = swap(after(halo, pair_x), n, 2)
         pair_layer = norm_layer(table, gain, [pair, swap(pair, n, 1), pair_x, swap(pair_x, n, 1)])
-        here[1] = carry(after(ready[1], here[2], pair_layer[0]), 0, 4)
-        aside = [(d, d ^ 1) for d in range(n) if d % 2 == d // 8]
-        halo_layer = norm_layer(table, gain, [halo, send(halo, aside), halo_x, send(halo_x, aside)])
-        traded, came_other, traded_other = {}, {}, {}
-        hold = []
-        for turn in (0, 3, 2, 1):
-            traded[turn] = carry(after(here[turn], *hold), 1, 0)
-            hold = [traded[turn]]
-            came_other[turn] = carry(here[turn], 0, 1)
-            route = [(u * n + (d ^ 1), u * n + d) for u, d in carriers]
-            traded_other[turn] = lax.ppermute(traded[turn], ("utt", "tm"), route)
-        weights = [own_part, swap(own_part, n, 1)]
-        for turn in range(4):
-            weights += [here[turn], traded[turn], came_other[turn], traded_other[turn]]
-        came = [part for turn in range(4) for part in (here[turn], came_other[turn])]
-        ids, tokens, asked = prepare(table, own_part, came, n)
+        halo_layer = norm_layer(table, gain, [halo, swap(halo, n, 1), halo_x, swap(halo_x, n, 1)])
+        traded = {3: trade(here[3])}
+        traded[2] = trade(after(here[2], traded[3]))
+        traded[1] = trade(after(here[1], traded[2]))
+        ids, tokens, asked = prepare(table, [ready[0], here[1], here[2], here[3]], n)
+        weights = [mine, mine_c, across, across_c]
+        for turn in (1, 2, 3):
+            for part in (here[turn], traded[turn]):
+                last = part is traded[1]
+                beside = after(part, own_layer[0], pair_layer[0], ids) if last else part
+                weights += [part, swap(beside, n, 1)]
         layered = [own_layer, pair_layer, halo_layer]
     else:
+        stem_x = swap(stem, n, 2)
         far = swap(near, n, 4)
         left = jnp.where(p == 0, near, far)
         right = jnp.where(p == 0, far, near)
@@ -561,7 +537,6 @@
 
     partial = cross_partial(base, table, tokens, asked, held, swap(held, n, 1))
     owned = [partial[0]] + [swap(partial[i], n, 8 * i) for i in range(1, n // 8)]
-    stay, leave = after(stay, partial[0]), after(leave, partial[0])
 
     pieces = []
     for turn, rows in enumerate((stay, leave)):

time: 119 us -> 93.6 us (0.79)
  starting transfers between devices: 56 us -> 32.9 us
  Pallas kernels: 24.7 us -> 22.4 us
  waiting for transfers between devices: 29.6 us -> 31 us
  local copies, waits for them, and re-layouts: 6.1 us -> 4.84 us
    ppermute x16 -> x3, starting transfers between devices: 28.7 us -> 4.56 us  [trade(): return lax.ppermute(block, 'utt', [(u, u ^ 1) for u in range(utts)])]
    ppermute x25 -> x33, waiting for transfers between devices: 15.4 us -> 25.4 us  [send(): return lax.ppermute(block, 'tm', route)]
    ppermute x16 -> x3, waiting for transfers between devices: 14.2 us -> 5.61 us  [trade(): return lax.ppermute(block, 'utt', [(u, u ^ 1) for u in range(utts)])]
    pallas_call x1, Pallas kernels: 2.38 us -> 0.94 us  [pack(): pl.pallas_call(pack_kernel, out_shape=(shape, shape), in_specs=[SMEM] + [...]
    ppermute x25 -> x33, starting transfers between devices: 27.2 us -> 28.3 us  [send(): return lax.ppermute(block, 'tm', route)]
    unnamed x28 -> x12, local copies, waits for them, and re-layouts: 2.79 us -> 3.1 us
  transfers between devices with their start and end apart: 41 -> 36, of which waited for: 10 -> 9; matrix products, arithmetic and copies ran while one was open for 3% -> 2% of each run, Pallas kernels for 8% -> 9%
where the time goes in v7:
time: 93.6 us; the launch traced here: 93.4 us
  starting transfers between devices  32.9 us (35%)
  waiting for transfers between devices  31 us (33%)
  Pallas kernels  22.4 us (24%)
  local copies, waits for them, and re-layouts  4.84 us (5%)
  other arithmetic  1.16 us (1%)
  between operations  1.1 us (1%)
    ppermute x33, starting transfers between devices, send(): return lax.ppermute(block, 'tm', route)  28.3 us
    ppermute x33, waiting for transfers between devices, send(): return lax.ppermute(block, 'tm', route)  25.4 us
    pallas_call x1, Pallas kernels, encoder(): pl.pallas_call(functools.partial(encoder_kernel, len(parts), depth), out_...  13.3 us
    ppermute x3, waiting for transfers between devices, trade(): return lax.ppermute(block, 'utt', [(u, u ^ 1) for u in range(utts)])  5.61 us
    pallas_call x3, Pallas kernels, norm_layer(): pl.pallas_call(functools.partial(norm_kernel, len(blocks) // 4), out_shap...  4.71 us
    ppermute x3, starting transfers between devices, trade(): return lax.ppermute(block, 'utt', [(u, u ^ 1) for u in range(utts)])  4.56 us
    unnamed x12, local copies, waits for them, and re-layouts  3.1 us
  transfers between devices with their start and end apart: 36, of which 9 were waited for; matrix products, arithmetic and copies ran while one was open for 2% of the time, Pallas kernels for 9%

profile of v7, /device:TPU:0, one launch (start us, length us, event | category | flops | bytes accessed | tf_op | source)
XLA Modules:
  0.0 93.4 jit_solution(11262507681231629427)
XLA Ops:
  0.6 0.0 copy-start.1
  0.7 0.1 stack.136.table.places
  0.9 0.0 copy-start
  0.9 1.1 %copy-done = bf16[80,3840]{1,0:T(8,128)(2,1)S(1)} copy-done((bf16[80,3840]{1,0:T(8,128)(2,1)S(1)}, bf16[80,3840]{1,0:T(8,128)(2,1)}, u32[]{:S(2)}) %copy-start) | copy-done | bytes 614424
  1.9 0.7 copy-done.2
  2.6 0.7 copy-done.3
  3.3 0.7 copy-done.4
  4.0 0.9 %shard_map.77 = (bf16[2,80,1024]{2,1,0:T(8,128)(2,1)S(1)}, bf16[2,80,1024]{2,1,0:T(8,128)(2,1)S(1)}) custom-call(s32[34]{0:T(128)S(1)} %stack.136.table.places, bf16[80,3840]{1,0:T(8,128)(2,1)S(1)} %copy-done, bf16[2,1280]{1,0:T(2,128)(2,1)S(1)} %copy-done.2, s32[2,16]{1,0:T(2,128)S(1)} %copy-done.3, s32[1,128]{1,0:T(1,128)S(1)} %bitcast.33), custom_call_target="tpu_custom_call" | custom-call | tf_op jit(solution)/shard_map/pallas_call | solution.py:89
  4.9 3.0 %collective-permute-start.1 = (bf16[2,80,1024]{2,1,0:T(8,128)(2,1)S(1)}, bf16[2,80,1024]{2,1,0:T(8,128)(2,1)S(1)}, u32[]{:S(2)}, u32[]{:S(2)}) collective-permute-start(bf16[2,80,1024]{2,1,0:T(8,128)(2,1)S(1)} %get-tuple-element.31), channel_id=1, source_target_pairs={{0,2},{1,3},{2,0},{3,1},{4,6},{5,7},{6,4},{7,5},{8,10},{9,11},{10,... | collective-permute-start | bytes 983048 | tf_op jit(solution)/shard_map/ppermute | solution.py:21
  7.9 1.6 %collective-permute-start.4 = (bf16[128,1280]{1,0:T(8,128)(2,1)}, bf16[128,1280]{1,0:T(8,128)(2,1)S(1)}, u32[]{:S(2)}, u32[]{:S(2)}) collective-permute-start(bf16[128,1280]{1,0:T(8,128)(2,1)} %refs_0_.1), channel_id=1, source_target_pairs={{0,4},{1,5},{2,6},{3,7},{4,0},{5,1},{6,2},{7,3},{8,12},{9,13},{10,... | collective-permute-start | bytes 983048 | tf_op jit(solution)/shard_map/ppermute | solution.py:21
  9.5 1.4 %collective-permute-start.8 = (bf16[128,1280]{1,0:T(8,128)(2,1)}, bf16[128,1280]{1,0:T(8,128)(2,1)}, u32[]{:S(2)}, u32[]{:S(2)}) collective-permute-start(bf16[128,1280]{1,0:T(8,128)(2,1)} %refs_0_.1), channel_id=1, source_target_pairs={{4,8},{5,9},{6,10},{7,11},{8,4},{9,5},{10,6},{11,7},{20,24},{21,25... | collective-permute-start | bytes 983048 | tf_op jit(solution)/shard_map/ppermute | solution.py:21
  10.9 0.0 collective-permute-start.13
  10.9 4.7 %collective-permute-done.1.refs_2_.refs_9_ = bf16[2,80,1024]{2,1,0:T(8,128)(2,1)S(1)} collective-permute-done((bf16[2,80,1024]{2,1,0:T(8,128)(2,1)S(1)}, bf16[2,80,1024]{2,1,0:T(8,128)(2,1)S(1)}, u32[]{:S(2)}, u32[]{:S(2)}) %collective-permute-start.1) | collective-permute-done | bytes 327712 | tf_op jit(solution)/shard_map/ppermute | solution.py:21
  15.6 0.0 collective-permute-start.14
  15.6 1.7 %collective-permute-start.2 = (bf16[128,1280]{1,0:T(8,128)(2,1)}, bf16[128,1280]{1,0:T(8,128)(2,1)S(1)}, u32[]{:S(2)}, u32[]{:S(2)}) collective-permute-start(bf16[128,1280]{1,0:T(8,128)(2,1)} %refs_0_.1), channel_id=1, source_target_pairs={{0,2},{1,3},{2,0},{3,1},{4,6},{5,7},{6,4},{7,5},{8,10},{9,11},{10,... | collective-permute-start | bytes 983048 | tf_op jit(solution)/shard_map/ppermute | solution.py:21
  17.4 4.6 %collective-permute-start.9 = (bf16[128,1280]{1,0:T(8,128)(2,1)}, bf16[128,1280]{1,0:T(8,128)(2,1)}, u32[]{:S(2)}, u32[]{:S(2)}) collective-permute-start(bf16[128,1280]{1,0:T(8,128)(2,1)} %collective-permute-done.8), channel_id=1, source_target_pairs={{0,4},{1,5},{2,6},{3,7},{4,0},{5,1},{6,2},{7,3},{8,12},{9,13},{10,... | collective-permute-start | bytes 983048 | tf_op jit(solution)/shard_map/ppermute | solution.py:21
  22.0 0.0 collective-permute-done.14.refs_3_.refs_10_
  22.0 0.6 shard_map.81
  22.6 2.7 %collective-permute-start.17 = (bf16[80,1024]{1,0:T(8,128)(2,1)S(1)}, bf16[80,1024]{1,0:T(8,128)(2,1)S(1)}, u32[]{:S(2)}, u32[]{:S(2)}) collective-permute-start(bf16[80,1024]{1,0:T(8,128)(2,1)S(1)} %get-tuple-element.44), channel_id=1, source_target_pairs={{0,12},{1,13},{2,14},{3,15},{4,8},{5,9},{6,10},{7,11},{8,4},{9,5},... | collective-permute-start | bytes 491528 | tf_op jit(solution)/shard_map/ppermute | solution.py:21
  25.3 0.0 collective-permute-start
  25.3 0.0 collective-permute-start.16
  25.3 0.6 collective-permute-done.2.refs_2_
  26.0 1.7 %collective-permute-start.6 = (bf16[128,1280]{1,0:T(8,128)(2,1)S(1)}, bf16[128,1280]{1,0:T(8,128)(2,1)S(1)}, u32[]{:S(2)}, u32[]{:S(2)}) collective-permute-start(bf16[128,1280]{1,0:T(8,128)(2,1)S(1)} %collective-permute-done.4.refs_0_), channel_id=1, source_target_pairs={{0,2},{1,3},{2,0},{3,1},{4,6},{5,7},{6,4},{7,5},{8,10},{9,11},{10,... | collective-permute-start | bytes 983048 | tf_op jit(solution)/shard_map/ppermute | solution.py:21
  27.7 8.4 %collective-permute-done.17.refs_3_.refs_19_ = bf16[80,1024]{1,0:T(8,128)(2,1)S(1)} collective-permute-done((bf16[80,1024]{1,0:T(8,128)(2,1)S(1)}, bf16[80,1024]{1,0:T(8,128)(2,1)S(1)}, u32[]{:S(2)}, u32[]{:S(2)}) %collective-permute-start.17) | collective-permute-done | bytes 163872 | tf_op jit(solution)/shard_map/ppermute | solution.py:21
  36.1 1.5 %collective-permute-start.19 = (bf16[80,1024]{1,0:T(8,128)(2,1)S(1)}, bf16[80,1024]{1,0:T(8,128)(2,1)S(1)}, u32[]{:S(2)}, u32[]{:S(2)}) collective-permute-start(bf16[80,1024]{1,0:T(8,128)(2,1)S(1)} %collective-permute-done.17.refs_3_.refs_19_), channel_id=1, source_target_pairs={{0,16},{16,0},{1,17},{17,1},{2,18},{18,2},{3,19},{19,3},{4,20},{20... | collective-permute-start | bytes 491528 | tf_op jit(solution)/shard_map/ppermute | solution.py:472
  37.7 0.0 collective-permute-done.9
  37.7 1.0 %broadcast_select_fusion.refs_0_ = bf16[128,1280]{1,0:T(8,128)(2,1)S(1)} fusion(bf16[128,1280]{1,0:T(8,128)(2,1)} %collective-permute-done.8, bf16[128,1280]{1,0:T(8,128)(2,1)} %collective-permute-done.9, pred[]{:T(512)S(6)} %or.3), kind=kLoop, calls=%fused_computation | loop fusion | flops 163840 | bytes 983041 | tf_op jit(solution)/shard_map/jit(_where)/select_n | solution.py:487
  38.7 0.6 collective-permute-start.11
  39.3 0.0 collective-permute-done.16.refs_2_.refs_15_
  39.3 0.0 collective-permute-start.5
  39.3 2.1 %collective-permute-done.19.refs_21_ = bf16[80,1024]{1,0:T(8,128)(2,1)S(1)} collective-permute-done((bf16[80,1024]{1,0:T(8,128)(2,1)S(1)}, bf16[80,1024]{1,0:T(8,128)(2,1)S(1)}, u32[]{:S(2)}, u32[]{:S(2)}) %collective-permute-start.19) | collective-permute-done | bytes 163872 | tf_op jit(solution)/shard_map/ppermute | solution.py:472
  41.5 0.0 collective-permute-start.3
  41.5 1.5 %collective-permute-start.20 = (bf16[80,1024]{1,0:T(8,128)(2,1)S(1)}, bf16[80,1024]{1,0:T(8,128)(2,1)S(1)}, u32[]{:S(2)}, u32[]{:S(2)}) collective-permute-start(bf16[80,1024]{1,0:T(8,128)(2,1)S(1)} %collective-permute-done.16.refs_2_.refs_15_), channel_id=1, source_target_pairs={{0,16},{16,0},{1,17},{17,1},{2,18},{18,2},{3,19},{19,3},{4,20},{20... | collective-permute-start | bytes 491528 | tf_op jit(solution)/shard_map/ppermute | solution.py:472
  43.0 1.6 %collective-permute-done.15.refs_1_.refs_11_ = bf16[80,1024]{1,0:T(8,128)(2,1)S(1)} collective-permute-done((bf16[80,1024]{1,0:T(8,128)(2,1)S(1)}, bf16[80,1024]{1,0:T(8,128)(2,1)S(1)}, u32[]{:S(2)}, u32[]{:S(2)}) %collective-permute-start.15) | collective-permute-done | bytes 163872 | tf_op jit(solution)/shard_map/ppermute | solution.py:21
  44.6 3.5 %collective-permute-done.20.refs_17_ = bf16[80,1024]{1,0:T(8,128)(2,1)S(1)} collective-permute-done((bf16[80,1024]{1,0:T(8,128)(2,1)S(1)}, bf16[80,1024]{1,0:T(8,128)(2,1)S(1)}, u32[]{:S(2)}, u32[]{:S(2)}) %collective-permute-start.20) | collective-permute-done | bytes 163872 | tf_op jit(solution)/shard_map/ppermute | solution.py:472
  48.1 0.5 collective-permute-start.12
  48.6 1.5 %collective-permute-start.21 = (bf16[80,1024]{1,0:T(8,128)(2,1)S(1)}, bf16[80,1024]{1,0:T(8,128)(2,1)S(1)}, u32[]{:S(2)}, u32[]{:S(2)}) collective-permute-start(bf16[80,1024]{1,0:T(8,128)(2,1)S(1)} %collective-permute-done.15.refs_1_.refs_11_), channel_id=1, source_target_pairs={{0,16},{16,0},{1,17},{17,1},{2,18},{18,2},{3,19},{19,3},{4,20},{20... | collective-permute-start | bytes 491528 | tf_op jit(solution)/shard_map/ppermute | solution.py:472
  50.2 1.3 %shard_map.82 = (f32[8,1536]{1,0:T(8,128)S(1)}, f32[80,320]{1,0:T(8,128)S(1)}, f32[16,64]{1,0:T(8,128)S(1)}) custom-call(s32[34]{0:T(128)S(1)} %stack.136.table.places, bf16[80,1024]{1,0:T(8,128)(2,1)S(1)} %get-tuple-element.43.refs_0_, bf16[80,1024]{1,0:T(8,128)(2,1)S(1)} %collective-permute-done.15.refs_1_.refs_11_, ...), custom_call_target="tpu_custom_call" | custom-call | tf_op jit(solution)/shard_map/pallas_call | solution.py:201
  51.5 1.6 %shard_map.78 = (bf16[512,1280]{1,0:T(8,128)(2,1)S(1)}, bf16[512,320]{1,0:T(8,128)(2,1)S(1)}) custom-call(s32[34]{0:T(128)S(1)} %stack.136.table.places, f32[1,1280]{1,0:T(1,128)S(1)} %reshape.10.gain, bf16[128,1280]{1,0:T(8,128)(2,1)S(1)} %copy-done.1, bf16[128,1280]{1,0:T(8,128)(2,1)S(1)} %collective-permute-done.refs_1_, ...), custom_call_target="tpu_custom_call" | custom-call | tf_op jit(solution)/shard_map/pallas_call | solution.py:156
  53.1 0.8 collective-permute-start.23
  53.8 1.6 %shard_map.79 = (bf16[512,1280]{1,0:T(8,128)(2,1)S(1)}, bf16[512,320]{1,0:T(8,128)(2,1)S(1)}) custom-call(s32[34]{0:T(128)S(1)} %stack.136.table.places, f32[1,1280]{1,0:T(1,128)S(1)} %reshape.10.gain, bf16[128,1280]{1,0:T(8,128)(2,1)S(1)} %collective-permute-done.4.refs_0_, bf16[128,1280]{1,0:T(8,128)(2,1)S(1)} %collective-permute-done.5.refs_1_, ...), custom_call_target="tpu_custom_call" | custom-call | tf_op jit(solution)/shard_map/pallas_call | solution.py:156
  55.4 0.1 collective-permute-start.25
  55.5 0.5 collective-permute-start.26
  56.0 0.1 collective-permute-start.24
  56.1 0.4 collective-permute-start.22
  56.5 1.6 %shard_map.80 = (bf16[512,1280]{1,0:T(8,128)(2,1)S(1)}, bf16[512,320]{1,0:T(8,128)(2,1)S(1)}) custom-call(s32[34]{0:T(128)S(1)} %stack.136.table.places, f32[1,1280]{1,0:T(1,128)S(1)} %reshape.10.gain, bf16[128,1280]{1,0:T(8,128)(2,1)S(1)} %broadcast_select_fusion.refs_0_, bf16[128,1280]{1,0:T(8,128)(2,1)S(1)} %collective-permute-done.10.refs_1_, ...), custom_call_target="tpu_custom_call" | custom-call | tf_op jit(solution)/shard_map/pallas_call | solution.py:156
  58.2 13.3 %shard_map.83 = (bf16[512,320]{1,0:T(8,128)(2,1)S(1)}, bf16[256,320]{1,0:T(8,128)(2,1)S(1)}, bf16[256,320]{1,0:T(8,128)(2,1)S(1)}) custom-call(s32[34]{0:T(128)S(1)} %stack.136.table.places, bf16[512,1280]{1,0:T(8,128)(2,1)S(1)} %get-tuple-element.33.refs_0_, bf16[512,320]{1,0:T(8,128)(2,1)S(1)} %get-tuple-element.34.refs_1_, ...), custom_call_target="tpu_custom_call" | custom-call | tf_op jit(solution)/shard_map/pallas_call | solution.py:321
  71.4 0.6 collective-permute-start.28
  72.0 0.7 collective-permute-start.27
  72.7 2.6 %collective-permute-start.31 = (bf16[512,320]{1,0:T(8,128)(2,1)S(1)}, bf16[512,320]{1,0:T(8,128)(2,1)S(1)}, u32[]{:S(2)}, u32[]{:S(2)}) collective-permute-start(bf16[512,320]{1,0:T(8,128)(2,1)S(1)} %get-tuple-element.53.memory), channel_id=1, source_target_pairs={{0,1},{1,0},{2,3},{3,2},{4,5},{5,4},{6,7},{7,6},{8,9},{9,8},{10,11... | collective-permute-start | bytes 983048 | tf_op jit(solution)/shard_map/ppermute | solution.py:21
  75.3 4.0 %collective-permute-done.28 = bf16[256,320]{1,0:T(8,128)(2,1)S(1)} collective-permute-done((bf16[256,320]{1,0:T(8,128)(2,1)S(1)}, bf16[256,320]{1,0:T(8,128)(2,1)S(1)}, u32[]{:S(2)}, u32[]{:S(2)}) %collective-permute-start.28) | collective-permute-done | bytes 163872 | tf_op jit(solution)/shard_map/ppermute | solution.py:21
  79.3 0.1 collective-permute-start.30
  79.4 0.5 collective-permute-start.29
  80.0 1.3 %shard_map.84 = (f32[40,128]{1,0:T(8,128)S(1)}, f32[40,128]{1,0:T(8,128)S(1)}) custom-call(s32[34]{0:T(128)S(1)} %stack.136.table.places, f32[80,320]{1,0:T(8,128)S(1)} %get-tuple-element.51.tokens, f32[16,64]{1,0:T(8,128)S(1)} %get-tuple-element.52.asked, bf16[512,320]{1,0:T(8,128)(2,1)S(1)} %get-tuple-element.53.memory, ...), custom_call_target="tpu_custom_call" | custom-call | tf_op jit(solution)/shard_map/pallas_call | solution.py:386
  81.3 0.6 collective-permute-start.32
  81.9 4.1 %collective-permute-done.32.refs_1_ = f32[40,128]{1,0:T(8,128)S(1)} collective-permute-done((f32[40,128]{1,0:T(8,128)S(1)}, f32[40,128]{1,0:T(8,128)S(1)}, u32[]{:S(2)}, u32[]{:S(2)}) %collective-permute-start.32) | collective-permute-done | bytes 20512 | tf_op jit(solution)/shard_map/ppermute | solution.py:21
  86.0 0.2 shard_map.85
  86.2 0.6 collective-permute-start.33
  86.8 1.3 %collective-permute-start.34 = (bf16[2,384]{1,0:T(2,128)(2,1)S(1)}, bf16[2,384]{1,0:T(2,128)(2,1)S(1)}, u32[]{:S(2)}, u32[]{:S(2)}) collective-permute-start(bf16[2,384]{1,0:T(2,128)(2,1)S(1)} %get-tuple-element.58), channel_id=1, source_target_pairs={{0,4},{1,5},{2,6},{3,7},{4,0},{5,1},{6,2},{7,3},{8,12},{9,13},{10,... | collective-permute-start | bytes 4616 | tf_op jit(solution)/shard_map/ppermute | solution.py:21
  88.1 1.7 %collective-permute-start.35 = (bf16[2,384]{1,0:T(2,128)(2,1)S(1)}, bf16[2,384]{1,0:T(2,128)(2,1)S(1)}, u32[]{:S(2)}, u32[]{:S(2)}) collective-permute-start(bf16[2,384]{1,0:T(2,128)(2,1)S(1)} %get-tuple-element.59), channel_id=1, source_target_pairs={{0,6},{1,7},{2,4},{3,5},{4,2},{5,3},{6,0},{7,1},{8,14},{9,15},{10,... | collective-permute-start | bytes 4616 | tf_op jit(solution)/shard_map/ppermute | solution.py:21
  89.8 0.1 select_select_fusion
  90.0 0.8 concatenate.6
  90.9 1.7 %collective-permute-done.35 = bf16[2,384]{1,0:T(2,128)(2,1)S(1)} collective-permute-done((bf16[2,384]{1,0:T(2,128)(2,1)S(1)}, bf16[2,384]{1,0:T(2,128)(2,1)S(1)}, u32[]{:S(2)}, u32[]{:S(2)}) %collective-permute-start.35) | collective-permute-done | bytes 1568 | tf_op jit(solution)/shard_map/ppermute | solution.py:21
  92.7 0.7 concatenate.7
  (54 shorter events, 0.2 us)
Async XLA Ops:
  0.6 24.7 %copy-start.1 = (bf16[128,1280]{1,0:T(8,128)(2,1)S(1)}, bf16[128,1280]{1,0:T(8,128)(2,1)}, u32[]{:S(2)}) copy-start(bf16[128,1280]{1,0:T(8,128)(2,1)} %refs_0_.1) | copy-start | bytes 983044
  0.9 1.1 %copy-start = (bf16[80,3840]{1,0:T(8,128)(2,1)S(1)}, bf16[80,3840]{1,0:T(8,128)(2,1)}, u32[]{:S(2)}) copy-start(bf16[80,3840]{1,0:T(8,128)(2,1)} %weight.1) | copy-start | bytes 1843204
  1.9 0.7 copy-start.2
  2.6 0.7 copy-start.3
  3.3 0.7 copy-start.4
  4.0 46.2 %copy-start.5 = (f32[1280]{0:T(1024)S(1)}, f32[1280]{0:T(1024)}, u32[]{:S(2)}) copy-start(f32[1280]{0:T(1024)} %param.7) | copy-start | bytes 15364
  4.9 10.7 %collective-permute-start.1 = (bf16[2,80,1024]{2,1,0:T(8,128)(2,1)S(1)}, bf16[2,80,1024]{2,1,0:T(8,128)(2,1)S(1)}, u32[]{:S(2)}, u32[]{:S(2)}) collective-permute-start(bf16[2,80,1024]{2,1,0:T(8,128)(2,1)S(1)} %get-tuple-element.31), channel_id=1, source_target_pairs={{0,2},{1,3},{2,0},{3,1},{4,6},{5,7},{6,4},{7,5},{8,10},{9,11},{10,... | collective-permute-start | bytes 983048 | tf_op jit(solution)/shard_map/ppermute | solution.py:21
  7.9 9.5 %collective-permute-start.4 = (bf16[128,1280]{1,0:T(8,128)(2,1)}, bf16[128,1280]{1,0:T(8,128)(2,1)S(1)}, u32[]{:S(2)}, u32[]{:S(2)}) collective-permute-start(bf16[128,1280]{1,0:T(8,128)(2,1)} %refs_0_.1), channel_id=1, source_target_pairs={{0,4},{1,5},{2,6},{3,7},{4,0},{5,1},{6,2},{7,3},{8,12},{9,13},{10,... | collective-permute-start | bytes 983048 | tf_op jit(solution)/shard_map/ppermute | solution.py:21
  9.5 7.9 %collective-permute-start.8 = (bf16[128,1280]{1,0:T(8,128)(2,1)}, bf16[128,1280]{1,0:T(8,128)(2,1)}, u32[]{:S(2)}, u32[]{:S(2)}) collective-permute-start(bf16[128,1280]{1,0:T(8,128)(2,1)} %refs_0_.1), channel_id=1, source_target_pairs={{4,8},{5,9},{6,10},{7,11},{8,4},{9,5},{10,6},{11,7},{20,24},{21,25... | collective-permute-start | bytes 983048 | tf_op jit(solution)/shard_map/ppermute | solution.py:21
  10.9 11.1 %collective-permute-start.13 = (bf16[2,80,1024]{2,1,0:T(8,128)(2,1)S(1)}, bf16[2,80,1024]{2,1,0:T(8,128)(2,1)S(1)}, u32[]{:S(2)}, u32[]{:S(2)}) collective-permute-start(bf16[2,80,1024]{2,1,0:T(8,128)(2,1)S(1)} %get-tuple-element.42.refs_0_.refs_7_), channel_id=1, source_target_pairs={{0,1},{1,0},{2,3},{3,2},{4,5},{5,4},{6,7},{7,6},{8,9},{9,8},{10,11... | collective-permute-start | bytes 983048 | tf_op jit(solution)/shard_map/ppermute | solution.py:21
  15.6 6.4 %collective-permute-start.14 = (bf16[2,80,1024]{2,1,0:T(8,128)(2,1)S(1)}, bf16[2,80,1024]{2,1,0:T(8,128)(2,1)S(1)}, u32[]{:S(2)}, u32[]{:S(2)}) collective-permute-start(bf16[2,80,1024]{2,1,0:T(8,128)(2,1)S(1)} %collective-permute-done.1.refs_2_.refs_9_), channel_id=1, source_target_pairs={{0,1},{1,0},{2,3},{3,2},{4,5},{5,4},{6,7},{7,6},{8,9},{9,8},{10,11... | collective-permute-start | bytes 983048 | tf_op jit(solution)/shard_map/ppermute | solution.py:21
  15.6 10.3 %collective-permute-start.2 = (bf16[128,1280]{1,0:T(8,128)(2,1)}, bf16[128,1280]{1,0:T(8,128)(2,1)S(1)}, u32[]{:S(2)}, u32[]{:S(2)}) collective-permute-start(bf16[128,1280]{1,0:T(8,128)(2,1)} %refs_0_.1), channel_id=1, source_target_pairs={{0,2},{1,3},{2,0},{3,1},{4,6},{5,7},{6,4},{7,5},{8,10},{9,11},{10,... | collective-permute-start | bytes 983048 | tf_op jit(solution)/shard_map/ppermute | solution.py:21
  17.4 20.3 %collective-permute-start.9 = (bf16[128,1280]{1,0:T(8,128)(2,1)}, bf16[128,1280]{1,0:T(8,128)(2,1)}, u32[]{:S(2)}, u32[]{:S(2)}) collective-permute-start(bf16[128,1280]{1,0:T(8,128)(2,1)} %collective-permute-done.8), channel_id=1, source_target_pairs={{0,4},{1,5},{2,6},{3,7},{4,0},{5,1},{6,2},{7,3},{8,12},{9,13},{10,... | collective-permute-start | bytes 983048 | tf_op jit(solution)/shard_map/ppermute | solution.py:21
  22.6 13.5 %collective-permute-start.17 = (bf16[80,1024]{1,0:T(8,128)(2,1)S(1)}, bf16[80,1024]{1,0:T(8,128)(2,1)S(1)}, u32[]{:S(2)}, u32[]{:S(2)}) collective-permute-start(bf16[80,1024]{1,0:T(8,128)(2,1)S(1)} %get-tuple-element.44), channel_id=1, source_target_pairs={{0,12},{1,13},{2,14},{3,15},{4,8},{5,9},{6,10},{7,11},{8,4},{9,5},... | collective-permute-start | bytes 491528 | tf_op jit(solution)/shard_map/ppermute | solution.py:21
  25.3 16.2 %collective-permute-start = (bf16[128,1280]{1,0:T(8,128)(2,1)S(1)}, bf16[128,1280]{1,0:T(8,128)(2,1)S(1)}, u32[]{:S(2)}, u32[]{:S(2)}) collective-permute-start(bf16[128,1280]{1,0:T(8,128)(2,1)S(1)} %copy-done.1), channel_id=1, source_target_pairs={{0,1},{1,0},{2,3},{3,2},{4,5},{5,4},{6,7},{7,6},{8,9},{9,8},{10,11... | collective-permute-start | bytes 983048 | tf_op jit(solution)/shard_map/ppermute | solution.py:21
  25.3 14.0 %collective-permute-start.16 = (bf16[80,1024]{1,0:T(8,128)(2,1)S(1)}, bf16[80,1024]{1,0:T(8,128)(2,1)S(1)}, u32[]{:S(2)}, u32[]{:S(2)}) collective-permute-start(bf16[80,1024]{1,0:T(8,128)(2,1)S(1)} %get-tuple-element.43.refs_0_), channel_id=1, source_target_pairs={{0,8},{1,9},{2,10},{3,11},{4,12},{5,13},{6,14},{7,15},{8,0},{9,1},... | collective-permute-start | bytes 491528 | tf_op jit(solution)/shard_map/ppermute | solution.py:21
  26.0 12.7 %collective-permute-start.6 = (bf16[128,1280]{1,0:T(8,128)(2,1)S(1)}, bf16[128,1280]{1,0:T(8,128)(2,1)S(1)}, u32[]{:S(2)}, u32[]{:S(2)}) collective-permute-start(bf16[128,1280]{1,0:T(8,128)(2,1)S(1)} %collective-permute-done.4.refs_0_), channel_id=1, source_target_pairs={{0,2},{1,3},{2,0},{3,1},{4,6},{5,7},{6,4},{7,5},{8,10},{9,11},{10,... | collective-permute-start | bytes 983048 | tf_op jit(solution)/shard_map/ppermute | solution.py:21
  36.1 5.3 %collective-permute-start.19 = (bf16[80,1024]{1,0:T(8,128)(2,1)S(1)}, bf16[80,1024]{1,0:T(8,128)(2,1)S(1)}, u32[]{:S(2)}, u32[]{:S(2)}) collective-permute-start(bf16[80,1024]{1,0:T(8,128)(2,1)S(1)} %collective-permute-done.17.refs_3_.refs_19_), channel_id=1, source_target_pairs={{0,16},{16,0},{1,17},{17,1},{2,18},{18,2},{3,19},{19,3},{4,20},{20... | collective-permute-start | bytes 491528 | tf_op jit(solution)/shard_map/ppermute | solution.py:472
  38.7 9.4 %collective-permute-start.11 = (bf16[128,1280]{1,0:T(8,128)(2,1)S(1)}, bf16[128,1280]{1,0:T(8,128)(2,1)S(1)}, u32[]{:S(2)}, u32[]{:S(2)}) collective-permute-start(bf16[128,1280]{1,0:T(8,128)(2,1)S(1)} %broadcast_select_fusion.refs_0_), channel_id=1, source_target_pairs={{0,2},{1,3},{2,0},{3,1},{4,6},{5,7},{6,4},{7,5},{8,10},{9,11},{10,... | collective-permute-start | bytes 983048 | tf_op jit(solution)/shard_map/ppermute | solution.py:21
  39.3 5.3 %collective-permute-start.15 = (bf16[80,1024]{1,0:T(8,128)(2,1)S(1)}, bf16[80,1024]{1,0:T(8,128)(2,1)S(1)}, u32[]{:S(2)}, u32[]{:S(2)}) collective-permute-start(bf16[80,1024]{1,0:T(8,128)(2,1)S(1)} %get-tuple-element.44), channel_id=1, source_target_pairs={{0,4},{1,5},{2,6},{3,7},{4,0},{5,1},{6,2},{7,3},{8,12},{9,13},{10,... | collective-permute-start | bytes 491528 | tf_op jit(solution)/shard_map/ppermute | solution.py:21
  39.3 9.3 %collective-permute-start.5 = (bf16[128,1280]{1,0:T(8,128)(2,1)S(1)}, bf16[128,1280]{1,0:T(8,128)(2,1)S(1)}, u32[]{:S(2)}, u32[]{:S(2)}) collective-permute-start(bf16[128,1280]{1,0:T(8,128)(2,1)S(1)} %collective-permute-done.4.refs_0_), channel_id=1, source_target_pairs={{0,1},{1,0},{2,3},{3,2},{4,5},{5,4},{6,7},{7,6},{8,9},{9,8},{10,11... | collective-permute-start | bytes 983048 | tf_op jit(solution)/shard_map/ppermute | solution.py:21
  41.5 8.7 %collective-permute-start.3 = (bf16[128,1280]{1,0:T(8,128)(2,1)S(1)}, bf16[128,1280]{1,0:T(8,128)(2,1)S(1)}, u32[]{:S(2)}, u32[]{:S(2)}) collective-permute-start(bf16[128,1280]{1,0:T(8,128)(2,1)S(1)} %collective-permute-done.2.refs_2_), channel_id=1, source_target_pairs={{0,1},{1,0},{2,3},{3,2},{4,5},{5,4},{6,7},{7,6},{8,9},{9,8},{10,11... | collective-permute-start | bytes 983048 | tf_op jit(solution)/shard_map/ppermute | solution.py:21
  41.5 6.6 %collective-permute-start.20 = (bf16[80,1024]{1,0:T(8,128)(2,1)S(1)}, bf16[80,1024]{1,0:T(8,128)(2,1)S(1)}, u32[]{:S(2)}, u32[]{:S(2)}) collective-permute-start(bf16[80,1024]{1,0:T(8,128)(2,1)S(1)} %collective-permute-done.16.refs_2_.refs_15_), channel_id=1, source_target_pairs={{0,16},{16,0},{1,17},{17,1},{2,18},{18,2},{3,19},{19,3},{4,20},{20... | collective-permute-start | bytes 491528 | tf_op jit(solution)/shard_map/ppermute | solution.py:472
  44.6 8.4 %collective-permute-start.7 = (bf16[128,1280]{1,0:T(8,128)(2,1)S(1)}, bf16[128,1280]{1,0:T(8,128)(2,1)S(1)}, u32[]{:S(2)}, u32[]{:S(2)}) collective-permute-start(bf16[128,1280]{1,0:T(8,128)(2,1)S(1)} %collective-permute-done.6.refs_2_), channel_id=1, source_target_pairs={{0,1},{1,0},{2,3},{3,2},{4,5},{5,4},{6,7},{7,6},{8,9},{9,8},{10,11... | collective-permute-start | bytes 983048 | tf_op jit(solution)/shard_map/ppermute | solution.py:21
  48.1 7.9 %collective-permute-start.10 = (bf16[128,1280]{1,0:T(8,128)(2,1)S(1)}, bf16[128,1280]{1,0:T(8,128)(2,1)S(1)}, u32[]{:S(2)}, u32[]{:S(2)}) collective-permute-start(bf16[128,1280]{1,0:T(8,128)(2,1)S(1)} %broadcast_select_fusion.refs_0_), channel_id=1, source_target_pairs={{0,1},{1,0},{2,3},{3,2},{4,5},{5,4},{6,7},{7,6},{8,9},{9,8},{10,11... | collective-permute-start | bytes 983048 | tf_op jit(solution)/shard_map/ppermute | solution.py:21
  48.1 8.0 %collective-permute-start.12 = (bf16[128,1280]{1,0:T(8,128)(2,1)S(1)}, bf16[128,1280]{1,0:T(8,128)(2,1)S(1)}, u32[]{:S(2)}, u32[]{:S(2)}) collective-permute-start(bf16[128,1280]{1,0:T(8,128)(2,1)S(1)} %collective-permute-done.11.refs_2_), channel_id=1, source_target_pairs={{0,1},{1,0},{2,3},{3,2},{4,5},{5,4},{6,7},{7,6},{8,9},{9,8},{10,11... | collective-permute-start | bytes 983048 | tf_op jit(solution)/shard_map/ppermute | solution.py:21
  48.6 6.8 %collective-permute-start.21 = (bf16[80,1024]{1,0:T(8,128)(2,1)S(1)}, bf16[80,1024]{1,0:T(8,128)(2,1)S(1)}, u32[]{:S(2)}, u32[]{:S(2)}) collective-permute-start(bf16[80,1024]{1,0:T(8,128)(2,1)S(1)} %collective-permute-done.15.refs_1_.refs_11_), channel_id=1, source_target_pairs={{0,16},{16,0},{1,17},{17,1},{2,18},{18,2},{3,19},{19,3},{4,20},{20... | collective-permute-start | bytes 491528 | tf_op jit(solution)/shard_map/ppermute | solution.py:472
  50.1 5.4 %collective-permute-start.18 = (bf16[80,1024]{1,0:T(8,128)(2,1)S(1)}, bf16[80,1024]{1,0:T(8,128)(2,1)S(1)}, u32[]{:S(2)}, u32[]{:S(2)}) collective-permute-start(bf16[80,1024]{1,0:T(8,128)(2,1)S(1)} %collective-permute-done.15.refs_1_.refs_11_), channel_id=1, source_target_pairs={{0,1},{1,0},{2,3},{3,2},{4,5},{5,4},{6,7},{7,6},{8,9},{9,8},{10,11... | collective-permute-start | bytes 491528 | tf_op jit(solution)/shard_map/ppermute | solution.py:21
  53.1 5.0 %collective-permute-start.23 = (bf16[80,1024]{1,0:T(8,128)(2,1)S(1)}, bf16[80,1024]{1,0:T(8,128)(2,1)S(1)}, u32[]{:S(2)}, u32[]{:S(2)}) collective-permute-start(bf16[80,1024]{1,0:T(8,128)(2,1)S(1)} %collective-permute-done.16.refs_2_.refs_15_), channel_id=1, source_target_pairs={{0,1},{1,0},{2,3},{3,2},{4,5},{5,4},{6,7},{7,6},{8,9},{9,8},{10,11... | collective-permute-start | bytes 491528 | tf_op jit(solution)/shard_map/ppermute | solution.py:21
  55.4 2.7 %collective-permute-start.25 = (bf16[80,1024]{1,0:T(8,128)(2,1)S(1)}, bf16[80,1024]{1,0:T(8,128)(2,1)S(1)}, u32[]{:S(2)}, u32[]{:S(2)}) collective-permute-start(bf16[80,1024]{1,0:T(8,128)(2,1)S(1)} %collective-permute-done.17.refs_3_.refs_19_), channel_id=1, source_target_pairs={{0,1},{1,0},{2,3},{3,2},{4,5},{5,4},{6,7},{7,6},{8,9},{9,8},{10,11... | collective-permute-start | bytes 491528 | tf_op jit(solution)/shard_map/ppermute | solution.py:21
  55.5 2.6 %collective-permute-start.26 = (bf16[80,1024]{1,0:T(8,128)(2,1)S(1)}, bf16[80,1024]{1,0:T(8,128)(2,1)S(1)}, u32[]{:S(2)}, u32[]{:S(2)}) collective-permute-start(bf16[80,1024]{1,0:T(8,128)(2,1)S(1)} %collective-permute-done.19.refs_21_), channel_id=1, source_target_pairs={{0,1},{1,0},{2,3},{3,2},{4,5},{5,4},{6,7},{7,6},{8,9},{9,8},{10,11... | collective-permute-start | bytes 491528 | tf_op jit(solution)/shard_map/ppermute | solution.py:21
  56.0 2.1 %collective-permute-start.24 = (bf16[80,1024]{1,0:T(8,128)(2,1)S(1)}, bf16[80,1024]{1,0:T(8,128)(2,1)S(1)}, u32[]{:S(2)}, u32[]{:S(2)}) collective-permute-start(bf16[80,1024]{1,0:T(8,128)(2,1)S(1)} %collective-permute-done.20.refs_17_), channel_id=1, source_target_pairs={{0,1},{1,0},{2,3},{3,2},{4,5},{5,4},{6,7},{7,6},{8,9},{9,8},{10,11... | collective-permute-start | bytes 491528 | tf_op jit(solution)/shard_map/ppermute | solution.py:21
  56.1 2.0 %collective-permute-start.22 = (bf16[80,1024]{1,0:T(8,128)(2,1)S(1)}, bf16[80,1024]{1,0:T(8,128)(2,1)S(1)}, u32[]{:S(2)}, u32[]{:S(2)}) collective-permute-start(bf16[80,1024]{1,0:T(8,128)(2,1)S(1)} %collective-permute-done.21.refs_13_), channel_id=1, source_target_pairs={{0,1},{1,0},{2,3},{3,2},{4,5},{5,4},{6,7},{7,6},{8,9},{9,8},{10,11... | collective-permute-start | bytes 491528 | tf_op jit(solution)/shard_map/ppermute | solution.py:21
  71.4 7.8 %collective-permute-start.28 = (bf16[256,320]{1,0:T(8,128)(2,1)S(1)}, bf16[256,320]{1,0:T(8,128)(2,1)S(1)}, u32[]{:S(2)}, u32[]{:S(2)}) collective-permute-start(bf16[256,320]{1,0:T(8,128)(2,1)S(1)} %get-tuple-element.50), channel_id=1, source_target_pairs={{0,2},{1,6},{2,0},{3,4},{4,3},{5,7},{6,1},{7,5},{8,10},{9,14},{10,... | collective-permute-start | bytes 491528 | tf_op jit(solution)/shard_map/ppermute | solution.py:21
  72.0 7.3 %collective-permute-start.27 = (bf16[256,320]{1,0:T(8,128)(2,1)S(1)}, bf16[256,320]{1,0:T(8,128)(2,1)S(1)}, u32[]{:S(2)}, u32[]{:S(2)}) collective-permute-start(bf16[256,320]{1,0:T(8,128)(2,1)S(1)} %get-tuple-element.49), channel_id=1, source_target_pairs={{0,0},{1,4},{2,2},{3,6},{4,1},{5,5},{6,3},{7,7},{8,8},{9,12},{10,1... | collective-permute-start | bytes 491528 | tf_op jit(solution)/shard_map/ppermute | solution.py:21
  72.7 7.2 %collective-permute-start.31 = (bf16[512,320]{1,0:T(8,128)(2,1)S(1)}, bf16[512,320]{1,0:T(8,128)(2,1)S(1)}, u32[]{:S(2)}, u32[]{:S(2)}) collective-permute-start(bf16[512,320]{1,0:T(8,128)(2,1)S(1)} %get-tuple-element.53.memory), channel_id=1, source_target_pairs={{0,1},{1,0},{2,3},{3,2},{4,5},{5,4},{6,7},{7,6},{8,9},{9,8},{10,11... | collective-permute-start | bytes 983048 | tf_op jit(solution)/shard_map/ppermute | solution.py:21
  79.3 10.5 %collective-permute-start.30 = (bf16[128,320]{1,0:T(8,128)(2,1)S(1)}, bf16[128,320]{1,0:T(8,128)(2,1)S(1)}, u32[]{:S(2)}, u32[]{:S(2)}) collective-permute-start(bf16[128,320]{1,0:T(8,128)(2,1)S(1)} %constant_dynamic-slice_fusion), channel_id=1, source_target_pairs={{0,1},{1,0},{2,3},{3,2},{4,5},{5,4},{6,7},{7,6},{8,9},{9,8},{10,11... | collective-permute-start | bytes 245768 | tf_op jit(solution)/shard_map/ppermute | solution.py:21
  79.4 10.4 %collective-permute-start.29 = (bf16[128,320]{1,0:T(8,128)(2,1)S(1)}, bf16[128,320]{1,0:T(8,128)(2,1)S(1)}, u32[]{:S(2)}, u32[]{:S(2)}) collective-permute-start(bf16[128,320]{1,0:T(8,128)(2,1)S(1)} %constant_dynamic-slice_fusion.1), channel_id=1, source_target_pairs={{0,1},{1,0},{2,3},{3,2},{4,5},{5,4},{6,7},{7,6},{8,9},{9,8},{10,11... | collective-permute-start | bytes 245768 | tf_op jit(solution)/shard_map/ppermute | solution.py:21
  81.3 4.7 %collective-permute-start.32 = (f32[40,128]{1,0:T(8,128)S(1)}, f32[40,128]{1,0:T(8,128)S(1)}, u32[]{:S(2)}, u32[]{:S(2)}) collective-permute-start(f32[40,128]{1,0:T(8,128)S(1)} %get-tuple-element.55), channel_id=1, source_target_pairs={{0,8},{1,9},{2,10},{3,11},{4,12},{5,13},{6,14},{7,15},{8,0},{9,1},... | collective-permute-start | bytes 61448 | tf_op jit(solution)/shard_map/ppermute | solution.py:21
  86.2 4.6 %collective-permute-start.33 = (bf16[2,384]{1,0:T(2,128)(2,1)S(1)}, bf16[2,384]{1,0:T(2,128)(2,1)S(1)}, u32[]{:S(2)}, u32[]{:S(2)}) collective-permute-start(bf16[2,384]{1,0:T(2,128)(2,1)S(1)} %get-tuple-element.57), channel_id=1, source_target_pairs={{0,2},{1,3},{2,0},{3,1},{4,6},{5,7},{6,4},{7,5},{8,10},{9,11},{10,... | collective-permute-start | bytes 4616 | tf_op jit(solution)/shard_map/ppermute | solution.py:21
  86.8 4.0 %collective-permute-start.34 = (bf16[2,384]{1,0:T(2,128)(2,1)S(1)}, bf16[2,384]{1,0:T(2,128)(2,1)S(1)}, u32[]{:S(2)}, u32[]{:S(2)}) collective-permute-start(bf16[2,384]{1,0:T(2,128)(2,1)S(1)} %get-tuple-element.58), channel_id=1, source_target_pairs={{0,4},{1,5},{2,6},{3,7},{4,0},{5,1},{6,2},{7,3},{8,12},{9,13},{10,... | collective-permute-start | bytes 4616 | tf_op jit(solution)/shard_map/ppermute | solution.py:21
  88.1 4.5 %collective-permute-start.35 = (bf16[2,384]{1,0:T(2,128)(2,1)S(1)}, bf16[2,384]{1,0:T(2,128)(2,1)S(1)}, u32[]{:S(2)}, u32[]{:S(2)}) collective-permute-start(bf16[2,384]{1,0:T(2,128)(2,1)S(1)} %get-tuple-element.59), channel_id=1, source_target_pairs={{0,6},{1,7},{2,4},{3,5},{4,2},{5,3},{6,0},{7,1},{8,14},{9,15},{10,... | collective-permute-start | bytes 4616 | tf_op jit(solution)/shard_map/ppermute | solution.py:21

commit v8 on v7

--- a/solution.py
+++ b/solution.py
@@ -96,7 +96,7 @@
 
 
 def load_kernel(table, *refs):
-    held, outs = refs[:4], refs[4:]
+    held, outs, other = refs[:4], refs[4:6], refs[6]
     x, c, p = table[6], table[7], table[5]
     own = jnp.broadcast_to(table[12], outs[0].shape) == 1
     flip_c = jnp.broadcast_to(c, (16, 128)) == 1
@@ -105,6 +105,8 @@
         mine, mine_c, across, across_c = [h[pl.ds(p ^ a, 1)][0] for h in held]
         out = outs[a]
         out[...] = jnp.where(own, mine, across)
+        if a == 1:
+            other[mine.shape[0] :, :] = jnp.where(own, across, mine)
         lanes = [part[:16, 896:] for part in (mine, mine_c, across, across_c)]
         rows = []
         for first, second in (lanes[:2], lanes[2:]):
@@ -116,15 +118,17 @@
             out[16 * j : 16 * j + 16, 896:] = jnp.where(
                 lane < HD, out[16 * j : 16 * j + 16, 896:], found
             )
+        if a == 1:
+            other[: mine.shape[0], :] = out[...]
 
 
 def load(table, *held):
     rows = held[0].shape[1]
     return pl.pallas_call(
         load_kernel,
-        out_shape=(jax.ShapeDtypeStruct((rows, 1024), BF),) * 2,
+        out_shape=tuple(jax.ShapeDtypeStruct((rows * i, 1024), BF) for i in (1, 1, 2)),
         in_specs=[SMEM] + [VMEM] * 4,
-        out_specs=(VMEM,) * 2,
+        out_specs=(VMEM,) * 3,
         compiler_params=pltpu.CompilerParams(vmem_limit_bytes=8 * 1024 * 1024),
     )(table, *held)
 
@@ -217,9 +221,14 @@
     parts = refs[7 : 7 + n_parts]
     memory, near, away, weight, residual, queries, keys, values = refs[7 + n_parts :]
     x = places[6]
-    for i, part in enumerate(parts):
-        row = pl.multiple_of(places[15 + i] * depth, 16)
-        weight[pl.ds(row, depth), :] = part[...] if len(part.shape) == 2 else part[pl.ds(places[5], 1)][0]
+    at = 15
+    for part in parts:
+        rows = [part[pl.ds(places[5], 1)][0]] if len(part.shape) == 3 else [
+            part[s * depth : s * depth + depth, :] for s in range(part.shape[0] // depth)
+        ]
+        for found in rows:
+            weight[pl.ds(pl.multiple_of(places[at] * depth, 16), depth), :] = found
+            at += 1
 
     for slab in range(3):
         values[:, 256 * slab + 128 : 256 * slab + 256] = jnp.ones((1536, 128), BF)
@@ -419,18 +428,29 @@
     )(*parts)
 
 
-def gather_groups(pieces, group):
-    wide, tail = [], []
-    for g in range(4):
-        turn = group ^ g
-        piece = jnp.where(
-            turn < 2,
-            jnp.where(turn == 0, pieces[0], pieces[1]),
-            jnp.where(turn == 2, pieces[2], pieces[3]),
-        )
-        wide.append(piece[:, :WIDE])
-        tail.append(piece[:, WIDE:GROUP])
-    return jnp.concatenate(wide + tail, axis=1)
+def gather_kernel(side, rows, table, *refs):
+    pieces, out = refs[:4], refs[4]
+    high, x = table[side], table[6]
+    start = pl.multiple_of(rows * high, rows) if pieces[0].shape[0] > rows else 0
+    flip = jnp.broadcast_to(x, (rows, HD)) == 1
+    held = [piece[pl.ds(start, rows), :] for piece in pieces]
+    for i, piece in enumerate(held):
+        group = (2 * high + x) ^ i
+        out[:, pl.ds(pl.multiple_of(WIDE * group, 128), WIDE)] = piece[:, :WIDE]
+    for i in range(2):
+        first, second = [piece[:, WIDE:GROUP] for piece in held[2 * i : 2 * i + 2]]
+        tail = jnp.concatenate([jnp.where(flip, second, first), jnp.where(flip, first, second)], axis=1)
+        out[:, pl.ds(pl.multiple_of(1024 + 128 * (high ^ i), 128), 128)] = tail
+
+
+def gather_groups(side, rows, table, pieces):
+    return pl.pallas_call(
+        functools.partial(gather_kernel, side, rows),
+        out_shape=jax.ShapeDtypeStruct((rows, 1280), BF),
+        in_specs=[SMEM] + [VMEM] * 4,
+        out_specs=VMEM,
+        compiler_params=pltpu.CompilerParams(vmem_limit_bytes=4 * 1024 * 1024),
+    )(table, *pieces)
 
 
 def on_device(stem, norm_gain, qkv_weight, segment_ids, dec_queries, stretch_mask):
@@ -452,9 +472,11 @@
     table += [512 * (p - c + 1), 512 * (2 - p - c), 1024 * c, 0, x == moved, 4 * quarter - 4, z]
     sources = [me, me ^ 1, me ^ 2, me ^ 3] if direct else [jnp.int32(0)]
     for turn in (1, 2, 3) if direct else ():
-        column = 4 * (z ^ turn) + c
-        for side in (moved, 1 - moved):
-            sources += [column + 2 * side, (column ^ 1) + 2 * side]
+        column, sides = 4 * (z ^ turn) + c, (2 * moved, 2 - 2 * moved)
+        if turn == 1:
+            sources += [core + side for core in (column, column ^ 1) for side in sides]
+        else:
+            sources += [core + side for side in sides for core in (column, column ^ 1)]
     table = scalars(table + sources + [4 * quarter, 4 * (quarter ^ 1), me])
     base = 15 + len(sources)
 
@@ -474,28 +496,29 @@
         mine, theirs = pack(
             table, qkv_weight, dec_queries, stretch_mask, segment_ids.reshape(1, -1)
         )
-        across = swap(theirs, n, 2)
+        stem_x = swap(stem, n, 2)
+        across = swap(after(theirs, stem_x, pair, near), n, 2)
         mine_c, across_c = swap(mine, n, 1), swap(across, n, 1)
-        stem_x = swap(after(stem, across), n, 2)
         relayed = swap(after(near, pair), n, 4)
-        ready = load(table, mine, mine_c, across, across_c)
-        here = {turn: swap(ready[turn % 2], n, 4 * turn) for turn in (3, 2, 1)}
-        own_layer = norm_layer(
-            table, gain, [stem, swap(stem, n, 1), stem_x, swap(stem_x, n, 1)]
-        )
-        pair_x = swap(after(pair, stem_x), n, 2)
+        ready = load(table, mine, mine_c, after(across, relayed), across_c)
+        here = {turn: swap(ready[turn % 2], n, 4 * turn) for turn in (3, 2)}
+        here[1] = swap(ready[2], n, 4)
+        stem_c, stem_xc = [swap(after(part, here[3]), n, 1) for part in (stem, stem_x)]
+        own_layer = norm_layer(table, gain, [stem, stem_c, stem_x, stem_xc])
+        pair_x = swap(after(pair, across), n, 2)
         halo = jnp.where((z == 1) | (z == 2), near, relayed)
         halo_x = swap(after(halo, pair_x), n, 2)
-        pair_layer = norm_layer(table, gain, [pair, swap(pair, n, 1), pair_x, swap(pair_x, n, 1)])
+        pair_c, pair_xc = [swap(after(part, here[3]), n, 1) for part in (pair, pair_x)]
+        pair_layer = norm_layer(table, gain, [pair, pair_c, pair_x, pair_xc])
         halo_layer = norm_layer(table, gain, [halo, swap(halo, n, 1), halo_x, swap(halo_x, n, 1)])
         traded = {3: trade(here[3])}
-        traded[2] = trade(after(here[2], traded[3]))
-        traded[1] = trade(after(here[1], traded[2]))
+        traded[2] = trade(after(here[2], here[1], traded[3]))
         ids, tokens, asked = prepare(table, [ready[0], here[1], here[2], here[3]], n)
         weights = [mine, mine_c, across, across_c]
-        for turn in (1, 2, 3):
+        weights += [here[1], swap(here[1], n, 1)]
+        for turn in (2, 3):
             for part in (here[turn], traded[turn]):
-                last = part is traded[1]
+                last = part is traded[2]
                 beside = after(part, own_layer[0], pair_layer[0], ids) if last else part
                 weights += [part, swap(beside, n, 1)]
         layered = [own_layer, pair_layer, halo_layer]
@@ -538,7 +561,7 @@
     partial = cross_partial(base, table, tokens, asked, held, swap(held, n, 1))
     owned = [partial[0]] + [swap(partial[i], n, 8 * i) for i in range(1, n // 8)]
 
-    pieces = []
+    got = []
     for turn, rows in enumerate((stay, leave)):
         route = [
             (
@@ -547,15 +570,12 @@
             )
             for d in range(n)
         ]
-        got = send(rows, route)
-        keep = lax.dynamic_slice_in_dim(got, 128 * c, 128, 0)
-        give = swap(lax.dynamic_slice_in_dim(got, 128 * (1 - c), 128, 0), n, 1)
-        pieces.append((keep, give))
-    memory = gather_groups([pieces[0][0], pieces[1][0], pieces[0][1], pieces[1][1]], 2 * c + x)
+        got.append(after(send(rows, route), owned[1]))
+    memory = gather_groups(7, 128, table, got + [swap(part, n, 1) for part in got])
 
     final = merge(owned)
     final = [final[0]] + [swap(final[i], n, 2 * i) for i in (1, 2, 3)]
-    cross_out = gather_groups(final, group)
+    cross_out = gather_groups(5, 2, table, final)
     return (memory, cross_out)
 
 

time: 93.6 us -> 95.6 us (1.021)
  waiting for transfers between devices: 31 us -> 34.7 us
  Pallas kernels: 22.4 us -> 25 us
  local copies, waits for them, and re-layouts: 4.84 us -> 3.21 us
  starting transfers between devices: 32.9 us -> 31.5 us
  other arithmetic: 1.16 us -> 0.04 us
    ppermute x33 -> x32, waiting for transfers between devices: 25.4 us -> 30.1 us  [send(): return lax.ppermute(block, 'tm', route)]
    pallas_call x1 -> x3, Pallas kernels: 0.59 us -> 3.2 us  [the longest x2 2.59 us: gather_groups(): pl.pallas_call(functools.partial(gather_kernel, side, rows), out_shape=ja...]
    concatenate x2 -> x0, local copies, waits for them, and re-layouts: 1.52 us -> none  [gather_groups(): return jnp.concatenate(wide + tail, axis=1)]
    ppermute x3 -> x2, starting transfers between devices: 4.56 us -> 3.04 us  [trade(): return lax.ppermute(block, 'utt', [(u, u ^ 1) for u in range(utts)])]
    ppermute x3 -> x2, waiting for transfers between devices: 5.61 us -> 4.58 us  [trade(): return lax.ppermute(block, 'utt', [(u, u ^ 1) for u in range(utts)])]
    select_n x1, other arithmetic: 1.01 us -> 0.04 us  [on_device(): halo = jnp.where((z == 1) | (z == 2), near, relayed)]
    ppermute x33 -> x32, starting transfers between devices: 28.3 us -> 28.5 us  [send(): return lax.ppermute(block, 'tm', route)]
  transfers between devices with their start and end apart: 36 -> 34, of which waited for: 9 -> 11; matrix products, arithmetic and copies ran while one was open for 2% -> 0% of each run, Pallas kernels for 9% -> 11%
where the time goes in v8:
time: 95.6 us; the launch traced here: 95.4 us
  waiting for transfers between devices  34.7 us (36%)
  starting transfers between devices  31.5 us (33%)
  Pallas kernels  25 us (26%)
  local copies, waits for them, and re-layouts  3.21 us (3%)
    ppermute x32, waiting for transfers between devices, send(): return lax.ppermute(block, 'tm', route)  30.1 us
    ppermute x32, starting transfers between devices, send(): return lax.ppermute(block, 'tm', route)  28.5 us
    pallas_call x1, Pallas kernels, encoder(): pl.pallas_call(functools.partial(encoder_kernel, len(parts), depth), out_...  13.3 us
    pallas_call x3, Pallas kernels, norm_layer(): pl.pallas_call(functools.partial(norm_kernel, len(blocks) // 4), out_shap...  4.72 us
    ppermute x2, waiting for transfers between devices, trade(): return lax.ppermute(block, 'utt', [(u, u ^ 1) for u in range(utts)])  4.58 us
    unnamed x12, local copies, waits for them, and re-layouts  3.1 us
    ppermute x2, starting transfers between devices, trade(): return lax.ppermute(block, 'utt', [(u, u ^ 1) for u in range(utts)])  3.04 us
    pallas_call x2, Pallas kernels, gather_groups(): pl.pallas_call(functools.partial(gather_kernel, side, rows), out_shape=ja...  2.59 us
  transfers between devices with their start and end apart: 34, of which 11 were waited for; matrix products, arithmetic and copies ran while one was open for 0% of the time, Pallas kernels for 11%

profile of v8, /device:TPU:0, one launch (start us, length us, event | category | flops | bytes accessed | tf_op | source)
XLA Modules:
  0.0 95.4 jit_solution(12032722371330393846)
XLA Ops:
  0.6 3.1 %collective-permute-start.2 = (bf16[128,1280]{1,0:T(8,128)(2,1)}, bf16[128,1280]{1,0:T(8,128)(2,1)S(1)}, u32[]{:S(2)}, u32[]{:S(2)}) collective-permute-start(bf16[128,1280]{1,0:T(8,128)(2,1)} %refs_0_.1), channel_id=1, source_target_pairs={{0,4},{1,5},{2,6},{3,7},{4,0},{5,1},{6,2},{7,3},{8,12},{9,13},{10,... | collective-permute-start | bytes 983048 | tf_op jit(solution)/shard_map/ppermute | solution.py:21
  3.7 1.5 %collective-permute-start.1 = (bf16[128,1280]{1,0:T(8,128)(2,1)}, bf16[128,1280]{1,0:T(8,128)(2,1)S(1)}, u32[]{:S(2)}, u32[]{:S(2)}) collective-permute-start(bf16[128,1280]{1,0:T(8,128)(2,1)} %refs_0_.1), channel_id=1, source_target_pairs={{0,2},{1,3},{2,0},{3,1},{4,6},{5,7},{6,4},{7,5},{8,10},{9,11},{10,... | collective-permute-start | bytes 983048 | tf_op jit(solution)/shard_map/ppermute | solution.py:21
  5.2 0.7 collective-permute-start.3
  6.0 0.1 stack.136.table.places
  6.1 0.0 copy-start
  6.1 1.1 %copy-done = bf16[80,3840]{1,0:T(8,128)(2,1)S(1)} copy-done((bf16[80,3840]{1,0:T(8,128)(2,1)S(1)}, bf16[80,3840]{1,0:T(8,128)(2,1)}, u32[]{:S(2)}) %copy-start) | copy-done | bytes 614424
  7.2 0.7 copy-done.2
  7.9 0.7 copy-done.3
  8.6 0.7 copy-done.4
  9.2 0.9 shard_map.77
  10.2 1.5 %collective-permute-done.2.refs_0_ = bf16[128,1280]{1,0:T(8,128)(2,1)S(1)} collective-permute-done((bf16[128,1280]{1,0:T(8,128)(2,1)}, bf16[128,1280]{1,0:T(8,128)(2,1)S(1)}, u32[]{:S(2)}, u32[]{:S(2)}) %collective-permute-start.2) | collective-permute-done | bytes 327712 | tf_op jit(solution)/shard_map/ppermute | solution.py:21
  11.6 1.5 %collective-permute-done.1.refs_2_ = bf16[128,1280]{1,0:T(8,128)(2,1)S(1)} collective-permute-done((bf16[128,1280]{1,0:T(8,128)(2,1)}, bf16[128,1280]{1,0:T(8,128)(2,1)S(1)}, u32[]{:S(2)}, u32[]{:S(2)}) %collective-permute-start.1) | collective-permute-done | bytes 327712 | tf_op jit(solution)/shard_map/ppermute | solution.py:21
  13.1 1.5 %collective-permute-start.4 = (bf16[2,80,1024]{2,1,0:T(8,128)(2,1)S(1)}, bf16[2,80,1024]{2,1,0:T(8,128)(2,1)S(1)}, u32[]{:S(2)}, u32[]{:S(2)}) collective-permute-start(bf16[2,80,1024]{2,1,0:T(8,128)(2,1)S(1)} %get-tuple-element.40), channel_id=1, source_target_pairs={{0,2},{1,3},{2,0},{3,1},{4,6},{5,7},{6,4},{7,5},{8,10},{9,11},{10,... | collective-permute-start | bytes 983048 | tf_op jit(solution)/shard_map/ppermute | solution.py:21
  14.6 3.6 %collective-permute-start.5 = (bf16[128,1280]{1,0:T(8,128)(2,1)S(1)}, bf16[128,1280]{1,0:T(8,128)(2,1)S(1)}, u32[]{:S(2)}, u32[]{:S(2)}) collective-permute-start(bf16[128,1280]{1,0:T(8,128)(2,1)S(1)} %collective-permute-done.3), channel_id=1, source_target_pairs={{0,4},{1,5},{2,6},{3,7},{4,0},{5,1},{6,2},{7,3},{8,12},{9,13},{10,... | collective-permute-start | bytes 983048 | tf_op jit(solution)/shard_map/ppermute | solution.py:21
  18.1 0.0 collective-permute-start
  18.1 3.2 %collective-permute-done.4.refs_2_.refs_9_ = bf16[2,80,1024]{2,1,0:T(8,128)(2,1)S(1)} collective-permute-done((bf16[2,80,1024]{2,1,0:T(8,128)(2,1)S(1)}, bf16[2,80,1024]{2,1,0:T(8,128)(2,1)S(1)}, u32[]{:S(2)}, u32[]{:S(2)}) %collective-permute-start.4) | collective-permute-done | bytes 327712 | tf_op jit(solution)/shard_map/ppermute | solution.py:21
  21.4 0.0 collective-permute-start.6
  21.4 3.0 %collective-permute-done.5 = bf16[128,1280]{1,0:T(8,128)(2,1)S(1)} collective-permute-done((bf16[128,1280]{1,0:T(8,128)(2,1)S(1)}, bf16[128,1280]{1,0:T(8,128)(2,1)S(1)}, u32[]{:S(2)}, u32[]{:S(2)}) %collective-permute-start.5) | collective-permute-done | bytes 327712 | tf_op jit(solution)/shard_map/ppermute | solution.py:21
  24.4 1.5 %collective-permute-start.11 = (bf16[128,1280]{1,0:T(8,128)(2,1)S(1)}, bf16[128,1280]{1,0:T(8,128)(2,1)S(1)}, u32[]{:S(2)}, u32[]{:S(2)}) collective-permute-start(bf16[128,1280]{1,0:T(8,128)(2,1)S(1)} %collective-permute-done.2.refs_0_), channel_id=1, source_target_pairs={{0,2},{1,3},{2,0},{3,1},{4,6},{5,7},{6,4},{7,5},{8,10},{9,11},{10,... | collective-permute-start | bytes 983048 | tf_op jit(solution)/shard_map/ppermute | solution.py:21
  25.9 0.6 shard_map.78
  26.5 1.8 %collective-permute-start.16 = (bf16[160,1024]{1,0:T(8,128)(2,1)S(1)}, bf16[160,1024]{1,0:T(8,128)(2,1)S(1)}, u32[]{:S(2)}, u32[]{:S(2)}) collective-permute-start(bf16[160,1024]{1,0:T(8,128)(2,1)S(1)} %get-tuple-element.57), channel_id=1, source_target_pairs={{0,4},{1,5},{2,6},{3,7},{4,0},{5,1},{6,2},{7,3},{8,12},{9,13},{10,... | collective-permute-start | bytes 983048 | tf_op jit(solution)/shard_map/ppermute | solution.py:21
  28.3 1.2 %collective-permute-start.17 = (bf16[80,1024]{1,0:T(8,128)(2,1)S(1)}, bf16[80,1024]{1,0:T(8,128)(2,1)S(1)}, u32[]{:S(2)}, u32[]{:S(2)}) collective-permute-start(bf16[80,1024]{1,0:T(8,128)(2,1)S(1)} %get-tuple-element.56.refs_0_), channel_id=1, source_target_pairs={{0,8},{1,9},{2,10},{3,11},{4,12},{5,13},{6,14},{7,15},{8,0},{9,1},... | collective-permute-start | bytes 491528 | tf_op jit(solution)/shard_map/ppermute | solution.py:21
  29.5 1.5 %collective-permute-start.7 = (bf16[80,1024]{1,0:T(8,128)(2,1)S(1)}, bf16[80,1024]{1,0:T(8,128)(2,1)S(1)}, u32[]{:S(2)}, u32[]{:S(2)}) collective-permute-start(bf16[80,1024]{1,0:T(8,128)(2,1)S(1)} %get-tuple-element.43), channel_id=1, source_target_pairs={{0,12},{1,13},{2,14},{3,15},{4,8},{5,9},{6,10},{7,11},{8,4},{9,5},... | collective-permute-start | bytes 491528 | tf_op jit(solution)/shard_map/ppermute | solution.py:21
  31.0 0.7 collective-permute-done.11.refs_2_
  31.7 1.5 %collective-permute-start.14 = (bf16[128,1280]{1,0:T(8,128)(2,1)S(1)}, bf16[128,1280]{1,0:T(8,128)(2,1)S(1)}, u32[]{:S(2)}, u32[]{:S(2)}) collective-permute-start(bf16[128,1280]{1,0:T(8,128)(2,1)S(1)} %broadcast_select_fusion.refs_0_), channel_id=1, source_target_pairs={{0,2},{1,3},{2,0},{3,1},{4,6},{5,7},{6,4},{7,5},{8,10},{9,11},{10,... | collective-permute-start | bytes 983048 | tf_op jit(solution)/shard_map/ppermute | solution.py:21
  33.2 12.2 %collective-permute-done.7.refs_3_.refs_17_ = bf16[80,1024]{1,0:T(8,128)(2,1)S(1)} collective-permute-done((bf16[80,1024]{1,0:T(8,128)(2,1)S(1)}, bf16[80,1024]{1,0:T(8,128)(2,1)S(1)}, u32[]{:S(2)}, u32[]{:S(2)}) %collective-permute-start.7) | collective-permute-done | bytes 163872 | tf_op jit(solution)/shard_map/ppermute | solution.py:21
  45.4 0.0 collective-permute-start.12
  45.4 1.5 %collective-permute-start.20 = (bf16[80,1024]{1,0:T(8,128)(2,1)S(1)}, bf16[80,1024]{1,0:T(8,128)(2,1)S(1)}, u32[]{:S(2)}, u32[]{:S(2)}) collective-permute-start(bf16[80,1024]{1,0:T(8,128)(2,1)S(1)} %collective-permute-done.7.refs_3_.refs_17_), channel_id=1, source_target_pairs={{0,16},{16,0},{1,17},{17,1},{2,18},{18,2},{3,19},{19,3},{4,20},{20... | collective-permute-start | bytes 491528 | tf_op jit(solution)/shard_map/ppermute | solution.py:494
  46.9 0.2 collective-permute-start.10
  47.1 0.0 collective-permute-done.16.refs_1_.refs_11_
  47.1 0.3 collective-permute-start.9
  47.4 4.6 %collective-permute-done.20.refs_19_ = bf16[80,1024]{1,0:T(8,128)(2,1)S(1)} collective-permute-done((bf16[80,1024]{1,0:T(8,128)(2,1)S(1)}, bf16[80,1024]{1,0:T(8,128)(2,1)S(1)}, u32[]{:S(2)}, u32[]{:S(2)}) %collective-permute-start.20) | collective-permute-done | bytes 163872 | tf_op jit(solution)/shard_map/ppermute | solution.py:494
  52.0 0.0 collective-permute-start.8
  52.0 0.0 collective-permute-done.14.refs_2_
  52.0 0.5 collective-permute-start.13
  52.5 0.1 collective-permute-start.15
  52.6 0.0 collective-permute-done.10.refs_1_
  52.6 1.5 %collective-permute-start.21 = (bf16[80,1024]{1,0:T(8,128)(2,1)S(1)}, bf16[80,1024]{1,0:T(8,128)(2,1)S(1)}, u32[]{:S(2)}, u32[]{:S(2)}) collective-permute-start(bf16[80,1024]{1,0:T(8,128)(2,1)S(1)} %collective-permute-done.17.refs_2_.refs_13_), channel_id=1, source_target_pairs={{0,16},{16,0},{1,17},{17,1},{2,18},{18,2},{3,19},{19,3},{4,20},{20... | collective-permute-start | bytes 491528 | tf_op jit(solution)/shard_map/ppermute | solution.py:494
  54.1 0.2 collective-permute-start.18
  54.3 1.3 %shard_map.82 = (f32[8,1536]{1,0:T(8,128)S(1)}, f32[80,320]{1,0:T(8,128)S(1)}, f32[16,64]{1,0:T(8,128)S(1)}) custom-call(s32[34]{0:T(128)S(1)} %stack.136.table.places, bf16[80,1024]{1,0:T(8,128)(2,1)S(1)} %get-tuple-element.56.refs_0_, bf16[160,1024]{1,0:T(8,128)(2,1)S(1)} %collective-permute-done.16.refs_1_.refs_11_, ...), custom_call_target="tpu_custom_call" | custom-call | tf_op jit(solution)/shard_map/pallas_call | solution.py:205
  55.6 1.6 %shard_map.80 = (bf16[512,1280]{1,0:T(8,128)(2,1)S(1)}, bf16[512,320]{1,0:T(8,128)(2,1)S(1)}) custom-call(s32[34]{0:T(128)S(1)} %stack.136.table.places, f32[1,1280]{1,0:T(1,128)S(1)} %reshape.10.gain, bf16[128,1280]{1,0:T(8,128)(2,1)S(1)} %collective-permute-done.2.refs_0_, bf16[128,1280]{1,0:T(8,128)(2,1)S(1)} %collective-permute-done.10.refs_1_, ...), custom_call_target="tpu_custom_call" | custom-call | tf_op jit(solution)/shard_map/pallas_call | solution.py:160
  57.2 0.6 collective-permute-start.19
  57.8 1.6 %shard_map.79 = (bf16[512,1280]{1,0:T(8,128)(2,1)S(1)}, bf16[512,320]{1,0:T(8,128)(2,1)S(1)}) custom-call(s32[34]{0:T(128)S(1)} %stack.136.table.places, f32[1,1280]{1,0:T(1,128)S(1)} %reshape.10.gain, bf16[128,1280]{1,0:T(8,128)(2,1)S(1)} %copy-done.1, bf16[128,1280]{1,0:T(8,128)(2,1)S(1)} %collective-permute-done.8.refs_1_, ...), custom_call_target="tpu_custom_call" | custom-call | tf_op jit(solution)/shard_map/pallas_call | solution.py:160
  59.4 0.1 collective-permute-start.23
  59.5 0.5 collective-permute-start.24
  60.0 0.1 collective-permute-start.22
  60.1 1.6 %shard_map.81 = (bf16[512,1280]{1,0:T(8,128)(2,1)S(1)}, bf16[512,320]{1,0:T(8,128)(2,1)S(1)}) custom-call(s32[34]{0:T(128)S(1)} %stack.136.table.places, f32[1,1280]{1,0:T(1,128)S(1)} %reshape.10.gain, bf16[128,1280]{1,0:T(8,128)(2,1)S(1)} %broadcast_select_fusion.refs_0_, bf16[128,1280]{1,0:T(8,128)(2,1)S(1)} %collective-permute-done.13.refs_1_, ...), custom_call_target="tpu_custom_call" | custom-call | tf_op jit(solution)/shard_map/pallas_call | solution.py:160
  61.7 13.3 %shard_map.83 = (bf16[512,320]{1,0:T(8,128)(2,1)S(1)}, bf16[256,320]{1,0:T(8,128)(2,1)S(1)}, bf16[256,320]{1,0:T(8,128)(2,1)S(1)}) custom-call(s32[34]{0:T(128)S(1)} %stack.136.table.places, bf16[512,1280]{1,0:T(8,128)(2,1)S(1)} %get-tuple-element.46.refs_0_, bf16[512,320]{1,0:T(8,128)(2,1)S(1)} %get-tuple-element.47.refs_1_, ...), custom_call_target="tpu_custom_call" | custom-call | tf_op jit(solution)/shard_map/pallas_call | solution.py:330
  75.0 0.5 collective-permute-start.26
  75.5 0.5 collective-permute-start.28
  76.0 0.7 collective-permute-start.25
  76.7 0.1 collective-permute-done.26.beside
  76.8 1.3 %shard_map.84 = (f32[40,128]{1,0:T(8,128)S(1)}, f32[40,128]{1,0:T(8,128)S(1)}) custom-call(s32[34]{0:T(128)S(1)} %stack.136.table.places, f32[80,320]{1,0:T(8,128)S(1)} %get-tuple-element.62.tokens, f32[16,64]{1,0:T(8,128)S(1)} %get-tuple-element.63.asked, bf16[512,320]{1,0:T(8,128)(2,1)S(1)} %get-tuple-element.64.memory, ...), custom_call_target="tpu_custom_call" | custom-call | tf_op jit(solution)/shard_map/pallas_call | solution.py:395
  78.2 1.7 %collective-permute-start.27 = (f32[40,128]{1,0:T(8,128)S(1)}, f32[40,128]{1,0:T(8,128)S(1)}, u32[]{:S(2)}, u32[]{:S(2)}) collective-permute-start(f32[40,128]{1,0:T(8,128)S(1)} %get-tuple-element.65), channel_id=1, source_target_pairs={{0,8},{1,9},{2,10},{3,11},{4,12},{5,13},{6,14},{7,15},{8,0},{9,1},... | collective-permute-start | bytes 61448 | tf_op jit(solution)/shard_map/ppermute | solution.py:21
  79.9 3.4 %collective-permute-done.28.refs_1_ = bf16[256,320]{1,0:T(8,128)(2,1)S(1)} collective-permute-done((bf16[256,320]{1,0:T(8,128)(2,1)S(1)}, bf16[256,320]{1,0:T(8,128)(2,1)S(1)}, u32[]{:S(2)}, u32[]{:S(2)}) %collective-permute-start.28) | collective-permute-done | bytes 163872 | tf_op jit(solution)/shard_map/ppermute | solution.py:21
  83.3 0.8 collective-permute-start.30
  84.1 0.0 collective-permute-start.29
  84.1 0.2 shard_map.86
  84.3 1.6 %collective-permute-start.31 = (bf16[2,384]{1,0:T(2,128)(2,1)S(1)}, bf16[2,384]{1,0:T(2,128)(2,1)S(1)}, u32[]{:S(2)}, u32[]{:S(2)}) collective-permute-start(bf16[2,384]{1,0:T(2,128)(2,1)S(1)} %get-tuple-element.71), channel_id=1, source_target_pairs={{0,2},{1,3},{2,0},{3,1},{4,6},{5,7},{6,4},{7,5},{8,10},{9,11},{10,... | collective-permute-start | bytes 4616 | tf_op jit(solution)/shard_map/ppermute | solution.py:21
  85.9 2.4 %collective-permute-start.32 = (bf16[2,384]{1,0:T(2,128)(2,1)S(1)}, bf16[2,384]{1,0:T(2,128)(2,1)S(1)}, u32[]{:S(2)}, u32[]{:S(2)}) collective-permute-start(bf16[2,384]{1,0:T(2,128)(2,1)S(1)} %get-tuple-element.72), channel_id=1, source_target_pairs={{0,4},{1,5},{2,6},{3,7},{4,0},{5,1},{6,2},{7,3},{8,12},{9,13},{10,... | collective-permute-start | bytes 4616 | tf_op jit(solution)/shard_map/ppermute | solution.py:21
  88.3 1.5 %collective-permute-done.32.refs_2_ = bf16[2,384]{1,0:T(2,128)(2,1)S(1)} collective-permute-done((bf16[2,384]{1,0:T(2,128)(2,1)S(1)}, bf16[2,384]{1,0:T(2,128)(2,1)S(1)}, u32[]{:S(2)}, u32[]{:S(2)}) %collective-permute-start.32) | collective-permute-done | bytes 1568 | tf_op jit(solution)/shard_map/ppermute | solution.py:21
  89.8 2.9 %collective-permute-done.33.refs_3_ = bf16[2,384]{1,0:T(2,128)(2,1)S(1)} collective-permute-done((bf16[2,384]{1,0:T(2,128)(2,1)S(1)}, bf16[2,384]{1,0:T(2,128)(2,1)S(1)}, u32[]{:S(2)}, u32[]{:S(2)}) %collective-permute-start.33) | collective-permute-done | bytes 1568 | tf_op jit(solution)/shard_map/ppermute | solution.py:21
  92.8 1.2 %shard_map.87 = bf16[2,1280]{1,0:T(2,128)(2,1)} custom-call(s32[34]{0:T(128)S(1)} %stack.136.table.places, bf16[2,384]{1,0:T(2,128)(2,1)S(1)} %get-tuple-element.70.refs_0_, bf16[2,384]{1,0:T(2,128)(2,1)S(1)} %collective-permute-done.31.refs_1_, bf16[2,384]{1,0:T(2,128)(2,1)S(1)} %collective-permute-done.32.refs_2_, ...), custom_call_target="tpu_custom_call" | custom-call | tf_op jit(solution)/shard_map/pallas_call | solution.py:447
  94.0 1.4 %shard_map.85 = bf16[128,1280]{1,0:T(8,128)(2,1)} custom-call(s32[34]{0:T(128)S(1)} %stack.136.table.places, bf16[256,320]{1,0:T(8,128)(2,1)S(1)} %collective-permute-done.25.refs_0_, bf16[256,320]{1,0:T(8,128)(2,1)S(1)} %collective-permute-done.28.refs_1_, bf16[256,320]{1,0:T(8,128)(2,1)S(1)} %collective-permute-done.29.refs_2_, ...), custom_call_target="tpu_custom_call" | custom-call | tf_op jit(solution)/shard_map/pallas_call | solution.py:447
  (30 shorter events, 0.1 us)
Async XLA Ops:
  0.6 11.0 %collective-permute-start.2 = (bf16[128,1280]{1,0:T(8,128)(2,1)}, bf16[128,1280]{1,0:T(8,128)(2,1)S(1)}, u32[]{:S(2)}, u32[]{:S(2)}) collective-permute-start(bf16[128,1280]{1,0:T(8,128)(2,1)} %refs_0_.1), channel_id=1, source_target_pairs={{0,4},{1,5},{2,6},{3,7},{4,0},{5,1},{6,2},{7,3},{8,12},{9,13},{10,... | collective-permute-start | bytes 983048 | tf_op jit(solution)/shard_map/ppermute | solution.py:21
  3.7 9.4 %collective-permute-start.1 = (bf16[128,1280]{1,0:T(8,128)(2,1)}, bf16[128,1280]{1,0:T(8,128)(2,1)S(1)}, u32[]{:S(2)}, u32[]{:S(2)}) collective-permute-start(bf16[128,1280]{1,0:T(8,128)(2,1)} %refs_0_.1), channel_id=1, source_target_pairs={{0,2},{1,3},{2,0},{3,1},{4,6},{5,7},{6,4},{7,5},{8,10},{9,11},{10,... | collective-permute-start | bytes 983048 | tf_op jit(solution)/shard_map/ppermute | solution.py:21
  5.2 7.9 %collective-permute-start.3 = (bf16[128,1280]{1,0:T(8,128)(2,1)}, bf16[128,1280]{1,0:T(8,128)(2,1)S(1)}, u32[]{:S(2)}, u32[]{:S(2)}) collective-permute-start(bf16[128,1280]{1,0:T(8,128)(2,1)} %refs_0_.1), channel_id=1, source_target_pairs={{4,8},{5,9},{6,10},{7,11},{8,4},{9,5},{10,6},{11,7},{20,24},{21,25... | collective-permute-start | bytes 983048 | tf_op jit(solution)/shard_map/ppermute | solution.py:21
  6.1 1.1 %copy-start = (bf16[80,3840]{1,0:T(8,128)(2,1)S(1)}, bf16[80,3840]{1,0:T(8,128)(2,1)}, u32[]{:S(2)}) copy-start(bf16[80,3840]{1,0:T(8,128)(2,1)} %weight.1) | copy-start | bytes 1843204
  7.2 0.7 copy-start.2
  7.9 0.7 copy-start.3
  8.6 0.7 copy-start.4
  9.2 42.8 %copy-start.1 = (bf16[128,1280]{1,0:T(8,128)(2,1)S(1)}, bf16[128,1280]{1,0:T(8,128)(2,1)}, u32[]{:S(2)}) copy-start(bf16[128,1280]{1,0:T(8,128)(2,1)} %refs_0_.1) | copy-start | bytes 983044
  9.2 45.1 %copy-start.5 = (f32[1280]{0:T(1024)S(1)}, f32[1280]{0:T(1024)}, u32[]{:S(2)}) copy-start(f32[1280]{0:T(1024)} %param.7) | copy-start | bytes 15364
  13.1 8.3 %collective-permute-start.4 = (bf16[2,80,1024]{2,1,0:T(8,128)(2,1)S(1)}, bf16[2,80,1024]{2,1,0:T(8,128)(2,1)S(1)}, u32[]{:S(2)}, u32[]{:S(2)}) collective-permute-start(bf16[2,80,1024]{2,1,0:T(8,128)(2,1)S(1)} %get-tuple-element.40), channel_id=1, source_target_pairs={{0,2},{1,3},{2,0},{3,1},{4,6},{5,7},{6,4},{7,5},{8,10},{9,11},{10,... | collective-permute-start | bytes 983048 | tf_op jit(solution)/shard_map/ppermute | solution.py:21
  14.6 9.8 %collective-permute-start.5 = (bf16[128,1280]{1,0:T(8,128)(2,1)S(1)}, bf16[128,1280]{1,0:T(8,128)(2,1)S(1)}, u32[]{:S(2)}, u32[]{:S(2)}) collective-permute-start(bf16[128,1280]{1,0:T(8,128)(2,1)S(1)} %collective-permute-done.3), channel_id=1, source_target_pairs={{0,4},{1,5},{2,6},{3,7},{4,0},{5,1},{6,2},{7,3},{8,12},{9,13},{10,... | collective-permute-start | bytes 983048 | tf_op jit(solution)/shard_map/ppermute | solution.py:21
  18.1 7.7 %collective-permute-start = (bf16[2,80,1024]{2,1,0:T(8,128)(2,1)S(1)}, bf16[2,80,1024]{2,1,0:T(8,128)(2,1)S(1)}, u32[]{:S(2)}, u32[]{:S(2)}) collective-permute-start(bf16[2,80,1024]{2,1,0:T(8,128)(2,1)S(1)} %get-tuple-element.38.refs_0_.refs_7_), channel_id=1, source_target_pairs={{0,1},{1,0},{2,3},{3,2},{4,5},{5,4},{6,7},{7,6},{8,9},{9,8},{10,11... | collective-permute-start | bytes 983048 | tf_op jit(solution)/shard_map/ppermute | solution.py:21
  21.4 4.5 %collective-permute-start.6 = (bf16[2,80,1024]{2,1,0:T(8,128)(2,1)S(1)}, bf16[2,80,1024]{2,1,0:T(8,128)(2,1)S(1)}, u32[]{:S(2)}, u32[]{:S(2)}) collective-permute-start(bf16[2,80,1024]{2,1,0:T(8,128)(2,1)S(1)} %collective-permute-done.4.refs_2_.refs_9_), channel_id=1, source_target_pairs={{0,1},{1,0},{2,3},{3,2},{4,5},{5,4},{6,7},{7,6},{8,9},{9,8},{10,11... | collective-permute-start | bytes 983048 | tf_op jit(solution)/shard_map/ppermute | solution.py:21
  24.4 7.3 %collective-permute-start.11 = (bf16[128,1280]{1,0:T(8,128)(2,1)S(1)}, bf16[128,1280]{1,0:T(8,128)(2,1)S(1)}, u32[]{:S(2)}, u32[]{:S(2)}) collective-permute-start(bf16[128,1280]{1,0:T(8,128)(2,1)S(1)} %collective-permute-done.2.refs_0_), channel_id=1, source_target_pairs={{0,2},{1,3},{2,0},{3,1},{4,6},{5,7},{6,4},{7,5},{8,10},{9,11},{10,... | collective-permute-start | bytes 983048 | tf_op jit(solution)/shard_map/ppermute | solution.py:21
  26.5 20.6 %collective-permute-start.16 = (bf16[160,1024]{1,0:T(8,128)(2,1)S(1)}, bf16[160,1024]{1,0:T(8,128)(2,1)S(1)}, u32[]{:S(2)}, u32[]{:S(2)}) collective-permute-start(bf16[160,1024]{1,0:T(8,128)(2,1)S(1)} %get-tuple-element.57), channel_id=1, source_target_pairs={{0,4},{1,5},{2,6},{3,7},{4,0},{5,1},{6,2},{7,3},{8,12},{9,13},{10,... | collective-permute-start | bytes 983048 | tf_op jit(solution)/shard_map/ppermute | solution.py:21
  28.3 18.6 %collective-permute-start.17 = (bf16[80,1024]{1,0:T(8,128)(2,1)S(1)}, bf16[80,1024]{1,0:T(8,128)(2,1)S(1)}, u32[]{:S(2)}, u32[]{:S(2)}) collective-permute-start(bf16[80,1024]{1,0:T(8,128)(2,1)S(1)} %get-tuple-element.56.refs_0_), channel_id=1, source_target_pairs={{0,8},{1,9},{2,10},{3,11},{4,12},{5,13},{6,14},{7,15},{8,0},{9,1},... | collective-permute-start | bytes 491528 | tf_op jit(solution)/shard_map/ppermute | solution.py:21
  29.5 15.9 %collective-permute-start.7 = (bf16[80,1024]{1,0:T(8,128)(2,1)S(1)}, bf16[80,1024]{1,0:T(8,128)(2,1)S(1)}, u32[]{:S(2)}, u32[]{:S(2)}) collective-permute-start(bf16[80,1024]{1,0:T(8,128)(2,1)S(1)} %get-tuple-element.43), channel_id=1, source_target_pairs={{0,12},{1,13},{2,14},{3,15},{4,8},{5,9},{6,10},{7,11},{8,4},{9,5},... | collective-permute-start | bytes 491528 | tf_op jit(solution)/shard_map/ppermute | solution.py:21
  31.7 20.3 %collective-permute-start.14 = (bf16[128,1280]{1,0:T(8,128)(2,1)S(1)}, bf16[128,1280]{1,0:T(8,128)(2,1)S(1)}, u32[]{:S(2)}, u32[]{:S(2)}) collective-permute-start(bf16[128,1280]{1,0:T(8,128)(2,1)S(1)} %broadcast_select_fusion.refs_0_), channel_id=1, source_target_pairs={{0,2},{1,3},{2,0},{3,1},{4,6},{5,7},{6,4},{7,5},{8,10},{9,11},{10,... | collective-permute-start | bytes 983048 | tf_op jit(solution)/shard_map/ppermute | solution.py:21
  45.4 7.1 %collective-permute-start.12 = (bf16[128,1280]{1,0:T(8,128)(2,1)S(1)}, bf16[128,1280]{1,0:T(8,128)(2,1)S(1)}, u32[]{:S(2)}, u32[]{:S(2)}) collective-permute-start(bf16[128,1280]{1,0:T(8,128)(2,1)S(1)} %collective-permute-done.11.refs_2_), channel_id=1, source_target_pairs={{0,1},{1,0},{2,3},{3,2},{4,5},{5,4},{6,7},{7,6},{8,9},{9,8},{10,11... | collective-permute-start | bytes 983048 | tf_op jit(solution)/shard_map/ppermute | solution.py:21
  45.4 6.6 %collective-permute-start.20 = (bf16[80,1024]{1,0:T(8,128)(2,1)S(1)}, bf16[80,1024]{1,0:T(8,128)(2,1)S(1)}, u32[]{:S(2)}, u32[]{:S(2)}) collective-permute-start(bf16[80,1024]{1,0:T(8,128)(2,1)S(1)} %collective-permute-done.7.refs_3_.refs_17_), channel_id=1, source_target_pairs={{0,16},{16,0},{1,17},{17,1},{2,18},{18,2},{3,19},{19,3},{4,20},{20... | collective-permute-start | bytes 491528 | tf_op jit(solution)/shard_map/ppermute | solution.py:494
  46.9 5.7 %collective-permute-start.10 = (bf16[128,1280]{1,0:T(8,128)(2,1)S(1)}, bf16[128,1280]{1,0:T(8,128)(2,1)S(1)}, u32[]{:S(2)}, u32[]{:S(2)}) collective-permute-start(bf16[128,1280]{1,0:T(8,128)(2,1)S(1)} %collective-permute-done.2.refs_0_), channel_id=1, source_target_pairs={{0,1},{1,0},{2,3},{3,2},{4,5},{5,4},{6,7},{7,6},{8,9},{9,8},{10,11... | collective-permute-start | bytes 983048 | tf_op jit(solution)/shard_map/ppermute | solution.py:21
  47.1 7.0 %collective-permute-start.9 = (bf16[128,1280]{1,0:T(8,128)(2,1)S(1)}, bf16[128,1280]{1,0:T(8,128)(2,1)S(1)}, u32[]{:S(2)}, u32[]{:S(2)}) collective-permute-start(bf16[128,1280]{1,0:T(8,128)(2,1)S(1)} %collective-permute-done.1.refs_2_), channel_id=1, source_target_pairs={{0,1},{1,0},{2,3},{3,2},{4,5},{5,4},{6,7},{7,6},{8,9},{9,8},{10,11... | collective-permute-start | bytes 983048 | tf_op jit(solution)/shard_map/ppermute | solution.py:21
  52.0 5.2 %collective-permute-start.8 = (bf16[128,1280]{1,0:T(8,128)(2,1)S(1)}, bf16[128,1280]{1,0:T(8,128)(2,1)S(1)}, u32[]{:S(2)}, u32[]{:S(2)}) collective-permute-start(bf16[128,1280]{1,0:T(8,128)(2,1)S(1)} %copy-done.1), channel_id=1, source_target_pairs={{0,1},{1,0},{2,3},{3,2},{4,5},{5,4},{6,7},{7,6},{8,9},{9,8},{10,11... | collective-permute-start | bytes 983048 | tf_op jit(solution)/shard_map/ppermute | solution.py:21
  52.0 7.5 %collective-permute-start.13 = (bf16[128,1280]{1,0:T(8,128)(2,1)S(1)}, bf16[128,1280]{1,0:T(8,128)(2,1)S(1)}, u32[]{:S(2)}, u32[]{:S(2)}) collective-permute-start(bf16[128,1280]{1,0:T(8,128)(2,1)S(1)} %broadcast_select_fusion.refs_0_), channel_id=1, source_target_pairs={{0,1},{1,0},{2,3},{3,2},{4,5},{5,4},{6,7},{7,6},{8,9},{9,8},{10,11... | collective-permute-start | bytes 983048 | tf_op jit(solution)/shard_map/ppermute | solution.py:21
  52.5 7.5 %collective-permute-start.15 = (bf16[128,1280]{1,0:T(8,128)(2,1)S(1)}, bf16[128,1280]{1,0:T(8,128)(2,1)S(1)}, u32[]{:S(2)}, u32[]{:S(2)}) collective-permute-start(bf16[128,1280]{1,0:T(8,128)(2,1)S(1)} %collective-permute-done.14.refs_2_), channel_id=1, source_target_pairs={{0,1},{1,0},{2,3},{3,2},{4,5},{5,4},{6,7},{7,6},{8,9},{9,8},{10,11... | collective-permute-start | bytes 983048 | tf_op jit(solution)/shard_map/ppermute | solution.py:21
  52.6 6.8 %collective-permute-start.21 = (bf16[80,1024]{1,0:T(8,128)(2,1)S(1)}, bf16[80,1024]{1,0:T(8,128)(2,1)S(1)}, u32[]{:S(2)}, u32[]{:S(2)}) collective-permute-start(bf16[80,1024]{1,0:T(8,128)(2,1)S(1)} %collective-permute-done.17.refs_2_.refs_13_), channel_id=1, source_target_pairs={{0,16},{16,0},{1,17},{17,1},{2,18},{18,2},{3,19},{19,3},{4,20},{20... | collective-permute-start | bytes 491528 | tf_op jit(solution)/shard_map/ppermute | solution.py:494
  54.1 7.6 %collective-permute-start.18 = (bf16[160,1024]{1,0:T(8,128)(2,1)S(1)}, bf16[160,1024]{1,0:T(8,128)(2,1)S(1)}, u32[]{:S(2)}, u32[]{:S(2)}) collective-permute-start(bf16[160,1024]{1,0:T(8,128)(2,1)S(1)} %collective-permute-done.16.refs_1_.refs_11_), channel_id=1, source_target_pairs={{0,1},{1,0},{2,3},{3,2},{4,5},{5,4},{6,7},{7,6},{8,9},{9,8},{10,11... | collective-permute-start | bytes 983048 | tf_op jit(solution)/shard_map/ppermute | solution.py:21
  57.2 4.5 %collective-permute-start.19 = (bf16[80,1024]{1,0:T(8,128)(2,1)S(1)}, bf16[80,1024]{1,0:T(8,128)(2,1)S(1)}, u32[]{:S(2)}, u32[]{:S(2)}) collective-permute-start(bf16[80,1024]{1,0:T(8,128)(2,1)S(1)} %collective-permute-done.17.refs_2_.refs_13_), channel_id=1, source_target_pairs={{0,1},{1,0},{2,3},{3,2},{4,5},{5,4},{6,7},{7,6},{8,9},{9,8},{10,11... | collective-permute-start | bytes 491528 | tf_op jit(solution)/shard_map/ppermute | solution.py:21
  59.4 2.3 %collective-permute-start.23 = (bf16[80,1024]{1,0:T(8,128)(2,1)S(1)}, bf16[80,1024]{1,0:T(8,128)(2,1)S(1)}, u32[]{:S(2)}, u32[]{:S(2)}) collective-permute-start(bf16[80,1024]{1,0:T(8,128)(2,1)S(1)} %collective-permute-done.7.refs_3_.refs_17_), channel_id=1, source_target_pairs={{0,1},{1,0},{2,3},{3,2},{4,5},{5,4},{6,7},{7,6},{8,9},{9,8},{10,11... | collective-permute-start | bytes 491528 | tf_op jit(solution)/shard_map/ppermute | solution.py:21
  59.5 2.2 %collective-permute-start.24 = (bf16[80,1024]{1,0:T(8,128)(2,1)S(1)}, bf16[80,1024]{1,0:T(8,128)(2,1)S(1)}, u32[]{:S(2)}, u32[]{:S(2)}) collective-permute-start(bf16[80,1024]{1,0:T(8,128)(2,1)S(1)} %collective-permute-done.20.refs_19_), channel_id=1, source_target_pairs={{0,1},{1,0},{2,3},{3,2},{4,5},{5,4},{6,7},{7,6},{8,9},{9,8},{10,11... | collective-permute-start | bytes 491528 | tf_op jit(solution)/shard_map/ppermute | solution.py:21
  60.0 1.7 %collective-permute-start.22 = (bf16[80,1024]{1,0:T(8,128)(2,1)S(1)}, bf16[80,1024]{1,0:T(8,128)(2,1)S(1)}, u32[]{:S(2)}, u32[]{:S(2)}) collective-permute-start(bf16[80,1024]{1,0:T(8,128)(2,1)S(1)} %collective-permute-done.21.refs_15_), channel_id=1, source_target_pairs={{0,1},{1,0},{2,3},{3,2},{4,5},{5,4},{6,7},{7,6},{8,9},{9,8},{10,11... | collective-permute-start | bytes 491528 | tf_op jit(solution)/shard_map/ppermute | solution.py:21
  75.0 1.8 %collective-permute-start.26 = (bf16[512,320]{1,0:T(8,128)(2,1)S(1)}, bf16[512,320]{1,0:T(8,128)(2,1)S(1)}, u32[]{:S(2)}, u32[]{:S(2)}) collective-permute-start(bf16[512,320]{1,0:T(8,128)(2,1)S(1)} %get-tuple-element.64.memory), channel_id=1, source_target_pairs={{0,1},{1,0},{2,3},{3,2},{4,5},{5,4},{6,7},{7,6},{8,9},{9,8},{10,11... | collective-permute-start | bytes 983048 | tf_op jit(solution)/shard_map/ppermute | solution.py:21
  75.5 7.8 %collective-permute-start.28 = (bf16[256,320]{1,0:T(8,128)(2,1)S(1)}, bf16[256,320]{1,0:T(8,128)(2,1)S(1)}, u32[]{:S(2)}, u32[]{:S(2)}) collective-permute-start(bf16[256,320]{1,0:T(8,128)(2,1)S(1)} %get-tuple-element.67), channel_id=1, source_target_pairs={{0,2},{1,6},{2,0},{3,4},{4,3},{5,7},{6,1},{7,5},{8,10},{9,14},{10,... | collective-permute-start | bytes 491528 | tf_op jit(solution)/shard_map/ppermute | solution.py:21
  76.0 8.1 %collective-permute-start.25 = (bf16[256,320]{1,0:T(8,128)(2,1)S(1)}, bf16[256,320]{1,0:T(8,128)(2,1)S(1)}, u32[]{:S(2)}, u32[]{:S(2)}) collective-permute-start(bf16[256,320]{1,0:T(8,128)(2,1)S(1)} %get-tuple-element.61), channel_id=1, source_target_pairs={{0,0},{1,4},{2,2},{3,6},{4,1},{5,5},{6,3},{7,7},{8,8},{9,12},{10,1... | collective-permute-start | bytes 491528 | tf_op jit(solution)/shard_map/ppermute | solution.py:21
  78.2 5.1 %collective-permute-start.27 = (f32[40,128]{1,0:T(8,128)S(1)}, f32[40,128]{1,0:T(8,128)S(1)}, u32[]{:S(2)}, u32[]{:S(2)}) collective-permute-start(f32[40,128]{1,0:T(8,128)S(1)} %get-tuple-element.65), channel_id=1, source_target_pairs={{0,8},{1,9},{2,10},{3,11},{4,12},{5,13},{6,14},{7,15},{8,0},{9,1},... | collective-permute-start | bytes 61448 | tf_op jit(solution)/shard_map/ppermute | solution.py:21
  83.3 10.7 %collective-permute-start.30 = (bf16[256,320]{1,0:T(8,128)(2,1)S(1)}, bf16[256,320]{1,0:T(8,128)(2,1)S(1)}, u32[]{:S(2)}, u32[]{:S(2)}) collective-permute-start(bf16[256,320]{1,0:T(8,128)(2,1)S(1)} %collective-permute-done.28.refs_1_), channel_id=1, source_target_pairs={{0,1},{1,0},{2,3},{3,2},{4,5},{5,4},{6,7},{7,6},{8,9},{9,8},{10,11... | collective-permute-start | bytes 491528 | tf_op jit(solution)/shard_map/ppermute | solution.py:21
  84.1 9.9 %collective-permute-start.29 = (bf16[256,320]{1,0:T(8,128)(2,1)S(1)}, bf16[256,320]{1,0:T(8,128)(2,1)S(1)}, u32[]{:S(2)}, u32[]{:S(2)}) collective-permute-start(bf16[256,320]{1,0:T(8,128)(2,1)S(1)} %collective-permute-done.25.refs_0_), channel_id=1, source_target_pairs={{0,1},{1,0},{2,3},{3,2},{4,5},{5,4},{6,7},{7,6},{8,9},{9,8},{10,11... | collective-permute-start | bytes 491528 | tf_op jit(solution)/shard_map/ppermute | solution.py:21
  84.3 3.9 %collective-permute-start.31 = (bf16[2,384]{1,0:T(2,128)(2,1)S(1)}, bf16[2,384]{1,0:T(2,128)(2,1)S(1)}, u32[]{:S(2)}, u32[]{:S(2)}) collective-permute-start(bf16[2,384]{1,0:T(2,128)(2,1)S(1)} %get-tuple-element.71), channel_id=1, source_target_pairs={{0,2},{1,3},{2,0},{3,1},{4,6},{5,7},{6,4},{7,5},{8,10},{9,11},{10,... | collective-permute-start | bytes 4616 | tf_op jit(solution)/shard_map/ppermute | solution.py:21
  85.9 3.9 %collective-permute-start.32 = (bf16[2,384]{1,0:T(2,128)(2,1)S(1)}, bf16[2,384]{1,0:T(2,128)(2,1)S(1)}, u32[]{:S(2)}, u32[]{:S(2)}) collective-permute-start(bf16[2,384]{1,0:T(2,128)(2,1)S(1)} %get-tuple-element.72), channel_id=1, source_target_pairs={{0,4},{1,5},{2,6},{3,7},{4,0},{5,1},{6,2},{7,3},{8,12},{9,13},{10,... | collective-permute-start | bytes 4616 | tf_op jit(solution)/shard_map/ppermute | solution.py:21
  88.3 4.5 %collective-permute-start.33 = (bf16[2,384]{1,0:T(2,128)(2,1)S(1)}, bf16[2,384]{1,0:T(2,128)(2,1)S(1)}, u32[]{:S(2)}, u32[]{:S(2)}) collective-permute-start(bf16[2,384]{1,0:T(2,128)(2,1)S(1)} %get-tuple-element.73), channel_id=1, source_target_pairs={{0,6},{1,7},{2,4},{3,5},{4,2},{5,3},{6,0},{7,1},{8,14},{9,15},{10,... | collective-permute-start | bytes 4616 | tf_op jit(solution)/shard_map/ppermute | solution.py:21

commit v9 on v8

--- a/solution.py
+++ b/solution.py
@@ -13,6 +13,7 @@
 BF = jnp.bfloat16
 F32 = jnp.float32
 LOW = -1e30
+CHEAP = pl.CostEstimate(flops=1, bytes_accessed=1, transcendentals=0)
 VMEM = pl.BlockSpec(memory_space=pltpu.VMEM)
 SMEM = pl.BlockSpec(memory_space=pltpu.SMEM)
 
@@ -51,7 +52,14 @@
     return jnp.concatenate(heads + [asked], axis=0)
 
 
-def pack_kernel(table, weight, queries, mask, segments, mine, theirs):
+def pack_kernel(table, *refs):
+    mine, theirs = refs[4:6]
+    weight, queries, mask, segments = held = refs[6:10]
+    copies = [pltpu.make_async_copy(refs[i], held[i], refs[10].at[i]) for i in range(4)]
+    for copy in copies:
+        copy.start()
+    for copy in copies:
+        copy.wait()
     rows, width = weight.shape[0], weight.shape[1] // 3
     blocks = mask.shape[1]
     ids = segments[...]
@@ -86,17 +94,20 @@
 
 def pack(table, weight, queries, mask, segments):
     shape = jax.ShapeDtypeStruct((2, weight.shape[0], 1024), BF)
+    given = (weight, queries, mask, segments)
     return pl.pallas_call(
         pack_kernel,
         out_shape=(shape, shape),
-        in_specs=[SMEM] + [VMEM] * 4,
+        in_specs=[SMEM] + [pl.BlockSpec(memory_space=pl.ANY)] * 4,
         out_specs=(VMEM,) * 2,
+        scratch_shapes=[pltpu.VMEM(a.shape, a.dtype) for a in given] + [pltpu.SemaphoreType.DMA((4,))],
+        cost_estimate=CHEAP,
         compiler_params=pltpu.CompilerParams(vmem_limit_bytes=8 * 1024 * 1024),
     )(table, weight, queries, mask, segments)
 
 
 def load_kernel(table, *refs):
-    held, outs, other = refs[:4], refs[4:6], refs[6]
+    held, outs = refs[:4], refs[4:]
     x, c, p = table[6], table[7], table[5]
     own = jnp.broadcast_to(table[12], outs[0].shape) == 1
     flip_c = jnp.broadcast_to(c, (16, 128)) == 1
@@ -105,8 +116,6 @@
         mine, mine_c, across, across_c = [h[pl.ds(p ^ a, 1)][0] for h in held]
         out = outs[a]
         out[...] = jnp.where(own, mine, across)
-        if a == 1:
-            other[mine.shape[0] :, :] = jnp.where(own, across, mine)
         lanes = [part[:16, 896:] for part in (mine, mine_c, across, across_c)]
         rows = []
         for first, second in (lanes[:2], lanes[2:]):
@@ -118,55 +127,46 @@
             out[16 * j : 16 * j + 16, 896:] = jnp.where(
                 lane < HD, out[16 * j : 16 * j + 16, 896:], found
             )
-        if a == 1:
-            other[: mine.shape[0], :] = out[...]
 
 
 def load(table, *held):
     rows = held[0].shape[1]
     return pl.pallas_call(
         load_kernel,
-        out_shape=tuple(jax.ShapeDtypeStruct((rows * i, 1024), BF) for i in (1, 1, 2)),
+        out_shape=(jax.ShapeDtypeStruct((rows, 1024), BF),) * 2,
         in_specs=[SMEM] + [VMEM] * 4,
-        out_specs=(VMEM,) * 3,
+        out_specs=(VMEM,) * 2,
+        cost_estimate=CHEAP,
         compiler_params=pltpu.CompilerParams(vmem_limit_bytes=8 * 1024 * 1024),
     )(table, *held)
 
 
-def norm_kernel(ways, table, gain, *refs):
-    blocks, (normed, residual) = refs[: 4 * ways], refs[4 * ways :]
+def norm_kernel(table, gain, here, across, out):
     group = table[4]
-    for i in range(4):
-        place = pl.multiple_of(table[i], 128)
-        values = blocks[i][...]
-        if ways == 2:
-            first = jnp.broadcast_to(table[5], values.shape) == 1
-            values = jnp.where(first, values, blocks[4 + i][...])
-        values = values.astype(F32)
+    for i, block in enumerate((here, across)):
+        rows = slice(128 * i, 128 * i + 128)
+        values = block[...].astype(F32)
         mean = jnp.mean(values, axis=-1, keepdims=True)
         centred = values - mean
         var = jnp.mean(centred * centred, axis=-1, keepdims=True)
-        normed[pl.ds(place, 128), :] = (centred * lax.rsqrt(var + 1e-05) * gain[...]).astype(BF)
-        block = blocks[i]
-        residual[pl.ds(place, 128), :WIDE] = block[
-            :, pl.ds(pl.multiple_of(group * WIDE, 128), WIDE)
-        ]
-        slab = block[:, pl.ds(pl.multiple_of(1024 + group // 2 * 128, 128), 128)]
-        odd = jnp.broadcast_to(lax.rem(group, 2), (128, HD)) == 1
-        residual[pl.ds(place, 128), WIDE:] = jnp.where(odd, slab[:, HD:], slab[:, :HD])
-
-
-def norm_layer(table, gain, blocks):
-    return pl.pallas_call(
-        functools.partial(norm_kernel, len(blocks) // 4),
-        out_shape=(
-            jax.ShapeDtypeStruct((512, 1280), BF),
-            jax.ShapeDtypeStruct((512, GROUP), BF),
-        ),
-        in_specs=[SMEM] + [VMEM] * (1 + len(blocks)),
-        out_specs=(VMEM, VMEM),
-        compiler_params=pltpu.CompilerParams(vmem_limit_bytes=16 * 1024 * 1024),
-    )(table, gain, *blocks)
+        out[rows, :1280] = (centred * lax.rsqrt(var + 1e-05) * gain[...]).astype(BF)
+        if out.shape[1] > 1280:
+            out[rows, 1280 : 1280 + WIDE] = block[:, pl.ds(pl.multiple_of(group * WIDE, 128), WIDE)]
+            slab = block[:, pl.ds(pl.multiple_of(1024 + group // 2 * 128, 128), 128)]
+            odd = jnp.broadcast_to(lax.rem(group, 2), (128, HD)) == 1
+            tail = jnp.where(odd, slab[:, HD:], slab[:, :HD])
+            out[rows, 1280 + WIDE :] = jnp.concatenate([tail, jnp.zeros_like(tail)], axis=1)
+
+
+def norm_half(table, gain, here, across, kept=True):
+    return pl.pallas_call(
+        norm_kernel,
+        out_shape=jax.ShapeDtypeStruct((256, 1664 if kept else 1280), BF),
+        in_specs=[SMEM] + [VMEM] * 3,
+        out_specs=VMEM,
+        cost_estimate=CHEAP,
+        compiler_params=pltpu.CompilerParams(vmem_limit_bytes=8 * 1024 * 1024),
+    )(table, gain, here, across)
 
 
 def prepare_kernel(table, *refs):
@@ -211,6 +211,7 @@
         ),
         in_specs=[SMEM] + [VMEM] * len(parts),
         out_specs=(VMEM,) * 3,
+        cost_estimate=CHEAP,
         compiler_params=pltpu.CompilerParams(vmem_limit_bytes=8 * 1024 * 1024),
     )(table, *parts)
 
@@ -232,26 +233,33 @@
 
     for slab in range(3):
         values[:, 256 * slab + 128 : 256 * slab + 256] = jnp.ones((1536, 128), BF)
-    for i, (normed, kept) in enumerate(layers):
-        place = pl.multiple_of(places[8 + i], 512)
-        found = jnp.dot(normed[...], weight[:, 256:896], preferred_element_type=F32).astype(BF)
-        keys[pl.ds(place, 512), :256] = found[:, :256]
-        keys[pl.ds(place, 512), 256:] = found[:, 512:]
-        for slab in range(3):
-            values[pl.ds(place, 512), 256 * slab : 256 * slab + 128] = found[
-                :, 256 + 128 * slab : 384 + 128 * slab
-            ]
+    spots = [places[i] for i in (0, 2, 1, 3)]
+    for i, halves in enumerate(layers):
+        place = places[8 + i]
+        normed = jnp.concatenate([half[:, :1280] for half in halves], axis=0)
+        found = jnp.dot(normed, weight[:, 256:896], preferred_element_type=F32).astype(BF)
+        for j, spot in enumerate(spots):
+            to = pl.ds(pl.multiple_of(place + spot, 128), 128)
+            block = found[128 * j : 128 * j + 128]
+            keys[to, :256] = block[:, :256]
+            keys[to, 256:] = block[:, 512:]
+            for slab in range(3):
+                values[to, 256 * slab : 256 * slab + 128] = block[:, 256 + 128 * slab : 384 + 128 * slab]
         if i < 2:
 
             @pl.when(place == 512)
             def _():
-                residual[...] = kept[...]
-                queries[:, :WIDE] = jnp.dot(
-                    normed[...], weight[:, :WIDE], preferred_element_type=F32
-                ).astype(BF)
-                tail = jnp.dot(normed[...], weight[:, 896:], preferred_element_type=F32).astype(BF)
+                normed = jnp.concatenate([half[:, :1280] for half in halves], axis=0)
+                wide = jnp.dot(normed, weight[:, :WIDE], preferred_element_type=F32).astype(BF)
+                tail = jnp.dot(normed, weight[:, 896:], preferred_element_type=F32).astype(BF)
                 lane = lax.broadcasted_iota(jnp.int32, tail.shape, 1)
-                queries[:, WIDE:] = jnp.where(lane < HD, tail, jnp.zeros_like(tail))
+                tail = jnp.where(lane < HD, tail, jnp.zeros_like(tail))
+                for j, spot in enumerate(spots):
+                    to = pl.ds(pl.multiple_of(spot, 128), 128)
+                    rows = slice(128 * j, 128 * j + 128)
+                    queries[to, :WIDE] = wide[rows]
+                    queries[to, WIDE:] = tail[rows]
+                    residual[to, :] = halves[j // 2][128 * (j % 2) : 128 * (j % 2) + 128, 1280:]
 
     side = lax.broadcasted_iota(jnp.int32, (8, 128), 0) == lax.broadcasted_iota(
         jnp.int32, (8, 128), 1
@@ -309,7 +317,7 @@
                 stem = residual[pl.ds(row, 128), span].astype(F32)
                 memory[pl.ds(row, 128), span] = (stem + context).astype(BF)
             else:
-                stem = residual[pl.ds(row, 128), WIDE:].astype(F32)
+                stem = residual[pl.ds(row, 128), WIDE:GROUP].astype(F32)
                 memory[pl.ds(row, 128), WIDE:] = (stem + out[:, HD:]).astype(BF)
 
     @pl.when(small)
@@ -326,7 +334,7 @@
 
 
 def encoder(places, layers, ids, parts, depth):
-    operands = [a for layer in layers for a in layer] + [ids] + parts
+    operands = layers + [ids] + parts
     return pl.pallas_call(
         functools.partial(encoder_kernel, len(parts), depth),
         out_shape=(
@@ -338,11 +346,12 @@
         out_specs=(VMEM, VMEM, VMEM),
         scratch_shapes=[
             pltpu.VMEM((1280, 1024), BF),
-            pltpu.VMEM((512, GROUP), BF),
+            pltpu.VMEM((512, 384), BF),
             pltpu.VMEM((512, 384), BF),
             pltpu.VMEM((1536, 384), BF),
             pltpu.VMEM((1536, 768), BF),
         ],
+        cost_estimate=CHEAP,
         compiler_params=pltpu.CompilerParams(vmem_limit_bytes=24 * 1024 * 1024),
     )(places, *operands)
 
@@ -398,6 +407,7 @@
         in_specs=[SMEM] + [VMEM] * 4,
         out_specs=(VMEM,) * (count // 8),
         scratch_shapes=[pltpu.VMEM((5 * count, GROUP), F32)],
+        cost_estimate=CHEAP,
         compiler_params=pltpu.CompilerParams(vmem_limit_bytes=12 * 1024 * 1024),
     )(table, tokens, asked, memory, beside)
 
@@ -424,6 +434,7 @@
         in_specs=[VMEM] * len(parts),
         out_specs=(VMEM,) * 4,
         scratch_shapes=[pltpu.VMEM((8, 384), F32)],
+        cost_estimate=CHEAP,
         compiler_params=pltpu.CompilerParams(vmem_limit_bytes=4 * 1024 * 1024),
     )(*parts)
 
@@ -449,6 +460,7 @@
         out_shape=jax.ShapeDtypeStruct((rows, 1280), BF),
         in_specs=[SMEM] + [VMEM] * 4,
         out_specs=VMEM,
+        cost_estimate=CHEAP,
         compiler_params=pltpu.CompilerParams(vmem_limit_bytes=4 * 1024 * 1024),
     )(table, *pieces)
 
@@ -472,11 +484,9 @@
     table += [512 * (p - c + 1), 512 * (2 - p - c), 1024 * c, 0, x == moved, 4 * quarter - 4, z]
     sources = [me, me ^ 1, me ^ 2, me ^ 3] if direct else [jnp.int32(0)]
     for turn in (1, 2, 3) if direct else ():
-        column, sides = 4 * (z ^ turn) + c, (2 * moved, 2 - 2 * moved)
-        if turn == 1:
-            sources += [core + side for core in (column, column ^ 1) for side in sides]
-        else:
-            sources += [core + side for side in sides for core in (column, column ^ 1)]
+        column = 4 * (z ^ turn) + c
+        for side in (2 * moved, 2 - 2 * moved):
+            sources += [column + side, (column ^ 1) + side]
     table = scalars(table + sources + [4 * quarter, 4 * (quarter ^ 1), me])
     base = 15 + len(sources)
 
@@ -496,48 +506,42 @@
         mine, theirs = pack(
             table, qkv_weight, dec_queries, stretch_mask, segment_ids.reshape(1, -1)
         )
-        stem_x = swap(stem, n, 2)
-        across = swap(after(theirs, stem_x, pair, near), n, 2)
+        across = swap(theirs, n, 2)
         mine_c, across_c = swap(mine, n, 1), swap(across, n, 1)
-        relayed = swap(after(near, pair), n, 4)
-        ready = load(table, mine, mine_c, after(across, relayed), across_c)
-        here = {turn: swap(ready[turn % 2], n, 4 * turn) for turn in (3, 2)}
-        here[1] = swap(ready[2], n, 4)
-        stem_c, stem_xc = [swap(after(part, here[3]), n, 1) for part in (stem, stem_x)]
-        own_layer = norm_layer(table, gain, [stem, stem_c, stem_x, stem_xc])
-        pair_x = swap(after(pair, across), n, 2)
+        ready = load(table, mine, mine_c, after(across, near, pair), across_c)
+        relayed = swap(after(near, ready[0]), n, 4)
+        stem_x = swap(after(stem, across), n, 2)
+        here = {turn: swap(ready[turn % 2], n, 4 * turn) for turn in (3, 2, 1)}
+        pair_x = swap(after(pair, ready[0]), n, 2)
         halo = jnp.where((z == 1) | (z == 2), near, relayed)
         halo_x = swap(after(halo, pair_x), n, 2)
-        pair_c, pair_xc = [swap(after(part, here[3]), n, 1) for part in (pair, pair_x)]
-        pair_layer = norm_layer(table, gain, [pair, pair_c, pair_x, pair_xc])
-        halo_layer = norm_layer(table, gain, [halo, swap(halo, n, 1), halo_x, swap(halo_x, n, 1)])
-        traded = {3: trade(here[3])}
-        traded[2] = trade(after(here[2], here[1], traded[3]))
         ids, tokens, asked = prepare(table, [ready[0], here[1], here[2], here[3]], n)
+        traded = {3: trade(after(here[3], pair_x)), 2: trade(after(here[2], here[3]))}
+        traded[1] = trade(after(here[1], ids))
+        own_half = norm_half(table, gain, stem, stem_x)
+        pair_half = norm_half(table, gain, pair, pair_x)
+        halo_half = norm_half(table, gain, halo, halo_x, False)
+        layered = [
+            own_half, swap(after(own_half, traded[3]), n, 1),
+            pair_half, swap(after(pair_half, traded[2]), n, 1),
+            halo_half, swap(after(halo_half, traded[1]), n, 1),
+        ]
         weights = [mine, mine_c, across, across_c]
-        weights += [here[1], swap(here[1], n, 1)]
-        for turn in (2, 3):
+        for turn in (1, 2, 3):
             for part in (here[turn], traded[turn]):
-                last = part is traded[2]
-                beside = after(part, own_layer[0], pair_layer[0], ids) if last else part
-                weights += [part, swap(beside, n, 1)]
-        layered = [own_layer, pair_layer, halo_layer]
+                weights += [part, swap(part, n, 1)]
     else:
         stem_x = swap(stem, n, 2)
         far = swap(near, n, 4)
         left = jnp.where(p == 0, near, far)
         right = jnp.where(p == 0, far, near)
         left_x, right_x = swap(left, n, 2), swap(right, n, 2)
-        halo = [
-            jnp.where(c == 0, left, right),
-            swap(jnp.where(c == 0, right, left), n, 1),
-            jnp.where(c == 0, left_x, right_x),
-            swap(jnp.where(c == 0, right_x, left_x), n, 1),
-        ]
-        pair_x = swap(pair, n, 2)
-        own = [stem, swap(stem, n, 1), stem_x, swap(stem_x, n, 1)]
-        other = [pair, swap(pair, n, 1), pair_x, swap(pair_x, n, 1)]
-        layered = [norm_layer(table, gain, blocks) for blocks in (own, other, halo)]
+        left = norm_half(table, gain, left, left_x, False)
+        right = norm_half(table, gain, right, right_x, False)
+        halo = [jnp.where(c == 0, left, right), swap(jnp.where(c == 0, right, left), n, 1)]
+        own = norm_half(table, gain, stem, stem_x)
+        other = norm_half(table, gain, pair, swap(pair, n, 2))
+        layered = [own, swap(own, n, 1), other, swap(other, n, 1)] + halo
         whole = lax.all_gather(qkv_weight, "tm", axis=0, tiled=True)
         grouped = jnp.stack([weight_group(whole, g) for g in range(4)])
         weights = [lax.dynamic_index_in_dim(grouped, group, 0, keepdims=False)]

time: 95.6 us -> 93 us (0.973)
  waiting for transfers between devices: 34.7 us -> 31.9 us
  starting transfers between devices: 31.5 us -> 33.6 us
  Pallas kernels: 25 us -> 23.4 us
  local copies, waits for them, and re-layouts: 3.21 us -> 1.87 us
  other arithmetic: 0.04 us -> 1.01 us
    ppermute x32 -> x30, waiting for transfers between devices: 30.1 us -> 27.4 us  [send(): return lax.ppermute(block, 'tm', route)]
    pallas_call x4, Pallas kernels: 5.33 us -> 3.53 us  [the longest x3 2.94 us: norm_half(): pl.pallas_call(norm_kernel, out_shape=jax.ShapeDtypeStruct((256, 1664 if...]
    ppermute x32 -> x30, starting transfers between devices: 28.5 us -> 30 us  [send(): return lax.ppermute(block, 'tm', route)]
    unnamed x12, local copies, waits for them, and re-layouts: 3.1 us -> 1.75 us
    select_n x1, other arithmetic: 0.04 us -> 1.01 us  [on_device(): halo = jnp.where((z == 1) | (z == 2), near, relayed)]
    ppermute x2 -> x3, starting transfers between devices: 3.04 us -> 3.61 us  [trade(): return lax.ppermute(block, 'utt', [(u, u ^ 1) for u in range(utts)])]
    ppermute x2 -> x3, waiting for transfers between devices: 4.58 us -> 4.56 us  [trade(): return lax.ppermute(block, 'utt', [(u, u ^ 1) for u in range(utts)])]
  transfers between devices with their start and end apart: 34 -> 33, of which waited for: 11 -> 17; matrix products, arithmetic and copies ran while one was open for 0% -> 1% of each run, Pallas kernels for 11% -> 8%
where the time goes in v9:
time: 93 us; the launch traced here: 92.8 us
  starting transfers between devices  33.6 us (36%)
  waiting for transfers between devices  31.9 us (34%)
  Pallas kernels  23.4 us (25%)
  local copies, waits for them, and re-layouts  1.87 us (2%)
  other arithmetic  1.01 us (1%)
    ppermute x30, starting transfers between devices, send(): return lax.ppermute(block, 'tm', route)  30 us
    ppermute x30, waiting for transfers between devices, send(): return lax.ppermute(block, 'tm', route)  27.4 us
    pallas_call x1, Pallas kernels, encoder(): pl.pallas_call(functools.partial(encoder_kernel, len(parts), depth), out_...  13.3 us
    ppermute x3, waiting for transfers between devices, trade(): return lax.ppermute(block, 'utt', [(u, u ^ 1) for u in range(utts)])  4.56 us
    ppermute x3, starting transfers between devices, trade(): return lax.ppermute(block, 'utt', [(u, u ^ 1) for u in range(utts)])  3.61 us
    pallas_call x3, Pallas kernels, norm_half(): pl.pallas_call(norm_kernel, out_shape=jax.ShapeDtypeStruct((256, 1664 if...  2.94 us
    pallas_call x2, Pallas kernels, gather_groups(): pl.pallas_call(functools.partial(gather_kernel, side, rows), out_shape=ja...  2.59 us
  transfers between devices with their start and end apart: 33, of which 17 were waited for; matrix products, arithmetic and copies ran while one was open for 1% of the time, Pallas kernels for 8%

profile of v9, /device:TPU:0, one launch (start us, length us, event | category | flops | bytes accessed | tf_op | source)
XLA Modules:
  0.0 92.8 jit_solution(1661440555048381184)
XLA Ops:
  0.7 0.0 copy-start.2
  0.7 0.1 stack.136.table.places
  0.9 0.0 copy-start.3
  0.9 0.0 copy-start.4
  0.9 0.5 copy-done.2
  1.4 0.1 copy-done.3
  1.5 1.1 %copy-done = bf16[80,3840]{1,0:T(8,128)(2,1)S(1)} copy-done((bf16[80,3840]{1,0:T(8,128)(2,1)S(1)}, bf16[80,3840]{1,0:T(8,128)(2,1)}, u32[]{:S(2)}) %copy-start) | copy-done | bytes 614424
  2.6 1.1 %shard_map.77 = (bf16[2,80,1024]{2,1,0:T(8,128)(2,1)S(1)}, bf16[2,80,1024]{2,1,0:T(8,128)(2,1)S(1)}) custom-call(s32[34]{0:T(128)S(1)} %stack.136.table.places, bf16[80,3840]{1,0:T(8,128)(2,1)S(1)} %copy-done, bf16[2,1280]{1,0:T(2,128)(2,1)S(1)} %copy-done.2, s32[2,16]{1,0:T(2,128)S(1)} %copy-done.3, s32[1,128]{1,0:T(1,128)S(1)} %bitcast.33), custom_call_target="tpu_custom_call" | custom-call | flops 1 | bytes 1 | tf_op jit(solution)/shard_map/pallas_call | solution.py:98
  3.8 3.0 %collective-permute-start = (bf16[2,80,1024]{2,1,0:T(8,128)(2,1)S(1)}, bf16[2,80,1024]{2,1,0:T(8,128)(2,1)S(1)}, u32[]{:S(2)}, u32[]{:S(2)}) collective-permute-start(bf16[2,80,1024]{2,1,0:T(8,128)(2,1)S(1)} %get-tuple-element.31), channel_id=1, source_target_pairs={{0,2},{1,3},{2,0},{3,1},{4,6},{5,7},{6,4},{7,5},{8,10},{9,11},{10,... | collective-permute-start | bytes 983048 | tf_op jit(solution)/shard_map/ppermute | solution.py:22
  6.8 1.6 %collective-permute-start.4 = (bf16[128,1280]{1,0:T(8,128)(2,1)S(1)}, bf16[128,1280]{1,0:T(8,128)(2,1)S(1)}, u32[]{:S(2)}, u32[]{:S(2)}) collective-permute-start(bf16[128,1280]{1,0:T(8,128)(2,1)S(1)} %copy-done.1), channel_id=1, source_target_pairs={{0,4},{1,5},{2,6},{3,7},{4,0},{5,1},{6,2},{7,3},{8,12},{9,13},{10,... | collective-permute-start | bytes 983048 | tf_op jit(solution)/shard_map/ppermute | solution.py:22
  8.4 0.7 collective-permute-start.3
  9.0 0.1 collective-permute-start.2
  9.1 5.4 %collective-permute-done.refs_2_.refs_9_ = bf16[2,80,1024]{2,1,0:T(8,128)(2,1)S(1)} collective-permute-done((bf16[2,80,1024]{2,1,0:T(8,128)(2,1)S(1)}, bf16[2,80,1024]{2,1,0:T(8,128)(2,1)S(1)}, u32[]{:S(2)}, u32[]{:S(2)}) %collective-permute-start) | collective-permute-done | bytes 327712 | tf_op jit(solution)/shard_map/ppermute | solution.py:22
  14.5 1.5 %collective-permute-done.4.here = bf16[128,1280]{1,0:T(8,128)(2,1)S(1)} collective-permute-done((bf16[128,1280]{1,0:T(8,128)(2,1)S(1)}, bf16[128,1280]{1,0:T(8,128)(2,1)S(1)}, u32[]{:S(2)}, u32[]{:S(2)}) %collective-permute-start.4) | collective-permute-done | bytes 327712 | tf_op jit(solution)/shard_map/ppermute | solution.py:22
  16.0 0.2 collective-permute-done.5.refs_3_.refs_10_
  16.1 0.6 shard_map.79
  16.7 1.8 %collective-permute-start.7 = (bf16[128,1280]{1,0:T(8,128)(2,1)S(1)}, bf16[128,1280]{1,0:T(8,128)(2,1)S(1)}, u32[]{:S(2)}, u32[]{:S(2)}) collective-permute-start(bf16[128,1280]{1,0:T(8,128)(2,1)S(1)} %collective-permute-done.4.here), channel_id=1, source_target_pairs={{0,2},{1,3},{2,0},{3,1},{4,6},{5,7},{6,4},{7,5},{8,10},{9,11},{10,... | collective-permute-start | bytes 983048 | tf_op jit(solution)/shard_map/ppermute | solution.py:22
  18.5 3.2 %collective-permute-start.13 = (bf16[128,1280]{1,0:T(8,128)(2,1)S(1)}, bf16[128,1280]{1,0:T(8,128)(2,1)}, u32[]{:S(2)}, u32[]{:S(2)}) collective-permute-start(bf16[128,1280]{1,0:T(8,128)(2,1)S(1)} %collective-permute-done.3), channel_id=1, source_target_pairs={{0,4},{1,5},{2,6},{3,7},{4,0},{5,1},{6,2},{7,3},{8,12},{9,13},{10,... | collective-permute-start | bytes 983048 | tf_op jit(solution)/shard_map/ppermute | solution.py:22
  21.8 2.6 %collective-permute-start.6 = (bf16[80,1024]{1,0:T(8,128)(2,1)S(1)}, bf16[80,1024]{1,0:T(8,128)(2,1)S(1)}, u32[]{:S(2)}, u32[]{:S(2)}) collective-permute-start(bf16[80,1024]{1,0:T(8,128)(2,1)S(1)} %get-tuple-element.35), channel_id=1, source_target_pairs={{0,12},{1,13},{2,14},{3,15},{4,8},{5,9},{6,10},{7,11},{8,4},{9,5},... | collective-permute-start | bytes 491528 | tf_op jit(solution)/shard_map/ppermute | solution.py:22
  24.4 1.5 %collective-permute-start.1 = (bf16[128,1280]{1,0:T(8,128)(2,1)S(1)}, bf16[128,1280]{1,0:T(8,128)(2,1)S(1)}, u32[]{:S(2)}, u32[]{:S(2)}) collective-permute-start(bf16[128,1280]{1,0:T(8,128)(2,1)S(1)} %copy-done.1), channel_id=1, source_target_pairs={{0,2},{1,3},{2,0},{3,1},{4,6},{5,7},{6,4},{7,5},{8,10},{9,11},{10,... | collective-permute-start | bytes 983048 | tf_op jit(solution)/shard_map/ppermute | solution.py:22
  25.9 10.7 %collective-permute-done.6.refs_3_.refs_19_ = bf16[80,1024]{1,0:T(8,128)(2,1)S(1)} collective-permute-done((bf16[80,1024]{1,0:T(8,128)(2,1)S(1)}, bf16[80,1024]{1,0:T(8,128)(2,1)S(1)}, u32[]{:S(2)}, u32[]{:S(2)}) %collective-permute-start.6) | collective-permute-done | bytes 163872 | tf_op jit(solution)/shard_map/ppermute | solution.py:22
  36.6 1.5 %collective-permute-start.11 = (bf16[80,1024]{1,0:T(8,128)(2,1)S(1)}, bf16[80,1024]{1,0:T(8,128)(2,1)S(1)}, u32[]{:S(2)}, u32[]{:S(2)}) collective-permute-start(bf16[80,1024]{1,0:T(8,128)(2,1)S(1)} %collective-permute-done.10.refs_2_.refs_15_), channel_id=1, source_target_pairs={{0,16},{16,0},{1,17},{17,1},{2,18},{18,2},{3,19},{19,3},{4,20},{20... | collective-permute-start | bytes 491528 | tf_op jit(solution)/shard_map/ppermute | solution.py:504
  38.1 0.5 collective-permute-start.8
  38.6 1.0 %broadcast_select_fusion.here = bf16[128,1280]{1,0:T(8,128)(2,1)S(1)} fusion(bf16[128,1280]{1,0:T(8,128)(2,1)S(1)} %collective-permute-done.3, bf16[128,1280]{1,0:T(8,128)(2,1)} %collective-permute-done.13, pred[]{:T(512)S(6)} %or.3), kind=kLoop, calls=%fused_computation | loop fusion | flops 163840 | bytes 983041 | tf_op jit(solution)/shard_map/jit(_where)/select_n | solution.py:516
  39.6 1.5 %collective-permute-start.14 = (bf16[128,1280]{1,0:T(8,128)(2,1)S(1)}, bf16[128,1280]{1,0:T(8,128)(2,1)S(1)}, u32[]{:S(2)}, u32[]{:S(2)}) collective-permute-start(bf16[128,1280]{1,0:T(8,128)(2,1)S(1)} %broadcast_select_fusion.here), channel_id=1, source_target_pairs={{0,2},{1,3},{2,0},{3,1},{4,6},{5,7},{6,4},{7,5},{8,10},{9,11},{10,... | collective-permute-start | bytes 983048 | tf_op jit(solution)/shard_map/ppermute | solution.py:22
  41.1 1.0 %shard_map.78.refs_0_ = bf16[256,1664]{1,0:T(8,128)(2,1)S(1)} custom-call(s32[34]{0:T(128)S(1)} %stack.136.table.places, f32[1,1280]{1,0:T(1,128)S(1)} %reshape.10.gain, bf16[128,1280]{1,0:T(8,128)(2,1)S(1)} %copy-done.1, bf16[128,1280]{1,0:T(8,128)(2,1)S(1)} %collective-permute-done.1.across), custom_call_target="tpu_custom_call" | custom-call | flops 1 | bytes 1 | tf_op jit(solution)/shard_map/pallas_call | solution.py:162
  42.1 1.0 %shard_map.80.refs_2_ = bf16[256,1664]{1,0:T(8,128)(2,1)S(1)} custom-call(s32[34]{0:T(128)S(1)} %stack.136.table.places, f32[1,1280]{1,0:T(1,128)S(1)} %reshape.10.gain, bf16[128,1280]{1,0:T(8,128)(2,1)S(1)} %collective-permute-done.4.here, bf16[128,1280]{1,0:T(8,128)(2,1)S(1)} %collective-permute-done.7.across), custom_call_target="tpu_custom_call" | custom-call | flops 1 | bytes 1 | tf_op jit(solution)/shard_map/pallas_call | solution.py:162
  43.1 0.1 collective-permute-start.12
  43.2 0.4 collective-permute-done.8.refs_21_
  43.6 0.1 collective-permute-start.9
  43.7 1.3 %shard_map.82 = (f32[8,1536]{1,0:T(8,128)S(1)}, f32[80,320]{1,0:T(8,128)S(1)}, f32[16,64]{1,0:T(8,128)S(1)}) custom-call(s32[34]{0:T(128)S(1)} %stack.136.table.places, bf16[80,1024]{1,0:T(8,128)(2,1)S(1)} %get-tuple-element.36.refs_0_, bf16[80,1024]{1,0:T(8,128)(2,1)S(1)} %collective-permute-done.15.refs_1_.refs_11_, ...), custom_call_target="tpu_custom_call" | custom-call | flops 1 | bytes 1 | tf_op jit(solution)/shard_map/pallas_call | solution.py:205
  45.0 1.6 %collective-permute-start.16 = (bf16[80,1024]{1,0:T(8,128)(2,1)S(1)}, bf16[80,1024]{1,0:T(8,128)(2,1)S(1)}, u32[]{:S(2)}, u32[]{:S(2)}) collective-permute-start(bf16[80,1024]{1,0:T(8,128)(2,1)S(1)} %collective-permute-done.15.refs_1_.refs_11_), channel_id=1, source_target_pairs={{0,16},{16,0},{1,17},{17,1},{2,18},{18,2},{3,19},{19,3},{4,20},{20... | collective-permute-start | bytes 491528 | tf_op jit(solution)/shard_map/ppermute | solution.py:504
  46.6 0.1 collective-permute-done.14.across
  46.8 1.0 %shard_map.81.refs_4_ = bf16[256,1280]{1,0:T(8,128)(2,1)S(1)} custom-call(s32[34]{0:T(128)S(1)} %stack.136.table.places, f32[1,1280]{1,0:T(1,128)S(1)} %reshape.10.gain, bf16[128,1280]{1,0:T(8,128)(2,1)S(1)} %broadcast_select_fusion.here, bf16[128,1280]{1,0:T(8,128)(2,1)S(1)} %collective-permute-done.14.across), custom_call_target="tpu_custom_call" | custom-call | flops 1 | bytes 1 | tf_op jit(solution)/shard_map/pallas_call | solution.py:162
  47.7 4.1 %collective-permute-done.16.refs_13_ = bf16[80,1024]{1,0:T(8,128)(2,1)S(1)} collective-permute-done((bf16[80,1024]{1,0:T(8,128)(2,1)S(1)}, bf16[80,1024]{1,0:T(8,128)(2,1)S(1)}, u32[]{:S(2)}, u32[]{:S(2)}) %collective-permute-start.16) | collective-permute-done | bytes 163872 | tf_op jit(solution)/shard_map/ppermute | solution.py:504
  51.9 0.5 collective-permute-start.18
  52.4 0.0 collective-permute-start.22
  52.4 1.8 %collective-permute-done.18.refs_12_ = bf16[80,1024]{1,0:T(8,128)(2,1)S(1)} collective-permute-done((bf16[80,1024]{1,0:T(8,128)(2,1)S(1)}, bf16[80,1024]{1,0:T(8,128)(2,1)S(1)}, u32[]{:S(2)}, u32[]{:S(2)}) %collective-permute-start.18) | collective-permute-done | bytes 163872 | tf_op jit(solution)/shard_map/ppermute | solution.py:22
  54.2 0.1 collective-permute-start.20
  54.3 0.1 collective-permute-done.22.refs_20_
  54.4 0.3 collective-permute-start.19
  54.7 0.9 collective-permute-done.20.refs_16_
  55.6 0.1 collective-permute-start.21
  55.7 0.1 collective-permute-done.19.refs_14_
  55.8 0.3 collective-permute-start.23
  56.1 0.9 collective-permute-done.21.refs_18_
  57.0 0.2 collective-permute-done.23.refs_22_
  57.2 13.3 %shard_map.83 = (bf16[512,320]{1,0:T(8,128)(2,1)S(1)}, bf16[256,320]{1,0:T(8,128)(2,1)S(1)}, bf16[256,320]{1,0:T(8,128)(2,1)S(1)}) custom-call(s32[34]{0:T(128)S(1)} %stack.136.table.places, bf16[256,1664]{1,0:T(8,128)(2,1)S(1)} %shard_map.78.refs_0_, bf16[256,1664]{1,0:T(8,128)(2,1)S(1)} %collective-permute-done.9.refs_1_, ...), custom_call_target="tpu_custom_call" | custom-call | flops 1 | bytes 1 | tf_op jit(solution)/shard_map/pallas_call | solution.py:338
  70.6 0.3 collective-permute-start.25
  70.9 1.5 %collective-permute-start.27 = (bf16[256,320]{1,0:T(8,128)(2,1)S(1)}, bf16[256,320]{1,0:T(8,128)(2,1)S(1)}, u32[]{:S(2)}, u32[]{:S(2)}) collective-permute-start(bf16[256,320]{1,0:T(8,128)(2,1)S(1)} %get-tuple-element.53), channel_id=1, source_target_pairs={{0,2},{1,6},{2,0},{3,4},{4,3},{5,7},{6,1},{7,5},{8,10},{9,14},{10,... | collective-permute-start | bytes 491528 | tf_op jit(solution)/shard_map/ppermute | solution.py:22
  72.4 0.7 collective-permute-start.24
  73.0 1.3 %shard_map.84 = (f32[40,128]{1,0:T(8,128)S(1)}, f32[40,128]{1,0:T(8,128)S(1)}) custom-call(s32[34]{0:T(128)S(1)} %stack.136.table.places, f32[80,320]{1,0:T(8,128)S(1)} %get-tuple-element.48.tokens, f32[16,64]{1,0:T(8,128)S(1)} %get-tuple-element.49.asked, bf16[512,320]{1,0:T(8,128)(2,1)S(1)} %get-tuple-element.50.memory, ...), custom_call_target="tpu_custom_call" | custom-call | flops 1 | bytes 1 | tf_op jit(solution)/shard_map/pallas_call | solution.py:404
  74.4 2.7 %collective-permute-start.26 = (f32[40,128]{1,0:T(8,128)S(1)}, f32[40,128]{1,0:T(8,128)S(1)}, u32[]{:S(2)}, u32[]{:S(2)}) collective-permute-start(f32[40,128]{1,0:T(8,128)S(1)} %get-tuple-element.51), channel_id=1, source_target_pairs={{0,8},{1,9},{2,10},{3,11},{4,12},{5,13},{6,14},{7,15},{8,0},{9,1},... | collective-permute-start | bytes 61448 | tf_op jit(solution)/shard_map/ppermute | solution.py:22
  77.1 1.6 %collective-permute-done.27.refs_1_ = bf16[256,320]{1,0:T(8,128)(2,1)S(1)} collective-permute-done((bf16[256,320]{1,0:T(8,128)(2,1)S(1)}, bf16[256,320]{1,0:T(8,128)(2,1)S(1)}, u32[]{:S(2)}, u32[]{:S(2)}) %collective-permute-start.27) | collective-permute-done | bytes 163872 | tf_op jit(solution)/shard_map/ppermute | solution.py:22
  78.7 0.4 collective-permute-done.26.refs_1_
  79.1 2.8 %collective-permute-start.28 = (bf16[256,320]{1,0:T(8,128)(2,1)S(1)}, bf16[256,320]{1,0:T(8,128)(2,1)S(1)}, u32[]{:S(2)}, u32[]{:S(2)}) collective-permute-start(bf16[256,320]{1,0:T(8,128)(2,1)S(1)} %collective-permute-done.24.refs_0_), channel_id=1, source_target_pairs={{0,1},{1,0},{2,3},{3,2},{4,5},{5,4},{6,7},{7,6},{8,9},{9,8},{10,11... | collective-permute-start | bytes 491528 | tf_op jit(solution)/shard_map/ppermute | solution.py:22
  81.9 0.2 shard_map.86
  82.1 0.6 collective-permute-start.30
  82.8 2.9 %collective-permute-start.31 = (bf16[2,384]{1,0:T(2,128)(2,1)S(1)}, bf16[2,384]{1,0:T(2,128)(2,1)S(1)}, u32[]{:S(2)}, u32[]{:S(2)}) collective-permute-start(bf16[2,384]{1,0:T(2,128)(2,1)S(1)} %get-tuple-element.58), channel_id=1, source_target_pairs={{0,4},{1,5},{2,6},{3,7},{4,0},{5,1},{6,2},{7,3},{8,12},{9,13},{10,... | collective-permute-start | bytes 4616 | tf_op jit(solution)/shard_map/ppermute | solution.py:22
  85.7 0.9 collective-permute-start.32
  86.6 0.7 collective-permute-done.31.refs_2_
  87.2 2.9 %collective-permute-done.32.refs_3_ = bf16[2,384]{1,0:T(2,128)(2,1)S(1)} collective-permute-done((bf16[2,384]{1,0:T(2,128)(2,1)S(1)}, bf16[2,384]{1,0:T(2,128)(2,1)S(1)}, u32[]{:S(2)}, u32[]{:S(2)}) %collective-permute-start.32) | collective-permute-done | bytes 1568 | tf_op jit(solution)/shard_map/ppermute | solution.py:22
  90.2 1.2 %shard_map.87 = bf16[2,1280]{1,0:T(2,128)(2,1)} custom-call(s32[34]{0:T(128)S(1)} %stack.136.table.places, bf16[2,384]{1,0:T(2,128)(2,1)S(1)} %get-tuple-element.56.refs_0_, bf16[2,384]{1,0:T(2,128)(2,1)S(1)} %collective-permute-done.30.refs_1_, bf16[2,384]{1,0:T(2,128)(2,1)S(1)} %collective-permute-done.31.refs_2_, ...), custom_call_target="tpu_custom_call" | custom-call | flops 1 | bytes 1 | tf_op jit(solution)/shard_map/pallas_call | solution.py:458
  91.4 1.4 %shard_map.85 = bf16[128,1280]{1,0:T(8,128)(2,1)} custom-call(s32[34]{0:T(128)S(1)} %stack.136.table.places, bf16[256,320]{1,0:T(8,128)(2,1)S(1)} %collective-permute-done.24.refs_0_, bf16[256,320]{1,0:T(8,128)(2,1)S(1)} %collective-permute-done.27.refs_1_, bf16[256,320]{1,0:T(8,128)(2,1)S(1)} %collective-permute-done.28.refs_2_, ...), custom_call_target="tpu_custom_call" | custom-call | flops 1 | bytes 1 | tf_op jit(solution)/shard_map/pallas_call | solution.py:458
  (28 shorter events, 0.1 us)
Async XLA Ops:
  0.7 0.7 copy-start.2
  0.9 0.7 copy-start.3
  0.9 0.7 copy-start.4
  1.5 1.1 %copy-start = (bf16[80,3840]{1,0:T(8,128)(2,1)S(1)}, bf16[80,3840]{1,0:T(8,128)(2,1)}, u32[]{:S(2)}) copy-start(bf16[80,3840]{1,0:T(8,128)(2,1)} %refs_0_.1) | copy-start | bytes 1843204
  2.6 4.2 %copy-start.1 = (bf16[128,1280]{1,0:T(8,128)(2,1)S(1)}, bf16[128,1280]{1,0:T(8,128)(2,1)}, u32[]{:S(2)}) copy-start(bf16[128,1280]{1,0:T(8,128)(2,1)} %here.1) | copy-start | bytes 983044
  3.8 10.7 %collective-permute-start = (bf16[2,80,1024]{2,1,0:T(8,128)(2,1)S(1)}, bf16[2,80,1024]{2,1,0:T(8,128)(2,1)S(1)}, u32[]{:S(2)}, u32[]{:S(2)}) collective-permute-start(bf16[2,80,1024]{2,1,0:T(8,128)(2,1)S(1)} %get-tuple-element.31), channel_id=1, source_target_pairs={{0,2},{1,3},{2,0},{3,1},{4,6},{5,7},{6,4},{7,5},{8,10},{9,11},{10,... | collective-permute-start | bytes 983048 | tf_op jit(solution)/shard_map/ppermute | solution.py:22
  6.8 9.2 %collective-permute-start.4 = (bf16[128,1280]{1,0:T(8,128)(2,1)S(1)}, bf16[128,1280]{1,0:T(8,128)(2,1)S(1)}, u32[]{:S(2)}, u32[]{:S(2)}) collective-permute-start(bf16[128,1280]{1,0:T(8,128)(2,1)S(1)} %copy-done.1), channel_id=1, source_target_pairs={{0,4},{1,5},{2,6},{3,7},{4,0},{5,1},{6,2},{7,3},{8,12},{9,13},{10,... | collective-permute-start | bytes 983048 | tf_op jit(solution)/shard_map/ppermute | solution.py:22
  8.4 7.6 %collective-permute-start.3 = (bf16[128,1280]{1,0:T(8,128)(2,1)S(1)}, bf16[128,1280]{1,0:T(8,128)(2,1)S(1)}, u32[]{:S(2)}, u32[]{:S(2)}) collective-permute-start(bf16[128,1280]{1,0:T(8,128)(2,1)S(1)} %copy-done.1), channel_id=1, source_target_pairs={{4,8},{5,9},{6,10},{7,11},{8,4},{9,5},{10,6},{11,7},{20,24},{21,25... | collective-permute-start | bytes 983048 | tf_op jit(solution)/shard_map/ppermute | solution.py:22
  9.0 6.9 %collective-permute-start.2 = (bf16[2,80,1024]{2,1,0:T(8,128)(2,1)S(1)}, bf16[2,80,1024]{2,1,0:T(8,128)(2,1)S(1)}, u32[]{:S(2)}, u32[]{:S(2)}) collective-permute-start(bf16[2,80,1024]{2,1,0:T(8,128)(2,1)S(1)} %get-tuple-element.33.refs_0_.refs_7_), channel_id=1, source_target_pairs={{0,1},{1,0},{2,3},{3,2},{4,5},{5,4},{6,7},{7,6},{8,9},{9,8},{10,11... | collective-permute-start | bytes 983048 | tf_op jit(solution)/shard_map/ppermute | solution.py:22
  14.5 1.6 %collective-permute-start.5 = (bf16[2,80,1024]{2,1,0:T(8,128)(2,1)S(1)}, bf16[2,80,1024]{2,1,0:T(8,128)(2,1)S(1)}, u32[]{:S(2)}, u32[]{:S(2)}) collective-permute-start(bf16[2,80,1024]{2,1,0:T(8,128)(2,1)S(1)} %collective-permute-done.refs_2_.refs_9_), channel_id=1, source_target_pairs={{0,1},{1,0},{2,3},{3,2},{4,5},{5,4},{6,7},{7,6},{8,9},{9,8},{10,11... | collective-permute-start | bytes 983048 | tf_op jit(solution)/shard_map/ppermute | solution.py:22
  16.7 21.4 %collective-permute-start.7 = (bf16[128,1280]{1,0:T(8,128)(2,1)S(1)}, bf16[128,1280]{1,0:T(8,128)(2,1)S(1)}, u32[]{:S(2)}, u32[]{:S(2)}) collective-permute-start(bf16[128,1280]{1,0:T(8,128)(2,1)S(1)} %collective-permute-done.4.here), channel_id=1, source_target_pairs={{0,2},{1,3},{2,0},{3,1},{4,6},{5,7},{6,4},{7,5},{8,10},{9,11},{10,... | collective-permute-start | bytes 983048 | tf_op jit(solution)/shard_map/ppermute | solution.py:22
  18.5 20.1 %collective-permute-start.13 = (bf16[128,1280]{1,0:T(8,128)(2,1)S(1)}, bf16[128,1280]{1,0:T(8,128)(2,1)}, u32[]{:S(2)}, u32[]{:S(2)}) collective-permute-start(bf16[128,1280]{1,0:T(8,128)(2,1)S(1)} %collective-permute-done.3), channel_id=1, source_target_pairs={{0,4},{1,5},{2,6},{3,7},{4,0},{5,1},{6,2},{7,3},{8,12},{9,13},{10,... | collective-permute-start | bytes 983048 | tf_op jit(solution)/shard_map/ppermute | solution.py:22
  21.8 14.8 %collective-permute-start.6 = (bf16[80,1024]{1,0:T(8,128)(2,1)S(1)}, bf16[80,1024]{1,0:T(8,128)(2,1)S(1)}, u32[]{:S(2)}, u32[]{:S(2)}) collective-permute-start(bf16[80,1024]{1,0:T(8,128)(2,1)S(1)} %get-tuple-element.35), channel_id=1, source_target_pairs={{0,12},{1,13},{2,14},{3,15},{4,8},{5,9},{6,10},{7,11},{8,4},{9,5},... | collective-permute-start | bytes 491528 | tf_op jit(solution)/shard_map/ppermute | solution.py:22
  24.4 12.2 %collective-permute-start.10 = (bf16[80,1024]{1,0:T(8,128)(2,1)S(1)}, bf16[80,1024]{1,0:T(8,128)(2,1)S(1)}, u32[]{:S(2)}, u32[]{:S(2)}) collective-permute-start(bf16[80,1024]{1,0:T(8,128)(2,1)S(1)} %get-tuple-element.36.refs_0_), channel_id=1, source_target_pairs={{0,8},{1,9},{2,10},{3,11},{4,12},{5,13},{6,14},{7,15},{8,0},{9,1},... | collective-permute-start | bytes 491528 | tf_op jit(solution)/shard_map/ppermute | solution.py:22
  24.4 16.7 %copy-start.5 = (f32[1280]{0:T(1024)S(1)}, f32[1280]{0:T(1024)}, u32[]{:S(2)}) copy-start(f32[1280]{0:T(1024)} %param.7) | copy-start | bytes 15364
  24.4 16.8 %collective-permute-start.1 = (bf16[128,1280]{1,0:T(8,128)(2,1)S(1)}, bf16[128,1280]{1,0:T(8,128)(2,1)S(1)}, u32[]{:S(2)}, u32[]{:S(2)}) collective-permute-start(bf16[128,1280]{1,0:T(8,128)(2,1)S(1)} %copy-done.1), channel_id=1, source_target_pairs={{0,2},{1,3},{2,0},{3,1},{4,6},{5,7},{6,4},{7,5},{8,10},{9,11},{10,... | collective-permute-start | bytes 983048 | tf_op jit(solution)/shard_map/ppermute | solution.py:22
  36.6 7.2 %collective-permute-start.15 = (bf16[80,1024]{1,0:T(8,128)(2,1)S(1)}, bf16[80,1024]{1,0:T(8,128)(2,1)S(1)}, u32[]{:S(2)}, u32[]{:S(2)}) collective-permute-start(bf16[80,1024]{1,0:T(8,128)(2,1)S(1)} %get-tuple-element.35), channel_id=1, source_target_pairs={{0,4},{1,5},{2,6},{3,7},{4,0},{5,1},{6,2},{7,3},{8,12},{9,13},{10,... | collective-permute-start | bytes 491528 | tf_op jit(solution)/shard_map/ppermute | solution.py:22
  36.6 6.6 %collective-permute-start.11 = (bf16[80,1024]{1,0:T(8,128)(2,1)S(1)}, bf16[80,1024]{1,0:T(8,128)(2,1)S(1)}, u32[]{:S(2)}, u32[]{:S(2)}) collective-permute-start(bf16[80,1024]{1,0:T(8,128)(2,1)S(1)} %collective-permute-done.10.refs_2_.refs_15_), channel_id=1, source_target_pairs={{0,16},{16,0},{1,17},{17,1},{2,18},{18,2},{3,19},{19,3},{4,20},{20... | collective-permute-start | bytes 491528 | tf_op jit(solution)/shard_map/ppermute | solution.py:504
  38.1 5.6 %collective-permute-start.8 = (bf16[80,1024]{1,0:T(8,128)(2,1)S(1)}, bf16[80,1024]{1,0:T(8,128)(2,1)S(1)}, u32[]{:S(2)}, u32[]{:S(2)}) collective-permute-start(bf16[80,1024]{1,0:T(8,128)(2,1)S(1)} %collective-permute-done.6.refs_3_.refs_19_), channel_id=1, source_target_pairs={{0,16},{16,0},{1,17},{17,1},{2,18},{18,2},{3,19},{19,3},{4,20},{20... | collective-permute-start | bytes 491528 | tf_op jit(solution)/shard_map/ppermute | solution.py:504
  39.6 7.1 %collective-permute-start.14 = (bf16[128,1280]{1,0:T(8,128)(2,1)S(1)}, bf16[128,1280]{1,0:T(8,128)(2,1)S(1)}, u32[]{:S(2)}, u32[]{:S(2)}) collective-permute-start(bf16[128,1280]{1,0:T(8,128)(2,1)S(1)} %broadcast_select_fusion.here), channel_id=1, source_target_pairs={{0,2},{1,3},{2,0},{3,1},{4,6},{5,7},{6,4},{7,5},{8,10},{9,11},{10,... | collective-permute-start | bytes 983048 | tf_op jit(solution)/shard_map/ppermute | solution.py:22
  43.1 14.1 %collective-permute-start.12 = (bf16[256,1664]{1,0:T(8,128)(2,1)S(1)}, bf16[256,1664]{1,0:T(8,128)(2,1)S(1)}, u32[]{:S(2)}, u32[]{:S(2)}) collective-permute-start(bf16[256,1664]{1,0:T(8,128)(2,1)S(1)} %shard_map.80.refs_2_), channel_id=1, source_target_pairs={{0,1},{1,0},{2,3},{3,2},{4,5},{5,4},{6,7},{7,6},{8,9},{9,8},{10,11... | collective-permute-start | bytes 2555912 | tf_op jit(solution)/shard_map/ppermute | solution.py:22
  43.6 13.6 %collective-permute-start.9 = (bf16[256,1664]{1,0:T(8,128)(2,1)S(1)}, bf16[256,1664]{1,0:T(8,128)(2,1)S(1)}, u32[]{:S(2)}, u32[]{:S(2)}) collective-permute-start(bf16[256,1664]{1,0:T(8,128)(2,1)S(1)} %shard_map.78.refs_0_), channel_id=1, source_target_pairs={{0,1},{1,0},{2,3},{3,2},{4,5},{5,4},{6,7},{7,6},{8,9},{9,8},{10,11... | collective-permute-start | bytes 2555912 | tf_op jit(solution)/shard_map/ppermute | solution.py:22
  45.0 6.8 %collective-permute-start.16 = (bf16[80,1024]{1,0:T(8,128)(2,1)S(1)}, bf16[80,1024]{1,0:T(8,128)(2,1)S(1)}, u32[]{:S(2)}, u32[]{:S(2)}) collective-permute-start(bf16[80,1024]{1,0:T(8,128)(2,1)S(1)} %collective-permute-done.15.refs_1_.refs_11_), channel_id=1, source_target_pairs={{0,16},{16,0},{1,17},{17,1},{2,18},{18,2},{3,19},{19,3},{4,20},{20... | collective-permute-start | bytes 491528 | tf_op jit(solution)/shard_map/ppermute | solution.py:504
  51.9 5.4 %collective-permute-start.17 = (bf16[256,1280]{1,0:T(8,128)(2,1)S(1)}, bf16[256,1280]{1,0:T(8,128)(2,1)S(1)}, u32[]{:S(2)}, u32[]{:S(2)}) collective-permute-start(bf16[256,1280]{1,0:T(8,128)(2,1)S(1)} %shard_map.81.refs_4_), channel_id=1, source_target_pairs={{0,1},{1,0},{2,3},{3,2},{4,5},{5,4},{6,7},{7,6},{8,9},{9,8},{10,11... | collective-permute-start | bytes 1966088 | tf_op jit(solution)/shard_map/ppermute | solution.py:22
  51.9 2.3 %collective-permute-start.18 = (bf16[80,1024]{1,0:T(8,128)(2,1)S(1)}, bf16[80,1024]{1,0:T(8,128)(2,1)S(1)}, u32[]{:S(2)}, u32[]{:S(2)}) collective-permute-start(bf16[80,1024]{1,0:T(8,128)(2,1)S(1)} %collective-permute-done.15.refs_1_.refs_11_), channel_id=1, source_target_pairs={{0,1},{1,0},{2,3},{3,2},{4,5},{5,4},{6,7},{7,6},{8,9},{9,8},{10,11... | collective-permute-start | bytes 491528 | tf_op jit(solution)/shard_map/ppermute | solution.py:22
  52.4 2.1 %collective-permute-start.22 = (bf16[80,1024]{1,0:T(8,128)(2,1)S(1)}, bf16[80,1024]{1,0:T(8,128)(2,1)S(1)}, u32[]{:S(2)}, u32[]{:S(2)}) collective-permute-start(bf16[80,1024]{1,0:T(8,128)(2,1)S(1)} %collective-permute-done.6.refs_3_.refs_19_), channel_id=1, source_target_pairs={{0,1},{1,0},{2,3},{3,2},{4,5},{5,4},{6,7},{7,6},{8,9},{9,8},{10,11... | collective-permute-start | bytes 491528 | tf_op jit(solution)/shard_map/ppermute | solution.py:22
  54.2 1.4 %collective-permute-start.20 = (bf16[80,1024]{1,0:T(8,128)(2,1)S(1)}, bf16[80,1024]{1,0:T(8,128)(2,1)S(1)}, u32[]{:S(2)}, u32[]{:S(2)}) collective-permute-start(bf16[80,1024]{1,0:T(8,128)(2,1)S(1)} %collective-permute-done.10.refs_2_.refs_15_), channel_id=1, source_target_pairs={{0,1},{1,0},{2,3},{3,2},{4,5},{5,4},{6,7},{7,6},{8,9},{9,8},{10,11... | collective-permute-start | bytes 491528 | tf_op jit(solution)/shard_map/ppermute | solution.py:22
  54.4 1.4 %collective-permute-start.19 = (bf16[80,1024]{1,0:T(8,128)(2,1)S(1)}, bf16[80,1024]{1,0:T(8,128)(2,1)S(1)}, u32[]{:S(2)}, u32[]{:S(2)}) collective-permute-start(bf16[80,1024]{1,0:T(8,128)(2,1)S(1)} %collective-permute-done.16.refs_13_), channel_id=1, source_target_pairs={{0,1},{1,0},{2,3},{3,2},{4,5},{5,4},{6,7},{7,6},{8,9},{9,8},{10,11... | collective-permute-start | bytes 491528 | tf_op jit(solution)/shard_map/ppermute | solution.py:22
  55.6 1.4 %collective-permute-start.21 = (bf16[80,1024]{1,0:T(8,128)(2,1)S(1)}, bf16[80,1024]{1,0:T(8,128)(2,1)S(1)}, u32[]{:S(2)}, u32[]{:S(2)}) collective-permute-start(bf16[80,1024]{1,0:T(8,128)(2,1)S(1)} %collective-permute-done.11.refs_17_), channel_id=1, source_target_pairs={{0,1},{1,0},{2,3},{3,2},{4,5},{5,4},{6,7},{7,6},{8,9},{9,8},{10,11... | collective-permute-start | bytes 491528 | tf_op jit(solution)/shard_map/ppermute | solution.py:22
  55.8 1.4 %collective-permute-start.23 = (bf16[80,1024]{1,0:T(8,128)(2,1)S(1)}, bf16[80,1024]{1,0:T(8,128)(2,1)S(1)}, u32[]{:S(2)}, u32[]{:S(2)}) collective-permute-start(bf16[80,1024]{1,0:T(8,128)(2,1)S(1)} %collective-permute-done.8.refs_21_), channel_id=1, source_target_pairs={{0,1},{1,0},{2,3},{3,2},{4,5},{5,4},{6,7},{7,6},{8,9},{9,8},{10,11... | collective-permute-start | bytes 491528 | tf_op jit(solution)/shard_map/ppermute | solution.py:22
  70.6 2.5 %collective-permute-start.25 = (bf16[512,320]{1,0:T(8,128)(2,1)S(1)}, bf16[512,320]{1,0:T(8,128)(2,1)S(1)}, u32[]{:S(2)}, u32[]{:S(2)}) collective-permute-start(bf16[512,320]{1,0:T(8,128)(2,1)S(1)} %get-tuple-element.50.memory), channel_id=1, source_target_pairs={{0,1},{1,0},{2,3},{3,2},{4,5},{5,4},{6,7},{7,6},{8,9},{9,8},{10,11... | collective-permute-start | bytes 983048 | tf_op jit(solution)/shard_map/ppermute | solution.py:22
  70.9 7.8 %collective-permute-start.27 = (bf16[256,320]{1,0:T(8,128)(2,1)S(1)}, bf16[256,320]{1,0:T(8,128)(2,1)S(1)}, u32[]{:S(2)}, u32[]{:S(2)}) collective-permute-start(bf16[256,320]{1,0:T(8,128)(2,1)S(1)} %get-tuple-element.53), channel_id=1, source_target_pairs={{0,2},{1,6},{2,0},{3,4},{4,3},{5,7},{6,1},{7,5},{8,10},{9,14},{10,... | collective-permute-start | bytes 491528 | tf_op jit(solution)/shard_map/ppermute | solution.py:22
  72.4 6.7 %collective-permute-start.24 = (bf16[256,320]{1,0:T(8,128)(2,1)S(1)}, bf16[256,320]{1,0:T(8,128)(2,1)S(1)}, u32[]{:S(2)}, u32[]{:S(2)}) collective-permute-start(bf16[256,320]{1,0:T(8,128)(2,1)S(1)} %get-tuple-element.47), channel_id=1, source_target_pairs={{0,0},{1,4},{2,2},{3,6},{4,1},{5,5},{6,3},{7,7},{8,8},{9,12},{10,1... | collective-permute-start | bytes 491528 | tf_op jit(solution)/shard_map/ppermute | solution.py:22
  74.4 4.7 %collective-permute-start.26 = (f32[40,128]{1,0:T(8,128)S(1)}, f32[40,128]{1,0:T(8,128)S(1)}, u32[]{:S(2)}, u32[]{:S(2)}) collective-permute-start(f32[40,128]{1,0:T(8,128)S(1)} %get-tuple-element.51), channel_id=1, source_target_pairs={{0,8},{1,9},{2,10},{3,11},{4,12},{5,13},{6,14},{7,15},{8,0},{9,1},... | collective-permute-start | bytes 61448 | tf_op jit(solution)/shard_map/ppermute | solution.py:22
  79.1 12.3 %collective-permute-start.28 = (bf16[256,320]{1,0:T(8,128)(2,1)S(1)}, bf16[256,320]{1,0:T(8,128)(2,1)S(1)}, u32[]{:S(2)}, u32[]{:S(2)}) collective-permute-start(bf16[256,320]{1,0:T(8,128)(2,1)S(1)} %collective-permute-done.24.refs_0_), channel_id=1, source_target_pairs={{0,1},{1,0},{2,3},{3,2},{4,5},{5,4},{6,7},{7,6},{8,9},{9,8},{10,11... | collective-permute-start | bytes 491528 | tf_op jit(solution)/shard_map/ppermute | solution.py:22
  81.9 9.5 %collective-permute-start.29 = (bf16[256,320]{1,0:T(8,128)(2,1)S(1)}, bf16[256,320]{1,0:T(8,128)(2,1)S(1)}, u32[]{:S(2)}, u32[]{:S(2)}) collective-permute-start(bf16[256,320]{1,0:T(8,128)(2,1)S(1)} %collective-permute-done.27.refs_1_), channel_id=1, source_target_pairs={{0,1},{1,0},{2,3},{3,2},{4,5},{5,4},{6,7},{7,6},{8,9},{9,8},{10,11... | collective-permute-start | bytes 491528 | tf_op jit(solution)/shard_map/ppermute | solution.py:22
  82.1 4.4 %collective-permute-start.30 = (bf16[2,384]{1,0:T(2,128)(2,1)S(1)}, bf16[2,384]{1,0:T(2,128)(2,1)S(1)}, u32[]{:S(2)}, u32[]{:S(2)}) collective-permute-start(bf16[2,384]{1,0:T(2,128)(2,1)S(1)} %get-tuple-element.57), channel_id=1, source_target_pairs={{0,2},{1,3},{2,0},{3,1},{4,6},{5,7},{6,4},{7,5},{8,10},{9,11},{10,... | collective-permute-start | bytes 4616 | tf_op jit(solution)/shard_map/ppermute | solution.py:22
  82.8 4.5 %collective-permute-start.31 = (bf16[2,384]{1,0:T(2,128)(2,1)S(1)}, bf16[2,384]{1,0:T(2,128)(2,1)S(1)}, u32[]{:S(2)}, u32[]{:S(2)}) collective-permute-start(bf16[2,384]{1,0:T(2,128)(2,1)S(1)} %get-tuple-element.58), channel_id=1, source_target_pairs={{0,4},{1,5},{2,6},{3,7},{4,0},{5,1},{6,2},{7,3},{8,12},{9,13},{10,... | collective-permute-start | bytes 4616 | tf_op jit(solution)/shard_map/ppermute | solution.py:22
  85.7 4.5 %collective-permute-start.32 = (bf16[2,384]{1,0:T(2,128)(2,1)S(1)}, bf16[2,384]{1,0:T(2,128)(2,1)S(1)}, u32[]{:S(2)}, u32[]{:S(2)}) collective-permute-start(bf16[2,384]{1,0:T(2,128)(2,1)S(1)} %get-tuple-element.59), channel_id=1, source_target_pairs={{0,6},{1,7},{2,4},{3,5},{4,2},{5,3},{6,0},{7,1},{8,14},{9,15},{10,... | collective-permute-start | bytes 4616 | tf_op jit(solution)/shard_map/ppermute | solution.py:22

commit v10 on v9

--- a/solution.py
+++ b/solution.py
@@ -170,7 +170,10 @@
 
 
 def prepare_kernel(table, *refs):
-    parts, (ids, tokens, asked) = refs[:-3], refs[-3:]
+    parts, (ids, tokens, asked, joined) = refs[:-4], refs[-4:]
+    rows = joined.shape[0] // 3
+    for i in range(3):
+        joined[rows * i : rows * i + rows, :] = parts[i + 1][...]
     first, x, core, z = table[13], table[6], table[7], table[14]
     count = asked.shape[0]
     ids[...] = jnp.zeros_like(ids)
@@ -208,9 +211,10 @@
             jax.ShapeDtypeStruct((8, 1536), F32),
             jax.ShapeDtypeStruct((5 * count, GROUP), F32),
             jax.ShapeDtypeStruct((count, HD), F32),
+            jax.ShapeDtypeStruct((3 * parts[0].shape[0], 1024), BF),
         ),
         in_specs=[SMEM] + [VMEM] * len(parts),
-        out_specs=(VMEM,) * 3,
+        out_specs=(VMEM,) * 4,
         cost_estimate=CHEAP,
         compiler_params=pltpu.CompilerParams(vmem_limit_bytes=8 * 1024 * 1024),
     )(table, *parts)
@@ -483,10 +487,9 @@
     table += [group, p, x, c]
     table += [512 * (p - c + 1), 512 * (2 - p - c), 1024 * c, 0, x == moved, 4 * quarter - 4, z]
     sources = [me, me ^ 1, me ^ 2, me ^ 3] if direct else [jnp.int32(0)]
-    for turn in (1, 2, 3) if direct else ():
-        column = 4 * (z ^ turn) + c
-        for side in (2 * moved, 2 - 2 * moved):
-            sources += [column + side, (column ^ 1) + side]
+    for side in (2 * moved, 2 - 2 * moved) if direct else ():
+        for core in (c, 1 - c):
+            sources += [4 * (z ^ turn) + side + core for turn in (1, 2, 3)]
     table = scalars(table + sources + [4 * quarter, 4 * (quarter ^ 1), me])
     base = 15 + len(sources)
 
@@ -515,21 +518,15 @@
         pair_x = swap(after(pair, ready[0]), n, 2)
         halo = jnp.where((z == 1) | (z == 2), near, relayed)
         halo_x = swap(after(halo, pair_x), n, 2)
-        ids, tokens, asked = prepare(table, [ready[0], here[1], here[2], here[3]], n)
-        traded = {3: trade(after(here[3], pair_x)), 2: trade(after(here[2], here[3]))}
-        traded[1] = trade(after(here[1], ids))
+        ids, tokens, asked, joined = prepare(table, [ready[0], here[1], here[2], here[3]], n)
+        traded = trade(joined)
         own_half = norm_half(table, gain, stem, stem_x)
         pair_half = norm_half(table, gain, pair, pair_x)
         halo_half = norm_half(table, gain, halo, halo_x, False)
-        layered = [
-            own_half, swap(after(own_half, traded[3]), n, 1),
-            pair_half, swap(after(pair_half, traded[2]), n, 1),
-            halo_half, swap(after(halo_half, traded[1]), n, 1),
-        ]
-        weights = [mine, mine_c, across, across_c]
-        for turn in (1, 2, 3):
-            for part in (here[turn], traded[turn]):
-                weights += [part, swap(part, n, 1)]
+        own_c, pair_c = swap(own_half, n, 1), swap(pair_half, n, 1)
+        layered = [own_half, own_c, pair_half, pair_c, halo_half, swap(halo_half, n, 1)]
+        weights = [mine, mine_c, across, across_c, joined, swap(joined, n, 1)]
+        weights += [traded, swap(after(traded, own_c, pair_c), n, 1)]
     else:
         stem_x = swap(stem, n, 2)
         far = swap(near, n, 4)
@@ -579,6 +576,7 @@
 
     final = merge(owned)
     final = [final[0]] + [swap(final[i], n, 2 * i) for i in (1, 2, 3)]
+    final[0] = after(final[0], memory)
     cross_out = gather_groups(5, 2, table, final)
     return (memory, cross_out)
 

time: 93 us -> 92.5 us (level)
  starting transfers between devices: 33.6 us -> 31.2 us
  waiting for transfers between devices: 31.9 us -> 33.8 us
    ppermute x30 -> x26, waiting for transfers between devices: 27.4 us -> 33.8 us  [send(): return lax.ppermute(block, 'tm', route)]
    ppermute x3 -> x1, waiting for transfers between devices: 4.56 us -> 0.01 us  [trade(): return lax.ppermute(block, 'utt', [(u, u ^ 1) for u in range(utts)])]
    ppermute x3 -> x1, starting transfers between devices: 3.61 us -> 1.58 us  [trade(): return lax.ppermute(block, 'utt', [(u, u ^ 1) for u in range(utts)])]
    ppermute x30 -> x26, starting transfers between devices: 30 us -> 29.6 us  [send(): return lax.ppermute(block, 'tm', route)]
  transfers between devices with their start and end apart: 33 -> 27, of which waited for: 17 -> 12; matrix products, arithmetic and copies ran while one was open for 1% -> 1% of each run, Pallas kernels for 8% -> 8%
where the time goes in v10:
time: 92.5 us; the launch traced here: 92.3 us
  waiting for transfers between devices  33.8 us (37%)
  starting transfers between devices  31.2 us (34%)
  Pallas kernels  23.5 us (25%)
  local copies, waits for them, and re-layouts  1.87 us (2%)
  other arithmetic  1.03 us (1%)
    ppermute x26, waiting for transfers between devices, send(): return lax.ppermute(block, 'tm', route)  33.8 us
    ppermute x26, starting transfers between devices, send(): return lax.ppermute(block, 'tm', route)  29.6 us
    pallas_call x1, Pallas kernels, encoder(): pl.pallas_call(functools.partial(encoder_kernel, len(parts), depth), out_...  13.3 us
    pallas_call x3, Pallas kernels, norm_half(): pl.pallas_call(norm_kernel, out_shape=jax.ShapeDtypeStruct((256, 1664 if...  2.93 us
    pallas_call x2, Pallas kernels, gather_groups(): pl.pallas_call(functools.partial(gather_kernel, side, rows), out_shape=ja...  2.59 us
  transfers between devices with their start and end apart: 27, of which 12 were waited for; matrix products, arithmetic and copies ran while one was open for 1% of the time, Pallas kernels for 8%

profile of v10, /device:TPU:0, one launch (start us, length us, event | category | flops | bytes accessed | tf_op | source)
XLA Modules:
  0.0 92.3 jit_solution(11300777393452518764)
XLA Ops:
  0.7 0.0 copy-start.2
  0.7 0.1 stack.136.table.places
  0.8 0.0 copy-start.3
  0.9 0.0 copy-start.4
  0.9 0.5 copy-done.2
  1.4 0.1 copy-done.3
  1.5 1.1 %copy-done = bf16[80,3840]{1,0:T(8,128)(2,1)S(1)} copy-done((bf16[80,3840]{1,0:T(8,128)(2,1)S(1)}, bf16[80,3840]{1,0:T(8,128)(2,1)}, u32[]{:S(2)}) %copy-start) | copy-done | bytes 614424
  2.6 1.1 %shard_map.77 = (bf16[2,80,1024]{2,1,0:T(8,128)(2,1)S(1)}, bf16[2,80,1024]{2,1,0:T(8,128)(2,1)S(1)}) custom-call(s32[34]{0:T(128)S(1)} %stack.136.table.places, bf16[80,3840]{1,0:T(8,128)(2,1)S(1)} %copy-done, bf16[2,1280]{1,0:T(2,128)(2,1)S(1)} %copy-done.2, s32[2,16]{1,0:T(2,128)S(1)} %copy-done.3, s32[1,128]{1,0:T(1,128)S(1)} %bitcast.33), custom_call_target="tpu_custom_call" | custom-call | flops 1 | bytes 1 | tf_op jit(solution)/shard_map/pallas_call | solution.py:98
  3.8 3.0 %collective-permute-start = (bf16[2,80,1024]{2,1,0:T(8,128)(2,1)S(1)}, bf16[2,80,1024]{2,1,0:T(8,128)(2,1)S(1)}, u32[]{:S(2)}, u32[]{:S(2)}) collective-permute-start(bf16[2,80,1024]{2,1,0:T(8,128)(2,1)S(1)} %get-tuple-element.28), channel_id=1, source_target_pairs={{0,2},{1,3},{2,0},{3,1},{4,6},{5,7},{6,4},{7,5},{8,10},{9,11},{10,... | collective-permute-start | bytes 983048 | tf_op jit(solution)/shard_map/ppermute | solution.py:22
  6.8 1.4 %collective-permute-start.5 = (bf16[128,1280]{1,0:T(8,128)(2,1)S(1)}, bf16[128,1280]{1,0:T(8,128)(2,1)}, u32[]{:S(2)}, u32[]{:S(2)}) collective-permute-start(bf16[128,1280]{1,0:T(8,128)(2,1)S(1)} %copy-done.1), channel_id=1, source_target_pairs={{4,8},{5,9},{6,10},{7,11},{8,4},{9,5},{10,6},{11,7},{20,24},{21,25... | collective-permute-start | bytes 983048 | tf_op jit(solution)/shard_map/ppermute | solution.py:22
  8.2 3.7 %collective-permute-start.3 = (bf16[128,1280]{1,0:T(8,128)(2,1)S(1)}, bf16[128,1280]{1,0:T(8,128)(2,1)S(1)}, u32[]{:S(2)}, u32[]{:S(2)}) collective-permute-start(bf16[128,1280]{1,0:T(8,128)(2,1)S(1)} %copy-done.1), channel_id=1, source_target_pairs={{0,4},{1,5},{2,6},{3,7},{4,0},{5,1},{6,2},{7,3},{8,12},{9,13},{10,... | collective-permute-start | bytes 983048 | tf_op jit(solution)/shard_map/ppermute | solution.py:22
  11.9 2.6 %collective-permute-done.refs_2_.refs_9_ = bf16[2,80,1024]{2,1,0:T(8,128)(2,1)S(1)} collective-permute-done((bf16[2,80,1024]{2,1,0:T(8,128)(2,1)S(1)}, bf16[2,80,1024]{2,1,0:T(8,128)(2,1)S(1)}, u32[]{:S(2)}, u32[]{:S(2)}) %collective-permute-start) | collective-permute-done | bytes 327712 | tf_op jit(solution)/shard_map/ppermute | solution.py:22
  14.5 0.0 collective-permute-start.6
  14.5 1.7 %collective-permute-start.1 = (bf16[128,1280]{1,0:T(8,128)(2,1)S(1)}, bf16[128,1280]{1,0:T(8,128)(2,1)S(1)}, u32[]{:S(2)}, u32[]{:S(2)}) collective-permute-start(bf16[128,1280]{1,0:T(8,128)(2,1)S(1)} %copy-done.1), channel_id=1, source_target_pairs={{0,2},{1,3},{2,0},{3,1},{4,6},{5,7},{6,4},{7,5},{8,10},{9,11},{10,... | collective-permute-start | bytes 983048 | tf_op jit(solution)/shard_map/ppermute | solution.py:22
  16.2 2.8 %collective-permute-done.3.here = bf16[128,1280]{1,0:T(8,128)(2,1)S(1)} collective-permute-done((bf16[128,1280]{1,0:T(8,128)(2,1)S(1)}, bf16[128,1280]{1,0:T(8,128)(2,1)S(1)}, u32[]{:S(2)}, u32[]{:S(2)}) %collective-permute-start.3) | collective-permute-done | bytes 327712 | tf_op jit(solution)/shard_map/ppermute | solution.py:22
  19.1 0.0 collective-permute-done.4.refs_1_.refs_8_
  19.1 0.0 collective-permute-done.6.refs_3_.refs_10_
  19.1 0.6 shard_map.79
  19.7 0.6 collective-permute-start.7
  20.3 1.7 %collective-permute-start.9 = (bf16[128,1280]{1,0:T(8,128)(2,1)}, bf16[128,1280]{1,0:T(8,128)(2,1)}, u32[]{:S(2)}, u32[]{:S(2)}) collective-permute-start(bf16[128,1280]{1,0:T(8,128)(2,1)} %collective-permute-done.5), channel_id=1, source_target_pairs={{0,4},{1,5},{2,6},{3,7},{4,0},{5,1},{6,2},{7,3},{8,12},{9,13},{10,... | collective-permute-start | bytes 983048 | tf_op jit(solution)/shard_map/ppermute | solution.py:22
  22.0 1.4 %collective-permute-start.14 = (bf16[80,1024]{1,0:T(8,128)(2,1)S(1)}, bf16[80,1024]{1,0:T(8,128)(2,1)S(1)}, u32[]{:S(2)}, u32[]{:S(2)}) collective-permute-start(bf16[80,1024]{1,0:T(8,128)(2,1)S(1)} %get-tuple-element.36), channel_id=1, source_target_pairs={{0,12},{1,13},{2,14},{3,15},{4,8},{5,9},{6,10},{7,11},{8,4},{9,5},... | collective-permute-start | bytes 491528 | tf_op jit(solution)/shard_map/ppermute | solution.py:22
  23.4 0.0 collective-permute-start.12
  23.4 1.6 %collective-permute-done.1.across = bf16[128,1280]{1,0:T(8,128)(2,1)S(1)} collective-permute-done((bf16[128,1280]{1,0:T(8,128)(2,1)S(1)}, bf16[128,1280]{1,0:T(8,128)(2,1)S(1)}, u32[]{:S(2)}, u32[]{:S(2)}) %collective-permute-start.1) | collective-permute-done | bytes 327712 | tf_op jit(solution)/shard_map/ppermute | solution.py:22
  25.0 2.8 %collective-permute-start.13 = (bf16[80,1024]{1,0:T(8,128)(2,1)S(1)}, bf16[80,1024]{1,0:T(8,128)(2,1)S(1)}, u32[]{:S(2)}, u32[]{:S(2)}) collective-permute-start(bf16[80,1024]{1,0:T(8,128)(2,1)S(1)} %get-tuple-element.32.refs_0_), channel_id=1, source_target_pairs={{0,8},{1,9},{2,10},{3,11},{4,12},{5,13},{6,14},{7,15},{8,0},{9,1},... | collective-permute-start | bytes 491528 | tf_op jit(solution)/shard_map/ppermute | solution.py:22
  27.8 1.0 %shard_map.78.refs_0_ = bf16[256,1664]{1,0:T(8,128)(2,1)S(1)} custom-call(s32[34]{0:T(128)S(1)} %stack.136.table.places, f32[1,1280]{1,0:T(1,128)S(1)} %reshape.10.gain, bf16[128,1280]{1,0:T(8,128)(2,1)S(1)} %copy-done.1, bf16[128,1280]{1,0:T(8,128)(2,1)S(1)} %collective-permute-done.1.across), custom_call_target="tpu_custom_call" | custom-call | flops 1 | bytes 1 | tf_op jit(solution)/shard_map/pallas_call | solution.py:162
  28.8 6.9 %collective-permute-done.14.refs_3_ = bf16[80,1024]{1,0:T(8,128)(2,1)S(1)} collective-permute-done((bf16[80,1024]{1,0:T(8,128)(2,1)S(1)}, bf16[80,1024]{1,0:T(8,128)(2,1)S(1)}, u32[]{:S(2)}, u32[]{:S(2)}) %collective-permute-start.14) | collective-permute-done | bytes 163872 | tf_op jit(solution)/shard_map/ppermute | solution.py:22
  35.7 3.3 %collective-permute-done.12.refs_1_ = bf16[80,1024]{1,0:T(8,128)(2,1)S(1)} collective-permute-done((bf16[80,1024]{1,0:T(8,128)(2,1)S(1)}, bf16[80,1024]{1,0:T(8,128)(2,1)S(1)}, u32[]{:S(2)}, u32[]{:S(2)}) %collective-permute-start.12) | collective-permute-done | bytes 163872 | tf_op jit(solution)/shard_map/ppermute | solution.py:22
  39.0 0.0 collective-permute-done.13.refs_2_
  39.0 1.3 %shard_map.82 = (f32[8,1536]{1,0:T(8,128)S(1)}, f32[80,320]{1,0:T(8,128)S(1)}, f32[16,64]{1,0:T(8,128)S(1)}, bf16[240,1024]{1,0:T(8,128)(2,1)S(1)}) custom-call(s32[34]{0:T(128)S(1)} %stack.136.table.places, bf16[80,1024]{1,0:T(8,128)(2,1)S(1)} %get-tuple-element.32.refs_0_, bf16[80,1024]{1,0:T(8,128)(2,1)S(1)} %collective-permute-done.12.refs_1_, ...), custom_call_target="tpu_custom_call" | custom-call | flops 1 | bytes 1 | tf_op jit(solution)/shard_map/pallas_call | solution.py:208
  40.3 1.6 %collective-permute-start.16 = (bf16[240,1024]{1,0:T(8,128)(2,1)S(1)}, bf16[240,1024]{1,0:T(8,128)(2,1)S(1)}, u32[]{:S(2)}, u32[]{:S(2)}) collective-permute-start(bf16[240,1024]{1,0:T(8,128)(2,1)S(1)} %get-tuple-element.38.refs_11_), channel_id=1, source_target_pairs={{0,16},{16,0},{1,17},{17,1},{2,18},{18,2},{3,19},{19,3},{4,20},{20... | collective-permute-start | bytes 1474568 | tf_op jit(solution)/shard_map/ppermute | solution.py:507
  41.9 0.0 collective-permute-done.7.across
  41.9 1.0 %shard_map.80.refs_2_ = bf16[256,1664]{1,0:T(8,128)(2,1)S(1)} custom-call(s32[34]{0:T(128)S(1)} %stack.136.table.places, f32[1,1280]{1,0:T(1,128)S(1)} %reshape.10.gain, bf16[128,1280]{1,0:T(8,128)(2,1)S(1)} %collective-permute-done.3.here, bf16[128,1280]{1,0:T(8,128)(2,1)S(1)} %collective-permute-done.7.across), custom_call_target="tpu_custom_call" | custom-call | flops 1 | bytes 1 | tf_op jit(solution)/shard_map/pallas_call | solution.py:162
  42.9 0.1 collective-permute-start.8
  43.0 1.0 %broadcast_select_fusion.here = bf16[128,1280]{1,0:T(8,128)(2,1)S(1)} fusion(bf16[128,1280]{1,0:T(8,128)(2,1)} %collective-permute-done.5, bf16[128,1280]{1,0:T(8,128)(2,1)} %collective-permute-done.9, pred[]{:T(512)S(6)} %or.3), kind=kLoop, calls=%fused_computation | loop fusion | flops 163840 | bytes 983041 | tf_op jit(solution)/shard_map/jit(_where)/select_n | solution.py:519
  44.0 1.6 %collective-permute-start.10 = (bf16[128,1280]{1,0:T(8,128)(2,1)S(1)}, bf16[128,1280]{1,0:T(8,128)(2,1)S(1)}, u32[]{:S(2)}, u32[]{:S(2)}) collective-permute-start(bf16[128,1280]{1,0:T(8,128)(2,1)S(1)} %broadcast_select_fusion.here), channel_id=1, source_target_pairs={{0,2},{1,3},{2,0},{3,1},{4,6},{5,7},{6,4},{7,5},{8,10},{9,11},{10,... | collective-permute-start | bytes 983048 | tf_op jit(solution)/shard_map/ppermute | solution.py:22
  45.6 8.6 %collective-permute-done.10.across = bf16[128,1280]{1,0:T(8,128)(2,1)S(1)} collective-permute-done((bf16[128,1280]{1,0:T(8,128)(2,1)S(1)}, bf16[128,1280]{1,0:T(8,128)(2,1)S(1)}, u32[]{:S(2)}, u32[]{:S(2)}) %collective-permute-start.10) | collective-permute-done | bytes 327712 | tf_op jit(solution)/shard_map/ppermute | solution.py:22
  54.2 1.0 %shard_map.81.refs_4_ = bf16[256,1280]{1,0:T(8,128)(2,1)S(1)} custom-call(s32[34]{0:T(128)S(1)} %stack.136.table.places, f32[1,1280]{1,0:T(1,128)S(1)} %reshape.10.gain, bf16[128,1280]{1,0:T(8,128)(2,1)S(1)} %broadcast_select_fusion.here, bf16[128,1280]{1,0:T(8,128)(2,1)S(1)} %collective-permute-done.10.across), custom_call_target="tpu_custom_call" | custom-call | flops 1 | bytes 1 | tf_op jit(solution)/shard_map/pallas_call | solution.py:162
  55.2 0.1 collective-permute-start.11
  55.2 0.5 collective-permute-start.15
  55.7 0.0 collective-permute-done.16.refs_13_
  55.7 0.0 collective-permute-done.2.refs_1_
  55.7 0.0 collective-permute-done.8.refs_3_
  55.7 0.1 collective-permute-start.17
  55.9 2.1 %collective-permute-done.15.refs_12_ = bf16[240,1024]{1,0:T(8,128)(2,1)S(1)} collective-permute-done((bf16[240,1024]{1,0:T(8,128)(2,1)S(1)}, bf16[240,1024]{1,0:T(8,128)(2,1)S(1)}, u32[]{:S(2)}, u32[]{:S(2)}) %collective-permute-start.15) | collective-permute-done | bytes 491552 | tf_op jit(solution)/shard_map/ppermute | solution.py:22
  58.0 0.7 collective-permute-done.17.refs_14_
  58.7 13.3 %shard_map.83 = (bf16[512,320]{1,0:T(8,128)(2,1)S(1)}, bf16[256,320]{1,0:T(8,128)(2,1)S(1)}, bf16[256,320]{1,0:T(8,128)(2,1)S(1)}) custom-call(s32[34]{0:T(128)S(1)} %stack.136.table.places, bf16[256,1664]{1,0:T(8,128)(2,1)S(1)} %shard_map.78.refs_0_, bf16[256,1664]{1,0:T(8,128)(2,1)S(1)} %collective-permute-done.2.refs_1_, ...), custom_call_target="tpu_custom_call" | custom-call | flops 1 | bytes 1 | tf_op jit(solution)/shard_map/pallas_call | solution.py:342
  72.0 0.2 collective-permute-start.19
  72.2 1.5 %collective-permute-start.21 = (bf16[256,320]{1,0:T(8,128)(2,1)S(1)}, bf16[256,320]{1,0:T(8,128)(2,1)S(1)}, u32[]{:S(2)}, u32[]{:S(2)}) collective-permute-start(bf16[256,320]{1,0:T(8,128)(2,1)S(1)} %get-tuple-element.46), channel_id=1, source_target_pairs={{0,2},{1,6},{2,0},{3,4},{4,3},{5,7},{6,1},{7,5},{8,10},{9,14},{10,... | collective-permute-start | bytes 491528 | tf_op jit(solution)/shard_map/ppermute | solution.py:22
  73.7 0.7 collective-permute-start.18
  74.4 0.0 collective-permute-done.19.beside
  74.4 1.3 %shard_map.84 = (f32[40,128]{1,0:T(8,128)S(1)}, f32[40,128]{1,0:T(8,128)S(1)}) custom-call(s32[34]{0:T(128)S(1)} %stack.136.table.places, f32[80,320]{1,0:T(8,128)S(1)} %get-tuple-element.41.tokens, f32[16,64]{1,0:T(8,128)S(1)} %get-tuple-element.42.asked, bf16[512,320]{1,0:T(8,128)(2,1)S(1)} %get-tuple-element.43.memory, ...), custom_call_target="tpu_custom_call" | custom-call | flops 1 | bytes 1 | tf_op jit(solution)/shard_map/pallas_call | solution.py:408
  75.7 2.7 %collective-permute-start.20 = (f32[40,128]{1,0:T(8,128)S(1)}, f32[40,128]{1,0:T(8,128)S(1)}, u32[]{:S(2)}, u32[]{:S(2)}) collective-permute-start(f32[40,128]{1,0:T(8,128)S(1)} %get-tuple-element.44), channel_id=1, source_target_pairs={{0,8},{1,9},{2,10},{3,11},{4,12},{5,13},{6,14},{7,15},{8,0},{9,1},... | collective-permute-start | bytes 61448 | tf_op jit(solution)/shard_map/ppermute | solution.py:22
  78.4 1.6 %collective-permute-done.21.refs_1_ = bf16[256,320]{1,0:T(8,128)(2,1)S(1)} collective-permute-done((bf16[256,320]{1,0:T(8,128)(2,1)S(1)}, bf16[256,320]{1,0:T(8,128)(2,1)S(1)}, u32[]{:S(2)}, u32[]{:S(2)}) %collective-permute-start.21) | collective-permute-done | bytes 163872 | tf_op jit(solution)/shard_map/ppermute | solution.py:22
  80.0 0.6 collective-permute-done.20.refs_1_
  80.6 1.6 %collective-permute-start.22 = (bf16[256,320]{1,0:T(8,128)(2,1)S(1)}, bf16[256,320]{1,0:T(8,128)(2,1)S(1)}, u32[]{:S(2)}, u32[]{:S(2)}) collective-permute-start(bf16[256,320]{1,0:T(8,128)(2,1)S(1)} %collective-permute-done.18.refs_0_), channel_id=1, source_target_pairs={{0,1},{1,0},{2,3},{3,2},{4,5},{5,4},{6,7},{7,6},{8,9},{9,8},{10,11... | collective-permute-start | bytes 491528 | tf_op jit(solution)/shard_map/ppermute | solution.py:22
  82.2 0.0 collective-permute-start.23
  82.2 0.2 shard_map.86
  82.4 1.4 %collective-permute-start.24 = (bf16[2,384]{1,0:T(2,128)(2,1)S(1)}, bf16[2,384]{1,0:T(2,128)(2,1)S(1)}, u32[]{:S(2)}, u32[]{:S(2)}) collective-permute-start(bf16[2,384]{1,0:T(2,128)(2,1)S(1)} %get-tuple-element.51), channel_id=1, source_target_pairs={{0,2},{1,3},{2,0},{3,1},{4,6},{5,7},{6,4},{7,5},{8,10},{9,11},{10,... | collective-permute-start | bytes 4616 | tf_op jit(solution)/shard_map/ppermute | solution.py:22
  83.8 2.7 %collective-permute-start.25 = (bf16[2,384]{1,0:T(2,128)(2,1)S(1)}, bf16[2,384]{1,0:T(2,128)(2,1)S(1)}, u32[]{:S(2)}, u32[]{:S(2)}) collective-permute-start(bf16[2,384]{1,0:T(2,128)(2,1)S(1)} %get-tuple-element.52), channel_id=1, source_target_pairs={{0,4},{1,5},{2,6},{3,7},{4,0},{5,1},{6,2},{7,3},{8,12},{9,13},{10,... | collective-permute-start | bytes 4616 | tf_op jit(solution)/shard_map/ppermute | solution.py:22
  86.6 0.1 collective-permute-start.26
  86.7 1.4 %shard_map.85 = bf16[128,1280]{1,0:T(8,128)(2,1)} custom-call(s32[34]{0:T(128)S(1)} %stack.136.table.places, bf16[256,320]{1,0:T(8,128)(2,1)S(1)} %collective-permute-done.18.refs_0_, bf16[256,320]{1,0:T(8,128)(2,1)S(1)} %collective-permute-done.21.refs_1_, bf16[256,320]{1,0:T(8,128)(2,1)S(1)} %collective-permute-done.22.refs_2_, ...), custom_call_target="tpu_custom_call" | custom-call | flops 1 | bytes 1 | tf_op jit(solution)/shard_map/pallas_call | solution.py:462
  88.0 0.1 collective-permute-done.25.refs_2_
  88.1 2.9 %collective-permute-done.26.refs_3_ = bf16[2,384]{1,0:T(2,128)(2,1)S(1)} collective-permute-done((bf16[2,384]{1,0:T(2,128)(2,1)S(1)}, bf16[2,384]{1,0:T(2,128)(2,1)S(1)}, u32[]{:S(2)}, u32[]{:S(2)}) %collective-permute-start.26) | collective-permute-done | bytes 1568 | tf_op jit(solution)/shard_map/ppermute | solution.py:22
  91.0 1.2 %shard_map.87 = bf16[2,1280]{1,0:T(2,128)(2,1)} custom-call(s32[34]{0:T(128)S(1)} %stack.136.table.places, bf16[2,384]{1,0:T(2,128)(2,1)S(1)} %get-tuple-element.50.refs_0_, bf16[2,384]{1,0:T(2,128)(2,1)S(1)} %collective-permute-done.24.refs_1_, bf16[2,384]{1,0:T(2,128)(2,1)S(1)} %collective-permute-done.25.refs_2_, ...), custom_call_target="tpu_custom_call" | custom-call | flops 1 | bytes 1 | tf_op jit(solution)/shard_map/pallas_call | solution.py:462
  (16 shorter events, 0.0 us)
Async XLA Ops:
  0.7 0.7 copy-start.2
  0.8 0.7 copy-start.3
  0.9 0.7 copy-start.4
  1.5 1.1 %copy-start = (bf16[80,3840]{1,0:T(8,128)(2,1)S(1)}, bf16[80,3840]{1,0:T(8,128)(2,1)}, u32[]{:S(2)}) copy-start(bf16[80,3840]{1,0:T(8,128)(2,1)} %refs_0_.1) | copy-start | bytes 1843204
  2.6 4.2 %copy-start.1 = (bf16[128,1280]{1,0:T(8,128)(2,1)S(1)}, bf16[128,1280]{1,0:T(8,128)(2,1)}, u32[]{:S(2)}) copy-start(bf16[128,1280]{1,0:T(8,128)(2,1)} %here.1) | copy-start | bytes 983044
  3.8 10.7 %collective-permute-start = (bf16[2,80,1024]{2,1,0:T(8,128)(2,1)S(1)}, bf16[2,80,1024]{2,1,0:T(8,128)(2,1)S(1)}, u32[]{:S(2)}, u32[]{:S(2)}) collective-permute-start(bf16[2,80,1024]{2,1,0:T(8,128)(2,1)S(1)} %get-tuple-element.28), channel_id=1, source_target_pairs={{0,2},{1,3},{2,0},{3,1},{4,6},{5,7},{6,4},{7,5},{8,10},{9,11},{10,... | collective-permute-start | bytes 983048 | tf_op jit(solution)/shard_map/ppermute | solution.py:22
  6.8 9.5 %collective-permute-start.5 = (bf16[128,1280]{1,0:T(8,128)(2,1)S(1)}, bf16[128,1280]{1,0:T(8,128)(2,1)}, u32[]{:S(2)}, u32[]{:S(2)}) collective-permute-start(bf16[128,1280]{1,0:T(8,128)(2,1)S(1)} %copy-done.1), channel_id=1, source_target_pairs={{4,8},{5,9},{6,10},{7,11},{8,4},{9,5},{10,6},{11,7},{20,24},{21,25... | collective-permute-start | bytes 983048 | tf_op jit(solution)/shard_map/ppermute | solution.py:22
  8.2 10.9 %collective-permute-start.3 = (bf16[128,1280]{1,0:T(8,128)(2,1)S(1)}, bf16[128,1280]{1,0:T(8,128)(2,1)S(1)}, u32[]{:S(2)}, u32[]{:S(2)}) collective-permute-start(bf16[128,1280]{1,0:T(8,128)(2,1)S(1)} %copy-done.1), channel_id=1, source_target_pairs={{0,4},{1,5},{2,6},{3,7},{4,0},{5,1},{6,2},{7,3},{8,12},{9,13},{10,... | collective-permute-start | bytes 983048 | tf_op jit(solution)/shard_map/ppermute | solution.py:22
  11.9 7.2 %collective-permute-start.4 = (bf16[2,80,1024]{2,1,0:T(8,128)(2,1)S(1)}, bf16[2,80,1024]{2,1,0:T(8,128)(2,1)S(1)}, u32[]{:S(2)}, u32[]{:S(2)}) collective-permute-start(bf16[2,80,1024]{2,1,0:T(8,128)(2,1)S(1)} %get-tuple-element.30.refs_0_.refs_7_), channel_id=1, source_target_pairs={{0,1},{1,0},{2,3},{3,2},{4,5},{5,4},{6,7},{7,6},{8,9},{9,8},{10,11... | collective-permute-start | bytes 983048 | tf_op jit(solution)/shard_map/ppermute | solution.py:22
  14.5 4.6 %collective-permute-start.6 = (bf16[2,80,1024]{2,1,0:T(8,128)(2,1)S(1)}, bf16[2,80,1024]{2,1,0:T(8,128)(2,1)S(1)}, u32[]{:S(2)}, u32[]{:S(2)}) collective-permute-start(bf16[2,80,1024]{2,1,0:T(8,128)(2,1)S(1)} %collective-permute-done.refs_2_.refs_9_), channel_id=1, source_target_pairs={{0,1},{1,0},{2,3},{3,2},{4,5},{5,4},{6,7},{7,6},{8,9},{9,8},{10,11... | collective-permute-start | bytes 983048 | tf_op jit(solution)/shard_map/ppermute | solution.py:22
  14.5 10.5 %collective-permute-start.1 = (bf16[128,1280]{1,0:T(8,128)(2,1)S(1)}, bf16[128,1280]{1,0:T(8,128)(2,1)S(1)}, u32[]{:S(2)}, u32[]{:S(2)}) collective-permute-start(bf16[128,1280]{1,0:T(8,128)(2,1)S(1)} %copy-done.1), channel_id=1, source_target_pairs={{0,2},{1,3},{2,0},{3,1},{4,6},{5,7},{6,4},{7,5},{8,10},{9,11},{10,... | collective-permute-start | bytes 983048 | tf_op jit(solution)/shard_map/ppermute | solution.py:22
  19.1 8.8 %copy-start.5 = (f32[1280]{0:T(1024)S(1)}, f32[1280]{0:T(1024)}, u32[]{:S(2)}) copy-start(f32[1280]{0:T(1024)} %param.7) | copy-start | bytes 15364
  19.7 22.3 %collective-permute-start.7 = (bf16[128,1280]{1,0:T(8,128)(2,1)S(1)}, bf16[128,1280]{1,0:T(8,128)(2,1)S(1)}, u32[]{:S(2)}, u32[]{:S(2)}) collective-permute-start(bf16[128,1280]{1,0:T(8,128)(2,1)S(1)} %collective-permute-done.3.here), channel_id=1, source_target_pairs={{0,2},{1,3},{2,0},{3,1},{4,6},{5,7},{6,4},{7,5},{8,10},{9,11},{10,... | collective-permute-start | bytes 983048 | tf_op jit(solution)/shard_map/ppermute | solution.py:22
  20.3 22.7 %collective-permute-start.9 = (bf16[128,1280]{1,0:T(8,128)(2,1)}, bf16[128,1280]{1,0:T(8,128)(2,1)}, u32[]{:S(2)}, u32[]{:S(2)}) collective-permute-start(bf16[128,1280]{1,0:T(8,128)(2,1)} %collective-permute-done.5), channel_id=1, source_target_pairs={{0,4},{1,5},{2,6},{3,7},{4,0},{5,1},{6,2},{7,3},{8,12},{9,13},{10,... | collective-permute-start | bytes 983048 | tf_op jit(solution)/shard_map/ppermute | solution.py:22
  22.0 13.7 %collective-permute-start.14 = (bf16[80,1024]{1,0:T(8,128)(2,1)S(1)}, bf16[80,1024]{1,0:T(8,128)(2,1)S(1)}, u32[]{:S(2)}, u32[]{:S(2)}) collective-permute-start(bf16[80,1024]{1,0:T(8,128)(2,1)S(1)} %get-tuple-element.36), channel_id=1, source_target_pairs={{0,12},{1,13},{2,14},{3,15},{4,8},{5,9},{6,10},{7,11},{8,4},{9,5},... | collective-permute-start | bytes 491528 | tf_op jit(solution)/shard_map/ppermute | solution.py:22
  23.4 15.6 %collective-permute-start.12 = (bf16[80,1024]{1,0:T(8,128)(2,1)S(1)}, bf16[80,1024]{1,0:T(8,128)(2,1)S(1)}, u32[]{:S(2)}, u32[]{:S(2)}) collective-permute-start(bf16[80,1024]{1,0:T(8,128)(2,1)S(1)} %get-tuple-element.36), channel_id=1, source_target_pairs={{0,4},{1,5},{2,6},{3,7},{4,0},{5,1},{6,2},{7,3},{8,12},{9,13},{10,... | collective-permute-start | bytes 491528 | tf_op jit(solution)/shard_map/ppermute | solution.py:22
  25.0 14.0 %collective-permute-start.13 = (bf16[80,1024]{1,0:T(8,128)(2,1)S(1)}, bf16[80,1024]{1,0:T(8,128)(2,1)S(1)}, u32[]{:S(2)}, u32[]{:S(2)}) collective-permute-start(bf16[80,1024]{1,0:T(8,128)(2,1)S(1)} %get-tuple-element.32.refs_0_), channel_id=1, source_target_pairs={{0,8},{1,9},{2,10},{3,11},{4,12},{5,13},{6,14},{7,15},{8,0},{9,1},... | collective-permute-start | bytes 491528 | tf_op jit(solution)/shard_map/ppermute | solution.py:22
  35.7 20.0 %collective-permute-start.2 = (bf16[256,1664]{1,0:T(8,128)(2,1)S(1)}, bf16[256,1664]{1,0:T(8,128)(2,1)S(1)}, u32[]{:S(2)}, u32[]{:S(2)}) collective-permute-start(bf16[256,1664]{1,0:T(8,128)(2,1)S(1)} %shard_map.78.refs_0_), channel_id=1, source_target_pairs={{0,1},{1,0},{2,3},{3,2},{4,5},{5,4},{6,7},{7,6},{8,9},{9,8},{10,11... | collective-permute-start | bytes 2555912 | tf_op jit(solution)/shard_map/ppermute | solution.py:22
  40.3 15.4 %collective-permute-start.16 = (bf16[240,1024]{1,0:T(8,128)(2,1)S(1)}, bf16[240,1024]{1,0:T(8,128)(2,1)S(1)}, u32[]{:S(2)}, u32[]{:S(2)}) collective-permute-start(bf16[240,1024]{1,0:T(8,128)(2,1)S(1)} %get-tuple-element.38.refs_11_), channel_id=1, source_target_pairs={{0,16},{16,0},{1,17},{17,1},{2,18},{18,2},{3,19},{19,3},{4,20},{20... | collective-permute-start | bytes 1474568 | tf_op jit(solution)/shard_map/ppermute | solution.py:507
  42.9 12.8 %collective-permute-start.8 = (bf16[256,1664]{1,0:T(8,128)(2,1)S(1)}, bf16[256,1664]{1,0:T(8,128)(2,1)S(1)}, u32[]{:S(2)}, u32[]{:S(2)}) collective-permute-start(bf16[256,1664]{1,0:T(8,128)(2,1)S(1)} %shard_map.80.refs_2_), channel_id=1, source_target_pairs={{0,1},{1,0},{2,3},{3,2},{4,5},{5,4},{6,7},{7,6},{8,9},{9,8},{10,11... | collective-permute-start | bytes 2555912 | tf_op jit(solution)/shard_map/ppermute | solution.py:22
  44.0 10.2 %collective-permute-start.10 = (bf16[128,1280]{1,0:T(8,128)(2,1)S(1)}, bf16[128,1280]{1,0:T(8,128)(2,1)S(1)}, u32[]{:S(2)}, u32[]{:S(2)}) collective-permute-start(bf16[128,1280]{1,0:T(8,128)(2,1)S(1)} %broadcast_select_fusion.here), channel_id=1, source_target_pairs={{0,2},{1,3},{2,0},{3,1},{4,6},{5,7},{6,4},{7,5},{8,10},{9,11},{10,... | collective-permute-start | bytes 983048 | tf_op jit(solution)/shard_map/ppermute | solution.py:22
  55.2 2.9 %collective-permute-start.11 = (bf16[256,1280]{1,0:T(8,128)(2,1)S(1)}, bf16[256,1280]{1,0:T(8,128)(2,1)S(1)}, u32[]{:S(2)}, u32[]{:S(2)}) collective-permute-start(bf16[256,1280]{1,0:T(8,128)(2,1)S(1)} %shard_map.81.refs_4_), channel_id=1, source_target_pairs={{0,1},{1,0},{2,3},{3,2},{4,5},{5,4},{6,7},{7,6},{8,9},{9,8},{10,11... | collective-permute-start | bytes 1966088 | tf_op jit(solution)/shard_map/ppermute | solution.py:22
  55.2 2.8 %collective-permute-start.15 = (bf16[240,1024]{1,0:T(8,128)(2,1)S(1)}, bf16[240,1024]{1,0:T(8,128)(2,1)S(1)}, u32[]{:S(2)}, u32[]{:S(2)}) collective-permute-start(bf16[240,1024]{1,0:T(8,128)(2,1)S(1)} %get-tuple-element.38.refs_11_), channel_id=1, source_target_pairs={{0,1},{1,0},{2,3},{3,2},{4,5},{5,4},{6,7},{7,6},{8,9},{9,8},{10,11... | collective-permute-start | bytes 1474568 | tf_op jit(solution)/shard_map/ppermute | solution.py:22
  55.7 3.0 %collective-permute-start.17 = (bf16[240,1024]{1,0:T(8,128)(2,1)S(1)}, bf16[240,1024]{1,0:T(8,128)(2,1)S(1)}, u32[]{:S(2)}, u32[]{:S(2)}) collective-permute-start(bf16[240,1024]{1,0:T(8,128)(2,1)S(1)} %collective-permute-done.16.refs_13_), channel_id=1, source_target_pairs={{0,1},{1,0},{2,3},{3,2},{4,5},{5,4},{6,7},{7,6},{8,9},{9,8},{10,11... | collective-permute-start | bytes 1474568 | tf_op jit(solution)/shard_map/ppermute | solution.py:22
  72.0 2.4 %collective-permute-start.19 = (bf16[512,320]{1,0:T(8,128)(2,1)S(1)}, bf16[512,320]{1,0:T(8,128)(2,1)S(1)}, u32[]{:S(2)}, u32[]{:S(2)}) collective-permute-start(bf16[512,320]{1,0:T(8,128)(2,1)S(1)} %get-tuple-element.43.memory), channel_id=1, source_target_pairs={{0,1},{1,0},{2,3},{3,2},{4,5},{5,4},{6,7},{7,6},{8,9},{9,8},{10,11... | collective-permute-start | bytes 983048 | tf_op jit(solution)/shard_map/ppermute | solution.py:22
  72.2 7.8 %collective-permute-start.21 = (bf16[256,320]{1,0:T(8,128)(2,1)S(1)}, bf16[256,320]{1,0:T(8,128)(2,1)S(1)}, u32[]{:S(2)}, u32[]{:S(2)}) collective-permute-start(bf16[256,320]{1,0:T(8,128)(2,1)S(1)} %get-tuple-element.46), channel_id=1, source_target_pairs={{0,2},{1,6},{2,0},{3,4},{4,3},{5,7},{6,1},{7,5},{8,10},{9,14},{10,... | collective-permute-start | bytes 491528 | tf_op jit(solution)/shard_map/ppermute | solution.py:22
  73.7 6.8 %collective-permute-start.18 = (bf16[256,320]{1,0:T(8,128)(2,1)S(1)}, bf16[256,320]{1,0:T(8,128)(2,1)S(1)}, u32[]{:S(2)}, u32[]{:S(2)}) collective-permute-start(bf16[256,320]{1,0:T(8,128)(2,1)S(1)} %get-tuple-element.40), channel_id=1, source_target_pairs={{0,0},{1,4},{2,2},{3,6},{4,1},{5,5},{6,3},{7,7},{8,8},{9,12},{10,1... | collective-permute-start | bytes 491528 | tf_op jit(solution)/shard_map/ppermute | solution.py:22
  75.7 4.8 %collective-permute-start.20 = (f32[40,128]{1,0:T(8,128)S(1)}, f32[40,128]{1,0:T(8,128)S(1)}, u32[]{:S(2)}, u32[]{:S(2)}) collective-permute-start(f32[40,128]{1,0:T(8,128)S(1)} %get-tuple-element.44), channel_id=1, source_target_pairs={{0,8},{1,9},{2,10},{3,11},{4,12},{5,13},{6,14},{7,15},{8,0},{9,1},... | collective-permute-start | bytes 61448 | tf_op jit(solution)/shard_map/ppermute | solution.py:22
  80.6 6.1 %collective-permute-start.22 = (bf16[256,320]{1,0:T(8,128)(2,1)S(1)}, bf16[256,320]{1,0:T(8,128)(2,1)S(1)}, u32[]{:S(2)}, u32[]{:S(2)}) collective-permute-start(bf16[256,320]{1,0:T(8,128)(2,1)S(1)} %collective-permute-done.18.refs_0_), channel_id=1, source_target_pairs={{0,1},{1,0},{2,3},{3,2},{4,5},{5,4},{6,7},{7,6},{8,9},{9,8},{10,11... | collective-permute-start | bytes 491528 | tf_op jit(solution)/shard_map/ppermute | solution.py:22
  82.2 4.5 %collective-permute-start.23 = (bf16[256,320]{1,0:T(8,128)(2,1)S(1)}, bf16[256,320]{1,0:T(8,128)(2,1)S(1)}, u32[]{:S(2)}, u32[]{:S(2)}) collective-permute-start(bf16[256,320]{1,0:T(8,128)(2,1)S(1)} %collective-permute-done.21.refs_1_), channel_id=1, source_target_pairs={{0,1},{1,0},{2,3},{3,2},{4,5},{5,4},{6,7},{7,6},{8,9},{9,8},{10,11... | collective-permute-start | bytes 491528 | tf_op jit(solution)/shard_map/ppermute | solution.py:22
  82.4 5.6 %collective-permute-start.24 = (bf16[2,384]{1,0:T(2,128)(2,1)S(1)}, bf16[2,384]{1,0:T(2,128)(2,1)S(1)}, u32[]{:S(2)}, u32[]{:S(2)}) collective-permute-start(bf16[2,384]{1,0:T(2,128)(2,1)S(1)} %get-tuple-element.51), channel_id=1, source_target_pairs={{0,2},{1,3},{2,0},{3,1},{4,6},{5,7},{6,4},{7,5},{8,10},{9,11},{10,... | collective-permute-start | bytes 4616 | tf_op jit(solution)/shard_map/ppermute | solution.py:22
  83.8 4.3 %collective-permute-start.25 = (bf16[2,384]{1,0:T(2,128)(2,1)S(1)}, bf16[2,384]{1,0:T(2,128)(2,1)S(1)}, u32[]{:S(2)}, u32[]{:S(2)}) collective-permute-start(bf16[2,384]{1,0:T(2,128)(2,1)S(1)} %get-tuple-element.52), channel_id=1, source_target_pairs={{0,4},{1,5},{2,6},{3,7},{4,0},{5,1},{6,2},{7,3},{8,12},{9,13},{10,... | collective-permute-start | bytes 4616 | tf_op jit(solution)/shard_map/ppermute | solution.py:22
  86.6 4.5 %collective-permute-start.26 = (bf16[2,384]{1,0:T(2,128)(2,1)S(1)}, bf16[2,384]{1,0:T(2,128)(2,1)S(1)}, u32[]{:S(2)}, u32[]{:S(2)}) collective-permute-start(bf16[2,384]{1,0:T(2,128)(2,1)S(1)} %get-tuple-element.53), channel_id=1, source_target_pairs={{0,6},{1,7},{2,4},{3,5},{4,2},{5,3},{6,0},{7,1},{8,14},{9,15},{10,... | collective-permute-start | bytes 4616 | tf_op jit(solution)/shard_map/ppermute | solution.py:22

commit v11 on v10

--- a/solution.py
+++ b/solution.py
@@ -517,16 +517,17 @@
         here = {turn: swap(ready[turn % 2], n, 4 * turn) for turn in (3, 2, 1)}
         pair_x = swap(after(pair, ready[0]), n, 2)
         halo = jnp.where((z == 1) | (z == 2), near, relayed)
-        halo_x = swap(after(halo, pair_x), n, 2)
-        ids, tokens, asked, joined = prepare(table, [ready[0], here[1], here[2], here[3]], n)
+        halo_x = swap(after(halo, pair_x, *here.values()), n, 2)
+        ids, tokens, asked, joined = prepare(table, [after(ready[0], halo), here[1], here[2], here[3]], n)
         traded = trade(joined)
         own_half = norm_half(table, gain, stem, stem_x)
         pair_half = norm_half(table, gain, pair, pair_x)
         halo_half = norm_half(table, gain, halo, halo_x, False)
         own_c, pair_c = swap(own_half, n, 1), swap(pair_half, n, 1)
-        layered = [own_half, own_c, pair_half, pair_c, halo_half, swap(halo_half, n, 1)]
-        weights = [mine, mine_c, across, across_c, joined, swap(joined, n, 1)]
-        weights += [traded, swap(after(traded, own_c, pair_c), n, 1)]
+        halo_c, joined_c = swap(after(halo_half, traded), n, 1), swap(joined, n, 1)
+        layered = [own_half, own_c, pair_half, pair_c, halo_half, halo_c]
+        weights = [mine, mine_c, across, across_c, joined, joined_c]
+        weights += [traded, swap(after(traded, own_c, pair_c, joined_c), n, 1)]
     else:
         stem_x = swap(stem, n, 2)
         far = swap(near, n, 4)

time: 92.5 us -> 87 us (0.941)
  starting transfers between devices: 31.2 us -> 26 us
    ppermute x26, starting transfers between devices: 29.6 us -> 24.4 us  [send(): return lax.ppermute(block, 'tm', route)]
  transfers between devices with their start and end apart: 27 -> 27, of which waited for: 12 -> 13; matrix products, arithmetic and copies ran while one was open for 1% -> 1% of each run, Pallas kernels for 8% -> 9%
where the time goes in v11:
time: 87 us; the launch traced here: 86.7 us
  waiting for transfers between devices  33.5 us (39%)
  starting transfers between devices  26 us (30%)
  Pallas kernels  23.5 us (27%)
  local copies, waits for them, and re-layouts  1.87 us (2%)
  other arithmetic  1.02 us (1%)
  between operations  0.9 us (1%)
    ppermute x26, waiting for transfers between devices, send(): return lax.ppermute(block, 'tm', route)  33.5 us
    ppermute x26, starting transfers between devices, send(): return lax.ppermute(block, 'tm', route)  24.4 us
    pallas_call x1, Pallas kernels, encoder(): pl.pallas_call(functools.partial(encoder_kernel, len(parts), depth), out_...  13.3 us
    pallas_call x3, Pallas kernels, norm_half(): pl.pallas_call(norm_kernel, out_shape=jax.ShapeDtypeStruct((256, 1664 if...  2.93 us
    pallas_call x2, Pallas kernels, gather_groups(): pl.pallas_call(functools.partial(gather_kernel, side, rows), out_shape=ja...  2.59 us
    unnamed x12, local copies, waits for them, and re-layouts  1.75 us
  transfers between devices with their start and end apart: 27, of which 13 were waited for; matrix products, arithmetic and copies ran while one was open for 1% of the time, Pallas kernels for 9%

profile of v11, /device:TPU:0, one launch (start us, length us, event | category | flops | bytes accessed | tf_op | source)
XLA Modules:
  0.0 86.7 jit_solution(13453533215335518736)
XLA Ops:
  0.7 0.0 copy-start.2
  0.7 0.1 stack.136.table.places
  0.8 0.0 copy-start.3
  0.9 0.0 copy-start.4
  0.9 0.5 copy-done.2
  1.4 0.1 copy-done.3
  1.5 1.1 %copy-done = bf16[80,3840]{1,0:T(8,128)(2,1)S(1)} copy-done((bf16[80,3840]{1,0:T(8,128)(2,1)S(1)}, bf16[80,3840]{1,0:T(8,128)(2,1)}, u32[]{:S(2)}) %copy-start) | copy-done | bytes 614424
  2.6 1.1 %shard_map.77 = (bf16[2,80,1024]{2,1,0:T(8,128)(2,1)S(1)}, bf16[2,80,1024]{2,1,0:T(8,128)(2,1)S(1)}) custom-call(s32[34]{0:T(128)S(1)} %stack.136.table.places, bf16[80,3840]{1,0:T(8,128)(2,1)S(1)} %copy-done, bf16[2,1280]{1,0:T(2,128)(2,1)S(1)} %copy-done.2, s32[2,16]{1,0:T(2,128)S(1)} %copy-done.3, s32[1,128]{1,0:T(1,128)S(1)} %bitcast.33), custom_call_target="tpu_custom_call" | custom-call | flops 1 | bytes 1 | tf_op jit(solution)/shard_map/pallas_call | solution.py:98
  3.8 3.0 %collective-permute-start = (bf16[2,80,1024]{2,1,0:T(8,128)(2,1)S(1)}, bf16[2,80,1024]{2,1,0:T(8,128)(2,1)S(1)}, u32[]{:S(2)}, u32[]{:S(2)}) collective-permute-start(bf16[2,80,1024]{2,1,0:T(8,128)(2,1)S(1)} %get-tuple-element.30), channel_id=1, source_target_pairs={{0,2},{1,3},{2,0},{3,1},{4,6},{5,7},{6,4},{7,5},{8,10},{9,11},{10,... | collective-permute-start | bytes 983048 | tf_op jit(solution)/shard_map/ppermute | solution.py:22
  6.8 0.7 collective-permute-start.5
  7.5 4.4 %collective-permute-start.3 = (bf16[128,1280]{1,0:T(8,128)(2,1)S(1)}, bf16[128,1280]{1,0:T(8,128)(2,1)S(1)}, u32[]{:S(2)}, u32[]{:S(2)}) collective-permute-start(bf16[128,1280]{1,0:T(8,128)(2,1)S(1)} %copy-done.1), channel_id=1, source_target_pairs={{0,4},{1,5},{2,6},{3,7},{4,0},{5,1},{6,2},{7,3},{8,12},{9,13},{10,... | collective-permute-start | bytes 983048 | tf_op jit(solution)/shard_map/ppermute | solution.py:22
  11.9 0.0 collective-permute-start.4
  11.9 2.6 %collective-permute-done.refs_2_.refs_9_ = bf16[2,80,1024]{2,1,0:T(8,128)(2,1)S(1)} collective-permute-done((bf16[2,80,1024]{2,1,0:T(8,128)(2,1)S(1)}, bf16[2,80,1024]{2,1,0:T(8,128)(2,1)S(1)}, u32[]{:S(2)}, u32[]{:S(2)}) %collective-permute-start) | collective-permute-done | bytes 327712 | tf_op jit(solution)/shard_map/ppermute | solution.py:22
  14.5 4.6 %collective-permute-done.3.here = bf16[128,1280]{1,0:T(8,128)(2,1)S(1)} collective-permute-done((bf16[128,1280]{1,0:T(8,128)(2,1)S(1)}, bf16[128,1280]{1,0:T(8,128)(2,1)S(1)}, u32[]{:S(2)}, u32[]{:S(2)}) %collective-permute-start.3) | collective-permute-done | bytes 327712 | tf_op jit(solution)/shard_map/ppermute | solution.py:22
  19.0 0.5 collective-permute-start.1
  19.6 0.0 collective-permute-done.6.refs_3_.refs_10_
  19.6 0.6 shard_map.79
  20.2 1.6 %collective-permute-start.7 = (bf16[128,1280]{1,0:T(8,128)(2,1)S(1)}, bf16[128,1280]{1,0:T(8,128)(2,1)S(1)}, u32[]{:S(2)}, u32[]{:S(2)}) collective-permute-start(bf16[128,1280]{1,0:T(8,128)(2,1)S(1)} %collective-permute-done.3.here), channel_id=1, source_target_pairs={{0,2},{1,3},{2,0},{3,1},{4,6},{5,7},{6,4},{7,5},{8,10},{9,11},{10,... | collective-permute-start | bytes 983048 | tf_op jit(solution)/shard_map/ppermute | solution.py:22
  21.7 1.7 %collective-permute-start.9 = (bf16[128,1280]{1,0:T(8,128)(2,1)S(1)}, bf16[128,1280]{1,0:T(8,128)(2,1)}, u32[]{:S(2)}, u32[]{:S(2)}) collective-permute-start(bf16[128,1280]{1,0:T(8,128)(2,1)S(1)} %collective-permute-done.5), channel_id=1, source_target_pairs={{0,4},{1,5},{2,6},{3,7},{4,0},{5,1},{6,2},{7,3},{8,12},{9,13},{10,... | collective-permute-start | bytes 983048 | tf_op jit(solution)/shard_map/ppermute | solution.py:22
  23.5 0.3 collective-permute-start.12
  23.8 1.4 %collective-permute-start.10 = (bf16[80,1024]{1,0:T(8,128)(2,1)S(1)}, bf16[80,1024]{1,0:T(8,128)(2,1)S(1)}, u32[]{:S(2)}, u32[]{:S(2)}) collective-permute-start(bf16[80,1024]{1,0:T(8,128)(2,1)S(1)} %get-tuple-element.37), channel_id=1, source_target_pairs={{0,12},{1,13},{2,14},{3,15},{4,8},{5,9},{6,10},{7,11},{8,4},{9,5},... | collective-permute-start | bytes 491528 | tf_op jit(solution)/shard_map/ppermute | solution.py:22
  25.1 4.5 %collective-permute-done.1.across = bf16[128,1280]{1,0:T(8,128)(2,1)S(1)} collective-permute-done((bf16[128,1280]{1,0:T(8,128)(2,1)S(1)}, bf16[128,1280]{1,0:T(8,128)(2,1)S(1)}, u32[]{:S(2)}, u32[]{:S(2)}) %collective-permute-start.1) | collective-permute-done | bytes 327712 | tf_op jit(solution)/shard_map/ppermute | solution.py:22
  29.7 1.6 %collective-permute-start.11 = (bf16[80,1024]{1,0:T(8,128)(2,1)S(1)}, bf16[80,1024]{1,0:T(8,128)(2,1)S(1)}, u32[]{:S(2)}, u32[]{:S(2)}) collective-permute-start(bf16[80,1024]{1,0:T(8,128)(2,1)S(1)} %get-tuple-element.39.refs_0_), channel_id=1, source_target_pairs={{0,8},{1,9},{2,10},{3,11},{4,12},{5,13},{6,14},{7,15},{8,0},{9,1},... | collective-permute-start | bytes 491528 | tf_op jit(solution)/shard_map/ppermute | solution.py:22
  31.3 1.0 %shard_map.78.refs_0_ = bf16[256,1664]{1,0:T(8,128)(2,1)S(1)} custom-call(s32[34]{0:T(128)S(1)} %stack.136.table.places, f32[1,1280]{1,0:T(1,128)S(1)} %reshape.10.gain, bf16[128,1280]{1,0:T(8,128)(2,1)S(1)} %copy-done.1, bf16[128,1280]{1,0:T(8,128)(2,1)S(1)} %collective-permute-done.1.across), custom_call_target="tpu_custom_call" | custom-call | flops 1 | bytes 1 | tf_op jit(solution)/shard_map/pallas_call | solution.py:162
  32.3 2.0 %collective-permute-done.7.across = bf16[128,1280]{1,0:T(8,128)(2,1)S(1)} collective-permute-done((bf16[128,1280]{1,0:T(8,128)(2,1)S(1)}, bf16[128,1280]{1,0:T(8,128)(2,1)S(1)}, u32[]{:S(2)}, u32[]{:S(2)}) %collective-permute-start.7) | collective-permute-done | bytes 327712 | tf_op jit(solution)/shard_map/ppermute | solution.py:22
  34.3 0.0 collective-permute-start.2
  34.3 1.0 %shard_map.80.refs_2_ = bf16[256,1664]{1,0:T(8,128)(2,1)S(1)} custom-call(s32[34]{0:T(128)S(1)} %stack.136.table.places, f32[1,1280]{1,0:T(1,128)S(1)} %reshape.10.gain, bf16[128,1280]{1,0:T(8,128)(2,1)S(1)} %collective-permute-done.3.here, bf16[128,1280]{1,0:T(8,128)(2,1)S(1)} %collective-permute-done.7.across), custom_call_target="tpu_custom_call" | custom-call | flops 1 | bytes 1 | tf_op jit(solution)/shard_map/pallas_call | solution.py:162
  35.3 0.0 collective-permute-done.9
  35.4 0.5 collective-permute-start.8
  35.9 1.0 %broadcast_select_fusion.here = bf16[128,1280]{1,0:T(8,128)(2,1)S(1)} fusion(bf16[128,1280]{1,0:T(8,128)(2,1)S(1)} %collective-permute-done.5, bf16[128,1280]{1,0:T(8,128)(2,1)} %collective-permute-done.9, pred[]{:T(512)S(6)} %or.3), kind=kLoop, calls=%fused_computation | loop fusion | flops 163840 | bytes 983041 | tf_op jit(solution)/shard_map/jit(_where)/select_n | solution.py:519
  36.9 2.8 %collective-permute-done.12.refs_1_ = bf16[80,1024]{1,0:T(8,128)(2,1)S(1)} collective-permute-done((bf16[80,1024]{1,0:T(8,128)(2,1)S(1)}, bf16[80,1024]{1,0:T(8,128)(2,1)S(1)}, u32[]{:S(2)}, u32[]{:S(2)}) %collective-permute-start.12) | collective-permute-done | bytes 163872 | tf_op jit(solution)/shard_map/ppermute | solution.py:22
  39.7 0.0 collective-permute-done.10.refs_3_
  39.7 1.4 %collective-permute-done.11.refs_2_ = bf16[80,1024]{1,0:T(8,128)(2,1)S(1)} collective-permute-done((bf16[80,1024]{1,0:T(8,128)(2,1)S(1)}, bf16[80,1024]{1,0:T(8,128)(2,1)S(1)}, u32[]{:S(2)}, u32[]{:S(2)}) %collective-permute-start.11) | collective-permute-done | bytes 163872 | tf_op jit(solution)/shard_map/ppermute | solution.py:22
  41.1 1.3 %shard_map.82 = (f32[8,1536]{1,0:T(8,128)S(1)}, f32[80,320]{1,0:T(8,128)S(1)}, f32[16,64]{1,0:T(8,128)S(1)}, bf16[240,1024]{1,0:T(8,128)(2,1)S(1)}) custom-call(s32[34]{0:T(128)S(1)} %stack.136.table.places, bf16[80,1024]{1,0:T(8,128)(2,1)S(1)} %get-tuple-element.39.refs_0_, bf16[80,1024]{1,0:T(8,128)(2,1)S(1)} %collective-permute-done.12.refs_1_, ...), custom_call_target="tpu_custom_call" | custom-call | flops 1 | bytes 1 | tf_op jit(solution)/shard_map/pallas_call | solution.py:208
  42.5 1.6 %collective-permute-start.14 = (bf16[240,1024]{1,0:T(8,128)(2,1)S(1)}, bf16[240,1024]{1,0:T(8,128)(2,1)S(1)}, u32[]{:S(2)}, u32[]{:S(2)}) collective-permute-start(bf16[240,1024]{1,0:T(8,128)(2,1)S(1)} %get-tuple-element.40.refs_11_), channel_id=1, source_target_pairs={{0,16},{16,0},{1,17},{17,1},{2,18},{18,2},{3,19},{19,3},{4,20},{20... | collective-permute-start | bytes 1474568 | tf_op jit(solution)/shard_map/ppermute | solution.py:507
  44.1 0.5 collective-permute-start.13
  44.6 0.0 collective-permute-start.16
  44.6 6.5 %collective-permute-done.13.across = bf16[128,1280]{1,0:T(8,128)(2,1)S(1)} collective-permute-done((bf16[128,1280]{1,0:T(8,128)(2,1)S(1)}, bf16[128,1280]{1,0:T(8,128)(2,1)S(1)}, u32[]{:S(2)}, u32[]{:S(2)}) %collective-permute-start.13) | collective-permute-done | bytes 327712 | tf_op jit(solution)/shard_map/ppermute | solution.py:22
  51.1 1.0 %shard_map.81.refs_4_ = bf16[256,1280]{1,0:T(8,128)(2,1)S(1)} custom-call(s32[34]{0:T(128)S(1)} %stack.136.table.places, f32[1,1280]{1,0:T(1,128)S(1)} %reshape.10.gain, bf16[128,1280]{1,0:T(8,128)(2,1)S(1)} %broadcast_select_fusion.here, bf16[128,1280]{1,0:T(8,128)(2,1)S(1)} %collective-permute-done.13.across), custom_call_target="tpu_custom_call" | custom-call | flops 1 | bytes 1 | tf_op jit(solution)/shard_map/pallas_call | solution.py:162
  52.1 0.1 collective-permute-start.15
  52.2 0.0 collective-permute-done.16.refs_12_
  52.2 0.0 collective-permute-done.8.refs_3_
  52.2 0.5 collective-permute-start.17
  52.8 1.5 %collective-permute-done.15.refs_5_ = bf16[256,1280]{1,0:T(8,128)(2,1)S(1)} collective-permute-done((bf16[256,1280]{1,0:T(8,128)(2,1)S(1)}, bf16[256,1280]{1,0:T(8,128)(2,1)S(1)}, u32[]{:S(2)}, u32[]{:S(2)}) %collective-permute-start.15) | collective-permute-done | bytes 655392 | tf_op jit(solution)/shard_map/ppermute | solution.py:22
  54.3 0.7 collective-permute-done.17.refs_14_
  55.0 13.3 %shard_map.83 = (bf16[512,320]{1,0:T(8,128)(2,1)S(1)}, bf16[256,320]{1,0:T(8,128)(2,1)S(1)}, bf16[256,320]{1,0:T(8,128)(2,1)S(1)}) custom-call(s32[34]{0:T(128)S(1)} %stack.136.table.places, bf16[256,1664]{1,0:T(8,128)(2,1)S(1)} %shard_map.78.refs_0_, bf16[256,1664]{1,0:T(8,128)(2,1)S(1)} %collective-permute-done.2.refs_1_, ...), custom_call_target="tpu_custom_call" | custom-call | flops 1 | bytes 1 | tf_op jit(solution)/shard_map/pallas_call | solution.py:342
  68.3 0.2 collective-permute-start.19
  68.5 0.5 collective-permute-start.21
  69.0 0.7 collective-permute-start.18
  69.7 0.4 collective-permute-done.19.beside
  70.1 1.3 %shard_map.84 = (f32[40,128]{1,0:T(8,128)S(1)}, f32[40,128]{1,0:T(8,128)S(1)}) custom-call(s32[34]{0:T(128)S(1)} %stack.136.table.places, f32[80,320]{1,0:T(8,128)S(1)} %get-tuple-element.45.tokens, f32[16,64]{1,0:T(8,128)S(1)} %get-tuple-element.46.asked, bf16[512,320]{1,0:T(8,128)(2,1)S(1)} %get-tuple-element.47.memory, ...), custom_call_target="tpu_custom_call" | custom-call | flops 1 | bytes 1 | tf_op jit(solution)/shard_map/pallas_call | solution.py:408
  71.4 1.4 %collective-permute-start.20 = (f32[40,128]{1,0:T(8,128)S(1)}, f32[40,128]{1,0:T(8,128)S(1)}, u32[]{:S(2)}, u32[]{:S(2)}) collective-permute-start(f32[40,128]{1,0:T(8,128)S(1)} %get-tuple-element.48), channel_id=1, source_target_pairs={{0,8},{1,9},{2,10},{3,11},{4,12},{5,13},{6,14},{7,15},{8,0},{9,1},... | collective-permute-start | bytes 61448 | tf_op jit(solution)/shard_map/ppermute | solution.py:22
  72.8 3.5 %collective-permute-done.21.refs_1_ = bf16[256,320]{1,0:T(8,128)(2,1)S(1)} collective-permute-done((bf16[256,320]{1,0:T(8,128)(2,1)S(1)}, bf16[256,320]{1,0:T(8,128)(2,1)S(1)}, u32[]{:S(2)}, u32[]{:S(2)}) %collective-permute-start.21) | collective-permute-done | bytes 163872 | tf_op jit(solution)/shard_map/ppermute | solution.py:22
  76.3 1.1 %collective-permute-start.22 = (bf16[256,320]{1,0:T(8,128)(2,1)S(1)}, bf16[256,320]{1,0:T(8,128)(2,1)S(1)}, u32[]{:S(2)}, u32[]{:S(2)}) collective-permute-start(bf16[256,320]{1,0:T(8,128)(2,1)S(1)} %collective-permute-done.18.refs_0_), channel_id=1, source_target_pairs={{0,1},{1,0},{2,3},{3,2},{4,5},{5,4},{6,7},{7,6},{8,9},{9,8},{10,11... | collective-permute-start | bytes 491528 | tf_op jit(solution)/shard_map/ppermute | solution.py:22
  77.4 0.0 collective-permute-start.23
  77.4 0.2 shard_map.86
  77.7 1.6 %collective-permute-start.24 = (bf16[2,384]{1,0:T(2,128)(2,1)S(1)}, bf16[2,384]{1,0:T(2,128)(2,1)S(1)}, u32[]{:S(2)}, u32[]{:S(2)}) collective-permute-start(bf16[2,384]{1,0:T(2,128)(2,1)S(1)} %get-tuple-element.55), channel_id=1, source_target_pairs={{0,2},{1,3},{2,0},{3,1},{4,6},{5,7},{6,4},{7,5},{8,10},{9,11},{10,... | collective-permute-start | bytes 4616 | tf_op jit(solution)/shard_map/ppermute | solution.py:22
  79.2 1.8 %collective-permute-start.25 = (bf16[2,384]{1,0:T(2,128)(2,1)S(1)}, bf16[2,384]{1,0:T(2,128)(2,1)S(1)}, u32[]{:S(2)}, u32[]{:S(2)}) collective-permute-start(bf16[2,384]{1,0:T(2,128)(2,1)S(1)} %get-tuple-element.56), channel_id=1, source_target_pairs={{0,4},{1,5},{2,6},{3,7},{4,0},{5,1},{6,2},{7,3},{8,12},{9,13},{10,... | collective-permute-start | bytes 4616 | tf_op jit(solution)/shard_map/ppermute | solution.py:22
  81.0 0.2 collective-permute-start.26
  81.2 0.0 collective-permute-done.22.refs_2_
  81.2 1.4 %shard_map.85 = bf16[128,1280]{1,0:T(8,128)(2,1)} custom-call(s32[34]{0:T(128)S(1)} %stack.136.table.places, bf16[256,320]{1,0:T(8,128)(2,1)S(1)} %collective-permute-done.18.refs_0_, bf16[256,320]{1,0:T(8,128)(2,1)S(1)} %collective-permute-done.21.refs_1_, bf16[256,320]{1,0:T(8,128)(2,1)S(1)} %collective-permute-done.22.refs_2_, ...), custom_call_target="tpu_custom_call" | custom-call | flops 1 | bytes 1 | tf_op jit(solution)/shard_map/pallas_call | solution.py:462
  82.6 0.2 collective-permute-done.25.refs_2_
  82.8 2.7 %collective-permute-done.26.refs_3_ = bf16[2,384]{1,0:T(2,128)(2,1)S(1)} collective-permute-done((bf16[2,384]{1,0:T(2,128)(2,1)S(1)}, bf16[2,384]{1,0:T(2,128)(2,1)S(1)}, u32[]{:S(2)}, u32[]{:S(2)}) %collective-permute-start.26) | collective-permute-done | bytes 1568 | tf_op jit(solution)/shard_map/ppermute | solution.py:22
  85.5 1.2 %shard_map.87 = bf16[2,1280]{1,0:T(2,128)(2,1)} custom-call(s32[34]{0:T(128)S(1)} %stack.136.table.places, bf16[2,384]{1,0:T(2,128)(2,1)S(1)} %get-tuple-element.54.refs_0_, bf16[2,384]{1,0:T(2,128)(2,1)S(1)} %collective-permute-done.24.refs_1_, bf16[2,384]{1,0:T(2,128)(2,1)S(1)} %collective-permute-done.25.refs_2_, ...), custom_call_target="tpu_custom_call" | custom-call | flops 1 | bytes 1 | tf_op jit(solution)/shard_map/pallas_call | solution.py:462
  (16 shorter events, 0.0 us)
Async XLA Ops:
  0.7 0.7 copy-start.2
  0.8 0.7 copy-start.3
  0.9 0.7 copy-start.4
  1.5 1.1 %copy-start = (bf16[80,3840]{1,0:T(8,128)(2,1)S(1)}, bf16[80,3840]{1,0:T(8,128)(2,1)}, u32[]{:S(2)}) copy-start(bf16[80,3840]{1,0:T(8,128)(2,1)} %refs_0_.1) | copy-start | bytes 1843204
  2.6 4.2 %copy-start.1 = (bf16[128,1280]{1,0:T(8,128)(2,1)S(1)}, bf16[128,1280]{1,0:T(8,128)(2,1)}, u32[]{:S(2)}) copy-start(bf16[128,1280]{1,0:T(8,128)(2,1)} %here.1) | copy-start | bytes 983044
  3.8 10.7 %collective-permute-start = (bf16[2,80,1024]{2,1,0:T(8,128)(2,1)S(1)}, bf16[2,80,1024]{2,1,0:T(8,128)(2,1)S(1)}, u32[]{:S(2)}, u32[]{:S(2)}) collective-permute-start(bf16[2,80,1024]{2,1,0:T(8,128)(2,1)S(1)} %get-tuple-element.30), channel_id=1, source_target_pairs={{0,2},{1,3},{2,0},{3,1},{4,6},{5,7},{6,4},{7,5},{8,10},{9,11},{10,... | collective-permute-start | bytes 983048 | tf_op jit(solution)/shard_map/ppermute | solution.py:22
  6.8 7.7 %collective-permute-start.5 = (bf16[128,1280]{1,0:T(8,128)(2,1)S(1)}, bf16[128,1280]{1,0:T(8,128)(2,1)S(1)}, u32[]{:S(2)}, u32[]{:S(2)}) collective-permute-start(bf16[128,1280]{1,0:T(8,128)(2,1)S(1)} %copy-done.1), channel_id=1, source_target_pairs={{4,8},{5,9},{6,10},{7,11},{8,4},{9,5},{10,6},{11,7},{20,24},{21,25... | collective-permute-start | bytes 983048 | tf_op jit(solution)/shard_map/ppermute | solution.py:22
  7.5 11.6 %collective-permute-start.3 = (bf16[128,1280]{1,0:T(8,128)(2,1)S(1)}, bf16[128,1280]{1,0:T(8,128)(2,1)S(1)}, u32[]{:S(2)}, u32[]{:S(2)}) collective-permute-start(bf16[128,1280]{1,0:T(8,128)(2,1)S(1)} %copy-done.1), channel_id=1, source_target_pairs={{0,4},{1,5},{2,6},{3,7},{4,0},{5,1},{6,2},{7,3},{8,12},{9,13},{10,... | collective-permute-start | bytes 983048 | tf_op jit(solution)/shard_map/ppermute | solution.py:22
  11.9 7.7 %collective-permute-start.4 = (bf16[2,80,1024]{2,1,0:T(8,128)(2,1)S(1)}, bf16[2,80,1024]{2,1,0:T(8,128)(2,1)S(1)}, u32[]{:S(2)}, u32[]{:S(2)}) collective-permute-start(bf16[2,80,1024]{2,1,0:T(8,128)(2,1)S(1)} %get-tuple-element.32.refs_0_.refs_7_), channel_id=1, source_target_pairs={{0,1},{1,0},{2,3},{3,2},{4,5},{5,4},{6,7},{7,6},{8,9},{9,8},{10,11... | collective-permute-start | bytes 983048 | tf_op jit(solution)/shard_map/ppermute | solution.py:22
  14.5 5.1 %collective-permute-start.6 = (bf16[2,80,1024]{2,1,0:T(8,128)(2,1)S(1)}, bf16[2,80,1024]{2,1,0:T(8,128)(2,1)S(1)}, u32[]{:S(2)}, u32[]{:S(2)}) collective-permute-start(bf16[2,80,1024]{2,1,0:T(8,128)(2,1)S(1)} %collective-permute-done.refs_2_.refs_9_), channel_id=1, source_target_pairs={{0,1},{1,0},{2,3},{3,2},{4,5},{5,4},{6,7},{7,6},{8,9},{9,8},{10,11... | collective-permute-start | bytes 983048 | tf_op jit(solution)/shard_map/ppermute | solution.py:22
  19.0 10.6 %collective-permute-start.1 = (bf16[128,1280]{1,0:T(8,128)(2,1)S(1)}, bf16[128,1280]{1,0:T(8,128)(2,1)S(1)}, u32[]{:S(2)}, u32[]{:S(2)}) collective-permute-start(bf16[128,1280]{1,0:T(8,128)(2,1)S(1)} %copy-done.1), channel_id=1, source_target_pairs={{0,2},{1,3},{2,0},{3,1},{4,6},{5,7},{6,4},{7,5},{8,10},{9,11},{10,... | collective-permute-start | bytes 983048 | tf_op jit(solution)/shard_map/ppermute | solution.py:22
  19.6 3.9 %copy-start.5 = (f32[1280]{0:T(1024)S(1)}, f32[1280]{0:T(1024)}, u32[]{:S(2)}) copy-start(f32[1280]{0:T(1024)} %param.7) | copy-start | bytes 15364
  20.2 14.1 %collective-permute-start.7 = (bf16[128,1280]{1,0:T(8,128)(2,1)S(1)}, bf16[128,1280]{1,0:T(8,128)(2,1)S(1)}, u32[]{:S(2)}, u32[]{:S(2)}) collective-permute-start(bf16[128,1280]{1,0:T(8,128)(2,1)S(1)} %collective-permute-done.3.here), channel_id=1, source_target_pairs={{0,2},{1,3},{2,0},{3,1},{4,6},{5,7},{6,4},{7,5},{8,10},{9,11},{10,... | collective-permute-start | bytes 983048 | tf_op jit(solution)/shard_map/ppermute | solution.py:22
  21.7 13.6 %collective-permute-start.9 = (bf16[128,1280]{1,0:T(8,128)(2,1)S(1)}, bf16[128,1280]{1,0:T(8,128)(2,1)}, u32[]{:S(2)}, u32[]{:S(2)}) collective-permute-start(bf16[128,1280]{1,0:T(8,128)(2,1)S(1)} %collective-permute-done.5), channel_id=1, source_target_pairs={{0,4},{1,5},{2,6},{3,7},{4,0},{5,1},{6,2},{7,3},{8,12},{9,13},{10,... | collective-permute-start | bytes 983048 | tf_op jit(solution)/shard_map/ppermute | solution.py:22
  23.5 16.2 %collective-permute-start.12 = (bf16[80,1024]{1,0:T(8,128)(2,1)S(1)}, bf16[80,1024]{1,0:T(8,128)(2,1)S(1)}, u32[]{:S(2)}, u32[]{:S(2)}) collective-permute-start(bf16[80,1024]{1,0:T(8,128)(2,1)S(1)} %get-tuple-element.37), channel_id=1, source_target_pairs={{0,4},{1,5},{2,6},{3,7},{4,0},{5,1},{6,2},{7,3},{8,12},{9,13},{10,... | collective-permute-start | bytes 491528 | tf_op jit(solution)/shard_map/ppermute | solution.py:22
  23.8 16.0 %collective-permute-start.10 = (bf16[80,1024]{1,0:T(8,128)(2,1)S(1)}, bf16[80,1024]{1,0:T(8,128)(2,1)S(1)}, u32[]{:S(2)}, u32[]{:S(2)}) collective-permute-start(bf16[80,1024]{1,0:T(8,128)(2,1)S(1)} %get-tuple-element.37), channel_id=1, source_target_pairs={{0,12},{1,13},{2,14},{3,15},{4,8},{5,9},{6,10},{7,11},{8,4},{9,5},... | collective-permute-start | bytes 491528 | tf_op jit(solution)/shard_map/ppermute | solution.py:22
  29.7 11.4 %collective-permute-start.11 = (bf16[80,1024]{1,0:T(8,128)(2,1)S(1)}, bf16[80,1024]{1,0:T(8,128)(2,1)S(1)}, u32[]{:S(2)}, u32[]{:S(2)}) collective-permute-start(bf16[80,1024]{1,0:T(8,128)(2,1)S(1)} %get-tuple-element.39.refs_0_), channel_id=1, source_target_pairs={{0,8},{1,9},{2,10},{3,11},{4,12},{5,13},{6,14},{7,15},{8,0},{9,1},... | collective-permute-start | bytes 491528 | tf_op jit(solution)/shard_map/ppermute | solution.py:22
  34.3 17.9 %collective-permute-start.2 = (bf16[256,1664]{1,0:T(8,128)(2,1)S(1)}, bf16[256,1664]{1,0:T(8,128)(2,1)S(1)}, u32[]{:S(2)}, u32[]{:S(2)}) collective-permute-start(bf16[256,1664]{1,0:T(8,128)(2,1)S(1)} %shard_map.78.refs_0_), channel_id=1, source_target_pairs={{0,1},{1,0},{2,3},{3,2},{4,5},{5,4},{6,7},{7,6},{8,9},{9,8},{10,11... | collective-permute-start | bytes 2555912 | tf_op jit(solution)/shard_map/ppermute | solution.py:22
  35.4 16.8 %collective-permute-start.8 = (bf16[256,1664]{1,0:T(8,128)(2,1)S(1)}, bf16[256,1664]{1,0:T(8,128)(2,1)S(1)}, u32[]{:S(2)}, u32[]{:S(2)}) collective-permute-start(bf16[256,1664]{1,0:T(8,128)(2,1)S(1)} %shard_map.80.refs_2_), channel_id=1, source_target_pairs={{0,1},{1,0},{2,3},{3,2},{4,5},{5,4},{6,7},{7,6},{8,9},{9,8},{10,11... | collective-permute-start | bytes 2555912 | tf_op jit(solution)/shard_map/ppermute | solution.py:22
  42.5 9.6 %collective-permute-start.14 = (bf16[240,1024]{1,0:T(8,128)(2,1)S(1)}, bf16[240,1024]{1,0:T(8,128)(2,1)S(1)}, u32[]{:S(2)}, u32[]{:S(2)}) collective-permute-start(bf16[240,1024]{1,0:T(8,128)(2,1)S(1)} %get-tuple-element.40.refs_11_), channel_id=1, source_target_pairs={{0,16},{16,0},{1,17},{17,1},{2,18},{18,2},{3,19},{19,3},{4,20},{20... | collective-permute-start | bytes 1474568 | tf_op jit(solution)/shard_map/ppermute | solution.py:507
  44.1 7.1 %collective-permute-start.13 = (bf16[128,1280]{1,0:T(8,128)(2,1)S(1)}, bf16[128,1280]{1,0:T(8,128)(2,1)S(1)}, u32[]{:S(2)}, u32[]{:S(2)}) collective-permute-start(bf16[128,1280]{1,0:T(8,128)(2,1)S(1)} %broadcast_select_fusion.here), channel_id=1, source_target_pairs={{0,2},{1,3},{2,0},{3,1},{4,6},{5,7},{6,4},{7,5},{8,10},{9,11},{10,... | collective-permute-start | bytes 983048 | tf_op jit(solution)/shard_map/ppermute | solution.py:22
  44.6 7.6 %collective-permute-start.16 = (bf16[240,1024]{1,0:T(8,128)(2,1)S(1)}, bf16[240,1024]{1,0:T(8,128)(2,1)S(1)}, u32[]{:S(2)}, u32[]{:S(2)}) collective-permute-start(bf16[240,1024]{1,0:T(8,128)(2,1)S(1)} %get-tuple-element.40.refs_11_), channel_id=1, source_target_pairs={{0,1},{1,0},{2,3},{3,2},{4,5},{5,4},{6,7},{7,6},{8,9},{9,8},{10,11... | collective-permute-start | bytes 1474568 | tf_op jit(solution)/shard_map/ppermute | solution.py:22
  52.1 2.2 %collective-permute-start.15 = (bf16[256,1280]{1,0:T(8,128)(2,1)S(1)}, bf16[256,1280]{1,0:T(8,128)(2,1)S(1)}, u32[]{:S(2)}, u32[]{:S(2)}) collective-permute-start(bf16[256,1280]{1,0:T(8,128)(2,1)S(1)} %shard_map.81.refs_4_), channel_id=1, source_target_pairs={{0,1},{1,0},{2,3},{3,2},{4,5},{5,4},{6,7},{7,6},{8,9},{9,8},{10,11... | collective-permute-start | bytes 1966088 | tf_op jit(solution)/shard_map/ppermute | solution.py:22
  52.2 2.8 %collective-permute-start.17 = (bf16[240,1024]{1,0:T(8,128)(2,1)S(1)}, bf16[240,1024]{1,0:T(8,128)(2,1)S(1)}, u32[]{:S(2)}, u32[]{:S(2)}) collective-permute-start(bf16[240,1024]{1,0:T(8,128)(2,1)S(1)} %collective-permute-done.14.refs_13_), channel_id=1, source_target_pairs={{0,1},{1,0},{2,3},{3,2},{4,5},{5,4},{6,7},{7,6},{8,9},{9,8},{10,11... | collective-permute-start | bytes 1474568 | tf_op jit(solution)/shard_map/ppermute | solution.py:22
  68.3 1.8 %collective-permute-start.19 = (bf16[512,320]{1,0:T(8,128)(2,1)S(1)}, bf16[512,320]{1,0:T(8,128)(2,1)S(1)}, u32[]{:S(2)}, u32[]{:S(2)}) collective-permute-start(bf16[512,320]{1,0:T(8,128)(2,1)S(1)} %get-tuple-element.47.memory), channel_id=1, source_target_pairs={{0,1},{1,0},{2,3},{3,2},{4,5},{5,4},{6,7},{7,6},{8,9},{9,8},{10,11... | collective-permute-start | bytes 983048 | tf_op jit(solution)/shard_map/ppermute | solution.py:22
  68.5 7.8 %collective-permute-start.21 = (bf16[256,320]{1,0:T(8,128)(2,1)S(1)}, bf16[256,320]{1,0:T(8,128)(2,1)S(1)}, u32[]{:S(2)}, u32[]{:S(2)}) collective-permute-start(bf16[256,320]{1,0:T(8,128)(2,1)S(1)} %get-tuple-element.50), channel_id=1, source_target_pairs={{0,2},{1,6},{2,0},{3,4},{4,3},{5,7},{6,1},{7,5},{8,10},{9,14},{10,... | collective-permute-start | bytes 491528 | tf_op jit(solution)/shard_map/ppermute | solution.py:22
  69.0 7.2 %collective-permute-start.18 = (bf16[256,320]{1,0:T(8,128)(2,1)S(1)}, bf16[256,320]{1,0:T(8,128)(2,1)S(1)}, u32[]{:S(2)}, u32[]{:S(2)}) collective-permute-start(bf16[256,320]{1,0:T(8,128)(2,1)S(1)} %get-tuple-element.44), channel_id=1, source_target_pairs={{0,0},{1,4},{2,2},{3,6},{4,1},{5,5},{6,3},{7,7},{8,8},{9,12},{10,1... | collective-permute-start | bytes 491528 | tf_op jit(solution)/shard_map/ppermute | solution.py:22
  71.4 4.9 %collective-permute-start.20 = (f32[40,128]{1,0:T(8,128)S(1)}, f32[40,128]{1,0:T(8,128)S(1)}, u32[]{:S(2)}, u32[]{:S(2)}) collective-permute-start(f32[40,128]{1,0:T(8,128)S(1)} %get-tuple-element.48), channel_id=1, source_target_pairs={{0,8},{1,9},{2,10},{3,11},{4,12},{5,13},{6,14},{7,15},{8,0},{9,1},... | collective-permute-start | bytes 61448 | tf_op jit(solution)/shard_map/ppermute | solution.py:22
  76.3 4.9 %collective-permute-start.22 = (bf16[256,320]{1,0:T(8,128)(2,1)S(1)}, bf16[256,320]{1,0:T(8,128)(2,1)S(1)}, u32[]{:S(2)}, u32[]{:S(2)}) collective-permute-start(bf16[256,320]{1,0:T(8,128)(2,1)S(1)} %collective-permute-done.18.refs_0_), channel_id=1, source_target_pairs={{0,1},{1,0},{2,3},{3,2},{4,5},{5,4},{6,7},{7,6},{8,9},{9,8},{10,11... | collective-permute-start | bytes 491528 | tf_op jit(solution)/shard_map/ppermute | solution.py:22
  77.4 3.8 %collective-permute-start.23 = (bf16[256,320]{1,0:T(8,128)(2,1)S(1)}, bf16[256,320]{1,0:T(8,128)(2,1)S(1)}, u32[]{:S(2)}, u32[]{:S(2)}) collective-permute-start(bf16[256,320]{1,0:T(8,128)(2,1)S(1)} %collective-permute-done.21.refs_1_), channel_id=1, source_target_pairs={{0,1},{1,0},{2,3},{3,2},{4,5},{5,4},{6,7},{7,6},{8,9},{9,8},{10,11... | collective-permute-start | bytes 491528 | tf_op jit(solution)/shard_map/ppermute | solution.py:22
  77.7 4.9 %collective-permute-start.24 = (bf16[2,384]{1,0:T(2,128)(2,1)S(1)}, bf16[2,384]{1,0:T(2,128)(2,1)S(1)}, u32[]{:S(2)}, u32[]{:S(2)}) collective-permute-start(bf16[2,384]{1,0:T(2,128)(2,1)S(1)} %get-tuple-element.55), channel_id=1, source_target_pairs={{0,2},{1,3},{2,0},{3,1},{4,6},{5,7},{6,4},{7,5},{8,10},{9,11},{10,... | collective-permute-start | bytes 4616 | tf_op jit(solution)/shard_map/ppermute | solution.py:22
  79.2 3.6 %collective-permute-start.25 = (bf16[2,384]{1,0:T(2,128)(2,1)S(1)}, bf16[2,384]{1,0:T(2,128)(2,1)S(1)}, u32[]{:S(2)}, u32[]{:S(2)}) collective-permute-start(bf16[2,384]{1,0:T(2,128)(2,1)S(1)} %get-tuple-element.56), channel_id=1, source_target_pairs={{0,4},{1,5},{2,6},{3,7},{4,0},{5,1},{6,2},{7,3},{8,12},{9,13},{10,... | collective-permute-start | bytes 4616 | tf_op jit(solution)/shard_map/ppermute | solution.py:22
  81.0 4.5 %collective-permute-start.26 = (bf16[2,384]{1,0:T(2,128)(2,1)S(1)}, bf16[2,384]{1,0:T(2,128)(2,1)S(1)}, u32[]{:S(2)}, u32[]{:S(2)}) collective-permute-start(bf16[2,384]{1,0:T(2,128)(2,1)S(1)} %get-tuple-element.57), channel_id=1, source_target_pairs={{0,6},{1,7},{2,4},{3,5},{4,2},{5,3},{6,0},{7,1},{8,14},{9,15},{10,... | collective-permute-start | bytes 4616 | tf_op jit(solution)/shard_map/ppermute | solution.py:22

commit v12 on v11

--- a/solution.py
+++ b/solution.py
@@ -170,7 +170,7 @@
 
 
 def prepare_kernel(table, *refs):
-    parts, (ids, tokens, asked, joined) = refs[:-4], refs[-4:]
+    parts, (ids, tokens, asked, joined, spans) = refs[:-5], refs[-5:]
     rows = joined.shape[0] // 3
     for i in range(3):
         joined[rows * i : rows * i + rows, :] = parts[i + 1][...]
@@ -203,6 +203,16 @@
                     [marks[0:1], marks[1:2]], axis=1
                 )
 
+    row = ids[0:1, :]
+    spot = lax.broadcasted_iota(jnp.int32, (1, 1536), 1).astype(F32)
+    for i in range(4):
+        own = ids[0:1, 512 + 128 * i : 640 + 128 * i]
+        shared = (row >= jnp.min(own)) & (row <= jnp.max(own))
+        low = jnp.min(jnp.where(shared, spot, 9999.0)).astype(jnp.int32) // 128
+        high = jnp.max(jnp.where(shared, spot, 0.0)).astype(jnp.int32) // 128
+        spans[2 * i] = low
+        spans[2 * i + 1] = high - low + 1
+
 
 def prepare(table, parts, count):
     return pl.pallas_call(
@@ -212,15 +222,16 @@
             jax.ShapeDtypeStruct((5 * count, GROUP), F32),
             jax.ShapeDtypeStruct((count, HD), F32),
             jax.ShapeDtypeStruct((3 * parts[0].shape[0], 1024), BF),
+            jax.ShapeDtypeStruct((8,), jnp.int32),
         ),
         in_specs=[SMEM] + [VMEM] * len(parts),
-        out_specs=(VMEM,) * 4,
+        out_specs=(VMEM,) * 4 + (SMEM,),
         cost_estimate=CHEAP,
         compiler_params=pltpu.CompilerParams(vmem_limit_bytes=8 * 1024 * 1024),
     )(table, *parts)
 
 
-def encoder_kernel(n_parts, depth, places, *refs):
+def encoder_kernel(n_parts, depth, places, spans, *refs):
     layers = [refs[2 * i : 2 * i + 2] for i in range(3)]
     ids = refs[6]
     parts = refs[7 : 7 + n_parts]
@@ -238,10 +249,16 @@
     for slab in range(3):
         values[:, 256 * slab + 128 : 256 * slab + 256] = jnp.ones((1536, 128), BF)
     spots = [places[i] for i in (0, 2, 1, 3)]
+    largest = [jnp.zeros((1, 256), F32), jnp.zeros((1, 128), F32)]
     for i, halves in enumerate(layers):
         place = places[8 + i]
         normed = jnp.concatenate([half[:, :1280] for half in halves], axis=0)
-        found = jnp.dot(normed, weight[:, 256:896], preferred_element_type=F32).astype(BF)
+        found = jnp.dot(normed, weight[:, 256:896], preferred_element_type=F32)
+        for j, lanes in enumerate((slice(0, 256), slice(512, 640))):
+            largest[j] = jnp.maximum(
+                largest[j], jnp.max(jnp.abs(found[:, lanes]), axis=0, keepdims=True)
+            )
+        found = found.astype(BF)
         for j, spot in enumerate(spots):
             to = pl.ds(pl.multiple_of(place + spot, 128), 128)
             block = found[128 * j : 128 * j + 128]
@@ -265,30 +282,21 @@
                     queries[to, WIDE:] = tail[rows]
                     residual[to, :] = halves[j // 2][128 * (j % 2) : 128 * (j % 2) + 128, 1280:]
 
-    side = lax.broadcasted_iota(jnp.int32, (8, 128), 0) == lax.broadcasted_iota(
-        jnp.int32, (8, 128), 1
-    ) // HD
-    sides = jnp.where(side, 1.0, 0.0).astype(BF)
-    only = jnp.where(side & (lax.broadcasted_iota(jnp.int32, (8, 128), 0) == 0), 1.0, 0.0).astype(BF)
-    most = []
-    for held in (queries, keys):
-        top = jnp.zeros((8, 1), F32)
-        for slab in range(3):
-            part = held[:, 128 * slab : 128 * slab + 128]
-            norms = lax.dot_general(
-                sides if slab < 2 else only,
-                part * part,
-                (((1,), (1,)), ((), ())),
-                preferred_element_type=F32,
-            )
-            top = jnp.maximum(top, jnp.max(norms, axis=-1, keepdims=True))
-        most.append(jnp.max(top))
-    small = most[0] * most[1] < 220000.0
-
-    def attend(step, shifted):
+    lane = lax.broadcasted_iota(jnp.int32, (8, 384), 1) // HD
+    head = lax.broadcasted_iota(jnp.int32, (8, 384), 0)
+    most = jnp.concatenate(largest, axis=1) * 1.01
+    most = jnp.where((lane == head) & (head < 5), most, 0.0).astype(BF)
+    bounds = lax.dot_general(
+        most, jnp.abs(queries[...]), (((1,), (1,)), ((), ())), preferred_element_type=F32
+    )
+    small = jnp.max(bounds) < 480.0
+
+    def attend(step, blocks, shifted):
+        count = 128 * blocks
+        start = pl.multiple_of(128 * jnp.minimum(spans[2 * step], 12 - blocks), 128)
         row = step * 128 if isinstance(step, int) else pl.multiple_of(step * 128, 128)
         mine = jnp.broadcast_to(ids[0:1, pl.ds(row + 512, 128)], (128, 128)).T[:, 0:1]
-        bias = jnp.where(mine == ids[0:1, pl.ds(row, 1152)], 0.0, LOW)
+        bias = jnp.where(mine == ids[0:1, pl.ds(start, count)], 0.0, LOW)
         lane = lax.broadcasted_iota(jnp.int32, (128, 128), 1)
         for slab in range(3):
             span = slice(128 * slab, 128 * slab + 128)
@@ -302,7 +310,7 @@
                 mask = jnp.concatenate([bias, bias], axis=0)
             scores = lax.dot_general(
                 query,
-                keys[pl.ds(row, 1152), span],
+                keys[pl.ds(start, count), span],
                 (((1,), (1,)), ((), ())),
                 preferred_element_type=F32,
             )
@@ -312,7 +320,7 @@
             raised = jnp.exp(scores).astype(BF)
             out = jnp.dot(
                 raised,
-                values[pl.ds(row, 1152), 256 * slab : 256 * slab + 256],
+                values[pl.ds(start, count), 256 * slab : 256 * slab + 256],
                 preferred_element_type=F32,
             )
             out = out[:, :128] / out[:, 128:]
@@ -324,20 +332,23 @@
                 stem = residual[pl.ds(row, 128), WIDE:GROUP].astype(F32)
                 memory[pl.ds(row, 128), WIDE:] = (stem + out[:, HD:]).astype(BF)
 
-    @pl.when(small)
-    def _():
-        for step in range(4):
-            attend(step, False)
+    for step in range(4):
+        needed = spans[2 * step + 1]
+        for least, blocks in ((0, 5), (5, 7), (7, 9)):
+
+            @pl.when(small & (needed > least) & ((needed <= blocks) | (blocks == 9)))
+            def _():
+                attend(step, blocks, False)
 
     @pl.when(jnp.logical_not(small))
     def _():
-        lax.fori_loop(0, 4, lambda step, carry: (attend(step, True), carry)[1], 0)
+        lax.fori_loop(0, 4, lambda step, carry: (attend(step, 9, True), carry)[1], 0)
 
     near[...] = memory[pl.ds(pl.multiple_of(256 * x, 256), 256), :]
     away[...] = memory[pl.ds(pl.multiple_of(256 * (1 - x), 256), 256), :]
 
 
-def encoder(places, layers, ids, parts, depth):
+def encoder(places, spans, layers, ids, parts, depth):
     operands = layers + [ids] + parts
     return pl.pallas_call(
         functools.partial(encoder_kernel, len(parts), depth),
@@ -346,7 +357,7 @@
             jax.ShapeDtypeStruct((256, GROUP), BF),
             jax.ShapeDtypeStruct((256, GROUP), BF),
         ),
-        in_specs=[SMEM] + [VMEM] * len(operands),
+        in_specs=[SMEM] * 2 + [VMEM] * len(operands),
         out_specs=(VMEM, VMEM, VMEM),
         scratch_shapes=[
             pltpu.VMEM((1280, 1024), BF),
@@ -357,7 +368,7 @@
         ],
         cost_estimate=CHEAP,
         compiler_params=pltpu.CompilerParams(vmem_limit_bytes=24 * 1024 * 1024),
-    )(places, *operands)
+    )(places, spans, *operands)
 
 
 def cross_kernel(base, table, tokens, asked, memory, beside, *refs):
@@ -518,7 +529,7 @@
         pair_x = swap(after(pair, ready[0]), n, 2)
         halo = jnp.where((z == 1) | (z == 2), near, relayed)
         halo_x = swap(after(halo, pair_x, *here.values()), n, 2)
-        ids, tokens, asked, joined = prepare(table, [after(ready[0], halo), here[1], here[2], here[3]], n)
+        ids, tokens, asked, joined, spans = prepare(table, [after(ready[0], halo), here[1], here[2], here[3]], n)
         traded = trade(joined)
         own_half = norm_half(table, gain, stem, stem_x)
         pair_half = norm_half(table, gain, pair, pair_x)
@@ -558,7 +569,8 @@
         marks = jnp.pad(marks, (512, 512))
         marks = lax.dynamic_slice_in_dim(marks, 512 * quarter, 1536, 0)
         ids = jnp.broadcast_to(marks[None], (8, 1536))
-    held, stay, leave = encoder(table, layered, ids, weights, depth)
+        spans = scalars([0, 9, 1, 9, 2, 9, 3, 9])
+    held, stay, leave = encoder(table, spans, layered, ids, weights, depth)
 
     partial = cross_partial(base, table, tokens, asked, held, swap(held, n, 1))
     owned = [partial[0]] + [swap(partial[i], n, 8 * i) for i in range(1, n // 8)]

time: 87 us -> 89.8 us (1.032)
  starting transfers between devices: 26 us -> 32.1 us
  waiting for transfers between devices: 33.5 us -> 29.4 us
    ppermute x26, starting transfers between devices: 24.4 us -> 30.5 us  [send(): return lax.ppermute(block, 'tm', route)]
    ppermute x26, waiting for transfers between devices: 33.5 us -> 28.1 us  [send(): return lax.ppermute(block, 'tm', route)]
    ppermute x1, waiting for transfers between devices: 0.01 us -> 1.3 us  [trade(): return lax.ppermute(block, 'utt', [(u, u ^ 1) for u in range(utts)])]
    pallas_call x1, Pallas kernels: 1.33 us -> 2.6 us  [prepare(): pl.pallas_call(prepare_kernel, out_shape=(jax.ShapeDtypeStruct((8, 1536),...]
  transfers between devices with their start and end apart: 27 -> 27, of which waited for: 13 -> 14; matrix products, arithmetic and copies ran while one was open for 1% -> 1% of each run, Pallas kernels for 9% -> 10%
where the time goes in v12:
time: 89.8 us; the launch traced here: 89.5 us
  starting transfers between devices  32.1 us (36%)
  waiting for transfers between devices  29.4 us (33%)
  Pallas kernels  24.1 us (27%)
  local copies, waits for them, and re-layouts  1.87 us (2%)
  other arithmetic  1.02 us (1%)
  between operations  0.9 us (1%)
    ppermute x26, starting transfers between devices, send(): return lax.ppermute(block, 'tm', route)  30.5 us
    ppermute x26, waiting for transfers between devices, send(): return lax.ppermute(block, 'tm', route)  28.1 us
    pallas_call x1, Pallas kernels, encoder(): pl.pallas_call(functools.partial(encoder_kernel, len(parts), depth), out_...  12.7 us
    pallas_call x3, Pallas kernels, norm_half(): pl.pallas_call(norm_kernel, out_shape=jax.ShapeDtypeStruct((256, 1664 if...  2.93 us
    pallas_call x1, Pallas kernels, prepare(): pl.pallas_call(prepare_kernel, out_shape=(jax.ShapeDtypeStruct((8, 1536),...  2.6 us
    pallas_call x2, Pallas kernels, gather_groups(): pl.pallas_call(functools.partial(gather_kernel, side, rows), out_shape=ja...  2.59 us
  transfers between devices with their start and end apart: 27, of which 14 were waited for; matrix products, arithmetic and copies ran while one was open for 1% of the time, Pallas kernels for 10%

profile of v12, /device:TPU:0, one launch (start us, length us, event | category | flops | bytes accessed | tf_op | source)
XLA Modules:
  0.0 89.5 jit_solution(16300372958803279489)
XLA Ops:
  0.7 0.0 copy-start.2
  0.7 0.1 stack.136.table.places
  0.8 0.0 copy-start.3
  0.9 0.0 copy-start.4
  0.9 0.5 copy-done.2
  1.4 0.1 copy-done.3
  1.5 1.1 %copy-done = bf16[80,3840]{1,0:T(8,128)(2,1)S(1)} copy-done((bf16[80,3840]{1,0:T(8,128)(2,1)S(1)}, bf16[80,3840]{1,0:T(8,128)(2,1)}, u32[]{:S(2)}) %copy-start) | copy-done | bytes 614424
  2.6 1.1 %shard_map.77 = (bf16[2,80,1024]{2,1,0:T(8,128)(2,1)S(1)}, bf16[2,80,1024]{2,1,0:T(8,128)(2,1)S(1)}) custom-call(s32[34]{0:T(128)S(1)} %stack.136.table.places, bf16[80,3840]{1,0:T(8,128)(2,1)S(1)} %copy-done, bf16[2,1280]{1,0:T(2,128)(2,1)S(1)} %copy-done.2, s32[2,16]{1,0:T(2,128)S(1)} %copy-done.3, s32[1,128]{1,0:T(1,128)S(1)} %bitcast.33), custom_call_target="tpu_custom_call" | custom-call | flops 1 | bytes 1 | tf_op jit(solution)/shard_map/pallas_call | solution.py:98
  3.8 3.0 %collective-permute-start.1 = (bf16[2,80,1024]{2,1,0:T(8,128)(2,1)S(1)}, bf16[2,80,1024]{2,1,0:T(8,128)(2,1)S(1)}, u32[]{:S(2)}, u32[]{:S(2)}) collective-permute-start(bf16[2,80,1024]{2,1,0:T(8,128)(2,1)S(1)} %get-tuple-element.32), channel_id=1, source_target_pairs={{0,2},{1,3},{2,0},{3,1},{4,6},{5,7},{6,4},{7,5},{8,10},{9,11},{10,... | collective-permute-start | bytes 983048 | tf_op jit(solution)/shard_map/ppermute | solution.py:22
  6.8 1.6 %collective-permute-start.3 = (bf16[128,1280]{1,0:T(8,128)(2,1)S(1)}, bf16[128,1280]{1,0:T(8,128)(2,1)S(1)}, u32[]{:S(2)}, u32[]{:S(2)}) collective-permute-start(bf16[128,1280]{1,0:T(8,128)(2,1)S(1)} %copy-done.1), channel_id=1, source_target_pairs={{0,4},{1,5},{2,6},{3,7},{4,0},{5,1},{6,2},{7,3},{8,12},{9,13},{10,... | collective-permute-start | bytes 983048 | tf_op jit(solution)/shard_map/ppermute | solution.py:22
  8.4 0.7 collective-permute-start.2
  9.0 0.1 collective-permute-start
  9.1 5.4 %collective-permute-done.1.refs_2_.refs_9_ = bf16[2,80,1024]{2,1,0:T(8,128)(2,1)S(1)} collective-permute-done((bf16[2,80,1024]{2,1,0:T(8,128)(2,1)S(1)}, bf16[2,80,1024]{2,1,0:T(8,128)(2,1)S(1)}, u32[]{:S(2)}, u32[]{:S(2)}) %collective-permute-start.1) | collective-permute-done | bytes 327712 | tf_op jit(solution)/shard_map/ppermute | solution.py:22
  14.5 0.0 collective-permute-start.4
  14.5 1.5 %collective-permute-done.3.here = bf16[128,1280]{1,0:T(8,128)(2,1)S(1)} collective-permute-done((bf16[128,1280]{1,0:T(8,128)(2,1)S(1)}, bf16[128,1280]{1,0:T(8,128)(2,1)S(1)}, u32[]{:S(2)}, u32[]{:S(2)}) %collective-permute-start.3) | collective-permute-done | bytes 327712 | tf_op jit(solution)/shard_map/ppermute | solution.py:22
  15.9 0.0 collective-permute-done.2
  15.9 0.4 collective-permute-start.9
  16.3 0.0 collective-permute-done.refs_1_.refs_8_
  16.3 0.0 collective-permute-done.4.refs_3_.refs_10_
  16.3 0.6 shard_map.78
  16.9 1.7 %collective-permute-start.11 = (bf16[128,1280]{1,0:T(8,128)(2,1)S(1)}, bf16[128,1280]{1,0:T(8,128)(2,1)S(1)}, u32[]{:S(2)}, u32[]{:S(2)}) collective-permute-start(bf16[128,1280]{1,0:T(8,128)(2,1)S(1)} %collective-permute-done.3.here), channel_id=1, source_target_pairs={{0,2},{1,3},{2,0},{3,1},{4,6},{5,7},{6,4},{7,5},{8,10},{9,11},{10,... | collective-permute-start | bytes 983048 | tf_op jit(solution)/shard_map/ppermute | solution.py:22
  18.7 4.6 %collective-permute-start.5 = (bf16[128,1280]{1,0:T(8,128)(2,1)S(1)}, bf16[128,1280]{1,0:T(8,128)(2,1)}, u32[]{:S(2)}, u32[]{:S(2)}) collective-permute-start(bf16[128,1280]{1,0:T(8,128)(2,1)S(1)} %collective-permute-done.2), channel_id=1, source_target_pairs={{0,4},{1,5},{2,6},{3,7},{4,0},{5,1},{6,2},{7,3},{8,12},{9,13},{10,... | collective-permute-start | bytes 983048 | tf_op jit(solution)/shard_map/ppermute | solution.py:22
  23.3 2.6 %collective-permute-start.8 = (bf16[80,1024]{1,0:T(8,128)(2,1)S(1)}, bf16[80,1024]{1,0:T(8,128)(2,1)S(1)}, u32[]{:S(2)}, u32[]{:S(2)}) collective-permute-start(bf16[80,1024]{1,0:T(8,128)(2,1)S(1)} %get-tuple-element.37), channel_id=1, source_target_pairs={{0,12},{1,13},{2,14},{3,15},{4,8},{5,9},{6,10},{7,11},{8,4},{9,5},... | collective-permute-start | bytes 491528 | tf_op jit(solution)/shard_map/ppermute | solution.py:22
  25.9 0.0 collective-permute-start.6
  25.9 0.7 collective-permute-done.9.across
  26.6 5.8 %collective-permute-start.7 = (bf16[80,1024]{1,0:T(8,128)(2,1)S(1)}, bf16[80,1024]{1,0:T(8,128)(2,1)S(1)}, u32[]{:S(2)}, u32[]{:S(2)}) collective-permute-start(bf16[80,1024]{1,0:T(8,128)(2,1)S(1)} %get-tuple-element.36.refs_0_), channel_id=1, source_target_pairs={{0,8},{1,9},{2,10},{3,11},{4,12},{5,13},{6,14},{7,15},{8,0},{9,1},... | collective-permute-start | bytes 491528 | tf_op jit(solution)/shard_map/ppermute | solution.py:22
  32.4 1.0 %shard_map.80.refs_0_ = bf16[256,1664]{1,0:T(8,128)(2,1)S(1)} custom-call(s32[34]{0:T(128)S(1)} %stack.136.table.places, f32[1,1280]{1,0:T(1,128)S(1)} %reshape.11.gain, bf16[128,1280]{1,0:T(8,128)(2,1)S(1)} %copy-done.1, bf16[128,1280]{1,0:T(8,128)(2,1)S(1)} %collective-permute-done.9.across), custom_call_target="tpu_custom_call" | custom-call | flops 1 | bytes 1 | tf_op jit(solution)/shard_map/pallas_call | solution.py:162
  33.4 0.0 collective-permute-done.11.across
  33.4 0.1 collective-permute-start.10
  33.4 1.0 %shard_map.81.refs_2_ = bf16[256,1664]{1,0:T(8,128)(2,1)S(1)} custom-call(s32[34]{0:T(128)S(1)} %stack.136.table.places, f32[1,1280]{1,0:T(1,128)S(1)} %reshape.11.gain, bf16[128,1280]{1,0:T(8,128)(2,1)S(1)} %collective-permute-done.3.here, bf16[128,1280]{1,0:T(8,128)(2,1)S(1)} %collective-permute-done.11.across), custom_call_target="tpu_custom_call" | custom-call | flops 1 | bytes 1 | tf_op jit(solution)/shard_map/pallas_call | solution.py:162
  34.4 1.8 %collective-permute-done.5 = bf16[128,1280]{1,0:T(8,128)(2,1)} collective-permute-done((bf16[128,1280]{1,0:T(8,128)(2,1)S(1)}, bf16[128,1280]{1,0:T(8,128)(2,1)}, u32[]{:S(2)}, u32[]{:S(2)}) %collective-permute-start.5) | collective-permute-done | bytes 327712 | tf_op jit(solution)/shard_map/ppermute | solution.py:22
  36.2 0.0 collective-permute-start.12
  36.2 1.0 %broadcast_select_fusion.here = bf16[128,1280]{1,0:T(8,128)(2,1)S(1)} fusion(bf16[128,1280]{1,0:T(8,128)(2,1)S(1)} %collective-permute-done.2, bf16[128,1280]{1,0:T(8,128)(2,1)} %collective-permute-done.5, pred[]{:T(512)S(6)} %or.3), kind=kLoop, calls=%fused_computation | loop fusion | flops 163840 | bytes 983041 | tf_op jit(solution)/shard_map/jit(_where)/select_n | solution.py:530
  37.3 0.8 collective-permute-done.8.refs_3_
  38.1 1.7 %collective-permute-done.6.refs_1_ = bf16[80,1024]{1,0:T(8,128)(2,1)S(1)} collective-permute-done((bf16[80,1024]{1,0:T(8,128)(2,1)S(1)}, bf16[80,1024]{1,0:T(8,128)(2,1)S(1)}, u32[]{:S(2)}, u32[]{:S(2)}) %collective-permute-start.6) | collective-permute-done | bytes 163872 | tf_op jit(solution)/shard_map/ppermute | solution.py:22
  39.7 0.0 collective-permute-done.7.refs_2_
  39.7 2.6 %shard_map.79 = (f32[8,1536]{1,0:T(8,128)S(1)}, f32[80,320]{1,0:T(8,128)S(1)}, f32[16,64]{1,0:T(8,128)S(1)}, bf16[240,1024]{1,0:T(8,128)(2,1)S(1)}, s32[8]{0:T(128)S(1)}) custom-call(s32[34]{0:T(128)S(1)} %stack.136.table.places, bf16[80,1024]{1,0:T(8,128)(2,1)S(1)} %get-tuple-element.36.refs_0_, bf16[80,1024]{1,0:T(8,128)(2,1)S(1)} %collective-permute-done.6.refs_1_, ...), custom_call_target="tpu_custom_call" | custom-call | flops 1 | bytes 1 | tf_op jit(solution)/shard_map/pallas_call | solution.py:218
  42.3 1.6 %collective-permute-start.14 = (bf16[240,1024]{1,0:T(8,128)(2,1)S(1)}, bf16[240,1024]{1,0:T(8,128)(2,1)S(1)}, u32[]{:S(2)}, u32[]{:S(2)}) collective-permute-start(bf16[240,1024]{1,0:T(8,128)(2,1)S(1)} %get-tuple-element.42.refs_11_), channel_id=1, source_target_pairs={{0,16},{16,0},{1,17},{17,1},{2,18},{18,2},{3,19},{19,3},{4,20},{20... | collective-permute-start | bytes 1474568 | tf_op jit(solution)/shard_map/ppermute | solution.py:518
  43.9 0.5 collective-permute-start.13
  44.5 0.0 collective-permute-start.16
  44.5 7.1 %collective-permute-done.13.across = bf16[128,1280]{1,0:T(8,128)(2,1)S(1)} collective-permute-done((bf16[128,1280]{1,0:T(8,128)(2,1)S(1)}, bf16[128,1280]{1,0:T(8,128)(2,1)S(1)}, u32[]{:S(2)}, u32[]{:S(2)}) %collective-permute-start.13) | collective-permute-done | bytes 327712 | tf_op jit(solution)/shard_map/ppermute | solution.py:22
  51.6 1.0 %shard_map.82.refs_4_ = bf16[256,1280]{1,0:T(8,128)(2,1)S(1)} custom-call(s32[34]{0:T(128)S(1)} %stack.136.table.places, f32[1,1280]{1,0:T(1,128)S(1)} %reshape.11.gain, bf16[128,1280]{1,0:T(8,128)(2,1)S(1)} %broadcast_select_fusion.here, bf16[128,1280]{1,0:T(8,128)(2,1)S(1)} %collective-permute-done.13.across), custom_call_target="tpu_custom_call" | custom-call | flops 1 | bytes 1 | tf_op jit(solution)/shard_map/pallas_call | solution.py:162
  52.5 1.3 %collective-permute-done.14.refs_13_ = bf16[240,1024]{1,0:T(8,128)(2,1)S(1)} collective-permute-done((bf16[240,1024]{1,0:T(8,128)(2,1)S(1)}, bf16[240,1024]{1,0:T(8,128)(2,1)S(1)}, u32[]{:S(2)}, u32[]{:S(2)}) %collective-permute-start.14) | collective-permute-done | bytes 491552 | tf_op jit(solution)/shard_map/ppermute | solution.py:518
  53.8 0.6 collective-permute-start.17
  54.4 1.5 %collective-permute-done.15.refs_5_ = bf16[256,1280]{1,0:T(8,128)(2,1)S(1)} collective-permute-done((bf16[256,1280]{1,0:T(8,128)(2,1)S(1)}, bf16[256,1280]{1,0:T(8,128)(2,1)S(1)}, u32[]{:S(2)}, u32[]{:S(2)}) %collective-permute-start.15) | collective-permute-done | bytes 655392 | tf_op jit(solution)/shard_map/ppermute | solution.py:22
  55.9 0.7 collective-permute-done.17.refs_14_
  56.6 12.7 %shard_map.83 = (bf16[512,320]{1,0:T(8,128)(2,1)S(1)}, bf16[256,320]{1,0:T(8,128)(2,1)S(1)}, bf16[256,320]{1,0:T(8,128)(2,1)S(1)}) custom-call(s32[34]{0:T(128)S(1)} %stack.136.table.places, s32[8]{0:T(128)S(1)} %get-tuple-element.38.spans, bf16[256,1664]{1,0:T(8,128)(2,1)S(1)} %shard_map.80.refs_0_, bf16[256,1664]{1,0:T(8,128)(2,1)S(1)} %collective-permute-done.10.refs_1_, ...), custom_call_target="tpu_custom_call" | custom-call | flops 1 | bytes 1 | tf_op jit(solution)/shard_map/pallas_call | solution.py:353
  69.4 0.2 collective-permute-start.19
  69.6 0.5 collective-permute-start.21
  70.1 0.7 collective-permute-start.18
  70.8 0.4 collective-permute-done.19.beside
  71.2 1.3 %shard_map.84 = (f32[40,128]{1,0:T(8,128)S(1)}, f32[40,128]{1,0:T(8,128)S(1)}) custom-call(s32[34]{0:T(128)S(1)} %stack.136.table.places, f32[80,320]{1,0:T(8,128)S(1)} %get-tuple-element.47.tokens, f32[16,64]{1,0:T(8,128)S(1)} %get-tuple-element.48.asked, bf16[512,320]{1,0:T(8,128)(2,1)S(1)} %get-tuple-element.49.memory, ...), custom_call_target="tpu_custom_call" | custom-call | flops 1 | bytes 1 | tf_op jit(solution)/shard_map/pallas_call | solution.py:419
  72.5 1.3 %collective-permute-start.20 = (f32[40,128]{1,0:T(8,128)S(1)}, f32[40,128]{1,0:T(8,128)S(1)}, u32[]{:S(2)}, u32[]{:S(2)}) collective-permute-start(f32[40,128]{1,0:T(8,128)S(1)} %get-tuple-element.50), channel_id=1, source_target_pairs={{0,8},{1,9},{2,10},{3,11},{4,12},{5,13},{6,14},{7,15},{8,0},{9,1},... | collective-permute-start | bytes 61448 | tf_op jit(solution)/shard_map/ppermute | solution.py:22
  73.8 3.6 %collective-permute-done.21.refs_1_ = bf16[256,320]{1,0:T(8,128)(2,1)S(1)} collective-permute-done((bf16[256,320]{1,0:T(8,128)(2,1)S(1)}, bf16[256,320]{1,0:T(8,128)(2,1)S(1)}, u32[]{:S(2)}, u32[]{:S(2)}) %collective-permute-start.21) | collective-permute-done | bytes 163872 | tf_op jit(solution)/shard_map/ppermute | solution.py:22
  77.4 1.1 %collective-permute-start.22 = (bf16[256,320]{1,0:T(8,128)(2,1)S(1)}, bf16[256,320]{1,0:T(8,128)(2,1)S(1)}, u32[]{:S(2)}, u32[]{:S(2)}) collective-permute-start(bf16[256,320]{1,0:T(8,128)(2,1)S(1)} %collective-permute-done.18.refs_0_), channel_id=1, source_target_pairs={{0,1},{1,0},{2,3},{3,2},{4,5},{5,4},{6,7},{7,6},{8,9},{9,8},{10,11... | collective-permute-start | bytes 491528 | tf_op jit(solution)/shard_map/ppermute | solution.py:22
  78.5 0.0 collective-permute-start.23
  78.5 0.2 shard_map.86
  78.7 1.6 %collective-permute-start.24 = (bf16[2,384]{1,0:T(2,128)(2,1)S(1)}, bf16[2,384]{1,0:T(2,128)(2,1)S(1)}, u32[]{:S(2)}, u32[]{:S(2)}) collective-permute-start(bf16[2,384]{1,0:T(2,128)(2,1)S(1)} %get-tuple-element.57), channel_id=1, source_target_pairs={{0,2},{1,3},{2,0},{3,1},{4,6},{5,7},{6,4},{7,5},{8,10},{9,11},{10,... | collective-permute-start | bytes 4616 | tf_op jit(solution)/shard_map/ppermute | solution.py:22
  80.3 3.5 %collective-permute-start.25 = (bf16[2,384]{1,0:T(2,128)(2,1)S(1)}, bf16[2,384]{1,0:T(2,128)(2,1)S(1)}, u32[]{:S(2)}, u32[]{:S(2)}) collective-permute-start(bf16[2,384]{1,0:T(2,128)(2,1)S(1)} %get-tuple-element.58), channel_id=1, source_target_pairs={{0,4},{1,5},{2,6},{3,7},{4,0},{5,1},{6,2},{7,3},{8,12},{9,13},{10,... | collective-permute-start | bytes 4616 | tf_op jit(solution)/shard_map/ppermute | solution.py:22
  83.8 0.1 collective-permute-start.26
  83.9 1.4 %shard_map.85 = bf16[128,1280]{1,0:T(8,128)(2,1)} custom-call(s32[34]{0:T(128)S(1)} %stack.136.table.places, bf16[256,320]{1,0:T(8,128)(2,1)S(1)} %collective-permute-done.18.refs_0_, bf16[256,320]{1,0:T(8,128)(2,1)S(1)} %collective-permute-done.21.refs_1_, bf16[256,320]{1,0:T(8,128)(2,1)S(1)} %collective-permute-done.22.refs_2_, ...), custom_call_target="tpu_custom_call" | custom-call | flops 1 | bytes 1 | tf_op jit(solution)/shard_map/pallas_call | solution.py:473
  85.3 0.1 collective-permute-done.25.refs_2_
  85.4 2.9 %collective-permute-done.26.refs_3_ = bf16[2,384]{1,0:T(2,128)(2,1)S(1)} collective-permute-done((bf16[2,384]{1,0:T(2,128)(2,1)S(1)}, bf16[2,384]{1,0:T(2,128)(2,1)S(1)}, u32[]{:S(2)}, u32[]{:S(2)}) %collective-permute-start.26) | collective-permute-done | bytes 1568 | tf_op jit(solution)/shard_map/ppermute | solution.py:22
  88.3 1.2 %shard_map.87 = bf16[2,1280]{1,0:T(2,128)(2,1)} custom-call(s32[34]{0:T(128)S(1)} %stack.136.table.places, bf16[2,384]{1,0:T(2,128)(2,1)S(1)} %get-tuple-element.56.refs_0_, bf16[2,384]{1,0:T(2,128)(2,1)S(1)} %collective-permute-done.24.refs_1_, bf16[2,384]{1,0:T(2,128)(2,1)S(1)} %collective-permute-done.25.refs_2_, ...), custom_call_target="tpu_custom_call" | custom-call | flops 1 | bytes 1 | tf_op jit(solution)/shard_map/pallas_call | solution.py:473
  (16 shorter events, 0.0 us)
Async XLA Ops:
  0.7 0.7 copy-start.2
  0.8 0.7 copy-start.3
  0.9 0.7 copy-start.4
  1.5 1.1 %copy-start = (bf16[80,3840]{1,0:T(8,128)(2,1)S(1)}, bf16[80,3840]{1,0:T(8,128)(2,1)}, u32[]{:S(2)}) copy-start(bf16[80,3840]{1,0:T(8,128)(2,1)} %refs_0_.1) | copy-start | bytes 1843204
  2.6 4.2 %copy-start.1 = (bf16[128,1280]{1,0:T(8,128)(2,1)S(1)}, bf16[128,1280]{1,0:T(8,128)(2,1)}, u32[]{:S(2)}) copy-start(bf16[128,1280]{1,0:T(8,128)(2,1)} %here.1) | copy-start | bytes 983044
  3.8 10.7 %collective-permute-start.1 = (bf16[2,80,1024]{2,1,0:T(8,128)(2,1)S(1)}, bf16[2,80,1024]{2,1,0:T(8,128)(2,1)S(1)}, u32[]{:S(2)}, u32[]{:S(2)}) collective-permute-start(bf16[2,80,1024]{2,1,0:T(8,128)(2,1)S(1)} %get-tuple-element.32), channel_id=1, source_target_pairs={{0,2},{1,3},{2,0},{3,1},{4,6},{5,7},{6,4},{7,5},{8,10},{9,11},{10,... | collective-permute-start | bytes 983048 | tf_op jit(solution)/shard_map/ppermute | solution.py:22
  6.8 9.2 %collective-permute-start.3 = (bf16[128,1280]{1,0:T(8,128)(2,1)S(1)}, bf16[128,1280]{1,0:T(8,128)(2,1)S(1)}, u32[]{:S(2)}, u32[]{:S(2)}) collective-permute-start(bf16[128,1280]{1,0:T(8,128)(2,1)S(1)} %copy-done.1), channel_id=1, source_target_pairs={{0,4},{1,5},{2,6},{3,7},{4,0},{5,1},{6,2},{7,3},{8,12},{9,13},{10,... | collective-permute-start | bytes 983048 | tf_op jit(solution)/shard_map/ppermute | solution.py:22
  8.4 7.6 %collective-permute-start.2 = (bf16[128,1280]{1,0:T(8,128)(2,1)S(1)}, bf16[128,1280]{1,0:T(8,128)(2,1)S(1)}, u32[]{:S(2)}, u32[]{:S(2)}) collective-permute-start(bf16[128,1280]{1,0:T(8,128)(2,1)S(1)} %copy-done.1), channel_id=1, source_target_pairs={{4,8},{5,9},{6,10},{7,11},{8,4},{9,5},{10,6},{11,7},{20,24},{21,25... | collective-permute-start | bytes 983048 | tf_op jit(solution)/shard_map/ppermute | solution.py:22
  9.0 7.3 %collective-permute-start = (bf16[2,80,1024]{2,1,0:T(8,128)(2,1)S(1)}, bf16[2,80,1024]{2,1,0:T(8,128)(2,1)S(1)}, u32[]{:S(2)}, u32[]{:S(2)}) collective-permute-start(bf16[2,80,1024]{2,1,0:T(8,128)(2,1)S(1)} %get-tuple-element.31.refs_0_.refs_7_), channel_id=1, source_target_pairs={{0,1},{1,0},{2,3},{3,2},{4,5},{5,4},{6,7},{7,6},{8,9},{9,8},{10,11... | collective-permute-start | bytes 983048 | tf_op jit(solution)/shard_map/ppermute | solution.py:22
  14.5 1.8 %collective-permute-start.4 = (bf16[2,80,1024]{2,1,0:T(8,128)(2,1)S(1)}, bf16[2,80,1024]{2,1,0:T(8,128)(2,1)S(1)}, u32[]{:S(2)}, u32[]{:S(2)}) collective-permute-start(bf16[2,80,1024]{2,1,0:T(8,128)(2,1)S(1)} %collective-permute-done.1.refs_2_.refs_9_), channel_id=1, source_target_pairs={{0,1},{1,0},{2,3},{3,2},{4,5},{5,4},{6,7},{7,6},{8,9},{9,8},{10,11... | collective-permute-start | bytes 983048 | tf_op jit(solution)/shard_map/ppermute | solution.py:22
  15.9 10.6 %collective-permute-start.9 = (bf16[128,1280]{1,0:T(8,128)(2,1)S(1)}, bf16[128,1280]{1,0:T(8,128)(2,1)S(1)}, u32[]{:S(2)}, u32[]{:S(2)}) collective-permute-start(bf16[128,1280]{1,0:T(8,128)(2,1)S(1)} %copy-done.1), channel_id=1, source_target_pairs={{0,2},{1,3},{2,0},{3,1},{4,6},{5,7},{6,4},{7,5},{8,10},{9,11},{10,... | collective-permute-start | bytes 983048 | tf_op jit(solution)/shard_map/ppermute | solution.py:22
  16.3 6.9 %copy-start.5 = (f32[1280]{0:T(1024)S(1)}, f32[1280]{0:T(1024)}, u32[]{:S(2)}) copy-start(f32[1280]{0:T(1024)} %param.7) | copy-start | bytes 15364
  16.9 16.4 %collective-permute-start.11 = (bf16[128,1280]{1,0:T(8,128)(2,1)S(1)}, bf16[128,1280]{1,0:T(8,128)(2,1)S(1)}, u32[]{:S(2)}, u32[]{:S(2)}) collective-permute-start(bf16[128,1280]{1,0:T(8,128)(2,1)S(1)} %collective-permute-done.3.here), channel_id=1, source_target_pairs={{0,2},{1,3},{2,0},{3,1},{4,6},{5,7},{6,4},{7,5},{8,10},{9,11},{10,... | collective-permute-start | bytes 983048 | tf_op jit(solution)/shard_map/ppermute | solution.py:22
  18.7 17.6 %collective-permute-start.5 = (bf16[128,1280]{1,0:T(8,128)(2,1)S(1)}, bf16[128,1280]{1,0:T(8,128)(2,1)}, u32[]{:S(2)}, u32[]{:S(2)}) collective-permute-start(bf16[128,1280]{1,0:T(8,128)(2,1)S(1)} %collective-permute-done.2), channel_id=1, source_target_pairs={{0,4},{1,5},{2,6},{3,7},{4,0},{5,1},{6,2},{7,3},{8,12},{9,13},{10,... | collective-permute-start | bytes 983048 | tf_op jit(solution)/shard_map/ppermute | solution.py:22
  23.3 14.8 %collective-permute-start.8 = (bf16[80,1024]{1,0:T(8,128)(2,1)S(1)}, bf16[80,1024]{1,0:T(8,128)(2,1)S(1)}, u32[]{:S(2)}, u32[]{:S(2)}) collective-permute-start(bf16[80,1024]{1,0:T(8,128)(2,1)S(1)} %get-tuple-element.37), channel_id=1, source_target_pairs={{0,12},{1,13},{2,14},{3,15},{4,8},{5,9},{6,10},{7,11},{8,4},{9,5},... | collective-permute-start | bytes 491528 | tf_op jit(solution)/shard_map/ppermute | solution.py:22
  25.9 13.8 %collective-permute-start.6 = (bf16[80,1024]{1,0:T(8,128)(2,1)S(1)}, bf16[80,1024]{1,0:T(8,128)(2,1)S(1)}, u32[]{:S(2)}, u32[]{:S(2)}) collective-permute-start(bf16[80,1024]{1,0:T(8,128)(2,1)S(1)} %get-tuple-element.37), channel_id=1, source_target_pairs={{0,4},{1,5},{2,6},{3,7},{4,0},{5,1},{6,2},{7,3},{8,12},{9,13},{10,... | collective-permute-start | bytes 491528 | tf_op jit(solution)/shard_map/ppermute | solution.py:22
  26.6 13.1 %collective-permute-start.7 = (bf16[80,1024]{1,0:T(8,128)(2,1)S(1)}, bf16[80,1024]{1,0:T(8,128)(2,1)S(1)}, u32[]{:S(2)}, u32[]{:S(2)}) collective-permute-start(bf16[80,1024]{1,0:T(8,128)(2,1)S(1)} %get-tuple-element.36.refs_0_), channel_id=1, source_target_pairs={{0,8},{1,9},{2,10},{3,11},{4,12},{5,13},{6,14},{7,15},{8,0},{9,1},... | collective-permute-start | bytes 491528 | tf_op jit(solution)/shard_map/ppermute | solution.py:22
  33.4 20.5 %collective-permute-start.10 = (bf16[256,1664]{1,0:T(8,128)(2,1)S(1)}, bf16[256,1664]{1,0:T(8,128)(2,1)S(1)}, u32[]{:S(2)}, u32[]{:S(2)}) collective-permute-start(bf16[256,1664]{1,0:T(8,128)(2,1)S(1)} %shard_map.80.refs_0_), channel_id=1, source_target_pairs={{0,1},{1,0},{2,3},{3,2},{4,5},{5,4},{6,7},{7,6},{8,9},{9,8},{10,11... | collective-permute-start | bytes 2555912 | tf_op jit(solution)/shard_map/ppermute | solution.py:22
  36.2 17.6 %collective-permute-start.12 = (bf16[256,1664]{1,0:T(8,128)(2,1)S(1)}, bf16[256,1664]{1,0:T(8,128)(2,1)S(1)}, u32[]{:S(2)}, u32[]{:S(2)}) collective-permute-start(bf16[256,1664]{1,0:T(8,128)(2,1)S(1)} %shard_map.81.refs_2_), channel_id=1, source_target_pairs={{0,1},{1,0},{2,3},{3,2},{4,5},{5,4},{6,7},{7,6},{8,9},{9,8},{10,11... | collective-permute-start | bytes 2555912 | tf_op jit(solution)/shard_map/ppermute | solution.py:22
  42.3 11.5 %collective-permute-start.14 = (bf16[240,1024]{1,0:T(8,128)(2,1)S(1)}, bf16[240,1024]{1,0:T(8,128)(2,1)S(1)}, u32[]{:S(2)}, u32[]{:S(2)}) collective-permute-start(bf16[240,1024]{1,0:T(8,128)(2,1)S(1)} %get-tuple-element.42.refs_11_), channel_id=1, source_target_pairs={{0,16},{16,0},{1,17},{17,1},{2,18},{18,2},{3,19},{19,3},{4,20},{20... | collective-permute-start | bytes 1474568 | tf_op jit(solution)/shard_map/ppermute | solution.py:518
  43.9 7.6 %collective-permute-start.13 = (bf16[128,1280]{1,0:T(8,128)(2,1)S(1)}, bf16[128,1280]{1,0:T(8,128)(2,1)S(1)}, u32[]{:S(2)}, u32[]{:S(2)}) collective-permute-start(bf16[128,1280]{1,0:T(8,128)(2,1)S(1)} %broadcast_select_fusion.here), channel_id=1, source_target_pairs={{0,2},{1,3},{2,0},{3,1},{4,6},{5,7},{6,4},{7,5},{8,10},{9,11},{10,... | collective-permute-start | bytes 983048 | tf_op jit(solution)/shard_map/ppermute | solution.py:22
  44.5 9.4 %collective-permute-start.16 = (bf16[240,1024]{1,0:T(8,128)(2,1)S(1)}, bf16[240,1024]{1,0:T(8,128)(2,1)S(1)}, u32[]{:S(2)}, u32[]{:S(2)}) collective-permute-start(bf16[240,1024]{1,0:T(8,128)(2,1)S(1)} %get-tuple-element.42.refs_11_), channel_id=1, source_target_pairs={{0,1},{1,0},{2,3},{3,2},{4,5},{5,4},{6,7},{7,6},{8,9},{9,8},{10,11... | collective-permute-start | bytes 1474568 | tf_op jit(solution)/shard_map/ppermute | solution.py:22
  53.8 2.1 %collective-permute-start.15 = (bf16[256,1280]{1,0:T(8,128)(2,1)S(1)}, bf16[256,1280]{1,0:T(8,128)(2,1)S(1)}, u32[]{:S(2)}, u32[]{:S(2)}) collective-permute-start(bf16[256,1280]{1,0:T(8,128)(2,1)S(1)} %shard_map.82.refs_4_), channel_id=1, source_target_pairs={{0,1},{1,0},{2,3},{3,2},{4,5},{5,4},{6,7},{7,6},{8,9},{9,8},{10,11... | collective-permute-start | bytes 1966088 | tf_op jit(solution)/shard_map/ppermute | solution.py:22
  53.8 2.8 %collective-permute-start.17 = (bf16[240,1024]{1,0:T(8,128)(2,1)S(1)}, bf16[240,1024]{1,0:T(8,128)(2,1)S(1)}, u32[]{:S(2)}, u32[]{:S(2)}) collective-permute-start(bf16[240,1024]{1,0:T(8,128)(2,1)S(1)} %collective-permute-done.14.refs_13_), channel_id=1, source_target_pairs={{0,1},{1,0},{2,3},{3,2},{4,5},{5,4},{6,7},{7,6},{8,9},{9,8},{10,11... | collective-permute-start | bytes 1474568 | tf_op jit(solution)/shard_map/ppermute | solution.py:22
  69.4 1.8 %collective-permute-start.19 = (bf16[512,320]{1,0:T(8,128)(2,1)S(1)}, bf16[512,320]{1,0:T(8,128)(2,1)S(1)}, u32[]{:S(2)}, u32[]{:S(2)}) collective-permute-start(bf16[512,320]{1,0:T(8,128)(2,1)S(1)} %get-tuple-element.49.memory), channel_id=1, source_target_pairs={{0,1},{1,0},{2,3},{3,2},{4,5},{5,4},{6,7},{7,6},{8,9},{9,8},{10,11... | collective-permute-start | bytes 983048 | tf_op jit(solution)/shard_map/ppermute | solution.py:22
  69.6 7.8 %collective-permute-start.21 = (bf16[256,320]{1,0:T(8,128)(2,1)S(1)}, bf16[256,320]{1,0:T(8,128)(2,1)S(1)}, u32[]{:S(2)}, u32[]{:S(2)}) collective-permute-start(bf16[256,320]{1,0:T(8,128)(2,1)S(1)} %get-tuple-element.52), channel_id=1, source_target_pairs={{0,2},{1,6},{2,0},{3,4},{4,3},{5,7},{6,1},{7,5},{8,10},{9,14},{10,... | collective-permute-start | bytes 491528 | tf_op jit(solution)/shard_map/ppermute | solution.py:22
  70.1 7.3 %collective-permute-start.18 = (bf16[256,320]{1,0:T(8,128)(2,1)S(1)}, bf16[256,320]{1,0:T(8,128)(2,1)S(1)}, u32[]{:S(2)}, u32[]{:S(2)}) collective-permute-start(bf16[256,320]{1,0:T(8,128)(2,1)S(1)} %get-tuple-element.46), channel_id=1, source_target_pairs={{0,0},{1,4},{2,2},{3,6},{4,1},{5,5},{6,3},{7,7},{8,8},{9,12},{10,1... | collective-permute-start | bytes 491528 | tf_op jit(solution)/shard_map/ppermute | solution.py:22
  72.5 4.9 %collective-permute-start.20 = (f32[40,128]{1,0:T(8,128)S(1)}, f32[40,128]{1,0:T(8,128)S(1)}, u32[]{:S(2)}, u32[]{:S(2)}) collective-permute-start(f32[40,128]{1,0:T(8,128)S(1)} %get-tuple-element.50), channel_id=1, source_target_pairs={{0,8},{1,9},{2,10},{3,11},{4,12},{5,13},{6,14},{7,15},{8,0},{9,1},... | collective-permute-start | bytes 61448 | tf_op jit(solution)/shard_map/ppermute | solution.py:22
  77.4 6.5 %collective-permute-start.22 = (bf16[256,320]{1,0:T(8,128)(2,1)S(1)}, bf16[256,320]{1,0:T(8,128)(2,1)S(1)}, u32[]{:S(2)}, u32[]{:S(2)}) collective-permute-start(bf16[256,320]{1,0:T(8,128)(2,1)S(1)} %collective-permute-done.18.refs_0_), channel_id=1, source_target_pairs={{0,1},{1,0},{2,3},{3,2},{4,5},{5,4},{6,7},{7,6},{8,9},{9,8},{10,11... | collective-permute-start | bytes 491528 | tf_op jit(solution)/shard_map/ppermute | solution.py:22
  78.5 5.4 %collective-permute-start.23 = (bf16[256,320]{1,0:T(8,128)(2,1)S(1)}, bf16[256,320]{1,0:T(8,128)(2,1)S(1)}, u32[]{:S(2)}, u32[]{:S(2)}) collective-permute-start(bf16[256,320]{1,0:T(8,128)(2,1)S(1)} %collective-permute-done.21.refs_1_), channel_id=1, source_target_pairs={{0,1},{1,0},{2,3},{3,2},{4,5},{5,4},{6,7},{7,6},{8,9},{9,8},{10,11... | collective-permute-start | bytes 491528 | tf_op jit(solution)/shard_map/ppermute | solution.py:22
  78.7 6.6 %collective-permute-start.24 = (bf16[2,384]{1,0:T(2,128)(2,1)S(1)}, bf16[2,384]{1,0:T(2,128)(2,1)S(1)}, u32[]{:S(2)}, u32[]{:S(2)}) collective-permute-start(bf16[2,384]{1,0:T(2,128)(2,1)S(1)} %get-tuple-element.57), channel_id=1, source_target_pairs={{0,2},{1,3},{2,0},{3,1},{4,6},{5,7},{6,4},{7,5},{8,10},{9,11},{10,... | collective-permute-start | bytes 4616 | tf_op jit(solution)/shard_map/ppermute | solution.py:22
  80.3 5.1 %collective-permute-start.25 = (bf16[2,384]{1,0:T(2,128)(2,1)S(1)}, bf16[2,384]{1,0:T(2,128)(2,1)S(1)}, u32[]{:S(2)}, u32[]{:S(2)}) collective-permute-start(bf16[2,384]{1,0:T(2,128)(2,1)S(1)} %get-tuple-element.58), channel_id=1, source_target_pairs={{0,4},{1,5},{2,6},{3,7},{4,0},{5,1},{6,2},{7,3},{8,12},{9,13},{10,... | collective-permute-start | bytes 4616 | tf_op jit(solution)/shard_map/ppermute | solution.py:22
  83.8 4.5 %collective-permute-start.26 = (bf16[2,384]{1,0:T(2,128)(2,1)S(1)}, bf16[2,384]{1,0:T(2,128)(2,1)S(1)}, u32[]{:S(2)}, u32[]{:S(2)}) collective-permute-start(bf16[2,384]{1,0:T(2,128)(2,1)S(1)} %get-tuple-element.59), channel_id=1, source_target_pairs={{0,6},{1,7},{2,4},{3,5},{4,2},{5,3},{6,0},{7,1},{8,14},{9,15},{10,... | collective-permute-start | bytes 4616 | tf_op jit(solution)/shard_map/ppermute | solution.py:22

commit v13 on v11

--- a/solution.py
+++ b/solution.py
@@ -170,18 +170,18 @@
 
 
 def prepare_kernel(table, *refs):
-    parts, (ids, tokens, asked, joined) = refs[:-4], refs[-4:]
-    rows = joined.shape[0] // 3
-    for i in range(3):
-        joined[rows * i : rows * i + rows, :] = parts[i + 1][...]
+    first_part, joined, (ids, tokens, asked) = refs[0], refs[1], refs[2:]
+    depth = joined.shape[0] // 3
     first, x, core, z = table[13], table[6], table[7], table[14]
     count = asked.shape[0]
     ids[...] = jnp.zeros_like(ids)
     tokens[...] = jnp.zeros_like(tokens)
     flip_c = jnp.broadcast_to(core, (2, HD)) == 1
     flip_x = jnp.broadcast_to(x, (2, HD)) == 1
-    for turn, part in enumerate(parts):
-        lanes = part[:64, 896:].astype(F32)[:, HD:]
+    for turn in range(4):
+        top = depth * (turn - 1)
+        part = joined[top : top + 64, 896:] if turn else first_part[:64, 896:]
+        lanes = part.astype(F32)[:, HD:]
         for h in range(6):
             rows = [lanes[16 * j + 2 * h : 16 * j + 2 * h + 2] for j in range(4)]
             low = jnp.where(flip_c, rows[1], rows[0])
@@ -204,20 +204,38 @@
                 )
 
 
-def prepare(table, parts, count):
+def prepare(table, own, joined, count):
     return pl.pallas_call(
         prepare_kernel,
         out_shape=(
             jax.ShapeDtypeStruct((8, 1536), F32),
             jax.ShapeDtypeStruct((5 * count, GROUP), F32),
             jax.ShapeDtypeStruct((count, HD), F32),
-            jax.ShapeDtypeStruct((3 * parts[0].shape[0], 1024), BF),
         ),
-        in_specs=[SMEM] + [VMEM] * len(parts),
-        out_specs=(VMEM,) * 4,
+        in_specs=[SMEM] + [VMEM] * 2,
+        out_specs=(VMEM,) * 3,
         cost_estimate=CHEAP,
         compiler_params=pltpu.CompilerParams(vmem_limit_bytes=8 * 1024 * 1024),
-    )(table, *parts)
+    )(table, own, joined)
+
+
+def join_kernel(*refs):
+    parts, out = refs[:-1], refs[-1]
+    rows = parts[0].shape[0]
+    for i, part in enumerate(parts):
+        out[rows * i : rows * i + rows, :] = part[...]
+
+
+def join(parts):
+    rows = parts[0].shape[0]
+    return pl.pallas_call(
+        join_kernel,
+        out_shape=jax.ShapeDtypeStruct((rows * len(parts), 1024), BF),
+        in_specs=[VMEM] * len(parts),
+        out_specs=VMEM,
+        cost_estimate=CHEAP,
+        compiler_params=pltpu.CompilerParams(vmem_limit_bytes=4 * 1024 * 1024),
+    )(*parts)
 
 
 def encoder_kernel(n_parts, depth, places, *refs):
@@ -238,10 +256,16 @@
     for slab in range(3):
         values[:, 256 * slab + 128 : 256 * slab + 256] = jnp.ones((1536, 128), BF)
     spots = [places[i] for i in (0, 2, 1, 3)]
+    largest = [jnp.zeros((1, 256), F32), jnp.zeros((1, 128), F32)]
     for i, halves in enumerate(layers):
         place = places[8 + i]
         normed = jnp.concatenate([half[:, :1280] for half in halves], axis=0)
-        found = jnp.dot(normed, weight[:, 256:896], preferred_element_type=F32).astype(BF)
+        found = jnp.dot(normed, weight[:, 256:896], preferred_element_type=F32)
+        for j, lanes in enumerate((slice(0, 256), slice(512, 640))):
+            largest[j] = jnp.maximum(
+                largest[j], jnp.max(jnp.abs(found[:, lanes]), axis=0, keepdims=True)
+            )
+        found = found.astype(BF)
         for j, spot in enumerate(spots):
             to = pl.ds(pl.multiple_of(place + spot, 128), 128)
             block = found[128 * j : 128 * j + 128]
@@ -265,25 +289,14 @@
                     queries[to, WIDE:] = tail[rows]
                     residual[to, :] = halves[j // 2][128 * (j % 2) : 128 * (j % 2) + 128, 1280:]
 
-    side = lax.broadcasted_iota(jnp.int32, (8, 128), 0) == lax.broadcasted_iota(
-        jnp.int32, (8, 128), 1
-    ) // HD
-    sides = jnp.where(side, 1.0, 0.0).astype(BF)
-    only = jnp.where(side & (lax.broadcasted_iota(jnp.int32, (8, 128), 0) == 0), 1.0, 0.0).astype(BF)
-    most = []
-    for held in (queries, keys):
-        top = jnp.zeros((8, 1), F32)
-        for slab in range(3):
-            part = held[:, 128 * slab : 128 * slab + 128]
-            norms = lax.dot_general(
-                sides if slab < 2 else only,
-                part * part,
-                (((1,), (1,)), ((), ())),
-                preferred_element_type=F32,
-            )
-            top = jnp.maximum(top, jnp.max(norms, axis=-1, keepdims=True))
-        most.append(jnp.max(top))
-    small = most[0] * most[1] < 220000.0
+    lane = lax.broadcasted_iota(jnp.int32, (8, 384), 1) // HD
+    head = lax.broadcasted_iota(jnp.int32, (8, 384), 0)
+    most = jnp.concatenate(largest, axis=1) * 1.01
+    most = jnp.where((lane == head) & (head < 5), most, 0.0).astype(BF)
+    bounds = lax.dot_general(
+        most, jnp.abs(queries[...]), (((1,), (1,)), ((), ())), preferred_element_type=F32
+    )
+    small = jnp.max(bounds) < 480.0
 
     def attend(step, shifted):
         row = step * 128 if isinstance(step, int) else pl.multiple_of(step * 128, 128)
@@ -518,11 +531,12 @@
         pair_x = swap(after(pair, ready[0]), n, 2)
         halo = jnp.where((z == 1) | (z == 2), near, relayed)
         halo_x = swap(after(halo, pair_x, *here.values()), n, 2)
-        ids, tokens, asked, joined = prepare(table, [after(ready[0], halo), here[1], here[2], here[3]], n)
+        joined = join([after(here[1], halo), here[2], here[3]])
         traded = trade(joined)
+        ids, tokens, asked = prepare(table, ready[0], joined, n)
         own_half = norm_half(table, gain, stem, stem_x)
         pair_half = norm_half(table, gain, pair, pair_x)
-        halo_half = norm_half(table, gain, halo, halo_x, False)
+        halo_half = norm_half(table, gain, halo, after(halo_x, ids), False)
         own_c, pair_c = swap(own_half, n, 1), swap(pair_half, n, 1)
         halo_c, joined_c = swap(after(halo_half, traded), n, 1), swap(joined, n, 1)
         layered = [own_half, own_c, pair_half, pair_c, halo_half, halo_c]

time: 87 us -> 85 us (0.977)
  waiting for transfers between devices: 33.5 us -> 32.3 us
    ppermute x26, waiting for transfers between devices: 33.5 us -> 32.3 us  [send(): return lax.ppermute(block, 'tm', route)]
where the time goes in v13:
time: 85 us; the launch traced here: 84.7 us
  waiting for transfers between devices  32.3 us (38%)
  starting transfers between devices  25.9 us (30%)
  Pallas kernels  22.8 us (27%)
  local copies, waits for them, and re-layouts  1.87 us (2%)
  other arithmetic  1.02 us (1%)
  between operations  0.91 us (1%)
    ppermute x26, waiting for transfers between devices, send(): return lax.ppermute(block, 'tm', route)  32.3 us
    ppermute x26, starting transfers between devices, send(): return lax.ppermute(block, 'tm', route)  24.3 us
    pallas_call x1, Pallas kernels, encoder(): pl.pallas_call(functools.partial(encoder_kernel, len(parts), depth), out_...  12.6 us
    pallas_call x3, Pallas kernels, norm_half(): pl.pallas_call(norm_kernel, out_shape=jax.ShapeDtypeStruct((256, 1664 if...  2.93 us
    pallas_call x2, Pallas kernels, gather_groups(): pl.pallas_call(functools.partial(gather_kernel, side, rows), out_shape=ja...  2.59 us
    unnamed x12, local copies, waits for them, and re-layouts  1.75 us
  transfers between devices with their start and end apart: 27, of which 13 were waited for; matrix products, arithmetic and copies ran while one was open for 1% of the time, Pallas kernels for 9%

profile of v13, /device:TPU:0, one launch (start us, length us, event | category | flops | bytes accessed | tf_op | source)
XLA Modules:
  0.0 84.7 jit_solution(10971634155109907594)
XLA Ops:
  0.7 0.0 copy-start.2
  0.7 0.1 stack.136.table.places
  0.8 0.0 copy-start.3
  0.9 0.0 copy-start.4
  0.9 0.5 copy-done.2
  1.4 0.1 copy-done.3
  1.5 1.1 %copy-done = bf16[80,3840]{1,0:T(8,128)(2,1)S(1)} copy-done((bf16[80,3840]{1,0:T(8,128)(2,1)S(1)}, bf16[80,3840]{1,0:T(8,128)(2,1)}, u32[]{:S(2)}) %copy-start) | copy-done | bytes 614424
  2.6 1.1 %shard_map.77 = (bf16[2,80,1024]{2,1,0:T(8,128)(2,1)S(1)}, bf16[2,80,1024]{2,1,0:T(8,128)(2,1)S(1)}) custom-call(s32[34]{0:T(128)S(1)} %stack.136.table.places, bf16[80,3840]{1,0:T(8,128)(2,1)S(1)} %copy-done, bf16[2,1280]{1,0:T(2,128)(2,1)S(1)} %copy-done.2, s32[2,16]{1,0:T(2,128)S(1)} %copy-done.3, s32[1,128]{1,0:T(1,128)S(1)} %bitcast.33), custom_call_target="tpu_custom_call" | custom-call | flops 1 | bytes 1 | tf_op jit(solution)/shard_map/pallas_call | solution.py:98
  3.8 3.0 %collective-permute-start = (bf16[2,80,1024]{2,1,0:T(8,128)(2,1)S(1)}, bf16[2,80,1024]{2,1,0:T(8,128)(2,1)S(1)}, u32[]{:S(2)}, u32[]{:S(2)}) collective-permute-start(bf16[2,80,1024]{2,1,0:T(8,128)(2,1)S(1)} %get-tuple-element.30), channel_id=1, source_target_pairs={{0,2},{1,3},{2,0},{3,1},{4,6},{5,7},{6,4},{7,5},{8,10},{9,11},{10,... | collective-permute-start | bytes 983048 | tf_op jit(solution)/shard_map/ppermute | solution.py:22
  6.8 0.7 collective-permute-start.5
  7.5 4.4 %collective-permute-start.3 = (bf16[128,1280]{1,0:T(8,128)(2,1)S(1)}, bf16[128,1280]{1,0:T(8,128)(2,1)S(1)}, u32[]{:S(2)}, u32[]{:S(2)}) collective-permute-start(bf16[128,1280]{1,0:T(8,128)(2,1)S(1)} %copy-done.1), channel_id=1, source_target_pairs={{0,4},{1,5},{2,6},{3,7},{4,0},{5,1},{6,2},{7,3},{8,12},{9,13},{10,... | collective-permute-start | bytes 983048 | tf_op jit(solution)/shard_map/ppermute | solution.py:22
  11.9 0.0 collective-permute-start.4
  11.9 2.6 %collective-permute-done.refs_2_.refs_9_ = bf16[2,80,1024]{2,1,0:T(8,128)(2,1)S(1)} collective-permute-done((bf16[2,80,1024]{2,1,0:T(8,128)(2,1)S(1)}, bf16[2,80,1024]{2,1,0:T(8,128)(2,1)S(1)}, u32[]{:S(2)}, u32[]{:S(2)}) %collective-permute-start) | collective-permute-done | bytes 327712 | tf_op jit(solution)/shard_map/ppermute | solution.py:22
  14.5 0.0 collective-permute-start.6
  14.5 0.0 collective-permute-done.5
  14.5 4.6 %collective-permute-done.3.here = bf16[128,1280]{1,0:T(8,128)(2,1)S(1)} collective-permute-done((bf16[128,1280]{1,0:T(8,128)(2,1)S(1)}, bf16[128,1280]{1,0:T(8,128)(2,1)S(1)}, u32[]{:S(2)}, u32[]{:S(2)}) %collective-permute-start.3) | collective-permute-done | bytes 327712 | tf_op jit(solution)/shard_map/ppermute | solution.py:22
  19.0 0.5 collective-permute-start.1
  19.6 0.6 shard_map.79
  20.2 1.6 %collective-permute-start.7 = (bf16[128,1280]{1,0:T(8,128)(2,1)S(1)}, bf16[128,1280]{1,0:T(8,128)(2,1)S(1)}, u32[]{:S(2)}, u32[]{:S(2)}) collective-permute-start(bf16[128,1280]{1,0:T(8,128)(2,1)S(1)} %collective-permute-done.3.here), channel_id=1, source_target_pairs={{0,2},{1,3},{2,0},{3,1},{4,6},{5,7},{6,4},{7,5},{8,10},{9,11},{10,... | collective-permute-start | bytes 983048 | tf_op jit(solution)/shard_map/ppermute | solution.py:22
  21.7 1.7 %collective-permute-start.9 = (bf16[128,1280]{1,0:T(8,128)(2,1)S(1)}, bf16[128,1280]{1,0:T(8,128)(2,1)}, u32[]{:S(2)}, u32[]{:S(2)}) collective-permute-start(bf16[128,1280]{1,0:T(8,128)(2,1)S(1)} %collective-permute-done.5), channel_id=1, source_target_pairs={{0,4},{1,5},{2,6},{3,7},{4,0},{5,1},{6,2},{7,3},{8,12},{9,13},{10,... | collective-permute-start | bytes 983048 | tf_op jit(solution)/shard_map/ppermute | solution.py:22
  23.5 0.3 collective-permute-start.12
  23.8 1.4 %collective-permute-start.10 = (bf16[80,1024]{1,0:T(8,128)(2,1)S(1)}, bf16[80,1024]{1,0:T(8,128)(2,1)S(1)}, u32[]{:S(2)}, u32[]{:S(2)}) collective-permute-start(bf16[80,1024]{1,0:T(8,128)(2,1)S(1)} %get-tuple-element.37), channel_id=1, source_target_pairs={{0,12},{1,13},{2,14},{3,15},{4,8},{5,9},{6,10},{7,11},{8,4},{9,5},... | collective-permute-start | bytes 491528 | tf_op jit(solution)/shard_map/ppermute | solution.py:22
  25.1 4.5 %collective-permute-done.1.across = bf16[128,1280]{1,0:T(8,128)(2,1)S(1)} collective-permute-done((bf16[128,1280]{1,0:T(8,128)(2,1)S(1)}, bf16[128,1280]{1,0:T(8,128)(2,1)S(1)}, u32[]{:S(2)}, u32[]{:S(2)}) %collective-permute-start.1) | collective-permute-done | bytes 327712 | tf_op jit(solution)/shard_map/ppermute | solution.py:22
  29.7 1.6 %collective-permute-start.11 = (bf16[80,1024]{1,0:T(8,128)(2,1)S(1)}, bf16[80,1024]{1,0:T(8,128)(2,1)S(1)}, u32[]{:S(2)}, u32[]{:S(2)}) collective-permute-start(bf16[80,1024]{1,0:T(8,128)(2,1)S(1)} %get-tuple-element.34.refs_0_), channel_id=1, source_target_pairs={{0,8},{1,9},{2,10},{3,11},{4,12},{5,13},{6,14},{7,15},{8,0},{9,1},... | collective-permute-start | bytes 491528 | tf_op jit(solution)/shard_map/ppermute | solution.py:22
  31.3 1.0 %shard_map.78.refs_0_ = bf16[256,1664]{1,0:T(8,128)(2,1)S(1)} custom-call(s32[34]{0:T(128)S(1)} %stack.136.table.places, f32[1,1280]{1,0:T(1,128)S(1)} %reshape.10.gain, bf16[128,1280]{1,0:T(8,128)(2,1)S(1)} %copy-done.1, bf16[128,1280]{1,0:T(8,128)(2,1)S(1)} %collective-permute-done.1.across), custom_call_target="tpu_custom_call" | custom-call | flops 1 | bytes 1 | tf_op jit(solution)/shard_map/pallas_call | solution.py:162
  32.3 2.0 %collective-permute-done.7.across = bf16[128,1280]{1,0:T(8,128)(2,1)S(1)} collective-permute-done((bf16[128,1280]{1,0:T(8,128)(2,1)S(1)}, bf16[128,1280]{1,0:T(8,128)(2,1)S(1)}, u32[]{:S(2)}, u32[]{:S(2)}) %collective-permute-start.7) | collective-permute-done | bytes 327712 | tf_op jit(solution)/shard_map/ppermute | solution.py:22
  34.3 1.0 %shard_map.80.refs_2_ = bf16[256,1664]{1,0:T(8,128)(2,1)S(1)} custom-call(s32[34]{0:T(128)S(1)} %stack.136.table.places, f32[1,1280]{1,0:T(1,128)S(1)} %reshape.10.gain, bf16[128,1280]{1,0:T(8,128)(2,1)S(1)} %collective-permute-done.3.here, bf16[128,1280]{1,0:T(8,128)(2,1)S(1)} %collective-permute-done.7.across), custom_call_target="tpu_custom_call" | custom-call | flops 1 | bytes 1 | tf_op jit(solution)/shard_map/pallas_call | solution.py:162
  35.3 0.0 collective-permute-done.9
  35.4 0.5 collective-permute-start.8
  35.9 1.0 %broadcast_select_fusion.here = bf16[128,1280]{1,0:T(8,128)(2,1)S(1)} fusion(bf16[128,1280]{1,0:T(8,128)(2,1)S(1)} %collective-permute-done.5, bf16[128,1280]{1,0:T(8,128)(2,1)} %collective-permute-done.9, pred[]{:T(512)S(6)} %or.3), kind=kLoop, calls=%fused_computation | loop fusion | flops 163840 | bytes 983041 | tf_op jit(solution)/shard_map/jit(_where)/select_n | solution.py:532
  36.9 2.8 %collective-permute-done.12.refs_0_ = bf16[80,1024]{1,0:T(8,128)(2,1)S(1)} collective-permute-done((bf16[80,1024]{1,0:T(8,128)(2,1)S(1)}, bf16[80,1024]{1,0:T(8,128)(2,1)S(1)}, u32[]{:S(2)}, u32[]{:S(2)}) %collective-permute-start.12) | collective-permute-done | bytes 163872 | tf_op jit(solution)/shard_map/ppermute | solution.py:22
  39.7 1.4 %collective-permute-done.11.refs_1_ = bf16[80,1024]{1,0:T(8,128)(2,1)S(1)} collective-permute-done((bf16[80,1024]{1,0:T(8,128)(2,1)S(1)}, bf16[80,1024]{1,0:T(8,128)(2,1)S(1)}, u32[]{:S(2)}, u32[]{:S(2)}) %collective-permute-start.11) | collective-permute-done | bytes 163872 | tf_op jit(solution)/shard_map/ppermute | solution.py:22
  41.2 1.6 %collective-permute-start.14 = (bf16[240,1024]{1,0:T(8,128)(2,1)S(1)}, bf16[240,1024]{1,0:T(8,128)(2,1)S(1)}, u32[]{:S(2)}, u32[]{:S(2)}) collective-permute-start(bf16[240,1024]{1,0:T(8,128)(2,1)S(1)} %shard_map.81.refs_1_.refs_11_), channel_id=1, source_target_pairs={{0,16},{16,0},{1,17},{17,1},{2,18},{18,2},{3,19},{19,3},{4,20},{20... | collective-permute-start | bytes 1474568 | tf_op jit(solution)/shard_map/ppermute | solution.py:520
  42.8 0.5 collective-permute-start.13
  43.3 1.3 %shard_map.82 = (f32[8,1536]{1,0:T(8,128)S(1)}, f32[80,320]{1,0:T(8,128)S(1)}, f32[16,64]{1,0:T(8,128)S(1)}) custom-call(s32[34]{0:T(128)S(1)} %stack.136.table.places, bf16[80,1024]{1,0:T(8,128)(2,1)S(1)} %get-tuple-element.34.refs_0_, bf16[240,1024]{1,0:T(8,128)(2,1)S(1)} %shard_map.81.refs_1_.refs_11_), custom_call_target="tpu_custom_call" | custom-call | flops 1 | bytes 1 | tf_op jit(solution)/shard_map/pallas_call | solution.py:208
  44.6 5.2 %collective-permute-done.13.across = bf16[128,1280]{1,0:T(8,128)(2,1)S(1)} collective-permute-done((bf16[128,1280]{1,0:T(8,128)(2,1)S(1)}, bf16[128,1280]{1,0:T(8,128)(2,1)S(1)}, u32[]{:S(2)}, u32[]{:S(2)}) %collective-permute-start.13) | collective-permute-done | bytes 327712 | tf_op jit(solution)/shard_map/ppermute | solution.py:22
  49.8 1.0 %shard_map.83.refs_4_ = bf16[256,1280]{1,0:T(8,128)(2,1)S(1)} custom-call(s32[34]{0:T(128)S(1)} %stack.136.table.places, f32[1,1280]{1,0:T(1,128)S(1)} %reshape.10.gain, bf16[128,1280]{1,0:T(8,128)(2,1)S(1)} %broadcast_select_fusion.here, bf16[128,1280]{1,0:T(8,128)(2,1)S(1)} %collective-permute-done.13.across), custom_call_target="tpu_custom_call" | custom-call | flops 1 | bytes 1 | tf_op jit(solution)/shard_map/pallas_call | solution.py:162
  50.8 0.0 collective-permute-done.14.refs_13_
  50.8 0.1 collective-permute-start.15
  50.9 0.0 collective-permute-done.2.refs_1_
  50.9 0.0 collective-permute-done.8.refs_3_
  50.9 0.5 collective-permute-start.17
  51.5 1.5 %collective-permute-done.15.refs_5_ = bf16[256,1280]{1,0:T(8,128)(2,1)S(1)} collective-permute-done((bf16[256,1280]{1,0:T(8,128)(2,1)S(1)}, bf16[256,1280]{1,0:T(8,128)(2,1)S(1)}, u32[]{:S(2)}, u32[]{:S(2)}) %collective-permute-start.15) | collective-permute-done | bytes 655392 | tf_op jit(solution)/shard_map/ppermute | solution.py:22
  53.0 0.7 collective-permute-done.17.refs_14_
  53.7 12.6 %shard_map.84 = (bf16[512,320]{1,0:T(8,128)(2,1)S(1)}, bf16[256,320]{1,0:T(8,128)(2,1)S(1)}, bf16[256,320]{1,0:T(8,128)(2,1)S(1)}) custom-call(s32[34]{0:T(128)S(1)} %stack.136.table.places, bf16[256,1664]{1,0:T(8,128)(2,1)S(1)} %shard_map.78.refs_0_, bf16[256,1664]{1,0:T(8,128)(2,1)S(1)} %collective-permute-done.2.refs_1_, ...), custom_call_target="tpu_custom_call" | custom-call | flops 1 | bytes 1 | tf_op jit(solution)/shard_map/pallas_call | solution.py:355
  66.3 0.2 collective-permute-start.19
  66.5 0.5 collective-permute-start.21
  67.0 0.7 collective-permute-start.18
  67.7 0.4 collective-permute-done.19.beside
  68.1 1.3 %shard_map.85 = (f32[40,128]{1,0:T(8,128)S(1)}, f32[40,128]{1,0:T(8,128)S(1)}) custom-call(s32[34]{0:T(128)S(1)} %stack.136.table.places, f32[80,320]{1,0:T(8,128)S(1)} %get-tuple-element.45.tokens, f32[16,64]{1,0:T(8,128)S(1)} %get-tuple-element.46.asked, bf16[512,320]{1,0:T(8,128)(2,1)S(1)} %get-tuple-element.47.memory, ...), custom_call_target="tpu_custom_call" | custom-call | flops 1 | bytes 1 | tf_op jit(solution)/shard_map/pallas_call | solution.py:421
  69.4 1.3 %collective-permute-start.20 = (f32[40,128]{1,0:T(8,128)S(1)}, f32[40,128]{1,0:T(8,128)S(1)}, u32[]{:S(2)}, u32[]{:S(2)}) collective-permute-start(f32[40,128]{1,0:T(8,128)S(1)} %get-tuple-element.48), channel_id=1, source_target_pairs={{0,8},{1,9},{2,10},{3,11},{4,12},{5,13},{6,14},{7,15},{8,0},{9,1},... | collective-permute-start | bytes 61448 | tf_op jit(solution)/shard_map/ppermute | solution.py:22
  70.7 3.6 %collective-permute-done.21.refs_1_ = bf16[256,320]{1,0:T(8,128)(2,1)S(1)} collective-permute-done((bf16[256,320]{1,0:T(8,128)(2,1)S(1)}, bf16[256,320]{1,0:T(8,128)(2,1)S(1)}, u32[]{:S(2)}, u32[]{:S(2)}) %collective-permute-start.21) | collective-permute-done | bytes 163872 | tf_op jit(solution)/shard_map/ppermute | solution.py:22
  74.3 0.0 collective-permute-done.20.refs_1_
  74.3 0.0 collective-permute-done.18.refs_0_
  74.3 1.1 %collective-permute-start.22 = (bf16[256,320]{1,0:T(8,128)(2,1)S(1)}, bf16[256,320]{1,0:T(8,128)(2,1)S(1)}, u32[]{:S(2)}, u32[]{:S(2)}) collective-permute-start(bf16[256,320]{1,0:T(8,128)(2,1)S(1)} %collective-permute-done.18.refs_0_), channel_id=1, source_target_pairs={{0,1},{1,0},{2,3},{3,2},{4,5},{5,4},{6,7},{7,6},{8,9},{9,8},{10,11... | collective-permute-start | bytes 491528 | tf_op jit(solution)/shard_map/ppermute | solution.py:22
  75.4 0.0 collective-permute-start.23
  75.4 0.2 shard_map.87
  75.6 1.6 %collective-permute-start.24 = (bf16[2,384]{1,0:T(2,128)(2,1)S(1)}, bf16[2,384]{1,0:T(2,128)(2,1)S(1)}, u32[]{:S(2)}, u32[]{:S(2)}) collective-permute-start(bf16[2,384]{1,0:T(2,128)(2,1)S(1)} %get-tuple-element.55), channel_id=1, source_target_pairs={{0,2},{1,3},{2,0},{3,1},{4,6},{5,7},{6,4},{7,5},{8,10},{9,11},{10,... | collective-permute-start | bytes 4616 | tf_op jit(solution)/shard_map/ppermute | solution.py:22
  77.2 1.8 %collective-permute-start.25 = (bf16[2,384]{1,0:T(2,128)(2,1)S(1)}, bf16[2,384]{1,0:T(2,128)(2,1)S(1)}, u32[]{:S(2)}, u32[]{:S(2)}) collective-permute-start(bf16[2,384]{1,0:T(2,128)(2,1)S(1)} %get-tuple-element.56), channel_id=1, source_target_pairs={{0,4},{1,5},{2,6},{3,7},{4,0},{5,1},{6,2},{7,3},{8,12},{9,13},{10,... | collective-permute-start | bytes 4616 | tf_op jit(solution)/shard_map/ppermute | solution.py:22
  79.0 0.2 collective-permute-start.26
  79.2 1.4 %shard_map.86 = bf16[128,1280]{1,0:T(8,128)(2,1)} custom-call(s32[34]{0:T(128)S(1)} %stack.136.table.places, bf16[256,320]{1,0:T(8,128)(2,1)S(1)} %collective-permute-done.18.refs_0_, bf16[256,320]{1,0:T(8,128)(2,1)S(1)} %collective-permute-done.21.refs_1_, bf16[256,320]{1,0:T(8,128)(2,1)S(1)} %collective-permute-done.22.refs_2_, ...), custom_call_target="tpu_custom_call" | custom-call | flops 1 | bytes 1 | tf_op jit(solution)/shard_map/pallas_call | solution.py:475
  80.6 0.2 collective-permute-done.25.refs_2_
  80.8 2.7 %collective-permute-done.26.refs_3_ = bf16[2,384]{1,0:T(2,128)(2,1)S(1)} collective-permute-done((bf16[2,384]{1,0:T(2,128)(2,1)S(1)}, bf16[2,384]{1,0:T(2,128)(2,1)S(1)}, u32[]{:S(2)}, u32[]{:S(2)}) %collective-permute-start.26) | collective-permute-done | bytes 1568 | tf_op jit(solution)/shard_map/ppermute | solution.py:22
  83.5 1.2 %shard_map.88 = bf16[2,1280]{1,0:T(2,128)(2,1)} custom-call(s32[34]{0:T(128)S(1)} %stack.136.table.places, bf16[2,384]{1,0:T(2,128)(2,1)S(1)} %get-tuple-element.54.refs_0_, bf16[2,384]{1,0:T(2,128)(2,1)S(1)} %collective-permute-done.24.refs_1_, bf16[2,384]{1,0:T(2,128)(2,1)S(1)} %collective-permute-done.25.refs_2_, ...), custom_call_target="tpu_custom_call" | custom-call | flops 1 | bytes 1 | tf_op jit(solution)/shard_map/pallas_call | solution.py:475
  (17 shorter events, 0.1 us)
Async XLA Ops:
  0.7 0.7 copy-start.2
  0.8 0.7 copy-start.3
  0.9 0.7 copy-start.4
  1.5 1.1 %copy-start = (bf16[80,3840]{1,0:T(8,128)(2,1)S(1)}, bf16[80,3840]{1,0:T(8,128)(2,1)}, u32[]{:S(2)}) copy-start(bf16[80,3840]{1,0:T(8,128)(2,1)} %refs_0_.1) | copy-start | bytes 1843204
  2.6 4.2 %copy-start.1 = (bf16[128,1280]{1,0:T(8,128)(2,1)S(1)}, bf16[128,1280]{1,0:T(8,128)(2,1)}, u32[]{:S(2)}) copy-start(bf16[128,1280]{1,0:T(8,128)(2,1)} %here.1) | copy-start | bytes 983044
  3.8 10.7 %collective-permute-start = (bf16[2,80,1024]{2,1,0:T(8,128)(2,1)S(1)}, bf16[2,80,1024]{2,1,0:T(8,128)(2,1)S(1)}, u32[]{:S(2)}, u32[]{:S(2)}) collective-permute-start(bf16[2,80,1024]{2,1,0:T(8,128)(2,1)S(1)} %get-tuple-element.30), channel_id=1, source_target_pairs={{0,2},{1,3},{2,0},{3,1},{4,6},{5,7},{6,4},{7,5},{8,10},{9,11},{10,... | collective-permute-start | bytes 983048 | tf_op jit(solution)/shard_map/ppermute | solution.py:22
  6.8 7.7 %collective-permute-start.5 = (bf16[128,1280]{1,0:T(8,128)(2,1)S(1)}, bf16[128,1280]{1,0:T(8,128)(2,1)S(1)}, u32[]{:S(2)}, u32[]{:S(2)}) collective-permute-start(bf16[128,1280]{1,0:T(8,128)(2,1)S(1)} %copy-done.1), channel_id=1, source_target_pairs={{4,8},{5,9},{6,10},{7,11},{8,4},{9,5},{10,6},{11,7},{20,24},{21,25... | collective-permute-start | bytes 983048 | tf_op jit(solution)/shard_map/ppermute | solution.py:22
  7.5 11.6 %collective-permute-start.3 = (bf16[128,1280]{1,0:T(8,128)(2,1)S(1)}, bf16[128,1280]{1,0:T(8,128)(2,1)S(1)}, u32[]{:S(2)}, u32[]{:S(2)}) collective-permute-start(bf16[128,1280]{1,0:T(8,128)(2,1)S(1)} %copy-done.1), channel_id=1, source_target_pairs={{0,4},{1,5},{2,6},{3,7},{4,0},{5,1},{6,2},{7,3},{8,12},{9,13},{10,... | collective-permute-start | bytes 983048 | tf_op jit(solution)/shard_map/ppermute | solution.py:22
  11.9 7.7 %collective-permute-start.4 = (bf16[2,80,1024]{2,1,0:T(8,128)(2,1)S(1)}, bf16[2,80,1024]{2,1,0:T(8,128)(2,1)S(1)}, u32[]{:S(2)}, u32[]{:S(2)}) collective-permute-start(bf16[2,80,1024]{2,1,0:T(8,128)(2,1)S(1)} %get-tuple-element.32.refs_0_.refs_7_), channel_id=1, source_target_pairs={{0,1},{1,0},{2,3},{3,2},{4,5},{5,4},{6,7},{7,6},{8,9},{9,8},{10,11... | collective-permute-start | bytes 983048 | tf_op jit(solution)/shard_map/ppermute | solution.py:22
  14.5 5.1 %collective-permute-start.6 = (bf16[2,80,1024]{2,1,0:T(8,128)(2,1)S(1)}, bf16[2,80,1024]{2,1,0:T(8,128)(2,1)S(1)}, u32[]{:S(2)}, u32[]{:S(2)}) collective-permute-start(bf16[2,80,1024]{2,1,0:T(8,128)(2,1)S(1)} %collective-permute-done.refs_2_.refs_9_), channel_id=1, source_target_pairs={{0,1},{1,0},{2,3},{3,2},{4,5},{5,4},{6,7},{7,6},{8,9},{9,8},{10,11... | collective-permute-start | bytes 983048 | tf_op jit(solution)/shard_map/ppermute | solution.py:22
  19.0 10.6 %collective-permute-start.1 = (bf16[128,1280]{1,0:T(8,128)(2,1)S(1)}, bf16[128,1280]{1,0:T(8,128)(2,1)S(1)}, u32[]{:S(2)}, u32[]{:S(2)}) collective-permute-start(bf16[128,1280]{1,0:T(8,128)(2,1)S(1)} %copy-done.1), channel_id=1, source_target_pairs={{0,2},{1,3},{2,0},{3,1},{4,6},{5,7},{6,4},{7,5},{8,10},{9,11},{10,... | collective-permute-start | bytes 983048 | tf_op jit(solution)/shard_map/ppermute | solution.py:22
  19.6 3.9 %copy-start.5 = (f32[1280]{0:T(1024)S(1)}, f32[1280]{0:T(1024)}, u32[]{:S(2)}) copy-start(f32[1280]{0:T(1024)} %param.7) | copy-start | bytes 15364
  20.2 14.1 %collective-permute-start.7 = (bf16[128,1280]{1,0:T(8,128)(2,1)S(1)}, bf16[128,1280]{1,0:T(8,128)(2,1)S(1)}, u32[]{:S(2)}, u32[]{:S(2)}) collective-permute-start(bf16[128,1280]{1,0:T(8,128)(2,1)S(1)} %collective-permute-done.3.here), channel_id=1, source_target_pairs={{0,2},{1,3},{2,0},{3,1},{4,6},{5,7},{6,4},{7,5},{8,10},{9,11},{10,... | collective-permute-start | bytes 983048 | tf_op jit(solution)/shard_map/ppermute | solution.py:22
  21.7 13.6 %collective-permute-start.9 = (bf16[128,1280]{1,0:T(8,128)(2,1)S(1)}, bf16[128,1280]{1,0:T(8,128)(2,1)}, u32[]{:S(2)}, u32[]{:S(2)}) collective-permute-start(bf16[128,1280]{1,0:T(8,128)(2,1)S(1)} %collective-permute-done.5), channel_id=1, source_target_pairs={{0,4},{1,5},{2,6},{3,7},{4,0},{5,1},{6,2},{7,3},{8,12},{9,13},{10,... | collective-permute-start | bytes 983048 | tf_op jit(solution)/shard_map/ppermute | solution.py:22
  23.5 16.2 %collective-permute-start.12 = (bf16[80,1024]{1,0:T(8,128)(2,1)S(1)}, bf16[80,1024]{1,0:T(8,128)(2,1)S(1)}, u32[]{:S(2)}, u32[]{:S(2)}) collective-permute-start(bf16[80,1024]{1,0:T(8,128)(2,1)S(1)} %get-tuple-element.37), channel_id=1, source_target_pairs={{0,4},{1,5},{2,6},{3,7},{4,0},{5,1},{6,2},{7,3},{8,12},{9,13},{10,... | collective-permute-start | bytes 491528 | tf_op jit(solution)/shard_map/ppermute | solution.py:22
  23.8 16.0 %collective-permute-start.10 = (bf16[80,1024]{1,0:T(8,128)(2,1)S(1)}, bf16[80,1024]{1,0:T(8,128)(2,1)S(1)}, u32[]{:S(2)}, u32[]{:S(2)}) collective-permute-start(bf16[80,1024]{1,0:T(8,128)(2,1)S(1)} %get-tuple-element.37), channel_id=1, source_target_pairs={{0,12},{1,13},{2,14},{3,15},{4,8},{5,9},{6,10},{7,11},{8,4},{9,5},... | collective-permute-start | bytes 491528 | tf_op jit(solution)/shard_map/ppermute | solution.py:22
  29.7 11.4 %collective-permute-start.11 = (bf16[80,1024]{1,0:T(8,128)(2,1)S(1)}, bf16[80,1024]{1,0:T(8,128)(2,1)S(1)}, u32[]{:S(2)}, u32[]{:S(2)}) collective-permute-start(bf16[80,1024]{1,0:T(8,128)(2,1)S(1)} %get-tuple-element.34.refs_0_), channel_id=1, source_target_pairs={{0,8},{1,9},{2,10},{3,11},{4,12},{5,13},{6,14},{7,15},{8,0},{9,1},... | collective-permute-start | bytes 491528 | tf_op jit(solution)/shard_map/ppermute | solution.py:22
  34.3 16.6 %collective-permute-start.2 = (bf16[256,1664]{1,0:T(8,128)(2,1)S(1)}, bf16[256,1664]{1,0:T(8,128)(2,1)S(1)}, u32[]{:S(2)}, u32[]{:S(2)}) collective-permute-start(bf16[256,1664]{1,0:T(8,128)(2,1)S(1)} %shard_map.78.refs_0_), channel_id=1, source_target_pairs={{0,1},{1,0},{2,3},{3,2},{4,5},{5,4},{6,7},{7,6},{8,9},{9,8},{10,11... | collective-permute-start | bytes 2555912 | tf_op jit(solution)/shard_map/ppermute | solution.py:22
  35.4 15.5 %collective-permute-start.8 = (bf16[256,1664]{1,0:T(8,128)(2,1)S(1)}, bf16[256,1664]{1,0:T(8,128)(2,1)S(1)}, u32[]{:S(2)}, u32[]{:S(2)}) collective-permute-start(bf16[256,1664]{1,0:T(8,128)(2,1)S(1)} %shard_map.80.refs_2_), channel_id=1, source_target_pairs={{0,1},{1,0},{2,3},{3,2},{4,5},{5,4},{6,7},{7,6},{8,9},{9,8},{10,11... | collective-permute-start | bytes 2555912 | tf_op jit(solution)/shard_map/ppermute | solution.py:22
  41.2 9.6 %collective-permute-start.14 = (bf16[240,1024]{1,0:T(8,128)(2,1)S(1)}, bf16[240,1024]{1,0:T(8,128)(2,1)S(1)}, u32[]{:S(2)}, u32[]{:S(2)}) collective-permute-start(bf16[240,1024]{1,0:T(8,128)(2,1)S(1)} %shard_map.81.refs_1_.refs_11_), channel_id=1, source_target_pairs={{0,16},{16,0},{1,17},{17,1},{2,18},{18,2},{3,19},{19,3},{4,20},{20... | collective-permute-start | bytes 1474568 | tf_op jit(solution)/shard_map/ppermute | solution.py:520
  42.8 7.1 %collective-permute-start.13 = (bf16[128,1280]{1,0:T(8,128)(2,1)S(1)}, bf16[128,1280]{1,0:T(8,128)(2,1)S(1)}, u32[]{:S(2)}, u32[]{:S(2)}) collective-permute-start(bf16[128,1280]{1,0:T(8,128)(2,1)S(1)} %broadcast_select_fusion.here), channel_id=1, source_target_pairs={{0,2},{1,3},{2,0},{3,1},{4,6},{5,7},{6,4},{7,5},{8,10},{9,11},{10,... | collective-permute-start | bytes 983048 | tf_op jit(solution)/shard_map/ppermute | solution.py:22
  43.3 7.6 %collective-permute-start.16 = (bf16[240,1024]{1,0:T(8,128)(2,1)S(1)}, bf16[240,1024]{1,0:T(8,128)(2,1)S(1)}, u32[]{:S(2)}, u32[]{:S(2)}) collective-permute-start(bf16[240,1024]{1,0:T(8,128)(2,1)S(1)} %shard_map.81.refs_1_.refs_11_), channel_id=1, source_target_pairs={{0,1},{1,0},{2,3},{3,2},{4,5},{5,4},{6,7},{7,6},{8,9},{9,8},{10,11... | collective-permute-start | bytes 1474568 | tf_op jit(solution)/shard_map/ppermute | solution.py:22
  50.8 2.2 %collective-permute-start.15 = (bf16[256,1280]{1,0:T(8,128)(2,1)S(1)}, bf16[256,1280]{1,0:T(8,128)(2,1)S(1)}, u32[]{:S(2)}, u32[]{:S(2)}) collective-permute-start(bf16[256,1280]{1,0:T(8,128)(2,1)S(1)} %shard_map.83.refs_4_), channel_id=1, source_target_pairs={{0,1},{1,0},{2,3},{3,2},{4,5},{5,4},{6,7},{7,6},{8,9},{9,8},{10,11... | collective-permute-start | bytes 1966088 | tf_op jit(solution)/shard_map/ppermute | solution.py:22
  50.9 2.8 %collective-permute-start.17 = (bf16[240,1024]{1,0:T(8,128)(2,1)S(1)}, bf16[240,1024]{1,0:T(8,128)(2,1)S(1)}, u32[]{:S(2)}, u32[]{:S(2)}) collective-permute-start(bf16[240,1024]{1,0:T(8,128)(2,1)S(1)} %collective-permute-done.14.refs_13_), channel_id=1, source_target_pairs={{0,1},{1,0},{2,3},{3,2},{4,5},{5,4},{6,7},{7,6},{8,9},{9,8},{10,11... | collective-permute-start | bytes 1474568 | tf_op jit(solution)/shard_map/ppermute | solution.py:22
  66.3 1.8 %collective-permute-start.19 = (bf16[512,320]{1,0:T(8,128)(2,1)S(1)}, bf16[512,320]{1,0:T(8,128)(2,1)S(1)}, u32[]{:S(2)}, u32[]{:S(2)}) collective-permute-start(bf16[512,320]{1,0:T(8,128)(2,1)S(1)} %get-tuple-element.47.memory), channel_id=1, source_target_pairs={{0,1},{1,0},{2,3},{3,2},{4,5},{5,4},{6,7},{7,6},{8,9},{9,8},{10,11... | collective-permute-start | bytes 983048 | tf_op jit(solution)/shard_map/ppermute | solution.py:22
  66.5 7.8 %collective-permute-start.21 = (bf16[256,320]{1,0:T(8,128)(2,1)S(1)}, bf16[256,320]{1,0:T(8,128)(2,1)S(1)}, u32[]{:S(2)}, u32[]{:S(2)}) collective-permute-start(bf16[256,320]{1,0:T(8,128)(2,1)S(1)} %get-tuple-element.50), channel_id=1, source_target_pairs={{0,2},{1,6},{2,0},{3,4},{4,3},{5,7},{6,1},{7,5},{8,10},{9,14},{10,... | collective-permute-start | bytes 491528 | tf_op jit(solution)/shard_map/ppermute | solution.py:22
  67.0 7.2 %collective-permute-start.18 = (bf16[256,320]{1,0:T(8,128)(2,1)S(1)}, bf16[256,320]{1,0:T(8,128)(2,1)S(1)}, u32[]{:S(2)}, u32[]{:S(2)}) collective-permute-start(bf16[256,320]{1,0:T(8,128)(2,1)S(1)} %get-tuple-element.44), channel_id=1, source_target_pairs={{0,0},{1,4},{2,2},{3,6},{4,1},{5,5},{6,3},{7,7},{8,8},{9,12},{10,1... | collective-permute-start | bytes 491528 | tf_op jit(solution)/shard_map/ppermute | solution.py:22
  69.4 4.9 %collective-permute-start.20 = (f32[40,128]{1,0:T(8,128)S(1)}, f32[40,128]{1,0:T(8,128)S(1)}, u32[]{:S(2)}, u32[]{:S(2)}) collective-permute-start(f32[40,128]{1,0:T(8,128)S(1)} %get-tuple-element.48), channel_id=1, source_target_pairs={{0,8},{1,9},{2,10},{3,11},{4,12},{5,13},{6,14},{7,15},{8,0},{9,1},... | collective-permute-start | bytes 61448 | tf_op jit(solution)/shard_map/ppermute | solution.py:22
  74.3 4.9 %collective-permute-start.22 = (bf16[256,320]{1,0:T(8,128)(2,1)S(1)}, bf16[256,320]{1,0:T(8,128)(2,1)S(1)}, u32[]{:S(2)}, u32[]{:S(2)}) collective-permute-start(bf16[256,320]{1,0:T(8,128)(2,1)S(1)} %collective-permute-done.18.refs_0_), channel_id=1, source_target_pairs={{0,1},{1,0},{2,3},{3,2},{4,5},{5,4},{6,7},{7,6},{8,9},{9,8},{10,11... | collective-permute-start | bytes 491528 | tf_op jit(solution)/shard_map/ppermute | solution.py:22
  75.4 3.8 %collective-permute-start.23 = (bf16[256,320]{1,0:T(8,128)(2,1)S(1)}, bf16[256,320]{1,0:T(8,128)(2,1)S(1)}, u32[]{:S(2)}, u32[]{:S(2)}) collective-permute-start(bf16[256,320]{1,0:T(8,128)(2,1)S(1)} %collective-permute-done.21.refs_1_), channel_id=1, source_target_pairs={{0,1},{1,0},{2,3},{3,2},{4,5},{5,4},{6,7},{7,6},{8,9},{9,8},{10,11... | collective-permute-start | bytes 491528 | tf_op jit(solution)/shard_map/ppermute | solution.py:22
  75.6 4.9 %collective-permute-start.24 = (bf16[2,384]{1,0:T(2,128)(2,1)S(1)}, bf16[2,384]{1,0:T(2,128)(2,1)S(1)}, u32[]{:S(2)}, u32[]{:S(2)}) collective-permute-start(bf16[2,384]{1,0:T(2,128)(2,1)S(1)} %get-tuple-element.55), channel_id=1, source_target_pairs={{0,2},{1,3},{2,0},{3,1},{4,6},{5,7},{6,4},{7,5},{8,10},{9,11},{10,... | collective-permute-start | bytes 4616 | tf_op jit(solution)/shard_map/ppermute | solution.py:22
  77.2 3.6 %collective-permute-start.25 = (bf16[2,384]{1,0:T(2,128)(2,1)S(1)}, bf16[2,384]{1,0:T(2,128)(2,1)S(1)}, u32[]{:S(2)}, u32[]{:S(2)}) collective-permute-start(bf16[2,384]{1,0:T(2,128)(2,1)S(1)} %get-tuple-element.56), channel_id=1, source_target_pairs={{0,4},{1,5},{2,6},{3,7},{4,0},{5,1},{6,2},{7,3},{8,12},{9,13},{10,... | collective-permute-start | bytes 4616 | tf_op jit(solution)/shard_map/ppermute | solution.py:22
  79.0 4.5 %collective-permute-start.26 = (bf16[2,384]{1,0:T(2,128)(2,1)S(1)}, bf16[2,384]{1,0:T(2,128)(2,1)S(1)}, u32[]{:S(2)}, u32[]{:S(2)}) collective-permute-start(bf16[2,384]{1,0:T(2,128)(2,1)S(1)} %get-tuple-element.57), channel_id=1, source_target_pairs={{0,6},{1,7},{2,4},{3,5},{4,2},{5,3},{6,0},{7,1},{8,14},{9,15},{10,... | collective-permute-start | bytes 4616 | tf_op jit(solution)/shard_map/ppermute | solution.py:22

commit v14 on v13

--- a/solution.py
+++ b/solution.py
@@ -527,7 +527,8 @@
         ready = load(table, mine, mine_c, after(across, near, pair), across_c)
         relayed = swap(after(near, ready[0]), n, 4)
         stem_x = swap(after(stem, across), n, 2)
-        here = {turn: swap(ready[turn % 2], n, 4 * turn) for turn in (3, 2, 1)}
+        here = {turn: swap(ready[turn % 2], n, 4 * turn) for turn in (3, 2)}
+        here[1] = swap(after(ready[1], stem_x), n, 4)
         pair_x = swap(after(pair, ready[0]), n, 2)
         halo = jnp.where((z == 1) | (z == 2), near, relayed)
         halo_x = swap(after(halo, pair_x, *here.values()), n, 2)

time: 85 us -> 85.2 us (level)
  waiting for transfers between devices: 32.3 us -> 33.2 us
    ppermute x1, waiting for transfers between devices: 0.01 us -> 1.3 us  [trade(): return lax.ppermute(block, 'utt', [(u, u ^ 1) for u in range(utts)])]
  transfers between devices with their start and end apart: 27 -> 27, of which waited for: 13 -> 14; matrix products, arithmetic and copies ran while one was open for 1% -> 1% of each run, Pallas kernels for 9% -> 9%
where the time goes in v14:
time: 85.2 us; the launch traced here: 85 us
  waiting for transfers between devices  33.2 us (39%)
  starting transfers between devices  25.3 us (30%)
  Pallas kernels  22.8 us (27%)
  local copies, waits for them, and re-layouts  1.87 us (2%)
  other arithmetic  1.02 us (1%)
  between operations  0.88 us (1%)
    ppermute x26, waiting for transfers between devices, send(): return lax.ppermute(block, 'tm', route)  31.9 us
    ppermute x26, starting transfers between devices, send(): return lax.ppermute(block, 'tm', route)  23.7 us
    pallas_call x1, Pallas kernels, encoder(): pl.pallas_call(functools.partial(encoder_kernel, len(parts), depth), out_...  12.6 us
    pallas_call x3, Pallas kernels, norm_half(): pl.pallas_call(norm_kernel, out_shape=jax.ShapeDtypeStruct((256, 1664 if...  2.93 us
    pallas_call x2, Pallas kernels, gather_groups(): pl.pallas_call(functools.partial(gather_kernel, side, rows), out_shape=ja...  2.59 us
    unnamed x12, local copies, waits for them, and re-layouts  1.75 us
  transfers between devices with their start and end apart: 27, of which 14 were waited for; matrix products, arithmetic and copies ran while one was open for 1% of the time, Pallas kernels for 9%

profile of v14, /device:TPU:0, one launch (start us, length us, event | category | flops | bytes accessed | tf_op | source)
XLA Modules:
  0.0 85.0 jit_solution(8715394843363648718)
XLA Ops:
  0.7 0.0 copy-start.2
  0.7 0.1 stack.136.table.places
  0.8 0.0 copy-start.3
  0.9 0.0 copy-start.4
  0.9 0.5 copy-done.2
  1.4 0.1 copy-done.3
  1.5 1.1 %copy-done = bf16[80,3840]{1,0:T(8,128)(2,1)S(1)} copy-done((bf16[80,3840]{1,0:T(8,128)(2,1)S(1)}, bf16[80,3840]{1,0:T(8,128)(2,1)}, u32[]{:S(2)}) %copy-start) | copy-done | bytes 614424
  2.6 1.1 %shard_map.77 = (bf16[2,80,1024]{2,1,0:T(8,128)(2,1)S(1)}, bf16[2,80,1024]{2,1,0:T(8,128)(2,1)S(1)}) custom-call(s32[34]{0:T(128)S(1)} %stack.136.table.places, bf16[80,3840]{1,0:T(8,128)(2,1)S(1)} %copy-done, bf16[2,1280]{1,0:T(2,128)(2,1)S(1)} %copy-done.2, s32[2,16]{1,0:T(2,128)S(1)} %copy-done.3, s32[1,128]{1,0:T(1,128)S(1)} %bitcast.33), custom_call_target="tpu_custom_call" | custom-call | flops 1 | bytes 1 | tf_op jit(solution)/shard_map/pallas_call | solution.py:98
  3.8 3.0 %collective-permute-start = (bf16[2,80,1024]{2,1,0:T(8,128)(2,1)S(1)}, bf16[2,80,1024]{2,1,0:T(8,128)(2,1)S(1)}, u32[]{:S(2)}, u32[]{:S(2)}) collective-permute-start(bf16[2,80,1024]{2,1,0:T(8,128)(2,1)S(1)} %get-tuple-element.31), channel_id=1, source_target_pairs={{0,2},{1,3},{2,0},{3,1},{4,6},{5,7},{6,4},{7,5},{8,10},{9,11},{10,... | collective-permute-start | bytes 983048 | tf_op jit(solution)/shard_map/ppermute | solution.py:22
  6.8 0.7 collective-permute-start.5
  7.5 4.4 %collective-permute-start.3 = (bf16[128,1280]{1,0:T(8,128)(2,1)S(1)}, bf16[128,1280]{1,0:T(8,128)(2,1)S(1)}, u32[]{:S(2)}, u32[]{:S(2)}) collective-permute-start(bf16[128,1280]{1,0:T(8,128)(2,1)S(1)} %copy-done.1), channel_id=1, source_target_pairs={{0,4},{1,5},{2,6},{3,7},{4,0},{5,1},{6,2},{7,3},{8,12},{9,13},{10,... | collective-permute-start | bytes 983048 | tf_op jit(solution)/shard_map/ppermute | solution.py:22
  11.9 0.0 collective-permute-start.4
  11.9 2.6 %collective-permute-done.refs_2_.refs_9_ = bf16[2,80,1024]{2,1,0:T(8,128)(2,1)S(1)} collective-permute-done((bf16[2,80,1024]{2,1,0:T(8,128)(2,1)S(1)}, bf16[2,80,1024]{2,1,0:T(8,128)(2,1)S(1)}, u32[]{:S(2)}, u32[]{:S(2)}) %collective-permute-start) | collective-permute-done | bytes 327712 | tf_op jit(solution)/shard_map/ppermute | solution.py:22
  14.5 4.6 %collective-permute-done.3.here = bf16[128,1280]{1,0:T(8,128)(2,1)S(1)} collective-permute-done((bf16[128,1280]{1,0:T(8,128)(2,1)S(1)}, bf16[128,1280]{1,0:T(8,128)(2,1)S(1)}, u32[]{:S(2)}, u32[]{:S(2)}) %collective-permute-start.3) | collective-permute-done | bytes 327712 | tf_op jit(solution)/shard_map/ppermute | solution.py:22
  19.0 0.5 collective-permute-start.1
  19.6 0.0 collective-permute-done.4.refs_1_.refs_8_
  19.6 0.0 collective-permute-done.6.refs_3_.refs_10_
  19.6 0.6 shard_map.79
  20.2 1.6 %collective-permute-start.7 = (bf16[128,1280]{1,0:T(8,128)(2,1)S(1)}, bf16[128,1280]{1,0:T(8,128)(2,1)S(1)}, u32[]{:S(2)}, u32[]{:S(2)}) collective-permute-start(bf16[128,1280]{1,0:T(8,128)(2,1)S(1)} %collective-permute-done.3.here), channel_id=1, source_target_pairs={{0,2},{1,3},{2,0},{3,1},{4,6},{5,7},{6,4},{7,5},{8,10},{9,11},{10,... | collective-permute-start | bytes 983048 | tf_op jit(solution)/shard_map/ppermute | solution.py:22
  21.7 1.7 %collective-permute-start.9 = (bf16[128,1280]{1,0:T(8,128)(2,1)S(1)}, bf16[128,1280]{1,0:T(8,128)(2,1)}, u32[]{:S(2)}, u32[]{:S(2)}) collective-permute-start(bf16[128,1280]{1,0:T(8,128)(2,1)S(1)} %collective-permute-done.5), channel_id=1, source_target_pairs={{0,4},{1,5},{2,6},{3,7},{4,0},{5,1},{6,2},{7,3},{8,12},{9,13},{10,... | collective-permute-start | bytes 983048 | tf_op jit(solution)/shard_map/ppermute | solution.py:22
  23.5 0.2 collective-permute-start.11
  23.7 2.5 %collective-permute-start.10 = (bf16[80,1024]{1,0:T(8,128)(2,1)S(1)}, bf16[80,1024]{1,0:T(8,128)(2,1)S(1)}, u32[]{:S(2)}, u32[]{:S(2)}) collective-permute-start(bf16[80,1024]{1,0:T(8,128)(2,1)S(1)} %get-tuple-element.39), channel_id=1, source_target_pairs={{0,12},{1,13},{2,14},{3,15},{4,8},{5,9},{6,10},{7,11},{8,4},{9,5},... | collective-permute-start | bytes 491528 | tf_op jit(solution)/shard_map/ppermute | solution.py:22
  26.1 3.6 %collective-permute-done.1.across = bf16[128,1280]{1,0:T(8,128)(2,1)S(1)} collective-permute-done((bf16[128,1280]{1,0:T(8,128)(2,1)S(1)}, bf16[128,1280]{1,0:T(8,128)(2,1)S(1)}, u32[]{:S(2)}, u32[]{:S(2)}) %collective-permute-start.1) | collective-permute-done | bytes 327712 | tf_op jit(solution)/shard_map/ppermute | solution.py:22
  29.7 1.7 %collective-permute-start.12 = (bf16[80,1024]{1,0:T(8,128)(2,1)S(1)}, bf16[80,1024]{1,0:T(8,128)(2,1)S(1)}, u32[]{:S(2)}, u32[]{:S(2)}) collective-permute-start(bf16[80,1024]{1,0:T(8,128)(2,1)S(1)} %get-tuple-element.39), channel_id=1, source_target_pairs={{0,4},{1,5},{2,6},{3,7},{4,0},{5,1},{6,2},{7,3},{8,12},{9,13},{10,... | collective-permute-start | bytes 491528 | tf_op jit(solution)/shard_map/ppermute | solution.py:22
  31.4 1.0 %shard_map.78.refs_0_ = bf16[256,1664]{1,0:T(8,128)(2,1)S(1)} custom-call(s32[34]{0:T(128)S(1)} %stack.136.table.places, f32[1,1280]{1,0:T(1,128)S(1)} %reshape.10.gain, bf16[128,1280]{1,0:T(8,128)(2,1)S(1)} %copy-done.1, bf16[128,1280]{1,0:T(8,128)(2,1)S(1)} %collective-permute-done.1.across), custom_call_target="tpu_custom_call" | custom-call | flops 1 | bytes 1 | tf_op jit(solution)/shard_map/pallas_call | solution.py:162
  32.4 1.9 %collective-permute-done.7.across = bf16[128,1280]{1,0:T(8,128)(2,1)S(1)} collective-permute-done((bf16[128,1280]{1,0:T(8,128)(2,1)S(1)}, bf16[128,1280]{1,0:T(8,128)(2,1)S(1)}, u32[]{:S(2)}, u32[]{:S(2)}) %collective-permute-start.7) | collective-permute-done | bytes 327712 | tf_op jit(solution)/shard_map/ppermute | solution.py:22
  34.3 0.0 collective-permute-start.2
  34.3 1.0 %shard_map.80.refs_2_ = bf16[256,1664]{1,0:T(8,128)(2,1)S(1)} custom-call(s32[34]{0:T(128)S(1)} %stack.136.table.places, f32[1,1280]{1,0:T(1,128)S(1)} %reshape.10.gain, bf16[128,1280]{1,0:T(8,128)(2,1)S(1)} %collective-permute-done.3.here, bf16[128,1280]{1,0:T(8,128)(2,1)S(1)} %collective-permute-done.7.across), custom_call_target="tpu_custom_call" | custom-call | flops 1 | bytes 1 | tf_op jit(solution)/shard_map/pallas_call | solution.py:162
  35.3 1.2 %collective-permute-done.9 = bf16[128,1280]{1,0:T(8,128)(2,1)} collective-permute-done((bf16[128,1280]{1,0:T(8,128)(2,1)S(1)}, bf16[128,1280]{1,0:T(8,128)(2,1)}, u32[]{:S(2)}, u32[]{:S(2)}) %collective-permute-start.9) | collective-permute-done | bytes 327712 | tf_op jit(solution)/shard_map/ppermute | solution.py:22
  36.6 0.0 collective-permute-start.8
  36.6 1.0 %broadcast_select_fusion.here = bf16[128,1280]{1,0:T(8,128)(2,1)S(1)} fusion(bf16[128,1280]{1,0:T(8,128)(2,1)S(1)} %collective-permute-done.5, bf16[128,1280]{1,0:T(8,128)(2,1)} %collective-permute-done.9, pred[]{:T(512)S(6)} %or.3), kind=kLoop, calls=%fused_computation | loop fusion | flops 163840 | bytes 983041 | tf_op jit(solution)/shard_map/jit(_where)/select_n | solution.py:533
  37.6 2.4 %collective-permute-done.12.refs_0_ = bf16[80,1024]{1,0:T(8,128)(2,1)S(1)} collective-permute-done((bf16[80,1024]{1,0:T(8,128)(2,1)S(1)}, bf16[80,1024]{1,0:T(8,128)(2,1)S(1)}, u32[]{:S(2)}, u32[]{:S(2)}) %collective-permute-start.12) | collective-permute-done | bytes 163872 | tf_op jit(solution)/shard_map/ppermute | solution.py:22
  40.0 1.6 %collective-permute-start.14 = (bf16[240,1024]{1,0:T(8,128)(2,1)S(1)}, bf16[240,1024]{1,0:T(8,128)(2,1)S(1)}, u32[]{:S(2)}, u32[]{:S(2)}) collective-permute-start(bf16[240,1024]{1,0:T(8,128)(2,1)S(1)} %shard_map.81.refs_1_.refs_11_), channel_id=1, source_target_pairs={{0,16},{16,0},{1,17},{17,1},{2,18},{18,2},{3,19},{19,3},{4,20},{20... | collective-permute-start | bytes 1474568 | tf_op jit(solution)/shard_map/ppermute | solution.py:520
  41.6 0.5 collective-permute-start.13
  42.1 0.0 collective-permute-start.16
  42.2 1.3 %shard_map.82 = (f32[8,1536]{1,0:T(8,128)S(1)}, f32[80,320]{1,0:T(8,128)S(1)}, f32[16,64]{1,0:T(8,128)S(1)}) custom-call(s32[34]{0:T(128)S(1)} %stack.136.table.places, bf16[80,1024]{1,0:T(8,128)(2,1)S(1)} %get-tuple-element.35.refs_0_, bf16[240,1024]{1,0:T(8,128)(2,1)S(1)} %shard_map.81.refs_1_.refs_11_), custom_call_target="tpu_custom_call" | custom-call | flops 1 | bytes 1 | tf_op jit(solution)/shard_map/pallas_call | solution.py:208
  43.5 5.6 %collective-permute-done.13.across = bf16[128,1280]{1,0:T(8,128)(2,1)S(1)} collective-permute-done((bf16[128,1280]{1,0:T(8,128)(2,1)S(1)}, bf16[128,1280]{1,0:T(8,128)(2,1)S(1)}, u32[]{:S(2)}, u32[]{:S(2)}) %collective-permute-start.13) | collective-permute-done | bytes 327712 | tf_op jit(solution)/shard_map/ppermute | solution.py:22
  49.1 1.0 %shard_map.83.refs_4_ = bf16[256,1280]{1,0:T(8,128)(2,1)S(1)} custom-call(s32[34]{0:T(128)S(1)} %stack.136.table.places, f32[1,1280]{1,0:T(1,128)S(1)} %reshape.10.gain, bf16[128,1280]{1,0:T(8,128)(2,1)S(1)} %broadcast_select_fusion.here, bf16[128,1280]{1,0:T(8,128)(2,1)S(1)} %collective-permute-done.13.across), custom_call_target="tpu_custom_call" | custom-call | flops 1 | bytes 1 | tf_op jit(solution)/shard_map/pallas_call | solution.py:162
  50.1 1.3 %collective-permute-done.14.refs_13_ = bf16[240,1024]{1,0:T(8,128)(2,1)S(1)} collective-permute-done((bf16[240,1024]{1,0:T(8,128)(2,1)S(1)}, bf16[240,1024]{1,0:T(8,128)(2,1)S(1)}, u32[]{:S(2)}, u32[]{:S(2)}) %collective-permute-start.14) | collective-permute-done | bytes 491552 | tf_op jit(solution)/shard_map/ppermute | solution.py:520
  51.4 0.0 collective-permute-start.15
  51.4 0.0 collective-permute-done.16.refs_12_
  51.4 0.0 collective-permute-done.2.refs_1_
  51.4 0.6 collective-permute-start.17
  52.0 1.5 %collective-permute-done.15.refs_5_ = bf16[256,1280]{1,0:T(8,128)(2,1)S(1)} collective-permute-done((bf16[256,1280]{1,0:T(8,128)(2,1)S(1)}, bf16[256,1280]{1,0:T(8,128)(2,1)S(1)}, u32[]{:S(2)}, u32[]{:S(2)}) %collective-permute-start.15) | collective-permute-done | bytes 655392 | tf_op jit(solution)/shard_map/ppermute | solution.py:22
  53.5 0.7 collective-permute-done.17.refs_14_
  54.2 12.6 %shard_map.84 = (bf16[512,320]{1,0:T(8,128)(2,1)S(1)}, bf16[256,320]{1,0:T(8,128)(2,1)S(1)}, bf16[256,320]{1,0:T(8,128)(2,1)S(1)}) custom-call(s32[34]{0:T(128)S(1)} %stack.136.table.places, bf16[256,1664]{1,0:T(8,128)(2,1)S(1)} %shard_map.78.refs_0_, bf16[256,1664]{1,0:T(8,128)(2,1)S(1)} %collective-permute-done.2.refs_1_, ...), custom_call_target="tpu_custom_call" | custom-call | flops 1 | bytes 1 | tf_op jit(solution)/shard_map/pallas_call | solution.py:355
  66.8 0.2 collective-permute-start.19
  67.0 0.5 collective-permute-start.21
  67.5 0.7 collective-permute-start.18
  68.2 0.4 collective-permute-done.19.beside
  68.6 1.3 %shard_map.85 = (f32[40,128]{1,0:T(8,128)S(1)}, f32[40,128]{1,0:T(8,128)S(1)}) custom-call(s32[34]{0:T(128)S(1)} %stack.136.table.places, f32[80,320]{1,0:T(8,128)S(1)} %get-tuple-element.47.tokens, f32[16,64]{1,0:T(8,128)S(1)} %get-tuple-element.48.asked, bf16[512,320]{1,0:T(8,128)(2,1)S(1)} %get-tuple-element.49.memory, ...), custom_call_target="tpu_custom_call" | custom-call | flops 1 | bytes 1 | tf_op jit(solution)/shard_map/pallas_call | solution.py:421
  69.9 0.2 collective-permute-start.20
  70.1 4.7 %collective-permute-done.21.refs_1_ = bf16[256,320]{1,0:T(8,128)(2,1)S(1)} collective-permute-done((bf16[256,320]{1,0:T(8,128)(2,1)S(1)}, bf16[256,320]{1,0:T(8,128)(2,1)S(1)}, u32[]{:S(2)}, u32[]{:S(2)}) %collective-permute-start.21) | collective-permute-done | bytes 163872 | tf_op jit(solution)/shard_map/ppermute | solution.py:22
  74.8 0.0 collective-permute-done.20.refs_1_
  74.8 1.1 %collective-permute-start.22 = (bf16[256,320]{1,0:T(8,128)(2,1)S(1)}, bf16[256,320]{1,0:T(8,128)(2,1)S(1)}, u32[]{:S(2)}, u32[]{:S(2)}) collective-permute-start(bf16[256,320]{1,0:T(8,128)(2,1)S(1)} %collective-permute-done.18.refs_0_), channel_id=1, source_target_pairs={{0,1},{1,0},{2,3},{3,2},{4,5},{5,4},{6,7},{7,6},{8,9},{9,8},{10,11... | collective-permute-start | bytes 491528 | tf_op jit(solution)/shard_map/ppermute | solution.py:22
  75.9 0.0 collective-permute-start.23
  75.9 0.2 shard_map.87
  76.2 1.6 %collective-permute-start.24 = (bf16[2,384]{1,0:T(2,128)(2,1)S(1)}, bf16[2,384]{1,0:T(2,128)(2,1)S(1)}, u32[]{:S(2)}, u32[]{:S(2)}) collective-permute-start(bf16[2,384]{1,0:T(2,128)(2,1)S(1)} %get-tuple-element.57), channel_id=1, source_target_pairs={{0,2},{1,3},{2,0},{3,1},{4,6},{5,7},{6,4},{7,5},{8,10},{9,11},{10,... | collective-permute-start | bytes 4616 | tf_op jit(solution)/shard_map/ppermute | solution.py:22
  77.7 1.6 %collective-permute-start.25 = (bf16[2,384]{1,0:T(2,128)(2,1)S(1)}, bf16[2,384]{1,0:T(2,128)(2,1)S(1)}, u32[]{:S(2)}, u32[]{:S(2)}) collective-permute-start(bf16[2,384]{1,0:T(2,128)(2,1)S(1)} %get-tuple-element.58), channel_id=1, source_target_pairs={{0,4},{1,5},{2,6},{3,7},{4,0},{5,1},{6,2},{7,3},{8,12},{9,13},{10,... | collective-permute-start | bytes 4616 | tf_op jit(solution)/shard_map/ppermute | solution.py:22
  79.3 0.4 collective-permute-start.26
  79.7 1.4 %shard_map.86 = bf16[128,1280]{1,0:T(8,128)(2,1)} custom-call(s32[34]{0:T(128)S(1)} %stack.136.table.places, bf16[256,320]{1,0:T(8,128)(2,1)S(1)} %collective-permute-done.18.refs_0_, bf16[256,320]{1,0:T(8,128)(2,1)S(1)} %collective-permute-done.21.refs_1_, bf16[256,320]{1,0:T(8,128)(2,1)S(1)} %collective-permute-done.22.refs_2_, ...), custom_call_target="tpu_custom_call" | custom-call | flops 1 | bytes 1 | tf_op jit(solution)/shard_map/pallas_call | solution.py:475
  81.1 0.2 collective-permute-done.25.refs_2_
  81.3 2.5 %collective-permute-done.26.refs_3_ = bf16[2,384]{1,0:T(2,128)(2,1)S(1)} collective-permute-done((bf16[2,384]{1,0:T(2,128)(2,1)S(1)}, bf16[2,384]{1,0:T(2,128)(2,1)S(1)}, u32[]{:S(2)}, u32[]{:S(2)}) %collective-permute-start.26) | collective-permute-done | bytes 1568 | tf_op jit(solution)/shard_map/ppermute | solution.py:22
  83.7 1.2 %shard_map.88 = bf16[2,1280]{1,0:T(2,128)(2,1)} custom-call(s32[34]{0:T(128)S(1)} %stack.136.table.places, bf16[2,384]{1,0:T(2,128)(2,1)S(1)} %get-tuple-element.56.refs_0_, bf16[2,384]{1,0:T(2,128)(2,1)S(1)} %collective-permute-done.24.refs_1_, bf16[2,384]{1,0:T(2,128)(2,1)S(1)} %collective-permute-done.25.refs_2_, ...), custom_call_target="tpu_custom_call" | custom-call | flops 1 | bytes 1 | tf_op jit(solution)/shard_map/pallas_call | solution.py:475
  (17 shorter events, 0.1 us)
Async XLA Ops:
  0.7 0.7 copy-start.2
  0.8 0.7 copy-start.3
  0.9 0.7 copy-start.4
  1.5 1.1 %copy-start = (bf16[80,3840]{1,0:T(8,128)(2,1)S(1)}, bf16[80,3840]{1,0:T(8,128)(2,1)}, u32[]{:S(2)}) copy-start(bf16[80,3840]{1,0:T(8,128)(2,1)} %refs_0_.1) | copy-start | bytes 1843204
  2.6 4.2 %copy-start.1 = (bf16[128,1280]{1,0:T(8,128)(2,1)S(1)}, bf16[128,1280]{1,0:T(8,128)(2,1)}, u32[]{:S(2)}) copy-start(bf16[128,1280]{1,0:T(8,128)(2,1)} %here.1) | copy-start | bytes 983044
  3.8 10.7 %collective-permute-start = (bf16[2,80,1024]{2,1,0:T(8,128)(2,1)S(1)}, bf16[2,80,1024]{2,1,0:T(8,128)(2,1)S(1)}, u32[]{:S(2)}, u32[]{:S(2)}) collective-permute-start(bf16[2,80,1024]{2,1,0:T(8,128)(2,1)S(1)} %get-tuple-element.31), channel_id=1, source_target_pairs={{0,2},{1,3},{2,0},{3,1},{4,6},{5,7},{6,4},{7,5},{8,10},{9,11},{10,... | collective-permute-start | bytes 983048 | tf_op jit(solution)/shard_map/ppermute | solution.py:22
  6.8 7.7 %collective-permute-start.5 = (bf16[128,1280]{1,0:T(8,128)(2,1)S(1)}, bf16[128,1280]{1,0:T(8,128)(2,1)S(1)}, u32[]{:S(2)}, u32[]{:S(2)}) collective-permute-start(bf16[128,1280]{1,0:T(8,128)(2,1)S(1)} %copy-done.1), channel_id=1, source_target_pairs={{4,8},{5,9},{6,10},{7,11},{8,4},{9,5},{10,6},{11,7},{20,24},{21,25... | collective-permute-start | bytes 983048 | tf_op jit(solution)/shard_map/ppermute | solution.py:22
  7.5 11.6 %collective-permute-start.3 = (bf16[128,1280]{1,0:T(8,128)(2,1)S(1)}, bf16[128,1280]{1,0:T(8,128)(2,1)S(1)}, u32[]{:S(2)}, u32[]{:S(2)}) collective-permute-start(bf16[128,1280]{1,0:T(8,128)(2,1)S(1)} %copy-done.1), channel_id=1, source_target_pairs={{0,4},{1,5},{2,6},{3,7},{4,0},{5,1},{6,2},{7,3},{8,12},{9,13},{10,... | collective-permute-start | bytes 983048 | tf_op jit(solution)/shard_map/ppermute | solution.py:22
  11.9 7.7 %collective-permute-start.4 = (bf16[2,80,1024]{2,1,0:T(8,128)(2,1)S(1)}, bf16[2,80,1024]{2,1,0:T(8,128)(2,1)S(1)}, u32[]{:S(2)}, u32[]{:S(2)}) collective-permute-start(bf16[2,80,1024]{2,1,0:T(8,128)(2,1)S(1)} %get-tuple-element.33.refs_0_.refs_7_), channel_id=1, source_target_pairs={{0,1},{1,0},{2,3},{3,2},{4,5},{5,4},{6,7},{7,6},{8,9},{9,8},{10,11... | collective-permute-start | bytes 983048 | tf_op jit(solution)/shard_map/ppermute | solution.py:22
  14.5 5.1 %collective-permute-start.6 = (bf16[2,80,1024]{2,1,0:T(8,128)(2,1)S(1)}, bf16[2,80,1024]{2,1,0:T(8,128)(2,1)S(1)}, u32[]{:S(2)}, u32[]{:S(2)}) collective-permute-start(bf16[2,80,1024]{2,1,0:T(8,128)(2,1)S(1)} %collective-permute-done.refs_2_.refs_9_), channel_id=1, source_target_pairs={{0,1},{1,0},{2,3},{3,2},{4,5},{5,4},{6,7},{7,6},{8,9},{9,8},{10,11... | collective-permute-start | bytes 983048 | tf_op jit(solution)/shard_map/ppermute | solution.py:22
  19.0 10.6 %collective-permute-start.1 = (bf16[128,1280]{1,0:T(8,128)(2,1)S(1)}, bf16[128,1280]{1,0:T(8,128)(2,1)S(1)}, u32[]{:S(2)}, u32[]{:S(2)}) collective-permute-start(bf16[128,1280]{1,0:T(8,128)(2,1)S(1)} %copy-done.1), channel_id=1, source_target_pairs={{0,2},{1,3},{2,0},{3,1},{4,6},{5,7},{6,4},{7,5},{8,10},{9,11},{10,... | collective-permute-start | bytes 983048 | tf_op jit(solution)/shard_map/ppermute | solution.py:22
  19.6 3.9 %copy-start.5 = (f32[1280]{0:T(1024)S(1)}, f32[1280]{0:T(1024)}, u32[]{:S(2)}) copy-start(f32[1280]{0:T(1024)} %param.7) | copy-start | bytes 15364
  20.2 14.1 %collective-permute-start.7 = (bf16[128,1280]{1,0:T(8,128)(2,1)S(1)}, bf16[128,1280]{1,0:T(8,128)(2,1)S(1)}, u32[]{:S(2)}, u32[]{:S(2)}) collective-permute-start(bf16[128,1280]{1,0:T(8,128)(2,1)S(1)} %collective-permute-done.3.here), channel_id=1, source_target_pairs={{0,2},{1,3},{2,0},{3,1},{4,6},{5,7},{6,4},{7,5},{8,10},{9,11},{10,... | collective-permute-start | bytes 983048 | tf_op jit(solution)/shard_map/ppermute | solution.py:22
  21.7 14.8 %collective-permute-start.9 = (bf16[128,1280]{1,0:T(8,128)(2,1)S(1)}, bf16[128,1280]{1,0:T(8,128)(2,1)}, u32[]{:S(2)}, u32[]{:S(2)}) collective-permute-start(bf16[128,1280]{1,0:T(8,128)(2,1)S(1)} %collective-permute-done.5), channel_id=1, source_target_pairs={{0,4},{1,5},{2,6},{3,7},{4,0},{5,1},{6,2},{7,3},{8,12},{9,13},{10,... | collective-permute-start | bytes 983048 | tf_op jit(solution)/shard_map/ppermute | solution.py:22
  23.5 16.5 %collective-permute-start.11 = (bf16[80,1024]{1,0:T(8,128)(2,1)S(1)}, bf16[80,1024]{1,0:T(8,128)(2,1)S(1)}, u32[]{:S(2)}, u32[]{:S(2)}) collective-permute-start(bf16[80,1024]{1,0:T(8,128)(2,1)S(1)} %get-tuple-element.35.refs_0_), channel_id=1, source_target_pairs={{0,8},{1,9},{2,10},{3,11},{4,12},{5,13},{6,14},{7,15},{8,0},{9,1},... | collective-permute-start | bytes 491528 | tf_op jit(solution)/shard_map/ppermute | solution.py:22
  23.7 16.3 %collective-permute-start.10 = (bf16[80,1024]{1,0:T(8,128)(2,1)S(1)}, bf16[80,1024]{1,0:T(8,128)(2,1)S(1)}, u32[]{:S(2)}, u32[]{:S(2)}) collective-permute-start(bf16[80,1024]{1,0:T(8,128)(2,1)S(1)} %get-tuple-element.39), channel_id=1, source_target_pairs={{0,12},{1,13},{2,14},{3,15},{4,8},{5,9},{6,10},{7,11},{8,4},{9,5},... | collective-permute-start | bytes 491528 | tf_op jit(solution)/shard_map/ppermute | solution.py:22
  29.7 10.3 %collective-permute-start.12 = (bf16[80,1024]{1,0:T(8,128)(2,1)S(1)}, bf16[80,1024]{1,0:T(8,128)(2,1)S(1)}, u32[]{:S(2)}, u32[]{:S(2)}) collective-permute-start(bf16[80,1024]{1,0:T(8,128)(2,1)S(1)} %get-tuple-element.39), channel_id=1, source_target_pairs={{0,4},{1,5},{2,6},{3,7},{4,0},{5,1},{6,2},{7,3},{8,12},{9,13},{10,... | collective-permute-start | bytes 491528 | tf_op jit(solution)/shard_map/ppermute | solution.py:22
  34.3 17.1 %collective-permute-start.2 = (bf16[256,1664]{1,0:T(8,128)(2,1)S(1)}, bf16[256,1664]{1,0:T(8,128)(2,1)S(1)}, u32[]{:S(2)}, u32[]{:S(2)}) collective-permute-start(bf16[256,1664]{1,0:T(8,128)(2,1)S(1)} %shard_map.78.refs_0_), channel_id=1, source_target_pairs={{0,1},{1,0},{2,3},{3,2},{4,5},{5,4},{6,7},{7,6},{8,9},{9,8},{10,11... | collective-permute-start | bytes 2555912 | tf_op jit(solution)/shard_map/ppermute | solution.py:22
  36.6 14.8 %collective-permute-start.8 = (bf16[256,1664]{1,0:T(8,128)(2,1)S(1)}, bf16[256,1664]{1,0:T(8,128)(2,1)S(1)}, u32[]{:S(2)}, u32[]{:S(2)}) collective-permute-start(bf16[256,1664]{1,0:T(8,128)(2,1)S(1)} %shard_map.80.refs_2_), channel_id=1, source_target_pairs={{0,1},{1,0},{2,3},{3,2},{4,5},{5,4},{6,7},{7,6},{8,9},{9,8},{10,11... | collective-permute-start | bytes 2555912 | tf_op jit(solution)/shard_map/ppermute | solution.py:22
  40.0 11.3 %collective-permute-start.14 = (bf16[240,1024]{1,0:T(8,128)(2,1)S(1)}, bf16[240,1024]{1,0:T(8,128)(2,1)S(1)}, u32[]{:S(2)}, u32[]{:S(2)}) collective-permute-start(bf16[240,1024]{1,0:T(8,128)(2,1)S(1)} %shard_map.81.refs_1_.refs_11_), channel_id=1, source_target_pairs={{0,16},{16,0},{1,17},{17,1},{2,18},{18,2},{3,19},{19,3},{4,20},{20... | collective-permute-start | bytes 1474568 | tf_op jit(solution)/shard_map/ppermute | solution.py:520
  41.6 7.5 %collective-permute-start.13 = (bf16[128,1280]{1,0:T(8,128)(2,1)S(1)}, bf16[128,1280]{1,0:T(8,128)(2,1)S(1)}, u32[]{:S(2)}, u32[]{:S(2)}) collective-permute-start(bf16[128,1280]{1,0:T(8,128)(2,1)S(1)} %broadcast_select_fusion.here), channel_id=1, source_target_pairs={{0,2},{1,3},{2,0},{3,1},{4,6},{5,7},{6,4},{7,5},{8,10},{9,11},{10,... | collective-permute-start | bytes 983048 | tf_op jit(solution)/shard_map/ppermute | solution.py:22
  42.1 9.2 %collective-permute-start.16 = (bf16[240,1024]{1,0:T(8,128)(2,1)S(1)}, bf16[240,1024]{1,0:T(8,128)(2,1)S(1)}, u32[]{:S(2)}, u32[]{:S(2)}) collective-permute-start(bf16[240,1024]{1,0:T(8,128)(2,1)S(1)} %shard_map.81.refs_1_.refs_11_), channel_id=1, source_target_pairs={{0,1},{1,0},{2,3},{3,2},{4,5},{5,4},{6,7},{7,6},{8,9},{9,8},{10,11... | collective-permute-start | bytes 1474568 | tf_op jit(solution)/shard_map/ppermute | solution.py:22
  51.4 2.1 %collective-permute-start.15 = (bf16[256,1280]{1,0:T(8,128)(2,1)S(1)}, bf16[256,1280]{1,0:T(8,128)(2,1)S(1)}, u32[]{:S(2)}, u32[]{:S(2)}) collective-permute-start(bf16[256,1280]{1,0:T(8,128)(2,1)S(1)} %shard_map.83.refs_4_), channel_id=1, source_target_pairs={{0,1},{1,0},{2,3},{3,2},{4,5},{5,4},{6,7},{7,6},{8,9},{9,8},{10,11... | collective-permute-start | bytes 1966088 | tf_op jit(solution)/shard_map/ppermute | solution.py:22
  51.4 2.8 %collective-permute-start.17 = (bf16[240,1024]{1,0:T(8,128)(2,1)S(1)}, bf16[240,1024]{1,0:T(8,128)(2,1)S(1)}, u32[]{:S(2)}, u32[]{:S(2)}) collective-permute-start(bf16[240,1024]{1,0:T(8,128)(2,1)S(1)} %collective-permute-done.14.refs_13_), channel_id=1, source_target_pairs={{0,1},{1,0},{2,3},{3,2},{4,5},{5,4},{6,7},{7,6},{8,9},{9,8},{10,11... | collective-permute-start | bytes 1474568 | tf_op jit(solution)/shard_map/ppermute | solution.py:22
  66.8 1.8 %collective-permute-start.19 = (bf16[512,320]{1,0:T(8,128)(2,1)S(1)}, bf16[512,320]{1,0:T(8,128)(2,1)S(1)}, u32[]{:S(2)}, u32[]{:S(2)}) collective-permute-start(bf16[512,320]{1,0:T(8,128)(2,1)S(1)} %get-tuple-element.49.memory), channel_id=1, source_target_pairs={{0,1},{1,0},{2,3},{3,2},{4,5},{5,4},{6,7},{7,6},{8,9},{9,8},{10,11... | collective-permute-start | bytes 983048 | tf_op jit(solution)/shard_map/ppermute | solution.py:22
  67.0 7.8 %collective-permute-start.21 = (bf16[256,320]{1,0:T(8,128)(2,1)S(1)}, bf16[256,320]{1,0:T(8,128)(2,1)S(1)}, u32[]{:S(2)}, u32[]{:S(2)}) collective-permute-start(bf16[256,320]{1,0:T(8,128)(2,1)S(1)} %get-tuple-element.52), channel_id=1, source_target_pairs={{0,2},{1,6},{2,0},{3,4},{4,3},{5,7},{6,1},{7,5},{8,10},{9,14},{10,... | collective-permute-start | bytes 491528 | tf_op jit(solution)/shard_map/ppermute | solution.py:22
  67.5 7.3 %collective-permute-start.18 = (bf16[256,320]{1,0:T(8,128)(2,1)S(1)}, bf16[256,320]{1,0:T(8,128)(2,1)S(1)}, u32[]{:S(2)}, u32[]{:S(2)}) collective-permute-start(bf16[256,320]{1,0:T(8,128)(2,1)S(1)} %get-tuple-element.46), channel_id=1, source_target_pairs={{0,0},{1,4},{2,2},{3,6},{4,1},{5,5},{6,3},{7,7},{8,8},{9,12},{10,1... | collective-permute-start | bytes 491528 | tf_op jit(solution)/shard_map/ppermute | solution.py:22
  69.9 4.9 %collective-permute-start.20 = (f32[40,128]{1,0:T(8,128)S(1)}, f32[40,128]{1,0:T(8,128)S(1)}, u32[]{:S(2)}, u32[]{:S(2)}) collective-permute-start(f32[40,128]{1,0:T(8,128)S(1)} %get-tuple-element.50), channel_id=1, source_target_pairs={{0,8},{1,9},{2,10},{3,11},{4,12},{5,13},{6,14},{7,15},{8,0},{9,1},... | collective-permute-start | bytes 61448 | tf_op jit(solution)/shard_map/ppermute | solution.py:22
  74.8 4.9 %collective-permute-start.22 = (bf16[256,320]{1,0:T(8,128)(2,1)S(1)}, bf16[256,320]{1,0:T(8,128)(2,1)S(1)}, u32[]{:S(2)}, u32[]{:S(2)}) collective-permute-start(bf16[256,320]{1,0:T(8,128)(2,1)S(1)} %collective-permute-done.18.refs_0_), channel_id=1, source_target_pairs={{0,1},{1,0},{2,3},{3,2},{4,5},{5,4},{6,7},{7,6},{8,9},{9,8},{10,11... | collective-permute-start | bytes 491528 | tf_op jit(solution)/shard_map/ppermute | solution.py:22
  75.9 3.8 %collective-permute-start.23 = (bf16[256,320]{1,0:T(8,128)(2,1)S(1)}, bf16[256,320]{1,0:T(8,128)(2,1)S(1)}, u32[]{:S(2)}, u32[]{:S(2)}) collective-permute-start(bf16[256,320]{1,0:T(8,128)(2,1)S(1)} %collective-permute-done.21.refs_1_), channel_id=1, source_target_pairs={{0,1},{1,0},{2,3},{3,2},{4,5},{5,4},{6,7},{7,6},{8,9},{9,8},{10,11... | collective-permute-start | bytes 491528 | tf_op jit(solution)/shard_map/ppermute | solution.py:22
  76.2 4.9 %collective-permute-start.24 = (bf16[2,384]{1,0:T(2,128)(2,1)S(1)}, bf16[2,384]{1,0:T(2,128)(2,1)S(1)}, u32[]{:S(2)}, u32[]{:S(2)}) collective-permute-start(bf16[2,384]{1,0:T(2,128)(2,1)S(1)} %get-tuple-element.57), channel_id=1, source_target_pairs={{0,2},{1,3},{2,0},{3,1},{4,6},{5,7},{6,4},{7,5},{8,10},{9,11},{10,... | collective-permute-start | bytes 4616 | tf_op jit(solution)/shard_map/ppermute | solution.py:22
  77.7 3.6 %collective-permute-start.25 = (bf16[2,384]{1,0:T(2,128)(2,1)S(1)}, bf16[2,384]{1,0:T(2,128)(2,1)S(1)}, u32[]{:S(2)}, u32[]{:S(2)}) collective-permute-start(bf16[2,384]{1,0:T(2,128)(2,1)S(1)} %get-tuple-element.58), channel_id=1, source_target_pairs={{0,4},{1,5},{2,6},{3,7},{4,0},{5,1},{6,2},{7,3},{8,12},{9,13},{10,... | collective-permute-start | bytes 4616 | tf_op jit(solution)/shard_map/ppermute | solution.py:22
  79.3 4.5 %collective-permute-start.26 = (bf16[2,384]{1,0:T(2,128)(2,1)S(1)}, bf16[2,384]{1,0:T(2,128)(2,1)S(1)}, u32[]{:S(2)}, u32[]{:S(2)}) collective-permute-start(bf16[2,384]{1,0:T(2,128)(2,1)S(1)} %get-tuple-element.59), channel_id=1, source_target_pairs={{0,6},{1,7},{2,4},{3,5},{4,2},{5,3},{6,0},{7,1},{8,14},{9,15},{10,... | collective-permute-start | bytes 4616 | tf_op jit(solution)/shard_map/ppermute | solution.py:22

commit v15 on v13

--- a/solution.py
+++ b/solution.py
@@ -524,6 +524,7 @@
         )
         across = swap(theirs, n, 2)
         mine_c, across_c = swap(mine, n, 1), swap(across, n, 1)
+        near = send(after(stem, mine_c), near_route)
         ready = load(table, mine, mine_c, after(across, near, pair), across_c)
         relayed = swap(after(near, ready[0]), n, 4)
         stem_x = swap(after(stem, across), n, 2)

time: 85 us -> 86.8 us (1.021)
  starting transfers between devices: 25.9 us -> 35.6 us
  waiting for transfers between devices: 32.3 us -> 27.5 us
  Pallas kernels: 22.8 us -> 19.7 us
    ppermute x26, starting transfers between devices: 24.3 us -> 34 us  [send(): return lax.ppermute(block, 'tm', route)]
    ppermute x26, waiting for transfers between devices: 32.3 us -> 26.2 us  [send(): return lax.ppermute(block, 'tm', route)]
    pallas_call x1, Pallas kernels: 12.6 us -> 9.52 us  [encoder(): pl.pallas_call(functools.partial(encoder_kernel, len(parts), depth), out_...]
    ppermute x1, waiting for transfers between devices: 0.01 us -> 1.3 us  [trade(): return lax.ppermute(block, 'utt', [(u, u ^ 1) for u in range(utts)])]
where the time goes in v15:
time: 86.8 us; the launch traced here: 86.6 us
  starting transfers between devices  35.6 us (41%)
  waiting for transfers between devices  27.5 us (32%)
  Pallas kernels  19.7 us (23%)
  local copies, waits for them, and re-layouts  1.87 us (2%)
  other arithmetic  1.02 us (1%)
  between operations  0.9 us (1%)
    ppermute x26, starting transfers between devices, send(): return lax.ppermute(block, 'tm', route)  34 us
    ppermute x26, waiting for transfers between devices, send(): return lax.ppermute(block, 'tm', route)  26.2 us
    pallas_call x1, Pallas kernels, encoder(): pl.pallas_call(functools.partial(encoder_kernel, len(parts), depth), out_...  9.52 us
    pallas_call x3, Pallas kernels, norm_half(): pl.pallas_call(norm_kernel, out_shape=jax.ShapeDtypeStruct((256, 1664 if...  2.93 us
    pallas_call x2, Pallas kernels, gather_groups(): pl.pallas_call(functools.partial(gather_kernel, side, rows), out_shape=ja...  2.59 us
    unnamed x12, local copies, waits for them, and re-layouts  1.76 us
  transfers between devices with their start and end apart: 27, of which 13 were waited for; matrix products, arithmetic and copies ran while one was open for 1% of the time, Pallas kernels for 9%

profile of v15, /device:TPU:0, one launch (start us, length us, event | category | flops | bytes accessed | tf_op | source)
XLA Modules:
  0.0 86.6 jit_solution(7717340102836533848)
XLA Ops:
  0.7 0.0 copy-start.2
  0.7 0.1 stack.136.table.places
  0.8 0.0 copy-start.3
  0.9 0.0 copy-start.4
  0.9 0.5 copy-done.2
  1.4 0.1 copy-done.3
  1.5 1.1 %copy-done = bf16[80,3840]{1,0:T(8,128)(2,1)S(1)} copy-done((bf16[80,3840]{1,0:T(8,128)(2,1)S(1)}, bf16[80,3840]{1,0:T(8,128)(2,1)}, u32[]{:S(2)}) %copy-start) | copy-done | bytes 614424
  2.6 1.1 %shard_map.77 = (bf16[2,80,1024]{2,1,0:T(8,128)(2,1)S(1)}, bf16[2,80,1024]{2,1,0:T(8,128)(2,1)S(1)}) custom-call(s32[34]{0:T(128)S(1)} %stack.136.table.places, bf16[80,3840]{1,0:T(8,128)(2,1)S(1)} %copy-done, bf16[2,1280]{1,0:T(2,128)(2,1)S(1)} %copy-done.2, s32[2,16]{1,0:T(2,128)S(1)} %copy-done.3, s32[1,128]{1,0:T(1,128)S(1)} %bitcast.33), custom_call_target="tpu_custom_call" | custom-call | flops 1 | bytes 1 | tf_op jit(solution)/shard_map/pallas_call | solution.py:98
  3.8 0.5 collective-permute-start.4
  4.3 2.6 %collective-permute-start = (bf16[2,80,1024]{2,1,0:T(8,128)(2,1)S(1)}, bf16[2,80,1024]{2,1,0:T(8,128)(2,1)S(1)}, u32[]{:S(2)}, u32[]{:S(2)}) collective-permute-start(bf16[2,80,1024]{2,1,0:T(8,128)(2,1)S(1)} %get-tuple-element.31), channel_id=1, source_target_pairs={{0,2},{1,3},{2,0},{3,1},{4,6},{5,7},{6,4},{7,5},{8,10},{9,11},{10,... | collective-permute-start | bytes 983048 | tf_op jit(solution)/shard_map/ppermute | solution.py:22
  6.9 1.6 %collective-permute-start.3 = (bf16[128,1280]{1,0:T(8,128)(2,1)S(1)}, bf16[128,1280]{1,0:T(8,128)(2,1)S(1)}, u32[]{:S(2)}, u32[]{:S(2)}) collective-permute-start(bf16[128,1280]{1,0:T(8,128)(2,1)S(1)} %copy-done.1), channel_id=1, source_target_pairs={{0,4},{1,5},{2,6},{3,7},{4,0},{5,1},{6,2},{7,3},{8,12},{9,13},{10,... | collective-permute-start | bytes 983048 | tf_op jit(solution)/shard_map/ppermute | solution.py:22
  8.4 0.0 collective-permute-done.4.refs_1_.refs_8_
  8.4 0.7 collective-permute-start.5
  9.1 6.0 %collective-permute-done.refs_2_.refs_9_ = bf16[2,80,1024]{2,1,0:T(8,128)(2,1)S(1)} collective-permute-done((bf16[2,80,1024]{2,1,0:T(8,128)(2,1)S(1)}, bf16[2,80,1024]{2,1,0:T(8,128)(2,1)S(1)}, u32[]{:S(2)}, u32[]{:S(2)}) %collective-permute-start) | collective-permute-done | bytes 327712 | tf_op jit(solution)/shard_map/ppermute | solution.py:22
  15.2 0.0 collective-permute-start.6
  15.2 1.8 %collective-permute-start.1 = (bf16[128,1280]{1,0:T(8,128)(2,1)S(1)}, bf16[128,1280]{1,0:T(8,128)(2,1)S(1)}, u32[]{:S(2)}, u32[]{:S(2)}) collective-permute-start(bf16[128,1280]{1,0:T(8,128)(2,1)S(1)} %copy-done.1), channel_id=1, source_target_pairs={{0,2},{1,3},{2,0},{3,1},{4,6},{5,7},{6,4},{7,5},{8,10},{9,11},{10,... | collective-permute-start | bytes 983048 | tf_op jit(solution)/shard_map/ppermute | solution.py:22
  16.9 0.0 collective-permute-done.3.here
  16.9 0.0 collective-permute-done.5
  16.9 0.0 collective-permute-done.6.refs_3_.refs_10_
  16.9 0.0 copy-start.5
  16.9 0.6 shard_map.79
  17.5 1.7 %collective-permute-start.7 = (bf16[128,1280]{1,0:T(8,128)(2,1)S(1)}, bf16[128,1280]{1,0:T(8,128)(2,1)S(1)}, u32[]{:S(2)}, u32[]{:S(2)}) collective-permute-start(bf16[128,1280]{1,0:T(8,128)(2,1)S(1)} %collective-permute-done.3.here), channel_id=1, source_target_pairs={{0,2},{1,3},{2,0},{3,1},{4,6},{5,7},{6,4},{7,5},{8,10},{9,11},{10,... | collective-permute-start | bytes 983048 | tf_op jit(solution)/shard_map/ppermute | solution.py:22
  19.2 3.2 %collective-permute-start.9 = (bf16[128,1280]{1,0:T(8,128)(2,1)S(1)}, bf16[128,1280]{1,0:T(8,128)(2,1)}, u32[]{:S(2)}, u32[]{:S(2)}) collective-permute-start(bf16[128,1280]{1,0:T(8,128)(2,1)S(1)} %collective-permute-done.5), channel_id=1, source_target_pairs={{0,4},{1,5},{2,6},{3,7},{4,0},{5,1},{6,2},{7,3},{8,12},{9,13},{10,... | collective-permute-start | bytes 983048 | tf_op jit(solution)/shard_map/ppermute | solution.py:22
  22.4 0.1 collective-permute-start.12
  22.5 2.6 %collective-permute-start.10 = (bf16[80,1024]{1,0:T(8,128)(2,1)S(1)}, bf16[80,1024]{1,0:T(8,128)(2,1)S(1)}, u32[]{:S(2)}, u32[]{:S(2)}) collective-permute-start(bf16[80,1024]{1,0:T(8,128)(2,1)S(1)} %get-tuple-element.39), channel_id=1, source_target_pairs={{0,12},{1,13},{2,14},{3,15},{4,8},{5,9},{6,10},{7,11},{8,4},{9,5},... | collective-permute-start | bytes 491528 | tf_op jit(solution)/shard_map/ppermute | solution.py:22
  25.2 0.5 collective-permute-done.1.across
  25.7 2.9 %collective-permute-start.11 = (bf16[80,1024]{1,0:T(8,128)(2,1)S(1)}, bf16[80,1024]{1,0:T(8,128)(2,1)S(1)}, u32[]{:S(2)}, u32[]{:S(2)}) collective-permute-start(bf16[80,1024]{1,0:T(8,128)(2,1)S(1)} %get-tuple-element.36.refs_0_), channel_id=1, source_target_pairs={{0,8},{1,9},{2,10},{3,11},{4,12},{5,13},{6,14},{7,15},{8,0},{9,1},... | collective-permute-start | bytes 491528 | tf_op jit(solution)/shard_map/ppermute | solution.py:22
  28.5 1.0 %shard_map.78.refs_0_ = bf16[256,1664]{1,0:T(8,128)(2,1)S(1)} custom-call(s32[34]{0:T(128)S(1)} %stack.136.table.places, f32[1,1280]{1,0:T(1,128)S(1)} %reshape.10.gain, bf16[128,1280]{1,0:T(8,128)(2,1)S(1)} %copy-done.1, bf16[128,1280]{1,0:T(8,128)(2,1)S(1)} %collective-permute-done.1.across), custom_call_target="tpu_custom_call" | custom-call | flops 1 | bytes 1 | tf_op jit(solution)/shard_map/pallas_call | solution.py:162
  29.5 2.8 %collective-permute-done.7.across = bf16[128,1280]{1,0:T(8,128)(2,1)S(1)} collective-permute-done((bf16[128,1280]{1,0:T(8,128)(2,1)S(1)}, bf16[128,1280]{1,0:T(8,128)(2,1)S(1)}, u32[]{:S(2)}, u32[]{:S(2)}) %collective-permute-start.7) | collective-permute-done | bytes 327712 | tf_op jit(solution)/shard_map/ppermute | solution.py:22
  32.3 0.0 collective-permute-start.2
  32.3 1.0 %shard_map.80.refs_2_ = bf16[256,1664]{1,0:T(8,128)(2,1)S(1)} custom-call(s32[34]{0:T(128)S(1)} %stack.136.table.places, f32[1,1280]{1,0:T(1,128)S(1)} %reshape.10.gain, bf16[128,1280]{1,0:T(8,128)(2,1)S(1)} %collective-permute-done.3.here, bf16[128,1280]{1,0:T(8,128)(2,1)S(1)} %collective-permute-done.7.across), custom_call_target="tpu_custom_call" | custom-call | flops 1 | bytes 1 | tf_op jit(solution)/shard_map/pallas_call | solution.py:162
  33.3 3.1 %collective-permute-done.9 = bf16[128,1280]{1,0:T(8,128)(2,1)} collective-permute-done((bf16[128,1280]{1,0:T(8,128)(2,1)S(1)}, bf16[128,1280]{1,0:T(8,128)(2,1)}, u32[]{:S(2)}, u32[]{:S(2)}) %collective-permute-start.9) | collective-permute-done | bytes 327712 | tf_op jit(solution)/shard_map/ppermute | solution.py:22
  36.4 1.0 %broadcast_select_fusion.here = bf16[128,1280]{1,0:T(8,128)(2,1)S(1)} fusion(bf16[128,1280]{1,0:T(8,128)(2,1)S(1)} %collective-permute-done.5, bf16[128,1280]{1,0:T(8,128)(2,1)} %collective-permute-done.9, pred[]{:T(512)S(6)} %or.3), kind=kLoop, calls=%fused_computation | loop fusion | flops 163840 | bytes 983041 | tf_op jit(solution)/shard_map/jit(_where)/select_n | solution.py:533
  37.5 1.6 %collective-permute-done.12.refs_0_ = bf16[80,1024]{1,0:T(8,128)(2,1)S(1)} collective-permute-done((bf16[80,1024]{1,0:T(8,128)(2,1)S(1)}, bf16[80,1024]{1,0:T(8,128)(2,1)S(1)}, u32[]{:S(2)}, u32[]{:S(2)}) %collective-permute-start.12) | collective-permute-done | bytes 163872 | tf_op jit(solution)/shard_map/ppermute | solution.py:22
  39.1 1.1 %collective-permute-done.10.refs_2_ = bf16[80,1024]{1,0:T(8,128)(2,1)S(1)} collective-permute-done((bf16[80,1024]{1,0:T(8,128)(2,1)S(1)}, bf16[80,1024]{1,0:T(8,128)(2,1)S(1)}, u32[]{:S(2)}, u32[]{:S(2)}) %collective-permute-start.10) | collective-permute-done | bytes 163872 | tf_op jit(solution)/shard_map/ppermute | solution.py:22
  40.2 0.0 collective-permute-done.11.refs_1_
  40.2 1.6 %collective-permute-start.14 = (bf16[240,1024]{1,0:T(8,128)(2,1)S(1)}, bf16[240,1024]{1,0:T(8,128)(2,1)S(1)}, u32[]{:S(2)}, u32[]{:S(2)}) collective-permute-start(bf16[240,1024]{1,0:T(8,128)(2,1)S(1)} %shard_map.81.refs_1_.refs_11_), channel_id=1, source_target_pairs={{0,16},{16,0},{1,17},{17,1},{2,18},{18,2},{3,19},{19,3},{4,20},{20... | collective-permute-start | bytes 1474568 | tf_op jit(solution)/shard_map/ppermute | solution.py:520
  41.8 1.5 %collective-permute-start.13 = (bf16[128,1280]{1,0:T(8,128)(2,1)S(1)}, bf16[128,1280]{1,0:T(8,128)(2,1)S(1)}, u32[]{:S(2)}, u32[]{:S(2)}) collective-permute-start(bf16[128,1280]{1,0:T(8,128)(2,1)S(1)} %broadcast_select_fusion.here), channel_id=1, source_target_pairs={{0,2},{1,3},{2,0},{3,1},{4,6},{5,7},{6,4},{7,5},{8,10},{9,11},{10,... | collective-permute-start | bytes 983048 | tf_op jit(solution)/shard_map/ppermute | solution.py:22
  43.3 0.0 collective-permute-start.16
  43.3 1.3 %shard_map.82 = (f32[8,1536]{1,0:T(8,128)S(1)}, f32[80,320]{1,0:T(8,128)S(1)}, f32[16,64]{1,0:T(8,128)S(1)}) custom-call(s32[34]{0:T(128)S(1)} %stack.136.table.places, bf16[80,1024]{1,0:T(8,128)(2,1)S(1)} %get-tuple-element.36.refs_0_, bf16[240,1024]{1,0:T(8,128)(2,1)S(1)} %shard_map.81.refs_1_.refs_11_), custom_call_target="tpu_custom_call" | custom-call | flops 1 | bytes 1 | tf_op jit(solution)/shard_map/pallas_call | solution.py:208
  44.6 4.3 %collective-permute-done.13.across = bf16[128,1280]{1,0:T(8,128)(2,1)S(1)} collective-permute-done((bf16[128,1280]{1,0:T(8,128)(2,1)S(1)}, bf16[128,1280]{1,0:T(8,128)(2,1)S(1)}, u32[]{:S(2)}, u32[]{:S(2)}) %collective-permute-start.13) | collective-permute-done | bytes 327712 | tf_op jit(solution)/shard_map/ppermute | solution.py:22
  49.0 1.0 %shard_map.83.refs_4_ = bf16[256,1280]{1,0:T(8,128)(2,1)S(1)} custom-call(s32[34]{0:T(128)S(1)} %stack.136.table.places, f32[1,1280]{1,0:T(1,128)S(1)} %reshape.10.gain, bf16[128,1280]{1,0:T(8,128)(2,1)S(1)} %broadcast_select_fusion.here, bf16[128,1280]{1,0:T(8,128)(2,1)S(1)} %collective-permute-done.13.across), custom_call_target="tpu_custom_call" | custom-call | flops 1 | bytes 1 | tf_op jit(solution)/shard_map/pallas_call | solution.py:162
  49.9 1.3 %collective-permute-done.14.refs_13_ = bf16[240,1024]{1,0:T(8,128)(2,1)S(1)} collective-permute-done((bf16[240,1024]{1,0:T(8,128)(2,1)S(1)}, bf16[240,1024]{1,0:T(8,128)(2,1)S(1)}, u32[]{:S(2)}, u32[]{:S(2)}) %collective-permute-start.14) | collective-permute-done | bytes 491552 | tf_op jit(solution)/shard_map/ppermute | solution.py:520
  51.2 0.0 collective-permute-done.2.refs_1_
  51.3 0.6 collective-permute-start.17
  51.8 1.5 %collective-permute-done.15.refs_5_ = bf16[256,1280]{1,0:T(8,128)(2,1)S(1)} collective-permute-done((bf16[256,1280]{1,0:T(8,128)(2,1)S(1)}, bf16[256,1280]{1,0:T(8,128)(2,1)S(1)}, u32[]{:S(2)}, u32[]{:S(2)}) %collective-permute-start.15) | collective-permute-done | bytes 655392 | tf_op jit(solution)/shard_map/ppermute | solution.py:22
  53.3 0.7 collective-permute-done.17.refs_14_
  54.0 9.5 %shard_map.84 = (bf16[512,320]{1,0:T(8,128)(2,1)S(1)}, bf16[256,320]{1,0:T(8,128)(2,1)S(1)}, bf16[256,320]{1,0:T(8,128)(2,1)S(1)}) custom-call(s32[34]{0:T(128)S(1)} %stack.136.table.places, bf16[256,1664]{1,0:T(8,128)(2,1)S(1)} %shard_map.78.refs_0_, bf16[256,1664]{1,0:T(8,128)(2,1)S(1)} %collective-permute-done.2.refs_1_, ...), custom_call_target="tpu_custom_call" | custom-call | flops 1 | bytes 1 | tf_op jit(solution)/shard_map/pallas_call | solution.py:355
  63.6 0.2 collective-permute-start.19
  63.8 4.6 %collective-permute-start.21 = (bf16[256,320]{1,0:T(8,128)(2,1)S(1)}, bf16[256,320]{1,0:T(8,128)(2,1)S(1)}, u32[]{:S(2)}, u32[]{:S(2)}) collective-permute-start(bf16[256,320]{1,0:T(8,128)(2,1)S(1)} %get-tuple-element.52), channel_id=1, source_target_pairs={{0,2},{1,6},{2,0},{3,4},{4,3},{5,7},{6,1},{7,5},{8,10},{9,14},{10,... | collective-permute-start | bytes 491528 | tf_op jit(solution)/shard_map/ppermute | solution.py:22
  68.3 0.7 collective-permute-start.18
  69.0 1.3 %shard_map.85 = (f32[40,128]{1,0:T(8,128)S(1)}, f32[40,128]{1,0:T(8,128)S(1)}) custom-call(s32[34]{0:T(128)S(1)} %stack.136.table.places, f32[80,320]{1,0:T(8,128)S(1)} %get-tuple-element.47.tokens, f32[16,64]{1,0:T(8,128)S(1)} %get-tuple-element.48.asked, bf16[512,320]{1,0:T(8,128)(2,1)S(1)} %get-tuple-element.49.memory, ...), custom_call_target="tpu_custom_call" | custom-call | flops 1 | bytes 1 | tf_op jit(solution)/shard_map/pallas_call | solution.py:421
  70.3 2.4 %collective-permute-start.20 = (f32[40,128]{1,0:T(8,128)S(1)}, f32[40,128]{1,0:T(8,128)S(1)}, u32[]{:S(2)}, u32[]{:S(2)}) collective-permute-start(f32[40,128]{1,0:T(8,128)S(1)} %get-tuple-element.50), channel_id=1, source_target_pairs={{0,8},{1,9},{2,10},{3,11},{4,12},{5,13},{6,14},{7,15},{8,0},{9,1},... | collective-permute-start | bytes 61448 | tf_op jit(solution)/shard_map/ppermute | solution.py:22
  72.8 1.3 %collective-permute-done.21.refs_1_ = bf16[256,320]{1,0:T(8,128)(2,1)S(1)} collective-permute-done((bf16[256,320]{1,0:T(8,128)(2,1)S(1)}, bf16[256,320]{1,0:T(8,128)(2,1)S(1)}, u32[]{:S(2)}, u32[]{:S(2)}) %collective-permute-start.21) | collective-permute-done | bytes 163872 | tf_op jit(solution)/shard_map/ppermute | solution.py:22
  74.1 1.0 %collective-permute-done.20.refs_1_ = f32[40,128]{1,0:T(8,128)S(1)} collective-permute-done((f32[40,128]{1,0:T(8,128)S(1)}, f32[40,128]{1,0:T(8,128)S(1)}, u32[]{:S(2)}, u32[]{:S(2)}) %collective-permute-start.20) | collective-permute-done | bytes 20512 | tf_op jit(solution)/shard_map/ppermute | solution.py:22
  75.1 2.1 %collective-permute-start.22 = (bf16[256,320]{1,0:T(8,128)(2,1)S(1)}, bf16[256,320]{1,0:T(8,128)(2,1)S(1)}, u32[]{:S(2)}, u32[]{:S(2)}) collective-permute-start(bf16[256,320]{1,0:T(8,128)(2,1)S(1)} %collective-permute-done.18.refs_0_), channel_id=1, source_target_pairs={{0,1},{1,0},{2,3},{3,2},{4,5},{5,4},{6,7},{7,6},{8,9},{9,8},{10,11... | collective-permute-start | bytes 491528 | tf_op jit(solution)/shard_map/ppermute | solution.py:22
  77.2 0.0 collective-permute-start.23
  77.2 0.2 shard_map.87
  77.5 0.7 collective-permute-start.24
  78.2 2.7 %collective-permute-start.25 = (bf16[2,384]{1,0:T(2,128)(2,1)S(1)}, bf16[2,384]{1,0:T(2,128)(2,1)S(1)}, u32[]{:S(2)}, u32[]{:S(2)}) collective-permute-start(bf16[2,384]{1,0:T(2,128)(2,1)S(1)} %get-tuple-element.58), channel_id=1, source_target_pairs={{0,4},{1,5},{2,6},{3,7},{4,0},{5,1},{6,2},{7,3},{8,12},{9,13},{10,... | collective-permute-start | bytes 4616 | tf_op jit(solution)/shard_map/ppermute | solution.py:22
  80.9 0.9 %collective-permute-start.26 = (bf16[2,384]{1,0:T(2,128)(2,1)S(1)}, bf16[2,384]{1,0:T(2,128)(2,1)S(1)}, u32[]{:S(2)}, u32[]{:S(2)}) collective-permute-start(bf16[2,384]{1,0:T(2,128)(2,1)S(1)} %get-tuple-element.59), channel_id=1, source_target_pairs={{0,6},{1,7},{2,4},{3,5},{4,2},{5,3},{6,0},{7,1},{8,14},{9,15},{10,... | collective-permute-start | bytes 4616 | tf_op jit(solution)/shard_map/ppermute | solution.py:22
  81.8 1.4 %shard_map.86 = bf16[128,1280]{1,0:T(8,128)(2,1)} custom-call(s32[34]{0:T(128)S(1)} %stack.136.table.places, bf16[256,320]{1,0:T(8,128)(2,1)S(1)} %collective-permute-done.18.refs_0_, bf16[256,320]{1,0:T(8,128)(2,1)S(1)} %collective-permute-done.21.refs_1_, bf16[256,320]{1,0:T(8,128)(2,1)S(1)} %collective-permute-done.22.refs_2_, ...), custom_call_target="tpu_custom_call" | custom-call | flops 1 | bytes 1 | tf_op jit(solution)/shard_map/pallas_call | solution.py:475
  83.2 2.1 %collective-permute-done.26.refs_3_ = bf16[2,384]{1,0:T(2,128)(2,1)S(1)} collective-permute-done((bf16[2,384]{1,0:T(2,128)(2,1)S(1)}, bf16[2,384]{1,0:T(2,128)(2,1)S(1)}, u32[]{:S(2)}, u32[]{:S(2)}) %collective-permute-start.26) | collective-permute-done | bytes 1568 | tf_op jit(solution)/shard_map/ppermute | solution.py:22
  85.3 1.2 %shard_map.88 = bf16[2,1280]{1,0:T(2,128)(2,1)} custom-call(s32[34]{0:T(128)S(1)} %stack.136.table.places, bf16[2,384]{1,0:T(2,128)(2,1)S(1)} %get-tuple-element.56.refs_0_, bf16[2,384]{1,0:T(2,128)(2,1)S(1)} %collective-permute-done.24.refs_1_, bf16[2,384]{1,0:T(2,128)(2,1)S(1)} %collective-permute-done.25.refs_2_, ...), custom_call_target="tpu_custom_call" | custom-call | flops 1 | bytes 1 | tf_op jit(solution)/shard_map/pallas_call | solution.py:475
  (17 shorter events, 0.1 us)
Async XLA Ops:
  0.7 0.7 copy-start.2
  0.8 0.7 copy-start.3
  0.9 0.7 copy-start.4
  1.5 1.1 %copy-start = (bf16[80,3840]{1,0:T(8,128)(2,1)S(1)}, bf16[80,3840]{1,0:T(8,128)(2,1)}, u32[]{:S(2)}) copy-start(bf16[80,3840]{1,0:T(8,128)(2,1)} %refs_0_.1) | copy-start | bytes 1843204
  2.6 4.2 %copy-start.1 = (bf16[128,1280]{1,0:T(8,128)(2,1)S(1)}, bf16[128,1280]{1,0:T(8,128)(2,1)}, u32[]{:S(2)}) copy-start(bf16[128,1280]{1,0:T(8,128)(2,1)} %here.1) | copy-start | bytes 983044
  3.8 4.7 %collective-permute-start.4 = (bf16[2,80,1024]{2,1,0:T(8,128)(2,1)S(1)}, bf16[2,80,1024]{2,1,0:T(8,128)(2,1)S(1)}, u32[]{:S(2)}, u32[]{:S(2)}) collective-permute-start(bf16[2,80,1024]{2,1,0:T(8,128)(2,1)S(1)} %get-tuple-element.33.refs_0_.refs_7_), channel_id=1, source_target_pairs={{0,1},{1,0},{2,3},{3,2},{4,5},{5,4},{6,7},{7,6},{8,9},{9,8},{10,11... | collective-permute-start | bytes 983048 | tf_op jit(solution)/shard_map/ppermute | solution.py:22
  4.3 10.9 %collective-permute-start = (bf16[2,80,1024]{2,1,0:T(8,128)(2,1)S(1)}, bf16[2,80,1024]{2,1,0:T(8,128)(2,1)S(1)}, u32[]{:S(2)}, u32[]{:S(2)}) collective-permute-start(bf16[2,80,1024]{2,1,0:T(8,128)(2,1)S(1)} %get-tuple-element.31), channel_id=1, source_target_pairs={{0,2},{1,3},{2,0},{3,1},{4,6},{5,7},{6,4},{7,5},{8,10},{9,11},{10,... | collective-permute-start | bytes 983048 | tf_op jit(solution)/shard_map/ppermute | solution.py:22
  6.9 10.1 %collective-permute-start.3 = (bf16[128,1280]{1,0:T(8,128)(2,1)S(1)}, bf16[128,1280]{1,0:T(8,128)(2,1)S(1)}, u32[]{:S(2)}, u32[]{:S(2)}) collective-permute-start(bf16[128,1280]{1,0:T(8,128)(2,1)S(1)} %copy-done.1), channel_id=1, source_target_pairs={{0,4},{1,5},{2,6},{3,7},{4,0},{5,1},{6,2},{7,3},{8,12},{9,13},{10,... | collective-permute-start | bytes 983048 | tf_op jit(solution)/shard_map/ppermute | solution.py:22
  8.4 8.5 %collective-permute-start.5 = (bf16[128,1280]{1,0:T(8,128)(2,1)S(1)}, bf16[128,1280]{1,0:T(8,128)(2,1)S(1)}, u32[]{:S(2)}, u32[]{:S(2)}) collective-permute-start(bf16[128,1280]{1,0:T(8,128)(2,1)S(1)} %copy-done.1), channel_id=1, source_target_pairs={{4,8},{5,9},{6,10},{7,11},{8,4},{9,5},{10,6},{11,7},{20,24},{21,25... | collective-permute-start | bytes 983048 | tf_op jit(solution)/shard_map/ppermute | solution.py:22
  15.2 1.8 %collective-permute-start.6 = (bf16[2,80,1024]{2,1,0:T(8,128)(2,1)S(1)}, bf16[2,80,1024]{2,1,0:T(8,128)(2,1)S(1)}, u32[]{:S(2)}, u32[]{:S(2)}) collective-permute-start(bf16[2,80,1024]{2,1,0:T(8,128)(2,1)S(1)} %collective-permute-done.refs_2_.refs_9_), channel_id=1, source_target_pairs={{0,1},{1,0},{2,3},{3,2},{4,5},{5,4},{6,7},{7,6},{8,9},{9,8},{10,11... | collective-permute-start | bytes 983048 | tf_op jit(solution)/shard_map/ppermute | solution.py:22
  15.2 10.5 %collective-permute-start.1 = (bf16[128,1280]{1,0:T(8,128)(2,1)S(1)}, bf16[128,1280]{1,0:T(8,128)(2,1)S(1)}, u32[]{:S(2)}, u32[]{:S(2)}) collective-permute-start(bf16[128,1280]{1,0:T(8,128)(2,1)S(1)} %copy-done.1), channel_id=1, source_target_pairs={{0,2},{1,3},{2,0},{3,1},{4,6},{5,7},{6,4},{7,5},{8,10},{9,11},{10,... | collective-permute-start | bytes 983048 | tf_op jit(solution)/shard_map/ppermute | solution.py:22
  16.9 5.5 %copy-start.5 = (f32[1280]{0:T(1024)S(1)}, f32[1280]{0:T(1024)}, u32[]{:S(2)}) copy-start(f32[1280]{0:T(1024)} %param.7) | copy-start | bytes 15364
  17.5 14.8 %collective-permute-start.7 = (bf16[128,1280]{1,0:T(8,128)(2,1)S(1)}, bf16[128,1280]{1,0:T(8,128)(2,1)S(1)}, u32[]{:S(2)}, u32[]{:S(2)}) collective-permute-start(bf16[128,1280]{1,0:T(8,128)(2,1)S(1)} %collective-permute-done.3.here), channel_id=1, source_target_pairs={{0,2},{1,3},{2,0},{3,1},{4,6},{5,7},{6,4},{7,5},{8,10},{9,11},{10,... | collective-permute-start | bytes 983048 | tf_op jit(solution)/shard_map/ppermute | solution.py:22
  19.2 17.2 %collective-permute-start.9 = (bf16[128,1280]{1,0:T(8,128)(2,1)S(1)}, bf16[128,1280]{1,0:T(8,128)(2,1)}, u32[]{:S(2)}, u32[]{:S(2)}) collective-permute-start(bf16[128,1280]{1,0:T(8,128)(2,1)S(1)} %collective-permute-done.5), channel_id=1, source_target_pairs={{0,4},{1,5},{2,6},{3,7},{4,0},{5,1},{6,2},{7,3},{8,12},{9,13},{10,... | collective-permute-start | bytes 983048 | tf_op jit(solution)/shard_map/ppermute | solution.py:22
  22.4 16.6 %collective-permute-start.12 = (bf16[80,1024]{1,0:T(8,128)(2,1)S(1)}, bf16[80,1024]{1,0:T(8,128)(2,1)S(1)}, u32[]{:S(2)}, u32[]{:S(2)}) collective-permute-start(bf16[80,1024]{1,0:T(8,128)(2,1)S(1)} %get-tuple-element.39), channel_id=1, source_target_pairs={{0,4},{1,5},{2,6},{3,7},{4,0},{5,1},{6,2},{7,3},{8,12},{9,13},{10,... | collective-permute-start | bytes 491528 | tf_op jit(solution)/shard_map/ppermute | solution.py:22
  22.5 17.7 %collective-permute-start.10 = (bf16[80,1024]{1,0:T(8,128)(2,1)S(1)}, bf16[80,1024]{1,0:T(8,128)(2,1)S(1)}, u32[]{:S(2)}, u32[]{:S(2)}) collective-permute-start(bf16[80,1024]{1,0:T(8,128)(2,1)S(1)} %get-tuple-element.39), channel_id=1, source_target_pairs={{0,12},{1,13},{2,14},{3,15},{4,8},{5,9},{6,10},{7,11},{8,4},{9,5},... | collective-permute-start | bytes 491528 | tf_op jit(solution)/shard_map/ppermute | solution.py:22
  25.7 14.5 %collective-permute-start.11 = (bf16[80,1024]{1,0:T(8,128)(2,1)S(1)}, bf16[80,1024]{1,0:T(8,128)(2,1)S(1)}, u32[]{:S(2)}, u32[]{:S(2)}) collective-permute-start(bf16[80,1024]{1,0:T(8,128)(2,1)S(1)} %get-tuple-element.36.refs_0_), channel_id=1, source_target_pairs={{0,8},{1,9},{2,10},{3,11},{4,12},{5,13},{6,14},{7,15},{8,0},{9,1},... | collective-permute-start | bytes 491528 | tf_op jit(solution)/shard_map/ppermute | solution.py:22
  32.3 18.9 %collective-permute-start.2 = (bf16[256,1664]{1,0:T(8,128)(2,1)S(1)}, bf16[256,1664]{1,0:T(8,128)(2,1)S(1)}, u32[]{:S(2)}, u32[]{:S(2)}) collective-permute-start(bf16[256,1664]{1,0:T(8,128)(2,1)S(1)} %shard_map.78.refs_0_), channel_id=1, source_target_pairs={{0,1},{1,0},{2,3},{3,2},{4,5},{5,4},{6,7},{7,6},{8,9},{9,8},{10,11... | collective-permute-start | bytes 2555912 | tf_op jit(solution)/shard_map/ppermute | solution.py:22
  36.4 14.8 %collective-permute-start.8 = (bf16[256,1664]{1,0:T(8,128)(2,1)S(1)}, bf16[256,1664]{1,0:T(8,128)(2,1)S(1)}, u32[]{:S(2)}, u32[]{:S(2)}) collective-permute-start(bf16[256,1664]{1,0:T(8,128)(2,1)S(1)} %shard_map.80.refs_2_), channel_id=1, source_target_pairs={{0,1},{1,0},{2,3},{3,2},{4,5},{5,4},{6,7},{7,6},{8,9},{9,8},{10,11... | collective-permute-start | bytes 2555912 | tf_op jit(solution)/shard_map/ppermute | solution.py:22
  40.2 11.0 %collective-permute-start.14 = (bf16[240,1024]{1,0:T(8,128)(2,1)S(1)}, bf16[240,1024]{1,0:T(8,128)(2,1)S(1)}, u32[]{:S(2)}, u32[]{:S(2)}) collective-permute-start(bf16[240,1024]{1,0:T(8,128)(2,1)S(1)} %shard_map.81.refs_1_.refs_11_), channel_id=1, source_target_pairs={{0,16},{16,0},{1,17},{17,1},{2,18},{18,2},{3,19},{19,3},{4,20},{20... | collective-permute-start | bytes 1474568 | tf_op jit(solution)/shard_map/ppermute | solution.py:520
  41.8 7.2 %collective-permute-start.13 = (bf16[128,1280]{1,0:T(8,128)(2,1)S(1)}, bf16[128,1280]{1,0:T(8,128)(2,1)S(1)}, u32[]{:S(2)}, u32[]{:S(2)}) collective-permute-start(bf16[128,1280]{1,0:T(8,128)(2,1)S(1)} %broadcast_select_fusion.here), channel_id=1, source_target_pairs={{0,2},{1,3},{2,0},{3,1},{4,6},{5,7},{6,4},{7,5},{8,10},{9,11},{10,... | collective-permute-start | bytes 983048 | tf_op jit(solution)/shard_map/ppermute | solution.py:22
  43.3 7.9 %collective-permute-start.16 = (bf16[240,1024]{1,0:T(8,128)(2,1)S(1)}, bf16[240,1024]{1,0:T(8,128)(2,1)S(1)}, u32[]{:S(2)}, u32[]{:S(2)}) collective-permute-start(bf16[240,1024]{1,0:T(8,128)(2,1)S(1)} %shard_map.81.refs_1_.refs_11_), channel_id=1, source_target_pairs={{0,1},{1,0},{2,3},{3,2},{4,5},{5,4},{6,7},{7,6},{8,9},{9,8},{10,11... | collective-permute-start | bytes 1474568 | tf_op jit(solution)/shard_map/ppermute | solution.py:22
  51.2 2.1 %collective-permute-start.15 = (bf16[256,1280]{1,0:T(8,128)(2,1)S(1)}, bf16[256,1280]{1,0:T(8,128)(2,1)S(1)}, u32[]{:S(2)}, u32[]{:S(2)}) collective-permute-start(bf16[256,1280]{1,0:T(8,128)(2,1)S(1)} %shard_map.83.refs_4_), channel_id=1, source_target_pairs={{0,1},{1,0},{2,3},{3,2},{4,5},{5,4},{6,7},{7,6},{8,9},{9,8},{10,11... | collective-permute-start | bytes 1966088 | tf_op jit(solution)/shard_map/ppermute | solution.py:22
  51.3 2.8 %collective-permute-start.17 = (bf16[240,1024]{1,0:T(8,128)(2,1)S(1)}, bf16[240,1024]{1,0:T(8,128)(2,1)S(1)}, u32[]{:S(2)}, u32[]{:S(2)}) collective-permute-start(bf16[240,1024]{1,0:T(8,128)(2,1)S(1)} %collective-permute-done.14.refs_13_), channel_id=1, source_target_pairs={{0,1},{1,0},{2,3},{3,2},{4,5},{5,4},{6,7},{7,6},{8,9},{9,8},{10,11... | collective-permute-start | bytes 1474568 | tf_op jit(solution)/shard_map/ppermute | solution.py:22
  63.6 5.5 %collective-permute-start.19 = (bf16[512,320]{1,0:T(8,128)(2,1)S(1)}, bf16[512,320]{1,0:T(8,128)(2,1)S(1)}, u32[]{:S(2)}, u32[]{:S(2)}) collective-permute-start(bf16[512,320]{1,0:T(8,128)(2,1)S(1)} %get-tuple-element.49.memory), channel_id=1, source_target_pairs={{0,1},{1,0},{2,3},{3,2},{4,5},{5,4},{6,7},{7,6},{8,9},{9,8},{10,11... | collective-permute-start | bytes 983048 | tf_op jit(solution)/shard_map/ppermute | solution.py:22
  63.8 10.3 %collective-permute-start.21 = (bf16[256,320]{1,0:T(8,128)(2,1)S(1)}, bf16[256,320]{1,0:T(8,128)(2,1)S(1)}, u32[]{:S(2)}, u32[]{:S(2)}) collective-permute-start(bf16[256,320]{1,0:T(8,128)(2,1)S(1)} %get-tuple-element.52), channel_id=1, source_target_pairs={{0,2},{1,6},{2,0},{3,4},{4,3},{5,7},{6,1},{7,5},{8,10},{9,14},{10,... | collective-permute-start | bytes 491528 | tf_op jit(solution)/shard_map/ppermute | solution.py:22
  68.3 6.7 %collective-permute-start.18 = (bf16[256,320]{1,0:T(8,128)(2,1)S(1)}, bf16[256,320]{1,0:T(8,128)(2,1)S(1)}, u32[]{:S(2)}, u32[]{:S(2)}) collective-permute-start(bf16[256,320]{1,0:T(8,128)(2,1)S(1)} %get-tuple-element.46), channel_id=1, source_target_pairs={{0,0},{1,4},{2,2},{3,6},{4,1},{5,5},{6,3},{7,7},{8,8},{9,12},{10,1... | collective-permute-start | bytes 491528 | tf_op jit(solution)/shard_map/ppermute | solution.py:22
  70.3 4.7 %collective-permute-start.20 = (f32[40,128]{1,0:T(8,128)S(1)}, f32[40,128]{1,0:T(8,128)S(1)}, u32[]{:S(2)}, u32[]{:S(2)}) collective-permute-start(f32[40,128]{1,0:T(8,128)S(1)} %get-tuple-element.50), channel_id=1, source_target_pairs={{0,8},{1,9},{2,10},{3,11},{4,12},{5,13},{6,14},{7,15},{8,0},{9,1},... | collective-permute-start | bytes 61448 | tf_op jit(solution)/shard_map/ppermute | solution.py:22
  75.1 6.7 %collective-permute-start.22 = (bf16[256,320]{1,0:T(8,128)(2,1)S(1)}, bf16[256,320]{1,0:T(8,128)(2,1)S(1)}, u32[]{:S(2)}, u32[]{:S(2)}) collective-permute-start(bf16[256,320]{1,0:T(8,128)(2,1)S(1)} %collective-permute-done.18.refs_0_), channel_id=1, source_target_pairs={{0,1},{1,0},{2,3},{3,2},{4,5},{5,4},{6,7},{7,6},{8,9},{9,8},{10,11... | collective-permute-start | bytes 491528 | tf_op jit(solution)/shard_map/ppermute | solution.py:22
  77.2 4.6 %collective-permute-start.23 = (bf16[256,320]{1,0:T(8,128)(2,1)S(1)}, bf16[256,320]{1,0:T(8,128)(2,1)S(1)}, u32[]{:S(2)}, u32[]{:S(2)}) collective-permute-start(bf16[256,320]{1,0:T(8,128)(2,1)S(1)} %collective-permute-done.21.refs_1_), channel_id=1, source_target_pairs={{0,1},{1,0},{2,3},{3,2},{4,5},{5,4},{6,7},{7,6},{8,9},{9,8},{10,11... | collective-permute-start | bytes 491528 | tf_op jit(solution)/shard_map/ppermute | solution.py:22
  77.5 5.7 %collective-permute-start.24 = (bf16[2,384]{1,0:T(2,128)(2,1)S(1)}, bf16[2,384]{1,0:T(2,128)(2,1)S(1)}, u32[]{:S(2)}, u32[]{:S(2)}) collective-permute-start(bf16[2,384]{1,0:T(2,128)(2,1)S(1)} %get-tuple-element.57), channel_id=1, source_target_pairs={{0,2},{1,3},{2,0},{3,1},{4,6},{5,7},{6,4},{7,5},{8,10},{9,11},{10,... | collective-permute-start | bytes 4616 | tf_op jit(solution)/shard_map/ppermute | solution.py:22
  78.2 5.0 %collective-permute-start.25 = (bf16[2,384]{1,0:T(2,128)(2,1)S(1)}, bf16[2,384]{1,0:T(2,128)(2,1)S(1)}, u32[]{:S(2)}, u32[]{:S(2)}) collective-permute-start(bf16[2,384]{1,0:T(2,128)(2,1)S(1)} %get-tuple-element.58), channel_id=1, source_target_pairs={{0,4},{1,5},{2,6},{3,7},{4,0},{5,1},{6,2},{7,3},{8,12},{9,13},{10,... | collective-permute-start | bytes 4616 | tf_op jit(solution)/shard_map/ppermute | solution.py:22
  80.9 4.5 %collective-permute-start.26 = (bf16[2,384]{1,0:T(2,128)(2,1)S(1)}, bf16[2,384]{1,0:T(2,128)(2,1)S(1)}, u32[]{:S(2)}, u32[]{:S(2)}) collective-permute-start(bf16[2,384]{1,0:T(2,128)(2,1)S(1)} %get-tuple-element.59), channel_id=1, source_target_pairs={{0,6},{1,7},{2,4},{3,5},{4,2},{5,3},{6,0},{7,1},{8,14},{9,15},{10,... | collective-permute-start | bytes 4616 | tf_op jit(solution)/shard_map/ppermute | solution.py:22

commit v16 on v13

--- a/solution.py
+++ b/solution.py
@@ -578,7 +578,7 @@
     owned = [partial[0]] + [swap(partial[i], n, 8 * i) for i in range(1, n // 8)]
 
     got = []
-    for turn, rows in enumerate((stay, leave)):
+    for turn, rows in enumerate((after(stay, partial[0]), leave)):
         route = [
             (
                 8 * (d // 8) + 4 * (d // 4 % 2) + (d & 2) + (d & 1),

time: 85 us -> 86.3 us (1.015)
  starting transfers between devices: 25.9 us -> 26.8 us
    ppermute x26, starting transfers between devices: 24.3 us -> 25.2 us  [send(): return lax.ppermute(block, 'tm', route)]
where the time goes in v16:
time: 86.3 us; the launch traced here: 86.1 us
  waiting for transfers between devices  32.7 us (38%)
  starting transfers between devices  26.8 us (31%)
  Pallas kernels  22.8 us (26%)
  local copies, waits for them, and re-layouts  1.87 us (2%)
  other arithmetic  1.02 us (1%)
  between operations  0.91 us (1%)
    ppermute x26, waiting for transfers between devices, send(): return lax.ppermute(block, 'tm', route)  32.7 us
    ppermute x26, starting transfers between devices, send(): return lax.ppermute(block, 'tm', route)  25.2 us
    pallas_call x1, Pallas kernels, encoder(): pl.pallas_call(functools.partial(encoder_kernel, len(parts), depth), out_...  12.6 us
    pallas_call x3, Pallas kernels, norm_half(): pl.pallas_call(norm_kernel, out_shape=jax.ShapeDtypeStruct((256, 1664 if...  2.93 us
    pallas_call x2, Pallas kernels, gather_groups(): pl.pallas_call(functools.partial(gather_kernel, side, rows), out_shape=ja...  2.59 us
    unnamed x12, local copies, waits for them, and re-layouts  1.75 us
  transfers between devices with their start and end apart: 27, of which 13 were waited for; matrix products, arithmetic and copies ran while one was open for 1% of the time, Pallas kernels for 9%

profile of v16, /device:TPU:0, one launch (start us, length us, event | category | flops | bytes accessed | tf_op | source)
XLA Modules:
  0.0 86.1 jit_solution(7119234580715570254)
XLA Ops:
  0.7 0.0 copy-start.2
  0.7 0.1 stack.136.table.places
  0.8 0.0 copy-start.3
  0.9 0.0 copy-start.4
  0.9 0.5 copy-done.2
  1.4 0.1 copy-done.3
  1.5 1.1 %copy-done = bf16[80,3840]{1,0:T(8,128)(2,1)S(1)} copy-done((bf16[80,3840]{1,0:T(8,128)(2,1)S(1)}, bf16[80,3840]{1,0:T(8,128)(2,1)}, u32[]{:S(2)}) %copy-start) | copy-done | bytes 614424
  2.6 1.1 %shard_map.77 = (bf16[2,80,1024]{2,1,0:T(8,128)(2,1)S(1)}, bf16[2,80,1024]{2,1,0:T(8,128)(2,1)S(1)}) custom-call(s32[34]{0:T(128)S(1)} %stack.136.table.places, bf16[80,3840]{1,0:T(8,128)(2,1)S(1)} %copy-done, bf16[2,1280]{1,0:T(2,128)(2,1)S(1)} %copy-done.2, s32[2,16]{1,0:T(2,128)S(1)} %copy-done.3, s32[1,128]{1,0:T(1,128)S(1)} %bitcast.33), custom_call_target="tpu_custom_call" | custom-call | flops 1 | bytes 1 | tf_op jit(solution)/shard_map/pallas_call | solution.py:98
  3.8 3.0 %collective-permute-start = (bf16[2,80,1024]{2,1,0:T(8,128)(2,1)S(1)}, bf16[2,80,1024]{2,1,0:T(8,128)(2,1)S(1)}, u32[]{:S(2)}, u32[]{:S(2)}) collective-permute-start(bf16[2,80,1024]{2,1,0:T(8,128)(2,1)S(1)} %get-tuple-element.31), channel_id=1, source_target_pairs={{0,2},{1,3},{2,0},{3,1},{4,6},{5,7},{6,4},{7,5},{8,10},{9,11},{10,... | collective-permute-start | bytes 983048 | tf_op jit(solution)/shard_map/ppermute | solution.py:22
  6.8 0.7 collective-permute-start.5
  7.5 4.4 %collective-permute-start.3 = (bf16[128,1280]{1,0:T(8,128)(2,1)S(1)}, bf16[128,1280]{1,0:T(8,128)(2,1)S(1)}, u32[]{:S(2)}, u32[]{:S(2)}) collective-permute-start(bf16[128,1280]{1,0:T(8,128)(2,1)S(1)} %copy-done.1), channel_id=1, source_target_pairs={{0,4},{1,5},{2,6},{3,7},{4,0},{5,1},{6,2},{7,3},{8,12},{9,13},{10,... | collective-permute-start | bytes 983048 | tf_op jit(solution)/shard_map/ppermute | solution.py:22
  11.9 0.0 collective-permute-start.4
  11.9 2.6 %collective-permute-done.refs_2_.refs_9_ = bf16[2,80,1024]{2,1,0:T(8,128)(2,1)S(1)} collective-permute-done((bf16[2,80,1024]{2,1,0:T(8,128)(2,1)S(1)}, bf16[2,80,1024]{2,1,0:T(8,128)(2,1)S(1)}, u32[]{:S(2)}, u32[]{:S(2)}) %collective-permute-start) | collective-permute-done | bytes 327712 | tf_op jit(solution)/shard_map/ppermute | solution.py:22
  14.5 0.0 collective-permute-start.6
  14.5 0.0 collective-permute-done.5
  14.5 4.6 %collective-permute-done.3.here = bf16[128,1280]{1,0:T(8,128)(2,1)S(1)} collective-permute-done((bf16[128,1280]{1,0:T(8,128)(2,1)S(1)}, bf16[128,1280]{1,0:T(8,128)(2,1)S(1)}, u32[]{:S(2)}, u32[]{:S(2)}) %collective-permute-start.3) | collective-permute-done | bytes 327712 | tf_op jit(solution)/shard_map/ppermute | solution.py:22
  19.0 0.5 collective-permute-start.1
  19.6 0.6 shard_map.79
  20.2 1.6 %collective-permute-start.7 = (bf16[128,1280]{1,0:T(8,128)(2,1)S(1)}, bf16[128,1280]{1,0:T(8,128)(2,1)S(1)}, u32[]{:S(2)}, u32[]{:S(2)}) collective-permute-start(bf16[128,1280]{1,0:T(8,128)(2,1)S(1)} %collective-permute-done.3.here), channel_id=1, source_target_pairs={{0,2},{1,3},{2,0},{3,1},{4,6},{5,7},{6,4},{7,5},{8,10},{9,11},{10,... | collective-permute-start | bytes 983048 | tf_op jit(solution)/shard_map/ppermute | solution.py:22
  21.7 1.7 %collective-permute-start.9 = (bf16[128,1280]{1,0:T(8,128)(2,1)S(1)}, bf16[128,1280]{1,0:T(8,128)(2,1)}, u32[]{:S(2)}, u32[]{:S(2)}) collective-permute-start(bf16[128,1280]{1,0:T(8,128)(2,1)S(1)} %collective-permute-done.5), channel_id=1, source_target_pairs={{0,4},{1,5},{2,6},{3,7},{4,0},{5,1},{6,2},{7,3},{8,12},{9,13},{10,... | collective-permute-start | bytes 983048 | tf_op jit(solution)/shard_map/ppermute | solution.py:22
  23.5 0.3 collective-permute-start.12
  23.8 1.4 %collective-permute-start.10 = (bf16[80,1024]{1,0:T(8,128)(2,1)S(1)}, bf16[80,1024]{1,0:T(8,128)(2,1)S(1)}, u32[]{:S(2)}, u32[]{:S(2)}) collective-permute-start(bf16[80,1024]{1,0:T(8,128)(2,1)S(1)} %get-tuple-element.38), channel_id=1, source_target_pairs={{0,12},{1,13},{2,14},{3,15},{4,8},{5,9},{6,10},{7,11},{8,4},{9,5},... | collective-permute-start | bytes 491528 | tf_op jit(solution)/shard_map/ppermute | solution.py:22
  25.1 4.5 %collective-permute-done.1.across = bf16[128,1280]{1,0:T(8,128)(2,1)S(1)} collective-permute-done((bf16[128,1280]{1,0:T(8,128)(2,1)S(1)}, bf16[128,1280]{1,0:T(8,128)(2,1)S(1)}, u32[]{:S(2)}, u32[]{:S(2)}) %collective-permute-start.1) | collective-permute-done | bytes 327712 | tf_op jit(solution)/shard_map/ppermute | solution.py:22
  29.7 1.6 %collective-permute-start.11 = (bf16[80,1024]{1,0:T(8,128)(2,1)S(1)}, bf16[80,1024]{1,0:T(8,128)(2,1)S(1)}, u32[]{:S(2)}, u32[]{:S(2)}) collective-permute-start(bf16[80,1024]{1,0:T(8,128)(2,1)S(1)} %get-tuple-element.35.refs_0_), channel_id=1, source_target_pairs={{0,8},{1,9},{2,10},{3,11},{4,12},{5,13},{6,14},{7,15},{8,0},{9,1},... | collective-permute-start | bytes 491528 | tf_op jit(solution)/shard_map/ppermute | solution.py:22
  31.3 1.0 %shard_map.78.refs_0_ = bf16[256,1664]{1,0:T(8,128)(2,1)S(1)} custom-call(s32[34]{0:T(128)S(1)} %stack.136.table.places, f32[1,1280]{1,0:T(1,128)S(1)} %reshape.10.gain, bf16[128,1280]{1,0:T(8,128)(2,1)S(1)} %copy-done.1, bf16[128,1280]{1,0:T(8,128)(2,1)S(1)} %collective-permute-done.1.across), custom_call_target="tpu_custom_call" | custom-call | flops 1 | bytes 1 | tf_op jit(solution)/shard_map/pallas_call | solution.py:162
  32.3 2.0 %collective-permute-done.7.across = bf16[128,1280]{1,0:T(8,128)(2,1)S(1)} collective-permute-done((bf16[128,1280]{1,0:T(8,128)(2,1)S(1)}, bf16[128,1280]{1,0:T(8,128)(2,1)S(1)}, u32[]{:S(2)}, u32[]{:S(2)}) %collective-permute-start.7) | collective-permute-done | bytes 327712 | tf_op jit(solution)/shard_map/ppermute | solution.py:22
  34.3 1.0 %shard_map.80.refs_2_ = bf16[256,1664]{1,0:T(8,128)(2,1)S(1)} custom-call(s32[34]{0:T(128)S(1)} %stack.136.table.places, f32[1,1280]{1,0:T(1,128)S(1)} %reshape.10.gain, bf16[128,1280]{1,0:T(8,128)(2,1)S(1)} %collective-permute-done.3.here, bf16[128,1280]{1,0:T(8,128)(2,1)S(1)} %collective-permute-done.7.across), custom_call_target="tpu_custom_call" | custom-call | flops 1 | bytes 1 | tf_op jit(solution)/shard_map/pallas_call | solution.py:162
  35.3 0.0 collective-permute-done.9
  35.4 0.5 collective-permute-start.8
  35.9 1.0 %broadcast_select_fusion.here = bf16[128,1280]{1,0:T(8,128)(2,1)S(1)} fusion(bf16[128,1280]{1,0:T(8,128)(2,1)S(1)} %collective-permute-done.5, bf16[128,1280]{1,0:T(8,128)(2,1)} %collective-permute-done.9, pred[]{:T(512)S(6)} %or.3), kind=kLoop, calls=%fused_computation | loop fusion | flops 163840 | bytes 983041 | tf_op jit(solution)/shard_map/jit(_where)/select_n | solution.py:532
  36.9 2.8 %collective-permute-done.12.refs_0_ = bf16[80,1024]{1,0:T(8,128)(2,1)S(1)} collective-permute-done((bf16[80,1024]{1,0:T(8,128)(2,1)S(1)}, bf16[80,1024]{1,0:T(8,128)(2,1)S(1)}, u32[]{:S(2)}, u32[]{:S(2)}) %collective-permute-start.12) | collective-permute-done | bytes 163872 | tf_op jit(solution)/shard_map/ppermute | solution.py:22
  39.7 1.4 %collective-permute-done.11.refs_1_ = bf16[80,1024]{1,0:T(8,128)(2,1)S(1)} collective-permute-done((bf16[80,1024]{1,0:T(8,128)(2,1)S(1)}, bf16[80,1024]{1,0:T(8,128)(2,1)S(1)}, u32[]{:S(2)}, u32[]{:S(2)}) %collective-permute-start.11) | collective-permute-done | bytes 163872 | tf_op jit(solution)/shard_map/ppermute | solution.py:22
  41.2 1.6 %collective-permute-start.14 = (bf16[240,1024]{1,0:T(8,128)(2,1)S(1)}, bf16[240,1024]{1,0:T(8,128)(2,1)S(1)}, u32[]{:S(2)}, u32[]{:S(2)}) collective-permute-start(bf16[240,1024]{1,0:T(8,128)(2,1)S(1)} %shard_map.81.refs_1_.refs_11_), channel_id=1, source_target_pairs={{0,16},{16,0},{1,17},{17,1},{2,18},{18,2},{3,19},{19,3},{4,20},{20... | collective-permute-start | bytes 1474568 | tf_op jit(solution)/shard_map/ppermute | solution.py:520
  42.8 0.5 collective-permute-start.13
  43.3 1.3 %shard_map.82 = (f32[8,1536]{1,0:T(8,128)S(1)}, f32[80,320]{1,0:T(8,128)S(1)}, f32[16,64]{1,0:T(8,128)S(1)}) custom-call(s32[34]{0:T(128)S(1)} %stack.136.table.places, bf16[80,1024]{1,0:T(8,128)(2,1)S(1)} %get-tuple-element.35.refs_0_, bf16[240,1024]{1,0:T(8,128)(2,1)S(1)} %shard_map.81.refs_1_.refs_11_), custom_call_target="tpu_custom_call" | custom-call | flops 1 | bytes 1 | tf_op jit(solution)/shard_map/pallas_call | solution.py:208
  44.6 5.2 %collective-permute-done.13.across = bf16[128,1280]{1,0:T(8,128)(2,1)S(1)} collective-permute-done((bf16[128,1280]{1,0:T(8,128)(2,1)S(1)}, bf16[128,1280]{1,0:T(8,128)(2,1)S(1)}, u32[]{:S(2)}, u32[]{:S(2)}) %collective-permute-start.13) | collective-permute-done | bytes 327712 | tf_op jit(solution)/shard_map/ppermute | solution.py:22
  49.8 1.0 %shard_map.83.refs_4_ = bf16[256,1280]{1,0:T(8,128)(2,1)S(1)} custom-call(s32[34]{0:T(128)S(1)} %stack.136.table.places, f32[1,1280]{1,0:T(1,128)S(1)} %reshape.10.gain, bf16[128,1280]{1,0:T(8,128)(2,1)S(1)} %broadcast_select_fusion.here, bf16[128,1280]{1,0:T(8,128)(2,1)S(1)} %collective-permute-done.13.across), custom_call_target="tpu_custom_call" | custom-call | flops 1 | bytes 1 | tf_op jit(solution)/shard_map/pallas_call | solution.py:162
  50.8 0.0 collective-permute-done.14.refs_13_
  50.8 0.1 collective-permute-start.15
  50.9 0.0 collective-permute-done.2.refs_1_
  50.9 0.0 collective-permute-done.8.refs_3_
  50.9 0.5 collective-permute-start.17
  51.5 1.5 %collective-permute-done.15.refs_5_ = bf16[256,1280]{1,0:T(8,128)(2,1)S(1)} collective-permute-done((bf16[256,1280]{1,0:T(8,128)(2,1)S(1)}, bf16[256,1280]{1,0:T(8,128)(2,1)S(1)}, u32[]{:S(2)}, u32[]{:S(2)}) %collective-permute-start.15) | collective-permute-done | bytes 655392 | tf_op jit(solution)/shard_map/ppermute | solution.py:22
  53.0 0.7 collective-permute-done.17.refs_14_
  53.7 12.6 %shard_map.84 = (bf16[512,320]{1,0:T(8,128)(2,1)S(1)}, bf16[256,320]{1,0:T(8,128)(2,1)S(1)}, bf16[256,320]{1,0:T(8,128)(2,1)S(1)}) custom-call(s32[34]{0:T(128)S(1)} %stack.136.table.places, bf16[256,1664]{1,0:T(8,128)(2,1)S(1)} %shard_map.78.refs_0_, bf16[256,1664]{1,0:T(8,128)(2,1)S(1)} %collective-permute-done.2.refs_1_, ...), custom_call_target="tpu_custom_call" | custom-call | flops 1 | bytes 1 | tf_op jit(solution)/shard_map/pallas_call | solution.py:355
  66.3 0.2 collective-permute-start.18
  66.5 0.5 collective-permute-start.21
  67.0 1.0 %collective-permute-done.18.beside = bf16[512,320]{1,0:T(8,128)(2,1)S(1)} collective-permute-done((bf16[512,320]{1,0:T(8,128)(2,1)S(1)}, bf16[512,320]{1,0:T(8,128)(2,1)S(1)}, u32[]{:S(2)}, u32[]{:S(2)}) %collective-permute-start.18) | collective-permute-done | bytes 327712 | tf_op jit(solution)/shard_map/ppermute | solution.py:22
  68.1 1.3 %shard_map.85 = (f32[40,128]{1,0:T(8,128)S(1)}, f32[40,128]{1,0:T(8,128)S(1)}) custom-call(s32[34]{0:T(128)S(1)} %stack.136.table.places, f32[80,320]{1,0:T(8,128)S(1)} %get-tuple-element.46.tokens, f32[16,64]{1,0:T(8,128)S(1)} %get-tuple-element.47.asked, bf16[512,320]{1,0:T(8,128)(2,1)S(1)} %get-tuple-element.48.memory, ...), custom_call_target="tpu_custom_call" | custom-call | flops 1 | bytes 1 | tf_op jit(solution)/shard_map/pallas_call | solution.py:421
  69.4 0.7 collective-permute-start.19
  70.1 1.3 %collective-permute-start.20 = (f32[40,128]{1,0:T(8,128)S(1)}, f32[40,128]{1,0:T(8,128)S(1)}, u32[]{:S(2)}, u32[]{:S(2)}) collective-permute-start(f32[40,128]{1,0:T(8,128)S(1)} %get-tuple-element.51), channel_id=1, source_target_pairs={{0,8},{1,9},{2,10},{3,11},{4,12},{5,13},{6,14},{7,15},{8,0},{9,1},... | collective-permute-start | bytes 61448 | tf_op jit(solution)/shard_map/ppermute | solution.py:22
  71.4 2.9 %collective-permute-done.21.refs_1_ = bf16[256,320]{1,0:T(8,128)(2,1)S(1)} collective-permute-done((bf16[256,320]{1,0:T(8,128)(2,1)S(1)}, bf16[256,320]{1,0:T(8,128)(2,1)S(1)}, u32[]{:S(2)}, u32[]{:S(2)}) %collective-permute-start.21) | collective-permute-done | bytes 163872 | tf_op jit(solution)/shard_map/ppermute | solution.py:22
  74.3 0.7 collective-permute-done.20.refs_1_
  74.9 0.6 collective-permute-start.23
  75.6 0.0 collective-permute-done.19.refs_0_
  75.6 1.4 %collective-permute-start.22 = (bf16[256,320]{1,0:T(8,128)(2,1)S(1)}, bf16[256,320]{1,0:T(8,128)(2,1)S(1)}, u32[]{:S(2)}, u32[]{:S(2)}) collective-permute-start(bf16[256,320]{1,0:T(8,128)(2,1)S(1)} %collective-permute-done.19.refs_0_), channel_id=1, source_target_pairs={{0,1},{1,0},{2,3},{3,2},{4,5},{5,4},{6,7},{7,6},{8,9},{9,8},{10,11... | collective-permute-start | bytes 491528 | tf_op jit(solution)/shard_map/ppermute | solution.py:22
  77.0 0.2 shard_map.87
  77.2 0.6 collective-permute-start.24
  77.8 2.6 %collective-permute-start.25 = (bf16[2,384]{1,0:T(2,128)(2,1)S(1)}, bf16[2,384]{1,0:T(2,128)(2,1)S(1)}, u32[]{:S(2)}, u32[]{:S(2)}) collective-permute-start(bf16[2,384]{1,0:T(2,128)(2,1)S(1)} %get-tuple-element.58), channel_id=1, source_target_pairs={{0,4},{1,5},{2,6},{3,7},{4,0},{5,1},{6,2},{7,3},{8,12},{9,13},{10,... | collective-permute-start | bytes 4616 | tf_op jit(solution)/shard_map/ppermute | solution.py:22
  80.4 0.4 collective-permute-start.26
  80.8 0.0 collective-permute-done.23.refs_3_
  80.8 1.4 %shard_map.86 = bf16[128,1280]{1,0:T(8,128)(2,1)} custom-call(s32[34]{0:T(128)S(1)} %stack.136.table.places, bf16[256,320]{1,0:T(8,128)(2,1)S(1)} %collective-permute-done.19.refs_0_, bf16[256,320]{1,0:T(8,128)(2,1)S(1)} %collective-permute-done.21.refs_1_, bf16[256,320]{1,0:T(8,128)(2,1)S(1)} %collective-permute-done.22.refs_2_, ...), custom_call_target="tpu_custom_call" | custom-call | flops 1 | bytes 1 | tf_op jit(solution)/shard_map/pallas_call | solution.py:475
  82.2 2.7 %collective-permute-done.26.refs_3_ = bf16[2,384]{1,0:T(2,128)(2,1)S(1)} collective-permute-done((bf16[2,384]{1,0:T(2,128)(2,1)S(1)}, bf16[2,384]{1,0:T(2,128)(2,1)S(1)}, u32[]{:S(2)}, u32[]{:S(2)}) %collective-permute-start.26) | collective-permute-done | bytes 1568 | tf_op jit(solution)/shard_map/ppermute | solution.py:22
  84.9 1.2 %shard_map.88 = bf16[2,1280]{1,0:T(2,128)(2,1)} custom-call(s32[34]{0:T(128)S(1)} %stack.136.table.places, bf16[2,384]{1,0:T(2,128)(2,1)S(1)} %get-tuple-element.56.refs_0_, bf16[2,384]{1,0:T(2,128)(2,1)S(1)} %collective-permute-done.24.refs_1_, bf16[2,384]{1,0:T(2,128)(2,1)S(1)} %collective-permute-done.25.refs_2_, ...), custom_call_target="tpu_custom_call" | custom-call | flops 1 | bytes 1 | tf_op jit(solution)/shard_map/pallas_call | solution.py:475
  (17 shorter events, 0.1 us)
Async XLA Ops:
  0.7 0.7 copy-start.2
  0.8 0.7 copy-start.3
  0.9 0.7 copy-start.4
  1.5 1.1 %copy-start = (bf16[80,3840]{1,0:T(8,128)(2,1)S(1)}, bf16[80,3840]{1,0:T(8,128)(2,1)}, u32[]{:S(2)}) copy-start(bf16[80,3840]{1,0:T(8,128)(2,1)} %refs_0_.1) | copy-start | bytes 1843204
  2.6 4.2 %copy-start.1 = (bf16[128,1280]{1,0:T(8,128)(2,1)S(1)}, bf16[128,1280]{1,0:T(8,128)(2,1)}, u32[]{:S(2)}) copy-start(bf16[128,1280]{1,0:T(8,128)(2,1)} %here.1) | copy-start | bytes 983044
  3.8 10.7 %collective-permute-start = (bf16[2,80,1024]{2,1,0:T(8,128)(2,1)S(1)}, bf16[2,80,1024]{2,1,0:T(8,128)(2,1)S(1)}, u32[]{:S(2)}, u32[]{:S(2)}) collective-permute-start(bf16[2,80,1024]{2,1,0:T(8,128)(2,1)S(1)} %get-tuple-element.31), channel_id=1, source_target_pairs={{0,2},{1,3},{2,0},{3,1},{4,6},{5,7},{6,4},{7,5},{8,10},{9,11},{10,... | collective-permute-start | bytes 983048 | tf_op jit(solution)/shard_map/ppermute | solution.py:22
  6.8 7.7 %collective-permute-start.5 = (bf16[128,1280]{1,0:T(8,128)(2,1)S(1)}, bf16[128,1280]{1,0:T(8,128)(2,1)S(1)}, u32[]{:S(2)}, u32[]{:S(2)}) collective-permute-start(bf16[128,1280]{1,0:T(8,128)(2,1)S(1)} %copy-done.1), channel_id=1, source_target_pairs={{4,8},{5,9},{6,10},{7,11},{8,4},{9,5},{10,6},{11,7},{20,24},{21,25... | collective-permute-start | bytes 983048 | tf_op jit(solution)/shard_map/ppermute | solution.py:22
  7.5 11.6 %collective-permute-start.3 = (bf16[128,1280]{1,0:T(8,128)(2,1)S(1)}, bf16[128,1280]{1,0:T(8,128)(2,1)S(1)}, u32[]{:S(2)}, u32[]{:S(2)}) collective-permute-start(bf16[128,1280]{1,0:T(8,128)(2,1)S(1)} %copy-done.1), channel_id=1, source_target_pairs={{0,4},{1,5},{2,6},{3,7},{4,0},{5,1},{6,2},{7,3},{8,12},{9,13},{10,... | collective-permute-start | bytes 983048 | tf_op jit(solution)/shard_map/ppermute | solution.py:22
  11.9 7.7 %collective-permute-start.4 = (bf16[2,80,1024]{2,1,0:T(8,128)(2,1)S(1)}, bf16[2,80,1024]{2,1,0:T(8,128)(2,1)S(1)}, u32[]{:S(2)}, u32[]{:S(2)}) collective-permute-start(bf16[2,80,1024]{2,1,0:T(8,128)(2,1)S(1)} %get-tuple-element.33.refs_0_.refs_7_), channel_id=1, source_target_pairs={{0,1},{1,0},{2,3},{3,2},{4,5},{5,4},{6,7},{7,6},{8,9},{9,8},{10,11... | collective-permute-start | bytes 983048 | tf_op jit(solution)/shard_map/ppermute | solution.py:22
  14.5 5.1 %collective-permute-start.6 = (bf16[2,80,1024]{2,1,0:T(8,128)(2,1)S(1)}, bf16[2,80,1024]{2,1,0:T(8,128)(2,1)S(1)}, u32[]{:S(2)}, u32[]{:S(2)}) collective-permute-start(bf16[2,80,1024]{2,1,0:T(8,128)(2,1)S(1)} %collective-permute-done.refs_2_.refs_9_), channel_id=1, source_target_pairs={{0,1},{1,0},{2,3},{3,2},{4,5},{5,4},{6,7},{7,6},{8,9},{9,8},{10,11... | collective-permute-start | bytes 983048 | tf_op jit(solution)/shard_map/ppermute | solution.py:22
  19.0 10.6 %collective-permute-start.1 = (bf16[128,1280]{1,0:T(8,128)(2,1)S(1)}, bf16[128,1280]{1,0:T(8,128)(2,1)S(1)}, u32[]{:S(2)}, u32[]{:S(2)}) collective-permute-start(bf16[128,1280]{1,0:T(8,128)(2,1)S(1)} %copy-done.1), channel_id=1, source_target_pairs={{0,2},{1,3},{2,0},{3,1},{4,6},{5,7},{6,4},{7,5},{8,10},{9,11},{10,... | collective-permute-start | bytes 983048 | tf_op jit(solution)/shard_map/ppermute | solution.py:22
  19.6 3.9 %copy-start.5 = (f32[1280]{0:T(1024)S(1)}, f32[1280]{0:T(1024)}, u32[]{:S(2)}) copy-start(f32[1280]{0:T(1024)} %param.7) | copy-start | bytes 15364
  20.2 14.1 %collective-permute-start.7 = (bf16[128,1280]{1,0:T(8,128)(2,1)S(1)}, bf16[128,1280]{1,0:T(8,128)(2,1)S(1)}, u32[]{:S(2)}, u32[]{:S(2)}) collective-permute-start(bf16[128,1280]{1,0:T(8,128)(2,1)S(1)} %collective-permute-done.3.here), channel_id=1, source_target_pairs={{0,2},{1,3},{2,0},{3,1},{4,6},{5,7},{6,4},{7,5},{8,10},{9,11},{10,... | collective-permute-start | bytes 983048 | tf_op jit(solution)/shard_map/ppermute | solution.py:22
  21.7 13.6 %collective-permute-start.9 = (bf16[128,1280]{1,0:T(8,128)(2,1)S(1)}, bf16[128,1280]{1,0:T(8,128)(2,1)}, u32[]{:S(2)}, u32[]{:S(2)}) collective-permute-start(bf16[128,1280]{1,0:T(8,128)(2,1)S(1)} %collective-permute-done.5), channel_id=1, source_target_pairs={{0,4},{1,5},{2,6},{3,7},{4,0},{5,1},{6,2},{7,3},{8,12},{9,13},{10,... | collective-permute-start | bytes 983048 | tf_op jit(solution)/shard_map/ppermute | solution.py:22
  23.5 16.2 %collective-permute-start.12 = (bf16[80,1024]{1,0:T(8,128)(2,1)S(1)}, bf16[80,1024]{1,0:T(8,128)(2,1)S(1)}, u32[]{:S(2)}, u32[]{:S(2)}) collective-permute-start(bf16[80,1024]{1,0:T(8,128)(2,1)S(1)} %get-tuple-element.38), channel_id=1, source_target_pairs={{0,4},{1,5},{2,6},{3,7},{4,0},{5,1},{6,2},{7,3},{8,12},{9,13},{10,... | collective-permute-start | bytes 491528 | tf_op jit(solution)/shard_map/ppermute | solution.py:22
  23.8 16.0 %collective-permute-start.10 = (bf16[80,1024]{1,0:T(8,128)(2,1)S(1)}, bf16[80,1024]{1,0:T(8,128)(2,1)S(1)}, u32[]{:S(2)}, u32[]{:S(2)}) collective-permute-start(bf16[80,1024]{1,0:T(8,128)(2,1)S(1)} %get-tuple-element.38), channel_id=1, source_target_pairs={{0,12},{1,13},{2,14},{3,15},{4,8},{5,9},{6,10},{7,11},{8,4},{9,5},... | collective-permute-start | bytes 491528 | tf_op jit(solution)/shard_map/ppermute | solution.py:22
  29.7 11.4 %collective-permute-start.11 = (bf16[80,1024]{1,0:T(8,128)(2,1)S(1)}, bf16[80,1024]{1,0:T(8,128)(2,1)S(1)}, u32[]{:S(2)}, u32[]{:S(2)}) collective-permute-start(bf16[80,1024]{1,0:T(8,128)(2,1)S(1)} %get-tuple-element.35.refs_0_), channel_id=1, source_target_pairs={{0,8},{1,9},{2,10},{3,11},{4,12},{5,13},{6,14},{7,15},{8,0},{9,1},... | collective-permute-start | bytes 491528 | tf_op jit(solution)/shard_map/ppermute | solution.py:22
  34.3 16.6 %collective-permute-start.2 = (bf16[256,1664]{1,0:T(8,128)(2,1)S(1)}, bf16[256,1664]{1,0:T(8,128)(2,1)S(1)}, u32[]{:S(2)}, u32[]{:S(2)}) collective-permute-start(bf16[256,1664]{1,0:T(8,128)(2,1)S(1)} %shard_map.78.refs_0_), channel_id=1, source_target_pairs={{0,1},{1,0},{2,3},{3,2},{4,5},{5,4},{6,7},{7,6},{8,9},{9,8},{10,11... | collective-permute-start | bytes 2555912 | tf_op jit(solution)/shard_map/ppermute | solution.py:22
  35.4 15.5 %collective-permute-start.8 = (bf16[256,1664]{1,0:T(8,128)(2,1)S(1)}, bf16[256,1664]{1,0:T(8,128)(2,1)S(1)}, u32[]{:S(2)}, u32[]{:S(2)}) collective-permute-start(bf16[256,1664]{1,0:T(8,128)(2,1)S(1)} %shard_map.80.refs_2_), channel_id=1, source_target_pairs={{0,1},{1,0},{2,3},{3,2},{4,5},{5,4},{6,7},{7,6},{8,9},{9,8},{10,11... | collective-permute-start | bytes 2555912 | tf_op jit(solution)/shard_map/ppermute | solution.py:22
  41.2 9.6 %collective-permute-start.14 = (bf16[240,1024]{1,0:T(8,128)(2,1)S(1)}, bf16[240,1024]{1,0:T(8,128)(2,1)S(1)}, u32[]{:S(2)}, u32[]{:S(2)}) collective-permute-start(bf16[240,1024]{1,0:T(8,128)(2,1)S(1)} %shard_map.81.refs_1_.refs_11_), channel_id=1, source_target_pairs={{0,16},{16,0},{1,17},{17,1},{2,18},{18,2},{3,19},{19,3},{4,20},{20... | collective-permute-start | bytes 1474568 | tf_op jit(solution)/shard_map/ppermute | solution.py:520
  42.8 7.1 %collective-permute-start.13 = (bf16[128,1280]{1,0:T(8,128)(2,1)S(1)}, bf16[128,1280]{1,0:T(8,128)(2,1)S(1)}, u32[]{:S(2)}, u32[]{:S(2)}) collective-permute-start(bf16[128,1280]{1,0:T(8,128)(2,1)S(1)} %broadcast_select_fusion.here), channel_id=1, source_target_pairs={{0,2},{1,3},{2,0},{3,1},{4,6},{5,7},{6,4},{7,5},{8,10},{9,11},{10,... | collective-permute-start | bytes 983048 | tf_op jit(solution)/shard_map/ppermute | solution.py:22
  43.3 7.6 %collective-permute-start.16 = (bf16[240,1024]{1,0:T(8,128)(2,1)S(1)}, bf16[240,1024]{1,0:T(8,128)(2,1)S(1)}, u32[]{:S(2)}, u32[]{:S(2)}) collective-permute-start(bf16[240,1024]{1,0:T(8,128)(2,1)S(1)} %shard_map.81.refs_1_.refs_11_), channel_id=1, source_target_pairs={{0,1},{1,0},{2,3},{3,2},{4,5},{5,4},{6,7},{7,6},{8,9},{9,8},{10,11... | collective-permute-start | bytes 1474568 | tf_op jit(solution)/shard_map/ppermute | solution.py:22
  50.8 2.2 %collective-permute-start.15 = (bf16[256,1280]{1,0:T(8,128)(2,1)S(1)}, bf16[256,1280]{1,0:T(8,128)(2,1)S(1)}, u32[]{:S(2)}, u32[]{:S(2)}) collective-permute-start(bf16[256,1280]{1,0:T(8,128)(2,1)S(1)} %shard_map.83.refs_4_), channel_id=1, source_target_pairs={{0,1},{1,0},{2,3},{3,2},{4,5},{5,4},{6,7},{7,6},{8,9},{9,8},{10,11... | collective-permute-start | bytes 1966088 | tf_op jit(solution)/shard_map/ppermute | solution.py:22
  50.9 2.8 %collective-permute-start.17 = (bf16[240,1024]{1,0:T(8,128)(2,1)S(1)}, bf16[240,1024]{1,0:T(8,128)(2,1)S(1)}, u32[]{:S(2)}, u32[]{:S(2)}) collective-permute-start(bf16[240,1024]{1,0:T(8,128)(2,1)S(1)} %collective-permute-done.14.refs_13_), channel_id=1, source_target_pairs={{0,1},{1,0},{2,3},{3,2},{4,5},{5,4},{6,7},{7,6},{8,9},{9,8},{10,11... | collective-permute-start | bytes 1474568 | tf_op jit(solution)/shard_map/ppermute | solution.py:22
  66.3 1.8 %collective-permute-start.18 = (bf16[512,320]{1,0:T(8,128)(2,1)S(1)}, bf16[512,320]{1,0:T(8,128)(2,1)S(1)}, u32[]{:S(2)}, u32[]{:S(2)}) collective-permute-start(bf16[512,320]{1,0:T(8,128)(2,1)S(1)} %get-tuple-element.48.memory), channel_id=1, source_target_pairs={{0,1},{1,0},{2,3},{3,2},{4,5},{5,4},{6,7},{7,6},{8,9},{9,8},{10,11... | collective-permute-start | bytes 983048 | tf_op jit(solution)/shard_map/ppermute | solution.py:22
  66.5 7.8 %collective-permute-start.21 = (bf16[256,320]{1,0:T(8,128)(2,1)S(1)}, bf16[256,320]{1,0:T(8,128)(2,1)S(1)}, u32[]{:S(2)}, u32[]{:S(2)}) collective-permute-start(bf16[256,320]{1,0:T(8,128)(2,1)S(1)} %get-tuple-element.53), channel_id=1, source_target_pairs={{0,2},{1,6},{2,0},{3,4},{4,3},{5,7},{6,1},{7,5},{8,10},{9,14},{10,... | collective-permute-start | bytes 491528 | tf_op jit(solution)/shard_map/ppermute | solution.py:22
  69.4 6.2 %collective-permute-start.19 = (bf16[256,320]{1,0:T(8,128)(2,1)S(1)}, bf16[256,320]{1,0:T(8,128)(2,1)S(1)}, u32[]{:S(2)}, u32[]{:S(2)}) collective-permute-start(bf16[256,320]{1,0:T(8,128)(2,1)S(1)} %get-tuple-element.50), channel_id=1, source_target_pairs={{0,0},{1,4},{2,2},{3,6},{4,1},{5,5},{6,3},{7,7},{8,8},{9,12},{10,1... | collective-permute-start | bytes 491528 | tf_op jit(solution)/shard_map/ppermute | solution.py:22
  70.1 4.9 %collective-permute-start.20 = (f32[40,128]{1,0:T(8,128)S(1)}, f32[40,128]{1,0:T(8,128)S(1)}, u32[]{:S(2)}, u32[]{:S(2)}) collective-permute-start(f32[40,128]{1,0:T(8,128)S(1)} %get-tuple-element.51), channel_id=1, source_target_pairs={{0,8},{1,9},{2,10},{3,11},{4,12},{5,13},{6,14},{7,15},{8,0},{9,1},... | collective-permute-start | bytes 61448 | tf_op jit(solution)/shard_map/ppermute | solution.py:22
  74.9 5.8 %collective-permute-start.23 = (bf16[256,320]{1,0:T(8,128)(2,1)S(1)}, bf16[256,320]{1,0:T(8,128)(2,1)S(1)}, u32[]{:S(2)}, u32[]{:S(2)}) collective-permute-start(bf16[256,320]{1,0:T(8,128)(2,1)S(1)} %collective-permute-done.21.refs_1_), channel_id=1, source_target_pairs={{0,1},{1,0},{2,3},{3,2},{4,5},{5,4},{6,7},{7,6},{8,9},{9,8},{10,11... | collective-permute-start | bytes 491528 | tf_op jit(solution)/shard_map/ppermute | solution.py:22
  75.6 5.2 %collective-permute-start.22 = (bf16[256,320]{1,0:T(8,128)(2,1)S(1)}, bf16[256,320]{1,0:T(8,128)(2,1)S(1)}, u32[]{:S(2)}, u32[]{:S(2)}) collective-permute-start(bf16[256,320]{1,0:T(8,128)(2,1)S(1)} %collective-permute-done.19.refs_0_), channel_id=1, source_target_pairs={{0,1},{1,0},{2,3},{3,2},{4,5},{5,4},{6,7},{7,6},{8,9},{9,8},{10,11... | collective-permute-start | bytes 491528 | tf_op jit(solution)/shard_map/ppermute | solution.py:22
  77.2 4.9 %collective-permute-start.24 = (bf16[2,384]{1,0:T(2,128)(2,1)S(1)}, bf16[2,384]{1,0:T(2,128)(2,1)S(1)}, u32[]{:S(2)}, u32[]{:S(2)}) collective-permute-start(bf16[2,384]{1,0:T(2,128)(2,1)S(1)} %get-tuple-element.57), channel_id=1, source_target_pairs={{0,2},{1,3},{2,0},{3,1},{4,6},{5,7},{6,4},{7,5},{8,10},{9,11},{10,... | collective-permute-start | bytes 4616 | tf_op jit(solution)/shard_map/ppermute | solution.py:22
  77.8 4.3 %collective-permute-start.25 = (bf16[2,384]{1,0:T(2,128)(2,1)S(1)}, bf16[2,384]{1,0:T(2,128)(2,1)S(1)}, u32[]{:S(2)}, u32[]{:S(2)}) collective-permute-start(bf16[2,384]{1,0:T(2,128)(2,1)S(1)} %get-tuple-element.58), channel_id=1, source_target_pairs={{0,4},{1,5},{2,6},{3,7},{4,0},{5,1},{6,2},{7,3},{8,12},{9,13},{10,... | collective-permute-start | bytes 4616 | tf_op jit(solution)/shard_map/ppermute | solution.py:22
  80.4 4.5 %collective-permute-start.26 = (bf16[2,384]{1,0:T(2,128)(2,1)S(1)}, bf16[2,384]{1,0:T(2,128)(2,1)S(1)}, u32[]{:S(2)}, u32[]{:S(2)}) collective-permute-start(bf16[2,384]{1,0:T(2,128)(2,1)S(1)} %get-tuple-element.59), channel_id=1, source_target_pairs={{0,6},{1,7},{2,4},{3,5},{4,2},{5,3},{6,0},{7,1},{8,14},{9,15},{10,... | collective-permute-start | bytes 4616 | tf_op jit(solution)/shard_map/ppermute | solution.py:22

commit v17 on v14

--- a/solution.py
+++ b/solution.py
@@ -524,6 +524,7 @@
         )
         across = swap(theirs, n, 2)
         mine_c, across_c = swap(mine, n, 1), swap(across, n, 1)
+        near = send(after(stem, mine_c), near_route)
         ready = load(table, mine, mine_c, after(across, near, pair), across_c)
         relayed = swap(after(near, ready[0]), n, 4)
         stem_x = swap(after(stem, across), n, 2)

time: 85.2 us -> 86.3 us (1.013)
  starting transfers between devices: 25.3 us -> 33.6 us
  waiting for transfers between devices: 33.2 us -> 29 us
  Pallas kernels: 22.8 us -> 19.7 us
    ppermute x26, starting transfers between devices: 23.7 us -> 32.1 us  [send(): return lax.ppermute(block, 'tm', route)]
    ppermute x26, waiting for transfers between devices: 31.9 us -> 27.7 us  [send(): return lax.ppermute(block, 'tm', route)]
    pallas_call x1, Pallas kernels: 12.6 us -> 9.52 us  [encoder(): pl.pallas_call(functools.partial(encoder_kernel, len(parts), depth), out_...]
  transfers between devices with their start and end apart: 27 -> 27, of which waited for: 14 -> 13; matrix products, arithmetic and copies ran while one was open for 1% -> 1% of each run, Pallas kernels for 9% -> 9%
where the time goes in v17:
time: 86.3 us; the launch traced here: 86.1 us
  starting transfers between devices  33.6 us (39%)
  waiting for transfers between devices  29 us (34%)
  Pallas kernels  19.7 us (23%)
  local copies, waits for them, and re-layouts  1.87 us (2%)
  other arithmetic  1.02 us (1%)
  between operations  0.9 us (1%)
    ppermute x26, starting transfers between devices, send(): return lax.ppermute(block, 'tm', route)  32.1 us
    ppermute x26, waiting for transfers between devices, send(): return lax.ppermute(block, 'tm', route)  27.7 us
    pallas_call x1, Pallas kernels, encoder(): pl.pallas_call(functools.partial(encoder_kernel, len(parts), depth), out_...  9.52 us
    pallas_call x3, Pallas kernels, norm_half(): pl.pallas_call(norm_kernel, out_shape=jax.ShapeDtypeStruct((256, 1664 if...  2.93 us
    pallas_call x2, Pallas kernels, gather_groups(): pl.pallas_call(functools.partial(gather_kernel, side, rows), out_shape=ja...  2.59 us
    unnamed x12, local copies, waits for them, and re-layouts  1.76 us
  transfers between devices with their start and end apart: 27, of which 13 were waited for; matrix products, arithmetic and copies ran while one was open for 1% of the time, Pallas kernels for 9%

profile of v17, /device:TPU:0, one launch (start us, length us, event | category | flops | bytes accessed | tf_op | source)
XLA Modules:
  0.0 86.1 jit_solution(15839124495543580926)
XLA Ops:
  0.7 0.0 copy-start.2
  0.7 0.1 stack.136.table.places
  0.8 0.0 copy-start.3
  0.9 0.0 copy-start.4
  0.9 0.5 copy-done.2
  1.4 0.1 copy-done.3
  1.5 1.1 %copy-done = bf16[80,3840]{1,0:T(8,128)(2,1)S(1)} copy-done((bf16[80,3840]{1,0:T(8,128)(2,1)S(1)}, bf16[80,3840]{1,0:T(8,128)(2,1)}, u32[]{:S(2)}) %copy-start) | copy-done | bytes 614424
  2.6 1.1 %shard_map.77 = (bf16[2,80,1024]{2,1,0:T(8,128)(2,1)S(1)}, bf16[2,80,1024]{2,1,0:T(8,128)(2,1)S(1)}) custom-call(s32[34]{0:T(128)S(1)} %stack.136.table.places, bf16[80,3840]{1,0:T(8,128)(2,1)S(1)} %copy-done, bf16[2,1280]{1,0:T(2,128)(2,1)S(1)} %copy-done.2, s32[2,16]{1,0:T(2,128)S(1)} %copy-done.3, s32[1,128]{1,0:T(1,128)S(1)} %bitcast.33), custom_call_target="tpu_custom_call" | custom-call | flops 1 | bytes 1 | tf_op jit(solution)/shard_map/pallas_call | solution.py:98
  3.8 0.5 collective-permute-start.4
  4.3 2.6 %collective-permute-start = (bf16[2,80,1024]{2,1,0:T(8,128)(2,1)S(1)}, bf16[2,80,1024]{2,1,0:T(8,128)(2,1)S(1)}, u32[]{:S(2)}, u32[]{:S(2)}) collective-permute-start(bf16[2,80,1024]{2,1,0:T(8,128)(2,1)S(1)} %get-tuple-element.32), channel_id=1, source_target_pairs={{0,2},{1,3},{2,0},{3,1},{4,6},{5,7},{6,4},{7,5},{8,10},{9,11},{10,... | collective-permute-start | bytes 983048 | tf_op jit(solution)/shard_map/ppermute | solution.py:22
  6.9 1.6 %collective-permute-start.3 = (bf16[128,1280]{1,0:T(8,128)(2,1)S(1)}, bf16[128,1280]{1,0:T(8,128)(2,1)S(1)}, u32[]{:S(2)}, u32[]{:S(2)}) collective-permute-start(bf16[128,1280]{1,0:T(8,128)(2,1)S(1)} %copy-done.1), channel_id=1, source_target_pairs={{0,4},{1,5},{2,6},{3,7},{4,0},{5,1},{6,2},{7,3},{8,12},{9,13},{10,... | collective-permute-start | bytes 983048 | tf_op jit(solution)/shard_map/ppermute | solution.py:22
  8.4 0.0 collective-permute-done.4.refs_1_.refs_8_
  8.4 0.7 collective-permute-start.5
  9.1 6.0 %collective-permute-done.refs_2_.refs_9_ = bf16[2,80,1024]{2,1,0:T(8,128)(2,1)S(1)} collective-permute-done((bf16[2,80,1024]{2,1,0:T(8,128)(2,1)S(1)}, bf16[2,80,1024]{2,1,0:T(8,128)(2,1)S(1)}, u32[]{:S(2)}, u32[]{:S(2)}) %collective-permute-start) | collective-permute-done | bytes 327712 | tf_op jit(solution)/shard_map/ppermute | solution.py:22
  15.2 1.8 %collective-permute-start.1 = (bf16[128,1280]{1,0:T(8,128)(2,1)S(1)}, bf16[128,1280]{1,0:T(8,128)(2,1)S(1)}, u32[]{:S(2)}, u32[]{:S(2)}) collective-permute-start(bf16[128,1280]{1,0:T(8,128)(2,1)S(1)} %copy-done.1), channel_id=1, source_target_pairs={{0,2},{1,3},{2,0},{3,1},{4,6},{5,7},{6,4},{7,5},{8,10},{9,11},{10,... | collective-permute-start | bytes 983048 | tf_op jit(solution)/shard_map/ppermute | solution.py:22
  16.9 0.0 copy-start.5
  16.9 0.6 shard_map.79
  17.5 1.7 %collective-permute-start.7 = (bf16[128,1280]{1,0:T(8,128)(2,1)S(1)}, bf16[128,1280]{1,0:T(8,128)(2,1)S(1)}, u32[]{:S(2)}, u32[]{:S(2)}) collective-permute-start(bf16[128,1280]{1,0:T(8,128)(2,1)S(1)} %collective-permute-done.3.here), channel_id=1, source_target_pairs={{0,2},{1,3},{2,0},{3,1},{4,6},{5,7},{6,4},{7,5},{8,10},{9,11},{10,... | collective-permute-start | bytes 983048 | tf_op jit(solution)/shard_map/ppermute | solution.py:22
  19.2 3.2 %collective-permute-start.9 = (bf16[128,1280]{1,0:T(8,128)(2,1)S(1)}, bf16[128,1280]{1,0:T(8,128)(2,1)}, u32[]{:S(2)}, u32[]{:S(2)}) collective-permute-start(bf16[128,1280]{1,0:T(8,128)(2,1)S(1)} %collective-permute-done.5), channel_id=1, source_target_pairs={{0,4},{1,5},{2,6},{3,7},{4,0},{5,1},{6,2},{7,3},{8,12},{9,13},{10,... | collective-permute-start | bytes 983048 | tf_op jit(solution)/shard_map/ppermute | solution.py:22
  22.4 1.2 %collective-permute-start.11 = (bf16[80,1024]{1,0:T(8,128)(2,1)S(1)}, bf16[80,1024]{1,0:T(8,128)(2,1)S(1)}, u32[]{:S(2)}, u32[]{:S(2)}) collective-permute-start(bf16[80,1024]{1,0:T(8,128)(2,1)S(1)} %get-tuple-element.37.refs_0_), channel_id=1, source_target_pairs={{0,8},{1,9},{2,10},{3,11},{4,12},{5,13},{6,14},{7,15},{8,0},{9,1},... | collective-permute-start | bytes 491528 | tf_op jit(solution)/shard_map/ppermute | solution.py:22
  23.7 1.5 %collective-permute-start.10 = (bf16[80,1024]{1,0:T(8,128)(2,1)S(1)}, bf16[80,1024]{1,0:T(8,128)(2,1)S(1)}, u32[]{:S(2)}, u32[]{:S(2)}) collective-permute-start(bf16[80,1024]{1,0:T(8,128)(2,1)S(1)} %get-tuple-element.41), channel_id=1, source_target_pairs={{0,12},{1,13},{2,14},{3,15},{4,8},{5,9},{6,10},{7,11},{8,4},{9,5},... | collective-permute-start | bytes 491528 | tf_op jit(solution)/shard_map/ppermute | solution.py:22
  25.2 0.5 collective-permute-done.1.across
  25.7 1.8 %collective-permute-start.12 = (bf16[80,1024]{1,0:T(8,128)(2,1)S(1)}, bf16[80,1024]{1,0:T(8,128)(2,1)S(1)}, u32[]{:S(2)}, u32[]{:S(2)}) collective-permute-start(bf16[80,1024]{1,0:T(8,128)(2,1)S(1)} %get-tuple-element.41), channel_id=1, source_target_pairs={{0,4},{1,5},{2,6},{3,7},{4,0},{5,1},{6,2},{7,3},{8,12},{9,13},{10,... | collective-permute-start | bytes 491528 | tf_op jit(solution)/shard_map/ppermute | solution.py:22
  27.5 1.0 %shard_map.78.refs_0_ = bf16[256,1664]{1,0:T(8,128)(2,1)S(1)} custom-call(s32[34]{0:T(128)S(1)} %stack.136.table.places, f32[1,1280]{1,0:T(1,128)S(1)} %reshape.10.gain, bf16[128,1280]{1,0:T(8,128)(2,1)S(1)} %copy-done.1, bf16[128,1280]{1,0:T(8,128)(2,1)S(1)} %collective-permute-done.1.across), custom_call_target="tpu_custom_call" | custom-call | flops 1 | bytes 1 | tf_op jit(solution)/shard_map/pallas_call | solution.py:162
  28.5 3.8 %collective-permute-done.7.across = bf16[128,1280]{1,0:T(8,128)(2,1)S(1)} collective-permute-done((bf16[128,1280]{1,0:T(8,128)(2,1)S(1)}, bf16[128,1280]{1,0:T(8,128)(2,1)S(1)}, u32[]{:S(2)}, u32[]{:S(2)}) %collective-permute-start.7) | collective-permute-done | bytes 327712 | tf_op jit(solution)/shard_map/ppermute | solution.py:22
  32.3 1.0 %shard_map.80.refs_2_ = bf16[256,1664]{1,0:T(8,128)(2,1)S(1)} custom-call(s32[34]{0:T(128)S(1)} %stack.136.table.places, f32[1,1280]{1,0:T(1,128)S(1)} %reshape.10.gain, bf16[128,1280]{1,0:T(8,128)(2,1)S(1)} %collective-permute-done.3.here, bf16[128,1280]{1,0:T(8,128)(2,1)S(1)} %collective-permute-done.7.across), custom_call_target="tpu_custom_call" | custom-call | flops 1 | bytes 1 | tf_op jit(solution)/shard_map/pallas_call | solution.py:162
  33.3 3.1 %collective-permute-done.9 = bf16[128,1280]{1,0:T(8,128)(2,1)} collective-permute-done((bf16[128,1280]{1,0:T(8,128)(2,1)S(1)}, bf16[128,1280]{1,0:T(8,128)(2,1)}, u32[]{:S(2)}, u32[]{:S(2)}) %collective-permute-start.9) | collective-permute-done | bytes 327712 | tf_op jit(solution)/shard_map/ppermute | solution.py:22
  36.4 0.0 collective-permute-start.8
  36.4 1.0 %broadcast_select_fusion.here = bf16[128,1280]{1,0:T(8,128)(2,1)S(1)} fusion(bf16[128,1280]{1,0:T(8,128)(2,1)S(1)} %collective-permute-done.5, bf16[128,1280]{1,0:T(8,128)(2,1)} %collective-permute-done.9, pred[]{:T(512)S(6)} %or.3), kind=kLoop, calls=%fused_computation | loop fusion | flops 163840 | bytes 983041 | tf_op jit(solution)/shard_map/jit(_where)/select_n | solution.py:534
  37.5 1.7 %collective-permute-done.12.refs_0_ = bf16[80,1024]{1,0:T(8,128)(2,1)S(1)} collective-permute-done((bf16[80,1024]{1,0:T(8,128)(2,1)S(1)}, bf16[80,1024]{1,0:T(8,128)(2,1)S(1)}, u32[]{:S(2)}, u32[]{:S(2)}) %collective-permute-start.12) | collective-permute-done | bytes 163872 | tf_op jit(solution)/shard_map/ppermute | solution.py:22
  39.2 1.0 %collective-permute-done.10.refs_2_ = bf16[80,1024]{1,0:T(8,128)(2,1)S(1)} collective-permute-done((bf16[80,1024]{1,0:T(8,128)(2,1)S(1)}, bf16[80,1024]{1,0:T(8,128)(2,1)S(1)}, u32[]{:S(2)}, u32[]{:S(2)}) %collective-permute-start.10) | collective-permute-done | bytes 163872 | tf_op jit(solution)/shard_map/ppermute | solution.py:22
  40.2 0.0 collective-permute-done.11.refs_1_
  40.3 1.6 %collective-permute-start.14 = (bf16[240,1024]{1,0:T(8,128)(2,1)S(1)}, bf16[240,1024]{1,0:T(8,128)(2,1)S(1)}, u32[]{:S(2)}, u32[]{:S(2)}) collective-permute-start(bf16[240,1024]{1,0:T(8,128)(2,1)S(1)} %shard_map.81.refs_1_.refs_11_), channel_id=1, source_target_pairs={{0,16},{16,0},{1,17},{17,1},{2,18},{18,2},{3,19},{19,3},{4,20},{20... | collective-permute-start | bytes 1474568 | tf_op jit(solution)/shard_map/ppermute | solution.py:520
  41.8 1.5 %collective-permute-start.13 = (bf16[128,1280]{1,0:T(8,128)(2,1)S(1)}, bf16[128,1280]{1,0:T(8,128)(2,1)S(1)}, u32[]{:S(2)}, u32[]{:S(2)}) collective-permute-start(bf16[128,1280]{1,0:T(8,128)(2,1)S(1)} %broadcast_select_fusion.here), channel_id=1, source_target_pairs={{0,2},{1,3},{2,0},{3,1},{4,6},{5,7},{6,4},{7,5},{8,10},{9,11},{10,... | collective-permute-start | bytes 983048 | tf_op jit(solution)/shard_map/ppermute | solution.py:22
  43.3 1.3 %shard_map.82 = (f32[8,1536]{1,0:T(8,128)S(1)}, f32[80,320]{1,0:T(8,128)S(1)}, f32[16,64]{1,0:T(8,128)S(1)}) custom-call(s32[34]{0:T(128)S(1)} %stack.136.table.places, bf16[80,1024]{1,0:T(8,128)(2,1)S(1)} %get-tuple-element.37.refs_0_, bf16[240,1024]{1,0:T(8,128)(2,1)S(1)} %shard_map.81.refs_1_.refs_11_), custom_call_target="tpu_custom_call" | custom-call | flops 1 | bytes 1 | tf_op jit(solution)/shard_map/pallas_call | solution.py:208
  44.7 4.3 %collective-permute-done.13.across = bf16[128,1280]{1,0:T(8,128)(2,1)S(1)} collective-permute-done((bf16[128,1280]{1,0:T(8,128)(2,1)S(1)}, bf16[128,1280]{1,0:T(8,128)(2,1)S(1)}, u32[]{:S(2)}, u32[]{:S(2)}) %collective-permute-start.13) | collective-permute-done | bytes 327712 | tf_op jit(solution)/shard_map/ppermute | solution.py:22
  49.0 1.0 %shard_map.83.refs_4_ = bf16[256,1280]{1,0:T(8,128)(2,1)S(1)} custom-call(s32[34]{0:T(128)S(1)} %stack.136.table.places, f32[1,1280]{1,0:T(1,128)S(1)} %reshape.10.gain, bf16[128,1280]{1,0:T(8,128)(2,1)S(1)} %broadcast_select_fusion.here, bf16[128,1280]{1,0:T(8,128)(2,1)S(1)} %collective-permute-done.13.across), custom_call_target="tpu_custom_call" | custom-call | flops 1 | bytes 1 | tf_op jit(solution)/shard_map/pallas_call | solution.py:162
  49.9 1.3 %collective-permute-done.14.refs_13_ = bf16[240,1024]{1,0:T(8,128)(2,1)S(1)} collective-permute-done((bf16[240,1024]{1,0:T(8,128)(2,1)S(1)}, bf16[240,1024]{1,0:T(8,128)(2,1)S(1)}, u32[]{:S(2)}, u32[]{:S(2)}) %collective-permute-start.14) | collective-permute-done | bytes 491552 | tf_op jit(solution)/shard_map/ppermute | solution.py:520
  51.2 0.0 collective-permute-start.15
  51.2 0.0 collective-permute-done.16.refs_12_
  51.2 0.0 collective-permute-done.2.refs_1_
  51.3 0.6 collective-permute-start.17
  51.8 1.5 %collective-permute-done.15.refs_5_ = bf16[256,1280]{1,0:T(8,128)(2,1)S(1)} collective-permute-done((bf16[256,1280]{1,0:T(8,128)(2,1)S(1)}, bf16[256,1280]{1,0:T(8,128)(2,1)S(1)}, u32[]{:S(2)}, u32[]{:S(2)}) %collective-permute-start.15) | collective-permute-done | bytes 655392 | tf_op jit(solution)/shard_map/ppermute | solution.py:22
  53.3 0.7 collective-permute-done.17.refs_14_
  54.0 9.5 %shard_map.84 = (bf16[512,320]{1,0:T(8,128)(2,1)S(1)}, bf16[256,320]{1,0:T(8,128)(2,1)S(1)}, bf16[256,320]{1,0:T(8,128)(2,1)S(1)}) custom-call(s32[34]{0:T(128)S(1)} %stack.136.table.places, bf16[256,1664]{1,0:T(8,128)(2,1)S(1)} %shard_map.78.refs_0_, bf16[256,1664]{1,0:T(8,128)(2,1)S(1)} %collective-permute-done.2.refs_1_, ...), custom_call_target="tpu_custom_call" | custom-call | flops 1 | bytes 1 | tf_op jit(solution)/shard_map/pallas_call | solution.py:355
  63.6 0.2 collective-permute-start.19
  63.8 4.6 %collective-permute-start.21 = (bf16[256,320]{1,0:T(8,128)(2,1)S(1)}, bf16[256,320]{1,0:T(8,128)(2,1)S(1)}, u32[]{:S(2)}, u32[]{:S(2)}) collective-permute-start(bf16[256,320]{1,0:T(8,128)(2,1)S(1)} %get-tuple-element.54), channel_id=1, source_target_pairs={{0,2},{1,6},{2,0},{3,4},{4,3},{5,7},{6,1},{7,5},{8,10},{9,14},{10,... | collective-permute-start | bytes 491528 | tf_op jit(solution)/shard_map/ppermute | solution.py:22
  68.3 0.7 collective-permute-start.18
  69.0 0.0 collective-permute-done.19.beside
  69.0 1.3 %shard_map.85 = (f32[40,128]{1,0:T(8,128)S(1)}, f32[40,128]{1,0:T(8,128)S(1)}) custom-call(s32[34]{0:T(128)S(1)} %stack.136.table.places, f32[80,320]{1,0:T(8,128)S(1)} %get-tuple-element.49.tokens, f32[16,64]{1,0:T(8,128)S(1)} %get-tuple-element.50.asked, bf16[512,320]{1,0:T(8,128)(2,1)S(1)} %get-tuple-element.51.memory, ...), custom_call_target="tpu_custom_call" | custom-call | flops 1 | bytes 1 | tf_op jit(solution)/shard_map/pallas_call | solution.py:421
  70.3 2.1 %collective-permute-start.20 = (f32[40,128]{1,0:T(8,128)S(1)}, f32[40,128]{1,0:T(8,128)S(1)}, u32[]{:S(2)}, u32[]{:S(2)}) collective-permute-start(f32[40,128]{1,0:T(8,128)S(1)} %get-tuple-element.52), channel_id=1, source_target_pairs={{0,8},{1,9},{2,10},{3,11},{4,12},{5,13},{6,14},{7,15},{8,0},{9,1},... | collective-permute-start | bytes 61448 | tf_op jit(solution)/shard_map/ppermute | solution.py:22
  72.5 1.6 %collective-permute-done.21.refs_1_ = bf16[256,320]{1,0:T(8,128)(2,1)S(1)} collective-permute-done((bf16[256,320]{1,0:T(8,128)(2,1)S(1)}, bf16[256,320]{1,0:T(8,128)(2,1)S(1)}, u32[]{:S(2)}, u32[]{:S(2)}) %collective-permute-start.21) | collective-permute-done | bytes 163872 | tf_op jit(solution)/shard_map/ppermute | solution.py:22
  74.1 1.1 %collective-permute-done.20.refs_1_ = f32[40,128]{1,0:T(8,128)S(1)} collective-permute-done((f32[40,128]{1,0:T(8,128)S(1)}, f32[40,128]{1,0:T(8,128)S(1)}, u32[]{:S(2)}, u32[]{:S(2)}) %collective-permute-start.20) | collective-permute-done | bytes 20512 | tf_op jit(solution)/shard_map/ppermute | solution.py:22
  75.2 0.0 collective-permute-done.18.refs_0_
  75.2 1.7 %collective-permute-start.22 = (bf16[256,320]{1,0:T(8,128)(2,1)S(1)}, bf16[256,320]{1,0:T(8,128)(2,1)S(1)}, u32[]{:S(2)}, u32[]{:S(2)}) collective-permute-start(bf16[256,320]{1,0:T(8,128)(2,1)S(1)} %collective-permute-done.18.refs_0_), channel_id=1, source_target_pairs={{0,1},{1,0},{2,3},{3,2},{4,5},{5,4},{6,7},{7,6},{8,9},{9,8},{10,11... | collective-permute-start | bytes 491528 | tf_op jit(solution)/shard_map/ppermute | solution.py:22
  76.8 0.0 collective-permute-start.23
  76.8 0.2 shard_map.87
  77.1 0.6 collective-permute-start.24
  77.7 2.7 %collective-permute-start.25 = (bf16[2,384]{1,0:T(2,128)(2,1)S(1)}, bf16[2,384]{1,0:T(2,128)(2,1)S(1)}, u32[]{:S(2)}, u32[]{:S(2)}) collective-permute-start(bf16[2,384]{1,0:T(2,128)(2,1)S(1)} %get-tuple-element.60), channel_id=1, source_target_pairs={{0,4},{1,5},{2,6},{3,7},{4,0},{5,1},{6,2},{7,3},{8,12},{9,13},{10,... | collective-permute-start | bytes 4616 | tf_op jit(solution)/shard_map/ppermute | solution.py:22
  80.4 0.9 %collective-permute-start.26 = (bf16[2,384]{1,0:T(2,128)(2,1)S(1)}, bf16[2,384]{1,0:T(2,128)(2,1)S(1)}, u32[]{:S(2)}, u32[]{:S(2)}) collective-permute-start(bf16[2,384]{1,0:T(2,128)(2,1)S(1)} %get-tuple-element.61), channel_id=1, source_target_pairs={{0,6},{1,7},{2,4},{3,5},{4,2},{5,3},{6,0},{7,1},{8,14},{9,15},{10,... | collective-permute-start | bytes 4616 | tf_op jit(solution)/shard_map/ppermute | solution.py:22
  81.3 0.0 collective-permute-done.22.refs_2_
  81.3 1.4 %shard_map.86 = bf16[128,1280]{1,0:T(8,128)(2,1)} custom-call(s32[34]{0:T(128)S(1)} %stack.136.table.places, bf16[256,320]{1,0:T(8,128)(2,1)S(1)} %collective-permute-done.18.refs_0_, bf16[256,320]{1,0:T(8,128)(2,1)S(1)} %collective-permute-done.21.refs_1_, bf16[256,320]{1,0:T(8,128)(2,1)S(1)} %collective-permute-done.22.refs_2_, ...), custom_call_target="tpu_custom_call" | custom-call | flops 1 | bytes 1 | tf_op jit(solution)/shard_map/pallas_call | solution.py:475
  82.7 2.2 %collective-permute-done.26.refs_3_ = bf16[2,384]{1,0:T(2,128)(2,1)S(1)} collective-permute-done((bf16[2,384]{1,0:T(2,128)(2,1)S(1)}, bf16[2,384]{1,0:T(2,128)(2,1)S(1)}, u32[]{:S(2)}, u32[]{:S(2)}) %collective-permute-start.26) | collective-permute-done | bytes 1568 | tf_op jit(solution)/shard_map/ppermute | solution.py:22
  84.9 1.2 %shard_map.88 = bf16[2,1280]{1,0:T(2,128)(2,1)} custom-call(s32[34]{0:T(128)S(1)} %stack.136.table.places, bf16[2,384]{1,0:T(2,128)(2,1)S(1)} %get-tuple-element.58.refs_0_, bf16[2,384]{1,0:T(2,128)(2,1)S(1)} %collective-permute-done.24.refs_1_, bf16[2,384]{1,0:T(2,128)(2,1)S(1)} %collective-permute-done.25.refs_2_, ...), custom_call_target="tpu_custom_call" | custom-call | flops 1 | bytes 1 | tf_op jit(solution)/shard_map/pallas_call | solution.py:475
  (17 shorter events, 0.1 us)
Async XLA Ops:
  0.7 0.7 copy-start.2
  0.8 0.7 copy-start.3
  0.9 0.7 copy-start.4
  1.5 1.1 %copy-start = (bf16[80,3840]{1,0:T(8,128)(2,1)S(1)}, bf16[80,3840]{1,0:T(8,128)(2,1)}, u32[]{:S(2)}) copy-start(bf16[80,3840]{1,0:T(8,128)(2,1)} %refs_0_.1) | copy-start | bytes 1843204
  2.6 4.2 %copy-start.1 = (bf16[128,1280]{1,0:T(8,128)(2,1)S(1)}, bf16[128,1280]{1,0:T(8,128)(2,1)}, u32[]{:S(2)}) copy-start(bf16[128,1280]{1,0:T(8,128)(2,1)} %here.1) | copy-start | bytes 983044
  3.8 4.7 %collective-permute-start.4 = (bf16[2,80,1024]{2,1,0:T(8,128)(2,1)S(1)}, bf16[2,80,1024]{2,1,0:T(8,128)(2,1)S(1)}, u32[]{:S(2)}, u32[]{:S(2)}) collective-permute-start(bf16[2,80,1024]{2,1,0:T(8,128)(2,1)S(1)} %get-tuple-element.34.refs_0_.refs_7_), channel_id=1, source_target_pairs={{0,1},{1,0},{2,3},{3,2},{4,5},{5,4},{6,7},{7,6},{8,9},{9,8},{10,11... | collective-permute-start | bytes 983048 | tf_op jit(solution)/shard_map/ppermute | solution.py:22
  4.3 10.9 %collective-permute-start = (bf16[2,80,1024]{2,1,0:T(8,128)(2,1)S(1)}, bf16[2,80,1024]{2,1,0:T(8,128)(2,1)S(1)}, u32[]{:S(2)}, u32[]{:S(2)}) collective-permute-start(bf16[2,80,1024]{2,1,0:T(8,128)(2,1)S(1)} %get-tuple-element.32), channel_id=1, source_target_pairs={{0,2},{1,3},{2,0},{3,1},{4,6},{5,7},{6,4},{7,5},{8,10},{9,11},{10,... | collective-permute-start | bytes 983048 | tf_op jit(solution)/shard_map/ppermute | solution.py:22
  6.9 10.1 %collective-permute-start.3 = (bf16[128,1280]{1,0:T(8,128)(2,1)S(1)}, bf16[128,1280]{1,0:T(8,128)(2,1)S(1)}, u32[]{:S(2)}, u32[]{:S(2)}) collective-permute-start(bf16[128,1280]{1,0:T(8,128)(2,1)S(1)} %copy-done.1), channel_id=1, source_target_pairs={{0,4},{1,5},{2,6},{3,7},{4,0},{5,1},{6,2},{7,3},{8,12},{9,13},{10,... | collective-permute-start | bytes 983048 | tf_op jit(solution)/shard_map/ppermute | solution.py:22
  8.4 8.5 %collective-permute-start.5 = (bf16[128,1280]{1,0:T(8,128)(2,1)S(1)}, bf16[128,1280]{1,0:T(8,128)(2,1)S(1)}, u32[]{:S(2)}, u32[]{:S(2)}) collective-permute-start(bf16[128,1280]{1,0:T(8,128)(2,1)S(1)} %copy-done.1), channel_id=1, source_target_pairs={{4,8},{5,9},{6,10},{7,11},{8,4},{9,5},{10,6},{11,7},{20,24},{21,25... | collective-permute-start | bytes 983048 | tf_op jit(solution)/shard_map/ppermute | solution.py:22
  15.2 1.8 %collective-permute-start.6 = (bf16[2,80,1024]{2,1,0:T(8,128)(2,1)S(1)}, bf16[2,80,1024]{2,1,0:T(8,128)(2,1)S(1)}, u32[]{:S(2)}, u32[]{:S(2)}) collective-permute-start(bf16[2,80,1024]{2,1,0:T(8,128)(2,1)S(1)} %collective-permute-done.refs_2_.refs_9_), channel_id=1, source_target_pairs={{0,1},{1,0},{2,3},{3,2},{4,5},{5,4},{6,7},{7,6},{8,9},{9,8},{10,11... | collective-permute-start | bytes 983048 | tf_op jit(solution)/shard_map/ppermute | solution.py:22
  15.2 10.5 %collective-permute-start.1 = (bf16[128,1280]{1,0:T(8,128)(2,1)S(1)}, bf16[128,1280]{1,0:T(8,128)(2,1)S(1)}, u32[]{:S(2)}, u32[]{:S(2)}) collective-permute-start(bf16[128,1280]{1,0:T(8,128)(2,1)S(1)} %copy-done.1), channel_id=1, source_target_pairs={{0,2},{1,3},{2,0},{3,1},{4,6},{5,7},{6,4},{7,5},{8,10},{9,11},{10,... | collective-permute-start | bytes 983048 | tf_op jit(solution)/shard_map/ppermute | solution.py:22
  16.9 5.5 %copy-start.5 = (f32[1280]{0:T(1024)S(1)}, f32[1280]{0:T(1024)}, u32[]{:S(2)}) copy-start(f32[1280]{0:T(1024)} %param.7) | copy-start | bytes 15364
  17.5 14.8 %collective-permute-start.7 = (bf16[128,1280]{1,0:T(8,128)(2,1)S(1)}, bf16[128,1280]{1,0:T(8,128)(2,1)S(1)}, u32[]{:S(2)}, u32[]{:S(2)}) collective-permute-start(bf16[128,1280]{1,0:T(8,128)(2,1)S(1)} %collective-permute-done.3.here), channel_id=1, source_target_pairs={{0,2},{1,3},{2,0},{3,1},{4,6},{5,7},{6,4},{7,5},{8,10},{9,11},{10,... | collective-permute-start | bytes 983048 | tf_op jit(solution)/shard_map/ppermute | solution.py:22
  19.2 17.2 %collective-permute-start.9 = (bf16[128,1280]{1,0:T(8,128)(2,1)S(1)}, bf16[128,1280]{1,0:T(8,128)(2,1)}, u32[]{:S(2)}, u32[]{:S(2)}) collective-permute-start(bf16[128,1280]{1,0:T(8,128)(2,1)S(1)} %collective-permute-done.5), channel_id=1, source_target_pairs={{0,4},{1,5},{2,6},{3,7},{4,0},{5,1},{6,2},{7,3},{8,12},{9,13},{10,... | collective-permute-start | bytes 983048 | tf_op jit(solution)/shard_map/ppermute | solution.py:22
  22.4 17.8 %collective-permute-start.11 = (bf16[80,1024]{1,0:T(8,128)(2,1)S(1)}, bf16[80,1024]{1,0:T(8,128)(2,1)S(1)}, u32[]{:S(2)}, u32[]{:S(2)}) collective-permute-start(bf16[80,1024]{1,0:T(8,128)(2,1)S(1)} %get-tuple-element.37.refs_0_), channel_id=1, source_target_pairs={{0,8},{1,9},{2,10},{3,11},{4,12},{5,13},{6,14},{7,15},{8,0},{9,1},... | collective-permute-start | bytes 491528 | tf_op jit(solution)/shard_map/ppermute | solution.py:22
  23.7 16.5 %collective-permute-start.10 = (bf16[80,1024]{1,0:T(8,128)(2,1)S(1)}, bf16[80,1024]{1,0:T(8,128)(2,1)S(1)}, u32[]{:S(2)}, u32[]{:S(2)}) collective-permute-start(bf16[80,1024]{1,0:T(8,128)(2,1)S(1)} %get-tuple-element.41), channel_id=1, source_target_pairs={{0,12},{1,13},{2,14},{3,15},{4,8},{5,9},{6,10},{7,11},{8,4},{9,5},... | collective-permute-start | bytes 491528 | tf_op jit(solution)/shard_map/ppermute | solution.py:22
  25.7 13.5 %collective-permute-start.12 = (bf16[80,1024]{1,0:T(8,128)(2,1)S(1)}, bf16[80,1024]{1,0:T(8,128)(2,1)S(1)}, u32[]{:S(2)}, u32[]{:S(2)}) collective-permute-start(bf16[80,1024]{1,0:T(8,128)(2,1)S(1)} %get-tuple-element.41), channel_id=1, source_target_pairs={{0,4},{1,5},{2,6},{3,7},{4,0},{5,1},{6,2},{7,3},{8,12},{9,13},{10,... | collective-permute-start | bytes 491528 | tf_op jit(solution)/shard_map/ppermute | solution.py:22
  32.3 18.9 %collective-permute-start.2 = (bf16[256,1664]{1,0:T(8,128)(2,1)S(1)}, bf16[256,1664]{1,0:T(8,128)(2,1)S(1)}, u32[]{:S(2)}, u32[]{:S(2)}) collective-permute-start(bf16[256,1664]{1,0:T(8,128)(2,1)S(1)} %shard_map.78.refs_0_), channel_id=1, source_target_pairs={{0,1},{1,0},{2,3},{3,2},{4,5},{5,4},{6,7},{7,6},{8,9},{9,8},{10,11... | collective-permute-start | bytes 2555912 | tf_op jit(solution)/shard_map/ppermute | solution.py:22
  36.4 14.8 %collective-permute-start.8 = (bf16[256,1664]{1,0:T(8,128)(2,1)S(1)}, bf16[256,1664]{1,0:T(8,128)(2,1)S(1)}, u32[]{:S(2)}, u32[]{:S(2)}) collective-permute-start(bf16[256,1664]{1,0:T(8,128)(2,1)S(1)} %shard_map.80.refs_2_), channel_id=1, source_target_pairs={{0,1},{1,0},{2,3},{3,2},{4,5},{5,4},{6,7},{7,6},{8,9},{9,8},{10,11... | collective-permute-start | bytes 2555912 | tf_op jit(solution)/shard_map/ppermute | solution.py:22
  40.3 11.0 %collective-permute-start.14 = (bf16[240,1024]{1,0:T(8,128)(2,1)S(1)}, bf16[240,1024]{1,0:T(8,128)(2,1)S(1)}, u32[]{:S(2)}, u32[]{:S(2)}) collective-permute-start(bf16[240,1024]{1,0:T(8,128)(2,1)S(1)} %shard_map.81.refs_1_.refs_11_), channel_id=1, source_target_pairs={{0,16},{16,0},{1,17},{17,1},{2,18},{18,2},{3,19},{19,3},{4,20},{20... | collective-permute-start | bytes 1474568 | tf_op jit(solution)/shard_map/ppermute | solution.py:520
  41.8 7.1 %collective-permute-start.13 = (bf16[128,1280]{1,0:T(8,128)(2,1)S(1)}, bf16[128,1280]{1,0:T(8,128)(2,1)S(1)}, u32[]{:S(2)}, u32[]{:S(2)}) collective-permute-start(bf16[128,1280]{1,0:T(8,128)(2,1)S(1)} %broadcast_select_fusion.here), channel_id=1, source_target_pairs={{0,2},{1,3},{2,0},{3,1},{4,6},{5,7},{6,4},{7,5},{8,10},{9,11},{10,... | collective-permute-start | bytes 983048 | tf_op jit(solution)/shard_map/ppermute | solution.py:22
  43.3 7.9 %collective-permute-start.16 = (bf16[240,1024]{1,0:T(8,128)(2,1)S(1)}, bf16[240,1024]{1,0:T(8,128)(2,1)S(1)}, u32[]{:S(2)}, u32[]{:S(2)}) collective-permute-start(bf16[240,1024]{1,0:T(8,128)(2,1)S(1)} %shard_map.81.refs_1_.refs_11_), channel_id=1, source_target_pairs={{0,1},{1,0},{2,3},{3,2},{4,5},{5,4},{6,7},{7,6},{8,9},{9,8},{10,11... | collective-permute-start | bytes 1474568 | tf_op jit(solution)/shard_map/ppermute | solution.py:22
  51.2 2.1 %collective-permute-start.15 = (bf16[256,1280]{1,0:T(8,128)(2,1)S(1)}, bf16[256,1280]{1,0:T(8,128)(2,1)S(1)}, u32[]{:S(2)}, u32[]{:S(2)}) collective-permute-start(bf16[256,1280]{1,0:T(8,128)(2,1)S(1)} %shard_map.83.refs_4_), channel_id=1, source_target_pairs={{0,1},{1,0},{2,3},{3,2},{4,5},{5,4},{6,7},{7,6},{8,9},{9,8},{10,11... | collective-permute-start | bytes 1966088 | tf_op jit(solution)/shard_map/ppermute | solution.py:22
  51.3 2.8 %collective-permute-start.17 = (bf16[240,1024]{1,0:T(8,128)(2,1)S(1)}, bf16[240,1024]{1,0:T(8,128)(2,1)S(1)}, u32[]{:S(2)}, u32[]{:S(2)}) collective-permute-start(bf16[240,1024]{1,0:T(8,128)(2,1)S(1)} %collective-permute-done.14.refs_13_), channel_id=1, source_target_pairs={{0,1},{1,0},{2,3},{3,2},{4,5},{5,4},{6,7},{7,6},{8,9},{9,8},{10,11... | collective-permute-start | bytes 1474568 | tf_op jit(solution)/shard_map/ppermute | solution.py:22
  63.6 5.5 %collective-permute-start.19 = (bf16[512,320]{1,0:T(8,128)(2,1)S(1)}, bf16[512,320]{1,0:T(8,128)(2,1)S(1)}, u32[]{:S(2)}, u32[]{:S(2)}) collective-permute-start(bf16[512,320]{1,0:T(8,128)(2,1)S(1)} %get-tuple-element.51.memory), channel_id=1, source_target_pairs={{0,1},{1,0},{2,3},{3,2},{4,5},{5,4},{6,7},{7,6},{8,9},{9,8},{10,11... | collective-permute-start | bytes 983048 | tf_op jit(solution)/shard_map/ppermute | solution.py:22
  63.8 10.3 %collective-permute-start.21 = (bf16[256,320]{1,0:T(8,128)(2,1)S(1)}, bf16[256,320]{1,0:T(8,128)(2,1)S(1)}, u32[]{:S(2)}, u32[]{:S(2)}) collective-permute-start(bf16[256,320]{1,0:T(8,128)(2,1)S(1)} %get-tuple-element.54), channel_id=1, source_target_pairs={{0,2},{1,6},{2,0},{3,4},{4,3},{5,7},{6,1},{7,5},{8,10},{9,14},{10,... | collective-permute-start | bytes 491528 | tf_op jit(solution)/shard_map/ppermute | solution.py:22
  68.3 6.8 %collective-permute-start.18 = (bf16[256,320]{1,0:T(8,128)(2,1)S(1)}, bf16[256,320]{1,0:T(8,128)(2,1)S(1)}, u32[]{:S(2)}, u32[]{:S(2)}) collective-permute-start(bf16[256,320]{1,0:T(8,128)(2,1)S(1)} %get-tuple-element.48), channel_id=1, source_target_pairs={{0,0},{1,4},{2,2},{3,6},{4,1},{5,5},{6,3},{7,7},{8,8},{9,12},{10,1... | collective-permute-start | bytes 491528 | tf_op jit(solution)/shard_map/ppermute | solution.py:22
  70.3 4.8 %collective-permute-start.20 = (f32[40,128]{1,0:T(8,128)S(1)}, f32[40,128]{1,0:T(8,128)S(1)}, u32[]{:S(2)}, u32[]{:S(2)}) collective-permute-start(f32[40,128]{1,0:T(8,128)S(1)} %get-tuple-element.52), channel_id=1, source_target_pairs={{0,8},{1,9},{2,10},{3,11},{4,12},{5,13},{6,14},{7,15},{8,0},{9,1},... | collective-permute-start | bytes 61448 | tf_op jit(solution)/shard_map/ppermute | solution.py:22
  75.2 6.1 %collective-permute-start.22 = (bf16[256,320]{1,0:T(8,128)(2,1)S(1)}, bf16[256,320]{1,0:T(8,128)(2,1)S(1)}, u32[]{:S(2)}, u32[]{:S(2)}) collective-permute-start(bf16[256,320]{1,0:T(8,128)(2,1)S(1)} %collective-permute-done.18.refs_0_), channel_id=1, source_target_pairs={{0,1},{1,0},{2,3},{3,2},{4,5},{5,4},{6,7},{7,6},{8,9},{9,8},{10,11... | collective-permute-start | bytes 491528 | tf_op jit(solution)/shard_map/ppermute | solution.py:22
  76.8 4.5 %collective-permute-start.23 = (bf16[256,320]{1,0:T(8,128)(2,1)S(1)}, bf16[256,320]{1,0:T(8,128)(2,1)S(1)}, u32[]{:S(2)}, u32[]{:S(2)}) collective-permute-start(bf16[256,320]{1,0:T(8,128)(2,1)S(1)} %collective-permute-done.21.refs_1_), channel_id=1, source_target_pairs={{0,1},{1,0},{2,3},{3,2},{4,5},{5,4},{6,7},{7,6},{8,9},{9,8},{10,11... | collective-permute-start | bytes 491528 | tf_op jit(solution)/shard_map/ppermute | solution.py:22
  77.1 5.6 %collective-permute-start.24 = (bf16[2,384]{1,0:T(2,128)(2,1)S(1)}, bf16[2,384]{1,0:T(2,128)(2,1)S(1)}, u32[]{:S(2)}, u32[]{:S(2)}) collective-permute-start(bf16[2,384]{1,0:T(2,128)(2,1)S(1)} %get-tuple-element.59), channel_id=1, source_target_pairs={{0,2},{1,3},{2,0},{3,1},{4,6},{5,7},{6,4},{7,5},{8,10},{9,11},{10,... | collective-permute-start | bytes 4616 | tf_op jit(solution)/shard_map/ppermute | solution.py:22
  77.7 5.0 %collective-permute-start.25 = (bf16[2,384]{1,0:T(2,128)(2,1)S(1)}, bf16[2,384]{1,0:T(2,128)(2,1)S(1)}, u32[]{:S(2)}, u32[]{:S(2)}) collective-permute-start(bf16[2,384]{1,0:T(2,128)(2,1)S(1)} %get-tuple-element.60), channel_id=1, source_target_pairs={{0,4},{1,5},{2,6},{3,7},{4,0},{5,1},{6,2},{7,3},{8,12},{9,13},{10,... | collective-permute-start | bytes 4616 | tf_op jit(solution)/shard_map/ppermute | solution.py:22
  80.4 4.5 %collective-permute-start.26 = (bf16[2,384]{1,0:T(2,128)(2,1)S(1)}, bf16[2,384]{1,0:T(2,128)(2,1)S(1)}, u32[]{:S(2)}, u32[]{:S(2)}) collective-permute-start(bf16[2,384]{1,0:T(2,128)(2,1)S(1)} %get-tuple-element.61), channel_id=1, source_target_pairs={{0,6},{1,7},{2,4},{3,5},{4,2},{5,3},{6,0},{7,1},{8,14},{9,15},{10,... | collective-permute-start | bytes 4616 | tf_op jit(solution)/shard_map/ppermute | solution.py:22
